TPU v7x, 32 devices: a whole 2x2x4 slice. The times are simulated.
32 devices in a mesh: dp: 8 (over y, x, core), fsdp: 4 (over z).
Axes of the slice: x: 2, y: 2, z: 4, core: 2. Of those that a mesh axis runs over, the one named last changes fastest.
Arguments:
- tokens: bfloat16 [8, 2048, 1024], P('dp', 'fsdp'), may hold values from -6 to 6
- memory_keys: bfloat16 [8, 1024, 1024], P('dp', 'fsdp'), may hold values from -6 to 6
- memory_values: bfloat16 [8, 1024, 1024], P('dp', 'fsdp'), may hold values from -6 to 6
- chosen: int32 [8, 8, 4], P('dp', 'fsdp'), may hold values from 0 to 7, all different within a row
- counts: int32 [8, 8, 4], P('dp', 'fsdp'), may hold values from 1 to 128
- w_query: bfloat16 [1024, 1024], P(('dp', 'fsdp')), may hold values from -0.1875 to 0.1875
- w_key: bfloat16 [1024, 1024], P(('dp', 'fsdp')), may hold values from -0.1875 to 0.1875
- w_value: bfloat16 [1024, 1024], P(('dp', 'fsdp')), may hold values from -0.1875 to 0.1875
- w_out: bfloat16 [1024, 1024], P(('dp', 'fsdp')), may hold values from -1.5 to 1.5
- w_gate: bfloat16 [1024, 2816], P(('dp', 'fsdp')), may hold values from -0.1875 to 0.1875
- w_up: bfloat16 [1024, 2816], P(('dp', 'fsdp')), may hold values from -0.1875 to 0.1875
- w_down: bfloat16 [2816, 1024], P(('dp', 'fsdp')), may hold values from -0.109375 to 0.109375
- gain_attn: bfloat16 [1024], P(('dp', 'fsdp')), may hold values from 0.5 to 1.5
- gain_ffn: bfloat16 [1024], P(('dp', 'fsdp')), may hold values from 0.5 to 1.5
- cotangent: bfloat16 [8, 2048, 1024], P('dp', 'fsdp'), may hold values from -6 to 6
Outputs:
- mixed: bfloat16 [8, 2048, 1024], P('dp', 'fsdp')
- tokens_grad: bfloat16 [8, 2048, 1024], P('dp', 'fsdp')
- grad_w_query: float32 [1024, 1024], P(('dp', 'fsdp'))
- grad_w_key: float32 [1024, 1024], P(('dp', 'fsdp'))
- grad_w_value: float32 [1024, 1024], P(('dp', 'fsdp'))
- grad_w_out: float32 [1024, 1024], P(('dp', 'fsdp'))
- grad_w_gate: float32 [1024, 2816], P(('dp', 'fsdp'))
- grad_w_up: float32 [1024, 2816], P(('dp', 'fsdp'))
- grad_w_down: float32 [2816, 1024], P(('dp', 'fsdp'))
- grad_gain_attn: float32 [1024], P(('dp', 'fsdp'))
- grad_gain_ffn: float32 [1024], P(('dp', 'fsdp'))
Inputs may be any that keep to these rules, and one draw needn't show every extreme that they name: `chosen`: each query block names 4 different memory blocks of its own sequence, and for every block index, some query block of some sequence names it (not necessarily of every sequence).
All inputs are finite; a program needn't handle non-finite values.
Results may differ from a plain program's by a relative error of at most 0.017.
Values may be sent and summed in bfloat16 or wider, within the bound.
No kernel may reach another device: no remote copies, remote signals or barrier semaphores. Data moves between devices by JAX's collectives and lax.ppermute only.
A program may use at most 256 MiB of HBM per device.

v0:
```python
import math

import jax
import jax.numpy as jnp
from jax import lax
from jax.sharding import PartitionSpec as P

HEAD_DIM = 128
QBLK = 256
MBLK = 128


EPSILON = 1e-06
NEGATIVE = -1e30


def norm_rows(values, gain):
    return values * lax.rsqrt(jnp.mean(values * values, -1, keepdims=True) + EPSILON) * gain


def norm_back(values, gain, upstream):
    factor = lax.rsqrt(jnp.mean(values * values, -1, keepdims=True) + EPSILON)
    scaled = upstream * gain
    gain_grad = jnp.sum(upstream * values * factor, axis=(0, 1))
    inner = jnp.mean(scaled * values, -1, keepdims=True)
    return (gain_grad, factor * scaled - values * factor**3 * inner)


def rotary(values, positions, direction):
    half_dim = HEAD_DIM // 2
    frequency = 10000.0 ** (-jnp.arange(half_dim, dtype=jnp.float32) / half_dim)
    angles = positions.astype(jnp.float32)[:, None] * frequency[None, :]
    cosine = jnp.cos(angles)[:, None, :]
    sine_part = direction * jnp.sin(angles)[:, None, :]
    shaped = values.reshape(values.shape[:-1] + (values.shape[-1] // HEAD_DIM, HEAD_DIM))
    front_half = shaped[..., :half_dim]
    back_half = shaped[..., half_dim:]
    turned = jnp.concatenate(
        [front_half * cosine - back_half * sine_part, back_half * cosine + front_half * sine_part],
        -1,
    )
    return turned.reshape(values.shape)


def project(left, weight):
    return jnp.einsum("std,de->ste", left, weight, preferred_element_type=jnp.float32)


def project_back(left, weight):
    return jnp.einsum("ste,de->std", left, weight, preferred_element_type=jnp.float32)


def weight_grad(left, right):
    return jnp.einsum("std,ste->de", left, right, preferred_element_type=jnp.float32)


def column_grad(left, right):
    return weight_grad(left, right)


def select_rows(memory_pair, mem_rows, block_count):
    picked = []
    for table in memory_pair:
        taken = jax.vmap(lambda whole, index: whole[index])(table, mem_rows)
        picked.append(taken.reshape(table.shape[0], block_count, -1, table.shape[-1]))
    return picked


def head_scores(query_head, key_head, mem_key_head, causal, valid_rows):
    seq_count, tok_rows, head_dim = query_head.shape
    score_scale = 1.0 / math.sqrt(head_dim)
    local_part = (
        jnp.einsum("sqd,skd->sqk", query_head, key_head, preferred_element_type=jnp.float32)
        * score_scale
    )
    local_part = jnp.where(causal[None], local_part, NEGATIVE)
    blocked = query_head.reshape(seq_count, -1, QBLK, head_dim)
    remote = (
        jnp.einsum("sbqd,sbmd->sbqm", blocked, mem_key_head, preferred_element_type=jnp.float32)
        * score_scale
    )
    remote = jnp.where(valid_rows[:, :, None, :], remote, NEGATIVE)
    return jnp.concatenate([local_part, remote.reshape(seq_count, tok_rows, -1)], -1)


def combine_values(weights_low, value_head, mem_value_head):
    key_count = value_head.shape[1]
    seq_count = weights_low.shape[0]
    local_out = jnp.einsum(
        "sqk,skd->sqd", weights_low[..., :key_count], value_head, preferred_element_type=jnp.float32
    )
    remote = weights_low[..., key_count:].reshape(
        seq_count, mem_value_head.shape[1], QBLK, mem_value_head.shape[2]
    )
    remote_out = jnp.einsum(
        "sbqm,sbmd->sbqd", remote, mem_value_head, preferred_element_type=jnp.float32
    )
    return local_out + remote_out.reshape(local_out.shape)


def attend_forward(queries, key_pair, mem_pair, causal, valid_rows):
    outputs = []
    log_totals = []
    for head_index in range(queries.shape[-1] // HEAD_DIM):
        columns = slice(head_index * HEAD_DIM, (head_index + 1) * HEAD_DIM)
        scores = head_scores(
            queries[..., columns],
            key_pair[0][..., columns],
            mem_pair[0][..., columns],
            causal,
            valid_rows,
        )
        maximum = jnp.max(scores, -1, keepdims=True)
        exponent = jnp.exp(scores - maximum)
        totals = jnp.sum(exponent, -1, keepdims=True)
        probs = (exponent / totals).astype(jnp.bfloat16)
        outputs.append(combine_values(probs, key_pair[1][..., columns], mem_pair[1][..., columns]))
        log_totals.append(maximum + jnp.log(totals))
    return (jnp.concatenate(outputs, -1), jnp.stack(log_totals))


def attend_backward(queries, key_pair, mem_pair, causal, valid_rows, log_totals, grad_attended):
    query_parts = []
    key_parts = []
    value_parts = []
    for head_index in range(queries.shape[-1] // HEAD_DIM):
        columns = slice(head_index * HEAD_DIM, (head_index + 1) * HEAD_DIM)
        query_head = queries[..., columns]
        key_head = key_pair[0][..., columns]
        value_head = key_pair[1][..., columns]
        mem_key_head = mem_pair[0][..., columns]
        mem_value_head = mem_pair[1][..., columns]
        grad_head = grad_attended[..., columns]
        seq_count, tok_rows, head_dim = query_head.shape
        key_count = key_head.shape[1]
        mem_count = mem_key_head.shape[2]
        score_scale = 1.0 / math.sqrt(head_dim)
        scores = head_scores(query_head, key_head, mem_key_head, causal, valid_rows)
        probs = jnp.exp(scores - log_totals[head_index])
        grad_local = jnp.einsum(
            "sqd,skd->sqk", grad_head, value_head, preferred_element_type=jnp.float32
        )
        grad_blocked = grad_head.reshape(seq_count, -1, QBLK, head_dim)
        grad_remote = jnp.einsum(
            "sbqd,sbmd->sbqm", grad_blocked, mem_value_head, preferred_element_type=jnp.float32
        )
        grad_probs = jnp.concatenate([grad_local, grad_remote.reshape(seq_count, tok_rows, -1)], -1)
        delta = jnp.sum(probs * grad_probs, -1, keepdims=True)
        grad_scores = (probs * (grad_probs - delta)).astype(jnp.bfloat16)
        local_scores = grad_scores[..., :key_count]
        remote_scores = grad_scores[..., key_count:].reshape(seq_count, -1, QBLK, mem_count)
        grad_query = jnp.einsum(
            "sqk,skd->sqd", local_scores, key_head, preferred_element_type=jnp.float32
        )
        grad_query = grad_query + jnp.einsum(
            "sbqm,sbmd->sbqd", remote_scores, mem_key_head, preferred_element_type=jnp.float32
        ).reshape(grad_query.shape)
        query_parts.append(score_scale * grad_query)
        key_parts.append(
            score_scale
            * jnp.einsum(
                "sqk,sqd->skd", local_scores, query_head, preferred_element_type=jnp.float32
            )
        )
        probs_low = probs[..., :key_count].astype(jnp.bfloat16)
        value_parts.append(
            jnp.einsum("sqk,sqd->skd", probs_low, grad_head, preferred_element_type=jnp.float32)
        )
    return (
        jnp.concatenate(query_parts, -1),
        jnp.concatenate(key_parts, -1),
        jnp.concatenate(value_parts, -1),
    )


def reduce_ffn(normed_two_low, grad_gate_low, grad_up_low, hidden_low, cotangent):
    gate_up = lax.psum_scatter(
        jnp.concatenate(
            [column_grad(normed_two_low, grad_gate_low), column_grad(normed_two_low, grad_up_low)],
            1,
        ),
        ("dp", "fsdp"),
        scatter_dimension=0,
        tiled=True,
    )
    down_share = lax.psum_scatter(
        column_grad(hidden_low, cotangent), ("dp", "fsdp"), scatter_dimension=0, tiled=True
    )
    hidden_width = gate_up.shape[1] // 2
    return (gate_up[:, :hidden_width], gate_up[:, hidden_width:], down_share)


def body(
    tokens,
    memory_keys,
    memory_values,
    chosen,
    counts,
    w_query,
    w_key,
    w_value,
    w_out,
    w_gate,
    w_up,
    w_down,
    gain_attn,
    gain_ffn,
    cotangent,
):
    shards = (w_query, w_key, w_value, w_out, w_gate, w_up, w_down, gain_attn, gain_ffn)
    weights_full = (
        lax.all_gather(shards[0], ("dp", "fsdp"), axis=0, tiled=True),
        lax.all_gather(shards[1], ("dp", "fsdp"), axis=0, tiled=True),
        lax.all_gather(shards[2], ("dp", "fsdp"), axis=0, tiled=True),
        lax.all_gather(shards[3], ("dp", "fsdp"), axis=0, tiled=True),
        lax.all_gather(shards[4], ("dp", "fsdp"), axis=0, tiled=True),
        lax.all_gather(shards[5], ("dp", "fsdp"), axis=0, tiled=True),
        lax.all_gather(shards[6], ("dp", "fsdp"), axis=0, tiled=True),
        lax.all_gather(shards[7], ("dp", "fsdp"), axis=0, tiled=True),
        lax.all_gather(shards[8], ("dp", "fsdp"), axis=0, tiled=True),
    )
    (
        query_full,
        key_full,
        value_full,
        out_full,
        gate_full,
        up_full,
        down_full,
        gain_one,
        gain_two,
    ) = weights_full
    seq_count, tok_rows, model_width = tokens.shape
    block_count = chosen.shape[1]
    positions = lax.axis_index("fsdp") * tok_rows + jnp.arange(tok_rows, dtype=jnp.int32)
    key_count = tok_rows * lax.axis_size("fsdp")
    causal = positions[:, None] >= jnp.arange(key_count, dtype=jnp.int32)[None, :]
    offsets = jnp.arange(MBLK, dtype=jnp.int32)
    mem_rows = (chosen[:, :, :, None] * MBLK + offsets).reshape(seq_count, -1)
    valid_rows = (offsets < counts[:, :, :, None]).reshape(seq_count, block_count, -1)
    inputs = tokens.astype(jnp.float32)
    normed_low = norm_rows(inputs, gain_one.astype(jnp.float32)).astype(jnp.bfloat16)
    queries = rotary(project(normed_low, query_full), positions, 1.0).astype(jnp.bfloat16)
    key_rows = rotary(project(normed_low, key_full), positions, 1.0).astype(jnp.bfloat16)
    value_rows = project(normed_low, value_full).astype(jnp.bfloat16)
    key_pair = (
        lax.all_gather(key_rows, "fsdp", axis=1, tiled=True),
        lax.all_gather(value_rows, "fsdp", axis=1, tiled=True),
    )
    memory_pair = (
        lax.all_gather(memory_keys, "fsdp", axis=1, tiled=True),
        lax.all_gather(memory_values, "fsdp", axis=1, tiled=True),
    )
    selected = select_rows(memory_pair, mem_rows, block_count)
    attended, log_totals = attend_forward(queries, key_pair, selected, causal, valid_rows)
    attended_low = attended.astype(jnp.bfloat16)
    middle = inputs + project(attended_low, out_full)
    normed_two_low = norm_rows(middle, gain_two.astype(jnp.float32)).astype(jnp.bfloat16)
    gate_act = project(normed_two_low, gate_full)
    up_act = project(normed_two_low, up_full)
    sigmoid_gate = jax.nn.sigmoid(gate_act)
    hidden_low = (gate_act * sigmoid_gate * up_act).astype(jnp.bfloat16)
    mixed = (middle + project(hidden_low, down_full)).astype(jnp.bfloat16)
    back_full = (
        lax.all_gather(shards[0], ("dp", "fsdp"), axis=0, tiled=True),
        lax.all_gather(shards[1], ("dp", "fsdp"), axis=0, tiled=True),
        lax.all_gather(shards[2], ("dp", "fsdp"), axis=0, tiled=True),
        lax.all_gather(shards[3], ("dp", "fsdp"), axis=0, tiled=True),
        lax.all_gather(shards[4], ("dp", "fsdp"), axis=0, tiled=True),
        lax.all_gather(shards[5], ("dp", "fsdp"), axis=0, tiled=True),
        lax.all_gather(shards[6], ("dp", "fsdp"), axis=0, tiled=True),
        lax.all_gather(shards[7], ("dp", "fsdp"), axis=0, tiled=True),
        lax.all_gather(shards[8], ("dp", "fsdp"), axis=0, tiled=True),
    )
    back_pair = (
        lax.all_gather(key_rows, "fsdp", axis=1, tiled=True),
        lax.all_gather(value_rows, "fsdp", axis=1, tiled=True),
    )
    back_memory = select_rows(
        (
            lax.all_gather(memory_keys, "fsdp", axis=1, tiled=True),
            lax.all_gather(memory_values, "fsdp", axis=1, tiled=True),
        ),
        mem_rows,
        block_count,
    )
    (
        query_back,
        key_back,
        value_back,
        out_back,
        gate_back,
        up_back,
        down_back,
        gain_one_back,
        gain_two_back,
    ) = back_full
    grad_output = cotangent.astype(jnp.float32)
    grad_hidden = project_back(cotangent, down_back)
    grad_gate_low = (
        grad_hidden * up_act * sigmoid_gate * (1.0 + gate_act * (1.0 - sigmoid_gate))
    ).astype(jnp.bfloat16)
    grad_up_low = (grad_hidden * gate_act * sigmoid_gate).astype(jnp.bfloat16)
    grad_normed_two = project_back(grad_gate_low, gate_back) + project_back(grad_up_low, up_back)
    grad_gain_two, grad_middle_norm = norm_back(
        middle, gain_two_back.astype(jnp.float32), grad_normed_two
    )
    grad_middle = grad_output + grad_middle_norm
    grad_branch_low = grad_middle.astype(jnp.bfloat16)
    grad_attended_low = project_back(grad_branch_low, out_back).astype(jnp.bfloat16)
    grad_queries, grad_keys_all, grad_values_all = attend_backward(
        queries, back_pair, back_memory, causal, valid_rows, log_totals, grad_attended_low
    )
    grad_keys, grad_values = (
        lax.psum_scatter(
            grad_keys_all.astype(jnp.bfloat16), "fsdp", scatter_dimension=1, tiled=True
        ).astype(jnp.float32),
        lax.psum_scatter(
            grad_values_all.astype(jnp.bfloat16), "fsdp", scatter_dimension=1, tiled=True
        ).astype(jnp.float32),
    )
    grad_query_low = rotary(grad_queries, positions, -1.0).astype(jnp.bfloat16)
    grad_key_low = rotary(grad_keys, positions, -1.0).astype(jnp.bfloat16)
    grad_value_low = grad_values.astype(jnp.bfloat16)
    grad_normed = (
        project_back(grad_query_low, query_back)
        + project_back(grad_key_low, key_back)
        + project_back(grad_value_low, value_back)
    )
    grad_gain_one, grad_input_norm = norm_back(
        inputs, gain_one_back.astype(jnp.float32), grad_normed
    )
    tokens_grad = (grad_middle + grad_input_norm).astype(jnp.bfloat16)
    attn_share = lax.psum_scatter(
        jnp.concatenate(
            [
                column_grad(normed_low, grad_query_low),
                column_grad(normed_low, grad_key_low),
                column_grad(normed_low, grad_value_low),
                column_grad(attended_low, grad_branch_low),
            ],
            1,
        ),
        ("dp", "fsdp"),
        scatter_dimension=0,
        tiled=True,
    )
    ffn_shares = reduce_ffn(normed_two_low, grad_gate_low, grad_up_low, hidden_low, cotangent)
    gain_one_share, gain_two_share = (
        lax.psum_scatter(grad_gain_one, ("dp", "fsdp"), scatter_dimension=0, tiled=True),
        lax.psum_scatter(grad_gain_two, ("dp", "fsdp"), scatter_dimension=0, tiled=True),
    )
    width = attn_share.shape[1] // 4
    return (
        mixed,
        tokens_grad,
        attn_share[:, :width],
        attn_share[:, width : 2 * width],
        attn_share[:, 2 * width : 3 * width],
        attn_share[:, 3 * width :],
        ffn_shares[0],
        ffn_shares[1],
        ffn_shares[2],
        gain_one_share,
        gain_two_share,
    )


def solution(mesh):
    in_specs = (
        P("dp", "fsdp", None),
        P("dp", "fsdp", None),
        P("dp", "fsdp", None),
        P("dp", "fsdp", None),
        P("dp", "fsdp", None),
        P(("dp", "fsdp"), None),
        P(("dp", "fsdp"), None),
        P(("dp", "fsdp"), None),
        P(("dp", "fsdp"), None),
        P(("dp", "fsdp"), None),
        P(("dp", "fsdp"), None),
        P(("dp", "fsdp"), None),
        P(("dp", "fsdp")),
        P(("dp", "fsdp")),
        P("dp", "fsdp", None),
    )
    out_specs = (
        P("dp", "fsdp", None),
        P("dp", "fsdp", None),
        P(("dp", "fsdp"), None),
        P(("dp", "fsdp"), None),
        P(("dp", "fsdp"), None),
        P(("dp", "fsdp"), None),
        P(("dp", "fsdp"), None),
        P(("dp", "fsdp"), None),
        P(("dp", "fsdp"), None),
        P(("dp", "fsdp")),
        P(("dp", "fsdp")),
    )
    return jax.shard_map(body, mesh=mesh, in_specs=in_specs, out_specs=out_specs, check_vma=False)
```

profile of v0, /device:TPU:0, one launch (start us, length us, event | category | flops | bytes accessed | tf_op | source)
XLA Modules:
  0.0 2165.5 jit_solution(1147998711420123806)
XLA Ops:
  12.3 42.1 %all-reduce.5 = (bf16[1024]{0:T(1024)(128)(2,1)S(1)}, bf16[1024]{0:T(1024)(128)(2,1)S(1)}) all-reduce(bf16[1024]{0:T(1024)(128)(2,1)S(1)} %dynamic-update-slice, bf16[1024]{0:T(1024)(128)(2,1)S(1)} %dynamic-update-slice.1), channel_id=1, replica_groups=mesh['dp'=8,'fsdp'=4] {'dp','fsdp'}, use_global_device_ids=true, to_apply=%add | all-reduce | flops 2048 | bytes 8192
  58.0 12.3 all-gather.15.cloned.1.call-done
  73.2 55.3 %all-gather.13.cloned.1.call-done = bf16[1024,1024]{1,0:T(8,128)(2,1)} async-done(((bf16[32,1024]{1,0:T(8,128)(2,1)}), bf16[1024,1024]{1,0:T(8,128)(2,1)}) %all-gather.13.cloned.1.call-update) | async-done | bytes 2097168 | tf_op jit(solution)/shard_map/all_gather | solution.py:212
  137.3 49.5 %all-gather.21.cloned.1.call-done = bf16[1024,1024]{1,0:T(8,128)(2,1)} async-done(((bf16[32,1024]{1,0:T(8,128)(2,1)}), bf16[1024,1024]{1,0:T(8,128)(2,1)}) %all-gather.21.cloned.1.call-update) | async-done | bytes 2097168 | tf_op jit(solution)/shard_map/all_gather | solution.py:214
  194.0 38.8 %all-gather.23.cloned.1.call-done = bf16[1,1024,1024]{2,1,0:T(8,128)(2,1)} async-done(((bf16[1,256,1024]{2,1,0:T(8,128)(2,1)}), bf16[1,1024,1024]{2,1,0:T(8,128)(2,1)}) %all-gather.23.cloned.1.call-update) | async-done | bytes 2097168 | tf_op jit(solution)/shard_map/all_gather | solution.py:252
  232.8 19.7 gather_fusion.1
  252.5 26.7 %all-gather.19.cloned.1.call-done = bf16[1,1024,1024]{2,1,0:T(8,128)(2,1)} async-done(((bf16[1,256,1024]{2,1,0:T(8,128)(2,1)}), bf16[1,1024,1024]{2,1,0:T(8,128)(2,1)}) %all-gather.19.cloned.1.call-update) | async-done | bytes 2097168 | tf_op jit(solution)/shard_map/all_gather | solution.py:251
  279.1 14.5 gather_fusion
  312.4 48.3 %all-gather.17.cloned.1.call-done = bf16[1,2048,1024]{1,2,0:T(8,128)(2,1)} async-done(((bf16[1,512,1024]{1,2,0:T(8,128)(2,1)}), bf16[1,2048,1024]{1,2,0:T(8,128)(2,1)}) %all-gather.17.cloned.1.call-update) | async-done | bytes 4194320 | tf_op jit(solution)/shard_map/all_gather | solution.py:247
  381.8 16.4 fusion.22
  467.8 31.7 %all-gather.25.cloned.1.call-done = bf16[1024,1024]{1,0:T(8,128)(2,1)} async-done(((bf16[32,1024]{1,0:T(8,128)(2,1)}), bf16[1024,1024]{1,0:T(8,128)(2,1)}) %all-gather.25.cloned.1.call-update) | async-done | bytes 2097168 | tf_op jit(solution)/shard_map/all_gather | solution.py:215
  505.6 63.0 %all-gather.29.cloned.1.call-done = bf16[1024,2816]{1,0:T(8,128)(2,1)} async-done(((bf16[32,2816]{1,0:T(8,128)(2,1)}), bf16[1024,2816]{1,0:T(8,128)(2,1)}) %all-gather.29.cloned.1.call-update) | async-done | bytes 5767184 | tf_op jit(solution)/shard_map/all_gather | solution.py:217
  577.2 60.4 %all-gather.27.cloned.1.call-done = bf16[1024,2816]{1,0:T(8,128)(2,1)} async-done(((bf16[32,2816]{1,0:T(8,128)(2,1)}), bf16[1024,2816]{1,0:T(8,128)(2,1)}) %all-gather.27.cloned.1.call-update) | async-done | bytes 5767184 | tf_op jit(solution)/shard_map/all_gather | solution.py:216
  646.2 60.6 %all-gather.31.cloned.1.call-done = bf16[2816,1024]{1,0:T(8,128)(2,1)} async-done(((bf16[88,1024]{1,0:T(8,128)(2,1)}), bf16[2816,1024]{1,0:T(8,128)(2,1)}) %all-gather.31.cloned.1.call-update) | async-done | bytes 5767184 | tf_op jit(solution)/shard_map/all_gather | solution.py:218
  706.8 11.9 multiply_convert_fusion
  765.2 10.8 multiply_reduce_fusion.6
  920.2 16.4 reduce-scatter.8.cloned.1.call-done
  946.7 69.6 %reduce-scatter.10.cloned.1.call-done = bf16[1,512,1024]{1,2,0:T(8,128)(2,1)} async-done(((bf16[1,2048,1024]{1,2,0:T(8,128)(2,1)}), bf16[1,512,1024]{1,2,0:T(8,128)(2,1)}) %reduce-scatter.10.cloned.1.call-update) | async-done | bytes 1048592 | tf_op jit(solution)/shard_map/reduce_scatter | solution.py:318
  1028.5 17.6 copy.132
  1063.2 9.6 fusion.183
  1088.3 43.7 %all-reduce.4 = (f32[1024]{0:T(1024)S(1)}, f32[1024]{0:T(1024)S(1)}) all-reduce(f32[1024]{0:T(1024)S(1)} %get-tuple-element.46, f32[1024]{0:T(1024)S(1)} %copy-done.119), channel_id=8, replica_groups=mesh['dp'=8,'fsdp'=4] {'dp','fsdp'}, use_global_device_ids=true, to_apply=%region_42.43.clone | all-reduce | flops 2048 | bytes 16384
  1136.4 275.4 %reduce-scatter.16.cloned.1.call-done = f32[32,4096]{1,0:T(8,128)} async-done(((f32[1024,4096]{1,0:T(8,128)}), f32[32,4096]{1,0:T(8,128)}) %reduce-scatter.16.cloned.1.call-update) | async-done | bytes 524304
  1413.7 492.7 %reduce-scatter.12.cloned.1.call-done = f32[32,5632]{1,0:T(8,128)} async-done(((f32[1024,5632]{1,0:T(8,128)}), f32[32,5632]{1,0:T(8,128)}) %reduce-scatter.12.cloned.1.call-update) | async-done | bytes 720912 | tf_op jit(solution)/shard_map/reduce_scatter | solution.py:177
  1908.3 250.4 %reduce-scatter.14.cloned.1.call-done = f32[88,1024]{1,0:T(8,128)} async-done(((f32[2816,1024]{1,0:T(8,128)}), f32[88,1024]{1,0:T(8,128)}) %reduce-scatter.14.cloned.1.call-update) | async-done | bytes 360464 | tf_op jit(solution)/shard_map/reduce_scatter | solution.py:186
  (544 shorter events, 412.6 us)
Async XLA Ops:
  7.2 186.8 %copy-start = (s32[1,2,4]{2,1,0:T(2,128)S(1)}, s32[1,2,4]{2,1,0:T(2,128)}, u32[]{:S(2)}) copy-start(s32[1,2,4]{2,1,0:T(2,128)} %param.19) | copy-start | bytes 100
  7.2 63.0 %all-gather.15.cloned.1.call-start = ((), (), s32[]{:S(2)}) async-start(), calls=%async_computation.6 | async-start | bytes 2162688 | tf_op jit(solution)/shard_map/all_gather | solution.py:213
  7.9 120.6 %all-gather.13.cloned.1.call-start = ((), (), s32[]{:S(2)}) async-start(), calls=%async_computation.5 | async-start | bytes 2162688 | tf_op jit(solution)/shard_map/all_gather | solution.py:212
  8.7 178.1 %all-gather.21.cloned.1.call-start = ((), (), s32[]{:S(2)}) async-start(), calls=%async_computation.9 | async-start | bytes 2162688 | tf_op jit(solution)/shard_map/all_gather | solution.py:214
  9.4 223.4 %all-gather.23.cloned.1.call-start = ((), (), s32[]{:S(2)}) async-start(), calls=%async_computation.10 | async-start | bytes 2621440 | tf_op jit(solution)/shard_map/all_gather | solution.py:252
  10.0 269.1 %all-gather.19.cloned.1.call-start = ((), (), s32[]{:S(2)}) async-start(), calls=%async_computation.8 | async-start | bytes 2621440 | tf_op jit(solution)/shard_map/all_gather | solution.py:251
  10.6 350.1 %all-gather.17.cloned.1.call-start = ((), (), s32[]{:S(2)}) async-start(), calls=%async_computation.7 | async-start | bytes 5242880 | tf_op jit(solution)/shard_map/all_gather | solution.py:247
  54.4 132.4 %copy-start.113 = (f32[1024]{0:T(1024)}, f32[1024]{0:T(1024)S(1)}, u32[]{:S(2)}) copy-start(f32[1024]{0:T(1024)S(1)} %convert_element_type.344) | copy-start | bytes 12292
  56.8 130.1 %copy-start.115 = (f32[512]{0:T(512)}, f32[512]{0:T(512)S(1)}, u32[]{:S(2)}) copy-start(f32[512]{0:T(512)S(1)} %get-tuple-element.125) | copy-start | bytes 6148
  58.0 77.4 %copy-start.88 = (f32[512,64]{0,1:T(8,128)}, f32[512,64]{0,1:T(8,128)S(1)}, u32[]{:S(2)}) copy-start(f32[512,64]{0,1:T(8,128)S(1)} %get-tuple-element.123) | copy-start | bytes 393220
  70.2 62.2 %copy-start.38 = (bf16[1,512,1024]{2,1,0:T(8,128)(2,1)S(1)}, bf16[1,512,1024]{2,1,0:T(8,128)(2,1)}, u32[]{:S(2)}) copy-start(bf16[1,512,1024]{2,1,0:T(8,128)(2,1)} %param.15) | copy-start | bytes 3145732
  137.3 56.5 %copy-start.120 = (s32[1,2,4]{2,1,0:T(2,128)S(1)}, s32[1,2,4]{2,1,0:T(2,128)}, u32[]{:S(2)}) copy-start(s32[1,2,4]{2,1,0:T(2,128)} %param.18) | copy-start | bytes 100
  137.3 314.7 %all-gather.33.cloned.1.call-start = ((), (), s32[]{:S(2)}) async-start(), calls=%async_computation.19 | async-start | bytes 5242880 | tf_op jit(solution)/shard_map/all_gather | solution.py:248
  190.7 308.8 %all-gather.25.cloned.1.call-start = ((), (), s32[]{:S(2)}) async-start(), calls=%async_computation.11 | async-start | bytes 2162688 | tf_op jit(solution)/shard_map/all_gather | solution.py:215
  191.4 377.1 %all-gather.29.cloned.1.call-start = ((), (), s32[]{:S(2)}) async-start(), calls=%async_computation.13 | async-start | bytes 5947392 | tf_op jit(solution)/shard_map/all_gather | solution.py:217
  192.2 445.4 %all-gather.27.cloned.1.call-start = ((), (), s32[]{:S(2)}) async-start(), calls=%async_computation.12 | async-start | bytes 5947392 | tf_op jit(solution)/shard_map/all_gather | solution.py:216
  192.8 514.0 %all-gather.31.cloned.1.call-start = ((), (), s32[]{:S(2)}) async-start(), calls=%async_computation.14 | async-start | bytes 5947392 | tf_op jit(solution)/shard_map/all_gather | solution.py:218
  193.5 743.1 %reduce-scatter.8.cloned.1.call-start = ((), (), s32[]{:S(2)}) async-start(), calls=%async_computation.15 | async-start | bytes 5242880 | tf_op jit(solution)/shard_map/reduce_scatter | solution.py:315
  312.4 56.0 %copy-start.41 = (bf16[1,512,8,128]{1,3,2,0:T(8,128)(2,1)S(1)}, bf16[1,512,8,128]{1,3,2,0:T(8,128)(2,1)}, u32[]{:S(2)}) copy-start(bf16[1,512,8,128]{1,3,2,0:T(8,128)(2,1)} %copy-done.40) | copy-start | bytes 3145732
  860.7 155.6 %reduce-scatter.10.cloned.1.call-start = ((), (), s32[]{:S(2)}) async-start(), calls=%async_computation.16 | async-start | bytes 5242880 | tf_op jit(solution)/shard_map/reduce_scatter | solution.py:318
  881.5 530.3 %reduce-scatter.16.cloned.1.call-start = ((), (), s32[]{:S(2)}) async-start(), calls=%async_computation.20 | async-start | bytes 17301504
  1046.1 860.3 %reduce-scatter.12.cloned.1.call-start = ((), (), s32[]{:S(2)}) async-start(), calls=%async_computation.17 | async-start | bytes 23789568 | tf_op jit(solution)/shard_map/reduce_scatter | solution.py:177
  1063.0 1095.7 %reduce-scatter.14.cloned.1.call-start = ((), (), s32[]{:S(2)}) async-start(), calls=%async_computation.18 | async-start | bytes 11894784 | tf_op jit(solution)/shard_map/reduce_scatter | solution.py:186
  1133.2 1025.6 %copy-start.1 = (s32[1,2,4]{2,1,0:T(2,128)S(1)}, s32[1,2,4]{2,1,0:T(2,128)}, u32[]{:S(2)}) copy-start(s32[1,2,4]{2,1,0:T(2,128)} %param.19) | copy-start | bytes 100
  (131 other events, 751.5 us)
Sparse Core Ops, SparseCore 0:
  11.0 59.2 all-gather.14
  73.1 55.3 all-gather.12
  131.4 55.3 all-gather.20
  188.2 44.5 all-gather.22
  234.2 44.8 all-gather.18
  281.1 79.4 all-gather.16
  362.2 79.2 all-gather.32
  444.5 55.0 all-gather.24
  502.4 66.1 all-gather.28
  571.3 66.2 all-gather.26
  640.4 66.2 all-gather.30
  860.8 75.7 reduce-scatter.7
  939.0 77.2 reduce-scatter.9
  1046.2 365.5 reduce-scatter.15
  1414.0 492.3 reduce-scatter.11
  1909.1 249.6 reduce-scatter.13
where the time goes:
time: 2170 us
  waiting for transfers between devices  1560 us (72%)
  matrix products  250 us (12%)
  other arithmetic  133 us (6%)
  local copies, waits for them, and re-layouts  122 us (6%)
  blocking collectives  85.8 us (4%)
    reduce_scatter x1, waiting for transfers between devices, reduce_ffn(): lax.psum_scatter(jnp.concatenate([column_grad(normed_two_low, grad_gate_l...  493 us
    unnamed x17, waiting for transfers between devices  281 us
    reduce_scatter x1, waiting for transfers between devices, reduce_ffn(): lax.psum_scatter(column_grad(hidden_low, cotangent), ('dp', 'fsdp'), scat...  250 us
    unnamed x2, blocking collectives  85.8 us
    reduce_scatter x1, waiting for transfers between devices, body(): lax.psum_scatter(grad_values_all.astype(jnp.bfloat16), 'fsdp', scatter_di...  69.6 us
    all_gather x1, waiting for transfers between devices, body(): lax.all_gather(shards[5], ('dp', 'fsdp'), axis=0, tiled=True)  63 us
    all_gather x1, waiting for transfers between devices, body(): lax.all_gather(shards[6], ('dp', 'fsdp'), axis=0, tiled=True)  60.6 us
    all_gather x1, waiting for transfers between devices, body(): lax.all_gather(shards[4], ('dp', 'fsdp'), axis=0, tiled=True)  60.4 us
  transfers between devices with their start and end apart: 16, of which 15 were waited for; matrix products, arithmetic and copies ran while one was open for 14% of the time, Pallas kernels for 0%

commit v1 on v0

v1 whole, which is shorter than its diff:
```python
import functools
import math

import jax
import jax.numpy as jnp
import numpy as np
from jax import lax
from jax.experimental import pallas as pl
from jax.experimental.pallas import tpu as pltpu
from jax.sharding import PartitionSpec as P

HEAD_DIM = 128
QBLK = 256
MBLK = 128
EPSILON = 1e-06
NEGATIVE = -1e30
SCALE = 1.0 / math.sqrt(HEAD_DIM)
LOG2E = math.log2(math.e)
MIB = 1 << 20
F32 = jnp.float32
BF16 = jnp.bfloat16
NT = (((1,), (1,)), ((), ()))
TN = (((0,), (0,)), ((), ()))


def dot(left, right, dims=(((1,), (0,)), ((), ()))):
    return lax.dot_general(left, right, dims, preferred_element_type=F32)


def rotary_tables(length):
    half_dim = HEAD_DIM // 2
    frequency = 10000.0 ** (-jnp.arange(half_dim, dtype=F32) / half_dim)
    angles = jnp.arange(length, dtype=jnp.int32).astype(F32)[:, None] * frequency[None, :]
    cosine, sine = jnp.cos(angles), jnp.sin(angles)
    return jnp.concatenate([cosine, cosine], 1), jnp.concatenate([-sine, sine], 1)


def qkv_kernel(heads, tok_ref, gain_ref, w_ref, cos_ref, sin_ref, qkv_ref, normed_ref):
    rows = tok_ref[...].astype(F32)
    factor = lax.rsqrt(jnp.mean(rows * rows, -1, keepdims=True) + EPSILON)
    normed = (rows * factor * gain_ref[...]).astype(BF16)
    normed_ref[...] = normed
    cosine, sine = cos_ref[...], sin_ref[...]
    for part in range(3):
        for head in range(heads):
            columns = slice((part * heads + head) * HEAD_DIM, (part * heads + head + 1) * HEAD_DIM)
            value = dot(normed, w_ref[:, columns])
            if part < 2:
                value = value * cosine + pltpu.roll(value, HEAD_DIM // 2, 1) * sine
            qkv_ref[:, columns] = value.astype(BF16)


def project_qkv(tokens_all, gain, w_qkv, cosine, sine, heads):
    length, width = tokens_all.shape
    columns = w_qkv.shape[1]
    block = QBLK
    return pl.pallas_call(
        functools.partial(qkv_kernel, heads),
        grid=(length // block,),
        in_specs=[
            pl.BlockSpec((block, width), lambda i: (i, 0)),
            pl.BlockSpec((1, width), lambda i: (0, 0)),
            pl.BlockSpec((width, columns), lambda i: (0, 0)),
            pl.BlockSpec((block, HEAD_DIM), lambda i: (i, 0)),
            pl.BlockSpec((block, HEAD_DIM), lambda i: (i, 0)),
        ],
        out_specs=[
            pl.BlockSpec((block, columns), lambda i: (i, 0)),
            pl.BlockSpec((block, width), lambda i: (i, 0)),
        ],
        out_shape=[
            jax.ShapeDtypeStruct((length, columns), BF16),
            jax.ShapeDtypeStruct((length, width), BF16),
        ],
        compiler_params=pltpu.CompilerParams(vmem_limit_bytes=48 * MIB),
        cost_estimate=pl.CostEstimate(
            flops=2 * length * width * columns, bytes_accessed=4 * length * (width + columns), transcendentals=0
        ),
        name="project_qkv",
    )(tokens_all, gain, w_qkv, cosine, sine)


def memory_bias(counts_ref, base, top, axis):
    shape = (1, top * MBLK) if axis == 1 else (top * MBLK, 1)
    column = lax.broadcasted_iota(jnp.int32, shape, axis)
    limit = jnp.zeros(shape, jnp.int32)
    for entry in range(top):
        inside = (column >= entry * MBLK) & (column < entry * MBLK + counts_ref[base + entry])
        limit = jnp.where(inside, 1, limit)
    return jnp.where(limit > 0, 0.0, NEGATIVE)


def pick_memory(ref, chosen_ref, base, top, columns):
    rows = [
        ref[pl.ds(pl.multiple_of(chosen_ref[base + entry] * MBLK, MBLK), MBLK), columns]
        for entry in range(top)
    ]
    return jnp.concatenate(rows, 0)


def forward_kernel(heads, top, chosen_ref, counts_ref, q_ref, k_ref, v_ref, mk_ref, mv_ref, out_ref, lse_ref):
    block = pl.program_id(0)
    base = block * top
    bias = memory_bias(counts_ref, base, top, 1)
    row = lax.broadcasted_iota(jnp.int32, (QBLK, QBLK), 0)
    column = lax.broadcasted_iota(jnp.int32, (QBLK, QBLK), 1)
    causal = row >= column
    own = pl.ds(pl.multiple_of(block * QBLK, QBLK), QBLK)
    unit = SCALE * LOG2E
    states = []
    for head in range(heads):
        columns = slice(head * HEAD_DIM, (head + 1) * HEAD_DIM)
        query = q_ref[:, columns]
        remote = dot(query, pick_memory(mk_ref, chosen_ref, base, top, columns), NT) * unit + bias
        local = jnp.where(causal, dot(query, k_ref[own, columns], NT) * unit, NEGATIVE)
        peak = jnp.maximum(jnp.max(remote, -1, keepdims=True), jnp.max(local, -1, keepdims=True))
        remote = jnp.exp2(remote - peak)
        local = jnp.exp2(local - peak)
        total = jnp.sum(remote, -1, keepdims=True) + jnp.sum(local, -1, keepdims=True)
        acc = dot(remote.astype(BF16), pick_memory(mv_ref, chosen_ref, base, top, columns))
        acc = acc + dot(local.astype(BF16), v_ref[own, columns])
        states.append((peak, total, acc))

    def step(index, states):
        rows = pl.ds(pl.multiple_of(index * QBLK, QBLK), QBLK)
        after = []
        for head in range(heads):
            columns = slice(head * HEAD_DIM, (head + 1) * HEAD_DIM)
            peak, total, acc = states[head]
            scores = dot(q_ref[:, columns], k_ref[rows, columns], NT) * unit
            higher = jnp.maximum(peak, jnp.max(scores, -1, keepdims=True))
            shrink = jnp.exp2(peak - higher)
            weights = jnp.exp2(scores - higher)
            total = total * shrink + jnp.sum(weights, -1, keepdims=True)
            acc = acc * shrink + dot(weights.astype(BF16), v_ref[rows, columns])
            after.append((higher, total, acc))
        return tuple(after)

    states = lax.fori_loop(0, block, step, tuple(states))
    for head in range(heads):
        columns = slice(head * HEAD_DIM, (head + 1) * HEAD_DIM)
        peak, total, acc = states[head]
        out_ref[:, columns] = (acc / total).astype(BF16)
        lse_ref[:, head : head + 1] = peak + jnp.log2(total)


def attend_forward(chosen, counts, qkv, memory, heads, top):
    length = qkv.shape[0]
    wide = heads * HEAD_DIM
    blocks = length // QBLK
    mem_rows = memory.shape[0]
    return pl.pallas_call(
        functools.partial(forward_kernel, heads, top),
        grid_spec=pltpu.PrefetchScalarGridSpec(
            num_scalar_prefetch=2,
            grid=(blocks,),
            in_specs=[
                pl.BlockSpec((QBLK, wide), lambda i, *_: (i, 0)),
                pl.BlockSpec((length, wide), lambda i, *_: (0, 1)),
                pl.BlockSpec((length, wide), lambda i, *_: (0, 2)),
                pl.BlockSpec((mem_rows, wide), lambda i, *_: (0, 0)),
                pl.BlockSpec((mem_rows, wide), lambda i, *_: (0, 1)),
            ],
            out_specs=[
                pl.BlockSpec((QBLK, wide), lambda i, *_: (i, 0)),
                pl.BlockSpec((QBLK, heads), lambda i, *_: (i, 0)),
            ],
        ),
        out_shape=[
            jax.ShapeDtypeStruct((length, wide), BF16),
            jax.ShapeDtypeStruct((length, heads), F32),
        ],
        compiler_params=pltpu.CompilerParams(vmem_limit_bytes=48 * MIB),
        cost_estimate=pl.CostEstimate(
            flops=4 * heads * length * HEAD_DIM * (length // 2 + top * MBLK),
            bytes_accessed=8 * length * wide,
            transcendentals=heads * length * (length // 2 + top * MBLK),
        ),
        name="attend_forward",
    )(chosen, counts, qkv, qkv, qkv, memory, memory)


def backward_kernel(
    heads, top, blocks, chosen_ref, counts_ref, q_ref, k_ref, v_ref, mk_ref, mv_ref, go_ref, out_ref, lse_ref,
    cos_ref, sin_ref, grad_ref, gk_ref, gv_ref,
):
    block = blocks - 1 - pl.program_id(0)
    base = block * top
    unit = SCALE * LOG2E
    bias = memory_bias(counts_ref, base, top, 0)
    key_at = lax.broadcasted_iota(jnp.int32, (QBLK, QBLK), 0)
    query_at = lax.broadcasted_iota(jnp.int32, (QBLK, QBLK), 1)
    causal = query_at >= key_at
    own = pl.ds(pl.multiple_of(block * QBLK, QBLK), QBLK)

    @pl.when(pl.program_id(0) == 0)
    def _():
        gk_ref[...] = jnp.zeros_like(gk_ref)
        gv_ref[...] = jnp.zeros_like(gv_ref)

    def spread(column):
        return jnp.transpose(jnp.broadcast_to(column, (QBLK, HEAD_DIM)))[:1]

    stats = []
    for head in range(heads):
        columns = slice(head * HEAD_DIM, (head + 1) * HEAD_DIM)
        grad = go_ref[:, columns]
        delta = jnp.sum(grad.astype(F32) * out_ref[:, columns].astype(F32), -1, keepdims=True)
        stats.append((spread(lse_ref[:, head : head + 1]), spread(delta)))

    def pair(head, keys, values, mask):
        columns = slice(head * HEAD_DIM, (head + 1) * HEAD_DIM)
        lse, delta = stats[head]
        scores = mask(dot(keys, q_ref[:, columns], NT) * unit)
        weights = jnp.exp2(scores - lse)
        grad_weights = dot(values, go_ref[:, columns], NT)
        grad_scores = (weights * (grad_weights - delta)).astype(BF16)
        return weights.astype(BF16), grad_scores

    def update(head, rows, weights, grad_scores):
        columns = slice(head * HEAD_DIM, (head + 1) * HEAD_DIM)
        gk_ref[rows, columns] += dot(grad_scores, q_ref[:, columns])
        gv_ref[rows, columns] += dot(weights, go_ref[:, columns])

    totals = []
    for head in range(heads):
        columns = slice(head * HEAD_DIM, (head + 1) * HEAD_DIM)
        keys = pick_memory(mk_ref, chosen_ref, base, top, columns)
        values = pick_memory(mv_ref, chosen_ref, base, top, columns)
        _, grad_scores = pair(head, keys, values, lambda scores: scores + bias)
        total = dot(grad_scores, keys, TN)
        keys = k_ref[own, columns]
        weights, grad_scores = pair(
            head, keys, v_ref[own, columns], lambda scores: jnp.where(causal, scores, NEGATIVE)
        )
        update(head, own, weights, grad_scores)
        totals.append(total + dot(grad_scores, keys, TN))

    def step(index, totals):
        rows = pl.ds(pl.multiple_of(index * QBLK, QBLK), QBLK)
        after = []
        for head in range(heads):
            columns = slice(head * HEAD_DIM, (head + 1) * HEAD_DIM)
            keys = k_ref[rows, columns]
            weights, grad_scores = pair(head, keys, v_ref[rows, columns], lambda scores: scores)
            update(head, rows, weights, grad_scores)
            after.append(totals[head] + dot(grad_scores, keys, TN))
        return tuple(after)

    totals = lax.fori_loop(0, block, step, tuple(totals))
    cosine, sine = cos_ref[...], sin_ref[...]

    def unturn(value):
        return value * cosine - pltpu.roll(value, HEAD_DIM // 2, 1) * sine

    wide = heads * HEAD_DIM
    for head in range(heads):
        columns = slice(head * HEAD_DIM, (head + 1) * HEAD_DIM)
        at = head * HEAD_DIM
        grad_ref[:, at : at + HEAD_DIM] = unturn(totals[head] * SCALE).astype(BF16)
        grad_key = gk_ref[own, columns] * SCALE
        grad_ref[:, wide + at : wide + at + HEAD_DIM] = unturn(grad_key).astype(BF16)
        grad_ref[:, 2 * wide + at : 2 * wide + at + HEAD_DIM] = gv_ref[own, columns].astype(BF16)


def attend_backward(chosen, counts, qkv, memory, grad_out, out, lse, cosine, sine, heads, top):
    length = qkv.shape[0]
    wide = heads * HEAD_DIM
    blocks = length // QBLK
    mem_rows = memory.shape[0]
    last = blocks - 1
    return pl.pallas_call(
        functools.partial(backward_kernel, heads, top, blocks),
        grid_spec=pltpu.PrefetchScalarGridSpec(
            num_scalar_prefetch=2,
            grid=(blocks,),
            in_specs=[
                pl.BlockSpec((QBLK, wide), lambda i, *_: (last - i, 0)),
                pl.BlockSpec((length, wide), lambda i, *_: (0, 1)),
                pl.BlockSpec((length, wide), lambda i, *_: (0, 2)),
                pl.BlockSpec((mem_rows, wide), lambda i, *_: (0, 0)),
                pl.BlockSpec((mem_rows, wide), lambda i, *_: (0, 1)),
                pl.BlockSpec((QBLK, wide), lambda i, *_: (last - i, 0)),
                pl.BlockSpec((QBLK, wide), lambda i, *_: (last - i, 0)),
                pl.BlockSpec((QBLK, heads), lambda i, *_: (last - i, 0)),
                pl.BlockSpec((QBLK, HEAD_DIM), lambda i, *_: (last - i, 0)),
                pl.BlockSpec((QBLK, HEAD_DIM), lambda i, *_: (last - i, 0)),
            ],
            out_specs=pl.BlockSpec((QBLK, 3 * wide), lambda i, *_: (last - i, 0)),
            scratch_shapes=[pltpu.VMEM((length, wide), F32), pltpu.VMEM((length, wide), F32)],
        ),
        out_shape=jax.ShapeDtypeStruct((length, 3 * wide), BF16),
        compiler_params=pltpu.CompilerParams(vmem_limit_bytes=48 * MIB),
        cost_estimate=pl.CostEstimate(
            flops=10 * heads * length * HEAD_DIM * (length // 2 + top * MBLK),
            bytes_accessed=16 * length * wide,
            transcendentals=heads * length * (length // 2 + top * MBLK),
        ),
        name="attend_backward",
    )(chosen, counts, qkv, qkv, qkv, memory, memory, grad_out, out, lse, cosine, sine)


def chain_gather(block, axis):
    size = lax.axis_size(axis)
    place = lax.axis_index(axis)
    up = [(i, i + 1) for i in range(size - 1)]
    down = [(i + 1, i) for i in range(size - 1)]
    from_below, from_above = [], []
    rising = falling = block
    for _ in range(size - 1):
        rising = lax.ppermute(rising, axis, up)
        falling = lax.ppermute(falling, axis, down)
        from_below.append(rising)
        from_above.append(falling)
    ordered = []
    for index in range(size):
        cases = []
        for mine in range(size):
            if mine == index:
                cases.append(block)
            elif mine > index:
                cases.append(from_below[mine - index - 1])
            else:
                cases.append(from_above[index - mine - 1])
        ordered.append(lax.select_n(place, *cases) if size > 2 else lax.select_n(place > 0, *cases))
    return ordered


def body(
    tokens, memory_keys, memory_values, chosen, counts, w_query, w_key, w_value, w_out, w_gate, w_up, w_down,
    gain_attn, gain_ffn, cotangent,
):
    ring, span = lax.axis_size("fsdp"), lax.axis_size("dp")
    rows, width = tokens.shape[1:]
    heads = width // HEAD_DIM // ring
    wide = heads * HEAD_DIM
    length = rows * ring
    top = chosen.shape[2]
    hidden_width = w_gate.shape[1]
    share = w_query.shape[0]
    mine = tokens[0]

    extra = 8 if share % 8 == 0 else 8 - share % 8
    parts = [w.reshape(share, ring, wide).transpose(1, 0, 2) for w in (w_query, w_key, w_value)]
    gains = jnp.pad(jnp.concatenate([gain_attn, gain_ffn]), (0, 3 * wide - 2 * share))
    gains = jnp.broadcast_to(gains, (ring, extra, 3 * wide))
    parcel = jnp.concatenate([jnp.concatenate(parts, 2), gains], 1)
    parcel = lax.all_to_all(parcel, "fsdp", 0, 0, tiled=True)
    parcel = lax.all_gather(parcel, "dp", axis=0, tiled=True)
    w_qkv = parcel[:, :share].reshape(width, 3 * wide)
    gain_one = parcel[:, share, :share].reshape(1, width).astype(F32)
    gain_two = parcel[:, share, share : 2 * share].reshape(1, width).astype(F32)

    picks = lax.all_gather(jnp.stack([chosen[0], counts[0]]), "fsdp", axis=1, tiled=True)
    chosen_all, counts_all = picks[0].reshape(-1), picks[1].reshape(-1)
    memory = jnp.concatenate(
        [m[0].reshape(-1, ring, wide).transpose(1, 0, 2) for m in (memory_keys, memory_values)], 2
    )
    memory = lax.all_to_all(memory, "fsdp", 0, 0, tiled=True).reshape(-1, 2 * wide)

    gathered = jnp.concatenate(chain_gather(mine, "fsdp"), 0)

    def whole(shard):
        near = lax.all_gather(shard, "fsdp", axis=0, tiled=True)
        return lax.all_gather(near, "dp", axis=0, tiled=True)

    first = whole(jnp.concatenate([w_gate, w_up, w_out], 1))
    down_full = whole(w_down)
    gate_up = first[:, : 2 * hidden_width]
    out_full = first[:, 2 * hidden_width :]

    cosine, sine = rotary_tables(length)
    qkv, normed = project_qkv(gathered, gain_one, w_qkv, cosine, sine, heads)
    attended_heads, lse = attend_forward(chosen_all, counts_all, qkv, memory, heads, top)
    attended = lax.all_to_all(attended_heads, "fsdp", 0, 1, tiled=True)

    middle = mine.astype(F32) + dot(attended, out_full)
    factor = lax.rsqrt(jnp.mean(middle * middle, -1, keepdims=True) + EPSILON)
    normed_two = (middle * factor * gain_two).astype(BF16)
    acts = dot(normed_two, gate_up)
    gate_act, up_act = acts[:, :hidden_width], acts[:, hidden_width:]
    sigmoid = jax.nn.sigmoid(gate_act)
    hidden = (gate_act * sigmoid * up_act).astype(BF16)
    mixed = (middle + dot(hidden, down_full)).astype(BF16)

    upstream = cotangent[0]
    grad_down = dot(hidden, upstream, TN).astype(BF16)
    grad_hidden = dot(upstream, down_full, NT)
    grad_gate = grad_hidden * up_act * sigmoid * (1.0 + gate_act * (1.0 - sigmoid))
    grad_up = grad_hidden * gate_act * sigmoid
    grad_acts = jnp.concatenate([grad_gate.astype(BF16), grad_up.astype(BF16)], 1)
    grad_gate_up = dot(normed_two, grad_acts, TN).astype(BF16)
    grad_normed_two = dot(grad_acts, gate_up, NT)

    def norm_back(values, factor, gain, grad):
        scaled = grad * gain
        inner = jnp.mean(scaled * values, -1, keepdims=True)
        return factor * scaled - values * factor**3 * inner

    gain_two_grad = jnp.sum(grad_normed_two * middle * factor, 0)
    grad_middle = upstream.astype(F32) + norm_back(middle, factor, gain_two, grad_normed_two)
    grad_branch = grad_middle.astype(BF16)
    grad_attended = dot(grad_branch, out_full, NT).astype(BF16)
    grad_heads = lax.all_to_all(grad_attended, "fsdp", 1, 0, tiled=True)
    grad_out = dot(attended, grad_branch, TN).astype(BF16)

    grad_qkv = attend_backward(
        chosen_all, counts_all, qkv, memory, grad_heads, attended_heads, lse, cosine, sine, heads, top
    )
    grad_w_qkv = dot(normed, grad_qkv, TN).astype(BF16)
    partial = dot(grad_qkv, w_qkv, NT)
    tokens_f32 = gathered.astype(F32)
    factor_all = lax.rsqrt(jnp.mean(tokens_f32 * tokens_f32, -1, keepdims=True) + EPSILON)
    gain_one_grad = jnp.sum(partial * tokens_f32 * factor_all, 0)
    grad_normed = lax.psum_scatter(
        partial.astype(BF16), "fsdp", scatter_dimension=0, tiled=True
    ).astype(F32)
    own = mine.astype(F32)
    own_factor = lax.rsqrt(jnp.mean(own * own, -1, keepdims=True) + EPSILON)
    tokens_grad = (grad_middle + norm_back(own, own_factor, gain_one, grad_normed)).astype(BF16)

    def reduced(grad):
        near = lax.psum_scatter(grad, "dp", scatter_dimension=0, tiled=True)
        return lax.psum_scatter(near, "fsdp", scatter_dimension=0, tiled=True).astype(F32)

    down_share = reduced(grad_down)
    gate_up_share = reduced(grad_gate_up)
    gain_columns = jnp.pad(jnp.stack([gain_one_grad, gain_two_grad], 1), ((0, 0), (0, HEAD_DIM - 2)))
    late = jnp.concatenate([grad_w_qkv, grad_out, gain_columns.astype(BF16)], 1)
    late = lax.psum_scatter(late, "dp", scatter_dimension=0, tiled=True)
    late = late.reshape(ring, share, late.shape[1])
    late = lax.all_to_all(late, "fsdp", 0, 0, tiled=True).astype(F32)
    projections = [
        late[:, :, part * wide : (part + 1) * wide].transpose(1, 0, 2).reshape(share, width) for part in range(3)
    ]
    out_share = jnp.sum(late[:, :, 3 * wide : 3 * wide + width], 0)
    gain_shares = jnp.sum(late[:, :, 3 * wide + width :], 0)
    return (
        mixed[None],
        tokens_grad[None],
        *projections,
        out_share,
        gate_up_share[:, :hidden_width],
        gate_up_share[:, hidden_width:],
        down_share,
        gain_shares[:, 0],
        gain_shares[:, 1],
    )


def solution(mesh):
    both = ("dp", "fsdp")
    rows, matrix, vector = P("dp", "fsdp", None), P(both, None), P(both)
    in_specs = (rows,) * 5 + (matrix,) * 7 + (vector,) * 2 + (rows,)
    out_specs = (rows,) * 2 + (matrix,) * 7 + (vector,) * 2
    return jax.shard_map(body, mesh=mesh, in_specs=in_specs, out_specs=out_specs, check_vma=False)
```

time: 2170 us -> 654 us (0.30)
  waiting for transfers between devices: 1560 us -> 287 us
  matrix products: 250 us -> 87 us
  other arithmetic: 133 us -> 29.9 us
  local copies, waits for them, and re-layouts: 122 us -> 30.9 us
  Pallas kernels: 0 us -> 84 us
  starting transfers between devices: 1.23 us -> 34.1 us
    reduce_scatter x4 -> x6, waiting for transfers between devices: 829 us -> 179 us  [the longest x2 54.1 us: reduced(): lax.psum_scatter(near, 'fsdp', scatter_dimension=0, tiled=True).astype(F32)]
    all_gather x11 -> x4, waiting for transfers between devices: 447 us -> 21.9 us  [the longest x1 21.9 us: whole(): near = lax.all_gather(shard, 'fsdp', axis=0, tiled=True)]
    unnamed x17 -> x10, waiting for transfers between devices: 281 us -> 1.47 us
    dot_general x101 -> x11, matrix products: 250 us -> 87 us  [dot(): return lax.dot_general(left, right, dims, preferred_element_type=F32)]
    unnamed x2 -> x0, blocking collectives: 85.8 us -> none
    pallas_call x0 -> x3, Pallas kernels: none -> 84 us  [the longest x1 39.3 us: attend_backward(): pl.pallas_call(functools.partial(backward_kernel, heads, top, blocks), gr...]
    all_gather x0 -> x2, blocking collectives: none -> 56 us  [the longest x1 37.9 us: body(): lax.all_gather(jnp.stack([chosen[0], counts[0]]), 'fsdp', axis=1, tiled=T...]
    all_to_all x0 -> x4, waiting for transfers between devices: none -> 52.7 us  [the longest x1 19.4 us: body(): late = lax.all_to_all(late, 'fsdp', 0, 0, tiled=True).astype(F32)]
  transfers between devices with their start and end apart: 16 -> 20, of which waited for: 15 -> 12; matrix products, arithmetic and copies ran while one was open for 14% -> 18% of each run, Pallas kernels for 0% -> 13%
where the time goes in v1:
time: 654 us; the launch traced here: 644 us
  waiting for transfers between devices  287 us (44%)
  matrix products  87 us (13%)
  Pallas kernels  84 us (13%)
  blocking collectives  76.7 us (12%)
  starting transfers between devices  34.1 us (5%)
  local copies, waits for them, and re-layouts  30.9 us (5%)
  other arithmetic  29.9 us (5%)
  between operations  15.1 us (2%)
    dot_general x11, matrix products, dot(): return lax.dot_general(left, right, dims, preferred_element_type=F32)  87 us
    reduce_scatter x2, waiting for transfers between devices, reduced(): lax.psum_scatter(near, 'fsdp', scatter_dimension=0, tiled=True).astype(F32)  54.1 us
    reduce_scatter x1, waiting for transfers between devices, body(): late = lax.psum_scatter(late, 'dp', scatter_dimension=0, tiled=True)  53 us
    reduce_scatter x1, waiting for transfers between devices, body(): lax.psum_scatter(partial.astype(BF16), 'fsdp', scatter_dimension=0, tiled...  47.4 us
    pallas_call x1, Pallas kernels, attend_backward(): pl.pallas_call(functools.partial(backward_kernel, heads, top, blocks), gr...  39.3 us
    all_gather x1, blocking collectives, body(): lax.all_gather(jnp.stack([chosen[0], counts[0]]), 'fsdp', axis=1, tiled=T...  37.9 us
    pallas_call x1, Pallas kernels, attend_forward(): pl.pallas_call(functools.partial(forward_kernel, heads, top), grid_spec=p...  33.1 us
    ppermute x3, waiting for transfers between devices, chain_gather(): rising = lax.ppermute(rising, axis, up)  26.1 us
  transfers between devices with their start and end apart: 20, of which 12 were waited for; matrix products, arithmetic and copies ran while one was open for 18% of the time, Pallas kernels for 13%

profile of v1, /device:TPU:0, one launch (start us, length us, event | category | flops | bytes accessed | tf_op | source)
XLA Modules:
  0.0 644.3 jit_solution(3218396753313585904)
XLA Ops:
  12.8 20.8 %all_to_all.53 = bf16[4,40,768]{2,1,0:T(8,128)(2,1)} all-to-all(bf16[4,40,768]{2,1,0:T(8,128)(2,1)S(1)} %copy.77), channel_id=1, replica_groups=mesh['dp'=8,'fsdp'=4] {'fsdp'}, dimensions={0} | all-to-all | bytes 491520 | tf_op jit(solution)/shard_map/all_to_all | solution.py:348
  33.7 21.9 %all-gather.7.cloned.1.call-done = bf16[128,6656]{1,0:T(8,128)(2,1)} async-done(((bf16[32,6656]{1,0:T(8,128)(2,1)}), bf16[128,6656]{1,0:T(8,128)(2,1)}) %all-gather.7.cloned.1.call-update) | async-done | bytes 1703952 | tf_op jit(solution)/shard_map/all_gather | solution.py:364
  55.7 18.1 %all_gather.22 = bf16[352,1024]{1,0:T(8,128)(2,1)} all-gather(bf16[88,1024]{1,0:T(8,128)(2,1)S(1)} %copy-done.15), channel_id=1, replica_groups=mesh['dp'=8,'fsdp'=4] {'fsdp'}, dimensions={0}, use_global_device_ids=true | all-gather | bytes 901120 | tf_op jit(solution)/shard_map/all_gather | solution.py:364
  76.6 18.5 %collective-permute-done = bf16[512,1024]{1,0:T(8,128)(2,1)S(1)} collective-permute-done((bf16[512,1024]{1,0:T(8,128)(2,1)S(1)}, bf16[512,1024]{1,0:T(8,128)(2,1)S(1)}, u32[]{:S(2)}, u32[]{:S(2)}) %collective-permute-start) | collective-permute-done | bytes 1048608 | tf_op jit(solution)/shard_map/ppermute | solution.py:311
  110.4 37.9 %all_gather.18 = s32[2,8,4]{2,0,1:T(2,128)S(1)} all-gather(s32[2,2,4]{2,0,1:T(2,128)S(1)} %pad_add_fusion), channel_id=1, replica_groups=mesh['dp'=8,'fsdp'=4] {'fsdp'}, dimensions={1}, use_global_device_ids=true | all-gather | bytes 320 | tf_op jit(solution)/shard_map/all_gather | solution.py:354
  158.4 7.7 %collective-permute-done.2 = bf16[512,1024]{1,0:T(8,128)(2,1)} collective-permute-done((bf16[512,1024]{1,0:T(8,128)(2,1)}, bf16[512,1024]{1,0:T(8,128)(2,1)}, u32[]{:S(2)}, u32[]{:S(2)}) %collective-permute-start.2) | collective-permute-done | bytes 1048608 | tf_op jit(solution)/shard_map/ppermute | solution.py:311
  180.5 11.6 %project_qkv.1 = (bf16[2048,768]{1,0:T(8,128)(2,1)}, bf16[2048,1024]{1,0:T(8,128)(2,1)}) custom-call(bf16[2048,1024]{1,0:T(8,128)(2,1)} %get-tuple-element.30.tok_ref, f32[1,1024]{1,0:T(1,128)S(1)} %reshape.144.gain_ref, bf16[1024,768]{1,0:T(8,128)(2,1)S(1)} %bitcast.68, f32[2048,128]{1,0:T(8,128)S(1)} %get-tuple-element.56.cos_ref, f32[2048,128]{1,0:T(8,128)S(1)} %copy-done), custom_call_target="tpu_custom_call" | custom-call | flops 3221225472 | bytes 14680064 | tf_op jit(solution)/shard_map/project_qkv/pallas_call | solution.py:57
  192.1 33.1 %attend_forward.1 = (bf16[2048,256]{1,0:T(8,128)(2,1)S(1)}, f32[2048,2]{1,0:T(8,128)S(1)}) custom-call(s32[32]{0:T(128)S(1)} %reshape_squeeze.14.chosen_ref, s32[32]{0:T(128)S(1)} %reshape_squeeze.15.counts_ref, bf16[2048,768]{1,0:T(8,128)(2,1)} %get-tuple-element.15.q_ref.k_ref.v_ref, bf16[2048,768]{1,0:T(8,128)(2,1)} %get-tuple-element.15.q_ref.k_ref.v_ref, ...), custom_call_target="tpu_custom_call" | custom-call | flops 3221225472 | bytes 4194304 | tf_op jit(solution)/shard_map/attend_forward/pallas_call | solution.py:152
  234.1 17.0 %all-to-all-done.2 = bf16[4,512,256]{1,2,0:T(8,128)(2,1)} async-done(((bf16[4,512,256]{1,2,0:T(8,128)(2,1)}), bf16[4,512,256]{1,2,0:T(8,128)(2,1)}, u32[]{:S(2)}, u32[]{:S(2)}) %all-to-all-start.2) | async-done | bytes 1048608 | tf_op jit(solution)/shard_map/all_to_all | solution.py:375
  256.0 13.2 %fusion.2 = f32[512,5632]{1,0:T(8,128)} fusion(bf16[1024,6656]{1,0:T(8,128)(2,1)} %all-gather.9.cloned.1.call-done, f32[512,1024]{1,0:T(8,128)S(1)} %get-tuple-element.53, f32[1024]{0:T(1024)S(1)} %reshape.145, f32[512]{0:T(512)S(1)} %get-tuple-element.51), kind=kOutput, calls=%fused_computation.5 | convolution fusion | flops 5907152896 | bytes 25171968 | tf_op jit(solution)/shard_map/dot_general | solution.py:27
  269.3 11.9 %multiply_convert_fusion.1 = (bf16[512,2816]{1,0:T(8,128)(2,1)}, bf16[512,2816]{1,0:T(8,128)(2,1)}, bf16[512,2816]{1,0:T(8,128)(2,1)S(1)}) fusion(f32[512,5632]{1,0:T(8,128)} %fusion.2, bf16[2816,1024]{1,0:T(8,128)(2,1)} %all-gather.11.cloned.1.call-done, bf16[1,512,1024]{2,1,0:T(8,128)(2,1)} %param.29), kind=kOutput, calls=%fused_computation.12 | convolution fusion | flops 2975858688 | bytes 27000832 | tf_op jit(solution)/shard_map/dot_general | solution.py:27
  288.0 12.4 %convolution_convert_fusion = bf16[1024,5632]{1,0:T(8,128)(2,1)} fusion(bf16[512,2816]{1,0:T(8,128)(2,1)} %get-tuple-element.32, bf16[512,2816]{1,0:T(8,128)(2,1)} %get-tuple-element.31, f32[512,1024]{1,0:T(8,128)} %copy-done.10, f32[1024]{0:T(1024)S(1)} %reshape.145, f32[512]{0:T(512)S(1)} %get-tuple-element.51), kind=kOutput, calls=%fused_computation | convolution fusion | flops 5924454400 | bytes 19404800 | tf_op jit(solution)/shard_map/dot_general | solution.py:27
  300.4 14.4 %multiply_reduce_fusion = (bf16[1024]{0:T(1024)(128)(2,1)S(1)}, f32[512]{0:T(512)S(1)}, f32[512,1024]{1,0:T(8,128)}) fusion(f32[512,1024]{1,0:T(8,128)} %copy-done.10, f32[512]{0:T(512)S(1)} %get-tuple-element.51, f32[1024]{0:T(1024)S(1)} %reshape.145, bf16[1024,6656]{1,0:T(8,128)(2,1)} %all-gather.9.cloned.1.call-done, ...), kind=kOutput, calls=%fused_computation.28 | convolution fusion | flops 5920258560 | bytes 21506048 | tf_op jit(solution)/shard_map/dot_general | solution.py:27
  332.3 16.2 %all-to-all-done.3 = bf16[512,4,256]{2,0,1:T(8,128)(2,1)} async-done(((bf16[512,4,256]{2,0,1:T(8,128)(2,1)}), bf16[512,4,256]{2,0,1:T(8,128)(2,1)}, u32[]{:S(2)}, u32[]{:S(2)}) %all-to-all-start.3) | async-done | bytes 1048608 | tf_op jit(solution)/shard_map/all_to_all | solution.py:404
  351.0 39.3 %attend_backward.1 = bf16[2048,768]{1,0:T(8,128)(2,1)} custom-call(s32[32]{0:T(128)S(1)} %reshape_squeeze.14.chosen_ref, s32[32]{0:T(128)S(1)} %reshape_squeeze.15.counts_ref, bf16[2048,768]{1,0:T(8,128)(2,1)} %get-tuple-element.15.q_ref.k_ref.v_ref, bf16[2048,768]{1,0:T(8,128)(2,1)} %get-tuple-element.15.q_ref.k_ref.v_ref, ...), custom_call_target="tpu_custom_call" | custom-call | flops 8053063680 | bytes 8388608 | tf_op jit(solution)/shard_map/attend_backward/pallas_call | solution.py:272
  390.3 7.6 %fusion.5 = (bf16[1024]{0:T(1024)(128)(2,1)S(1)}, bf16[2048,1024]{1,0:T(8,128)(2,1)}) fusion(bf16[2048,1024]{1,0:T(8,128)(2,1)S(1)} %copy-done.9, f32[2048]{0:T(1024)S(1)} %add_rsqrt_fusion, bf16[2048,768]{1,0:T(8,128)(2,1)} %attend_backward.1, bf16[1024,768]{1,0:T(8,128)(2,1)S(1)} %bitcast.69), kind=kOutput, calls=%fused_computation.8 | convolution fusion | flops 3231710208 | bytes 13117440 | tf_op jit(solution)/shard_map/dot_general | solution.py:27
  403.8 6.3 copy.86
  411.7 24.9 %reduce-scatter.11.cloned.1.call-done = bf16[128,5632]{1,0:T(8,128)(2,1)} async-done(((bf16[1024,5632]{1,0:T(8,128)(2,1)}), bf16[128,5632]{1,0:T(8,128)(2,1)}) %reduce-scatter.11.cloned.1.call-update) | async-done | bytes 1441808 | tf_op jit(solution)/shard_map/reduce_scatter | solution.py:423
  437.6 53.0 %reduce-scatter.19.cloned.1.call-done = bf16[128,1920]{1,0:T(8,128)(2,1)} async-done(((bf16[1024,1920]{1,0:T(8,128)(2,1)}), bf16[128,1920]{1,0:T(8,128)(2,1)}) %reduce-scatter.19.cloned.1.call-update) | async-done | bytes 491536 | tf_op jit(solution)/shard_map/reduce_scatter | solution.py:430
  495.5 7.8 %fusion.22 = bf16[1,512,1024]{2,1,0:T(8,128)(2,1)} fusion(f32[512,1024]{1,0:T(8,128)S(1)} %copy-done.11, bf16[512,2816]{1,0:T(8,128)(2,1)} %copy-done.19, bf16[2816,1024]{1,0:T(8,128)(2,1)} %all-gather.11.cloned.1.call-done), kind=kOutput, calls=%fused_computation.44 | convolution fusion | flops 2953838592 | bytes 11796480 | tf_op jit(solution)/shard_map/dot_general | solution.py:27
  503.3 19.4 %all-to-all-done.4 = bf16[4,32,1920]{2,1,0:T(8,128)(2,1)} async-done(((bf16[4,32,1920]{2,1,0:T(8,128)(2,1)}), bf16[4,32,1920]{2,1,0:T(8,128)(2,1)}, u32[]{:S(2)}, u32[]{:S(2)}) %all-to-all-start.4) | async-done | bytes 491552 | tf_op jit(solution)/shard_map/all_to_all | solution.py:432
  527.3 47.4 %reduce-scatter.9.cloned.1.call-done = bf16[512,1024]{1,0:T(8,128)(2,1)} async-done(((bf16[2048,1024]{1,0:T(8,128)(2,1)}), bf16[512,1024]{1,0:T(8,128)(2,1)}) %reduce-scatter.9.cloned.1.call-update) | async-done | bytes 1048592 | tf_op jit(solution)/shard_map/reduce_scatter | solution.py:415
  579.3 21.1 %reduce-scatter.17.cloned.1.call-done = bf16[88,1024]{1,0:T(8,128)(2,1)} async-done(((bf16[352,1024]{1,0:T(8,128)(2,1)}), bf16[88,1024]{1,0:T(8,128)(2,1)}) %reduce-scatter.17.cloned.1.call-update) | async-done | bytes 180240 | tf_op jit(solution)/shard_map/reduce_scatter | solution.py:424
  602.1 33.0 %reduce-scatter.13.cloned.1.call-done = bf16[32,5632]{1,0:T(8,128)(2,1)} async-done(((bf16[128,5632]{1,0:T(8,128)(2,1)}), bf16[32,5632]{1,0:T(8,128)(2,1)}) %reduce-scatter.13.cloned.1.call-update) | async-done | bytes 360464 | tf_op jit(solution)/shard_map/reduce_scatter | solution.py:424
  (138 shorter events, 114.7 us)
Async XLA Ops:
  7.2 48.4 %all-gather.7.cloned.1.call-start = ((), (), s32[]{:S(2)}) async-start(), calls=%async_computation.12 | async-start | bytes 2129920 | tf_op jit(solution)/shard_map/all_gather | solution.py:364
  9.1 92.6 %copy-start.14 = (bf16[1,256,1024]{2,1,0:T(8,128)(2,1)S(1)}, bf16[1,256,1024]{2,1,0:T(8,128)(2,1)}, u32[]{:S(2)}) copy-start(bf16[1,256,1024]{2,1,0:T(8,128)(2,1)} %param.16) | copy-start | bytes 1572868
  9.1 167.5 %all-gather.5.cloned.1.call-start = ((), (), s32[]{:S(2)}) async-start(), calls=%async_computation.11 | async-start | bytes 2211840 | tf_op jit(solution)/shard_map/all_gather | solution.py:349
  33.6 217.5 %all-gather.9.cloned.1.call-start = ((), (), s32[]{:S(2)}) async-start(), calls=%async_computation.13 | async-start | bytes 15335424 | tf_op jit(solution)/shard_map/all_gather | solution.py:365
  55.6 213.7 %all-gather.11.cloned.1.call-start = ((), (), s32[]{:S(2)}) async-start(), calls=%async_computation.14 | async-start | bytes 6488064 | tf_op jit(solution)/shard_map/all_gather | solution.py:365
  73.8 21.2 %collective-permute-start = (bf16[512,1024]{1,0:T(8,128)(2,1)S(1)}, bf16[512,1024]{1,0:T(8,128)(2,1)S(1)}, u32[]{:S(2)}, u32[]{:S(2)}) collective-permute-start(bf16[512,1024]{1,0:T(8,128)(2,1)S(1)} %bitcast.71), channel_id=1, source_target_pairs={{0,1},{1,2},{2,3},{4,5},{5,6},{6,7},{8,9},{9,10},{10,11},{12,13},{... | collective-permute-start | bytes 3145736 | tf_op jit(solution)/shard_map/ppermute | solution.py:311
  75.3 25.1 %collective-permute-start.3 = (bf16[512,1024]{1,0:T(8,128)(2,1)S(1)}, bf16[512,1024]{1,0:T(8,128)(2,1)}, u32[]{:S(2)}, u32[]{:S(2)}) collective-permute-start(bf16[512,1024]{1,0:T(8,128)(2,1)S(1)} %bitcast.72), channel_id=1, source_target_pairs={{1,0},{2,1},{3,2},{5,4},{6,5},{7,6},{9,8},{10,9},{11,10},{13,12},{... | collective-permute-start | bytes 3145736 | tf_op jit(solution)/shard_map/ppermute | solution.py:312
  95.0 53.2 %collective-permute-start.1 = (bf16[512,1024]{1,0:T(8,128)(2,1)S(1)}, bf16[512,1024]{1,0:T(8,128)(2,1)}, u32[]{:S(2)}, u32[]{:S(2)}) collective-permute-start(bf16[512,1024]{1,0:T(8,128)(2,1)S(1)} %collective-permute-done), channel_id=1, source_target_pairs={{0,1},{1,2},{2,3},{4,5},{5,6},{6,7},{8,9},{9,10},{10,11},{12,13},{... | collective-permute-start | bytes 3145736 | tf_op jit(solution)/shard_map/ppermute | solution.py:311
  100.4 51.2 %collective-permute-start.4 = (bf16[512,1024]{1,0:T(8,128)(2,1)}, bf16[512,1024]{1,0:T(8,128)(2,1)}, u32[]{:S(2)}, u32[]{:S(2)}) collective-permute-start(bf16[512,1024]{1,0:T(8,128)(2,1)} %collective-permute-done.3), channel_id=1, source_target_pairs={{1,0},{2,1},{3,2},{5,4},{6,5},{7,6},{9,8},{10,9},{11,10},{13,12},{... | collective-permute-start | bytes 3145736 | tf_op jit(solution)/shard_map/ppermute | solution.py:312
  104.8 87.4 %all-to-all-start.1 = ((bf16[4,256,512]{2,1,0:T(8,128)(2,1)}), bf16[4,256,512]{2,1,0:T(8,128)(2,1)}, u32[]{:S(2)}, u32[]{:S(2)}) async-start(bf16[4,256,512]{2,1,0:T(8,128)(2,1)} %pad_maximum_fusion.7), calls=%async_computation.1 | async-start | bytes 2097152 | tf_op jit(solution)/shard_map/all_to_all | solution.py:359
  148.2 17.8 %collective-permute-start.2 = (bf16[512,1024]{1,0:T(8,128)(2,1)}, bf16[512,1024]{1,0:T(8,128)(2,1)}, u32[]{:S(2)}, u32[]{:S(2)}) collective-permute-start(bf16[512,1024]{1,0:T(8,128)(2,1)} %collective-permute-done.1), channel_id=1, source_target_pairs={{0,1},{1,2},{2,3},{4,5},{5,6},{6,7},{8,9},{9,10},{10,11},{12,13},{... | collective-permute-start | bytes 3145736 | tf_op jit(solution)/shard_map/ppermute | solution.py:311
  151.6 19.5 %collective-permute-start.5 = (bf16[512,1024]{1,0:T(8,128)(2,1)}, bf16[512,1024]{1,0:T(8,128)(2,1)}, u32[]{:S(2)}, u32[]{:S(2)}) collective-permute-start(bf16[512,1024]{1,0:T(8,128)(2,1)} %collective-permute-done.4), channel_id=1, source_target_pairs={{1,0},{2,1},{3,2},{5,4},{6,5},{7,6},{9,8},{10,9},{11,10},{13,12},{... | collective-permute-start | bytes 3145736 | tf_op jit(solution)/shard_map/ppermute | solution.py:312
  229.5 21.6 %all-to-all-start.2 = ((bf16[4,512,256]{1,2,0:T(8,128)(2,1)}), bf16[4,512,256]{1,2,0:T(8,128)(2,1)}, u32[]{:S(2)}, u32[]{:S(2)}) async-start(bf16[4,512,256]{1,2,0:T(8,128)(2,1)} %copy.80), calls=%async_computation.2 | async-start | bytes 2097152 | tf_op jit(solution)/shard_map/all_to_all | solution.py:375
  233.9 177.1 %reduce-scatter.15.cloned.1.call-start = ((), (), s32[]{:S(2)}) async-start(), calls=%async_computation.18 | async-start | bytes 6488064 | tf_op jit(solution)/shard_map/reduce_scatter | solution.py:423
  287.7 148.9 %reduce-scatter.11.cloned.1.call-start = ((), (), s32[]{:S(2)}) async-start(), calls=%async_computation.16 | async-start | bytes 12976128 | tf_op jit(solution)/shard_map/reduce_scatter | solution.py:423
  323.1 25.4 %all-to-all-start.3 = ((bf16[512,4,256]{2,0,1:T(8,128)(2,1)}), bf16[512,4,256]{2,0,1:T(8,128)(2,1)}, u32[]{:S(2)}, u32[]{:S(2)}) async-start(bf16[512,4,256]{2,0,1:T(8,128)(2,1)} %bitcast.73), calls=%async_computation.3 | async-start | bytes 2097152 | tf_op jit(solution)/shard_map/all_to_all | solution.py:404
  327.4 163.2 %reduce-scatter.19.cloned.1.call-start = ((), (), s32[]{:S(2)}) async-start(), calls=%async_computation.20 | async-start | bytes 4423680 | tf_op jit(solution)/shard_map/reduce_scatter | solution.py:430
  410.2 164.5 %reduce-scatter.9.cloned.1.call-start = ((), (), s32[]{:S(2)}) async-start(), calls=%async_computation.15 | async-start | bytes 5242880 | tf_op jit(solution)/shard_map/reduce_scatter | solution.py:415
  410.2 85.3 %copy-start.11 = (f32[512,1024]{1,0:T(8,128)S(1)}, f32[512,1024]{1,0:T(8,128)}, u32[]{:S(2)}) copy-start(f32[512,1024]{1,0:T(8,128)} %copy-done.10) | copy-start | bytes 6291460
  410.9 189.5 %reduce-scatter.17.cloned.1.call-start = ((), (), s32[]{:S(2)}) async-start(), calls=%async_computation.19 | async-start | bytes 901120 | tf_op jit(solution)/shard_map/reduce_scatter | solution.py:424
  411.7 223.4 %reduce-scatter.13.cloned.1.call-start = ((), (), s32[]{:S(2)}) async-start(), calls=%async_computation.17 | async-start | bytes 1802240 | tf_op jit(solution)/shard_map/reduce_scatter | solution.py:424
  490.6 32.1 %all-to-all-start.4 = ((bf16[4,32,1920]{2,1,0:T(8,128)(2,1)}), bf16[4,32,1920]{2,1,0:T(8,128)(2,1)}, u32[]{:S(2)}, u32[]{:S(2)}) async-start(bf16[4,32,1920]{2,1,0:T(8,128)(2,1)} %bitcast.75), calls=%async_computation.5 | async-start | bytes 983040 | tf_op jit(solution)/shard_map/all_to_all | solution.py:432
  503.3 71.3 %copy-start.6 = (bf16[1,512,1024]{2,1,0:T(8,128)(2,1)S(1)}, bf16[1,512,1024]{2,1,0:T(8,128)(2,1)}, u32[]{:S(2)}) copy-start(bf16[1,512,1024]{2,1,0:T(8,128)(2,1)} %param.15) | copy-start | bytes 3145732
  503.3 73.1 %copy-start.8 = (f32[512,1024]{1,0:T(8,128)S(1)}, f32[512,1024]{1,0:T(8,128)}, u32[]{:S(2)}) copy-start(f32[512,1024]{1,0:T(8,128)} %copy-done.7) | copy-start | bytes 6291460
  (17 other events, 208.5 us)
Sparse Core Ops, SparseCore 0:
  10.2 45.3 all-gather.6
  57.5 26.4 all-gather.4
  85.9 76.5 all-gather.8
  164.2 43.3 all-gather.10
  287.8 58.1 reduce-scatter.14
  349.8 86.7 reduce-scatter.10
  440.6 49.9 reduce-scatter.18
  492.9 81.7 reduce-scatter.8
  577.1 23.3 reduce-scatter.16
  602.7 32.3 reduce-scatter.12

commit v2 on v1

--- a/solution.py
+++ b/solution.py
@@ -35,11 +35,10 @@
     return jnp.concatenate([cosine, cosine], 1), jnp.concatenate([-sine, sine], 1)
 
 
-def qkv_kernel(heads, tok_ref, gain_ref, w_ref, cos_ref, sin_ref, qkv_ref, normed_ref):
+def qkv_kernel(heads, tok_ref, gain_ref, w_ref, cos_ref, sin_ref, qkv_ref):
     rows = tok_ref[...].astype(F32)
     factor = lax.rsqrt(jnp.mean(rows * rows, -1, keepdims=True) + EPSILON)
     normed = (rows * factor * gain_ref[...]).astype(BF16)
-    normed_ref[...] = normed
     cosine, sine = cos_ref[...], sin_ref[...]
     for part in range(3):
         for head in range(heads):
@@ -64,14 +63,8 @@
             pl.BlockSpec((block, HEAD_DIM), lambda i: (i, 0)),
             pl.BlockSpec((block, HEAD_DIM), lambda i: (i, 0)),
         ],
-        out_specs=[
-            pl.BlockSpec((block, columns), lambda i: (i, 0)),
-            pl.BlockSpec((block, width), lambda i: (i, 0)),
-        ],
-        out_shape=[
-            jax.ShapeDtypeStruct((length, columns), BF16),
-            jax.ShapeDtypeStruct((length, width), BF16),
-        ],
+        out_specs=pl.BlockSpec((block, columns), lambda i: (i, 0)),
+        out_shape=jax.ShapeDtypeStruct((length, columns), BF16),
         compiler_params=pltpu.CompilerParams(vmem_limit_bytes=48 * MIB),
         cost_estimate=pl.CostEstimate(
             flops=2 * length * width * columns, bytes_accessed=4 * length * (width + columns), transcendentals=0
@@ -182,7 +175,7 @@
 
 def backward_kernel(
     heads, top, blocks, chosen_ref, counts_ref, q_ref, k_ref, v_ref, mk_ref, mv_ref, go_ref, out_ref, lse_ref,
-    cos_ref, sin_ref, grad_ref, gk_ref, gv_ref,
+    cos_ref, sin_ref, tok_ref, gain_ref, w_ref, partial_ref, grad_w_ref, gain_grad_ref, gk_ref, gv_ref, grad_s, gw_s,
 ):
     block = blocks - 1 - pl.program_id(0)
     base = block * top
@@ -197,6 +190,8 @@
     def _():
         gk_ref[...] = jnp.zeros_like(gk_ref)
         gv_ref[...] = jnp.zeros_like(gv_ref)
+        gw_s[...] = jnp.zeros_like(gw_s)
+        gain_grad_ref[...] = jnp.zeros_like(gain_grad_ref)
 
     def spread(column):
         return jnp.transpose(jnp.broadcast_to(column, (QBLK, HEAD_DIM)))[:1]
@@ -257,14 +252,30 @@
     for head in range(heads):
         columns = slice(head * HEAD_DIM, (head + 1) * HEAD_DIM)
         at = head * HEAD_DIM
-        grad_ref[:, at : at + HEAD_DIM] = unturn(totals[head] * SCALE).astype(BF16)
+        grad_s[:, at : at + HEAD_DIM] = unturn(totals[head] * SCALE).astype(BF16)
         grad_key = gk_ref[own, columns] * SCALE
-        grad_ref[:, wide + at : wide + at + HEAD_DIM] = unturn(grad_key).astype(BF16)
-        grad_ref[:, 2 * wide + at : 2 * wide + at + HEAD_DIM] = gv_ref[own, columns].astype(BF16)
-
-
-def attend_backward(chosen, counts, qkv, memory, grad_out, out, lse, cosine, sine, heads, top):
+        grad_s[:, wide + at : wide + at + HEAD_DIM] = unturn(grad_key).astype(BF16)
+        grad_s[:, 2 * wide + at : 2 * wide + at + HEAD_DIM] = gv_ref[own, columns].astype(BF16)
+
+    rows = tok_ref[...].astype(F32)
+    rows = rows * lax.rsqrt(jnp.mean(rows * rows, -1, keepdims=True) + EPSILON)
+    normed = (rows * gain_ref[...]).astype(BF16)
+    grad = grad_s[...]
+    partial = dot(grad, w_ref[...], NT)
+    partial_ref[...] = partial.astype(BF16)
+    gain_grad_ref[...] += jnp.sum(partial * rows, 0, keepdims=True)
+    gw_s[...] += dot(normed, grad, TN)
+
+    @pl.when(block == 0)
+    def _():
+        grad_w_ref[...] = gw_s[...].astype(BF16)
+
+
+def attend_backward(
+    chosen, counts, qkv, memory, grad_out, out, lse, cosine, sine, tokens_all, gain, w_qkv, heads, top
+):
     length = qkv.shape[0]
+    width = tokens_all.shape[1]
     wide = heads * HEAD_DIM
     blocks = length // QBLK
     mem_rows = memory.shape[0]
@@ -285,11 +296,27 @@
                 pl.BlockSpec((QBLK, heads), lambda i, *_: (last - i, 0)),
                 pl.BlockSpec((QBLK, HEAD_DIM), lambda i, *_: (last - i, 0)),
                 pl.BlockSpec((QBLK, HEAD_DIM), lambda i, *_: (last - i, 0)),
+                pl.BlockSpec((QBLK, width), lambda i, *_: (last - i, 0)),
+                pl.BlockSpec((1, width), lambda i, *_: (0, 0)),
+                pl.BlockSpec((width, 3 * wide), lambda i, *_: (0, 0)),
             ],
-            out_specs=pl.BlockSpec((QBLK, 3 * wide), lambda i, *_: (last - i, 0)),
-            scratch_shapes=[pltpu.VMEM((length, wide), F32), pltpu.VMEM((length, wide), F32)],
+            out_specs=[
+                pl.BlockSpec((QBLK, width), lambda i, *_: (last - i, 0)),
+                pl.BlockSpec((width, 3 * wide), lambda i, *_: (0, 0)),
+                pl.BlockSpec((1, width), lambda i, *_: (0, 0)),
+            ],
+            scratch_shapes=[
+                pltpu.VMEM((length, wide), F32),
+                pltpu.VMEM((length, wide), F32),
+                pltpu.VMEM((QBLK, 3 * wide), BF16),
+                pltpu.VMEM((width, 3 * wide), F32),
+            ],
         ),
-        out_shape=jax.ShapeDtypeStruct((length, 3 * wide), BF16),
+        out_shape=[
+            jax.ShapeDtypeStruct((length, width), BF16),
+            jax.ShapeDtypeStruct((width, 3 * wide), BF16),
+            jax.ShapeDtypeStruct((1, width), F32),
+        ],
         compiler_params=pltpu.CompilerParams(vmem_limit_bytes=48 * MIB),
         cost_estimate=pl.CostEstimate(
             flops=10 * heads * length * HEAD_DIM * (length // 2 + top * MBLK),
@@ -297,19 +324,194 @@
             transcendentals=heads * length * (length // 2 + top * MBLK),
         ),
         name="attend_backward",
-    )(chosen, counts, qkv, qkv, qkv, memory, memory, grad_out, out, lse, cosine, sine)
+    )(
+        chosen, counts, qkv, qkv, qkv, memory, memory, grad_out, out, lse, cosine, sine, tokens_all, gain, w_qkv
+    )
+
+
+def ffn_kernel(
+    span, merged, tok_ref, att_ref, cot_ref, gain_ref, out_w, gate_w, up_w, down_w,
+    mixed_ref, grad_mid_ref, grad_att_ref, gain_grad_ref, grads_ref, *rest,
+):
+    if not merged:
+        down_grads_ref, rest = rest[0], rest[1:]
+    middle_s, normed_s, turned_s, mixed_s, upstream_s, gate_s, up_s, down_s, out_s, sems, late_sems = rest
+    step, steps = pl.program_id(0), pl.num_programs(0)
+    width = tok_ref.shape[1]
+    share = width // span
+    wide = gate_w.shape[1]
+    hidden_width = down_s.shape[0]
+    tall = hidden_width // span
+    lanes = width // wide
+    first = tall * lanes if merged else 0
+    slot = step % 2
+
+    @pl.when(step == 0)
+    def _():
+        middle = tok_ref[...].astype(F32) + dot(att_ref[...], out_w[...])
+        middle_s[...] = middle
+        factor = lax.rsqrt(jnp.mean(middle * middle, -1, keepdims=True) + EPSILON)
+        normed = (middle * factor * gain_ref[...]).astype(BF16)
+        normed_s[...] = normed
+        turned_s[...] = jnp.transpose(normed)
+        mixed_s[...] = middle
+        upstream_s[...] = jnp.zeros_like(upstream_s)
+
+    def copy_out(kind, which, index):
+        source = (gate_s, up_s)[kind].at[which]
+        start = first + (lanes + kind * steps + index) * share
+        target = grads_ref.at[:, pl.ds(start, share), :]
+        return pltpu.make_async_copy(source, target, sems.at[kind, which])
+
+    normed = normed_s[...]
+    upstream = cot_ref[...]
+    gate_act = dot(normed, gate_w[...])
+    up_act = dot(normed, up_w[...])
+    grad_hidden = dot(upstream, down_w[...], NT)
+    sigmoid = jax.nn.sigmoid(gate_act)
+    silu = gate_act * sigmoid
+    hidden = (silu * up_act).astype(BF16)
+    grad_gate = (grad_hidden * up_act * sigmoid * (1.0 + gate_act * (1.0 - sigmoid))).astype(BF16)
+    grad_up = (grad_hidden * silu).astype(BF16)
+    mixed_s[...] += dot(hidden, down_w[...])
+    upstream_s[...] += dot(grad_gate, gate_w[...], NT) + dot(grad_up, up_w[...], NT)
+    down_s[pl.ds(pl.multiple_of(step * wide, wide), wide), :] = dot(hidden, upstream, TN).astype(BF16)
+
+    @pl.when(step >= 2)
+    def _():
+        copy_out(0, slot, step - 2).wait()
+        copy_out(1, slot, step - 2).wait()
+
+    turned = turned_s[...]
+    gate_s[slot] = dot(turned, grad_gate).astype(BF16).reshape(span, share, wide)
+    up_s[slot] = dot(turned, grad_up).astype(BF16).reshape(span, share, wide)
+    copy_out(0, slot, step).start()
+    copy_out(1, slot, step).start()
+
+    @pl.when(step == steps - 1)
+    def _():
+        copies = []
+        if merged:
+            for place in range(span):
+                for lane in range(lanes):
+                    copies.append(
+                        pltpu.make_async_copy(
+                            down_s.at[pl.ds(place * tall, tall), pl.ds(lane * wide, wide)],
+                            grads_ref.at[place, pl.ds(lane * tall, tall), :],
+                            late_sems.at[len(copies)],
+                        )
+                    )
+        else:
+            copies.append(pltpu.make_async_copy(down_s, down_grads_ref, late_sems.at[0]))
+        for copy in copies:
+            copy.start()
+        mixed_ref[...] = mixed_s[...].astype(BF16)
+        middle = middle_s[...]
+        grad = upstream_s[...]
+        factor = lax.rsqrt(jnp.mean(middle * middle, -1, keepdims=True) + EPSILON)
+        gain_grad_ref[...] = jnp.sum(grad * middle * factor, 0, keepdims=True)
+        scaled = grad * gain_ref[...]
+        inner = jnp.mean(scaled * middle, -1, keepdims=True)
+        grad_middle = cot_ref[...].astype(F32) + factor * scaled - middle * (factor * factor * factor * inner)
+        grad_mid_ref[...] = grad_middle
+        branch = grad_middle.astype(BF16)
+        grad_att_ref[...] = dot(branch, out_w[...], NT).astype(BF16)
+        turned_att = jnp.transpose(att_ref[...])
+        for lane in range(lanes):
+            columns = slice(lane * wide, (lane + 1) * wide)
+            out_s[lane] = dot(turned_att, branch[:, columns]).astype(BF16).reshape(span, share, wide)
+            more = pltpu.make_async_copy(
+                out_s.at[lane],
+                grads_ref.at[:, pl.ds(first + lane * share, share), :],
+                late_sems.at[len(copies)],
+            )
+            more.start()
+            copies.append(more)
+        for copy in copies:
+            copy.wait()
+        copy_out(0, 1 - slot, step - 1).wait()
+        copy_out(1, 1 - slot, step - 1).wait()
+        copy_out(0, slot, step).wait()
+        copy_out(1, slot, step).wait()
+
+
+def feed_forward(tokens, attended, upstream, gain, weights, w_down, span):
+    rows, width = tokens.shape
+    hidden_width = w_down.shape[0]
+    wide = 2 * HEAD_DIM
+    steps = hidden_width // wide
+    lanes = width // wide
+    share = width // span
+    tall = hidden_width // span
+    merged = tall % 16 == 0
+    total = (lanes + 2 * steps) * share + (lanes * tall if merged else 0)
+    shapes = [
+        jax.ShapeDtypeStruct((rows, width), BF16),
+        jax.ShapeDtypeStruct((rows, width), F32),
+        jax.ShapeDtypeStruct((rows, width), BF16),
+        jax.ShapeDtypeStruct((1, width), F32),
+        jax.ShapeDtypeStruct((span, total, wide), BF16),
+    ]
+    specs = [
+        pl.BlockSpec((rows, width), lambda i: (0, 0)),
+        pl.BlockSpec((rows, width), lambda i: (0, 0)),
+        pl.BlockSpec((rows, width), lambda i: (0, 0)),
+        pl.BlockSpec((1, width), lambda i: (0, 0)),
+        pl.BlockSpec(memory_space=pl.ANY),
+    ]
+    if not merged:
+        shapes.append(jax.ShapeDtypeStruct((hidden_width, width), BF16))
+        specs.append(pl.BlockSpec(memory_space=pl.ANY))
+    return pl.pallas_call(
+        functools.partial(ffn_kernel, span, merged),
+        grid=(steps,),
+        in_specs=[
+            pl.BlockSpec((rows, width), lambda i: (0, 0)),
+            pl.BlockSpec((rows, width), lambda i: (0, 0)),
+            pl.BlockSpec((rows, width), lambda i: (0, 0)),
+            pl.BlockSpec((1, width), lambda i: (0, 0)),
+            pl.BlockSpec((width, width), lambda i: (0, 0)),
+            pl.BlockSpec((width, wide), lambda i: (0, lanes + i)),
+            pl.BlockSpec((width, wide), lambda i: (0, lanes + steps + i)),
+            pl.BlockSpec((wide, width), lambda i: (i, 0)),
+        ],
+        out_specs=specs,
+        out_shape=shapes,
+        scratch_shapes=[
+            pltpu.VMEM((rows, width), F32),
+            pltpu.VMEM((rows, width), BF16),
+            pltpu.VMEM((width, rows), BF16),
+            pltpu.VMEM((rows, width), F32),
+            pltpu.VMEM((rows, width), F32),
+            pltpu.VMEM((2, span, share, wide), BF16),
+            pltpu.VMEM((2, span, share, wide), BF16),
+            pltpu.VMEM((hidden_width, width), BF16),
+            pltpu.VMEM((lanes, span, share, wide), BF16),
+            pltpu.SemaphoreType.DMA((2, 2)),
+            pltpu.SemaphoreType.DMA(((span * lanes if merged else 1) + lanes,)),
+        ],
+        compiler_params=pltpu.CompilerParams(vmem_limit_bytes=56 * MIB),
+        cost_estimate=pl.CostEstimate(
+            flops=6 * rows * width * (3 * hidden_width + width),
+            bytes_accessed=4 * width * (3 * hidden_width + width),
+            transcendentals=rows * hidden_width,
+        ),
+        name="feed_forward",
+    )(tokens, attended, upstream, gain, weights, weights, weights, w_down)
+
+
+def after(value, earlier):
+    return lax.optimization_barrier((value, earlier))[0]
 
 
 def chain_gather(block, axis):
     size = lax.axis_size(axis)
     place = lax.axis_index(axis)
-    up = [(i, i + 1) for i in range(size - 1)]
-    down = [(i + 1, i) for i in range(size - 1)]
     from_below, from_above = [], []
     rising = falling = block
-    for _ in range(size - 1):
-        rising = lax.ppermute(rising, axis, up)
-        falling = lax.ppermute(falling, axis, down)
+    for step in range(size - 1):
+        rising = lax.ppermute(rising, axis, [(i, i + 1) for i in range(step, size - 1)])
+        falling = lax.ppermute(falling, axis, [(i + 1, i) for i in range(size - 1 - step)])
         from_below.append(rising)
         from_above.append(falling)
     ordered = []
@@ -323,7 +525,27 @@
             else:
                 cases.append(from_above[index - mine - 1])
         ordered.append(lax.select_n(place, *cases) if size > 2 else lax.select_n(place > 0, *cases))
-    return ordered
+    return ordered, list(zip(from_below, from_above))
+
+
+def chain_scatter(partial, axis):
+    size = lax.axis_size(axis)
+    place = lax.axis_index(axis)
+    rows = partial.shape[0] // size
+
+    def block(index):
+        return lax.dynamic_slice_in_dim(partial, jnp.clip(index, 0, size - 1) * rows, rows, 0).astype(F32)
+
+    rising = falling = None
+    for step in range(size - 1):
+        up, down = block(size - 1 - step + place), block(step - size + 1 + place)
+        if step:
+            up, down = up + rising.astype(F32), down + falling.astype(F32)
+        rising = lax.ppermute(up.astype(BF16), axis, [(i, i + 1) for i in range(step + 1)])
+        falling = lax.ppermute(
+            down.astype(BF16), axis, [(i, i - 1) for i in range(size - 1 - step, size)]
+        )
+    return block(place) + rising.astype(F32) + falling.astype(F32)
 
 
 def body(
@@ -342,109 +564,100 @@
 
     extra = 8 if share % 8 == 0 else 8 - share % 8
     parts = [w.reshape(share, ring, wide).transpose(1, 0, 2) for w in (w_query, w_key, w_value)]
-    gains = jnp.pad(jnp.concatenate([gain_attn, gain_ffn]), (0, 3 * wide - 2 * share))
-    gains = jnp.broadcast_to(gains, (ring, extra, 3 * wide))
-    parcel = jnp.concatenate([jnp.concatenate(parts, 2), gains], 1)
+    choices = jnp.concatenate([chosen[0].reshape(-1), counts[0].reshape(-1)]).astype(BF16)
+    notes = jnp.stack(
+        [
+            jnp.pad(row, (0, 3 * wide - row.shape[0]))
+            for row in (jnp.concatenate([gain_attn, gain_ffn]), choices)
+        ]
+    )
+    notes = jnp.broadcast_to(jnp.pad(notes, ((0, extra - 2), (0, 0))), (ring, extra, 3 * wide))
+    parcel = jnp.concatenate([jnp.concatenate(parts, 2), notes], 1)
     parcel = lax.all_to_all(parcel, "fsdp", 0, 0, tiled=True)
+    picks = parcel[:, share + 1, : choices.shape[0]].astype(jnp.int32).reshape(ring, 2, -1)
+    chosen_all, counts_all = picks[:, 0].reshape(-1), picks[:, 1].reshape(-1)
+    shards = jnp.concatenate([w_out, w_gate, w_up], 1)
+    near, steps = chain_gather(shards, "fsdp")
+    near_down, down_steps = chain_gather(after(w_down, steps[0]), "fsdp")
+    gathered, token_steps = chain_gather(after(mine, down_steps[-2]), "fsdp")
     parcel = lax.all_gather(parcel, "dp", axis=0, tiled=True)
     w_qkv = parcel[:, :share].reshape(width, 3 * wide)
     gain_one = parcel[:, share, :share].reshape(1, width).astype(F32)
     gain_two = parcel[:, share, share : 2 * share].reshape(1, width).astype(F32)
-
-    picks = lax.all_gather(jnp.stack([chosen[0], counts[0]]), "fsdp", axis=1, tiled=True)
-    chosen_all, counts_all = picks[0].reshape(-1), picks[1].reshape(-1)
+    first = lax.all_gather(after(jnp.concatenate(near, 0), w_qkv), "dp", axis=0, tiled=True)
+    gathered = jnp.concatenate(gathered, 0)
+
     memory = jnp.concatenate(
         [m[0].reshape(-1, ring, wide).transpose(1, 0, 2) for m in (memory_keys, memory_values)], 2
     )
-    memory = lax.all_to_all(memory, "fsdp", 0, 0, tiled=True).reshape(-1, 2 * wide)
-
-    gathered = jnp.concatenate(chain_gather(mine, "fsdp"), 0)
-
-    def whole(shard):
-        near = lax.all_gather(shard, "fsdp", axis=0, tiled=True)
-        return lax.all_gather(near, "dp", axis=0, tiled=True)
-
-    first = whole(jnp.concatenate([w_gate, w_up, w_out], 1))
-    down_full = whole(w_down)
-    gate_up = first[:, : 2 * hidden_width]
-    out_full = first[:, 2 * hidden_width :]
+    memory = lax.all_to_all(after(memory, token_steps[-2]), "fsdp", 0, 0, tiled=True).reshape(-1, 2 * wide)
+    down_full = lax.all_gather(after(jnp.concatenate(near_down, 0), first), "dp", axis=0, tiled=True)
 
     cosine, sine = rotary_tables(length)
-    qkv, normed = project_qkv(gathered, gain_one, w_qkv, cosine, sine, heads)
+    qkv = project_qkv(gathered, gain_one, w_qkv, cosine, sine, heads)
     attended_heads, lse = attend_forward(chosen_all, counts_all, qkv, memory, heads, top)
     attended = lax.all_to_all(attended_heads, "fsdp", 0, 1, tiled=True)
 
-    middle = mine.astype(F32) + dot(attended, out_full)
-    factor = lax.rsqrt(jnp.mean(middle * middle, -1, keepdims=True) + EPSILON)
-    normed_two = (middle * factor * gain_two).astype(BF16)
-    acts = dot(normed_two, gate_up)
-    gate_act, up_act = acts[:, :hidden_width], acts[:, hidden_width:]
-    sigmoid = jax.nn.sigmoid(gate_act)
-    hidden = (gate_act * sigmoid * up_act).astype(BF16)
-    mixed = (middle + dot(hidden, down_full)).astype(BF16)
-
     upstream = cotangent[0]
-    grad_down = dot(hidden, upstream, TN).astype(BF16)
-    grad_hidden = dot(upstream, down_full, NT)
-    grad_gate = grad_hidden * up_act * sigmoid * (1.0 + gate_act * (1.0 - sigmoid))
-    grad_up = grad_hidden * gate_act * sigmoid
-    grad_acts = jnp.concatenate([grad_gate.astype(BF16), grad_up.astype(BF16)], 1)
-    grad_gate_up = dot(normed_two, grad_acts, TN).astype(BF16)
-    grad_normed_two = dot(grad_acts, gate_up, NT)
-
-    def norm_back(values, factor, gain, grad):
-        scaled = grad * gain
-        inner = jnp.mean(scaled * values, -1, keepdims=True)
-        return factor * scaled - values * factor**3 * inner
-
-    gain_two_grad = jnp.sum(grad_normed_two * middle * factor, 0)
-    grad_middle = upstream.astype(F32) + norm_back(middle, factor, gain_two, grad_normed_two)
-    grad_branch = grad_middle.astype(BF16)
-    grad_attended = dot(grad_branch, out_full, NT).astype(BF16)
+    mixed, grad_middle, grad_attended, gain_two_grad, grads, *grad_down = feed_forward(
+        mine, attended, upstream, gain_two, first, down_full, span
+    )
     grad_heads = lax.all_to_all(grad_attended, "fsdp", 1, 0, tiled=True)
-    grad_out = dot(attended, grad_branch, TN).astype(BF16)
-
-    grad_qkv = attend_backward(
-        chosen_all, counts_all, qkv, memory, grad_heads, attended_heads, lse, cosine, sine, heads, top
+    grads = lax.psum_scatter(grads, "dp", scatter_dimension=0, tiled=True)[0]
+
+    partial, grad_w_qkv, gain_one_grad = attend_backward(
+        chosen_all, counts_all, qkv, memory, grad_heads, attended_heads, lse, cosine, sine, gathered, gain_one,
+        w_qkv, heads, top,
     )
-    grad_w_qkv = dot(normed, grad_qkv, TN).astype(BF16)
-    partial = dot(grad_qkv, w_qkv, NT)
-    tokens_f32 = gathered.astype(F32)
-    factor_all = lax.rsqrt(jnp.mean(tokens_f32 * tokens_f32, -1, keepdims=True) + EPSILON)
-    gain_one_grad = jnp.sum(partial * tokens_f32 * factor_all, 0)
-    grad_normed = lax.psum_scatter(
-        partial.astype(BF16), "fsdp", scatter_dimension=0, tiled=True
-    ).astype(F32)
+    grad_normed = chain_scatter(partial, "fsdp")
     own = mine.astype(F32)
-    own_factor = lax.rsqrt(jnp.mean(own * own, -1, keepdims=True) + EPSILON)
-    tokens_grad = (grad_middle + norm_back(own, own_factor, gain_one, grad_normed)).astype(BF16)
-
-    def reduced(grad):
-        near = lax.psum_scatter(grad, "dp", scatter_dimension=0, tiled=True)
-        return lax.psum_scatter(near, "fsdp", scatter_dimension=0, tiled=True).astype(F32)
-
-    down_share = reduced(grad_down)
-    gate_up_share = reduced(grad_gate_up)
-    gain_columns = jnp.pad(jnp.stack([gain_one_grad, gain_two_grad], 1), ((0, 0), (0, HEAD_DIM - 2)))
-    late = jnp.concatenate([grad_w_qkv, grad_out, gain_columns.astype(BF16)], 1)
-    late = lax.psum_scatter(late, "dp", scatter_dimension=0, tiled=True)
-    late = late.reshape(ring, share, late.shape[1])
+    factor = lax.rsqrt(jnp.mean(own * own, -1, keepdims=True) + EPSILON)
+    scaled = grad_normed * gain_one
+    inner = jnp.mean(scaled * own, -1, keepdims=True)
+    tokens_grad = (grad_middle + factor * scaled - own * (factor * factor * factor * inner)).astype(BF16)
+
+    def along_z(pieces):
+        return jnp.sum(lax.all_to_all(pieces, "fsdp", 0, 0, tiled=True).astype(F32), 0)
+
+    gains = jnp.concatenate([gain_one_grad, gain_two_grad], 0).reshape(2, span, -1).transpose(1, 0, 2)
+    gains = jnp.pad(gains.astype(BF16), ((0, 0), (0, extra - 2), (0, 3 * wide - gains.shape[2])))
+    late = jnp.concatenate([grad_w_qkv.reshape(span, -1, 3 * wide), gains], 1)
+    late = jnp.sum(lax.all_to_all(late, "dp", 0, 0, tiled=True).astype(F32), 0).astype(BF16)
+    gains = late[-extra : 2 - extra, : ring * share].reshape(2, ring, share).transpose(1, 0, 2)
+    gains = jnp.pad(gains, ((0, 0), (0, extra - 2), (0, 3 * wide - share)))
+    late = jnp.concatenate([late[:-extra].reshape(ring, share, 3 * wide), gains], 1)
     late = lax.all_to_all(late, "fsdp", 0, 0, tiled=True).astype(F32)
     projections = [
-        late[:, :, part * wide : (part + 1) * wide].transpose(1, 0, 2).reshape(share, width) for part in range(3)
+        late[:, :share, part * wide : (part + 1) * wide].transpose(1, 0, 2).reshape(share, width)
+        for part in range(3)
     ]
-    out_share = jnp.sum(late[:, :, 3 * wide : 3 * wide + width], 0)
-    gain_shares = jnp.sum(late[:, :, 3 * wide + width :], 0)
+    gain_shares = jnp.sum(late[:, share : share + 2, :share], 0)
+
+    strip = grads.shape[1]
+    lanes = width // strip
+    tall = w_down.shape[0]
+    if grad_down:
+        down = lax.psum_scatter(grad_down[0], "dp", scatter_dimension=0, tiled=True)
+        down = down.reshape(ring, tall, lanes, strip).transpose(0, 2, 1, 3)
+    else:
+        down = grads[: ring * tall * lanes].reshape(lanes, ring, tall, strip).transpose(1, 0, 2, 3)
+        grads = grads[ring * tall * lanes :]
+    grads = grads.reshape(-1, ring, share, strip).transpose(1, 0, 2, 3)
+    pieces = along_z(
+        jnp.concatenate([down.reshape(ring, -1, strip), grads.reshape(ring, -1, strip)], 1)
+    )
+    down_share = pieces[: lanes * tall].reshape(lanes, tall, strip).transpose(1, 0, 2).reshape(tall, width)
+    others = pieces[lanes * tall :].reshape(-1, share, strip).transpose(1, 0, 2).reshape(share, -1)
     return (
         mixed[None],
         tokens_grad[None],
         *projections,
-        out_share,
-        gate_up_share[:, :hidden_width],
-        gate_up_share[:, hidden_width:],
+        others[:, :width],
+        others[:, width : width + hidden_width],
+        others[:, width + hidden_width :],
         down_share,
-        gain_shares[:, 0],
-        gain_shares[:, 1],
+        gain_shares[0],
+        gain_shares[1],
     )
 
 

time: 654 us -> 631 us (0.965); the launches traced: 644 us -> 629 us
  matrix products: 87 us -> 0 us
  blocking collectives: 76.7 us -> 0 us
  starting transfers between devices: 34.1 us -> 93.1 us
  Pallas kernels: 84 us -> 138 us
  waiting for transfers between devices: 287 us -> 316 us
  other arithmetic: 29.9 us -> 41.1 us
    ppermute x6 -> x24, waiting for transfers between devices: 31.2 us -> 188 us  [the longest x9 96.7 us: chain_gather(): lax.ppermute(falling, axis, [(i + 1, i) for i in range(size - 1 - step)])]
    reduce_scatter x6 -> x1, waiting for transfers between devices: 179 us -> 27.7 us  [body(): grads = lax.psum_scatter(grads, 'dp', scatter_dimension=0, tiled=True)[0]]
    dot_general x11 -> x0, matrix products: 87 us -> none  [dot(): return lax.dot_general(left, right, dims, preferred_element_type=F32)]
    all_gather x2 -> x0, blocking collectives: 56 us -> none  [the longest x1 37.9 us: body(): lax.all_gather(jnp.stack([chosen[0], counts[0]]), 'fsdp', axis=1, tiled=T...]
    pallas_call x0 -> x1, Pallas kernels: none -> 43.8 us  [feed_forward(): pl.pallas_call(functools.partial(ffn_kernel, span, merged), grid=(steps,)...]
    ppermute x6 -> x24, starting transfers between devices: 14 us -> 49.6 us  [the longest x9 20.7 us: chain_gather(): lax.ppermute(rising, axis, [(i, i + 1) for i in range(step, size - 1)])]
    all_gather x3 -> x2, waiting for transfers between devices: 21.9 us -> 54.6 us  [the longest x1 54.6 us: body(): lax.all_gather(after(jnp.concatenate(near, 0), w_qkv), 'dp', axis=0, tile...]
    all_to_all x1 -> x0, blocking collectives: 20.8 us -> none  [body(): parcel = lax.all_to_all(parcel, 'fsdp', 0, 0, tiled=True)]
  transfers between devices with their start and end apart: 20 -> 35, of which waited for: 12 -> 19; matrix products, arithmetic and copies ran while one was open for 18% -> 8% of each run, Pallas kernels for 13% -> 15%
where the time goes in v2:
time: 631 us; the launch traced here: 629 us
  waiting for transfers between devices  316 us (50%)
  Pallas kernels  138 us (22%)
  starting transfers between devices  93.1 us (15%)
  other arithmetic  41.1 us (7%)
  local copies, waits for them, and re-layouts  26.8 us (4%)
  between operations  14.3 us (2%)
    ppermute x9, waiting for transfers between devices, chain_gather(): lax.ppermute(falling, axis, [(i + 1, i) for i in range(size - 1 - step)])  96.7 us
    all_gather x1, waiting for transfers between devices, body(): lax.all_gather(after(jnp.concatenate(near, 0), w_qkv), 'dp', axis=0, tile...  54.6 us
    pallas_call x1, Pallas kernels, attend_backward(): pl.pallas_call(functools.partial(backward_kernel, heads, top, blocks), gr...  49.5 us
    ppermute x3, waiting for transfers between devices, chain_scatter(): lax.ppermute(up.astype(BF16), axis, [(i, i + 1) for i in range(step + 1)])  47 us
    ppermute x3, waiting for transfers between devices, chain_scatter(): lax.ppermute(down.astype(BF16), axis, [(i, i - 1) for i in range(size - 1...  44.1 us
    pallas_call x1, Pallas kernels, feed_forward(): pl.pallas_call(functools.partial(ffn_kernel, span, merged), grid=(steps,)...  43.8 us
    pallas_call x1, Pallas kernels, attend_forward(): pl.pallas_call(functools.partial(forward_kernel, heads, top), grid_spec=p...  33.7 us
    reduce_scatter x1, waiting for transfers between devices, body(): grads = lax.psum_scatter(grads, 'dp', scatter_dimension=0, tiled=True)[0]  27.7 us
  transfers between devices with their start and end apart: 35, of which 19 were waited for; matrix products, arithmetic and copies ran while one was open for 8% of the time, Pallas kernels for 15%

profile of v2, /device:TPU:0, one launch (start us, length us, event | category | flops | bytes accessed | tf_op | source)
XLA Modules:
  0.0 628.8 jit_solution(9275903014983050914)
XLA Ops:
  13.1 6.3 %all-to-all-start = ((bf16[4,40,768]{2,1,0:T(8,128)(2,1)}), bf16[4,40,768]{2,1,0:T(8,128)(2,1)S(1)}, u32[]{:S(2)}, u32[]{:S(2)}) async-start(bf16[4,40,768]{2,1,0:T(8,128)(2,1)} %copy.68), calls=%async_computation | async-start | bytes 491520 | tf_op jit(solution)/shard_map/all_to_all | solution.py:576
  29.8 5.8 collective-permute-done.1
  37.6 11.3 %collective-permute-done.14 = bf16[32,6656]{1,0:T(8,128)(2,1)S(1)} collective-permute-done((bf16[32,6656]{1,0:T(8,128)(2,1)S(1)}, bf16[32,6656]{1,0:T(8,128)(2,1)S(1)}, u32[]{:S(2)}, u32[]{:S(2)}) %collective-permute-start.14) | collective-permute-done | bytes 426016 | tf_op jit(solution)/shard_map/ppermute | solution.py:514
  51.0 10.3 %collective-permute-done.15 = bf16[32,6656]{1,0:T(8,128)(2,1)S(1)} collective-permute-done((bf16[32,6656]{1,0:T(8,128)(2,1)S(1)}, bf16[32,6656]{1,0:T(8,128)(2,1)S(1)}, u32[]{:S(2)}, u32[]{:S(2)}) %collective-permute-start.15) | collective-permute-done | bytes 426016 | tf_op jit(solution)/shard_map/ppermute | solution.py:514
  74.3 5.2 collective-permute-done.5
  81.5 5.4 collective-permute-done.17
  87.9 54.6 %all-gather.6.cloned.1.call-done.out_w.gate_w.up_w = bf16[1024,6656]{1,0:T(8,128)(2,1)} async-done(((bf16[128,6656]{1,0:T(8,128)(2,1)}), bf16[1024,6656]{1,0:T(8,128)(2,1)}) %all-gather.6.cloned.1.call-update) | async-done | bytes 13631504 | tf_op jit(solution)/shard_map/all_gather | solution.py:587
  143.8 5.6 collective-permute-start.6
  149.4 20.4 %collective-permute-done.9 = bf16[512,1024]{1,0:T(8,128)(2,1)} collective-permute-done((bf16[512,1024]{1,0:T(8,128)(2,1)S(1)}, bf16[512,1024]{1,0:T(8,128)(2,1)}, u32[]{:S(2)}, u32[]{:S(2)}) %collective-permute-start.9) | collective-permute-done | bytes 1048608 | tf_op jit(solution)/shard_map/ppermute | solution.py:514
  175.8 20.7 %collective-permute-done.10 = bf16[512,1024]{1,0:T(8,128)(2,1)} collective-permute-done((bf16[512,1024]{1,0:T(8,128)(2,1)}, bf16[512,1024]{1,0:T(8,128)(2,1)}, u32[]{:S(2)}, u32[]{:S(2)}) %collective-permute-start.10) | collective-permute-done | bytes 1048608 | tf_op jit(solution)/shard_map/ppermute | solution.py:514
  205.6 7.9 %all-to-all-start.1 = ((bf16[4,256,512]{2,1,0:T(8,128)(2,1)}), bf16[4,256,512]{2,1,0:T(8,128)(2,1)}, u32[]{:S(2)}, u32[]{:S(2)}) async-start(bf16[4,256,512]{2,1,0:T(8,128)(2,1)} %pad_maximum_fusion.5), calls=%async_computation.1 | async-start | bytes 2097152 | tf_op jit(solution)/shard_map/all_to_all | solution.py:593
  214.9 15.9 %collective-permute-done.11 = bf16[512,1024]{1,0:T(8,128)(2,1)} collective-permute-done((bf16[512,1024]{1,0:T(8,128)(2,1)}, bf16[512,1024]{1,0:T(8,128)(2,1)}, u32[]{:S(2)}, u32[]{:S(2)}) %collective-permute-start.11) | collective-permute-done | bytes 1048608 | tf_op jit(solution)/shard_map/ppermute | solution.py:514
  236.1 10.9 %project_qkv.1.q_ref.k_ref.v_ref = bf16[2048,768]{1,0:T(8,128)(2,1)} custom-call(bf16[2048,1024]{1,0:T(8,128)(2,1)} %pad_maximum_fusion.tok_ref, f32[1,1024]{1,0:T(1,128)S(1)} %reshape.176.gain_ref, bf16[1024,768]{1,0:T(8,128)(2,1)S(1)} %bitcast.76, f32[2048,128]{1,0:T(8,128)S(1)} %get-tuple-element.75.cos_ref, f32[2048,128]{1,0:T(8,128)S(1)} %copy-done.1), custom_call_target="tpu_custom_call" | custom-call | flops 3221225472 | bytes 14680064 | tf_op jit(solution)/shard_map/project_qkv/pallas_call | solution.py:56
  247.0 33.7 %attend_forward.1 = (bf16[2048,256]{1,0:T(8,128)(2,1)}, f32[2048,2]{1,0:T(8,128)S(1)}) custom-call(s32[32]{0:T(128)S(1)} %reshape_squeeze.24.chosen_ref, s32[32]{0:T(128)S(1)} %reshape_squeeze.25.counts_ref, bf16[2048,768]{1,0:T(8,128)(2,1)} %project_qkv.1.q_ref.k_ref.v_ref, bf16[2048,768]{1,0:T(8,128)(2,1)} %project_qkv.1.q_ref.k_ref.v_ref, ...), custom_call_target="tpu_custom_call" | custom-call | flops 3221225472 | bytes 4194304 | tf_op jit(solution)/shard_map/attend_forward/pallas_call | solution.py:145
  281.7 12.7 %all-to-all-start.2 = ((bf16[4,512,256]{2,1,0:T(8,128)(2,1)}), bf16[4,512,256]{2,1,0:T(8,128)(2,1)S(1)}, u32[]{:S(2)}, u32[]{:S(2)}) async-start(bf16[4,512,256]{2,1,0:T(8,128)(2,1)} %bitcast.8), calls=%async_computation.2 | async-start | bytes 2097152 | tf_op jit(solution)/shard_map/all_to_all | solution.py:599
  295.1 15.4 %all-to-all-done.2 = bf16[4,512,256]{2,1,0:T(8,128)(2,1)S(1)} async-done(((bf16[4,512,256]{2,1,0:T(8,128)(2,1)}), bf16[4,512,256]{2,1,0:T(8,128)(2,1)S(1)}, u32[]{:S(2)}, u32[]{:S(2)}) %all-to-all-start.2) | async-done | bytes 1048608 | tf_op jit(solution)/shard_map/all_to_all | solution.py:599
  311.6 43.8 %feed_forward.1 = (bf16[512,1024]{1,0:T(8,128)(2,1)}, f32[512,1024]{1,0:T(8,128)}, bf16[512,1024]{1,0:T(8,128)(2,1)}, f32[1,1024]{1,0:T(1,128)}, bf16[8,4736,256]{2,1,0:T(8,128)(2,1)}) custom-call(bf16[512,1024]{1,0:T(8,128)(2,1)} %bitcast.80, bf16[512,1024]{1,0:T(8,128)(2,1)} %bitcast.95, bf16[512,1024]{1,0:T(8,128)(2,1)} %bitcast.107, ...), custom_call_target="tpu_custom_call" | custom-call | flops 29796335616 | bytes 38797312 | tf_op jit(solution)/shard_map/feed_forward/pallas_call | solution.py:465
  361.4 15.6 %all-to-all-done.3 = bf16[512,4,256]{2,0,1:T(8,128)(2,1)S(1)} async-done(((bf16[512,4,256]{2,0,1:T(8,128)(2,1)}), bf16[512,4,256]{2,0,1:T(8,128)(2,1)S(1)}, u32[]{:S(2)}, u32[]{:S(2)}) %all-to-all-start.3) | async-done | bytes 1048608 | tf_op jit(solution)/shard_map/all_to_all | solution.py:605
  378.5 49.5 %attend_backward.1 = (bf16[2048,1024]{1,0:T(8,128)(2,1)}, bf16[1024,768]{1,0:T(8,128)(2,1)}, f32[1,1024]{1,0:T(1,128)S(1)}) custom-call(s32[32]{0:T(128)S(1)} %reshape_squeeze.24.chosen_ref, s32[32]{0:T(128)S(1)} %reshape_squeeze.25.counts_ref, bf16[2048,768]{1,0:T(8,128)(2,1)} %project_qkv.1.q_ref.k_ref.v_ref, ...), custom_call_target="tpu_custom_call" | custom-call | flops 8053063680 | bytes 8388608 | tf_op jit(solution)/shard_map/attend_backward/pallas_call | solution.py:283
  447.7 5.4 collective-permute-start.19
  453.1 11.3 %all-to-all-done.4 = bf16[8,136,768]{2,1,0:T(8,128)(2,1)S(1)} async-done(((bf16[8,136,768]{2,1,0:T(8,128)(2,1)}), bf16[8,136,768]{2,1,0:T(8,128)(2,1)S(1)}, u32[]{:S(2)}, u32[]{:S(2)}) %all-to-all-start.4) | async-done | bytes 1671200 | tf_op jit(solution)/shard_map/all_to_all | solution.py:625
  470.1 27.7 %reduce-scatter.2.cloned.1.call-done = bf16[1,4736,256]{2,1,0:T(8,128)(2,1)} async-done(((bf16[8,4736,256]{2,1,0:T(8,128)(2,1)}), bf16[1,4736,256]{2,1,0:T(8,128)(2,1)}) %reduce-scatter.2.cloned.1.call-update) | async-done | bytes 2424848 | tf_op jit(solution)/shard_map/reduce_scatter | solution.py:606
  526.9 42.0 %collective-permute-done.20 = bf16[512,1024]{1,0:T(8,128)(2,1)} collective-permute-done((bf16[512,1024]{1,0:T(8,128)(2,1)}, bf16[512,1024]{1,0:T(8,128)(2,1)}, u32[]{:S(2)}, u32[]{:S(2)}) %collective-permute-start.20) | collective-permute-done | bytes 1048608 | tf_op jit(solution)/shard_map/ppermute | solution.py:544
  569.0 44.1 %collective-permute-done.23 = bf16[512,1024]{1,0:T(8,128)(2,1)} collective-permute-done((bf16[512,1024]{1,0:T(8,128)(2,1)}, bf16[512,1024]{1,0:T(8,128)(2,1)}, u32[]{:S(2)}, u32[]{:S(2)}) %collective-permute-start.23) | collective-permute-done | bytes 1048608 | tf_op jit(solution)/shard_map/ppermute | solution.py:545
  (171 shorter events, 132.6 us)
Async XLA Ops:
  13.1 15.9 %all-to-all-start = ((bf16[4,40,768]{2,1,0:T(8,128)(2,1)}), bf16[4,40,768]{2,1,0:T(8,128)(2,1)S(1)}, u32[]{:S(2)}, u32[]{:S(2)}) async-start(bf16[4,40,768]{2,1,0:T(8,128)(2,1)} %copy.68), calls=%async_computation | async-start | bytes 491520 | tf_op jit(solution)/shard_map/all_to_all | solution.py:576
  19.5 43.3 %all-gather.4.cloned.1.call-start = ((), (), s32[]{:S(2)}) async-start(), calls=%async_computation.8 | async-start | bytes 2211840 | tf_op jit(solution)/shard_map/all_gather | solution.py:583
  20.4 15.3 %collective-permute-start.1 = (bf16[32,6656]{1,0:T(8,128)(2,1)S(1)}, bf16[32,6656]{1,0:T(8,128)(2,1)S(1)}, u32[]{:S(2)}, u32[]{:S(2)}) collective-permute-start(bf16[32,6656]{1,0:T(8,128)(2,1)S(1)} %constant_dynamic-update-slice_fusion), channel_id=1, source_target_pairs={{1,0},{2,1},{3,2},{5,4},{6,5},{7,6},{9,8},{10,9},{11,10},{13,12},{... | collective-permute-start | bytes 1277960 | tf_op jit(solution)/shard_map/ppermute | solution.py:514
  21.7 15.3 %collective-permute-start = (bf16[32,6656]{1,0:T(8,128)(2,1)S(1)}, bf16[32,6656]{1,0:T(8,128)(2,1)S(1)}, u32[]{:S(2)}, u32[]{:S(2)}) collective-permute-start(bf16[32,6656]{1,0:T(8,128)(2,1)S(1)} %constant_dynamic-update-slice_fusion), channel_id=1, source_target_pairs={{0,1},{1,2},{2,3},{4,5},{5,6},{6,7},{8,9},{9,10},{10,11},{12,13},{... | collective-permute-start | bytes 1277960 | tf_op jit(solution)/shard_map/ppermute | solution.py:513
  29.8 112.7 %all-gather.6.cloned.1.call-start = ((), (), s32[]{:S(2)}) async-start(), calls=%async_computation.9 | async-start | bytes 15335424 | tf_op jit(solution)/shard_map/all_gather | solution.py:587
  64.4 247.1 %all-gather.8.cloned.1.call-start = ((), (), s32[]{:S(2)}) async-start(), calls=%async_computation.10 | async-start | bytes 6488064 | tf_op jit(solution)/shard_map/all_gather | solution.py:594
  142.5 27.3 %collective-permute-start.9 = (bf16[512,1024]{1,0:T(8,128)(2,1)S(1)}, bf16[512,1024]{1,0:T(8,128)(2,1)}, u32[]{:S(2)}, u32[]{:S(2)}) collective-permute-start(bf16[512,1024]{1,0:T(8,128)(2,1)S(1)} %bitcast.81), channel_id=1, source_target_pairs={{1,0},{2,1},{3,2},{5,4},{6,5},{7,6},{9,8},{10,9},{11,10},{13,12},{... | collective-permute-start | bytes 3145736 | tf_op jit(solution)/shard_map/ppermute | solution.py:514
  143.8 27.3 %collective-permute-start.6 = (bf16[512,1024]{1,0:T(8,128)(2,1)S(1)}, bf16[512,1024]{1,0:T(8,128)(2,1)}, u32[]{:S(2)}, u32[]{:S(2)}) collective-permute-start(bf16[512,1024]{1,0:T(8,128)(2,1)S(1)} %bitcast.82), channel_id=1, source_target_pairs={{0,1},{1,2},{2,3},{4,5},{5,6},{6,7},{8,9},{9,10},{10,11},{12,13},{... | collective-permute-start | bytes 3145736 | tf_op jit(solution)/shard_map/ppermute | solution.py:513
  169.9 26.7 %collective-permute-start.10 = (bf16[512,1024]{1,0:T(8,128)(2,1)}, bf16[512,1024]{1,0:T(8,128)(2,1)}, u32[]{:S(2)}, u32[]{:S(2)}) collective-permute-start(bf16[512,1024]{1,0:T(8,128)(2,1)} %collective-permute-done.9), channel_id=1, source_target_pairs={{1,0},{2,1},{5,4},{6,5},{9,8},{10,9},{13,12},{14,13},{17,16},{18,1... | collective-permute-start | bytes 3145736 | tf_op jit(solution)/shard_map/ppermute | solution.py:514
  171.2 26.7 %collective-permute-start.7 = (bf16[512,1024]{1,0:T(8,128)(2,1)}, bf16[512,1024]{1,0:T(8,128)(2,1)}, u32[]{:S(2)}, u32[]{:S(2)}) collective-permute-start(bf16[512,1024]{1,0:T(8,128)(2,1)} %collective-permute-done.6), channel_id=1, source_target_pairs={{1,2},{2,3},{5,6},{6,7},{9,10},{10,11},{13,14},{14,15},{17,18},{18... | collective-permute-start | bytes 3145736 | tf_op jit(solution)/shard_map/ppermute | solution.py:513
  196.6 34.2 %collective-permute-start.11 = (bf16[512,1024]{1,0:T(8,128)(2,1)}, bf16[512,1024]{1,0:T(8,128)(2,1)}, u32[]{:S(2)}, u32[]{:S(2)}) collective-permute-start(bf16[512,1024]{1,0:T(8,128)(2,1)} %collective-permute-done.10), channel_id=1, source_target_pairs={{1,0},{5,4},{9,8},{13,12},{17,16},{21,20},{25,24},{29,28}} | collective-permute-start | bytes 3145736 | tf_op jit(solution)/shard_map/ppermute | solution.py:514
  197.9 32.9 %collective-permute-start.8 = (bf16[512,1024]{1,0:T(8,128)(2,1)}, bf16[512,1024]{1,0:T(8,128)(2,1)}, u32[]{:S(2)}, u32[]{:S(2)}) collective-permute-start(bf16[512,1024]{1,0:T(8,128)(2,1)} %collective-permute-done.7), channel_id=1, source_target_pairs={{2,3},{6,7},{10,11},{14,15},{18,19},{22,23},{26,27},{30,31}} | collective-permute-start | bytes 3145736 | tf_op jit(solution)/shard_map/ppermute | solution.py:513
  205.6 41.4 %all-to-all-start.1 = ((bf16[4,256,512]{2,1,0:T(8,128)(2,1)}), bf16[4,256,512]{2,1,0:T(8,128)(2,1)}, u32[]{:S(2)}, u32[]{:S(2)}) async-start(bf16[4,256,512]{2,1,0:T(8,128)(2,1)} %pad_maximum_fusion.5), calls=%async_computation.1 | async-start | bytes 2097152 | tf_op jit(solution)/shard_map/all_to_all | solution.py:593
  281.7 28.7 %all-to-all-start.2 = ((bf16[4,512,256]{2,1,0:T(8,128)(2,1)}), bf16[4,512,256]{2,1,0:T(8,128)(2,1)S(1)}, u32[]{:S(2)}, u32[]{:S(2)}) async-start(bf16[4,512,256]{2,1,0:T(8,128)(2,1)} %bitcast.8), calls=%async_computation.2 | async-start | bytes 2097152 | tf_op jit(solution)/shard_map/all_to_all | solution.py:599
  294.4 203.4 %reduce-scatter.2.cloned.1.call-start = ((), (), s32[]{:S(2)}) async-start(), calls=%async_computation.11 | async-start | bytes 21823488 | tf_op jit(solution)/shard_map/reduce_scatter | solution.py:606
  357.6 19.4 %all-to-all-start.3 = ((bf16[512,4,256]{2,0,1:T(8,128)(2,1)}), bf16[512,4,256]{2,0,1:T(8,128)(2,1)S(1)}, u32[]{:S(2)}, u32[]{:S(2)}) async-start(bf16[512,4,256]{2,0,1:T(8,128)(2,1)} %bitcast.86), calls=%async_computation.3 | async-start | bytes 2097152 | tf_op jit(solution)/shard_map/all_to_all | solution.py:605
  430.8 13.9 %collective-permute-start.18 = (bf16[512,1024]{1,0:T(8,128)(2,1)}, bf16[512,1024]{1,0:T(8,128)(2,1)}, u32[]{:S(2)}, u32[]{:S(2)}) collective-permute-start(bf16[512,1024]{1,0:T(8,128)(2,1)} %get-tuple-element.49), channel_id=1, source_target_pairs={{0,1},{4,5},{8,9},{12,13},{16,17},{20,21},{24,25},{28,29}} | collective-permute-start | bytes 3145736 | tf_op jit(solution)/shard_map/ppermute | solution.py:544
  434.5 29.9 %all-to-all-start.4 = ((bf16[8,136,768]{2,1,0:T(8,128)(2,1)}), bf16[8,136,768]{2,1,0:T(8,128)(2,1)S(1)}, u32[]{:S(2)}, u32[]{:S(2)}) async-start(bf16[8,136,768]{2,1,0:T(8,128)(2,1)} %fusion.5), calls=%async_computation.4 | async-start | bytes 3342336 | tf_op jit(solution)/shard_map/all_to_all | solution.py:625
  438.1 69.1 %collective-permute-start.21 = (bf16[512,1024]{1,0:T(8,128)(2,1)S(1)}, bf16[512,1024]{1,0:T(8,128)(2,1)}, u32[]{:S(2)}, u32[]{:S(2)}) collective-permute-start(bf16[512,1024]{1,0:T(8,128)(2,1)S(1)} %get-tuple-element.50), channel_id=1, source_target_pairs={{3,2},{7,6},{11,10},{15,14},{19,18},{23,22},{27,26},{31,30}} | collective-permute-start | bytes 3145736 | tf_op jit(solution)/shard_map/ppermute | solution.py:545
  447.7 59.6 %collective-permute-start.19 = (bf16[512,1024]{1,0:T(8,128)(2,1)}, bf16[512,1024]{1,0:T(8,128)(2,1)}, u32[]{:S(2)}, u32[]{:S(2)}) collective-permute-start(bf16[512,1024]{1,0:T(8,128)(2,1)} %add_convert_fusion.3), channel_id=1, source_target_pairs={{0,1},{1,2},{4,5},{5,6},{8,9},{9,10},{12,13},{13,14},{16,17},{17,1... | collective-permute-start | bytes 3145736 | tf_op jit(solution)/shard_map/ppermute | solution.py:544
  465.5 36.5 %all-to-all-start.5 = ((bf16[4,40,768]{2,1,0:T(8,128)(2,1)}), bf16[4,40,768]{2,1,0:T(8,128)(2,1)S(1)}, u32[]{:S(2)}, u32[]{:S(2)}) async-start(bf16[4,40,768]{2,1,0:T(8,128)(2,1)} %fusion.9), calls=%async_computation.5 | async-start | bytes 491520 | tf_op jit(solution)/shard_map/all_to_all | solution.py:629
  502.7 116.8 %all-to-all-start.6 = ((bf16[4,1184,256]{2,1,0:T(8,128)(2,1)}), bf16[4,1184,256]{2,1,0:T(8,128)(2,1)S(1)}, u32[]{:S(2)}, u32[]{:S(2)}) async-start(bf16[4,1184,256]{2,1,0:T(8,128)(2,1)} %pad_maximum_fusion.1), calls=%async_computation.7 | async-start | bytes 4849664 | tf_op jit(solution)/shard_map/all_to_all | solution.py:620
  513.5 55.5 %collective-permute-start.20 = (bf16[512,1024]{1,0:T(8,128)(2,1)}, bf16[512,1024]{1,0:T(8,128)(2,1)}, u32[]{:S(2)}, u32[]{:S(2)}) collective-permute-start(bf16[512,1024]{1,0:T(8,128)(2,1)} %get-tuple-element.47), channel_id=1, source_target_pairs={{0,1},{1,2},{2,3},{4,5},{5,6},{6,7},{8,9},{9,10},{10,11},{12,13},{... | collective-permute-start | bytes 3145736 | tf_op jit(solution)/shard_map/ppermute | solution.py:544
  521.2 91.9 %collective-permute-start.23 = (bf16[512,1024]{1,0:T(8,128)(2,1)}, bf16[512,1024]{1,0:T(8,128)(2,1)}, u32[]{:S(2)}, u32[]{:S(2)}) collective-permute-start(bf16[512,1024]{1,0:T(8,128)(2,1)} %add_convert_fusion), channel_id=1, source_target_pairs={{1,0},{2,1},{3,2},{5,4},{6,5},{7,6},{9,8},{10,9},{11,10},{13,12},{... | collective-permute-start | bytes 3145736 | tf_op jit(solution)/shard_map/ppermute | solution.py:545
  (29 other events, 694.6 us)
Sparse Core Ops, SparseCore 0:
  29.9 25.5 all-gather.3
  64.5 77.9 all-gather.5
  144.4 43.3 all-gather.7
  355.5 142.2 reduce-scatter.1

commit v3 on v2

--- a/solution.py
+++ b/solution.py
@@ -504,28 +504,34 @@
     return lax.optimization_barrier((value, earlier))[0]
 
 
-def chain_gather(block, axis):
+def chain_gather(blocks, axis):
     size = lax.axis_size(axis)
     place = lax.axis_index(axis)
-    from_below, from_above = [], []
-    rising = falling = block
+    steps = []
+    rising = falling = tuple(blocks)
     for step in range(size - 1):
-        rising = lax.ppermute(rising, axis, [(i, i + 1) for i in range(step, size - 1)])
-        falling = lax.ppermute(falling, axis, [(i + 1, i) for i in range(size - 1 - step)])
-        from_below.append(rising)
-        from_above.append(falling)
-    ordered = []
-    for index in range(size):
-        cases = []
-        for mine in range(size):
-            if mine == index:
-                cases.append(block)
-            elif mine > index:
-                cases.append(from_below[mine - index - 1])
-            else:
-                cases.append(from_above[index - mine - 1])
-        ordered.append(lax.select_n(place, *cases) if size > 2 else lax.select_n(place > 0, *cases))
-    return ordered, list(zip(from_below, from_above))
+        up = [(i, i + 1) for i in range(step, size - 1)]
+        down = [(i + 1, i) for i in range(size - 1 - step)]
+        rising = tuple(lax.ppermute(block, axis, up) for block in rising)
+        falling = tuple(lax.ppermute(block, axis, down) for block in falling)
+        if len(blocks) > 1:
+            rising, falling = lax.optimization_barrier((rising, falling))
+        steps.append((rising, falling))
+    results = []
+    for number, block in enumerate(blocks):
+        ordered = []
+        for index in range(size):
+            cases = []
+            for mine in range(size):
+                if mine == index:
+                    cases.append(block)
+                elif mine > index:
+                    cases.append(steps[mine - index - 1][0][number])
+                else:
+                    cases.append(steps[index - mine - 1][1][number])
+            ordered.append(lax.select_n(place, *cases) if size > 2 else lax.select_n(place > 0, *cases))
+        results.append(ordered)
+    return results, steps
 
 
 def chain_scatter(partial, axis):
@@ -545,7 +551,7 @@
         falling = lax.ppermute(
             down.astype(BF16), axis, [(i, i - 1) for i in range(size - 1 - step, size)]
         )
-    return block(place) + rising.astype(F32) + falling.astype(F32)
+    return block(place) + rising.astype(F32) + falling.astype(F32), (rising, falling)
 
 
 def body(
@@ -577,21 +583,20 @@
     picks = parcel[:, share + 1, : choices.shape[0]].astype(jnp.int32).reshape(ring, 2, -1)
     chosen_all, counts_all = picks[:, 0].reshape(-1), picks[:, 1].reshape(-1)
     shards = jnp.concatenate([w_out, w_gate, w_up], 1)
-    near, steps = chain_gather(shards, "fsdp")
-    near_down, down_steps = chain_gather(after(w_down, steps[0]), "fsdp")
-    gathered, token_steps = chain_gather(after(mine, down_steps[-2]), "fsdp")
+    (near, near_down), steps = chain_gather((shards, w_down), "fsdp")
+    (gathered,), token_steps = chain_gather((after(mine, steps[-2]),), "fsdp")
     parcel = lax.all_gather(parcel, "dp", axis=0, tiled=True)
     w_qkv = parcel[:, :share].reshape(width, 3 * wide)
     gain_one = parcel[:, share, :share].reshape(1, width).astype(F32)
     gain_two = parcel[:, share, share : 2 * share].reshape(1, width).astype(F32)
-    first = lax.all_gather(after(jnp.concatenate(near, 0), w_qkv), "dp", axis=0, tiled=True)
+    first = lax.all_gather(jnp.concatenate(near, 0), "dp", axis=0, tiled=True)
     gathered = jnp.concatenate(gathered, 0)
 
     memory = jnp.concatenate(
         [m[0].reshape(-1, ring, wide).transpose(1, 0, 2) for m in (memory_keys, memory_values)], 2
     )
     memory = lax.all_to_all(after(memory, token_steps[-2]), "fsdp", 0, 0, tiled=True).reshape(-1, 2 * wide)
-    down_full = lax.all_gather(after(jnp.concatenate(near_down, 0), first), "dp", axis=0, tiled=True)
+    down_full = lax.all_gather(jnp.concatenate(near_down, 0), "dp", axis=0, tiled=True)
 
     cosine, sine = rotary_tables(length)
     qkv = project_qkv(gathered, gain_one, w_qkv, cosine, sine, heads)
@@ -609,7 +614,8 @@
         chosen_all, counts_all, qkv, memory, grad_heads, attended_heads, lse, cosine, sine, gathered, gain_one,
         w_qkv, heads, top,
     )
-    grad_normed = chain_scatter(partial, "fsdp")
+    grad_normed, last_step = chain_scatter(partial, "fsdp")
+    grads = after(grads, last_step)
     own = mine.astype(F32)
     factor = lax.rsqrt(jnp.mean(own * own, -1, keepdims=True) + EPSILON)
     scaled = grad_normed * gain_one

time: 631 us -> 508 us (0.81)
  waiting for transfers between devices: 316 us -> 201 us
  starting transfers between devices: 93.1 us -> 73.4 us
  blocking collectives: 0 us -> 14.7 us
    all_gather x2, waiting for transfers between devices: 54.6 us -> 0.01 us  [the longest x1 0.01 us: body(): lax.all_gather(jnp.concatenate(near_down, 0), 'dp', axis=0, tiled=True)]
    all_to_all x1, waiting for transfers between devices: 0.01 us -> 36.8 us  [along_z(): lax.all_to_all(pieces, 'fsdp', 0, 0, tiled=True).astype(F32)]
    ppermute x3, waiting for transfers between devices: 44.1 us -> 8.46 us  [chain_scatter(): lax.ppermute(down.astype(BF16), axis, [(i, i - 1) for i in range(size - 1...]
    reduce_scatter x1, waiting for transfers between devices: 27.7 us -> 0.01 us  [body(): grads = lax.psum_scatter(grads, 'dp', scatter_dimension=0, tiled=True)[0]]
    ppermute x3, waiting for transfers between devices: 47 us -> 28.8 us  [chain_scatter(): lax.ppermute(up.astype(BF16), axis, [(i, i + 1) for i in range(step + 1)])]
    all_to_all x0 -> x1, blocking collectives: none -> 14.7 us  [body(): parcel = lax.all_to_all(parcel, 'fsdp', 0, 0, tiled=True)]
    ppermute x18, waiting for transfers between devices: 96.9 us -> 82.7 us  [the longest x9 75.8 us: chain_gather(): falling = tuple((lax.ppermute(block, axis, down) for block in falling))]
    all_to_all x1, starting transfers between devices: 12.7 us -> 4.5 us  [body(): attended = lax.all_to_all(attended_heads, 'fsdp', 0, 1, tiled=True)]
  transfers between devices with their start and end apart: 35 -> 34, of which waited for: 19 -> 13; matrix products, arithmetic and copies ran while one was open for 8% -> 10% of each run, Pallas kernels for 15% -> 19%
where the time goes in v3:
time: 508 us; the launch traced here: 506 us
  waiting for transfers between devices  201 us (40%)
  Pallas kernels  138 us (27%)
  starting transfers between devices  73.4 us (14%)
  other arithmetic  39.8 us (8%)
  local copies, waits for them, and re-layouts  24.1 us (5%)
  blocking collectives  14.7 us (3%)
  between operations  14.4 us (3%)
    ppermute x9, waiting for transfers between devices, chain_gather(): falling = tuple((lax.ppermute(block, axis, down) for block in falling))  75.8 us
    pallas_call x1, Pallas kernels, attend_backward(): pl.pallas_call(functools.partial(backward_kernel, heads, top, blocks), gr...  49.7 us
    pallas_call x1, Pallas kernels, feed_forward(): pl.pallas_call(functools.partial(ffn_kernel, span, merged), grid=(steps,)...  43.8 us
    all_to_all x1, waiting for transfers between devices, along_z(): lax.all_to_all(pieces, 'fsdp', 0, 0, tiled=True).astype(F32)  36.8 us
    pallas_call x1, Pallas kernels, attend_forward(): pl.pallas_call(functools.partial(forward_kernel, heads, top), grid_spec=p...  33.9 us
    ppermute x3, waiting for transfers between devices, chain_scatter(): lax.ppermute(up.astype(BF16), axis, [(i, i + 1) for i in range(step + 1)])  28.8 us
    ppermute x9, starting transfers between devices, chain_gather(): rising = tuple((lax.ppermute(block, axis, up) for block in rising))  19.6 us
    all_to_all x1, waiting for transfers between devices, body(): grad_heads = lax.all_to_all(grad_attended, 'fsdp', 1, 0, tiled=True)  15.6 us
  transfers between devices with their start and end apart: 34, of which 13 were waited for; matrix products, arithmetic and copies ran while one was open for 10% of the time, Pallas kernels for 19%

profile of v3, /device:TPU:0, one launch (start us, length us, event | category | flops | bytes accessed | tf_op | source)
XLA Modules:
  0.0 506.2 jit_solution(7565387476816779760)
XLA Ops:
  12.6 14.7 %all_to_all.63 = bf16[4,40,768]{2,1,0:T(8,128)(2,1)} all-to-all(bf16[4,40,768]{2,1,0:T(8,128)(2,1)S(1)} %copy.68), channel_id=1, replica_groups=mesh['dp'=8,'fsdp'=4] {'fsdp'}, dimensions={0} | all-to-all | bytes 491520 | tf_op jit(solution)/shard_map/all_to_all | solution.py:582
  28.8 4.6 collective-permute-start
  36.8 6.8 %collective-permute-done.1 = bf16[88,1024]{1,0:T(8,128)(2,1)S(1)} collective-permute-done((bf16[88,1024]{1,0:T(8,128)(2,1)S(1)}, bf16[88,1024]{1,0:T(8,128)(2,1)S(1)}, u32[]{:S(2)}, u32[]{:S(2)}) %collective-permute-start.1) | collective-permute-done | bytes 180256 | tf_op jit(solution)/shard_map/ppermute | solution.py:515
  48.3 13.4 %collective-permute-done.7 = bf16[88,1024]{1,0:T(8,128)(2,1)} collective-permute-done((bf16[88,1024]{1,0:T(8,128)(2,1)S(1)}, bf16[88,1024]{1,0:T(8,128)(2,1)}, u32[]{:S(2)}, u32[]{:S(2)}) %collective-permute-start.7) | collective-permute-done | bytes 180256 | tf_op jit(solution)/shard_map/ppermute | solution.py:516
  66.3 10.6 %collective-permute-done.17 = bf16[88,1024]{1,0:T(8,128)(2,1)} collective-permute-done((bf16[88,1024]{1,0:T(8,128)(2,1)}, bf16[88,1024]{1,0:T(8,128)(2,1)}, u32[]{:S(2)}, u32[]{:S(2)}) %collective-permute-start.17) | collective-permute-done | bytes 180256 | tf_op jit(solution)/shard_map/ppermute | solution.py:516
  82.2 5.6 %collective-permute-start.8 = (bf16[512,1024]{1,0:T(8,128)(2,1)S(1)}, bf16[512,1024]{1,0:T(8,128)(2,1)}, u32[]{:S(2)}, u32[]{:S(2)}) collective-permute-start(bf16[512,1024]{1,0:T(8,128)(2,1)S(1)} %bitcast.82), channel_id=1, source_target_pairs={{0,1},{1,2},{2,3},{4,5},{5,6},{6,7},{8,9},{9,10},{10,11},{12,13},{... | collective-permute-start | bytes 3145736 | tf_op jit(solution)/shard_map/ppermute | solution.py:515
  87.8 16.5 %collective-permute-done.11 = bf16[512,1024]{1,0:T(8,128)(2,1)S(1)} collective-permute-done((bf16[512,1024]{1,0:T(8,128)(2,1)S(1)}, bf16[512,1024]{1,0:T(8,128)(2,1)S(1)}, u32[]{:S(2)}, u32[]{:S(2)}) %collective-permute-start.11) | collective-permute-done | bytes 1048608 | tf_op jit(solution)/shard_map/ppermute | solution.py:516
  110.2 17.1 %collective-permute-done.12 = bf16[512,1024]{1,0:T(8,128)(2,1)} collective-permute-done((bf16[512,1024]{1,0:T(8,128)(2,1)S(1)}, bf16[512,1024]{1,0:T(8,128)(2,1)}, u32[]{:S(2)}, u32[]{:S(2)}) %collective-permute-start.12) | collective-permute-done | bytes 1048608 | tf_op jit(solution)/shard_map/ppermute | solution.py:516
  136.4 5.3 %all-to-all-start.1 = ((bf16[4,256,512]{2,1,0:T(8,128)(2,1)}), bf16[4,256,512]{2,1,0:T(8,128)(2,1)}, u32[]{:S(2)}, u32[]{:S(2)}) async-start(bf16[4,256,512]{2,1,0:T(8,128)(2,1)} %pad_maximum_fusion.5), calls=%async_computation.1 | async-start | bytes 2097152 | tf_op jit(solution)/shard_map/all_to_all | solution.py:598
  144.6 18.3 %collective-permute-done.13 = bf16[512,1024]{1,0:T(8,128)(2,1)} collective-permute-done((bf16[512,1024]{1,0:T(8,128)(2,1)}, bf16[512,1024]{1,0:T(8,128)(2,1)}, u32[]{:S(2)}, u32[]{:S(2)}) %collective-permute-start.13) | collective-permute-done | bytes 1048608 | tf_op jit(solution)/shard_map/ppermute | solution.py:516
  167.7 10.9 %project_qkv.1.q_ref.k_ref.v_ref = bf16[2048,768]{1,0:T(8,128)(2,1)} custom-call(bf16[2048,1024]{1,0:T(8,128)(2,1)} %pad_maximum_fusion.tok_ref, f32[1,1024]{1,0:T(1,128)S(1)} %reshape.172.gain_ref, bf16[1024,768]{1,0:T(8,128)(2,1)S(1)} %bitcast.77, f32[2048,128]{1,0:T(8,128)S(1)} %get-tuple-element.95.cos_ref, f32[2048,128]{1,0:T(8,128)S(1)} %copy-done.1), custom_call_target="tpu_custom_call" | custom-call | flops 3221225472 | bytes 14680064 | tf_op jit(solution)/shard_map/project_qkv/pallas_call | solution.py:56
  178.5 33.9 %attend_forward.1 = (bf16[2048,256]{1,0:T(8,128)(2,1)}, f32[2048,2]{1,0:T(8,128)S(1)}) custom-call(s32[32]{0:T(128)S(1)} %reshape_squeeze.24.chosen_ref, s32[32]{0:T(128)S(1)} %reshape_squeeze.25.counts_ref, bf16[2048,768]{1,0:T(8,128)(2,1)} %project_qkv.1.q_ref.k_ref.v_ref, bf16[2048,768]{1,0:T(8,128)(2,1)} %project_qkv.1.q_ref.k_ref.v_ref, ...), custom_call_target="tpu_custom_call" | custom-call | flops 3221225472 | bytes 4194304 | tf_op jit(solution)/shard_map/attend_forward/pallas_call | solution.py:145
  213.5 4.5 all-to-all-start.2
  218.6 15.2 %all-to-all-done.2 = bf16[4,512,256]{2,1,0:T(8,128)(2,1)S(1)} async-done(((bf16[4,512,256]{2,1,0:T(8,128)(2,1)}), bf16[4,512,256]{2,1,0:T(8,128)(2,1)S(1)}, u32[]{:S(2)}, u32[]{:S(2)}) %all-to-all-start.2) | async-done | bytes 1048608 | tf_op jit(solution)/shard_map/all_to_all | solution.py:604
  235.0 43.8 %feed_forward.1 = (bf16[512,1024]{1,0:T(8,128)(2,1)}, f32[512,1024]{1,0:T(8,128)}, bf16[512,1024]{1,0:T(8,128)(2,1)}, f32[1,1024]{1,0:T(1,128)}, bf16[8,4736,256]{2,1,0:T(8,128)(2,1)}) custom-call(bf16[512,1024]{1,0:T(8,128)(2,1)} %bitcast.80, bf16[512,1024]{1,0:T(8,128)(2,1)} %bitcast.96, bf16[512,1024]{1,0:T(8,128)(2,1)} %bitcast.109, ...), custom_call_target="tpu_custom_call" | custom-call | flops 29796335616 | bytes 38797312 | tf_op jit(solution)/shard_map/feed_forward/pallas_call | solution.py:465
  284.9 15.6 %all-to-all-done.3 = bf16[512,4,256]{2,0,1:T(8,128)(2,1)S(1)} async-done(((bf16[512,4,256]{2,0,1:T(8,128)(2,1)}), bf16[512,4,256]{2,0,1:T(8,128)(2,1)S(1)}, u32[]{:S(2)}, u32[]{:S(2)}) %all-to-all-start.3) | async-done | bytes 1048608 | tf_op jit(solution)/shard_map/all_to_all | solution.py:610
  301.9 49.7 %attend_backward.1 = (bf16[2048,1024]{1,0:T(8,128)(2,1)}, bf16[1024,768]{1,0:T(8,128)(2,1)}, f32[1,1024]{1,0:T(1,128)S(1)}) custom-call(s32[32]{0:T(128)S(1)} %reshape_squeeze.24.chosen_ref, s32[32]{0:T(128)S(1)} %reshape_squeeze.25.counts_ref, bf16[2048,768]{1,0:T(8,128)(2,1)} %project_qkv.1.q_ref.k_ref.v_ref, ...), custom_call_target="tpu_custom_call" | custom-call | flops 8053063680 | bytes 8388608 | tf_op jit(solution)/shard_map/attend_backward/pallas_call | solution.py:283
  356.6 16.7 %collective-permute-done.18 = bf16[512,1024]{1,0:T(8,128)(2,1)S(1)} collective-permute-done((bf16[512,1024]{1,0:T(8,128)(2,1)S(1)}, bf16[512,1024]{1,0:T(8,128)(2,1)S(1)}, u32[]{:S(2)}, u32[]{:S(2)}) %collective-permute-start.18) | collective-permute-done | bytes 1048608 | tf_op jit(solution)/shard_map/ppermute | solution.py:550
  374.9 4.5 collective-permute-start.19
  379.4 12.2 %collective-permute-done.19 = bf16[512,1024]{1,0:T(8,128)(2,1)S(1)} collective-permute-done((bf16[512,1024]{1,0:T(8,128)(2,1)S(1)}, bf16[512,1024]{1,0:T(8,128)(2,1)S(1)}, u32[]{:S(2)}, u32[]{:S(2)}) %collective-permute-start.19) | collective-permute-done | bytes 1048608 | tf_op jit(solution)/shard_map/ppermute | solution.py:550
  411.1 13.7 %all-to-all-done.4 = bf16[8,136,768]{2,1,0:T(8,128)(2,1)S(1)} async-done(((bf16[8,136,768]{2,1,0:T(8,128)(2,1)}), bf16[8,136,768]{2,1,0:T(8,128)(2,1)S(1)}, u32[]{:S(2)}, u32[]{:S(2)}) %all-to-all-start.4) | async-done | bytes 1671200 | tf_op jit(solution)/shard_map/all_to_all | solution.py:631
  425.8 5.7 %all-to-all-start.5 = ((bf16[4,40,768]{2,1,0:T(8,128)(2,1)}), bf16[4,40,768]{2,1,0:T(8,128)(2,1)S(1)}, u32[]{:S(2)}, u32[]{:S(2)}) async-start(bf16[4,40,768]{2,1,0:T(8,128)(2,1)} %fusion.9), calls=%async_computation.5 | async-start | bytes 491520 | tf_op jit(solution)/shard_map/all_to_all | solution.py:635
  431.5 8.5 %collective-permute-done.23 = bf16[512,1024]{1,0:T(8,128)(2,1)} collective-permute-done((bf16[512,1024]{1,0:T(8,128)(2,1)}, bf16[512,1024]{1,0:T(8,128)(2,1)}, u32[]{:S(2)}, u32[]{:S(2)}) %collective-permute-start.23) | collective-permute-done | bytes 1048608 | tf_op jit(solution)/shard_map/ppermute | solution.py:551
  460.0 36.8 %all-to-all-done.6 = bf16[4,1184,256]{2,1,0:T(8,128)(2,1)S(1)} async-done(((bf16[4,1184,256]{2,1,0:T(8,128)(2,1)}), bf16[4,1184,256]{2,1,0:T(8,128)(2,1)S(1)}, u32[]{:S(2)}, u32[]{:S(2)}) %all-to-all-start.6) | async-done | bytes 2424864 | tf_op jit(solution)/shard_map/all_to_all | solution.py:626
  (172 shorter events, 107.3 us)
Async XLA Ops:
  7.2 134.7 %all-gather.4.cloned.1.call-start = ((), (), s32[]{:S(2)}) async-start(), calls=%async_computation.8 | async-start | bytes 2211840 | tf_op jit(solution)/shard_map/all_gather | solution.py:588
  27.4 207.6 %all-gather.8.cloned.1.call-start = ((), (), s32[]{:S(2)}) async-start(), calls=%async_computation.10 | async-start | bytes 6488064 | tf_op jit(solution)/shard_map/all_gather | solution.py:599
  27.5 16.2 %collective-permute-start.2 = (bf16[32,6656]{1,0:T(8,128)(2,1)S(1)}, bf16[32,6656]{1,0:T(8,128)(2,1)S(1)}, u32[]{:S(2)}, u32[]{:S(2)}) collective-permute-start(bf16[32,6656]{1,0:T(8,128)(2,1)S(1)} %constant_dynamic-update-slice_fusion), channel_id=1, source_target_pairs={{1,0},{2,1},{3,2},{5,4},{6,5},{7,6},{9,8},{10,9},{11,10},{13,12},{... | collective-permute-start | bytes 1277960 | tf_op jit(solution)/shard_map/ppermute | solution.py:516
  43.7 18.0 %collective-permute-start.4 = (bf16[32,6656]{1,0:T(8,128)(2,1)S(1)}, bf16[32,6656]{1,0:T(8,128)(2,1)S(1)}, u32[]{:S(2)}, u32[]{:S(2)}) collective-permute-start(bf16[32,6656]{1,0:T(8,128)(2,1)S(1)} %collective-permute-done), channel_id=1, source_target_pairs={{1,2},{2,3},{5,6},{6,7},{9,10},{10,11},{13,14},{14,15},{17,18},{18... | collective-permute-start | bytes 1277960 | tf_op jit(solution)/shard_map/ppermute | solution.py:515
  44.4 17.3 %collective-permute-start.6 = (bf16[32,6656]{1,0:T(8,128)(2,1)S(1)}, bf16[32,6656]{1,0:T(8,128)(2,1)S(1)}, u32[]{:S(2)}, u32[]{:S(2)}) collective-permute-start(bf16[32,6656]{1,0:T(8,128)(2,1)S(1)} %collective-permute-done.2), channel_id=1, source_target_pairs={{1,0},{2,1},{5,4},{6,5},{9,8},{10,9},{13,12},{14,13},{17,16},{18,1... | collective-permute-start | bytes 1277960 | tf_op jit(solution)/shard_map/ppermute | solution.py:516
  79.1 155.9 %all-gather.6.cloned.1.call-start = ((), (), s32[]{:S(2)}) async-start(), calls=%async_computation.9 | async-start | bytes 15335424 | tf_op jit(solution)/shard_map/all_gather | solution.py:592
  80.9 23.3 %collective-permute-start.11 = (bf16[512,1024]{1,0:T(8,128)(2,1)S(1)}, bf16[512,1024]{1,0:T(8,128)(2,1)S(1)}, u32[]{:S(2)}, u32[]{:S(2)}) collective-permute-start(bf16[512,1024]{1,0:T(8,128)(2,1)S(1)} %bitcast.81), channel_id=1, source_target_pairs={{1,0},{2,1},{3,2},{5,4},{6,5},{7,6},{9,8},{10,9},{11,10},{13,12},{... | collective-permute-start | bytes 3145736 | tf_op jit(solution)/shard_map/ppermute | solution.py:516
  82.2 23.3 %collective-permute-start.8 = (bf16[512,1024]{1,0:T(8,128)(2,1)S(1)}, bf16[512,1024]{1,0:T(8,128)(2,1)}, u32[]{:S(2)}, u32[]{:S(2)}) collective-permute-start(bf16[512,1024]{1,0:T(8,128)(2,1)S(1)} %bitcast.82), channel_id=1, source_target_pairs={{0,1},{1,2},{2,3},{4,5},{5,6},{6,7},{8,9},{9,10},{10,11},{12,13},{... | collective-permute-start | bytes 3145736 | tf_op jit(solution)/shard_map/ppermute | solution.py:515
  104.3 23.1 %collective-permute-start.12 = (bf16[512,1024]{1,0:T(8,128)(2,1)S(1)}, bf16[512,1024]{1,0:T(8,128)(2,1)}, u32[]{:S(2)}, u32[]{:S(2)}) collective-permute-start(bf16[512,1024]{1,0:T(8,128)(2,1)S(1)} %collective-permute-done.11), channel_id=1, source_target_pairs={{1,0},{2,1},{5,4},{6,5},{9,8},{10,9},{13,12},{14,13},{17,16},{18,1... | collective-permute-start | bytes 3145736 | tf_op jit(solution)/shard_map/ppermute | solution.py:516
  105.5 23.1 %collective-permute-start.9 = (bf16[512,1024]{1,0:T(8,128)(2,1)}, bf16[512,1024]{1,0:T(8,128)(2,1)}, u32[]{:S(2)}, u32[]{:S(2)}) collective-permute-start(bf16[512,1024]{1,0:T(8,128)(2,1)} %collective-permute-done.8), channel_id=1, source_target_pairs={{1,2},{2,3},{5,6},{6,7},{9,10},{10,11},{13,14},{14,15},{17,18},{18... | collective-permute-start | bytes 3145736 | tf_op jit(solution)/shard_map/ppermute | solution.py:515
  127.4 35.5 %collective-permute-start.13 = (bf16[512,1024]{1,0:T(8,128)(2,1)}, bf16[512,1024]{1,0:T(8,128)(2,1)}, u32[]{:S(2)}, u32[]{:S(2)}) collective-permute-start(bf16[512,1024]{1,0:T(8,128)(2,1)} %collective-permute-done.12), channel_id=1, source_target_pairs={{1,0},{5,4},{9,8},{13,12},{17,16},{21,20},{25,24},{29,28}} | collective-permute-start | bytes 3145736 | tf_op jit(solution)/shard_map/ppermute | solution.py:516
  128.7 34.2 %collective-permute-start.10 = (bf16[512,1024]{1,0:T(8,128)(2,1)}, bf16[512,1024]{1,0:T(8,128)(2,1)}, u32[]{:S(2)}, u32[]{:S(2)}) collective-permute-start(bf16[512,1024]{1,0:T(8,128)(2,1)} %collective-permute-done.9), channel_id=1, source_target_pairs={{2,3},{6,7},{10,11},{14,15},{18,19},{22,23},{26,27},{30,31}} | collective-permute-start | bytes 3145736 | tf_op jit(solution)/shard_map/ppermute | solution.py:515
  136.4 42.1 %all-to-all-start.1 = ((bf16[4,256,512]{2,1,0:T(8,128)(2,1)}), bf16[4,256,512]{2,1,0:T(8,128)(2,1)}, u32[]{:S(2)}, u32[]{:S(2)}) async-start(bf16[4,256,512]{2,1,0:T(8,128)(2,1)} %pad_maximum_fusion.5), calls=%async_computation.1 | async-start | bytes 2097152 | tf_op jit(solution)/shard_map/all_to_all | solution.py:598
  213.5 20.4 %all-to-all-start.2 = ((bf16[4,512,256]{2,1,0:T(8,128)(2,1)}), bf16[4,512,256]{2,1,0:T(8,128)(2,1)S(1)}, u32[]{:S(2)}, u32[]{:S(2)}) async-start(bf16[4,512,256]{2,1,0:T(8,128)(2,1)} %bitcast.8), calls=%async_computation.2 | async-start | bytes 2097152 | tf_op jit(solution)/shard_map/all_to_all | solution.py:604
  218.0 222.0 %reduce-scatter.2.cloned.1.call-start = ((), (), s32[]{:S(2)}) async-start(), calls=%async_computation.11 | async-start | bytes 21823488 | tf_op jit(solution)/shard_map/reduce_scatter | solution.py:611
  281.1 19.4 %all-to-all-start.3 = ((bf16[512,4,256]{2,0,1:T(8,128)(2,1)}), bf16[512,4,256]{2,0,1:T(8,128)(2,1)S(1)}, u32[]{:S(2)}, u32[]{:S(2)}) async-start(bf16[512,4,256]{2,0,1:T(8,128)(2,1)} %bitcast.73), calls=%async_computation.3 | async-start | bytes 2097152 | tf_op jit(solution)/shard_map/all_to_all | solution.py:610
  353.5 19.8 %collective-permute-start.18 = (bf16[512,1024]{1,0:T(8,128)(2,1)S(1)}, bf16[512,1024]{1,0:T(8,128)(2,1)S(1)}, u32[]{:S(2)}, u32[]{:S(2)}) collective-permute-start(bf16[512,1024]{1,0:T(8,128)(2,1)S(1)} %get-tuple-element.69), channel_id=1, source_target_pairs={{0,1},{4,5},{8,9},{12,13},{16,17},{20,21},{24,25},{28,29}} | collective-permute-start | bytes 3145736 | tf_op jit(solution)/shard_map/ppermute | solution.py:550
  354.9 24.5 %collective-permute-start.21 = (bf16[512,1024]{1,0:T(8,128)(2,1)S(1)}, bf16[512,1024]{1,0:T(8,128)(2,1)}, u32[]{:S(2)}, u32[]{:S(2)}) collective-permute-start(bf16[512,1024]{1,0:T(8,128)(2,1)S(1)} %get-tuple-element.70), channel_id=1, source_target_pairs={{3,2},{7,6},{11,10},{15,14},{19,18},{23,22},{27,26},{31,30}} | collective-permute-start | bytes 3145736 | tf_op jit(solution)/shard_map/ppermute | solution.py:551
  374.9 16.7 %collective-permute-start.19 = (bf16[512,1024]{1,0:T(8,128)(2,1)S(1)}, bf16[512,1024]{1,0:T(8,128)(2,1)S(1)}, u32[]{:S(2)}, u32[]{:S(2)}) collective-permute-start(bf16[512,1024]{1,0:T(8,128)(2,1)S(1)} %add_convert_fusion.3), channel_id=1, source_target_pairs={{0,1},{1,2},{4,5},{5,6},{8,9},{9,10},{12,13},{13,14},{16,17},{17,1... | collective-permute-start | bytes 3145736 | tf_op jit(solution)/shard_map/ppermute | solution.py:550
  398.9 25.9 %all-to-all-start.4 = ((bf16[8,136,768]{2,1,0:T(8,128)(2,1)}), bf16[8,136,768]{2,1,0:T(8,128)(2,1)S(1)}, u32[]{:S(2)}, u32[]{:S(2)}) async-start(bf16[8,136,768]{2,1,0:T(8,128)(2,1)} %fusion.5), calls=%async_computation.4 | async-start | bytes 3342336 | tf_op jit(solution)/shard_map/all_to_all | solution.py:631
  402.7 28.9 %collective-permute-start.20 = (bf16[512,1024]{1,0:T(8,128)(2,1)}, bf16[512,1024]{1,0:T(8,128)(2,1)S(1)}, u32[]{:S(2)}, u32[]{:S(2)}) collective-permute-start(bf16[512,1024]{1,0:T(8,128)(2,1)} %get-tuple-element.67), channel_id=1, source_target_pairs={{0,1},{1,2},{2,3},{4,5},{5,6},{6,7},{8,9},{9,10},{10,11},{12,13},{... | collective-permute-start | bytes 3145736 | tf_op jit(solution)/shard_map/ppermute | solution.py:550
  409.8 30.2 %collective-permute-start.23 = (bf16[512,1024]{1,0:T(8,128)(2,1)}, bf16[512,1024]{1,0:T(8,128)(2,1)}, u32[]{:S(2)}, u32[]{:S(2)}) collective-permute-start(bf16[512,1024]{1,0:T(8,128)(2,1)} %add_convert_fusion), channel_id=1, source_target_pairs={{1,0},{2,1},{3,2},{5,4},{6,5},{7,6},{9,8},{10,9},{11,10},{13,12},{... | collective-permute-start | bytes 3145736 | tf_op jit(solution)/shard_map/ppermute | solution.py:551
  425.8 18.7 %all-to-all-start.5 = ((bf16[4,40,768]{2,1,0:T(8,128)(2,1)}), bf16[4,40,768]{2,1,0:T(8,128)(2,1)S(1)}, u32[]{:S(2)}, u32[]{:S(2)}) async-start(bf16[4,40,768]{2,1,0:T(8,128)(2,1)} %fusion.9), calls=%async_computation.5 | async-start | bytes 491520 | tf_op jit(solution)/shard_map/all_to_all | solution.py:635
  445.2 51.6 %all-to-all-start.6 = ((bf16[4,1184,256]{2,1,0:T(8,128)(2,1)}), bf16[4,1184,256]{2,1,0:T(8,128)(2,1)S(1)}, u32[]{:S(2)}, u32[]{:S(2)}) async-start(bf16[4,1184,256]{2,1,0:T(8,128)(2,1)} %pad_maximum_fusion.1), calls=%async_computation.7 | async-start | bytes 4849664 | tf_op jit(solution)/shard_map/all_to_all | solution.py:626
  (28 other events, 310.4 us)
Sparse Core Ops, SparseCore 0:
  27.5 26.4 all-gather.3
  79.2 41.5 all-gather.7
  122.6 76.5 all-gather.5
  279.0 127.3 reduce-scatter.1

commit v4 on v3

--- a/solution.py
+++ b/solution.py
@@ -40,19 +40,23 @@
     factor = lax.rsqrt(jnp.mean(rows * rows, -1, keepdims=True) + EPSILON)
     normed = (rows * factor * gain_ref[...]).astype(BF16)
     cosine, sine = cos_ref[...], sin_ref[...]
+    wide = heads * HEAD_DIM
     for part in range(3):
+        values = dot(normed, w_ref[:, part * wide : (part + 1) * wide])
         for head in range(heads):
-            columns = slice((part * heads + head) * HEAD_DIM, (part * heads + head + 1) * HEAD_DIM)
-            value = dot(normed, w_ref[:, columns])
+            value = values[:, head * HEAD_DIM : (head + 1) * HEAD_DIM]
             if part < 2:
                 value = value * cosine + pltpu.roll(value, HEAD_DIM // 2, 1) * sine
-            qkv_ref[:, columns] = value.astype(BF16)
+            if part == 0:
+                value = value * (SCALE * LOG2E)
+            at = part * wide + head * HEAD_DIM
+            qkv_ref[:, at : at + HEAD_DIM] = value.astype(BF16)
 
 
 def project_qkv(tokens_all, gain, w_qkv, cosine, sine, heads):
     length, width = tokens_all.shape
     columns = w_qkv.shape[1]
-    block = QBLK
+    block = 2 * QBLK
     return pl.pallas_call(
         functools.partial(qkv_kernel, heads),
         grid=(length // block,),
@@ -91,72 +95,82 @@
     return jnp.concatenate(rows, 0)
 
 
-def forward_kernel(heads, top, chosen_ref, counts_ref, q_ref, k_ref, v_ref, mk_ref, mv_ref, out_ref, lse_ref):
+def forward_kernel(
+    heads, top, chosen_ref, counts_ref, q_ref, k_ref, v_ref, mk_ref, mv_ref, out_ref, lse_ref, acc_s, peak_s
+):
     block = pl.program_id(0)
-    base = block * top
-    bias = memory_bias(counts_ref, base, top, 1)
-    row = lax.broadcasted_iota(jnp.int32, (QBLK, QBLK), 0)
-    column = lax.broadcasted_iota(jnp.int32, (QBLK, QBLK), 1)
-    causal = row >= column
-    own = pl.ds(pl.multiple_of(block * QBLK, QBLK), QBLK)
-    unit = SCALE * LOG2E
-    states = []
+    rows = q_ref.shape[0]
+    subs = rows // QBLK
+    own = pl.ds(pl.multiple_of(block * rows, rows), rows)
+    causal = lax.broadcasted_iota(jnp.int32, (rows, rows), 0) >= lax.broadcasted_iota(jnp.int32, (rows, rows), 1)
+    ones = jnp.ones((rows, HEAD_DIM), BF16)
+    mem_ones = jnp.ones((top * MBLK, HEAD_DIM), BF16)
+    biases = [memory_bias(counts_ref, (block * subs + sub) * top, top, 1) for sub in range(subs)]
     for head in range(heads):
         columns = slice(head * HEAD_DIM, (head + 1) * HEAD_DIM)
-        query = q_ref[:, columns]
-        remote = dot(query, pick_memory(mk_ref, chosen_ref, base, top, columns), NT) * unit + bias
-        local = jnp.where(causal, dot(query, k_ref[own, columns], NT) * unit, NEGATIVE)
-        peak = jnp.maximum(jnp.max(remote, -1, keepdims=True), jnp.max(local, -1, keepdims=True))
-        remote = jnp.exp2(remote - peak)
-        local = jnp.exp2(local - peak)
-        total = jnp.sum(remote, -1, keepdims=True) + jnp.sum(local, -1, keepdims=True)
-        acc = dot(remote.astype(BF16), pick_memory(mv_ref, chosen_ref, base, top, columns))
-        acc = acc + dot(local.astype(BF16), v_ref[own, columns])
-        states.append((peak, total, acc))
-
-    def step(index, states):
-        rows = pl.ds(pl.multiple_of(index * QBLK, QBLK), QBLK)
-        after = []
+        remote = []
+        for sub in range(subs):
+            keys = pick_memory(mk_ref, chosen_ref, (block * subs + sub) * top, top, columns)
+            query = q_ref[sub * QBLK : (sub + 1) * QBLK, columns]
+            remote.append(dot(query, keys, NT) + biases[sub])
+        local = jnp.where(causal, dot(q_ref[:, columns], k_ref[own, columns], NT), NEGATIVE)
+        peak = jnp.max(local, -1, keepdims=True)
+        peak = jnp.maximum(peak, jnp.concatenate([jnp.max(r, -1, keepdims=True) for r in remote], 0))
+        values = jnp.concatenate([v_ref[own, columns], ones], 1)
+        acc = dot(jnp.exp2(local - peak).astype(BF16), values)
+        more = []
+        for sub in range(subs):
+            values = pick_memory(mv_ref, chosen_ref, (block * subs + sub) * top, top, columns)
+            weights = jnp.exp2(remote[sub] - peak[sub * QBLK : (sub + 1) * QBLK]).astype(BF16)
+            more.append(dot(weights, jnp.concatenate([values, mem_ones], 1)))
+        acc_s[head] = acc + jnp.concatenate(more, 0)
+        peak_s[head] = jnp.broadcast_to(peak, (rows, HEAD_DIM))
+
+    def step(index, carry):
+        there = pl.ds(pl.multiple_of(index * rows, rows), rows)
         for head in range(heads):
             columns = slice(head * HEAD_DIM, (head + 1) * HEAD_DIM)
-            peak, total, acc = states[head]
-            scores = dot(q_ref[:, columns], k_ref[rows, columns], NT) * unit
+            peak = peak_s[head][:, :1]
+            scores = dot(q_ref[:, columns], k_ref[there, columns], NT)
             higher = jnp.maximum(peak, jnp.max(scores, -1, keepdims=True))
-            shrink = jnp.exp2(peak - higher)
-            weights = jnp.exp2(scores - higher)
-            total = total * shrink + jnp.sum(weights, -1, keepdims=True)
-            acc = acc * shrink + dot(weights.astype(BF16), v_ref[rows, columns])
-            after.append((higher, total, acc))
-        return tuple(after)
-
-    states = lax.fori_loop(0, block, step, tuple(states))
+            weights = jnp.exp2(scores - higher).astype(BF16)
+            values = jnp.concatenate([v_ref[there, columns], ones], 1)
+            acc_s[head] = acc_s[head] * jnp.exp2(peak - higher) + dot(weights, values)
+            peak_s[head] = jnp.broadcast_to(higher, (rows, HEAD_DIM))
+        return carry
+
+    lax.fori_loop(0, block, step, 0)
     for head in range(heads):
         columns = slice(head * HEAD_DIM, (head + 1) * HEAD_DIM)
-        peak, total, acc = states[head]
-        out_ref[:, columns] = (acc / total).astype(BF16)
-        lse_ref[:, head : head + 1] = peak + jnp.log2(total)
+        total = acc_s[head][:, HEAD_DIM:]
+        out_ref[:, columns] = (acc_s[head][:, :HEAD_DIM] / total).astype(BF16)
+        lse_ref[:, head : head + 1] = peak_s[head][:, :1] + jnp.log2(total[:, :1])
 
 
 def attend_forward(chosen, counts, qkv, memory, heads, top):
     length = qkv.shape[0]
     wide = heads * HEAD_DIM
-    blocks = length // QBLK
+    rows = min(2 * QBLK, length)
     mem_rows = memory.shape[0]
     return pl.pallas_call(
         functools.partial(forward_kernel, heads, top),
         grid_spec=pltpu.PrefetchScalarGridSpec(
             num_scalar_prefetch=2,
-            grid=(blocks,),
+            grid=(length // rows,),
             in_specs=[
-                pl.BlockSpec((QBLK, wide), lambda i, *_: (i, 0)),
+                pl.BlockSpec((rows, wide), lambda i, *_: (i, 0)),
                 pl.BlockSpec((length, wide), lambda i, *_: (0, 1)),
                 pl.BlockSpec((length, wide), lambda i, *_: (0, 2)),
                 pl.BlockSpec((mem_rows, wide), lambda i, *_: (0, 0)),
                 pl.BlockSpec((mem_rows, wide), lambda i, *_: (0, 1)),
             ],
             out_specs=[
-                pl.BlockSpec((QBLK, wide), lambda i, *_: (i, 0)),
-                pl.BlockSpec((QBLK, heads), lambda i, *_: (i, 0)),
+                pl.BlockSpec((rows, wide), lambda i, *_: (i, 0)),
+                pl.BlockSpec((rows, heads), lambda i, *_: (i, 0)),
+            ],
+            scratch_shapes=[
+                pltpu.VMEM((heads, rows, 2 * HEAD_DIM), F32),
+                pltpu.VMEM((heads, rows, HEAD_DIM), F32),
             ],
         ),
         out_shape=[
@@ -174,96 +188,92 @@
 
 
 def backward_kernel(
-    heads, top, blocks, chosen_ref, counts_ref, q_ref, k_ref, v_ref, mk_ref, mv_ref, go_ref, out_ref, lse_ref,
-    cos_ref, sin_ref, tok_ref, gain_ref, w_ref, partial_ref, grad_w_ref, gain_grad_ref, gk_ref, gv_ref, grad_s, gw_s,
+    heads, top, chosen_ref, counts_ref, q_ref, k_ref, v_ref, mk_ref, mv_ref, go_ref, out_ref, lse_ref,
+    cos_ref, sin_ref, tok_ref, gain_ref, w_ref, partial_ref, grad_w_ref, gain_grad_ref,
+    gk_s, gv_s, gq_s, grad_s, gw_s,
 ):
-    block = blocks - 1 - pl.program_id(0)
-    base = block * top
-    unit = SCALE * LOG2E
-    bias = memory_bias(counts_ref, base, top, 0)
-    key_at = lax.broadcasted_iota(jnp.int32, (QBLK, QBLK), 0)
-    query_at = lax.broadcasted_iota(jnp.int32, (QBLK, QBLK), 1)
+    block = pl.num_programs(0) - 1 - pl.program_id(0)
+    rows = q_ref.shape[0]
+    subs = rows // QBLK
+    wide = heads * HEAD_DIM
+    own = pl.ds(pl.multiple_of(block * rows, rows), rows)
+    key_at = lax.broadcasted_iota(jnp.int32, (rows, rows), 0)
+    query_at = lax.broadcasted_iota(jnp.int32, (rows, rows), 1)
     causal = query_at >= key_at
-    own = pl.ds(pl.multiple_of(block * QBLK, QBLK), QBLK)
 
     @pl.when(pl.program_id(0) == 0)
     def _():
-        gk_ref[...] = jnp.zeros_like(gk_ref)
-        gv_ref[...] = jnp.zeros_like(gv_ref)
+        gk_s[...] = jnp.zeros_like(gk_s)
+        gv_s[...] = jnp.zeros_like(gv_s)
         gw_s[...] = jnp.zeros_like(gw_s)
         gain_grad_ref[...] = jnp.zeros_like(gain_grad_ref)
 
     def spread(column):
-        return jnp.transpose(jnp.broadcast_to(column, (QBLK, HEAD_DIM)))[:1]
+        return jnp.transpose(jnp.broadcast_to(column, (rows, HEAD_DIM)))[:1]
 
     stats = []
     for head in range(heads):
         columns = slice(head * HEAD_DIM, (head + 1) * HEAD_DIM)
-        grad = go_ref[:, columns]
-        delta = jnp.sum(grad.astype(F32) * out_ref[:, columns].astype(F32), -1, keepdims=True)
+        delta = jnp.sum(go_ref[:, columns].astype(F32) * out_ref[:, columns].astype(F32), -1, keepdims=True)
         stats.append((spread(lse_ref[:, head : head + 1]), spread(delta)))
 
-    def pair(head, keys, values, mask):
+    def pair(head, queries, keys, values, mask):
         columns = slice(head * HEAD_DIM, (head + 1) * HEAD_DIM)
         lse, delta = stats[head]
-        scores = mask(dot(keys, q_ref[:, columns], NT) * unit)
-        weights = jnp.exp2(scores - lse)
-        grad_weights = dot(values, go_ref[:, columns], NT)
-        grad_scores = (weights * (grad_weights - delta)).astype(BF16)
-        return weights.astype(BF16), grad_scores
-
-    def update(head, rows, weights, grad_scores):
-        columns = slice(head * HEAD_DIM, (head + 1) * HEAD_DIM)
-        gk_ref[rows, columns] += dot(grad_scores, q_ref[:, columns])
-        gv_ref[rows, columns] += dot(weights, go_ref[:, columns])
-
-    totals = []
+        scores = mask(dot(keys, q_ref[queries, columns], NT))
+        weights = jnp.exp2(scores - lse[:, queries])
+        grad_weights = dot(values, go_ref[queries, columns], NT)
+        return weights.astype(BF16), (weights * (grad_weights - delta[:, queries])).astype(BF16)
+
+    every = slice(0, rows)
     for head in range(heads):
         columns = slice(head * HEAD_DIM, (head + 1) * HEAD_DIM)
-        keys = pick_memory(mk_ref, chosen_ref, base, top, columns)
-        values = pick_memory(mv_ref, chosen_ref, base, top, columns)
-        _, grad_scores = pair(head, keys, values, lambda scores: scores + bias)
-        total = dot(grad_scores, keys, TN)
-        keys = k_ref[own, columns]
-        weights, grad_scores = pair(
-            head, keys, v_ref[own, columns], lambda scores: jnp.where(causal, scores, NEGATIVE)
-        )
-        update(head, own, weights, grad_scores)
-        totals.append(total + dot(grad_scores, keys, TN))
-
-    def step(index, totals):
-        rows = pl.ds(pl.multiple_of(index * QBLK, QBLK), QBLK)
-        after = []
+        for sub in range(subs):
+            base = (block * subs + sub) * top
+            queries = slice(sub * QBLK, (sub + 1) * QBLK)
+            keys = pick_memory(mk_ref, chosen_ref, base, top, columns)
+            values = pick_memory(mv_ref, chosen_ref, base, top, columns)
+            bias = memory_bias(counts_ref, base, top, 0)
+            _, grad_scores = pair(head, queries, keys, values, lambda scores: scores + bias)
+            gq_s[queries, columns] = dot(grad_scores, keys, TN)
+
+    def local(head, there, mask):
+        columns = slice(head * HEAD_DIM, (head + 1) * HEAD_DIM)
+        keys = k_ref[there, columns]
+        weights, grad_scores = pair(head, every, keys, v_ref[there, columns], mask)
+        gk_s[there, columns] += dot(grad_scores, q_ref[:, columns])
+        gv_s[there, columns] += dot(weights, go_ref[:, columns])
+        gq_s[:, columns] += dot(grad_scores, keys, TN)
+
+    for head in range(heads):
+        local(head, own, lambda scores: jnp.where(causal, scores, NEGATIVE))
+
+    def step(index, carry):
         for head in range(heads):
-            columns = slice(head * HEAD_DIM, (head + 1) * HEAD_DIM)
-            keys = k_ref[rows, columns]
-            weights, grad_scores = pair(head, keys, v_ref[rows, columns], lambda scores: scores)
-            update(head, rows, weights, grad_scores)
-            after.append(totals[head] + dot(grad_scores, keys, TN))
-        return tuple(after)
-
-    totals = lax.fori_loop(0, block, step, tuple(totals))
+            local(head, pl.ds(pl.multiple_of(index * rows, rows), rows), lambda scores: scores)
+        return carry
+
+    lax.fori_loop(0, block, step, 0)
     cosine, sine = cos_ref[...], sin_ref[...]
 
     def unturn(value):
         return value * cosine - pltpu.roll(value, HEAD_DIM // 2, 1) * sine
 
-    wide = heads * HEAD_DIM
     for head in range(heads):
         columns = slice(head * HEAD_DIM, (head + 1) * HEAD_DIM)
         at = head * HEAD_DIM
-        grad_s[:, at : at + HEAD_DIM] = unturn(totals[head] * SCALE).astype(BF16)
-        grad_key = gk_ref[own, columns] * SCALE
+        grad_s[:, at : at + HEAD_DIM] = unturn(gq_s[:, columns] * SCALE).astype(BF16)
+        grad_key = gk_s[own, columns] * (1.0 / LOG2E)
         grad_s[:, wide + at : wide + at + HEAD_DIM] = unturn(grad_key).astype(BF16)
-        grad_s[:, 2 * wide + at : 2 * wide + at + HEAD_DIM] = gv_ref[own, columns].astype(BF16)
-
-    rows = tok_ref[...].astype(F32)
-    rows = rows * lax.rsqrt(jnp.mean(rows * rows, -1, keepdims=True) + EPSILON)
-    normed = (rows * gain_ref[...]).astype(BF16)
+        grad_s[:, 2 * wide + at : 2 * wide + at + HEAD_DIM] = gv_s[own, columns].astype(BF16)
+
+    tokens = tok_ref[...].astype(F32)
+    tokens = tokens * lax.rsqrt(jnp.mean(tokens * tokens, -1, keepdims=True) + EPSILON)
+    normed = (tokens * gain_ref[...]).astype(BF16)
     grad = grad_s[...]
     partial = dot(grad, w_ref[...], NT)
     partial_ref[...] = partial.astype(BF16)
-    gain_grad_ref[...] += jnp.sum(partial * rows, 0, keepdims=True)
+    gain_grad_ref[...] += jnp.sum(partial * tokens, 0, keepdims=True)
     gw_s[...] += dot(normed, grad, TN)
 
     @pl.when(block == 0)
@@ -277,38 +287,39 @@
     length = qkv.shape[0]
     width = tokens_all.shape[1]
     wide = heads * HEAD_DIM
-    blocks = length // QBLK
+    rows = min(2 * QBLK, length)
     mem_rows = memory.shape[0]
-    last = blocks - 1
+    last = length // rows - 1
     return pl.pallas_call(
-        functools.partial(backward_kernel, heads, top, blocks),
+        functools.partial(backward_kernel, heads, top),
         grid_spec=pltpu.PrefetchScalarGridSpec(
             num_scalar_prefetch=2,
-            grid=(blocks,),
+            grid=(last + 1,),
             in_specs=[
-                pl.BlockSpec((QBLK, wide), lambda i, *_: (last - i, 0)),
+                pl.BlockSpec((rows, wide), lambda i, *_: (last - i, 0)),
                 pl.BlockSpec((length, wide), lambda i, *_: (0, 1)),
                 pl.BlockSpec((length, wide), lambda i, *_: (0, 2)),
                 pl.BlockSpec((mem_rows, wide), lambda i, *_: (0, 0)),
                 pl.BlockSpec((mem_rows, wide), lambda i, *_: (0, 1)),
-                pl.BlockSpec((QBLK, wide), lambda i, *_: (last - i, 0)),
-                pl.BlockSpec((QBLK, wide), lambda i, *_: (last - i, 0)),
-                pl.BlockSpec((QBLK, heads), lambda i, *_: (last - i, 0)),
-                pl.BlockSpec((QBLK, HEAD_DIM), lambda i, *_: (last - i, 0)),
-                pl.BlockSpec((QBLK, HEAD_DIM), lambda i, *_: (last - i, 0)),
-                pl.BlockSpec((QBLK, width), lambda i, *_: (last - i, 0)),
+                pl.BlockSpec((rows, wide), lambda i, *_: (last - i, 0)),
+                pl.BlockSpec((rows, wide), lambda i, *_: (last - i, 0)),
+                pl.BlockSpec((rows, heads), lambda i, *_: (last - i, 0)),
+                pl.BlockSpec((rows, HEAD_DIM), lambda i, *_: (last - i, 0)),
+                pl.BlockSpec((rows, HEAD_DIM), lambda i, *_: (last - i, 0)),
+                pl.BlockSpec((rows, width), lambda i, *_: (last - i, 0)),
                 pl.BlockSpec((1, width), lambda i, *_: (0, 0)),
                 pl.BlockSpec((width, 3 * wide), lambda i, *_: (0, 0)),
             ],
             out_specs=[
-                pl.BlockSpec((QBLK, width), lambda i, *_: (last - i, 0)),
+                pl.BlockSpec((rows, width), lambda i, *_: (last - i, 0)),
                 pl.BlockSpec((width, 3 * wide), lambda i, *_: (0, 0)),
                 pl.BlockSpec((1, width), lambda i, *_: (0, 0)),
             ],
             scratch_shapes=[
                 pltpu.VMEM((length, wide), F32),
                 pltpu.VMEM((length, wide), F32),
-                pltpu.VMEM((QBLK, 3 * wide), BF16),
+                pltpu.VMEM((rows, wide), F32),
+                pltpu.VMEM((rows, 3 * wide), BF16),
                 pltpu.VMEM((width, 3 * wide), F32),
             ],
         ),
@@ -365,8 +376,9 @@
 
     normed = normed_s[...]
     upstream = cot_ref[...]
-    gate_act = dot(normed, gate_w[...])
-    up_act = dot(normed, up_w[...])
+    both = jnp.concatenate([gate_w[...], up_w[...]], 1)
+    acts = dot(normed, both)
+    gate_act, up_act = acts[:, :wide], acts[:, wide:]
     grad_hidden = dot(upstream, down_w[...], NT)
     sigmoid = jax.nn.sigmoid(gate_act)
     silu = gate_act * sigmoid
@@ -374,7 +386,8 @@
     grad_gate = (grad_hidden * up_act * sigmoid * (1.0 + gate_act * (1.0 - sigmoid))).astype(BF16)
     grad_up = (grad_hidden * silu).astype(BF16)
     mixed_s[...] += dot(hidden, down_w[...])
-    upstream_s[...] += dot(grad_gate, gate_w[...], NT) + dot(grad_up, up_w[...], NT)
+    grad_acts = jnp.concatenate([grad_gate, grad_up], 1)
+    upstream_s[...] += dot(grad_acts, both, NT)
     down_s[pl.ds(pl.multiple_of(step * wide, wide), wide), :] = dot(hidden, upstream, TN).astype(BF16)
 
     @pl.when(step >= 2)
@@ -382,9 +395,9 @@
         copy_out(0, slot, step - 2).wait()
         copy_out(1, slot, step - 2).wait()
 
-    turned = turned_s[...]
-    gate_s[slot] = dot(turned, grad_gate).astype(BF16).reshape(span, share, wide)
-    up_s[slot] = dot(turned, grad_up).astype(BF16).reshape(span, share, wide)
+    weight_grads = dot(turned_s[...], grad_acts).astype(BF16)
+    gate_s[slot] = weight_grads[:, :wide].reshape(span, share, wide)
+    up_s[slot] = weight_grads[:, wide:].reshape(span, share, wide)
     copy_out(0, slot, step).start()
     copy_out(1, slot, step).start()
 
@@ -543,6 +556,7 @@
         return lax.dynamic_slice_in_dim(partial, jnp.clip(index, 0, size - 1) * rows, rows, 0).astype(F32)
 
     rising = falling = None
+    steps = []
     for step in range(size - 1):
         up, down = block(size - 1 - step + place), block(step - size + 1 + place)
         if step:
@@ -551,7 +565,8 @@
         falling = lax.ppermute(
             down.astype(BF16), axis, [(i, i - 1) for i in range(size - 1 - step, size)]
         )
-    return block(place) + rising.astype(F32) + falling.astype(F32), (rising, falling)
+        steps.append((rising, falling))
+    return block(place), steps
 
 
 def body(
@@ -614,16 +629,8 @@
         chosen_all, counts_all, qkv, memory, grad_heads, attended_heads, lse, cosine, sine, gathered, gain_one,
         w_qkv, heads, top,
     )
-    grad_normed, last_step = chain_scatter(partial, "fsdp")
-    grads = after(grads, last_step)
-    own = mine.astype(F32)
-    factor = lax.rsqrt(jnp.mean(own * own, -1, keepdims=True) + EPSILON)
-    scaled = grad_normed * gain_one
-    inner = jnp.mean(scaled * own, -1, keepdims=True)
-    tokens_grad = (grad_middle + factor * scaled - own * (factor * factor * factor * inner)).astype(BF16)
-
-    def along_z(pieces):
-        return jnp.sum(lax.all_to_all(pieces, "fsdp", 0, 0, tiled=True).astype(F32), 0)
+    own_term, steps = chain_scatter(partial, "fsdp")
+    grads = after(grads, steps[-2])
 
     gains = jnp.concatenate([gain_one_grad, gain_two_grad], 0).reshape(2, span, -1).transpose(1, 0, 2)
     gains = jnp.pad(gains.astype(BF16), ((0, 0), (0, extra - 2), (0, 3 * wide - gains.shape[2])))
@@ -649,9 +656,16 @@
         down = grads[: ring * tall * lanes].reshape(lanes, ring, tall, strip).transpose(1, 0, 2, 3)
         grads = grads[ring * tall * lanes :]
     grads = grads.reshape(-1, ring, share, strip).transpose(1, 0, 2, 3)
-    pieces = along_z(
-        jnp.concatenate([down.reshape(ring, -1, strip), grads.reshape(ring, -1, strip)], 1)
-    )
+    pieces = jnp.concatenate([down.reshape(ring, -1, strip), grads.reshape(ring, -1, strip)], 1)
+    rising, falling = after(steps[-1], pieces)
+    grad_normed = own_term + rising.astype(F32) + falling.astype(F32)
+    own = mine.astype(F32)
+    factor = lax.rsqrt(jnp.mean(own * own, -1, keepdims=True) + EPSILON)
+    scaled = grad_normed * gain_one
+    inner = jnp.mean(scaled * own, -1, keepdims=True)
+    tokens_grad = (grad_middle + factor * scaled - own * (factor * factor * factor * inner)).astype(BF16)
+
+    pieces = jnp.sum(lax.all_to_all(pieces, "fsdp", 0, 0, tiled=True).astype(F32), 0)
     down_share = pieces[: lanes * tall].reshape(lanes, tall, strip).transpose(1, 0, 2).reshape(tall, width)
     others = pieces[lanes * tall :].reshape(-1, share, strip).transpose(1, 0, 2).reshape(share, -1)
     return (

time: 508 us -> 515 us (1.014)
  the two profiles are of different devices: /device:TPU:0 before, /device:TPU:8 now
where the time goes in v4:
time: 515 us; the launch traced here: 513 us
  waiting for transfers between devices  193 us (37%)
  starting transfers between devices  115 us (22%)
  Pallas kernels  112 us (22%)
  other arithmetic  41.5 us (8%)
  local copies, waits for them, and re-layouts  25.3 us (5%)
  between operations  14.4 us (3%)
  blocking collectives  12 us (2%)
    ppermute x3, waiting for transfers between devices, chain_scatter(): lax.ppermute(down.astype(BF16), axis, [(i, i - 1) for i in range(size - 1...  90.3 us
    ppermute x9, waiting for transfers between devices, chain_gather(): falling = tuple((lax.ppermute(block, axis, down) for block in falling))  55.3 us
    pallas_call x1, Pallas kernels, feed_forward(): pl.pallas_call(functools.partial(ffn_kernel, span, merged), grid=(steps,)...  43.9 us
    pallas_call x1, Pallas kernels, attend_backward(): pl.pallas_call(functools.partial(backward_kernel, heads, top), grid_spec=...  39.1 us
    ppermute x9, starting transfers between devices, chain_gather(): falling = tuple((lax.ppermute(block, axis, down) for block in falling))  29.4 us
    pallas_call x1, Pallas kernels, attend_forward(): pl.pallas_call(functools.partial(forward_kernel, heads, top), grid_spec=p...  21.4 us
    ppermute x9, starting transfers between devices, chain_gather(): rising = tuple((lax.ppermute(block, axis, up) for block in rising))  21.2 us
    all_to_all x1, starting transfers between devices, body(): late = lax.all_to_all(late, 'fsdp', 0, 0, tiled=True).astype(F32)  16.9 us
  transfers between devices with their start and end apart: 34, of which 13 were waited for; matrix products, arithmetic and copies ran while one was open for 11% of the time, Pallas kernels for 13%

profile of v4, /device:TPU:8, one launch (start us, length us, event | category | flops | bytes accessed | tf_op | source)
XLA Modules:
  0.0 513.5 jit_solution(7511195428251417793)
XLA Ops:
  12.6 12.0 %all_to_all.63 = bf16[4,40,768]{2,1,0:T(8,128)(2,1)} all-to-all(bf16[4,40,768]{2,1,0:T(8,128)(2,1)S(1)} %copy.68), channel_id=1, replica_groups=mesh['dp'=8,'fsdp'=4] {'fsdp'}, dimensions={0} | all-to-all | bytes 491520 | tf_op jit(solution)/shard_map/all_to_all | solution.py:597
  36.5 6.7 %collective-permute-done.1 = bf16[88,1024]{1,0:T(8,128)(2,1)S(1)} collective-permute-done((bf16[88,1024]{1,0:T(8,128)(2,1)S(1)}, bf16[88,1024]{1,0:T(8,128)(2,1)S(1)}, u32[]{:S(2)}, u32[]{:S(2)}) %collective-permute-start.1) | collective-permute-done | bytes 180256 | tf_op jit(solution)/shard_map/ppermute | solution.py:528
  48.0 4.6 collective-permute-start.5
  66.6 6.8 %collective-permute-done.17 = bf16[88,1024]{1,0:T(8,128)(2,1)} collective-permute-done((bf16[88,1024]{1,0:T(8,128)(2,1)}, bf16[88,1024]{1,0:T(8,128)(2,1)}, u32[]{:S(2)}, u32[]{:S(2)}) %collective-permute-start.17) | collective-permute-done | bytes 180256 | tf_op jit(solution)/shard_map/ppermute | solution.py:529
  77.3 4.5 collective-permute-start.11
  83.7 17.0 %collective-permute-done.11 = bf16[512,1024]{1,0:T(8,128)(2,1)S(1)} collective-permute-done((bf16[512,1024]{1,0:T(8,128)(2,1)S(1)}, bf16[512,1024]{1,0:T(8,128)(2,1)S(1)}, u32[]{:S(2)}, u32[]{:S(2)}) %collective-permute-start.11) | collective-permute-done | bytes 1048608 | tf_op jit(solution)/shard_map/ppermute | solution.py:529
  111.6 12.2 %collective-permute-done.12 = bf16[512,1024]{1,0:T(8,128)(2,1)} collective-permute-done((bf16[512,1024]{1,0:T(8,128)(2,1)S(1)}, bf16[512,1024]{1,0:T(8,128)(2,1)}, u32[]{:S(2)}, u32[]{:S(2)}) %collective-permute-start.12) | collective-permute-done | bytes 1048608 | tf_op jit(solution)/shard_map/ppermute | solution.py:529
  123.8 5.5 %collective-permute-start.13 = (bf16[512,1024]{1,0:T(8,128)(2,1)}, bf16[512,1024]{1,0:T(8,128)(2,1)}, u32[]{:S(2)}, u32[]{:S(2)}) collective-permute-start(bf16[512,1024]{1,0:T(8,128)(2,1)} %collective-permute-done.12), channel_id=1, source_target_pairs={{1,0},{5,4},{9,8},{13,12},{17,16},{21,20},{25,24},{29,28}} | collective-permute-start | bytes 3145736 | tf_op jit(solution)/shard_map/ppermute | solution.py:529
  144.3 15.1 %collective-permute-done.13 = bf16[512,1024]{1,0:T(8,128)(2,1)} collective-permute-done((bf16[512,1024]{1,0:T(8,128)(2,1)}, bf16[512,1024]{1,0:T(8,128)(2,1)}, u32[]{:S(2)}, u32[]{:S(2)}) %collective-permute-start.13) | collective-permute-done | bytes 1048608 | tf_op jit(solution)/shard_map/ppermute | solution.py:529
  163.8 7.4 %project_qkv.1.q_ref.k_ref.v_ref = bf16[2048,768]{1,0:T(8,128)(2,1)} custom-call(bf16[2048,1024]{1,0:T(8,128)(2,1)} %pad_maximum_fusion.tok_ref, f32[1,1024]{1,0:T(1,128)S(1)} %reshape.172.gain_ref, bf16[1024,768]{1,0:T(8,128)(2,1)S(1)} %bitcast.77, f32[2048,128]{1,0:T(8,128)S(1)} %get-tuple-element.99.cos_ref, f32[2048,128]{1,0:T(8,128)S(1)} %copy-done.1), custom_call_target="tpu_custom_call" | custom-call | flops 3221225472 | bytes 14680064 | tf_op jit(solution)/shard_map/project_qkv/pallas_call | solution.py:60
  171.3 21.4 %attend_forward.1 = (bf16[2048,256]{1,0:T(8,128)(2,1)}, f32[2048,2]{1,0:T(8,128)S(1)}) custom-call(s32[32]{0:T(128)S(1)} %reshape_squeeze.24.chosen_ref, s32[32]{0:T(128)S(1)} %reshape_squeeze.25.counts_ref, bf16[2048,768]{1,0:T(8,128)(2,1)} %project_qkv.1.q_ref.k_ref.v_ref, bf16[2048,768]{1,0:T(8,128)(2,1)} %project_qkv.1.q_ref.k_ref.v_ref, ...), custom_call_target="tpu_custom_call" | custom-call | flops 3221225472 | bytes 4194304 | tf_op jit(solution)/shard_map/attend_forward/pallas_call | solution.py:155
  193.6 7.3 %all-to-all-start.2 = ((bf16[4,512,256]{2,1,0:T(8,128)(2,1)}), bf16[4,512,256]{2,1,0:T(8,128)(2,1)S(1)}, u32[]{:S(2)}, u32[]{:S(2)}) async-start(bf16[4,512,256]{2,1,0:T(8,128)(2,1)} %bitcast.8), calls=%async_computation.2 | async-start | bytes 2097152 | tf_op jit(solution)/shard_map/all_to_all | solution.py:619
  201.6 12.0 %all-to-all-done.2 = bf16[4,512,256]{2,1,0:T(8,128)(2,1)S(1)} async-done(((bf16[4,512,256]{2,1,0:T(8,128)(2,1)}), bf16[4,512,256]{2,1,0:T(8,128)(2,1)S(1)}, u32[]{:S(2)}, u32[]{:S(2)}) %all-to-all-start.2) | async-done | bytes 1048608 | tf_op jit(solution)/shard_map/all_to_all | solution.py:619
  214.7 43.9 %feed_forward.1 = (bf16[512,1024]{1,0:T(8,128)(2,1)}, f32[512,1024]{1,0:T(8,128)}, bf16[512,1024]{1,0:T(8,128)(2,1)}, f32[1,1024]{1,0:T(1,128)}, bf16[8,4736,256]{2,1,0:T(8,128)(2,1)}) custom-call(bf16[512,1024]{1,0:T(8,128)(2,1)} %bitcast.80, bf16[512,1024]{1,0:T(8,128)(2,1)} %bitcast.96, bf16[512,1024]{1,0:T(8,128)(2,1)} %bitcast.109, ...), custom_call_target="tpu_custom_call" | custom-call | flops 29796335616 | bytes 38797312 | tf_op jit(solution)/shard_map/feed_forward/pallas_call | solution.py:478
  260.9 6.8 %all-to-all-start.3 = ((bf16[512,4,256]{2,0,1:T(8,128)(2,1)}), bf16[512,4,256]{2,0,1:T(8,128)(2,1)S(1)}, u32[]{:S(2)}, u32[]{:S(2)}) async-start(bf16[512,4,256]{2,0,1:T(8,128)(2,1)} %bitcast.73), calls=%async_computation.3 | async-start | bytes 2097152 | tf_op jit(solution)/shard_map/all_to_all | solution.py:625
  267.7 12.7 %all-to-all-done.3 = bf16[512,4,256]{2,0,1:T(8,128)(2,1)S(1)} async-done(((bf16[512,4,256]{2,0,1:T(8,128)(2,1)}), bf16[512,4,256]{2,0,1:T(8,128)(2,1)S(1)}, u32[]{:S(2)}, u32[]{:S(2)}) %all-to-all-start.3) | async-done | bytes 1048608 | tf_op jit(solution)/shard_map/all_to_all | solution.py:625
  281.9 39.1 %attend_backward.1 = (bf16[2048,1024]{1,0:T(8,128)(2,1)}, bf16[1024,768]{1,0:T(8,128)(2,1)}, f32[1,1024]{1,0:T(1,128)S(1)}) custom-call(s32[32]{0:T(128)S(1)} %reshape_squeeze.24.chosen_ref, s32[32]{0:T(128)S(1)} %reshape_squeeze.25.counts_ref, bf16[2048,768]{1,0:T(8,128)(2,1)} %project_qkv.1.q_ref.k_ref.v_ref, ...), custom_call_target="tpu_custom_call" | custom-call | flops 8053063680 | bytes 8388608 | tf_op jit(solution)/shard_map/attend_backward/pallas_call | solution.py:293
  336.5 6.2 %collective-permute-done.18 = bf16[512,1024]{1,0:T(8,128)(2,1)} collective-permute-done((bf16[512,1024]{1,0:T(8,128)(2,1)S(1)}, bf16[512,1024]{1,0:T(8,128)(2,1)}, u32[]{:S(2)}, u32[]{:S(2)}) %collective-permute-start.18) | collective-permute-done | bytes 1048608 | tf_op jit(solution)/shard_map/ppermute | solution.py:564
  342.7 27.4 %collective-permute-done.22 = bf16[512,1024]{1,0:T(8,128)(2,1)} collective-permute-done((bf16[512,1024]{1,0:T(8,128)(2,1)}, bf16[512,1024]{1,0:T(8,128)(2,1)}, u32[]{:S(2)}, u32[]{:S(2)}) %collective-permute-start.22) | collective-permute-done | bytes 1048608 | tf_op jit(solution)/shard_map/ppermute | solution.py:565
  370.1 4.5 add_convert_fusion
  379.6 16.9 %all-to-all-start.5 = ((bf16[4,40,768]{2,1,0:T(8,128)(2,1)}), bf16[4,40,768]{2,1,0:T(8,128)(2,1)S(1)}, u32[]{:S(2)}, u32[]{:S(2)}) async-start(bf16[4,40,768]{2,1,0:T(8,128)(2,1)} %fusion.9), calls=%async_computation.6 | async-start | bytes 491520 | tf_op jit(solution)/shard_map/all_to_all | solution.py:642
  396.5 8.6 %reduce-scatter.2.cloned.1.call-done = bf16[1,4736,256]{2,1,0:T(8,128)(2,1)} async-done(((bf16[8,4736,256]{2,1,0:T(8,128)(2,1)}), bf16[1,4736,256]{2,1,0:T(8,128)(2,1)}) %reduce-scatter.2.cloned.1.call-update) | async-done | bytes 2424848 | tf_op jit(solution)/shard_map/reduce_scatter | solution.py:626
  410.3 10.9 %all-to-all-start.6 = ((bf16[4,1184,256]{2,1,0:T(8,128)(2,1)}), bf16[4,1184,256]{2,1,0:T(8,128)(2,1)S(1)}, u32[]{:S(2)}, u32[]{:S(2)}) async-start(bf16[4,1184,256]{2,1,0:T(8,128)(2,1)} %pad_maximum_fusion.1), calls=%async_computation.7 | async-start | bytes 4849664 | tf_op jit(solution)/shard_map/all_to_all | solution.py:668
  434.9 62.9 %collective-permute-done.23 = bf16[512,1024]{1,0:T(8,128)(2,1)} collective-permute-done((bf16[512,1024]{1,0:T(8,128)(2,1)}, bf16[512,1024]{1,0:T(8,128)(2,1)}, u32[]{:S(2)}, u32[]{:S(2)}) %collective-permute-start.23) | collective-permute-done | bytes 1048608 | tf_op jit(solution)/shard_map/ppermute | solution.py:565
  (170 shorter events, 126.9 us)
Async XLA Ops:
  7.2 134.4 %all-gather.4.cloned.1.call-start = ((), (), s32[]{:S(2)}) async-start(), calls=%async_computation.8 | async-start | bytes 2211840 | tf_op jit(solution)/shard_map/all_gather | solution.py:603
  24.6 190.1 %all-gather.8.cloned.1.call-start = ((), (), s32[]{:S(2)}) async-start(), calls=%async_computation.10 | async-start | bytes 6488064 | tf_op jit(solution)/shard_map/all_gather | solution.py:614
  24.7 18.4 %collective-permute-start.2 = (bf16[32,6656]{1,0:T(8,128)(2,1)S(1)}, bf16[32,6656]{1,0:T(8,128)(2,1)S(1)}, u32[]{:S(2)}, u32[]{:S(2)}) collective-permute-start(bf16[32,6656]{1,0:T(8,128)(2,1)S(1)} %constant_dynamic-update-slice_fusion), channel_id=1, source_target_pairs={{1,0},{2,1},{3,2},{5,4},{6,5},{7,6},{9,8},{10,9},{11,10},{13,12},{... | collective-permute-start | bytes 1277960 | tf_op jit(solution)/shard_map/ppermute | solution.py:529
  28.4 14.7 %collective-permute-start = (bf16[32,6656]{1,0:T(8,128)(2,1)S(1)}, bf16[32,6656]{1,0:T(8,128)(2,1)S(1)}, u32[]{:S(2)}, u32[]{:S(2)}) collective-permute-start(bf16[32,6656]{1,0:T(8,128)(2,1)S(1)} %constant_dynamic-update-slice_fusion), channel_id=1, source_target_pairs={{0,1},{1,2},{2,3},{4,5},{5,6},{6,7},{8,9},{9,10},{10,11},{12,13},{... | collective-permute-start | bytes 1277960 | tf_op jit(solution)/shard_map/ppermute | solution.py:528
  43.2 17.3 %collective-permute-start.4 = (bf16[32,6656]{1,0:T(8,128)(2,1)S(1)}, bf16[32,6656]{1,0:T(8,128)(2,1)S(1)}, u32[]{:S(2)}, u32[]{:S(2)}) collective-permute-start(bf16[32,6656]{1,0:T(8,128)(2,1)S(1)} %collective-permute-done), channel_id=1, source_target_pairs={{1,2},{2,3},{5,6},{6,7},{9,10},{10,11},{13,14},{14,15},{17,18},{18... | collective-permute-start | bytes 1277960 | tf_op jit(solution)/shard_map/ppermute | solution.py:528
  75.5 139.2 %all-gather.6.cloned.1.call-start = ((), (), s32[]{:S(2)}) async-start(), calls=%async_computation.9 | async-start | bytes 15335424 | tf_op jit(solution)/shard_map/all_gather | solution.py:607
  77.3 23.4 %collective-permute-start.11 = (bf16[512,1024]{1,0:T(8,128)(2,1)S(1)}, bf16[512,1024]{1,0:T(8,128)(2,1)S(1)}, u32[]{:S(2)}, u32[]{:S(2)}) collective-permute-start(bf16[512,1024]{1,0:T(8,128)(2,1)S(1)} %bitcast.81), channel_id=1, source_target_pairs={{1,0},{2,1},{3,2},{5,4},{6,5},{7,6},{9,8},{10,9},{11,10},{13,12},{... | collective-permute-start | bytes 3145736 | tf_op jit(solution)/shard_map/ppermute | solution.py:529
  81.8 23.3 %collective-permute-start.8 = (bf16[512,1024]{1,0:T(8,128)(2,1)S(1)}, bf16[512,1024]{1,0:T(8,128)(2,1)}, u32[]{:S(2)}, u32[]{:S(2)}) collective-permute-start(bf16[512,1024]{1,0:T(8,128)(2,1)S(1)} %bitcast.82), channel_id=1, source_target_pairs={{0,1},{1,2},{2,3},{4,5},{5,6},{6,7},{8,9},{9,10},{10,11},{12,13},{... | collective-permute-start | bytes 3145736 | tf_op jit(solution)/shard_map/ppermute | solution.py:528
  100.8 23.0 %collective-permute-start.12 = (bf16[512,1024]{1,0:T(8,128)(2,1)S(1)}, bf16[512,1024]{1,0:T(8,128)(2,1)}, u32[]{:S(2)}, u32[]{:S(2)}) collective-permute-start(bf16[512,1024]{1,0:T(8,128)(2,1)S(1)} %collective-permute-done.11), channel_id=1, source_target_pairs={{1,0},{2,1},{5,4},{6,5},{9,8},{10,9},{13,12},{14,13},{17,16},{18,1... | collective-permute-start | bytes 3145736 | tf_op jit(solution)/shard_map/ppermute | solution.py:529
  105.2 24.1 %collective-permute-start.9 = (bf16[512,1024]{1,0:T(8,128)(2,1)}, bf16[512,1024]{1,0:T(8,128)(2,1)}, u32[]{:S(2)}, u32[]{:S(2)}) collective-permute-start(bf16[512,1024]{1,0:T(8,128)(2,1)} %collective-permute-done.8), channel_id=1, source_target_pairs={{1,2},{2,3},{5,6},{6,7},{9,10},{10,11},{13,14},{14,15},{17,18},{18... | collective-permute-start | bytes 3145736 | tf_op jit(solution)/shard_map/ppermute | solution.py:528
  123.8 35.6 %collective-permute-start.13 = (bf16[512,1024]{1,0:T(8,128)(2,1)}, bf16[512,1024]{1,0:T(8,128)(2,1)}, u32[]{:S(2)}, u32[]{:S(2)}) collective-permute-start(bf16[512,1024]{1,0:T(8,128)(2,1)} %collective-permute-done.12), channel_id=1, source_target_pairs={{1,0},{5,4},{9,8},{13,12},{17,16},{21,20},{25,24},{29,28}} | collective-permute-start | bytes 3145736 | tf_op jit(solution)/shard_map/ppermute | solution.py:529
  129.2 30.1 %collective-permute-start.10 = (bf16[512,1024]{1,0:T(8,128)(2,1)}, bf16[512,1024]{1,0:T(8,128)(2,1)}, u32[]{:S(2)}, u32[]{:S(2)}) collective-permute-start(bf16[512,1024]{1,0:T(8,128)(2,1)} %collective-permute-done.9), channel_id=1, source_target_pairs={{2,3},{6,7},{10,11},{14,15},{18,19},{22,23},{26,27},{30,31}} | collective-permute-start | bytes 3145736 | tf_op jit(solution)/shard_map/ppermute | solution.py:528
  137.0 34.3 %all-to-all-start.1 = ((bf16[4,256,512]{2,1,0:T(8,128)(2,1)}), bf16[4,256,512]{2,1,0:T(8,128)(2,1)}, u32[]{:S(2)}, u32[]{:S(2)}) async-start(bf16[4,256,512]{2,1,0:T(8,128)(2,1)} %pad_maximum_fusion.5), calls=%async_computation.1 | async-start | bytes 2097152 | tf_op jit(solution)/shard_map/all_to_all | solution.py:613
  193.6 20.0 %all-to-all-start.2 = ((bf16[4,512,256]{2,1,0:T(8,128)(2,1)}), bf16[4,512,256]{2,1,0:T(8,128)(2,1)S(1)}, u32[]{:S(2)}, u32[]{:S(2)}) async-start(bf16[4,512,256]{2,1,0:T(8,128)(2,1)} %bitcast.8), calls=%async_computation.2 | async-start | bytes 2097152 | tf_op jit(solution)/shard_map/all_to_all | solution.py:619
  200.9 204.1 %reduce-scatter.2.cloned.1.call-start = ((), (), s32[]{:S(2)}) async-start(), calls=%async_computation.11 | async-start | bytes 21823488 | tf_op jit(solution)/shard_map/reduce_scatter | solution.py:626
  260.9 19.5 %all-to-all-start.3 = ((bf16[512,4,256]{2,0,1:T(8,128)(2,1)}), bf16[512,4,256]{2,0,1:T(8,128)(2,1)S(1)}, u32[]{:S(2)}, u32[]{:S(2)}) async-start(bf16[512,4,256]{2,0,1:T(8,128)(2,1)} %bitcast.73), calls=%async_computation.3 | async-start | bytes 2097152 | tf_op jit(solution)/shard_map/all_to_all | solution.py:625
  325.8 16.9 %collective-permute-start.18 = (bf16[512,1024]{1,0:T(8,128)(2,1)S(1)}, bf16[512,1024]{1,0:T(8,128)(2,1)}, u32[]{:S(2)}, u32[]{:S(2)}) collective-permute-start(bf16[512,1024]{1,0:T(8,128)(2,1)S(1)} %get-tuple-element.74), channel_id=1, source_target_pairs={{0,1},{4,5},{8,9},{12,13},{16,17},{20,21},{24,25},{28,29}} | collective-permute-start | bytes 3145736 | tf_op jit(solution)/shard_map/ppermute | solution.py:564
  330.2 39.9 %collective-permute-start.22 = (bf16[512,1024]{1,0:T(8,128)(2,1)}, bf16[512,1024]{1,0:T(8,128)(2,1)}, u32[]{:S(2)}, u32[]{:S(2)}) collective-permute-start(bf16[512,1024]{1,0:T(8,128)(2,1)} %add_convert_fusion.1), channel_id=1, source_target_pairs={{2,1},{3,2},{6,5},{7,6},{10,9},{11,10},{14,13},{15,14},{18,17},{19... | collective-permute-start | bytes 3145736 | tf_op jit(solution)/shard_map/ppermute | solution.py:565
  332.9 45.6 %all-to-all-start.4 = ((bf16[8,136,768]{2,1,0:T(8,128)(2,1)}), bf16[8,136,768]{2,1,0:T(8,128)(2,1)S(1)}, u32[]{:S(2)}, u32[]{:S(2)}) async-start(bf16[8,136,768]{2,1,0:T(8,128)(2,1)} %fusion.5), calls=%async_computation.5 | async-start | bytes 3342336 | tf_op jit(solution)/shard_map/all_to_all | solution.py:638
  374.6 21.9 %collective-permute-start.19 = (bf16[512,1024]{1,0:T(8,128)(2,1)}, bf16[512,1024]{1,0:T(8,128)(2,1)S(1)}, u32[]{:S(2)}, u32[]{:S(2)}) collective-permute-start(bf16[512,1024]{1,0:T(8,128)(2,1)} %get-tuple-element.72), channel_id=1, source_target_pairs={{0,1},{1,2},{4,5},{5,6},{8,9},{9,10},{12,13},{13,14},{16,17},{17,1... | collective-permute-start | bytes 3145736 | tf_op jit(solution)/shard_map/ppermute | solution.py:564
  379.6 30.0 %all-to-all-start.5 = ((bf16[4,40,768]{2,1,0:T(8,128)(2,1)}), bf16[4,40,768]{2,1,0:T(8,128)(2,1)S(1)}, u32[]{:S(2)}, u32[]{:S(2)}) async-start(bf16[4,40,768]{2,1,0:T(8,128)(2,1)} %fusion.9), calls=%async_computation.6 | async-start | bytes 491520 | tf_op jit(solution)/shard_map/all_to_all | solution.py:642
  410.3 93.8 %all-to-all-start.6 = ((bf16[4,1184,256]{2,1,0:T(8,128)(2,1)}), bf16[4,1184,256]{2,1,0:T(8,128)(2,1)S(1)}, u32[]{:S(2)}, u32[]{:S(2)}) async-start(bf16[4,1184,256]{2,1,0:T(8,128)(2,1)} %pad_maximum_fusion.1), calls=%async_computation.7 | async-start | bytes 4849664 | tf_op jit(solution)/shard_map/all_to_all | solution.py:668
  421.2 76.6 %collective-permute-start.23 = (bf16[512,1024]{1,0:T(8,128)(2,1)}, bf16[512,1024]{1,0:T(8,128)(2,1)}, u32[]{:S(2)}, u32[]{:S(2)}) collective-permute-start(bf16[512,1024]{1,0:T(8,128)(2,1)} %get-tuple-element.71), channel_id=1, source_target_pairs={{1,0},{2,1},{3,2},{5,4},{6,5},{7,6},{9,8},{10,9},{11,10},{13,12},{... | collective-permute-start | bytes 3145736 | tf_op jit(solution)/shard_map/ppermute | solution.py:565
  426.2 71.5 %collective-permute-start.20 = (bf16[512,1024]{1,0:T(8,128)(2,1)}, bf16[512,1024]{1,0:T(8,128)(2,1)}, u32[]{:S(2)}, u32[]{:S(2)}) collective-permute-start(bf16[512,1024]{1,0:T(8,128)(2,1)} %add_convert_fusion.2), channel_id=1, source_target_pairs={{0,1},{1,2},{2,3},{4,5},{5,6},{6,7},{8,9},{9,10},{10,11},{12,13},{... | collective-permute-start | bytes 3145736 | tf_op jit(solution)/shard_map/ppermute | solution.py:564
  (27 other events, 398.7 us)
Sparse Core Ops, SparseCore 0:
  24.7 27.6 all-gather.3
  75.6 43.5 all-gather.7
  121.1 76.5 all-gather.5
  258.8 146.2 reduce-scatter.1

commit v5 on v4

--- a/solution.py
+++ b/solution.py
@@ -7,6 +7,7 @@
 from jax import lax
 from jax.experimental import pallas as pl
 from jax.experimental.pallas import tpu as pltpu
+from jax.sharding import Mesh
 from jax.sharding import PartitionSpec as P
 
 HEAD_DIM = 128
@@ -19,6 +20,7 @@
 MIB = 1 << 20
 F32 = jnp.float32
 BF16 = jnp.bfloat16
+DP = ("chip", "core")
 NT = (((1,), (1,)), ((), ()))
 TN = (((0,), (0,)), ((), ()))
 
@@ -561,10 +563,10 @@
         up, down = block(size - 1 - step + place), block(step - size + 1 + place)
         if step:
             up, down = up + rising.astype(F32), down + falling.astype(F32)
-        rising = lax.ppermute(up.astype(BF16), axis, [(i, i + 1) for i in range(step + 1)])
-        falling = lax.ppermute(
-            down.astype(BF16), axis, [(i, i - 1) for i in range(size - 1 - step, size)]
-        )
+        up, down = lax.optimization_barrier((up.astype(BF16), down.astype(BF16)))
+        rising = lax.ppermute(up, axis, [(i, i + 1) for i in range(step + 1)])
+        falling = lax.ppermute(down, axis, [(i, i - 1) for i in range(size - 1 - step, size)])
+        rising, falling = lax.optimization_barrier((rising, falling))
         steps.append((rising, falling))
     return block(place), steps
 
@@ -573,7 +575,7 @@
     tokens, memory_keys, memory_values, chosen, counts, w_query, w_key, w_value, w_out, w_gate, w_up, w_down,
     gain_attn, gain_ffn, cotangent,
 ):
-    ring, span = lax.axis_size("fsdp"), lax.axis_size("dp")
+    ring, span = lax.axis_size("fsdp"), lax.axis_size(DP)
     rows, width = tokens.shape[1:]
     heads = width // HEAD_DIM // ring
     wide = heads * HEAD_DIM
@@ -600,18 +602,18 @@
     shards = jnp.concatenate([w_out, w_gate, w_up], 1)
     (near, near_down), steps = chain_gather((shards, w_down), "fsdp")
     (gathered,), token_steps = chain_gather((after(mine, steps[-2]),), "fsdp")
-    parcel = lax.all_gather(parcel, "dp", axis=0, tiled=True)
+    parcel = lax.all_gather(parcel, DP, axis=0, tiled=True)
     w_qkv = parcel[:, :share].reshape(width, 3 * wide)
     gain_one = parcel[:, share, :share].reshape(1, width).astype(F32)
     gain_two = parcel[:, share, share : 2 * share].reshape(1, width).astype(F32)
-    first = lax.all_gather(jnp.concatenate(near, 0), "dp", axis=0, tiled=True)
+    first = lax.all_gather(jnp.concatenate(near, 0), DP, axis=0, tiled=True)
     gathered = jnp.concatenate(gathered, 0)
 
     memory = jnp.concatenate(
         [m[0].reshape(-1, ring, wide).transpose(1, 0, 2) for m in (memory_keys, memory_values)], 2
     )
     memory = lax.all_to_all(after(memory, token_steps[-2]), "fsdp", 0, 0, tiled=True).reshape(-1, 2 * wide)
-    down_full = lax.all_gather(jnp.concatenate(near_down, 0), "dp", axis=0, tiled=True)
+    down_full = lax.all_gather(jnp.concatenate(near_down, 0), DP, axis=0, tiled=True)
 
     cosine, sine = rotary_tables(length)
     qkv = project_qkv(gathered, gain_one, w_qkv, cosine, sine, heads)
@@ -623,19 +625,24 @@
         mine, attended, upstream, gain_two, first, down_full, span
     )
     grad_heads = lax.all_to_all(grad_attended, "fsdp", 1, 0, tiled=True)
-    grads = lax.psum_scatter(grads, "dp", scatter_dimension=0, tiled=True)[0]
+    grads = lax.psum_scatter(grads, DP, scatter_dimension=0, tiled=True)[0]
 
     partial, grad_w_qkv, gain_one_grad = attend_backward(
         chosen_all, counts_all, qkv, memory, grad_heads, attended_heads, lse, cosine, sine, gathered, gain_one,
         w_qkv, heads, top,
     )
     own_term, steps = chain_scatter(partial, "fsdp")
-    grads = after(grads, steps[-2])
+    grads = after(grads, steps[-1])
 
     gains = jnp.concatenate([gain_one_grad, gain_two_grad], 0).reshape(2, span, -1).transpose(1, 0, 2)
     gains = jnp.pad(gains.astype(BF16), ((0, 0), (0, extra - 2), (0, 3 * wide - gains.shape[2])))
     late = jnp.concatenate([grad_w_qkv.reshape(span, -1, 3 * wide), gains], 1)
-    late = jnp.sum(lax.all_to_all(late, "dp", 0, 0, tiled=True).astype(F32), 0).astype(BF16)
+    late = late.reshape(span // 2, 2, late.shape[1], 3 * wide)
+    core = lax.axis_index("core")
+    taken = lax.ppermute(lax.dynamic_index_in_dim(late, 1 - core, 1, keepdims=False), "core", [(0, 1), (1, 0)])
+    late = lax.dynamic_index_in_dim(late, core, 1, keepdims=False).astype(F32) + taken.astype(F32)
+    late = after(late.astype(BF16), steps[0])
+    late = jnp.sum(lax.all_to_all(late, "chip", 0, 0, tiled=True).astype(F32), 0).astype(BF16)
     gains = late[-extra : 2 - extra, : ring * share].reshape(2, ring, share).transpose(1, 0, 2)
     gains = jnp.pad(gains, ((0, 0), (0, extra - 2), (0, 3 * wide - share)))
     late = jnp.concatenate([late[:-extra].reshape(ring, share, 3 * wide), gains], 1)
@@ -650,14 +657,14 @@
     lanes = width // strip
     tall = w_down.shape[0]
     if grad_down:
-        down = lax.psum_scatter(grad_down[0], "dp", scatter_dimension=0, tiled=True)
+        down = lax.psum_scatter(grad_down[0], DP, scatter_dimension=0, tiled=True)
         down = down.reshape(ring, tall, lanes, strip).transpose(0, 2, 1, 3)
     else:
         down = grads[: ring * tall * lanes].reshape(lanes, ring, tall, strip).transpose(1, 0, 2, 3)
         grads = grads[ring * tall * lanes :]
     grads = grads.reshape(-1, ring, share, strip).transpose(1, 0, 2, 3)
     pieces = jnp.concatenate([down.reshape(ring, -1, strip), grads.reshape(ring, -1, strip)], 1)
-    rising, falling = after(steps[-1], pieces)
+    rising, falling = steps[-1]
     grad_normed = own_term + rising.astype(F32) + falling.astype(F32)
     own = mine.astype(F32)
     factor = lax.rsqrt(jnp.mean(own * own, -1, keepdims=True) + EPSILON)
@@ -665,7 +672,7 @@
     inner = jnp.mean(scaled * own, -1, keepdims=True)
     tokens_grad = (grad_middle + factor * scaled - own * (factor * factor * factor * inner)).astype(BF16)
 
-    pieces = jnp.sum(lax.all_to_all(pieces, "fsdp", 0, 0, tiled=True).astype(F32), 0)
+    pieces = lax.psum_scatter(pieces, "fsdp", scatter_dimension=0, tiled=True)[0].astype(F32)
     down_share = pieces[: lanes * tall].reshape(lanes, tall, strip).transpose(1, 0, 2).reshape(tall, width)
     others = pieces[lanes * tall :].reshape(-1, share, strip).transpose(1, 0, 2).reshape(share, -1)
     return (
@@ -682,8 +689,10 @@
 
 
 def solution(mesh):
-    both = ("dp", "fsdp")
-    rows, matrix, vector = P("dp", "fsdp", None), P(both, None), P(both)
+    span, ring = mesh.shape["dp"], mesh.shape["fsdp"]
+    fine = Mesh(mesh.devices.reshape(span // 2, 2, ring), DP + ("fsdp",))
+    every = DP + ("fsdp",)
+    rows, matrix, vector = P(DP, "fsdp", None), P(every, None), P(every)
     in_specs = (rows,) * 5 + (matrix,) * 7 + (vector,) * 2 + (rows,)
     out_specs = (rows,) * 2 + (matrix,) * 7 + (vector,) * 2
-    return jax.shard_map(body, mesh=mesh, in_specs=in_specs, out_specs=out_specs, check_vma=False)
+    return jax.shard_map(body, mesh=fine, in_specs=in_specs, out_specs=out_specs, check_vma=False)

time: 515 us -> 477 us (0.926)
  the two profiles are of different devices: /device:TPU:8 before, /device:TPU:0 now
where the time goes in v5:
time: 477 us; the launch traced here: 475 us
  waiting for transfers between devices  191 us (40%)
  Pallas kernels  111 us (23%)
  starting transfers between devices  67 us (14%)
  other arithmetic  35.4 us (7%)
  blocking collectives  30.5 us (6%)
  local copies, waits for them, and re-layouts  25.7 us (5%)
  between operations  14.4 us (3%)
    ppermute x9, waiting for transfers between devices, chain_gather(): falling = tuple((lax.ppermute(block, axis, down) for block in falling))  75.8 us
    ppermute x3, waiting for transfers between devices, chain_scatter(): rising = lax.ppermute(up, axis, [(i, i + 1) for i in range(step + 1)])  52.5 us
    pallas_call x1, Pallas kernels, feed_forward(): pl.pallas_call(functools.partial(ffn_kernel, span, merged), grid=(steps,)...  43.9 us
    pallas_call x1, Pallas kernels, attend_backward(): pl.pallas_call(functools.partial(backward_kernel, heads, top), grid_spec=...  38.7 us
    pallas_call x1, Pallas kernels, attend_forward(): pl.pallas_call(functools.partial(forward_kernel, heads, top), grid_spec=p...  21.4 us
    ppermute x9, starting transfers between devices, chain_gather(): rising = tuple((lax.ppermute(block, axis, up) for block in rising))  19.7 us
    all_to_all x1, blocking collectives, body(): lax.all_to_all(late, 'chip', 0, 0, tiled=True).astype(F32)  15.8 us
    all_to_all x1, waiting for transfers between devices, body(): grad_heads = lax.all_to_all(grad_attended, 'fsdp', 1, 0, tiled=True)  15.6 us
  transfers between devices with their start and end apart: 34, of which 15 were waited for; matrix products, arithmetic and copies ran while one was open for 9% of the time, Pallas kernels for 14%

profile of v5, /device:TPU:0, one launch (start us, length us, event | category | flops | bytes accessed | tf_op | source)
XLA Modules:
  0.0 475.2 jit_solution(7105664324364436720)
XLA Ops:
  12.6 14.7 %all_to_all.58 = bf16[4,40,768]{2,1,0:T(8,128)(2,1)} all-to-all(bf16[4,40,768]{2,1,0:T(8,128)(2,1)S(1)} %copy.68), channel_id=1, replica_groups=mesh['chip'=4,'core'=2,'fsdp'=4] {'fsdp'}, dimensions={0} | all-to-all | bytes 491520 | tf_op jit(solution)/shard_map/all_to_all | solution.py:599
  28.8 4.6 collective-permute-start
  36.8 6.8 %collective-permute-done.1 = bf16[88,1024]{1,0:T(8,128)(2,1)S(1)} collective-permute-done((bf16[88,1024]{1,0:T(8,128)(2,1)S(1)}, bf16[88,1024]{1,0:T(8,128)(2,1)S(1)}, u32[]{:S(2)}, u32[]{:S(2)}) %collective-permute-start.1) | collective-permute-done | bytes 180256 | tf_op jit(solution)/shard_map/ppermute | solution.py:530
  48.3 13.4 %collective-permute-done.7 = bf16[88,1024]{1,0:T(8,128)(2,1)} collective-permute-done((bf16[88,1024]{1,0:T(8,128)(2,1)S(1)}, bf16[88,1024]{1,0:T(8,128)(2,1)}, u32[]{:S(2)}, u32[]{:S(2)}) %collective-permute-start.7) | collective-permute-done | bytes 180256 | tf_op jit(solution)/shard_map/ppermute | solution.py:531
  66.3 10.6 %collective-permute-done.17 = bf16[88,1024]{1,0:T(8,128)(2,1)} collective-permute-done((bf16[88,1024]{1,0:T(8,128)(2,1)}, bf16[88,1024]{1,0:T(8,128)(2,1)}, u32[]{:S(2)}, u32[]{:S(2)}) %collective-permute-start.17) | collective-permute-done | bytes 180256 | tf_op jit(solution)/shard_map/ppermute | solution.py:531
  82.2 5.6 %collective-permute-start.8 = (bf16[512,1024]{1,0:T(8,128)(2,1)S(1)}, bf16[512,1024]{1,0:T(8,128)(2,1)}, u32[]{:S(2)}, u32[]{:S(2)}) collective-permute-start(bf16[512,1024]{1,0:T(8,128)(2,1)S(1)} %bitcast.90), channel_id=1, source_target_pairs={{0,1},{1,2},{2,3},{4,5},{5,6},{6,7},{8,9},{9,10},{10,11},{12,13},{... | collective-permute-start | bytes 3145736 | tf_op jit(solution)/shard_map/ppermute | solution.py:530
  87.8 16.5 %collective-permute-done.11 = bf16[512,1024]{1,0:T(8,128)(2,1)S(1)} collective-permute-done((bf16[512,1024]{1,0:T(8,128)(2,1)S(1)}, bf16[512,1024]{1,0:T(8,128)(2,1)S(1)}, u32[]{:S(2)}, u32[]{:S(2)}) %collective-permute-start.11) | collective-permute-done | bytes 1048608 | tf_op jit(solution)/shard_map/ppermute | solution.py:531
  110.2 17.1 %collective-permute-done.12 = bf16[512,1024]{1,0:T(8,128)(2,1)} collective-permute-done((bf16[512,1024]{1,0:T(8,128)(2,1)S(1)}, bf16[512,1024]{1,0:T(8,128)(2,1)}, u32[]{:S(2)}, u32[]{:S(2)}) %collective-permute-start.12) | collective-permute-done | bytes 1048608 | tf_op jit(solution)/shard_map/ppermute | solution.py:531
  136.4 5.3 %all-to-all-start.1 = ((bf16[4,256,512]{2,1,0:T(8,128)(2,1)}), bf16[4,256,512]{2,1,0:T(8,128)(2,1)}, u32[]{:S(2)}, u32[]{:S(2)}) async-start(bf16[4,256,512]{2,1,0:T(8,128)(2,1)} %pad_maximum_fusion.5), calls=%async_computation.1 | async-start | bytes 2097152 | tf_op jit(solution)/shard_map/all_to_all | solution.py:615
  144.6 18.3 %collective-permute-done.13 = bf16[512,1024]{1,0:T(8,128)(2,1)} collective-permute-done((bf16[512,1024]{1,0:T(8,128)(2,1)}, bf16[512,1024]{1,0:T(8,128)(2,1)}, u32[]{:S(2)}, u32[]{:S(2)}) %collective-permute-start.13) | collective-permute-done | bytes 1048608 | tf_op jit(solution)/shard_map/ppermute | solution.py:531
  167.6 7.4 %project_qkv.1.q_ref.k_ref.v_ref = bf16[2048,768]{1,0:T(8,128)(2,1)} custom-call(bf16[2048,1024]{1,0:T(8,128)(2,1)} %pad_maximum_fusion.tok_ref, f32[1,1024]{1,0:T(1,128)S(1)} %reshape.180.gain_ref, bf16[1024,768]{1,0:T(8,128)(2,1)S(1)} %bitcast.85, f32[2048,128]{1,0:T(8,128)S(1)} %get-tuple-element.123.cos_ref, f32[2048,128]{1,0:T(8,128)S(1)} %copy-done.1), custom_call_target="tpu_custom_call" | custom-call | flops 3221225472 | bytes 14680064 | tf_op jit(solution)/shard_map/project_qkv/pallas_call | solution.py:62
  175.0 21.4 %attend_forward.1 = (bf16[2048,256]{1,0:T(8,128)(2,1)}, f32[2048,2]{1,0:T(8,128)S(1)}) custom-call(s32[32]{0:T(128)S(1)} %reshape_squeeze.24.chosen_ref, s32[32]{0:T(128)S(1)} %reshape_squeeze.25.counts_ref, bf16[2048,768]{1,0:T(8,128)(2,1)} %project_qkv.1.q_ref.k_ref.v_ref, bf16[2048,768]{1,0:T(8,128)(2,1)} %project_qkv.1.q_ref.k_ref.v_ref, ...), custom_call_target="tpu_custom_call" | custom-call | flops 3221225472 | bytes 4194304 | tf_op jit(solution)/shard_map/attend_forward/pallas_call | solution.py:157
  197.3 4.5 all-to-all-start.2
  202.6 15.2 %all-to-all-done.2 = bf16[4,512,256]{2,1,0:T(8,128)(2,1)S(1)} async-done(((bf16[4,512,256]{2,1,0:T(8,128)(2,1)}), bf16[4,512,256]{2,1,0:T(8,128)(2,1)S(1)}, u32[]{:S(2)}, u32[]{:S(2)}) %all-to-all-start.2) | async-done | bytes 1048608 | tf_op jit(solution)/shard_map/all_to_all | solution.py:621
  218.9 43.9 %feed_forward.1 = (bf16[512,1024]{1,0:T(8,128)(2,1)}, f32[512,1024]{1,0:T(8,128)}, bf16[512,1024]{1,0:T(8,128)(2,1)}, f32[1,1024]{1,0:T(1,128)}, bf16[8,4736,256]{2,1,0:T(8,128)(2,1)}) custom-call(bf16[512,1024]{1,0:T(8,128)(2,1)} %bitcast.88, bf16[512,1024]{1,0:T(8,128)(2,1)} %bitcast.105, bf16[512,1024]{1,0:T(8,128)(2,1)} %bitcast.120, ...), custom_call_target="tpu_custom_call" | custom-call | flops 29796335616 | bytes 38797312 | tf_op jit(solution)/shard_map/feed_forward/pallas_call | solution.py:480
  269.0 15.6 %all-to-all-done.3 = bf16[512,4,256]{2,0,1:T(8,128)(2,1)S(1)} async-done(((bf16[512,4,256]{2,0,1:T(8,128)(2,1)}), bf16[512,4,256]{2,0,1:T(8,128)(2,1)S(1)}, u32[]{:S(2)}, u32[]{:S(2)}) %all-to-all-start.3) | async-done | bytes 1048608 | tf_op jit(solution)/shard_map/all_to_all | solution.py:627
  286.1 38.7 %attend_backward.1 = (bf16[2048,1024]{1,0:T(8,128)(2,1)}, bf16[1024,768]{1,0:T(8,128)(2,1)}, f32[1,1024]{1,0:T(1,128)S(1)}) custom-call(s32[32]{0:T(128)S(1)} %reshape_squeeze.24.chosen_ref, s32[32]{0:T(128)S(1)} %reshape_squeeze.25.counts_ref, bf16[2048,768]{1,0:T(8,128)(2,1)} %project_qkv.1.q_ref.k_ref.v_ref, ...), custom_call_target="tpu_custom_call" | custom-call | flops 8053063680 | bytes 8388608 | tf_op jit(solution)/shard_map/attend_backward/pallas_call | solution.py:295
  329.5 21.8 %collective-permute-done.18 = bf16[512,1024]{1,0:T(8,128)(2,1)S(1)} collective-permute-done((bf16[512,1024]{1,0:T(8,128)(2,1)S(1)}, bf16[512,1024]{1,0:T(8,128)(2,1)S(1)}, u32[]{:S(2)}, u32[]{:S(2)}) %collective-permute-start.18) | collective-permute-done | bytes 1048608 | tf_op jit(solution)/shard_map/ppermute | solution.py:567
  360.3 20.8 %collective-permute-done.20 = bf16[512,1024]{1,0:T(8,128)(2,1)S(1)} collective-permute-done((bf16[512,1024]{1,0:T(8,128)(2,1)}, bf16[512,1024]{1,0:T(8,128)(2,1)S(1)}, u32[]{:S(2)}, u32[]{:S(2)}) %collective-permute-start.20) | collective-permute-done | bytes 1048608 | tf_op jit(solution)/shard_map/ppermute | solution.py:567
  383.6 9.1 %collective-permute-start.22 = (bf16[512,1024]{1,0:T(8,128)(2,1)S(1)}, bf16[512,1024]{1,0:T(8,128)(2,1)}, u32[]{:S(2)}, u32[]{:S(2)}) collective-permute-start(bf16[512,1024]{1,0:T(8,128)(2,1)S(1)} %get-tuple-element.77), channel_id=1, source_target_pairs={{0,1},{1,2},{2,3},{4,5},{5,6},{6,7},{8,9},{9,10},{10,11},{12,13},{... | collective-permute-start | bytes 3145736 | tf_op jit(solution)/shard_map/ppermute | solution.py:567
  393.9 10.0 %collective-permute-done.22 = bf16[512,1024]{1,0:T(8,128)(2,1)} collective-permute-done((bf16[512,1024]{1,0:T(8,128)(2,1)S(1)}, bf16[512,1024]{1,0:T(8,128)(2,1)}, u32[]{:S(2)}, u32[]{:S(2)}) %collective-permute-start.22) | collective-permute-done | bytes 1048608 | tf_op jit(solution)/shard_map/ppermute | solution.py:567
  403.9 5.5 %collective-permute-done.23 = bf16[512,1024]{1,0:T(8,128)(2,1)} collective-permute-done((bf16[512,1024]{1,0:T(8,128)(2,1)S(1)}, bf16[512,1024]{1,0:T(8,128)(2,1)}, u32[]{:S(2)}, u32[]{:S(2)}) %collective-permute-start.23) | collective-permute-done | bytes 1048608 | tf_op jit(solution)/shard_map/ppermute | solution.py:568
  418.1 15.8 %all_to_all.59 = bf16[4,136,768]{2,1,0:T(8,128)(2,1)S(1)} all-to-all(bf16[4,136,768]{2,1,0:T(8,128)(2,1)S(1)} %fusion.4), channel_id=1, replica_groups=mesh['chip'=4,'core'=2,'fsdp'=4] {'chip'}, dimensions={0} | all-to-all | bytes 1671168 | tf_op jit(solution)/shard_map/all_to_all | solution.py:645
  439.2 15.2 %all-to-all-done.5 = bf16[4,40,768]{2,1,0:T(8,128)(2,1)S(1)} async-done(((bf16[4,40,768]{2,1,0:T(8,128)(2,1)}), bf16[4,40,768]{2,1,0:T(8,128)(2,1)S(1)}, u32[]{:S(2)}, u32[]{:S(2)}) %all-to-all-start.5) | async-done | bytes 245792 | tf_op jit(solution)/shard_map/all_to_all | solution.py:649
  (170 shorter events, 103.1 us)
Async XLA Ops:
  7.2 134.7 %all-gather.4.cloned.1.call-start = ((), (), s32[]{:S(2)}) async-start(), calls=%async_computation.8 | async-start | bytes 2211840 | tf_op jit(solution)/shard_map/all_gather | solution.py:605
  27.4 191.5 %all-gather.8.cloned.1.call-start = ((), (), s32[]{:S(2)}) async-start(), calls=%async_computation.10 | async-start | bytes 6488064 | tf_op jit(solution)/shard_map/all_gather | solution.py:616
  27.5 16.2 %collective-permute-start.2 = (bf16[32,6656]{1,0:T(8,128)(2,1)S(1)}, bf16[32,6656]{1,0:T(8,128)(2,1)S(1)}, u32[]{:S(2)}, u32[]{:S(2)}) collective-permute-start(bf16[32,6656]{1,0:T(8,128)(2,1)S(1)} %constant_dynamic-update-slice_fusion), channel_id=1, source_target_pairs={{1,0},{2,1},{3,2},{5,4},{6,5},{7,6},{9,8},{10,9},{11,10},{13,12},{... | collective-permute-start | bytes 1277960 | tf_op jit(solution)/shard_map/ppermute | solution.py:531
  43.7 18.0 %collective-permute-start.4 = (bf16[32,6656]{1,0:T(8,128)(2,1)S(1)}, bf16[32,6656]{1,0:T(8,128)(2,1)S(1)}, u32[]{:S(2)}, u32[]{:S(2)}) collective-permute-start(bf16[32,6656]{1,0:T(8,128)(2,1)S(1)} %collective-permute-done), channel_id=1, source_target_pairs={{1,2},{2,3},{5,6},{6,7},{9,10},{10,11},{13,14},{14,15},{17,18},{18... | collective-permute-start | bytes 1277960 | tf_op jit(solution)/shard_map/ppermute | solution.py:530
  44.4 17.3 %collective-permute-start.6 = (bf16[32,6656]{1,0:T(8,128)(2,1)S(1)}, bf16[32,6656]{1,0:T(8,128)(2,1)S(1)}, u32[]{:S(2)}, u32[]{:S(2)}) collective-permute-start(bf16[32,6656]{1,0:T(8,128)(2,1)S(1)} %collective-permute-done.2), channel_id=1, source_target_pairs={{1,0},{2,1},{5,4},{6,5},{9,8},{10,9},{13,12},{14,13},{17,16},{18,1... | collective-permute-start | bytes 1277960 | tf_op jit(solution)/shard_map/ppermute | solution.py:531
  79.0 139.9 %all-gather.6.cloned.1.call-start = ((), (), s32[]{:S(2)}) async-start(), calls=%async_computation.9 | async-start | bytes 15335424 | tf_op jit(solution)/shard_map/all_gather | solution.py:609
  80.9 23.3 %collective-permute-start.11 = (bf16[512,1024]{1,0:T(8,128)(2,1)S(1)}, bf16[512,1024]{1,0:T(8,128)(2,1)S(1)}, u32[]{:S(2)}, u32[]{:S(2)}) collective-permute-start(bf16[512,1024]{1,0:T(8,128)(2,1)S(1)} %bitcast.89), channel_id=1, source_target_pairs={{1,0},{2,1},{3,2},{5,4},{6,5},{7,6},{9,8},{10,9},{11,10},{13,12},{... | collective-permute-start | bytes 3145736 | tf_op jit(solution)/shard_map/ppermute | solution.py:531
  82.2 23.3 %collective-permute-start.8 = (bf16[512,1024]{1,0:T(8,128)(2,1)S(1)}, bf16[512,1024]{1,0:T(8,128)(2,1)}, u32[]{:S(2)}, u32[]{:S(2)}) collective-permute-start(bf16[512,1024]{1,0:T(8,128)(2,1)S(1)} %bitcast.90), channel_id=1, source_target_pairs={{0,1},{1,2},{2,3},{4,5},{5,6},{6,7},{8,9},{9,10},{10,11},{12,13},{... | collective-permute-start | bytes 3145736 | tf_op jit(solution)/shard_map/ppermute | solution.py:530
  104.2 23.1 %collective-permute-start.12 = (bf16[512,1024]{1,0:T(8,128)(2,1)S(1)}, bf16[512,1024]{1,0:T(8,128)(2,1)}, u32[]{:S(2)}, u32[]{:S(2)}) collective-permute-start(bf16[512,1024]{1,0:T(8,128)(2,1)S(1)} %collective-permute-done.11), channel_id=1, source_target_pairs={{1,0},{2,1},{5,4},{6,5},{9,8},{10,9},{13,12},{14,13},{17,16},{18,1... | collective-permute-start | bytes 3145736 | tf_op jit(solution)/shard_map/ppermute | solution.py:531
  105.5 23.1 %collective-permute-start.9 = (bf16[512,1024]{1,0:T(8,128)(2,1)}, bf16[512,1024]{1,0:T(8,128)(2,1)}, u32[]{:S(2)}, u32[]{:S(2)}) collective-permute-start(bf16[512,1024]{1,0:T(8,128)(2,1)} %collective-permute-done.8), channel_id=1, source_target_pairs={{1,2},{2,3},{5,6},{6,7},{9,10},{10,11},{13,14},{14,15},{17,18},{18... | collective-permute-start | bytes 3145736 | tf_op jit(solution)/shard_map/ppermute | solution.py:530
  127.4 35.5 %collective-permute-start.13 = (bf16[512,1024]{1,0:T(8,128)(2,1)}, bf16[512,1024]{1,0:T(8,128)(2,1)}, u32[]{:S(2)}, u32[]{:S(2)}) collective-permute-start(bf16[512,1024]{1,0:T(8,128)(2,1)} %collective-permute-done.12), channel_id=1, source_target_pairs={{1,0},{5,4},{9,8},{13,12},{17,16},{21,20},{25,24},{29,28}} | collective-permute-start | bytes 3145736 | tf_op jit(solution)/shard_map/ppermute | solution.py:531
  128.7 34.2 %collective-permute-start.10 = (bf16[512,1024]{1,0:T(8,128)(2,1)}, bf16[512,1024]{1,0:T(8,128)(2,1)}, u32[]{:S(2)}, u32[]{:S(2)}) collective-permute-start(bf16[512,1024]{1,0:T(8,128)(2,1)} %collective-permute-done.9), channel_id=1, source_target_pairs={{2,3},{6,7},{10,11},{14,15},{18,19},{22,23},{26,27},{30,31}} | collective-permute-start | bytes 3145736 | tf_op jit(solution)/shard_map/ppermute | solution.py:530
  136.4 38.6 %all-to-all-start.1 = ((bf16[4,256,512]{2,1,0:T(8,128)(2,1)}), bf16[4,256,512]{2,1,0:T(8,128)(2,1)}, u32[]{:S(2)}, u32[]{:S(2)}) async-start(bf16[4,256,512]{2,1,0:T(8,128)(2,1)} %pad_maximum_fusion.5), calls=%async_computation.1 | async-start | bytes 2097152 | tf_op jit(solution)/shard_map/all_to_all | solution.py:615
  197.3 20.5 %all-to-all-start.2 = ((bf16[4,512,256]{2,1,0:T(8,128)(2,1)}), bf16[4,512,256]{2,1,0:T(8,128)(2,1)S(1)}, u32[]{:S(2)}, u32[]{:S(2)}) async-start(bf16[4,512,256]{2,1,0:T(8,128)(2,1)} %bitcast.8), calls=%async_computation.2 | async-start | bytes 2097152 | tf_op jit(solution)/shard_map/all_to_all | solution.py:621
  201.9 207.5 %reduce-scatter.3.cloned.1.call-start = ((), (), s32[]{:S(2)}) async-start(), calls=%async_computation.11 | async-start | bytes 21823488 | tf_op jit(solution)/shard_map/reduce_scatter | solution.py:628
  265.1 19.5 %all-to-all-start.3 = ((bf16[512,4,256]{2,0,1:T(8,128)(2,1)}), bf16[512,4,256]{2,0,1:T(8,128)(2,1)S(1)}, u32[]{:S(2)}, u32[]{:S(2)}) async-start(bf16[512,4,256]{2,0,1:T(8,128)(2,1)} %bitcast.81), calls=%async_computation.3 | async-start | bytes 2097152 | tf_op jit(solution)/shard_map/all_to_all | solution.py:627
  268.7 196.4 %reduce-scatter.5.cloned.1.call-start = ((), (), s32[]{:S(2)}) async-start(), calls=%async_computation.12 | async-start | bytes 3031040 | tf_op jit(solution)/shard_map/reduce_scatter | solution.py:675
  326.5 24.8 %collective-permute-start.18 = (bf16[512,1024]{1,0:T(8,128)(2,1)S(1)}, bf16[512,1024]{1,0:T(8,128)(2,1)S(1)}, u32[]{:S(2)}, u32[]{:S(2)}) collective-permute-start(bf16[512,1024]{1,0:T(8,128)(2,1)S(1)} %get-tuple-element.69), channel_id=1, source_target_pairs={{0,1},{4,5},{8,9},{12,13},{16,17},{20,21},{24,25},{28,29}} | collective-permute-start | bytes 3145736 | tf_op jit(solution)/shard_map/ppermute | solution.py:567
  327.8 23.5 %collective-permute-start.19 = (bf16[512,1024]{1,0:T(8,128)(2,1)S(1)}, bf16[512,1024]{1,0:T(8,128)(2,1)}, u32[]{:S(2)}, u32[]{:S(2)}) collective-permute-start(bf16[512,1024]{1,0:T(8,128)(2,1)S(1)} %get-tuple-element.70), channel_id=1, source_target_pairs={{3,2},{7,6},{11,10},{15,14},{19,18},{23,22},{27,26},{31,30}} | collective-permute-start | bytes 3145736 | tf_op jit(solution)/shard_map/ppermute | solution.py:568
  355.2 25.8 %collective-permute-start.20 = (bf16[512,1024]{1,0:T(8,128)(2,1)}, bf16[512,1024]{1,0:T(8,128)(2,1)S(1)}, u32[]{:S(2)}, u32[]{:S(2)}) collective-permute-start(bf16[512,1024]{1,0:T(8,128)(2,1)} %get-tuple-element.73), channel_id=1, source_target_pairs={{0,1},{1,2},{4,5},{5,6},{8,9},{9,10},{12,13},{13,14},{16,17},{17,1... | collective-permute-start | bytes 3145736 | tf_op jit(solution)/shard_map/ppermute | solution.py:567
  359.6 21.5 %collective-permute-start.21 = (bf16[512,1024]{1,0:T(8,128)(2,1)S(1)}, bf16[512,1024]{1,0:T(8,128)(2,1)S(1)}, u32[]{:S(2)}, u32[]{:S(2)}) collective-permute-start(bf16[512,1024]{1,0:T(8,128)(2,1)S(1)} %get-tuple-element.74), channel_id=1, source_target_pairs={{2,1},{3,2},{6,5},{7,6},{10,9},{11,10},{14,13},{15,14},{18,17},{19... | collective-permute-start | bytes 3145736 | tf_op jit(solution)/shard_map/ppermute | solution.py:568
  383.6 20.3 %collective-permute-start.22 = (bf16[512,1024]{1,0:T(8,128)(2,1)S(1)}, bf16[512,1024]{1,0:T(8,128)(2,1)}, u32[]{:S(2)}, u32[]{:S(2)}) collective-permute-start(bf16[512,1024]{1,0:T(8,128)(2,1)S(1)} %get-tuple-element.77), channel_id=1, source_target_pairs={{0,1},{1,2},{2,3},{4,5},{5,6},{6,7},{8,9},{9,10},{10,11},{12,13},{... | collective-permute-start | bytes 3145736 | tf_op jit(solution)/shard_map/ppermute | solution.py:567
  392.6 16.8 %collective-permute-start.23 = (bf16[512,1024]{1,0:T(8,128)(2,1)S(1)}, bf16[512,1024]{1,0:T(8,128)(2,1)}, u32[]{:S(2)}, u32[]{:S(2)}) collective-permute-start(bf16[512,1024]{1,0:T(8,128)(2,1)S(1)} %get-tuple-element.78), channel_id=1, source_target_pairs={{1,0},{2,1},{3,2},{5,4},{6,5},{7,6},{9,8},{10,9},{11,10},{13,12},{... | collective-permute-start | bytes 3145736 | tf_op jit(solution)/shard_map/ppermute | solution.py:568
  434.8 19.5 %all-to-all-start.5 = ((bf16[4,40,768]{2,1,0:T(8,128)(2,1)}), bf16[4,40,768]{2,1,0:T(8,128)(2,1)S(1)}, u32[]{:S(2)}, u32[]{:S(2)}) async-start(bf16[4,40,768]{2,1,0:T(8,128)(2,1)} %fusion.12), calls=%async_computation.5 | async-start | bytes 491520 | tf_op jit(solution)/shard_map/all_to_all | solution.py:649
  (26 other events, 272.4 us)
Sparse Core Ops, SparseCore 0:
  27.5 26.4 all-gather.3
  79.2 41.5 all-gather.7
  122.6 76.5 all-gather.5
  263.0 127.5 reduce-scatter.2
  414.1 50.9 reduce-scatter.4

commit v6 on v5

v6 whole, which is shorter than its diff:
```python
import functools
import math

import jax
import jax.numpy as jnp
import numpy as np
from jax import lax
from jax.experimental import pallas as pl
from jax.experimental.pallas import tpu as pltpu
from jax.sharding import Mesh
from jax.sharding import PartitionSpec as P

HEAD_DIM = 128
QBLK = 256
MBLK = 128
EPSILON = 1e-06
NEGATIVE = -1e30
SCALE = 1.0 / math.sqrt(HEAD_DIM)
LOG2E = math.log2(math.e)
MIB = 1 << 20
F32 = jnp.float32
BF16 = jnp.bfloat16
DP = ("chip", "core")
NT = (((1,), (1,)), ((), ()))
TN = (((0,), (0,)), ((), ()))


def dot(left, right, dims=(((1,), (0,)), ((), ()))):
    return lax.dot_general(left, right, dims, preferred_element_type=F32)


def rotary_tables(length):
    half_dim = HEAD_DIM // 2
    frequency = 10000.0 ** (-jnp.arange(half_dim, dtype=F32) / half_dim)
    angles = jnp.arange(length, dtype=jnp.int32).astype(F32)[:, None] * frequency[None, :]
    cosine, sine = jnp.cos(angles), jnp.sin(angles)
    return jnp.concatenate([cosine, cosine], 1), jnp.concatenate([-sine, sine], 1)


def qkv_kernel(heads, place_ref, tok_ref, gain_ref, wq_ref, wk_ref, wv_ref, cos_ref, sin_ref, qkv_ref):
    rows = tok_ref[...].astype(F32)
    factor = lax.rsqrt(jnp.mean(rows * rows, -1, keepdims=True) + EPSILON)
    normed = (rows * factor * gain_ref[...]).astype(BF16)
    cosine, sine = cos_ref[...], sin_ref[...]
    for part, w_ref in enumerate((wq_ref, wk_ref, wv_ref)):
        values = dot(normed, w_ref[...])
        for head in range(heads):
            value = values[:, head * HEAD_DIM : (head + 1) * HEAD_DIM]
            if part < 2:
                value = value * cosine + pltpu.roll(value, HEAD_DIM // 2, 1) * sine
            if part == 0:
                value = value * (SCALE * LOG2E)
            at = (part * heads + head) * HEAD_DIM
            qkv_ref[:, at : at + HEAD_DIM] = value.astype(BF16)


def project_qkv(place, tokens_all, gain, w_qkv, cosine, sine, heads, ring):
    length, width = tokens_all.shape
    wide = heads * HEAD_DIM
    block = 2 * QBLK
    part = [pl.BlockSpec((width, wide), lambda i, place, p=p: (0, p * ring + place[0])) for p in range(3)]
    return pl.pallas_call(
        functools.partial(qkv_kernel, heads),
        grid_spec=pltpu.PrefetchScalarGridSpec(
            num_scalar_prefetch=1,
            grid=(length // block,),
            in_specs=[
                pl.BlockSpec((block, width), lambda i, _: (i, 0)),
                pl.BlockSpec((1, width), lambda i, _: (0, 0)),
                *part,
                pl.BlockSpec((block, HEAD_DIM), lambda i, _: (i, 0)),
                pl.BlockSpec((block, HEAD_DIM), lambda i, _: (i, 0)),
            ],
            out_specs=pl.BlockSpec((block, 3 * wide), lambda i, _: (i, 0)),
        ),
        out_shape=jax.ShapeDtypeStruct((length, 3 * wide), BF16),
        compiler_params=pltpu.CompilerParams(vmem_limit_bytes=48 * MIB),
        cost_estimate=pl.CostEstimate(
            flops=6 * length * width * wide, bytes_accessed=4 * length * (width + 3 * wide), transcendentals=0
        ),
        name="project_qkv",
    )(place, tokens_all, gain, w_qkv, w_qkv, w_qkv, cosine, sine)


def memory_bias(counts_ref, base, top, axis):
    shape = (1, top * MBLK) if axis == 1 else (top * MBLK, 1)
    column = lax.broadcasted_iota(jnp.int32, shape, axis)
    limit = jnp.zeros(shape, jnp.int32)
    for entry in range(top):
        inside = (column >= entry * MBLK) & (column < entry * MBLK + counts_ref[base + entry])
        limit = jnp.where(inside, 1, limit)
    return jnp.where(limit > 0, 0.0, NEGATIVE)


def pick_memory(ref, chosen_ref, base, top):
    rows = [
        ref[pl.ds(pl.multiple_of(chosen_ref[base + entry] * MBLK, MBLK), MBLK), :]
        for entry in range(top)
    ]
    return jnp.concatenate(rows, 0)


def forward_kernel(
    top, chosen_ref, counts_ref, q_ref, k_ref, v_ref, mk_ref, mv_ref, out_ref, lse_ref, acc_s, peak_s
):
    block = pl.program_id(0)
    rows = q_ref.shape[0]
    subs = rows // QBLK
    own = pl.ds(pl.multiple_of(block * rows, rows), rows)
    causal = lax.broadcasted_iota(jnp.int32, (rows, rows), 0) >= lax.broadcasted_iota(jnp.int32, (rows, rows), 1)
    ones = jnp.ones((rows, HEAD_DIM), BF16)
    mem_ones = jnp.ones((top * MBLK, HEAD_DIM), BF16)
    remote = []
    for sub in range(subs):
        base = (block * subs + sub) * top
        keys = pick_memory(mk_ref, chosen_ref, base, top)
        query = q_ref[sub * QBLK : (sub + 1) * QBLK, :]
        remote.append(dot(query, keys, NT) + memory_bias(counts_ref, base, top, 1))
    local = jnp.where(causal, dot(q_ref[...], k_ref[own, :], NT), NEGATIVE)
    peak = jnp.max(local, -1, keepdims=True)
    peak = jnp.maximum(peak, jnp.concatenate([jnp.max(r, -1, keepdims=True) for r in remote], 0))
    acc = dot(jnp.exp2(local - peak).astype(BF16), jnp.concatenate([v_ref[own, :], ones], 1))
    more = []
    for sub in range(subs):
        values = pick_memory(mv_ref, chosen_ref, (block * subs + sub) * top, top)
        weights = jnp.exp2(remote[sub] - peak[sub * QBLK : (sub + 1) * QBLK]).astype(BF16)
        more.append(dot(weights, jnp.concatenate([values, mem_ones], 1)))
    acc_s[...] = acc + jnp.concatenate(more, 0)
    peak_s[...] = jnp.broadcast_to(peak, (rows, HEAD_DIM))

    def step(index, carry):
        there = pl.ds(pl.multiple_of(index * rows, rows), rows)
        peak = peak_s[:, :1]
        scores = dot(q_ref[...], k_ref[there, :], NT)
        higher = jnp.maximum(peak, jnp.max(scores, -1, keepdims=True))
        weights = jnp.exp2(scores - higher).astype(BF16)
        values = jnp.concatenate([v_ref[there, :], ones], 1)
        acc_s[...] = acc_s[...] * jnp.exp2(peak - higher) + dot(weights, values)
        peak_s[...] = jnp.broadcast_to(higher, (rows, HEAD_DIM))
        return carry

    lax.fori_loop(0, block, step, 0)
    total = acc_s[:, HEAD_DIM:]
    out_ref[...] = (acc_s[:, :HEAD_DIM] / total).astype(BF16)
    lse_ref[...] = peak_s[:, :1] + jnp.log2(total[:, :1])


def attend_forward(chosen, counts, qkv, memory, head, heads, top):
    length = qkv.shape[0]
    rows = min(2 * QBLK, length)
    mem_rows = memory.shape[0]
    return pl.pallas_call(
        functools.partial(forward_kernel, top),
        grid_spec=pltpu.PrefetchScalarGridSpec(
            num_scalar_prefetch=2,
            grid=(length // rows,),
            in_specs=[
                pl.BlockSpec((rows, HEAD_DIM), lambda i, *_: (i, head)),
                pl.BlockSpec((length, HEAD_DIM), lambda i, *_: (0, heads + head)),
                pl.BlockSpec((length, HEAD_DIM), lambda i, *_: (0, 2 * heads + head)),
                pl.BlockSpec((mem_rows, HEAD_DIM), lambda i, *_: (0, head)),
                pl.BlockSpec((mem_rows, HEAD_DIM), lambda i, *_: (0, heads + head)),
            ],
            out_specs=[
                pl.BlockSpec((rows, HEAD_DIM), lambda i, *_: (i, 0)),
                pl.BlockSpec((rows, 1), lambda i, *_: (i, 0)),
            ],
            scratch_shapes=[
                pltpu.VMEM((rows, 2 * HEAD_DIM), F32),
                pltpu.VMEM((rows, HEAD_DIM), F32),
            ],
        ),
        out_shape=[
            jax.ShapeDtypeStruct((length, HEAD_DIM), BF16),
            jax.ShapeDtypeStruct((length, 1), F32),
        ],
        compiler_params=pltpu.CompilerParams(vmem_limit_bytes=48 * MIB),
        cost_estimate=pl.CostEstimate(
            flops=4 * length * HEAD_DIM * (length // 2 + top * MBLK),
            bytes_accessed=8 * length * HEAD_DIM,
            transcendentals=length * (length // 2 + top * MBLK),
        ),
        name="attend_forward",
    )(chosen, counts, qkv, qkv, qkv, memory, memory)


def backward_kernel(
    top, chosen_ref, counts_ref, place_ref, q_ref, k_ref, v_ref, mk_ref, mv_ref, go_ref, out_ref, lse_ref,
    cos_ref, sin_ref, tok_ref, gain_ref, wq_ref, wk_ref, wv_ref, grad_ref, grad_w_ref, gain_grad_ref,
    gk_s, gv_s, gq_s, gw_s,
):
    block = pl.num_programs(0) - 1 - pl.program_id(0)
    rows = q_ref.shape[0]
    subs = rows // QBLK
    own = pl.ds(pl.multiple_of(block * rows, rows), rows)
    key_at = lax.broadcasted_iota(jnp.int32, (rows, rows), 0)
    query_at = lax.broadcasted_iota(jnp.int32, (rows, rows), 1)
    causal = query_at >= key_at

    @pl.when(pl.program_id(0) == 0)
    def _():
        gk_s[...] = jnp.zeros_like(gk_s)
        gv_s[...] = jnp.zeros_like(gv_s)
        gw_s[...] = jnp.zeros_like(gw_s)

    def spread(column):
        return jnp.transpose(jnp.broadcast_to(column, (rows, HEAD_DIM)))[:1]

    lse = spread(lse_ref[...])
    delta = spread(jnp.sum(go_ref[...].astype(F32) * out_ref[...].astype(F32), -1, keepdims=True))

    def pair(queries, keys, values, mask):
        scores = mask(dot(keys, q_ref[queries, :], NT))
        weights = jnp.exp2(scores - lse[:, queries])
        grad_weights = dot(values, go_ref[queries, :], NT)
        return weights.astype(BF16), (weights * (grad_weights - delta[:, queries])).astype(BF16)

    for sub in range(subs):
        base = (block * subs + sub) * top
        queries = slice(sub * QBLK, (sub + 1) * QBLK)
        keys = pick_memory(mk_ref, chosen_ref, base, top)
        values = pick_memory(mv_ref, chosen_ref, base, top)
        bias = memory_bias(counts_ref, base, top, 0)
        _, grad_scores = pair(queries, keys, values, lambda scores: scores + bias)
        gq_s[queries, :] = dot(grad_scores, keys, TN)

    def local(there, mask):
        keys = k_ref[there, :]
        weights, grad_scores = pair(slice(0, rows), keys, v_ref[there, :], mask)
        gk_s[there, :] += dot(grad_scores, q_ref[...])
        gv_s[there, :] += dot(weights, go_ref[...])
        gq_s[...] += dot(grad_scores, keys, TN)

    local(own, lambda scores: jnp.where(causal, scores, NEGATIVE))

    def step(index, carry):
        local(pl.ds(pl.multiple_of(index * rows, rows), rows), lambda scores: scores)
        return carry

    lax.fori_loop(0, block, step, 0)
    cosine, sine = cos_ref[...], sin_ref[...]

    def unturn(value):
        return value * cosine - pltpu.roll(value, HEAD_DIM // 2, 1) * sine

    grad = jnp.concatenate(
        [
            unturn(gq_s[...] * SCALE).astype(BF16),
            unturn(gk_s[own, :] * (1.0 / LOG2E)).astype(BF16),
            gv_s[own, :].astype(BF16),
        ],
        1,
    )
    grad_ref[...] = grad
    tokens = tok_ref[...].astype(F32)
    tokens = tokens * lax.rsqrt(jnp.mean(tokens * tokens, -1, keepdims=True) + EPSILON)
    gw_s[...] += dot(tokens.astype(BF16), grad, TN)

    @pl.when(block == 0)
    def _():
        raw = gw_s[...]
        weights = jnp.concatenate([wq_ref[...], wk_ref[...], wv_ref[...]], 1).astype(F32)
        gain_grad_ref[...] = jnp.sum(raw * weights, -1, keepdims=True)
        grad_w_ref[...] = (raw * gain_ref[...]).astype(BF16)


def attend_backward(
    chosen, counts, place, qkv, memory, grad_out, out, lse, cosine, sine, tokens_all, gain, w_qkv, head, heads, top, ring
):
    length = qkv.shape[0]
    width = tokens_all.shape[1]
    rows = min(2 * QBLK, length)
    mem_rows = memory.shape[0]
    last = length // rows - 1
    parts = [
        pl.BlockSpec((width, HEAD_DIM), lambda i, c, n, place, p=p: (0, (p * ring + place[0]) * heads + head))
        for p in range(3)
    ]
    return pl.pallas_call(
        functools.partial(backward_kernel, top),
        grid_spec=pltpu.PrefetchScalarGridSpec(
            num_scalar_prefetch=3,
            grid=(last + 1,),
            in_specs=[
                pl.BlockSpec((rows, HEAD_DIM), lambda i, *_: (last - i, head)),
                pl.BlockSpec((length, HEAD_DIM), lambda i, *_: (0, heads + head)),
                pl.BlockSpec((length, HEAD_DIM), lambda i, *_: (0, 2 * heads + head)),
                pl.BlockSpec((mem_rows, HEAD_DIM), lambda i, *_: (0, head)),
                pl.BlockSpec((mem_rows, HEAD_DIM), lambda i, *_: (0, heads + head)),
                pl.BlockSpec((rows, HEAD_DIM), lambda i, *_: (last - i, 0)),
                pl.BlockSpec((rows, HEAD_DIM), lambda i, *_: (last - i, 0)),
                pl.BlockSpec((rows, 1), lambda i, *_: (last - i, 0)),
                pl.BlockSpec((rows, HEAD_DIM), lambda i, *_: (last - i, 0)),
                pl.BlockSpec((rows, HEAD_DIM), lambda i, *_: (last - i, 0)),
                pl.BlockSpec((rows, width), lambda i, *_: (last - i, 0)),
                pl.BlockSpec((width, 1), lambda i, *_: (0, 0)),
                *parts,
            ],
            out_specs=[
                pl.BlockSpec((rows, 3 * HEAD_DIM), lambda i, *_: (last - i, 0)),
                pl.BlockSpec((width, 3 * HEAD_DIM), lambda i, *_: (0, 0)),
                pl.BlockSpec((width, 1), lambda i, *_: (0, 0)),
            ],
            scratch_shapes=[
                pltpu.VMEM((length, HEAD_DIM), F32),
                pltpu.VMEM((length, HEAD_DIM), F32),
                pltpu.VMEM((rows, HEAD_DIM), F32),
                pltpu.VMEM((width, 3 * HEAD_DIM), F32),
            ],
        ),
        out_shape=[
            jax.ShapeDtypeStruct((length, 3 * HEAD_DIM), BF16),
            jax.ShapeDtypeStruct((width, 3 * HEAD_DIM), BF16),
            jax.ShapeDtypeStruct((width, 1), F32),
        ],
        compiler_params=pltpu.CompilerParams(vmem_limit_bytes=48 * MIB),
        cost_estimate=pl.CostEstimate(
            flops=10 * length * HEAD_DIM * (length // 2 + top * MBLK),
            bytes_accessed=16 * length * HEAD_DIM,
            transcendentals=length * (length // 2 + top * MBLK),
        ),
        name="attend_backward",
    )(
        chosen, counts, place, qkv, qkv, qkv, memory, memory, grad_out, out, lse, cosine, sine, tokens_all, gain,
        w_qkv, w_qkv, w_qkv,
    )


def finish_kernel(heads, tok_ref, gain_ref, mid_ref, w_ref, *refs):
    grads, out_ref = refs[:-1], refs[-1]
    ring = grads[0].shape[0]
    width = tok_ref.shape[1]
    wide = heads * HEAD_DIM
    total = None
    for part in range(3):
        lanes = slice(part * HEAD_DIM, (part + 1) * HEAD_DIM)
        for place in range(ring):
            left = [grad[place, :, lanes] for grad in grads]
            left = jnp.concatenate(left, 1) if heads > 1 else left[0]
            at = (part * ring + place) * wide
            term = dot(left, w_ref[:, at : at + wide], NT)
            total = term if total is None else total + term
    own = tok_ref[...].astype(F32)
    factor = lax.rsqrt(jnp.mean(own * own, -1, keepdims=True) + EPSILON)
    scaled = total * gain_ref[...]
    inner = jnp.mean(scaled * own, -1, keepdims=True)
    out_ref[...] = (mid_ref[...] + factor * scaled - own * (factor * factor * factor * inner)).astype(BF16)


def finish_tokens(tokens, gain, grad_middle, w_qkv, grads):
    rows, width = tokens.shape
    ring = grads[0].shape[0]
    heads = len(grads)
    block = min(rows, QBLK)
    return pl.pallas_call(
        functools.partial(finish_kernel, heads),
        grid=(rows // block,),
        in_specs=[
            pl.BlockSpec((block, width), lambda i: (i, 0)),
            pl.BlockSpec((1, width), lambda i: (0, 0)),
            pl.BlockSpec((block, width), lambda i: (i, 0)),
            pl.BlockSpec(w_qkv.shape, lambda i: (0, 0)),
            *[pl.BlockSpec((ring, block, 3 * HEAD_DIM), lambda i: (0, i, 0)) for _ in grads],
        ],
        out_specs=pl.BlockSpec((block, width), lambda i: (i, 0)),
        out_shape=jax.ShapeDtypeStruct((rows, width), BF16),
        compiler_params=pltpu.CompilerParams(vmem_limit_bytes=48 * MIB),
        cost_estimate=pl.CostEstimate(
            flops=6 * rows * width * width, bytes_accessed=8 * width * width, transcendentals=0
        ),
        name="finish_tokens",
    )(tokens, gain, grad_middle, w_qkv, *grads)


def ffn_kernel(
    span, merged, heads, tok_ref, cot_ref, gain_ref, out_w, gate_w, up_w, down_w, *rest
):
    att_refs, rest = rest[:heads], rest[heads:]
    mixed_ref, grad_mid_ref, gain_grad_ref, grads_ref, *rest = rest
    grad_att_refs, rest = rest[:heads], rest[heads:]
    if not merged:
        down_grads_ref, rest = rest[0], rest[1:]
    att_s, middle_s, normed_s, turned_s, mixed_s, upstream_s, gate_s, up_s, down_s, out_s, sems, late_sems = rest
    step, steps = pl.program_id(0), pl.num_programs(0)
    width = tok_ref.shape[1]
    share = width // span
    wide = gate_w.shape[1]
    hidden_width = down_s.shape[0]
    tall = hidden_width // span
    lanes = width // wide
    first = tall * lanes if merged else 0
    slot = step % 2

    @pl.when(step == 0)
    def _():
        for place in range(att_refs[0].shape[0]):
            for head in range(heads):
                at = (place * heads + head) * HEAD_DIM
                att_s[:, at : at + HEAD_DIM] = att_refs[head][place]
        middle = tok_ref[...].astype(F32) + dot(att_s[...], out_w[...])
        middle_s[...] = middle
        factor = lax.rsqrt(jnp.mean(middle * middle, -1, keepdims=True) + EPSILON)
        normed = (middle * factor * gain_ref[...]).astype(BF16)
        normed_s[...] = normed
        turned_s[...] = jnp.transpose(normed)
        mixed_s[...] = middle
        upstream_s[...] = jnp.zeros_like(upstream_s)

    def copy_out(kind, which, index):
        source = (gate_s, up_s)[kind].at[which]
        start = first + (lanes + kind * steps + index) * share
        target = grads_ref.at[:, pl.ds(start, share), :]
        return pltpu.make_async_copy(source, target, sems.at[kind, which])

    normed = normed_s[...]
    upstream = cot_ref[...]
    both = jnp.concatenate([gate_w[...], up_w[...]], 1)
    acts = dot(normed, both)
    gate_act, up_act = acts[:, :wide], acts[:, wide:]
    grad_hidden = dot(upstream, down_w[...], NT)
    sigmoid = jax.nn.sigmoid(gate_act)
    silu = gate_act * sigmoid
    hidden = (silu * up_act).astype(BF16)
    grad_gate = (grad_hidden * up_act * sigmoid * (1.0 + gate_act * (1.0 - sigmoid))).astype(BF16)
    grad_up = (grad_hidden * silu).astype(BF16)
    mixed_s[...] += dot(hidden, down_w[...])
    grad_acts = jnp.concatenate([grad_gate, grad_up], 1)
    upstream_s[...] += dot(grad_acts, both, NT)
    down_s[pl.ds(pl.multiple_of(step * wide, wide), wide), :] = dot(hidden, upstream, TN).astype(BF16)

    @pl.when(step >= 2)
    def _():
        copy_out(0, slot, step - 2).wait()
        copy_out(1, slot, step - 2).wait()

    weight_grads = dot(turned_s[...], grad_acts).astype(BF16)
    gate_s[slot] = weight_grads[:, :wide].reshape(span, share, wide)
    up_s[slot] = weight_grads[:, wide:].reshape(span, share, wide)
    copy_out(0, slot, step).start()
    copy_out(1, slot, step).start()

    @pl.when(step == steps - 1)
    def _():
        copies = []
        if merged:
            for place in range(span):
                for lane in range(lanes):
                    copies.append(
                        pltpu.make_async_copy(
                            down_s.at[pl.ds(place * tall, tall), pl.ds(lane * wide, wide)],
                            grads_ref.at[place, pl.ds(lane * tall, tall), :],
                            late_sems.at[len(copies)],
                        )
                    )
        else:
            copies.append(pltpu.make_async_copy(down_s, down_grads_ref, late_sems.at[0]))
        for copy in copies:
            copy.start()
        mixed_ref[...] = mixed_s[...].astype(BF16)
        middle = middle_s[...]
        grad = upstream_s[...]
        factor = lax.rsqrt(jnp.mean(middle * middle, -1, keepdims=True) + EPSILON)
        gain_grad_ref[...] = jnp.sum(grad * middle * factor, 0, keepdims=True)
        scaled = grad * gain_ref[...]
        inner = jnp.mean(scaled * middle, -1, keepdims=True)
        grad_middle = cot_ref[...].astype(F32) + factor * scaled - middle * (factor * factor * factor * inner)
        grad_mid_ref[...] = grad_middle
        branch = grad_middle.astype(BF16)
        grad_att = dot(branch, out_w[...], NT).astype(BF16)
        for place in range(att_refs[0].shape[0]):
            for head in range(heads):
                at = (place * heads + head) * HEAD_DIM
                grad_att_refs[head][place] = grad_att[:, at : at + HEAD_DIM]
        turned_att = jnp.transpose(att_s[...])
        for lane in range(lanes):
            columns = slice(lane * wide, (lane + 1) * wide)
            out_s[lane] = dot(turned_att, branch[:, columns]).astype(BF16).reshape(span, share, wide)
            more = pltpu.make_async_copy(
                out_s.at[lane],
                grads_ref.at[:, pl.ds(first + lane * share, share), :],
                late_sems.at[len(copies)],
            )
            more.start()
            copies.append(more)
        for copy in copies:
            copy.wait()
        copy_out(0, 1 - slot, step - 1).wait()
        copy_out(1, 1 - slot, step - 1).wait()
        copy_out(0, slot, step).wait()
        copy_out(1, slot, step).wait()


def feed_forward(tokens, attended, upstream, gain, weights, w_down, span):
    rows, width = tokens.shape
    heads, ring = len(attended), attended[0].shape[0]
    hidden_width = w_down.shape[0]
    wide = 2 * HEAD_DIM
    steps = hidden_width // wide
    lanes = width // wide
    share = width // span
    tall = hidden_width // span
    merged = tall % 16 == 0
    total = (lanes + 2 * steps) * share + (lanes * tall if merged else 0)
    shapes = [
        jax.ShapeDtypeStruct((rows, width), BF16),
        jax.ShapeDtypeStruct((rows, width), F32),
        jax.ShapeDtypeStruct((1, width), F32),
        jax.ShapeDtypeStruct((span, total, wide), BF16),
        *[jax.ShapeDtypeStruct((ring, rows, HEAD_DIM), BF16) for _ in attended],
    ]
    by_head = [pl.BlockSpec((ring, rows, HEAD_DIM), lambda i: (0, 0, 0)) for _ in attended]
    specs = [
        pl.BlockSpec((rows, width), lambda i: (0, 0)),
        pl.BlockSpec((rows, width), lambda i: (0, 0)),
        pl.BlockSpec((1, width), lambda i: (0, 0)),
        pl.BlockSpec(memory_space=pl.ANY),
        *by_head,
    ]
    if not merged:
        shapes.append(jax.ShapeDtypeStruct((hidden_width, width), BF16))
        specs.append(pl.BlockSpec(memory_space=pl.ANY))
    return pl.pallas_call(
        functools.partial(ffn_kernel, span, merged, heads),
        grid=(steps,),
        in_specs=[
            pl.BlockSpec((rows, width), lambda i: (0, 0)),
            pl.BlockSpec((rows, width), lambda i: (0, 0)),
            pl.BlockSpec((1, width), lambda i: (0, 0)),
            pl.BlockSpec((width, width), lambda i: (0, 0)),
            pl.BlockSpec((width, wide), lambda i: (0, lanes + i)),
            pl.BlockSpec((width, wide), lambda i: (0, lanes + steps + i)),
            pl.BlockSpec((wide, width), lambda i: (i, 0)),
            *by_head,
        ],
        out_specs=specs,
        out_shape=shapes,
        scratch_shapes=[
            pltpu.VMEM((rows, width), BF16),
            pltpu.VMEM((rows, width), F32),
            pltpu.VMEM((rows, width), BF16),
            pltpu.VMEM((width, rows), BF16),
            pltpu.VMEM((rows, width), F32),
            pltpu.VMEM((rows, width), F32),
            pltpu.VMEM((2, span, share, wide), BF16),
            pltpu.VMEM((2, span, share, wide), BF16),
            pltpu.VMEM((hidden_width, width), BF16),
            pltpu.VMEM((lanes, span, share, wide), BF16),
            pltpu.SemaphoreType.DMA((2, 2)),
            pltpu.SemaphoreType.DMA(((span * lanes if merged else 1) + lanes,)),
        ],
        compiler_params=pltpu.CompilerParams(vmem_limit_bytes=56 * MIB),
        cost_estimate=pl.CostEstimate(
            flops=6 * rows * width * (3 * hidden_width + width),
            bytes_accessed=4 * width * (3 * hidden_width + width),
            transcendentals=rows * hidden_width,
        ),
        name="feed_forward",
    )(tokens, upstream, gain, weights, weights, weights, w_down, *attended)


def after(value, earlier):
    return lax.optimization_barrier((value, earlier))[0]


def chain_gather(blocks, axis):
    size = lax.axis_size(axis)
    place = lax.axis_index(axis)
    steps = []
    rising = falling = tuple(blocks)
    for step in range(size - 1):
        up = [(i, i + 1) for i in range(step, size - 1)]
        down = [(i + 1, i) for i in range(size - 1 - step)]
        rising = tuple(lax.ppermute(block, axis, up) for block in rising)
        falling = tuple(lax.ppermute(block, axis, down) for block in falling)
        if len(blocks) > 1:
            rising, falling = lax.optimization_barrier((rising, falling))
        steps.append((rising, falling))
    results = []
    for number, block in enumerate(blocks):
        ordered = []
        for index in range(size):
            cases = []
            for mine in range(size):
                if mine == index:
                    cases.append(block)
                elif mine > index:
                    cases.append(steps[mine - index - 1][0][number])
                else:
                    cases.append(steps[index - mine - 1][1][number])
            ordered.append(lax.select_n(place, *cases) if size > 2 else lax.select_n(place > 0, *cases))
        results.append(ordered)
    return results, steps


def shift_gather(block, axis):
    size = lax.axis_size(axis)
    place = lax.axis_index(axis)
    taken = [block]
    for far in range(1, size):
        taken.append(lax.ppermute(block, axis, [(i, (i + far) % size) for i in range(size)]))
    ordered = []
    for index in range(size):
        cases = [taken[(mine - index) % size] for mine in range(size)]
        ordered.append(lax.select_n(place, *cases) if size > 2 else lax.select_n(place > 0, *cases))
    return ordered


def exchange(blocks, axis):
    return lax.all_to_all(blocks, axis, 0, 0, tiled=True)


def body(
    tokens, memory_keys, memory_values, chosen, counts, w_query, w_key, w_value, w_out, w_gate, w_up, w_down,
    gain_attn, gain_ffn, cotangent,
):
    ring, span = lax.axis_size("fsdp"), lax.axis_size(DP)
    rows, width = tokens.shape[1:]
    heads = width // HEAD_DIM // ring
    wide = heads * HEAD_DIM
    length = rows * ring
    top = chosen.shape[2]
    hidden_width = w_gate.shape[1]
    share = w_query.shape[0]
    mine = tokens[0]

    extra = 8 if share % 8 == 0 else 8 - share % 8
    choices = jnp.concatenate([chosen[0].reshape(-1), counts[0].reshape(-1)]).astype(BF16)
    notes = [
        jnp.pad(row, (0, 3 * width - row.shape[0]))[None]
        for row in (jnp.concatenate([gain_attn, gain_ffn]), choices)
    ]
    notes.append(jnp.zeros((extra - 2, 3 * width), BF16))
    parcel = jnp.concatenate([jnp.concatenate([w_query, w_key, w_value], 1), *notes], 0)
    parcel = jnp.stack(shift_gather(parcel, "fsdp"))
    picks = parcel[:, share + 1, : choices.shape[0]].astype(jnp.int32).reshape(ring, 2, -1)
    chosen_all, counts_all = picks[:, 0].reshape(-1), picks[:, 1].reshape(-1)
    parcel = lax.all_gather(parcel, DP, axis=0, tiled=True)
    shards = jnp.concatenate([w_out, w_gate, w_up], 1)
    (near, near_down), steps = chain_gather((shards, w_down), "fsdp")
    (gathered,), token_steps = chain_gather((after(mine, steps[-2]),), "fsdp")
    w_qkv = parcel[:, :share].reshape(width, 3 * width)
    gain_one = parcel[:, share, :share].reshape(1, width).astype(F32)
    gain_two = parcel[:, share, share : 2 * share].reshape(1, width).astype(F32)
    first = lax.all_gather(jnp.concatenate(near, 0), DP, axis=0, tiled=True)
    gathered = jnp.concatenate(gathered, 0)

    memory = jnp.concatenate(
        [m[0].reshape(-1, ring, wide).transpose(1, 0, 2) for m in (memory_keys, memory_values)], 2
    )
    memory = exchange(after(memory, token_steps[-2]), "fsdp").reshape(-1, 2 * wide)
    down_full = lax.all_gather(jnp.concatenate(near_down, 0), DP, axis=0, tiled=True)

    cosine, sine = rotary_tables(length)
    place = lax.axis_index("fsdp").astype(jnp.int32).reshape(1)
    qkv = project_qkv(place, gathered, gain_one, w_qkv, cosine, sine, heads, ring)
    outs, stats, attended = [], [], []
    for head in range(heads):
        out, lse = attend_forward(chosen_all, counts_all, qkv, memory, head, heads, top)
        outs.append(out)
        stats.append(lse)
        attended.append(exchange(out.reshape(ring, rows, HEAD_DIM), "fsdp"))

    mixed, grad_middle, gain_two_grad, grads, *others = feed_forward(
        mine, attended, cotangent[0], gain_two, first, down_full, span
    )
    grad_heads, grad_down = others[:heads], others[heads:]
    grads = lax.psum_scatter(grads, DP, scatter_dimension=0, tiled=True)[0]
    column = gain_one.reshape(width, 1)
    returned, weight_grads, gain_one_grad = [], [], 0.0
    for head in range(heads):
        grad_out = exchange(grad_heads[head], "fsdp").reshape(length, HEAD_DIM)
        if head:
            qkv = after(qkv, weight_grads[-1])
        grad, grad_w, gain_grad = attend_backward(
            chosen_all, counts_all, place, qkv, memory, grad_out, outs[head], stats[head], cosine, sine, gathered,
            column, w_qkv, head, heads, top, ring,
        )
        returned.append(exchange(grad.reshape(ring, rows, 3 * HEAD_DIM), "fsdp"))
        weight_grads.append(grad_w)
        gain_one_grad = gain_one_grad + gain_grad

    gains = jnp.stack([gain_one_grad.reshape(span, -1), gain_two_grad.reshape(span, -1)], 1)
    gains = jnp.pad(gains.astype(BF16), ((0, 0), (0, extra - 2), (0, 3 * wide - gains.shape[2])))
    late = jnp.concatenate(weight_grads, 1).reshape(span, -1, 3 * wide)
    late = jnp.concatenate([late, gains], 1)
    late = late.reshape(span // 2, 2, late.shape[1], 3 * wide)
    core = lax.axis_index("core")
    taken = lax.ppermute(lax.dynamic_index_in_dim(late, 1 - core, 1, keepdims=False), "core", [(0, 1), (1, 0)])
    late = lax.dynamic_index_in_dim(late, core, 1, keepdims=False).astype(F32) + taken.astype(F32)
    late = jnp.sum(exchange(late.astype(BF16), "chip").astype(F32), 0).astype(BF16)
    grads = after(grads, late)
    gains = late[-extra : 2 - extra, : ring * share].reshape(2, ring, share).transpose(1, 0, 2)
    gains = jnp.pad(gains, ((0, 0), (0, extra - 2), (0, 3 * wide - share)))
    late = jnp.concatenate([late[:-extra].reshape(ring, share, 3 * wide), gains], 1)
    late = exchange(late, "fsdp").astype(F32)
    projections = [
        jnp.concatenate(
            [
                late[:, :share, (head * 3 + part) * HEAD_DIM : (head * 3 + part + 1) * HEAD_DIM]
                for head in range(heads)
            ],
            2,
        )
        .transpose(1, 0, 2)
        .reshape(share, width)
        for part in range(3)
    ]
    gain_shares = jnp.sum(late[:, share : share + 2, :share], 0)
    tokens_grad = finish_tokens(mine, gain_one, grad_middle, w_qkv, returned)

    strip = grads.shape[1]
    lanes = width // strip
    tall = w_down.shape[0]
    if grad_down:
        down = lax.psum_scatter(grad_down[0], DP, scatter_dimension=0, tiled=True)
        down = down.reshape(ring, tall, lanes, strip).transpose(0, 2, 1, 3)
    else:
        down = grads[: ring * tall * lanes].reshape(lanes, ring, tall, strip).transpose(1, 0, 2, 3)
        grads = grads[ring * tall * lanes :]
    grads = grads.reshape(-1, ring, share, strip).transpose(1, 0, 2, 3)
    pieces = jnp.concatenate([down.reshape(ring, -1, strip), grads.reshape(ring, -1, strip)], 1)
    pieces = lax.psum_scatter(pieces, "fsdp", scatter_dimension=0, tiled=True)[0].astype(F32)
    down_share = pieces[: lanes * tall].reshape(lanes, tall, strip).transpose(1, 0, 2).reshape(tall, width)
    others = pieces[lanes * tall :].reshape(-1, share, strip).transpose(1, 0, 2).reshape(share, -1)
    return (
        mixed[None],
        tokens_grad[None],
        *projections,
        others[:, :width],
        others[:, width : width + hidden_width],
        others[:, width + hidden_width :],
        down_share,
        gain_shares[0],
        gain_shares[1],
    )


def solution(mesh):
    span, ring = mesh.shape["dp"], mesh.shape["fsdp"]
    fine = Mesh(mesh.devices.reshape(span // 2, 2, ring), DP + ("fsdp",))
    every = DP + ("fsdp",)
    rows, matrix, vector = P(DP, "fsdp", None), P(every, None), P(every)
    in_specs = (rows,) * 5 + (matrix,) * 7 + (vector,) * 2 + (rows,)
    out_specs = (rows,) * 2 + (matrix,) * 7 + (vector,) * 2
    return jax.shard_map(body, mesh=fine, in_specs=in_specs, out_specs=out_specs, check_vma=False)
```

time: 477 us -> 586 us (1.23); the launches traced: 475 us -> 577 us
  waiting for transfers between devices: 191 us -> 251 us
  Pallas kernels: 111 us -> 133 us
  starting transfers between devices: 67 us -> 79 us
  blocking collectives: 30.5 us -> 39.6 us
  other arithmetic: 35.4 us -> 27.3 us
  local copies, waits for them, and re-layouts: 25.7 us -> 32.5 us
    all_to_all x4 -> x7, waiting for transfers between devices: 46 us -> 111 us  [exchange(): return lax.all_to_all(blocks, axis, 0, 0, tiled=True)]
    ppermute x6 -> x3, waiting for transfers between devices: 58.1 us -> 15.7 us  [shift_gather(): lax.ppermute(block, axis, [(i, (i + far) % size) for i in range(size)])]
    reduce_scatter x1, waiting for transfers between devices: 0.01 us -> 31.4 us  [body(): grads = lax.psum_scatter(grads, DP, scatter_dimension=0, tiled=True)[0]]
    pallas_call x4 -> x7, Pallas kernels: 111 us -> 133 us  [the longest x2 44.7 us: attend_backward(): pl.pallas_call(functools.partial(backward_kernel, top), grid_spec=pltpu.P...]
    all_to_all x4 -> x7, starting transfers between devices: 16.9 us -> 37.5 us  [exchange(): return lax.all_to_all(blocks, axis, 0, 0, tiled=True)]
    ppermute x6 -> x3, starting transfers between devices: 18.4 us -> 6.13 us  [shift_gather(): lax.ppermute(block, axis, [(i, (i + far) % size) for i in range(size)])]
    all_to_all x2, blocking collectives: 30.5 us -> 39.6 us  [exchange(): return lax.all_to_all(blocks, axis, 0, 0, tiled=True)]
    convert_element_type x5 -> x2, other arithmetic: 7.71 us -> 0.25 us  [the longest x1 0.22 us: body(): late.astype(BF16)]
  transfers between devices with their start and end apart: 34 -> 34, of which waited for: 15 -> 13; matrix products, arithmetic and copies ran while one was open for 9% -> 6% of each run, Pallas kernels for 14% -> 15%
where the time goes in v6:
time: 586 us; the launch traced here: 577 us
  waiting for transfers between devices  251 us (43%)
  Pallas kernels  133 us (23%)
  starting transfers between devices  79 us (13%)
  blocking collectives  39.6 us (7%)
  local copies, waits for them, and re-layouts  32.5 us (6%)
  other arithmetic  27.3 us (5%)
  between operations  14.7 us (3%)
    all_to_all x7, waiting for transfers between devices, exchange(): return lax.all_to_all(blocks, axis, 0, 0, tiled=True)  111 us
    ppermute x9, waiting for transfers between devices, chain_gather(): falling = tuple((lax.ppermute(block, axis, down) for block in falling))  83.2 us
    pallas_call x2, Pallas kernels, attend_backward(): pl.pallas_call(functools.partial(backward_kernel, top), grid_spec=pltpu.P...  44.7 us
    pallas_call x1, Pallas kernels, feed_forward(): pl.pallas_call(functools.partial(ffn_kernel, span, merged, heads), grid=(...  43.8 us
    all_to_all x2, blocking collectives, exchange(): return lax.all_to_all(blocks, axis, 0, 0, tiled=True)  39.6 us
    all_to_all x7, starting transfers between devices, exchange(): return lax.all_to_all(blocks, axis, 0, 0, tiled=True)  37.5 us
    reduce_scatter x1, waiting for transfers between devices, body(): grads = lax.psum_scatter(grads, DP, scatter_dimension=0, tiled=True)[0]  31.4 us
    pallas_call x2, Pallas kernels, attend_forward(): pl.pallas_call(functools.partial(forward_kernel, top), grid_spec=pltpu.Pr...  29.6 us
  transfers between devices with their start and end apart: 34, of which 13 were waited for; matrix products, arithmetic and copies ran while one was open for 6% of the time, Pallas kernels for 15%

profile of v6, /device:TPU:0, one launch (start us, length us, event | category | flops | bytes accessed | tf_op | source)
XLA Modules:
  0.0 577.0 jit_solution(4218747619056567042)
XLA Ops:
  16.8 10.9 %collective-permute-done.1 = bf16[40,3072]{1,0:T(8,128)(2,1)S(1)} collective-permute-done((bf16[40,3072]{1,0:T(8,128)(2,1)S(1)}, bf16[40,3072]{1,0:T(8,128)(2,1)S(1)}, u32[]{:S(2)}, u32[]{:S(2)}) %collective-permute-start.1) | collective-permute-done | bytes 245792 | tf_op jit(solution)/shard_map/ppermute | solution.py:600
  37.5 7.4 %collective-permute-start.3 = (bf16[32,6656]{1,0:T(8,128)(2,1)S(1)}, bf16[32,6656]{1,0:T(8,128)(2,1)S(1)}, u32[]{:S(2)}, u32[]{:S(2)}) collective-permute-start(bf16[32,6656]{1,0:T(8,128)(2,1)S(1)} %constant_dynamic-update-slice_fusion), channel_id=1, source_target_pairs={{0,1},{1,2},{2,3},{4,5},{5,6},{6,7},{8,9},{9,10},{10,11},{12,13},{... | collective-permute-start | bytes 1277960 | tf_op jit(solution)/shard_map/ppermute | solution.py:573
  50.6 7.4 %collective-permute-done.4 = bf16[88,1024]{1,0:T(8,128)(2,1)S(1)} collective-permute-done((bf16[88,1024]{1,0:T(8,128)(2,1)S(1)}, bf16[88,1024]{1,0:T(8,128)(2,1)S(1)}, u32[]{:S(2)}, u32[]{:S(2)}) %collective-permute-start.4) | collective-permute-done | bytes 180256 | tf_op jit(solution)/shard_map/ppermute | solution.py:573
  62.0 17.7 %collective-permute-done.10 = bf16[88,1024]{1,0:T(8,128)(2,1)S(1)} collective-permute-done((bf16[88,1024]{1,0:T(8,128)(2,1)S(1)}, bf16[88,1024]{1,0:T(8,128)(2,1)S(1)}, u32[]{:S(2)}, u32[]{:S(2)}) %collective-permute-start.10) | collective-permute-done | bytes 180256 | tf_op jit(solution)/shard_map/ppermute | solution.py:574
  83.6 12.6 %collective-permute-done.14 = bf16[88,1024]{1,0:T(8,128)(2,1)S(1)} collective-permute-done((bf16[88,1024]{1,0:T(8,128)(2,1)S(1)}, bf16[88,1024]{1,0:T(8,128)(2,1)S(1)}, u32[]{:S(2)}, u32[]{:S(2)}) %collective-permute-start.14) | collective-permute-done | bytes 180256 | tf_op jit(solution)/shard_map/ppermute | solution.py:574
  106.0 17.7 %collective-permute-done.18 = bf16[512,1024]{1,0:T(8,128)(2,1)S(1)} collective-permute-done((bf16[512,1024]{1,0:T(8,128)(2,1)S(1)}, bf16[512,1024]{1,0:T(8,128)(2,1)S(1)}, u32[]{:S(2)}, u32[]{:S(2)}) %collective-permute-start.18) | collective-permute-done | bytes 1048608 | tf_op jit(solution)/shard_map/ppermute | solution.py:574
  129.7 17.6 %collective-permute-done.19 = bf16[512,1024]{1,0:T(8,128)(2,1)} collective-permute-done((bf16[512,1024]{1,0:T(8,128)(2,1)S(1)}, bf16[512,1024]{1,0:T(8,128)(2,1)}, u32[]{:S(2)}, u32[]{:S(2)}) %collective-permute-start.19) | collective-permute-done | bytes 1048608 | tf_op jit(solution)/shard_map/ppermute | solution.py:574
  156.8 5.9 %all-to-all-start = ((bf16[4,256,512]{2,1,0:T(8,128)(2,1)}), bf16[4,256,512]{2,1,0:T(8,128)(2,1)}, u32[]{:S(2)}, u32[]{:S(2)}) async-start(bf16[4,256,512]{2,1,0:T(8,128)(2,1)} %pad_maximum_fusion.6), calls=%async_computation | async-start | bytes 2097152 | tf_op jit(solution)/shard_map/all_to_all | solution.py:609
  162.9 17.6 %collective-permute-done.20 = bf16[512,1024]{1,0:T(8,128)(2,1)S(1)} collective-permute-done((bf16[512,1024]{1,0:T(8,128)(2,1)}, bf16[512,1024]{1,0:T(8,128)(2,1)S(1)}, u32[]{:S(2)}, u32[]{:S(2)}) %collective-permute-start.20) | collective-permute-done | bytes 1048608 | tf_op jit(solution)/shard_map/ppermute | solution.py:574
  186.1 6.4 %slice.103 = bf16[32,32,3072]{2,1,0:T(8,128)(2,1)} slice(bf16[32,40,3072]{2,1,0:T(8,128)(2,1)} %all-gather.4.cloned.1.call-done), slice={[0:32], [0:32], [0:3072]} | slice | bytes 12582912 | tf_op jit(solution)/shard_map/slice | solution.py:641
  192.5 6.7 %project_qkv.1.q_ref.k_ref.v_ref = bf16[2048,768]{1,0:T(8,128)(2,1)S(1)} custom-call(s32[1]{0:T(128)} %bitcast.6.place_ref, bf16[2048,1024]{1,0:T(8,128)(2,1)} %pad_maximum_fusion.tok_ref, f32[1,1024]{1,0:T(1,128)S(1)} %reshape.179.gain_ref, bf16[1024,3072]{1,0:T(8,128)(2,1)} %bitcast.85, bf16[1024,3072]{1,0:T(8,128)(2,1)} %bitcast.86, ...), custom_call_target="tpu_custom_call" | custom-call | flops 3221225472 | bytes 14680064 | tf_op jit(solution)/shard_map/project_qkv/pallas_call | solution.py:62
  199.2 14.9 %attend_forward.3 = (bf16[2048,128]{1,0:T(8,128)(2,1)S(1)}, f32[2048,1]{1,0:T(8,128)S(1)}) custom-call(s32[32]{0:T(128)S(1)} %reshape_squeeze.24.chosen_ref, s32[32]{0:T(128)S(1)} %reshape_squeeze.25.counts_ref, bf16[2048,768]{1,0:T(8,128)(2,1)S(1)} %project_qkv.1.q_ref.k_ref.v_ref, bf16[2048,768]{1,0:T(8,128)(2,1)S(1)} %project_qkv.1.q_ref.k_ref.v_ref, ...), custom_call_target="tpu_custom_call" | custom-call | flops 1610612736 | bytes 2097152 | tf_op jit(solution)/shard_map/attend_forward/pallas_call | solution.py:152
  216.0 9.3 %all-to-all-start.2 = ((bf16[4,512,128]{2,1,0:T(8,128)(2,1)}), bf16[4,512,128]{2,1,0:T(8,128)(2,1)}, u32[]{:S(2)}, u32[]{:S(2)}) async-start(bf16[4,512,128]{2,1,0:T(8,128)(2,1)} %bitcast.81), calls=%async_computation.2 | async-start | bytes 1048576 | tf_op jit(solution)/shard_map/all_to_all | solution.py:609
  225.2 14.7 %attend_forward.2 = (bf16[2048,128]{1,0:T(8,128)(2,1)S(1)}, f32[2048,1]{1,0:T(8,128)S(1)}) custom-call(s32[32]{0:T(128)S(1)} %reshape_squeeze.24.chosen_ref, s32[32]{0:T(128)S(1)} %reshape_squeeze.25.counts_ref, bf16[2048,768]{1,0:T(8,128)(2,1)S(1)} %project_qkv.1.q_ref.k_ref.v_ref, bf16[2048,768]{1,0:T(8,128)(2,1)S(1)} %project_qkv.1.q_ref.k_ref.v_ref, ...), custom_call_target="tpu_custom_call" | custom-call | flops 1610612736 | bytes 2097152 | tf_op jit(solution)/shard_map/attend_forward/pallas_call | solution.py:152
  247.6 9.4 %all-to-all-done.1.rest_0_ = bf16[4,512,128]{2,1,0:T(8,128)(2,1)S(1)} async-done(((bf16[4,512,128]{2,1,0:T(8,128)(2,1)}), bf16[4,512,128]{2,1,0:T(8,128)(2,1)S(1)}, u32[]{:S(2)}, u32[]{:S(2)}) %all-to-all-start.1) | async-done | bytes 524320 | tf_op jit(solution)/shard_map/all_to_all | solution.py:609
  257.9 43.8 %feed_forward.1 = (bf16[512,1024]{1,0:T(8,128)(2,1)}, f32[512,1024]{1,0:T(8,128)}, f32[1,1024]{1,0:T(1,128)}, bf16[8,4736,256]{2,1,0:T(8,128)(2,1)}, bf16[4,512,...) custom-call(bf16[512,1024]{1,0:T(8,128)(2,1)} %bitcast.76, bf16[512,1024]{1,0:T(8,128)(2,1)} %bitcast.121, ...), custom_call_target="tpu_custom_call" | custom-call | flops 29796335616 | bytes 38797312 | tf_op jit(solution)/shard_map/feed_forward/pallas_call | solution.py:522
  302.7 14.8 %all_to_all.45 = bf16[4,512,128]{2,1,0:T(8,128)(2,1)} all-to-all(bf16[4,512,128]{2,1,0:T(8,128)(2,1)S(1)} %copy-done.22), channel_id=1, replica_groups=mesh['chip'=4,'core'=2,'fsdp'=4] {'fsdp'}, dimensions={0} | all-to-all | bytes 1048576 | tf_op jit(solution)/shard_map/all_to_all | solution.py:609
  325.3 22.6 %attend_backward.2 = (bf16[2048,384]{1,0:T(8,128)(2,1)}, bf16[1024,384]{1,0:T(8,128)(2,1)S(1)}, f32[1024,1]{1,0:T(8,128)S(1)}) custom-call(s32[32]{0:T(128)S(1)} %reshape_squeeze.24.chosen_ref, s32[32]{0:T(128)S(1)} %reshape_squeeze.25.counts_ref, s32[1]{0:T(128)} %bitcast.6.place_ref, bf16[2048,768]{1,0:T(8,128)(2,1)} %copy-done, ...), custom_call_target="tpu_custom_call" | custom-call | flops 4026531840 | bytes 4194304 | tf_op jit(solution)/shard_map/attend_backward/pallas_call | solution.py:279
  350.9 22.0 %attend_backward.3 = (bf16[2048,384]{1,0:T(8,128)(2,1)}, bf16[1024,384]{1,0:T(8,128)(2,1)S(1)}, f32[1024,1]{1,0:T(8,128)S(1)}) custom-call(s32[32]{0:T(128)S(1)} %reshape_squeeze.24.chosen_ref, s32[32]{0:T(128)S(1)} %reshape_squeeze.25.counts_ref, s32[1]{0:T(128)} %bitcast.6.place_ref, bf16[2048,768]{1,0:T(8,128)(2,1)} %copy-done, ...), custom_call_target="tpu_custom_call" | custom-call | flops 4026531840 | bytes 4194304 | tf_op jit(solution)/shard_map/attend_backward/pallas_call | solution.py:279
  376.0 24.8 %all_to_all.46 = bf16[4,136,768]{2,1,0:T(8,128)(2,1)S(1)} all-to-all(bf16[4,136,768]{2,1,0:T(8,128)(2,1)S(1)} %fusion), channel_id=1, replica_groups=mesh['chip'=4,'core'=2,'fsdp'=4] {'chip'}, dimensions={0} | all-to-all | bytes 1671168 | tf_op jit(solution)/shard_map/all_to_all | solution.py:609
  406.9 31.4 %reduce-scatter.3.cloned.1.call-done = bf16[1,4736,256]{2,1,0:T(8,128)(2,1)} async-done(((bf16[8,4736,256]{2,1,0:T(8,128)(2,1)}), bf16[1,4736,256]{2,1,0:T(8,128)(2,1)}) %reduce-scatter.3.cloned.1.call-update) | async-done | bytes 2424848 | tf_op jit(solution)/shard_map/reduce_scatter | solution.py:667
  449.4 70.0 %all-to-all-done.6.refs_1_ = bf16[4,512,384]{2,1,0:T(8,128)(2,1)S(1)} async-done(((bf16[4,512,384]{2,1,0:T(8,128)(2,1)}), bf16[4,512,384]{2,1,0:T(8,128)(2,1)S(1)}, u32[]{:S(2)}, u32[]{:S(2)}) %all-to-all-start.6) | async-done | bytes 1572896 | tf_op jit(solution)/shard_map/all_to_all | solution.py:609
  525.9 31.6 %all-to-all-done.4.refs_0_ = bf16[4,512,384]{2,1,0:T(8,128)(2,1)S(1)} async-done(((bf16[4,512,384]{2,1,0:T(8,128)(2,1)}), bf16[4,512,384]{2,1,0:T(8,128)(2,1)S(1)}, u32[]{:S(2)}, u32[]{:S(2)}) %all-to-all-start.4) | async-done | bytes 1572896 | tf_op jit(solution)/shard_map/all_to_all | solution.py:609
  558.8 7.9 %finish_tokens.1 = bf16[512,1024]{1,0:T(8,128)(2,1)} custom-call(bf16[512,1024]{1,0:T(8,128)(2,1)S(1)} %bitcast.80, f32[1,1024]{1,0:T(1,128)S(1)} %reshape.179.gain_ref, f32[512,1024]{1,0:T(8,128)} %get-tuple-element.60.mid_ref, bf16[1024,3072]{1,0:T(8,128)(2,1)} %bitcast.94, bf16[4,512,384]{2,1,0:T(8,128)(2,1)S(1)} %all-to-all-done.4.refs_0_, ...), custom_call_target="tpu_custom_call" | custom-call | flops 3221225472 | bytes 8388608 | tf_op jit(solution)/shard_map/finish_tokens/pallas_call | solution.py:355
  (191 shorter events, 117.1 us)
Async XLA Ops:
  7.2 177.8 %all-gather.4.cloned.1.call-start = ((), (), s32[]{:S(2)}) async-start(), calls=%async_computation.11 | async-start | bytes 8847360 | tf_op jit(solution)/shard_map/all_gather | solution.py:637
  10.7 17.1 %collective-permute-start.1 = (bf16[40,3072]{1,0:T(8,128)(2,1)S(1)}, bf16[40,3072]{1,0:T(8,128)(2,1)S(1)}, u32[]{:S(2)}, u32[]{:S(2)}) collective-permute-start(bf16[40,3072]{1,0:T(8,128)(2,1)S(1)} %maximum_maximum_fusion), channel_id=1, source_target_pairs={{0,2},{1,3},{2,0},{3,1},{4,6},{5,7},{6,4},{7,5},{8,10},{9,11},{10,... | collective-permute-start | bytes 737288 | tf_op jit(solution)/shard_map/ppermute | solution.py:600
  36.1 211.5 %all-gather.8.cloned.1.call-start = ((), (), s32[]{:S(2)}) async-start(), calls=%async_computation.13 | async-start | bytes 6488064 | tf_op jit(solution)/shard_map/all_gather | solution.py:651
  36.2 21.8 %collective-permute-start.5 = (bf16[32,6656]{1,0:T(8,128)(2,1)S(1)}, bf16[32,6656]{1,0:T(8,128)(2,1)S(1)}, u32[]{:S(2)}, u32[]{:S(2)}) collective-permute-start(bf16[32,6656]{1,0:T(8,128)(2,1)S(1)} %constant_dynamic-update-slice_fusion), channel_id=1, source_target_pairs={{1,0},{2,1},{3,2},{5,4},{6,5},{7,6},{9,8},{10,9},{11,10},{13,12},{... | collective-permute-start | bytes 1277960 | tf_op jit(solution)/shard_map/ppermute | solution.py:574
  37.5 20.5 %collective-permute-start.3 = (bf16[32,6656]{1,0:T(8,128)(2,1)S(1)}, bf16[32,6656]{1,0:T(8,128)(2,1)S(1)}, u32[]{:S(2)}, u32[]{:S(2)}) collective-permute-start(bf16[32,6656]{1,0:T(8,128)(2,1)S(1)} %constant_dynamic-update-slice_fusion), channel_id=1, source_target_pairs={{0,1},{1,2},{2,3},{4,5},{5,6},{6,7},{8,9},{9,10},{10,11},{12,13},{... | collective-permute-start | bytes 1277960 | tf_op jit(solution)/shard_map/ppermute | solution.py:573
  58.0 21.6 %collective-permute-start.7 = (bf16[32,6656]{1,0:T(8,128)(2,1)S(1)}, bf16[32,6656]{1,0:T(8,128)(2,1)S(1)}, u32[]{:S(2)}, u32[]{:S(2)}) collective-permute-start(bf16[32,6656]{1,0:T(8,128)(2,1)S(1)} %collective-permute-done.3), channel_id=1, source_target_pairs={{1,2},{2,3},{5,6},{6,7},{9,10},{10,11},{13,14},{14,15},{17,18},{18... | collective-permute-start | bytes 1277960 | tf_op jit(solution)/shard_map/ppermute | solution.py:573
  58.7 21.0 %collective-permute-start.9 = (bf16[32,6656]{1,0:T(8,128)(2,1)S(1)}, bf16[32,6656]{1,0:T(8,128)(2,1)S(1)}, u32[]{:S(2)}, u32[]{:S(2)}) collective-permute-start(bf16[32,6656]{1,0:T(8,128)(2,1)S(1)} %collective-permute-done.5), channel_id=1, source_target_pairs={{1,0},{2,1},{5,4},{6,5},{9,8},{10,9},{13,12},{14,13},{17,16},{18,1... | collective-permute-start | bytes 1277960 | tf_op jit(solution)/shard_map/ppermute | solution.py:574
  60.7 19.0 %collective-permute-start.10 = (bf16[88,1024]{1,0:T(8,128)(2,1)S(1)}, bf16[88,1024]{1,0:T(8,128)(2,1)S(1)}, u32[]{:S(2)}, u32[]{:S(2)}) collective-permute-start(bf16[88,1024]{1,0:T(8,128)(2,1)S(1)} %collective-permute-done.6), channel_id=1, source_target_pairs={{1,0},{2,1},{5,4},{6,5},{9,8},{10,9},{13,12},{14,13},{17,16},{18,1... | collective-permute-start | bytes 540680 | tf_op jit(solution)/shard_map/ppermute | solution.py:574
  79.7 16.6 %collective-permute-start.11 = (bf16[32,6656]{1,0:T(8,128)(2,1)S(1)}, bf16[32,6656]{1,0:T(8,128)(2,1)S(1)}, u32[]{:S(2)}, u32[]{:S(2)}) collective-permute-start(bf16[32,6656]{1,0:T(8,128)(2,1)S(1)} %collective-permute-done.7), channel_id=1, source_target_pairs={{2,3},{6,7},{10,11},{14,15},{18,19},{22,23},{26,27},{30,31}} | collective-permute-start | bytes 1277960 | tf_op jit(solution)/shard_map/ppermute | solution.py:573
  97.3 159.8 %all-gather.6.cloned.1.call-start = ((), (), s32[]{:S(2)}) async-start(), calls=%async_computation.12 | async-start | bytes 15335424 | tf_op jit(solution)/shard_map/all_gather | solution.py:644
  99.2 24.5 %collective-permute-start.18 = (bf16[512,1024]{1,0:T(8,128)(2,1)S(1)}, bf16[512,1024]{1,0:T(8,128)(2,1)S(1)}, u32[]{:S(2)}, u32[]{:S(2)}) collective-permute-start(bf16[512,1024]{1,0:T(8,128)(2,1)S(1)} %bitcast.77), channel_id=1, source_target_pairs={{1,0},{2,1},{3,2},{5,4},{6,5},{7,6},{9,8},{10,9},{11,10},{13,12},{... | collective-permute-start | bytes 3145736 | tf_op jit(solution)/shard_map/ppermute | solution.py:574
  100.5 24.5 %collective-permute-start.15 = (bf16[512,1024]{1,0:T(8,128)(2,1)S(1)}, bf16[512,1024]{1,0:T(8,128)(2,1)}, u32[]{:S(2)}, u32[]{:S(2)}) collective-permute-start(bf16[512,1024]{1,0:T(8,128)(2,1)S(1)} %bitcast.78), channel_id=1, source_target_pairs={{0,1},{1,2},{2,3},{4,5},{5,6},{6,7},{8,9},{9,10},{10,11},{12,13},{... | collective-permute-start | bytes 3145736 | tf_op jit(solution)/shard_map/ppermute | solution.py:573
  123.7 23.7 %collective-permute-start.19 = (bf16[512,1024]{1,0:T(8,128)(2,1)S(1)}, bf16[512,1024]{1,0:T(8,128)(2,1)}, u32[]{:S(2)}, u32[]{:S(2)}) collective-permute-start(bf16[512,1024]{1,0:T(8,128)(2,1)S(1)} %collective-permute-done.18), channel_id=1, source_target_pairs={{1,0},{2,1},{5,4},{6,5},{9,8},{10,9},{13,12},{14,13},{17,16},{18,1... | collective-permute-start | bytes 3145736 | tf_op jit(solution)/shard_map/ppermute | solution.py:574
  125.0 23.7 %collective-permute-start.16 = (bf16[512,1024]{1,0:T(8,128)(2,1)}, bf16[512,1024]{1,0:T(8,128)(2,1)}, u32[]{:S(2)}, u32[]{:S(2)}) collective-permute-start(bf16[512,1024]{1,0:T(8,128)(2,1)} %collective-permute-done.15), channel_id=1, source_target_pairs={{1,2},{2,3},{5,6},{6,7},{9,10},{10,11},{13,14},{14,15},{17,18},{18... | collective-permute-start | bytes 3145736 | tf_op jit(solution)/shard_map/ppermute | solution.py:573
  147.3 33.2 %collective-permute-start.20 = (bf16[512,1024]{1,0:T(8,128)(2,1)}, bf16[512,1024]{1,0:T(8,128)(2,1)S(1)}, u32[]{:S(2)}, u32[]{:S(2)}) collective-permute-start(bf16[512,1024]{1,0:T(8,128)(2,1)} %collective-permute-done.19), channel_id=1, source_target_pairs={{1,0},{5,4},{9,8},{13,12},{17,16},{21,20},{25,24},{29,28}} | collective-permute-start | bytes 3145736 | tf_op jit(solution)/shard_map/ppermute | solution.py:574
  148.6 31.9 %collective-permute-start.17 = (bf16[512,1024]{1,0:T(8,128)(2,1)}, bf16[512,1024]{1,0:T(8,128)(2,1)}, u32[]{:S(2)}, u32[]{:S(2)}) collective-permute-start(bf16[512,1024]{1,0:T(8,128)(2,1)} %collective-permute-done.16), channel_id=1, source_target_pairs={{2,3},{6,7},{10,11},{14,15},{18,19},{22,23},{26,27},{30,31}} | collective-permute-start | bytes 3145736 | tf_op jit(solution)/shard_map/ppermute | solution.py:573
  156.8 42.4 %all-to-all-start = ((bf16[4,256,512]{2,1,0:T(8,128)(2,1)}), bf16[4,256,512]{2,1,0:T(8,128)(2,1)}, u32[]{:S(2)}, u32[]{:S(2)}) async-start(bf16[4,256,512]{2,1,0:T(8,128)(2,1)} %pad_maximum_fusion.6), calls=%async_computation | async-start | bytes 2097152 | tf_op jit(solution)/shard_map/all_to_all | solution.py:609
  216.0 25.7 %all-to-all-start.2 = ((bf16[4,512,128]{2,1,0:T(8,128)(2,1)}), bf16[4,512,128]{2,1,0:T(8,128)(2,1)}, u32[]{:S(2)}, u32[]{:S(2)}) async-start(bf16[4,512,128]{2,1,0:T(8,128)(2,1)} %bitcast.81), calls=%async_computation.2 | async-start | bytes 1048576 | tf_op jit(solution)/shard_map/all_to_all | solution.py:609
  246.8 191.5 %reduce-scatter.3.cloned.1.call-start = ((), (), s32[]{:S(2)}) async-start(), calls=%async_computation.14 | async-start | bytes 21823488 | tf_op jit(solution)/shard_map/reduce_scatter | solution.py:667
  317.5 32.1 %all-to-all-start.5 = ((bf16[4,512,128]{2,1,0:T(8,128)(2,1)}), bf16[4,512,128]{2,1,0:T(8,128)(2,1)S(1)}, u32[]{:S(2)}, u32[]{:S(2)}) async-start(bf16[4,512,128]{2,1,0:T(8,128)(2,1)} %get-tuple-element.66), calls=%async_computation.5 | async-start | bytes 1048576 | tf_op jit(solution)/shard_map/all_to_all | solution.py:609
  401.8 40.3 %all-to-all-start.8 = ((bf16[4,40,768]{2,1,0:T(8,128)(2,1)}), bf16[4,40,768]{2,1,0:T(8,128)(2,1)S(1)}, u32[]{:S(2)}, u32[]{:S(2)}) async-start(bf16[4,40,768]{2,1,0:T(8,128)(2,1)} %fusion.8), calls=%async_computation.8 | async-start | bytes 491520 | tf_op jit(solution)/shard_map/all_to_all | solution.py:609
  442.1 77.3 %all-to-all-start.6 = ((bf16[4,512,384]{2,1,0:T(8,128)(2,1)}), bf16[4,512,384]{2,1,0:T(8,128)(2,1)S(1)}, u32[]{:S(2)}, u32[]{:S(2)}) async-start(bf16[4,512,384]{2,1,0:T(8,128)(2,1)} %bitcast.107), calls=%async_computation.6 | async-start | bytes 3145728 | tf_op jit(solution)/shard_map/all_to_all | solution.py:609
  446.7 120.0 %reduce-scatter.5.cloned.1.call-start = ((), (), s32[]{:S(2)}) async-start(), calls=%async_computation.15 | async-start | bytes 3031040 | tf_op jit(solution)/shard_map/reduce_scatter | solution.py:722
  519.4 38.1 %all-to-all-start.4 = ((bf16[4,512,384]{2,1,0:T(8,128)(2,1)}), bf16[4,512,384]{2,1,0:T(8,128)(2,1)S(1)}, u32[]{:S(2)}, u32[]{:S(2)}) async-start(bf16[4,512,384]{2,1,0:T(8,128)(2,1)} %bitcast.106), calls=%async_computation.4 | async-start | bytes 3145728 | tf_op jit(solution)/shard_map/all_to_all | solution.py:609
  (38 other events, 334.9 us)
Sparse Core Ops, SparseCore 0:
  36.2 56.5 all-gather.3
  97.4 41.5 all-gather.7
  140.9 76.5 all-gather.5
  301.8 136.3 reduce-scatter.2
  449.6 72.0 reduce-scatter.4

commit v7 on v6

--- a/solution.py
+++ b/solution.py
@@ -37,49 +37,46 @@
     return jnp.concatenate([cosine, cosine], 1), jnp.concatenate([-sine, sine], 1)
 
 
-def qkv_kernel(heads, place_ref, tok_ref, gain_ref, wq_ref, wk_ref, wv_ref, cos_ref, sin_ref, qkv_ref):
+def qkv_kernel(heads, tok_ref, gain_ref, w_ref, cos_ref, sin_ref, qkv_ref):
     rows = tok_ref[...].astype(F32)
     factor = lax.rsqrt(jnp.mean(rows * rows, -1, keepdims=True) + EPSILON)
     normed = (rows * factor * gain_ref[...]).astype(BF16)
     cosine, sine = cos_ref[...], sin_ref[...]
-    for part, w_ref in enumerate((wq_ref, wk_ref, wv_ref)):
-        values = dot(normed, w_ref[...])
+    wide = heads * HEAD_DIM
+    for part in range(3):
+        values = dot(normed, w_ref[:, part * wide : (part + 1) * wide])
         for head in range(heads):
             value = values[:, head * HEAD_DIM : (head + 1) * HEAD_DIM]
             if part < 2:
                 value = value * cosine + pltpu.roll(value, HEAD_DIM // 2, 1) * sine
             if part == 0:
                 value = value * (SCALE * LOG2E)
-            at = (part * heads + head) * HEAD_DIM
+            at = part * wide + head * HEAD_DIM
             qkv_ref[:, at : at + HEAD_DIM] = value.astype(BF16)
 
 
-def project_qkv(place, tokens_all, gain, w_qkv, cosine, sine, heads, ring):
+def project_qkv(tokens_all, gain, w_qkv, cosine, sine, heads):
     length, width = tokens_all.shape
-    wide = heads * HEAD_DIM
+    columns = w_qkv.shape[1]
     block = 2 * QBLK
-    part = [pl.BlockSpec((width, wide), lambda i, place, p=p: (0, p * ring + place[0])) for p in range(3)]
     return pl.pallas_call(
         functools.partial(qkv_kernel, heads),
-        grid_spec=pltpu.PrefetchScalarGridSpec(
-            num_scalar_prefetch=1,
-            grid=(length // block,),
-            in_specs=[
-                pl.BlockSpec((block, width), lambda i, _: (i, 0)),
-                pl.BlockSpec((1, width), lambda i, _: (0, 0)),
-                *part,
-                pl.BlockSpec((block, HEAD_DIM), lambda i, _: (i, 0)),
-                pl.BlockSpec((block, HEAD_DIM), lambda i, _: (i, 0)),
-            ],
-            out_specs=pl.BlockSpec((block, 3 * wide), lambda i, _: (i, 0)),
-        ),
-        out_shape=jax.ShapeDtypeStruct((length, 3 * wide), BF16),
+        grid=(length // block,),
+        in_specs=[
+            pl.BlockSpec((block, width), lambda i: (i, 0)),
+            pl.BlockSpec((1, width), lambda i: (0, 0)),
+            pl.BlockSpec((width, columns), lambda i: (0, 0)),
+            pl.BlockSpec((block, HEAD_DIM), lambda i: (i, 0)),
+            pl.BlockSpec((block, HEAD_DIM), lambda i: (i, 0)),
+        ],
+        out_specs=pl.BlockSpec((block, columns), lambda i: (i, 0)),
+        out_shape=jax.ShapeDtypeStruct((length, columns), BF16),
         compiler_params=pltpu.CompilerParams(vmem_limit_bytes=48 * MIB),
         cost_estimate=pl.CostEstimate(
-            flops=6 * length * width * wide, bytes_accessed=4 * length * (width + 3 * wide), transcendentals=0
+            flops=2 * length * width * columns, bytes_accessed=4 * length * (width + columns), transcendentals=0
         ),
         name="project_qkv",
-    )(place, tokens_all, gain, w_qkv, w_qkv, w_qkv, cosine, sine)
+    )(tokens_all, gain, w_qkv, cosine, sine)
 
 
 def memory_bias(counts_ref, base, top, axis):
@@ -92,16 +89,16 @@
     return jnp.where(limit > 0, 0.0, NEGATIVE)
 
 
-def pick_memory(ref, chosen_ref, base, top):
+def pick_memory(ref, chosen_ref, base, top, columns=slice(None)):
     rows = [
-        ref[pl.ds(pl.multiple_of(chosen_ref[base + entry] * MBLK, MBLK), MBLK), :]
+        ref[pl.ds(pl.multiple_of(chosen_ref[base + entry] * MBLK, MBLK), MBLK), columns]
         for entry in range(top)
     ]
     return jnp.concatenate(rows, 0)
 
 
 def forward_kernel(
-    top, chosen_ref, counts_ref, q_ref, k_ref, v_ref, mk_ref, mv_ref, out_ref, lse_ref, acc_s, peak_s
+    heads, top, chosen_ref, counts_ref, q_ref, k_ref, v_ref, mk_ref, mv_ref, out_ref, lse_ref, acc_s, peak_s
 ):
     block = pl.program_id(0)
     rows = q_ref.shape[0]
@@ -110,82 +107,90 @@
     causal = lax.broadcasted_iota(jnp.int32, (rows, rows), 0) >= lax.broadcasted_iota(jnp.int32, (rows, rows), 1)
     ones = jnp.ones((rows, HEAD_DIM), BF16)
     mem_ones = jnp.ones((top * MBLK, HEAD_DIM), BF16)
-    remote = []
-    for sub in range(subs):
-        base = (block * subs + sub) * top
-        keys = pick_memory(mk_ref, chosen_ref, base, top)
-        query = q_ref[sub * QBLK : (sub + 1) * QBLK, :]
-        remote.append(dot(query, keys, NT) + memory_bias(counts_ref, base, top, 1))
-    local = jnp.where(causal, dot(q_ref[...], k_ref[own, :], NT), NEGATIVE)
-    peak = jnp.max(local, -1, keepdims=True)
-    peak = jnp.maximum(peak, jnp.concatenate([jnp.max(r, -1, keepdims=True) for r in remote], 0))
-    acc = dot(jnp.exp2(local - peak).astype(BF16), jnp.concatenate([v_ref[own, :], ones], 1))
-    more = []
-    for sub in range(subs):
-        values = pick_memory(mv_ref, chosen_ref, (block * subs + sub) * top, top)
-        weights = jnp.exp2(remote[sub] - peak[sub * QBLK : (sub + 1) * QBLK]).astype(BF16)
-        more.append(dot(weights, jnp.concatenate([values, mem_ones], 1)))
-    acc_s[...] = acc + jnp.concatenate(more, 0)
-    peak_s[...] = jnp.broadcast_to(peak, (rows, HEAD_DIM))
+    biases = [memory_bias(counts_ref, (block * subs + sub) * top, top, 1) for sub in range(subs)]
+    for head in range(heads):
+        columns = slice(head * HEAD_DIM, (head + 1) * HEAD_DIM)
+        remote = []
+        for sub in range(subs):
+            keys = pick_memory(mk_ref, chosen_ref, (block * subs + sub) * top, top, columns)
+            query = q_ref[sub * QBLK : (sub + 1) * QBLK, columns]
+            remote.append(dot(query, keys, NT) + biases[sub])
+        local = jnp.where(causal, dot(q_ref[:, columns], k_ref[own, columns], NT), NEGATIVE)
+        peak = jnp.max(local, -1, keepdims=True)
+        peak = jnp.maximum(peak, jnp.concatenate([jnp.max(r, -1, keepdims=True) for r in remote], 0))
+        values = jnp.concatenate([v_ref[own, columns], ones], 1)
+        acc = dot(jnp.exp2(local - peak).astype(BF16), values)
+        more = []
+        for sub in range(subs):
+            values = pick_memory(mv_ref, chosen_ref, (block * subs + sub) * top, top, columns)
+            weights = jnp.exp2(remote[sub] - peak[sub * QBLK : (sub + 1) * QBLK]).astype(BF16)
+            more.append(dot(weights, jnp.concatenate([values, mem_ones], 1)))
+        acc_s[head] = acc + jnp.concatenate(more, 0)
+        peak_s[head] = jnp.broadcast_to(peak, (rows, HEAD_DIM))
 
     def step(index, carry):
         there = pl.ds(pl.multiple_of(index * rows, rows), rows)
-        peak = peak_s[:, :1]
-        scores = dot(q_ref[...], k_ref[there, :], NT)
-        higher = jnp.maximum(peak, jnp.max(scores, -1, keepdims=True))
-        weights = jnp.exp2(scores - higher).astype(BF16)
-        values = jnp.concatenate([v_ref[there, :], ones], 1)
-        acc_s[...] = acc_s[...] * jnp.exp2(peak - higher) + dot(weights, values)
-        peak_s[...] = jnp.broadcast_to(higher, (rows, HEAD_DIM))
+        for head in range(heads):
+            columns = slice(head * HEAD_DIM, (head + 1) * HEAD_DIM)
+            peak = peak_s[head][:, :1]
+            scores = dot(q_ref[:, columns], k_ref[there, columns], NT)
+            higher = jnp.maximum(peak, jnp.max(scores, -1, keepdims=True))
+            weights = jnp.exp2(scores - higher).astype(BF16)
+            values = jnp.concatenate([v_ref[there, columns], ones], 1)
+            acc_s[head] = acc_s[head] * jnp.exp2(peak - higher) + dot(weights, values)
+            peak_s[head] = jnp.broadcast_to(higher, (rows, HEAD_DIM))
         return carry
 
     lax.fori_loop(0, block, step, 0)
-    total = acc_s[:, HEAD_DIM:]
-    out_ref[...] = (acc_s[:, :HEAD_DIM] / total).astype(BF16)
-    lse_ref[...] = peak_s[:, :1] + jnp.log2(total[:, :1])
-
-
-def attend_forward(chosen, counts, qkv, memory, head, heads, top):
+    for head in range(heads):
+        columns = slice(head * HEAD_DIM, (head + 1) * HEAD_DIM)
+        total = acc_s[head][:, HEAD_DIM:]
+        out_ref[:, columns] = (acc_s[head][:, :HEAD_DIM] / total).astype(BF16)
+        lse_ref[:, head : head + 1] = peak_s[head][:, :1] + jnp.log2(total[:, :1])
+
+
+def attend_forward(chosen, counts, qkv, memory, heads, top):
     length = qkv.shape[0]
+    wide = heads * HEAD_DIM
     rows = min(2 * QBLK, length)
     mem_rows = memory.shape[0]
     return pl.pallas_call(
-        functools.partial(forward_kernel, top),
+        functools.partial(forward_kernel, heads, top),
         grid_spec=pltpu.PrefetchScalarGridSpec(
             num_scalar_prefetch=2,
             grid=(length // rows,),
             in_specs=[
-                pl.BlockSpec((rows, HEAD_DIM), lambda i, *_: (i, head)),
-                pl.BlockSpec((length, HEAD_DIM), lambda i, *_: (0, heads + head)),
-                pl.BlockSpec((length, HEAD_DIM), lambda i, *_: (0, 2 * heads + head)),
-                pl.BlockSpec((mem_rows, HEAD_DIM), lambda i, *_: (0, head)),
-                pl.BlockSpec((mem_rows, HEAD_DIM), lambda i, *_: (0, heads + head)),
+                pl.BlockSpec((rows, wide), lambda i, *_: (i, 0)),
+                pl.BlockSpec((length, wide), lambda i, *_: (0, 1)),
+                pl.BlockSpec((length, wide), lambda i, *_: (0, 2)),
+                pl.BlockSpec((mem_rows, wide), lambda i, *_: (0, 0)),
+                pl.BlockSpec((mem_rows, wide), lambda i, *_: (0, 1)),
             ],
             out_specs=[
-                pl.BlockSpec((rows, HEAD_DIM), lambda i, *_: (i, 0)),
-                pl.BlockSpec((rows, 1), lambda i, *_: (i, 0)),
+                pl.BlockSpec((rows, wide), lambda i, *_: (i, 0)),
+                pl.BlockSpec((rows, heads), lambda i, *_: (i, 0)),
             ],
             scratch_shapes=[
-                pltpu.VMEM((rows, 2 * HEAD_DIM), F32),
-                pltpu.VMEM((rows, HEAD_DIM), F32),
+                pltpu.VMEM((heads, rows, 2 * HEAD_DIM), F32),
+                pltpu.VMEM((heads, rows, HEAD_DIM), F32),
             ],
         ),
         out_shape=[
-            jax.ShapeDtypeStruct((length, HEAD_DIM), BF16),
-            jax.ShapeDtypeStruct((length, 1), F32),
+            jax.ShapeDtypeStruct((length, wide), BF16),
+            jax.ShapeDtypeStruct((length, heads), F32),
         ],
         compiler_params=pltpu.CompilerParams(vmem_limit_bytes=48 * MIB),
         cost_estimate=pl.CostEstimate(
-            flops=4 * length * HEAD_DIM * (length // 2 + top * MBLK),
-            bytes_accessed=8 * length * HEAD_DIM,
-            transcendentals=length * (length // 2 + top * MBLK),
+            flops=4 * heads * length * HEAD_DIM * (length // 2 + top * MBLK),
+            bytes_accessed=8 * length * wide,
+            transcendentals=heads * length * (length // 2 + top * MBLK),
         ),
         name="attend_forward",
     )(chosen, counts, qkv, qkv, qkv, memory, memory)
 
 
 def backward_kernel(
-    top, chosen_ref, counts_ref, place_ref, q_ref, k_ref, v_ref, mk_ref, mv_ref, go_ref, out_ref, lse_ref,
+    head, top, chosen_ref, counts_ref, q_ref, k_ref, v_ref, mk_ref, mv_ref, go_ref, out_ref, lse_ref,
     cos_ref, sin_ref, tok_ref, gain_ref, wq_ref, wk_ref, wv_ref, grad_ref, grad_w_ref, gain_grad_ref,
     gk_s, gv_s, gq_s, gw_s,
 ):
@@ -206,7 +211,7 @@
     def spread(column):
         return jnp.transpose(jnp.broadcast_to(column, (rows, HEAD_DIM)))[:1]
 
-    lse = spread(lse_ref[...])
+    lse = spread(lse_ref[:, head : head + 1])
     delta = spread(jnp.sum(go_ref[...].astype(F32) * out_ref[...].astype(F32), -1, keepdims=True))
 
     def pair(queries, keys, values, mask):
@@ -265,7 +270,7 @@
 
 
 def attend_backward(
-    chosen, counts, place, qkv, memory, grad_out, out, lse, cosine, sine, tokens_all, gain, w_qkv, head, heads, top, ring
+    chosen, counts, qkv, memory, grad_out, out, lse, cosine, sine, tokens_all, gain, w_qkv, head, heads, top
 ):
     length = qkv.shape[0]
     width = tokens_all.shape[1]
@@ -273,13 +278,12 @@
     mem_rows = memory.shape[0]
     last = length // rows - 1
     parts = [
-        pl.BlockSpec((width, HEAD_DIM), lambda i, c, n, place, p=p: (0, (p * ring + place[0]) * heads + head))
-        for p in range(3)
+        pl.BlockSpec((width, HEAD_DIM), lambda i, c, n, p=p: (0, p * heads + head)) for p in range(3)
     ]
     return pl.pallas_call(
-        functools.partial(backward_kernel, top),
+        functools.partial(backward_kernel, head, top),
         grid_spec=pltpu.PrefetchScalarGridSpec(
-            num_scalar_prefetch=3,
+            num_scalar_prefetch=2,
             grid=(last + 1,),
             in_specs=[
                 pl.BlockSpec((rows, HEAD_DIM), lambda i, *_: (last - i, head)),
@@ -288,8 +292,8 @@
                 pl.BlockSpec((mem_rows, HEAD_DIM), lambda i, *_: (0, head)),
                 pl.BlockSpec((mem_rows, HEAD_DIM), lambda i, *_: (0, heads + head)),
                 pl.BlockSpec((rows, HEAD_DIM), lambda i, *_: (last - i, 0)),
-                pl.BlockSpec((rows, HEAD_DIM), lambda i, *_: (last - i, 0)),
-                pl.BlockSpec((rows, 1), lambda i, *_: (last - i, 0)),
+                pl.BlockSpec((rows, HEAD_DIM), lambda i, *_: (last - i, head)),
+                pl.BlockSpec((rows, heads), lambda i, *_: (last - i, 0)),
                 pl.BlockSpec((rows, HEAD_DIM), lambda i, *_: (last - i, 0)),
                 pl.BlockSpec((rows, HEAD_DIM), lambda i, *_: (last - i, 0)),
                 pl.BlockSpec((rows, width), lambda i, *_: (last - i, 0)),
@@ -321,7 +325,7 @@
         ),
         name="attend_backward",
     )(
-        chosen, counts, place, qkv, qkv, qkv, memory, memory, grad_out, out, lse, cosine, sine, tokens_all, gain,
+        chosen, counts, qkv, qkv, qkv, memory, memory, grad_out, out, lse, cosine, sine, tokens_all, gain,
         w_qkv, w_qkv, w_qkv,
     )
 
@@ -375,7 +379,7 @@
 def ffn_kernel(
     span, merged, heads, tok_ref, cot_ref, gain_ref, out_w, gate_w, up_w, down_w, *rest
 ):
-    att_refs, rest = rest[:heads], rest[heads:]
+    att_ref, rest = rest[0], rest[1:]
     mixed_ref, grad_mid_ref, gain_grad_ref, grads_ref, *rest = rest
     grad_att_refs, rest = rest[:heads], rest[heads:]
     if not merged:
@@ -393,10 +397,9 @@
 
     @pl.when(step == 0)
     def _():
-        for place in range(att_refs[0].shape[0]):
-            for head in range(heads):
-                at = (place * heads + head) * HEAD_DIM
-                att_s[:, at : at + HEAD_DIM] = att_refs[head][place]
+        for place in range(att_ref.shape[0]):
+            at = place * heads * HEAD_DIM
+            att_s[:, at : at + heads * HEAD_DIM] = att_ref[place]
         middle = tok_ref[...].astype(F32) + dot(att_s[...], out_w[...])
         middle_s[...] = middle
         factor = lax.rsqrt(jnp.mean(middle * middle, -1, keepdims=True) + EPSILON)
@@ -467,7 +470,7 @@
         grad_mid_ref[...] = grad_middle
         branch = grad_middle.astype(BF16)
         grad_att = dot(branch, out_w[...], NT).astype(BF16)
-        for place in range(att_refs[0].shape[0]):
+        for place in range(att_ref.shape[0]):
             for head in range(heads):
                 at = (place * heads + head) * HEAD_DIM
                 grad_att_refs[head][place] = grad_att[:, at : at + HEAD_DIM]
@@ -492,7 +495,8 @@
 
 def feed_forward(tokens, attended, upstream, gain, weights, w_down, span):
     rows, width = tokens.shape
-    heads, ring = len(attended), attended[0].shape[0]
+    ring = attended.shape[0]
+    heads = attended.shape[2] // HEAD_DIM
     hidden_width = w_down.shape[0]
     wide = 2 * HEAD_DIM
     steps = hidden_width // wide
@@ -506,9 +510,9 @@
         jax.ShapeDtypeStruct((rows, width), F32),
         jax.ShapeDtypeStruct((1, width), F32),
         jax.ShapeDtypeStruct((span, total, wide), BF16),
-        *[jax.ShapeDtypeStruct((ring, rows, HEAD_DIM), BF16) for _ in attended],
+        *[jax.ShapeDtypeStruct((ring, rows, HEAD_DIM), BF16) for _ in range(heads)],
     ]
-    by_head = [pl.BlockSpec((ring, rows, HEAD_DIM), lambda i: (0, 0, 0)) for _ in attended]
+    by_head = [pl.BlockSpec((ring, rows, HEAD_DIM), lambda i: (0, 0, 0)) for _ in range(heads)]
     specs = [
         pl.BlockSpec((rows, width), lambda i: (0, 0)),
         pl.BlockSpec((rows, width), lambda i: (0, 0)),
@@ -530,7 +534,7 @@
             pl.BlockSpec((width, wide), lambda i: (0, lanes + i)),
             pl.BlockSpec((width, wide), lambda i: (0, lanes + steps + i)),
             pl.BlockSpec((wide, width), lambda i: (i, 0)),
-            *by_head,
+            pl.BlockSpec(attended.shape, lambda i: (0, 0, 0)),
         ],
         out_specs=specs,
         out_shape=shapes,
@@ -555,7 +559,7 @@
             transcendentals=rows * hidden_width,
         ),
         name="feed_forward",
-    )(tokens, upstream, gain, weights, weights, weights, w_down, *attended)
+    )(tokens, upstream, gain, weights, weights, weights, w_down, attended)
 
 
 def after(value, earlier):
@@ -624,21 +628,24 @@
     mine = tokens[0]
 
     extra = 8 if share % 8 == 0 else 8 - share % 8
+    parts = [w.reshape(share, ring, wide).transpose(1, 0, 2) for w in (w_query, w_key, w_value)]
     choices = jnp.concatenate([chosen[0].reshape(-1), counts[0].reshape(-1)]).astype(BF16)
-    notes = [
-        jnp.pad(row, (0, 3 * width - row.shape[0]))[None]
-        for row in (jnp.concatenate([gain_attn, gain_ffn]), choices)
-    ]
-    notes.append(jnp.zeros((extra - 2, 3 * width), BF16))
-    parcel = jnp.concatenate([jnp.concatenate([w_query, w_key, w_value], 1), *notes], 0)
-    parcel = jnp.stack(shift_gather(parcel, "fsdp"))
+    notes = jnp.stack(
+        [
+            jnp.pad(row, (0, 3 * wide - row.shape[0]))
+            for row in (jnp.concatenate([gain_attn, gain_ffn]), choices)
+        ]
+    )
+    notes = jnp.broadcast_to(jnp.pad(notes, ((0, extra - 2), (0, 0))), (ring, extra, 3 * wide))
+    parcel = jnp.concatenate([jnp.concatenate(parts, 2), notes], 1)
+    parcel = lax.all_to_all(parcel, "fsdp", 0, 0, tiled=True)
     picks = parcel[:, share + 1, : choices.shape[0]].astype(jnp.int32).reshape(ring, 2, -1)
     chosen_all, counts_all = picks[:, 0].reshape(-1), picks[:, 1].reshape(-1)
-    parcel = lax.all_gather(parcel, DP, axis=0, tiled=True)
     shards = jnp.concatenate([w_out, w_gate, w_up], 1)
     (near, near_down), steps = chain_gather((shards, w_down), "fsdp")
     (gathered,), token_steps = chain_gather((after(mine, steps[-2]),), "fsdp")
-    w_qkv = parcel[:, :share].reshape(width, 3 * width)
+    parcel = lax.all_gather(parcel, DP, axis=0, tiled=True)
+    w_qkv = parcel[:, :share].reshape(width, 3 * wide)
     gain_one = parcel[:, share, :share].reshape(1, width).astype(F32)
     gain_two = parcel[:, share, share : 2 * share].reshape(1, width).astype(F32)
     first = lax.all_gather(jnp.concatenate(near, 0), DP, axis=0, tiled=True)
@@ -651,20 +658,20 @@
     down_full = lax.all_gather(jnp.concatenate(near_down, 0), DP, axis=0, tiled=True)
 
     cosine, sine = rotary_tables(length)
-    place = lax.axis_index("fsdp").astype(jnp.int32).reshape(1)
-    qkv = project_qkv(place, gathered, gain_one, w_qkv, cosine, sine, heads, ring)
-    outs, stats, attended = [], [], []
-    for head in range(heads):
-        out, lse = attend_forward(chosen_all, counts_all, qkv, memory, head, heads, top)
-        outs.append(out)
-        stats.append(lse)
-        attended.append(exchange(out.reshape(ring, rows, HEAD_DIM), "fsdp"))
+    qkv = project_qkv(gathered, gain_one, w_qkv, cosine, sine, heads)
+    out, lse = attend_forward(chosen_all, counts_all, qkv, memory, heads, top)
+    attended = exchange(out.reshape(ring, rows, wide), "fsdp")
+
+    projections = after(jnp.concatenate([w_query, w_key, w_value], 1), qkv)
+    projections = jnp.concatenate(shift_gather(projections, "fsdp"), 0)
+    projections, attended = lax.optimization_barrier((projections, attended))
+    w_all = lax.all_gather(after(projections, down_full), DP, axis=0, tiled=True)
 
     mixed, grad_middle, gain_two_grad, grads, *others = feed_forward(
         mine, attended, cotangent[0], gain_two, first, down_full, span
     )
     grad_heads, grad_down = others[:heads], others[heads:]
-    grads = lax.psum_scatter(grads, DP, scatter_dimension=0, tiled=True)[0]
+    grads = lax.psum_scatter(after(grads, w_all), DP, scatter_dimension=0, tiled=True)[0]
     column = gain_one.reshape(width, 1)
     returned, weight_grads, gain_one_grad = [], [], 0.0
     for head in range(heads):
@@ -672,8 +679,8 @@
         if head:
             qkv = after(qkv, weight_grads[-1])
         grad, grad_w, gain_grad = attend_backward(
-            chosen_all, counts_all, place, qkv, memory, grad_out, outs[head], stats[head], cosine, sine, gathered,
-            column, w_qkv, head, heads, top, ring,
+            chosen_all, counts_all, qkv, memory, grad_out, out, lse, cosine, sine, gathered, column, w_qkv, head,
+            heads, top,
         )
         returned.append(exchange(grad.reshape(ring, rows, 3 * HEAD_DIM), "fsdp"))
         weight_grads.append(grad_w)
@@ -682,13 +689,13 @@
     gains = jnp.stack([gain_one_grad.reshape(span, -1), gain_two_grad.reshape(span, -1)], 1)
     gains = jnp.pad(gains.astype(BF16), ((0, 0), (0, extra - 2), (0, 3 * wide - gains.shape[2])))
     late = jnp.concatenate(weight_grads, 1).reshape(span, -1, 3 * wide)
-    late = jnp.concatenate([late, gains], 1)
+    late = after(jnp.concatenate([late, gains], 1), returned[0])
     late = late.reshape(span // 2, 2, late.shape[1], 3 * wide)
     core = lax.axis_index("core")
     taken = lax.ppermute(lax.dynamic_index_in_dim(late, 1 - core, 1, keepdims=False), "core", [(0, 1), (1, 0)])
     late = lax.dynamic_index_in_dim(late, core, 1, keepdims=False).astype(F32) + taken.astype(F32)
     late = jnp.sum(exchange(late.astype(BF16), "chip").astype(F32), 0).astype(BF16)
-    grads = after(grads, late)
+    grads = after(grads, (late, returned[-1]))
     gains = late[-extra : 2 - extra, : ring * share].reshape(2, ring, share).transpose(1, 0, 2)
     gains = jnp.pad(gains, ((0, 0), (0, extra - 2), (0, 3 * wide - share)))
     late = jnp.concatenate([late[:-extra].reshape(ring, share, 3 * wide), gains], 1)
@@ -706,7 +713,7 @@
         for part in range(3)
     ]
     gain_shares = jnp.sum(late[:, share : share + 2, :share], 0)
-    tokens_grad = finish_tokens(mine, gain_one, grad_middle, w_qkv, returned)
+    tokens_grad = finish_tokens(mine, gain_one, grad_middle, w_all, returned)
 
     strip = grads.shape[1]
     lanes = width // strip

time: 586 us -> 515 us (0.88)
  waiting for transfers between devices: 251 us -> 191 us
  starting transfers between devices: 79 us -> 58.8 us
  blocking collectives: 39.6 us -> 58.7 us
  Pallas kernels: 133 us -> 125 us
    all_to_all x7 -> x6, waiting for transfers between devices: 111 us -> 51 us  [exchange(): return lax.all_to_all(blocks, axis, 0, 0, tiled=True)]
    reduce_scatter x1, waiting for transfers between devices: 31.4 us -> 0.01 us  [body(): lax.psum_scatter(after(grads, w_all), DP, scatter_dimension=0, tiled=True)]
    reduce_scatter x1, waiting for transfers between devices: 0.01 us -> 27.8 us  [body(): lax.psum_scatter(pieces, 'fsdp', scatter_dimension=0, tiled=True)[0]]
    ppermute x9, waiting for transfers between devices: 83.2 us -> 67.6 us  [chain_gather(): falling = tuple((lax.ppermute(block, axis, down) for block in falling))]
    all_to_all x0 -> x1, blocking collectives: none -> 14.7 us  [body(): parcel = lax.all_to_all(parcel, 'fsdp', 0, 0, tiled=True)]
    ppermute x9, waiting for transfers between devices: 7.4 us -> 21.7 us  [chain_gather(): rising = tuple((lax.ppermute(block, axis, up) for block in rising))]
    all_to_all x7 -> x6, starting transfers between devices: 37.5 us -> 25.4 us  [exchange(): return lax.all_to_all(blocks, axis, 0, 0, tiled=True)]
    pallas_call x5 -> x4, Pallas kernels: 81 us -> 72.9 us  [the longest x2 44.2 us: attend_backward(): pl.pallas_call(functools.partial(backward_kernel, head, top), grid_spec=p...]
  transfers between devices with their start and end apart: 34 -> 34, of which waited for: 13 -> 16; matrix products, arithmetic and copies ran while one was open for 6% -> 7% of each run, Pallas kernels for 15% -> 25%
where the time goes in v7:
time: 515 us; the launch traced here: 506 us
  waiting for transfers between devices  191 us (37%)
  Pallas kernels  125 us (24%)
  starting transfers between devices  58.8 us (11%)
  blocking collectives  58.7 us (11%)
  local copies, waits for them, and re-layouts  28.9 us (6%)
  other arithmetic  28.9 us (6%)
  between operations  15.3 us (3%)
    ppermute x9, waiting for transfers between devices, chain_gather(): falling = tuple((lax.ppermute(block, axis, down) for block in falling))  67.6 us
    all_to_all x6, waiting for transfers between devices, exchange(): return lax.all_to_all(blocks, axis, 0, 0, tiled=True)  51 us
    pallas_call x2, Pallas kernels, attend_backward(): pl.pallas_call(functools.partial(backward_kernel, head, top), grid_spec=p...  44.2 us
    all_to_all x2, blocking collectives, exchange(): return lax.all_to_all(blocks, axis, 0, 0, tiled=True)  43.9 us
    pallas_call x1, Pallas kernels, feed_forward(): pl.pallas_call(functools.partial(ffn_kernel, span, merged, heads), grid=(...  43.8 us
    reduce_scatter x1, waiting for transfers between devices, body(): lax.psum_scatter(pieces, 'fsdp', scatter_dimension=0, tiled=True)[0]  27.8 us
    all_to_all x6, starting transfers between devices, exchange(): return lax.all_to_all(blocks, axis, 0, 0, tiled=True)  25.4 us
    ppermute x9, waiting for transfers between devices, chain_gather(): rising = tuple((lax.ppermute(block, axis, up) for block in rising))  21.7 us
  transfers between devices with their start and end apart: 34, of which 16 were waited for; matrix products, arithmetic and copies ran while one was open for 7% of the time, Pallas kernels for 25%

profile of v7, /device:TPU:0, one launch (start us, length us, event | category | flops | bytes accessed | tf_op | source)
XLA Modules:
  0.0 506.2 jit_solution(15977041262885729937)
XLA Ops:
  12.6 14.7 %all_to_all.45 = bf16[4,40,768]{2,1,0:T(8,128)(2,1)} all-to-all(bf16[4,40,768]{2,1,0:T(8,128)(2,1)S(1)} %copy.66), channel_id=1, replica_groups=mesh['chip'=4,'core'=2,'fsdp'=4] {'fsdp'}, dimensions={0} | all-to-all | bytes 491520 | tf_op jit(solution)/shard_map/all_to_all | solution.py:641
  31.0 4.6 collective-permute-start.1
  49.8 14.5 %collective-permute-done.7 = bf16[88,1024]{1,0:T(8,128)(2,1)} collective-permute-done((bf16[88,1024]{1,0:T(8,128)(2,1)S(1)}, bf16[88,1024]{1,0:T(8,128)(2,1)}, u32[]{:S(2)}, u32[]{:S(2)}) %collective-permute-start.7) | collective-permute-done | bytes 180256 | tf_op jit(solution)/shard_map/ppermute | solution.py:578
  69.0 10.1 %collective-permute-done.11 = bf16[88,1024]{1,0:T(8,128)(2,1)} collective-permute-done((bf16[88,1024]{1,0:T(8,128)(2,1)}, bf16[88,1024]{1,0:T(8,128)(2,1)}, u32[]{:S(2)}, u32[]{:S(2)}) %collective-permute-start.11) | collective-permute-done | bytes 180256 | tf_op jit(solution)/shard_map/ppermute | solution.py:578
  85.8 17.6 %collective-permute-done.12 = bf16[512,1024]{1,0:T(8,128)(2,1)S(1)} collective-permute-done((bf16[512,1024]{1,0:T(8,128)(2,1)S(1)}, bf16[512,1024]{1,0:T(8,128)(2,1)S(1)}, u32[]{:S(2)}, u32[]{:S(2)}) %collective-permute-start.12) | collective-permute-done | bytes 1048608 | tf_op jit(solution)/shard_map/ppermute | solution.py:577
  115.0 16.0 %collective-permute-done.16 = bf16[512,1024]{1,0:T(8,128)(2,1)} collective-permute-done((bf16[512,1024]{1,0:T(8,128)(2,1)S(1)}, bf16[512,1024]{1,0:T(8,128)(2,1)}, u32[]{:S(2)}, u32[]{:S(2)}) %collective-permute-start.16) | collective-permute-done | bytes 1048608 | tf_op jit(solution)/shard_map/ppermute | solution.py:578
  138.8 5.1 %all-to-all-start.1 = ((bf16[4,256,512]{2,1,0:T(8,128)(2,1)}), bf16[4,256,512]{2,1,0:T(8,128)(2,1)S(1)}, u32[]{:S(2)}, u32[]{:S(2)}) async-start(bf16[4,256,512]{2,1,0:T(8,128)(2,1)} %pad_maximum_fusion.6), calls=%async_computation.1 | async-start | bytes 2097152 | tf_op jit(solution)/shard_map/all_to_all | solution.py:613
  146.8 19.9 %collective-permute-done.17 = bf16[512,1024]{1,0:T(8,128)(2,1)} collective-permute-done((bf16[512,1024]{1,0:T(8,128)(2,1)}, bf16[512,1024]{1,0:T(8,128)(2,1)}, u32[]{:S(2)}, u32[]{:S(2)}) %collective-permute-start.17) | collective-permute-done | bytes 1048608 | tf_op jit(solution)/shard_map/ppermute | solution.py:578
  172.2 7.6 %project_qkv.1.q_ref.k_ref.v_ref = bf16[2048,768]{1,0:T(8,128)(2,1)} custom-call(bf16[2048,1024]{1,0:T(8,128)(2,1)} %pad_maximum_fusion.tok_ref, f32[1,1024]{1,0:T(1,128)S(1)} %reshape.185.gain_ref, bf16[1024,768]{1,0:T(8,128)(2,1)S(1)} %bitcast.67, f32[2048,128]{1,0:T(8,128)S(1)} %copy-done.1, f32[2048,128]{1,0:T(8,128)S(1)} %copy-done.2), custom_call_target="tpu_custom_call" | custom-call | flops 3221225472 | bytes 14680064 | tf_op jit(solution)/shard_map/project_qkv/pallas_call | solution.py:62
  179.8 21.1 %attend_forward.1 = (bf16[2048,256]{1,0:T(8,128)(2,1)}, f32[2048,2]{1,0:T(8,128)S(1)}) custom-call(s32[32]{0:T(128)S(1)} %reshape_squeeze.24.chosen_ref, s32[32]{0:T(128)S(1)} %reshape_squeeze.25.counts_ref, bf16[2048,768]{1,0:T(8,128)(2,1)} %project_qkv.1.q_ref.k_ref.v_ref, bf16[2048,768]{1,0:T(8,128)(2,1)} %project_qkv.1.q_ref.k_ref.v_ref, ...), custom_call_target="tpu_custom_call" | custom-call | flops 3221225472 | bytes 4194304 | tf_op jit(solution)/shard_map/attend_forward/pallas_call | solution.py:157
  200.8 4.4 all-to-all-start.2
  211.2 10.3 %collective-permute-done.18 = bf16[32,3072]{1,0:T(8,128)(2,1)S(1)} collective-permute-done((bf16[32,3072]{1,0:T(8,128)(2,1)S(1)}, bf16[32,3072]{1,0:T(8,128)(2,1)S(1)}, u32[]{:S(2)}, u32[]{:S(2)}) %collective-permute-start.18) | collective-permute-done | bytes 196640 | tf_op jit(solution)/shard_map/ppermute | solution.py:604
  221.5 7.8 %collective-permute-done.19 = bf16[32,3072]{1,0:T(8,128)(2,1)S(1)} collective-permute-done((bf16[32,3072]{1,0:T(8,128)(2,1)S(1)}, bf16[32,3072]{1,0:T(8,128)(2,1)S(1)}, u32[]{:S(2)}, u32[]{:S(2)}) %collective-permute-start.19) | collective-permute-done | bytes 196640 | tf_op jit(solution)/shard_map/ppermute | solution.py:604
  231.2 43.8 %feed_forward.1 = (bf16[512,1024]{1,0:T(8,128)(2,1)}, f32[512,1024]{1,0:T(8,128)}, f32[1,1024]{1,0:T(1,128)}, bf16[8,4736,256]{2,1,0:T(8,128)(2,1)}, bf16[4,512,...) custom-call(bf16[512,1024]{1,0:T(8,128)(2,1)} %bitcast.81, bf16[512,1024]{1,0:T(8,128)(2,1)} %bitcast.115, ...), custom_call_target="tpu_custom_call" | custom-call | flops 29796335616 | bytes 38797312 | tf_op jit(solution)/shard_map/feed_forward/pallas_call | solution.py:526
  278.2 19.4 %all_to_all.46 = bf16[4,512,128]{2,1,0:T(8,128)(2,1)} all-to-all(bf16[4,512,128]{2,1,0:T(8,128)(2,1)S(1)} %copy-done.17), channel_id=1, replica_groups=mesh['chip'=4,'core'=2,'fsdp'=4] {'fsdp'}, dimensions={0} | all-to-all | bytes 1048576 | tf_op jit(solution)/shard_map/all_to_all | solution.py:613
  303.7 22.4 %attend_backward.2 = (bf16[2048,384]{1,0:T(8,128)(2,1)}, bf16[1024,384]{1,0:T(8,128)(2,1)S(1)}, f32[1024,1]{1,0:T(8,128)S(1)}) custom-call(s32[32]{0:T(128)S(1)} %reshape_squeeze.24.chosen_ref, s32[32]{0:T(128)S(1)} %reshape_squeeze.25.counts_ref, bf16[2048,768]{1,0:T(8,128)(2,1)} %project_qkv.1.q_ref.k_ref.v_ref, ...), custom_call_target="tpu_custom_call" | custom-call | flops 4026531840 | bytes 4194304 | tf_op jit(solution)/shard_map/attend_backward/pallas_call | solution.py:283
  328.6 5.4 %all-to-all-start.4 = ((bf16[4,512,384]{2,1,0:T(8,128)(2,1)}), bf16[4,512,384]{2,1,0:T(8,128)(2,1)S(1)}, u32[]{:S(2)}, u32[]{:S(2)}) async-start(bf16[4,512,384]{2,1,0:T(8,128)(2,1)} %bitcast.100), calls=%async_computation.4 | async-start | bytes 3145728 | tf_op jit(solution)/shard_map/all_to_all | solution.py:613
  336.4 21.8 %attend_backward.3 = (bf16[2048,384]{1,0:T(8,128)(2,1)}, bf16[1024,384]{1,0:T(8,128)(2,1)S(1)}, f32[1024,1]{1,0:T(8,128)S(1)}) custom-call(s32[32]{0:T(128)S(1)} %reshape_squeeze.24.chosen_ref, s32[32]{0:T(128)S(1)} %reshape_squeeze.25.counts_ref, bf16[2048,768]{1,0:T(8,128)(2,1)} %project_qkv.1.q_ref.k_ref.v_ref, ...), custom_call_target="tpu_custom_call" | custom-call | flops 4026531840 | bytes 4194304 | tf_op jit(solution)/shard_map/attend_backward/pallas_call | solution.py:283
  360.0 10.0 %all-to-all-done.4.refs_0_ = bf16[4,512,384]{2,1,0:T(8,128)(2,1)S(1)} async-done(((bf16[4,512,384]{2,1,0:T(8,128)(2,1)}), bf16[4,512,384]{2,1,0:T(8,128)(2,1)S(1)}, u32[]{:S(2)}, u32[]{:S(2)}) %all-to-all-start.4) | async-done | bytes 1572896 | tf_op jit(solution)/shard_map/all_to_all | solution.py:613
  375.3 24.5 %all_to_all.47 = bf16[4,136,768]{2,1,0:T(8,128)(2,1)} all-to-all(bf16[4,136,768]{2,1,0:T(8,128)(2,1)S(1)} %fusion.2), channel_id=1, replica_groups=mesh['chip'=4,'core'=2,'fsdp'=4] {'chip'}, dimensions={0} | all-to-all | bytes 1671168 | tf_op jit(solution)/shard_map/all_to_all | solution.py:613
  404.8 35.0 %all-to-all-done.6.refs_1_ = bf16[4,512,384]{2,1,0:T(8,128)(2,1)S(1)} async-done(((bf16[4,512,384]{2,1,0:T(8,128)(2,1)}), bf16[4,512,384]{2,1,0:T(8,128)(2,1)S(1)}, u32[]{:S(2)}, u32[]{:S(2)}) %all-to-all-start.6) | async-done | bytes 1572896 | tf_op jit(solution)/shard_map/all_to_all | solution.py:613
  450.9 8.0 %finish_tokens.1 = bf16[512,1024]{1,0:T(8,128)(2,1)} custom-call(bf16[512,1024]{1,0:T(8,128)(2,1)S(1)} %bitcast.84, f32[1,1024]{1,0:T(1,128)S(1)} %reshape.185.gain_ref, f32[512,1024]{1,0:T(8,128)} %get-tuple-element.65.mid_ref, bf16[1024,3072]{1,0:T(8,128)(2,1)} %all-gather.11.cloned.1.call-done.w_ref, bf16[4,512,384]{2,1,0:T(8,128)(2,1)S(1)} %all-to-all-done.4.refs_0_, ...), custom_call_target="tpu_custom_call" | custom-call | flops 3221225472 | bytes 8388608 | tf_op jit(solution)/shard_map/finish_tokens/pallas_call | solution.py:359
  458.9 6.0 %all-to-all-done.8 = bf16[4,40,768]{2,1,0:T(8,128)(2,1)S(1)} async-done(((bf16[4,40,768]{2,1,0:T(8,128)(2,1)}), bf16[4,40,768]{2,1,0:T(8,128)(2,1)S(1)}, u32[]{:S(2)}, u32[]{:S(2)}) %all-to-all-start.8) | async-done | bytes 245792 | tf_op jit(solution)/shard_map/all_to_all | solution.py:613
  467.6 27.8 %reduce-scatter.5.cloned.1.call-done = bf16[1,1184,256]{2,1,0:T(8,128)(2,1)} async-done(((bf16[4,1184,256]{2,1,0:T(8,128)(2,1)}), bf16[1,1184,256]{2,1,0:T(8,128)(2,1)}) %reduce-scatter.5.cloned.1.call-update) | async-done | bytes 606224 | tf_op jit(solution)/shard_map/reduce_scatter | solution.py:729
  (192 shorter events, 113.1 us)
Async XLA Ops:
  7.2 136.9 %all-gather.5.cloned.1.call-start = ((), (), s32[]{:S(2)}) async-start(), calls=%async_computation.11 | async-start | bytes 2211840 | tf_op jit(solution)/shard_map/all_gather | solution.py:647
  27.4 202.9 %all-gather.9.cloned.1.call-start = ((), (), s32[]{:S(2)}) async-start(), calls=%async_computation.13 | async-start | bytes 6488064 | tf_op jit(solution)/shard_map/all_gather | solution.py:658
  27.5 17.6 %collective-permute-start = (bf16[32,6656]{1,0:T(8,128)(2,1)S(1)}, bf16[32,6656]{1,0:T(8,128)(2,1)S(1)}, u32[]{:S(2)}, u32[]{:S(2)}) collective-permute-start(bf16[32,6656]{1,0:T(8,128)(2,1)S(1)} %constant_dynamic-update-slice_fusion), channel_id=1, source_target_pairs={{0,1},{1,2},{2,3},{4,5},{5,6},{6,7},{8,9},{9,10},{10,11},{12,13},{... | collective-permute-start | bytes 1277960 | tf_op jit(solution)/shard_map/ppermute | solution.py:577
  45.1 19.2 %collective-permute-start.4 = (bf16[32,6656]{1,0:T(8,128)(2,1)S(1)}, bf16[32,6656]{1,0:T(8,128)(2,1)S(1)}, u32[]{:S(2)}, u32[]{:S(2)}) collective-permute-start(bf16[32,6656]{1,0:T(8,128)(2,1)S(1)} %collective-permute-done), channel_id=1, source_target_pairs={{1,2},{2,3},{5,6},{6,7},{9,10},{10,11},{13,14},{14,15},{17,18},{18... | collective-permute-start | bytes 1277960 | tf_op jit(solution)/shard_map/ppermute | solution.py:577
  45.8 18.5 %collective-permute-start.6 = (bf16[32,6656]{1,0:T(8,128)(2,1)S(1)}, bf16[32,6656]{1,0:T(8,128)(2,1)S(1)}, u32[]{:S(2)}, u32[]{:S(2)}) collective-permute-start(bf16[32,6656]{1,0:T(8,128)(2,1)S(1)} %collective-permute-done.2), channel_id=1, source_target_pairs={{1,0},{2,1},{5,4},{6,5},{9,8},{10,9},{13,12},{14,13},{17,16},{18,1... | collective-permute-start | bytes 1277960 | tf_op jit(solution)/shard_map/ppermute | solution.py:578
  48.5 15.8 %collective-permute-start.7 = (bf16[88,1024]{1,0:T(8,128)(2,1)S(1)}, bf16[88,1024]{1,0:T(8,128)(2,1)}, u32[]{:S(2)}, u32[]{:S(2)}) collective-permute-start(bf16[88,1024]{1,0:T(8,128)(2,1)S(1)} %collective-permute-done.3), channel_id=1, source_target_pairs={{1,0},{2,1},{5,4},{6,5},{9,8},{10,9},{13,12},{14,13},{17,16},{18,1... | collective-permute-start | bytes 540680 | tf_op jit(solution)/shard_map/ppermute | solution.py:578
  81.2 150.0 %all-gather.7.cloned.1.call-start = ((), (), s32[]{:S(2)}) async-start(), calls=%async_computation.12 | async-start | bytes 15335424 | tf_op jit(solution)/shard_map/all_gather | solution.py:651
  83.1 20.3 %collective-permute-start.12 = (bf16[512,1024]{1,0:T(8,128)(2,1)S(1)}, bf16[512,1024]{1,0:T(8,128)(2,1)S(1)}, u32[]{:S(2)}, u32[]{:S(2)}) collective-permute-start(bf16[512,1024]{1,0:T(8,128)(2,1)S(1)} %bitcast.82), channel_id=1, source_target_pairs={{0,1},{1,2},{2,3},{4,5},{5,6},{6,7},{8,9},{9,10},{10,11},{12,13},{... | collective-permute-start | bytes 3145736 | tf_op jit(solution)/shard_map/ppermute | solution.py:577
  84.5 23.3 %collective-permute-start.15 = (bf16[512,1024]{1,0:T(8,128)(2,1)S(1)}, bf16[512,1024]{1,0:T(8,128)(2,1)S(1)}, u32[]{:S(2)}, u32[]{:S(2)}) collective-permute-start(bf16[512,1024]{1,0:T(8,128)(2,1)S(1)} %bitcast.83), channel_id=1, source_target_pairs={{1,0},{2,1},{3,2},{5,4},{6,5},{7,6},{9,8},{10,9},{11,10},{13,12},{... | collective-permute-start | bytes 3145736 | tf_op jit(solution)/shard_map/ppermute | solution.py:578
  107.9 23.1 %collective-permute-start.16 = (bf16[512,1024]{1,0:T(8,128)(2,1)S(1)}, bf16[512,1024]{1,0:T(8,128)(2,1)}, u32[]{:S(2)}, u32[]{:S(2)}) collective-permute-start(bf16[512,1024]{1,0:T(8,128)(2,1)S(1)} %collective-permute-done.15), channel_id=1, source_target_pairs={{1,0},{2,1},{5,4},{6,5},{9,8},{10,9},{13,12},{14,13},{17,16},{18,1... | collective-permute-start | bytes 3145736 | tf_op jit(solution)/shard_map/ppermute | solution.py:578
  113.3 33.4 %collective-permute-start.14 = (bf16[512,1024]{1,0:T(8,128)(2,1)}, bf16[512,1024]{1,0:T(8,128)(2,1)}, u32[]{:S(2)}, u32[]{:S(2)}) collective-permute-start(bf16[512,1024]{1,0:T(8,128)(2,1)} %collective-permute-done.13), channel_id=1, source_target_pairs={{2,3},{6,7},{10,11},{14,15},{18,19},{22,23},{26,27},{30,31}} | collective-permute-start | bytes 3145736 | tf_op jit(solution)/shard_map/ppermute | solution.py:577
  131.0 35.7 %collective-permute-start.17 = (bf16[512,1024]{1,0:T(8,128)(2,1)}, bf16[512,1024]{1,0:T(8,128)(2,1)}, u32[]{:S(2)}, u32[]{:S(2)}) collective-permute-start(bf16[512,1024]{1,0:T(8,128)(2,1)} %collective-permute-done.16), channel_id=1, source_target_pairs={{1,0},{5,4},{9,8},{13,12},{17,16},{21,20},{25,24},{29,28}} | collective-permute-start | bytes 3145736 | tf_op jit(solution)/shard_map/ppermute | solution.py:578
  138.8 41.0 %all-to-all-start.1 = ((bf16[4,256,512]{2,1,0:T(8,128)(2,1)}), bf16[4,256,512]{2,1,0:T(8,128)(2,1)S(1)}, u32[]{:S(2)}, u32[]{:S(2)}) async-start(bf16[4,256,512]{2,1,0:T(8,128)(2,1)} %pad_maximum_fusion.6), calls=%async_computation.1 | async-start | bytes 2097152 | tf_op jit(solution)/shard_map/all_to_all | solution.py:613
  200.8 29.4 %all-to-all-start.2 = ((bf16[4,512,256]{2,1,0:T(8,128)(2,1)}), bf16[4,512,256]{2,1,0:T(8,128)(2,1)}, u32[]{:S(2)}, u32[]{:S(2)}) async-start(bf16[4,512,256]{2,1,0:T(8,128)(2,1)} %bitcast.9), calls=%async_computation.2 | async-start | bytes 2097152 | tf_op jit(solution)/shard_map/all_to_all | solution.py:613
  205.3 71.9 %all-gather.11.cloned.1.call-start = ((), (), s32[]{:S(2)}) async-start(), calls=%async_computation.14 | async-start | bytes 7077888 | tf_op jit(solution)/shard_map/all_gather | solution.py:668
  205.4 16.1 %collective-permute-start.18 = (bf16[32,3072]{1,0:T(8,128)(2,1)S(1)}, bf16[32,3072]{1,0:T(8,128)(2,1)S(1)}, u32[]{:S(2)}, u32[]{:S(2)}) collective-permute-start(bf16[32,3072]{1,0:T(8,128)(2,1)S(1)} %pad_maximum_fusion.10), channel_id=1, source_target_pairs={{0,1},{1,2},{2,3},{3,0},{4,5},{5,6},{6,7},{7,4},{8,9},{9,10},{10,1... | collective-permute-start | bytes 589832 | tf_op jit(solution)/shard_map/ppermute | solution.py:604
  207.3 21.9 %collective-permute-start.19 = (bf16[32,3072]{1,0:T(8,128)(2,1)S(1)}, bf16[32,3072]{1,0:T(8,128)(2,1)S(1)}, u32[]{:S(2)}, u32[]{:S(2)}) collective-permute-start(bf16[32,3072]{1,0:T(8,128)(2,1)S(1)} %pad_maximum_fusion.10), channel_id=1, source_target_pairs={{0,2},{1,3},{2,0},{3,1},{4,6},{5,7},{6,4},{7,5},{8,10},{9,11},{10,... | collective-permute-start | bytes 589832 | tf_op jit(solution)/shard_map/ppermute | solution.py:604
  209.7 19.5 %collective-permute-start.20 = (bf16[32,3072]{1,0:T(8,128)(2,1)S(1)}, bf16[32,3072]{1,0:T(8,128)(2,1)S(1)}, u32[]{:S(2)}, u32[]{:S(2)}) collective-permute-start(bf16[32,3072]{1,0:T(8,128)(2,1)S(1)} %pad_maximum_fusion.10), channel_id=1, source_target_pairs={{0,3},{1,0},{2,1},{3,2},{4,7},{5,4},{6,5},{7,6},{8,11},{9,8},{10,9... | collective-permute-start | bytes 589832 | tf_op jit(solution)/shard_map/ppermute | solution.py:604
  230.3 209.4 %reduce-scatter.3.cloned.1.call-start = ((), (), s32[]{:S(2)}) async-start(), calls=%async_computation.15 | async-start | bytes 21823488 | tf_op jit(solution)/shard_map/reduce_scatter | solution.py:674
  297.6 30.2 %all-to-all-start.5 = ((bf16[4,512,128]{2,1,0:T(8,128)(2,1)}), bf16[4,512,128]{2,1,0:T(8,128)(2,1)S(1)}, u32[]{:S(2)}, u32[]{:S(2)}) async-start(bf16[4,512,128]{2,1,0:T(8,128)(2,1)} %get-tuple-element.73), calls=%async_computation.5 | async-start | bytes 1048576 | tf_op jit(solution)/shard_map/all_to_all | solution.py:613
  328.6 41.3 %all-to-all-start.4 = ((bf16[4,512,384]{2,1,0:T(8,128)(2,1)}), bf16[4,512,384]{2,1,0:T(8,128)(2,1)S(1)}, u32[]{:S(2)}, u32[]{:S(2)}) async-start(bf16[4,512,384]{2,1,0:T(8,128)(2,1)} %bitcast.100), calls=%async_computation.4 | async-start | bytes 3145728 | tf_op jit(solution)/shard_map/all_to_all | solution.py:613
  399.9 39.9 %all-to-all-start.6 = ((bf16[4,512,384]{2,1,0:T(8,128)(2,1)}), bf16[4,512,384]{2,1,0:T(8,128)(2,1)S(1)}, u32[]{:S(2)}, u32[]{:S(2)}) async-start(bf16[4,512,384]{2,1,0:T(8,128)(2,1)} %bitcast.99), calls=%async_computation.6 | async-start | bytes 3145728 | tf_op jit(solution)/shard_map/all_to_all | solution.py:613
  403.4 92.0 %reduce-scatter.5.cloned.1.call-start = ((), (), s32[]{:S(2)}) async-start(), calls=%async_computation.16 | async-start | bytes 3031040 | tf_op jit(solution)/shard_map/reduce_scatter | solution.py:729
  446.3 18.7 %all-to-all-start.8 = ((bf16[4,40,768]{2,1,0:T(8,128)(2,1)}), bf16[4,40,768]{2,1,0:T(8,128)(2,1)S(1)}, u32[]{:S(2)}, u32[]{:S(2)}) async-start(bf16[4,40,768]{2,1,0:T(8,128)(2,1)} %fusion.6), calls=%async_computation.8 | async-start | bytes 491520 | tf_op jit(solution)/shard_map/all_to_all | solution.py:613
  (36 other events, 407.3 us)
Sparse Core Ops, SparseCore 0:
  27.5 26.4 all-gather.4
  81.3 41.5 all-gather.8
  124.8 76.5 all-gather.6
  230.4 46.7 all-gather.10
  280.7 137.2 reduce-scatter.2
  444.4 50.9 reduce-scatter.4

commit v8 on v5

--- a/solution.py
+++ b/solution.py
@@ -549,7 +549,7 @@
     return results, steps
 
 
-def chain_scatter(partial, axis):
+def chain_scatter(partial, axis, beside):
     size = lax.axis_size(axis)
     place = lax.axis_index(axis)
     rows = partial.shape[0] // size
@@ -558,17 +558,27 @@
         return lax.dynamic_slice_in_dim(partial, jnp.clip(index, 0, size - 1) * rows, rows, 0).astype(F32)
 
     rising = falling = None
-    steps = []
     for step in range(size - 1):
         up, down = block(size - 1 - step + place), block(step - size + 1 + place)
+        extra = None
         if step:
             up, down = up + rising.astype(F32), down + falling.astype(F32)
-        up, down = lax.optimization_barrier((up.astype(BF16), down.astype(BF16)))
+            extra = beside[step - 1]() if step <= len(beside) else None
+        up, down, _ = lax.optimization_barrier((up.astype(BF16), down.astype(BF16), extra))
         rising = lax.ppermute(up, axis, [(i, i + 1) for i in range(step + 1)])
         falling = lax.ppermute(down, axis, [(i, i - 1) for i in range(size - 1 - step, size)])
         rising, falling = lax.optimization_barrier((rising, falling))
-        steps.append((rising, falling))
-    return block(place), steps
+    return block(place) + rising.astype(F32) + falling.astype(F32)
+
+
+def direct_exchange(blocks, axis):
+    size = lax.axis_size(axis)
+    place = lax.axis_index(axis)
+    taken = [lax.dynamic_index_in_dim(blocks, place, 0, keepdims=False)]
+    for far in range(1, size):
+        give = lax.dynamic_index_in_dim(blocks, (place + far) % size, 0, keepdims=False)
+        taken.append(lax.ppermute(give, axis, [(i, (i + far) % size) for i in range(size)]))
+    return taken
 
 
 def body(
@@ -631,28 +641,36 @@
         chosen_all, counts_all, qkv, memory, grad_heads, attended_heads, lse, cosine, sine, gathered, gain_one,
         w_qkv, heads, top,
     )
-    own_term, steps = chain_scatter(partial, "fsdp")
-    grads = after(grads, steps[-1])
-
     gains = jnp.concatenate([gain_one_grad, gain_two_grad], 0).reshape(2, span, -1).transpose(1, 0, 2)
     gains = jnp.pad(gains.astype(BF16), ((0, 0), (0, extra - 2), (0, 3 * wide - gains.shape[2])))
     late = jnp.concatenate([grad_w_qkv.reshape(span, -1, 3 * wide), gains], 1)
     late = late.reshape(span // 2, 2, late.shape[1], 3 * wide)
     core = lax.axis_index("core")
-    taken = lax.ppermute(lax.dynamic_index_in_dim(late, 1 - core, 1, keepdims=False), "core", [(0, 1), (1, 0)])
-    late = lax.dynamic_index_in_dim(late, core, 1, keepdims=False).astype(F32) + taken.astype(F32)
-    late = after(late.astype(BF16), steps[0])
-    late = jnp.sum(lax.all_to_all(late, "chip", 0, 0, tiled=True).astype(F32), 0).astype(BF16)
+    sums = []
+
+    def between_cores():
+        give = lax.dynamic_index_in_dim(late, 1 - core, 1, keepdims=False)
+        keep = lax.dynamic_index_in_dim(late, core, 1, keepdims=False)
+        taken = lax.ppermute(give, "core", [(0, 1), (1, 0)])
+        sums.append((keep.astype(F32) + taken.astype(F32)).astype(BF16))
+        return sums[-1]
+
+    def between_chips():
+        sums.append(sum(piece.astype(F32) for piece in direct_exchange(sums[-1], "chip")).astype(BF16))
+        return sums[-1]
+
+    grad_normed = chain_scatter(partial, "fsdp", [between_cores, between_chips])
+    late = sums[-1]
+    own = mine.astype(F32)
+    factor = lax.rsqrt(jnp.mean(own * own, -1, keepdims=True) + EPSILON)
+    scaled = grad_normed * gain_one
+    inner = jnp.mean(scaled * own, -1, keepdims=True)
+    tokens_grad = (grad_middle + factor * scaled - own * (factor * factor * factor * inner)).astype(BF16)
+
     gains = late[-extra : 2 - extra, : ring * share].reshape(2, ring, share).transpose(1, 0, 2)
     gains = jnp.pad(gains, ((0, 0), (0, extra - 2), (0, 3 * wide - share)))
     late = jnp.concatenate([late[:-extra].reshape(ring, share, 3 * wide), gains], 1)
-    late = lax.all_to_all(late, "fsdp", 0, 0, tiled=True).astype(F32)
-    projections = [
-        late[:, :share, part * wide : (part + 1) * wide].transpose(1, 0, 2).reshape(share, width)
-        for part in range(3)
-    ]
-    gain_shares = jnp.sum(late[:, share : share + 2, :share], 0)
-
+    grads = after(grads, grad_normed)
     strip = grads.shape[1]
     lanes = width // strip
     tall = w_down.shape[0]
@@ -664,15 +682,18 @@
         grads = grads[ring * tall * lanes :]
     grads = grads.reshape(-1, ring, share, strip).transpose(1, 0, 2, 3)
     pieces = jnp.concatenate([down.reshape(ring, -1, strip), grads.reshape(ring, -1, strip)], 1)
-    rising, falling = steps[-1]
-    grad_normed = own_term + rising.astype(F32) + falling.astype(F32)
-    own = mine.astype(F32)
-    factor = lax.rsqrt(jnp.mean(own * own, -1, keepdims=True) + EPSILON)
-    scaled = grad_normed * gain_one
-    inner = jnp.mean(scaled * own, -1, keepdims=True)
-    tokens_grad = (grad_middle + factor * scaled - own * (factor * factor * factor * inner)).astype(BF16)
-
-    pieces = lax.psum_scatter(pieces, "fsdp", scatter_dimension=0, tiled=True)[0].astype(F32)
+    pieces = sum(piece.astype(F32) for piece in direct_exchange(pieces, "fsdp"))
+    late = direct_exchange(late, "fsdp")
+    place = lax.axis_index("fsdp")
+    gain_shares = sum(piece.astype(F32) for piece in late)[share : share + 2, :share]
+    in_order = [
+        lax.select_n(place if ring > 2 else place > 0, *[late[(here - source) % ring] for here in range(ring)])
+        for source in range(ring)
+    ]
+    projections = [
+        jnp.concatenate([piece[:share, part * wide : (part + 1) * wide] for piece in in_order], 1).astype(F32)
+        for part in range(3)
+    ]
     down_share = pieces[: lanes * tall].reshape(lanes, tall, strip).transpose(1, 0, 2).reshape(tall, width)
     others = pieces[lanes * tall :].reshape(-1, share, strip).transpose(1, 0, 2).reshape(share, -1)
     return (

time: 477 us -> 502 us (1.052)
  the two profiles are of different devices: /device:TPU:0 before, /device:TPU:12 now
where the time goes in v8:
time: 502 us; the launch traced here: 494 us
  waiting for transfers between devices  201 us (40%)
  Pallas kernels  112 us (22%)
  starting transfers between devices  96.3 us (19%)
  other arithmetic  35.4 us (7%)
  local copies, waits for them, and re-layouts  23 us (5%)
  between operations  14.9 us (3%)
  blocking collectives  12 us (2%)
    ppermute x9, waiting for transfers between devices, direct_exchange(): lax.ppermute(give, axis, [(i, (i + far) % size) for i in range(size)])  90.9 us
    ppermute x9, waiting for transfers between devices, chain_gather(): falling = tuple((lax.ppermute(block, axis, down) for block in falling))  55.3 us
    pallas_call x1, Pallas kernels, feed_forward(): pl.pallas_call(functools.partial(ffn_kernel, span, merged), grid=(steps,)...  43.9 us
    pallas_call x1, Pallas kernels, attend_backward(): pl.pallas_call(functools.partial(backward_kernel, heads, top), grid_spec=...  39.1 us
    ppermute x9, starting transfers between devices, chain_gather(): falling = tuple((lax.ppermute(block, axis, down) for block in falling))  29.4 us
    pallas_call x1, Pallas kernels, attend_forward(): pl.pallas_call(functools.partial(forward_kernel, heads, top), grid_spec=p...  21.4 us
    ppermute x9, starting transfers between devices, chain_gather(): rising = tuple((lax.ppermute(block, axis, up) for block in rising))  21.2 us
    ppermute x3, waiting for transfers between devices, chain_scatter(): rising = lax.ppermute(up, axis, [(i, i + 1) for i in range(step + 1)])  19.5 us
  transfers between devices with their start and end apart: 41, of which 19 were waited for; matrix products, arithmetic and copies ran while one was open for 9% of the time, Pallas kernels for 14%

profile of v8, /device:TPU:12, one launch (start us, length us, event | category | flops | bytes accessed | tf_op | source)
XLA Modules:
  0.0 494.0 jit_solution(13917458001104576642)
XLA Ops:
  12.6 12.0 %all_to_all.48 = bf16[4,40,768]{2,1,0:T(8,128)(2,1)} all-to-all(bf16[4,40,768]{2,1,0:T(8,128)(2,1)S(1)} %copy.64), channel_id=1, replica_groups=mesh['chip'=4,'core'=2,'fsdp'=4] {'fsdp'}, dimensions={0} | all-to-all | bytes 491520 | tf_op jit(solution)/shard_map/all_to_all | solution.py:609
  36.5 6.7 %collective-permute-done.1 = bf16[88,1024]{1,0:T(8,128)(2,1)S(1)} collective-permute-done((bf16[88,1024]{1,0:T(8,128)(2,1)S(1)}, bf16[88,1024]{1,0:T(8,128)(2,1)S(1)}, u32[]{:S(2)}, u32[]{:S(2)}) %collective-permute-start.1) | collective-permute-done | bytes 180256 | tf_op jit(solution)/shard_map/ppermute | solution.py:530
  48.0 4.6 collective-permute-start.5
  66.7 6.8 %collective-permute-done.17 = bf16[88,1024]{1,0:T(8,128)(2,1)} collective-permute-done((bf16[88,1024]{1,0:T(8,128)(2,1)}, bf16[88,1024]{1,0:T(8,128)(2,1)}, u32[]{:S(2)}, u32[]{:S(2)}) %collective-permute-start.17) | collective-permute-done | bytes 180256 | tf_op jit(solution)/shard_map/ppermute | solution.py:531
  77.4 4.5 collective-permute-start.11
  83.8 17.0 %collective-permute-done.11 = bf16[512,1024]{1,0:T(8,128)(2,1)S(1)} collective-permute-done((bf16[512,1024]{1,0:T(8,128)(2,1)S(1)}, bf16[512,1024]{1,0:T(8,128)(2,1)S(1)}, u32[]{:S(2)}, u32[]{:S(2)}) %collective-permute-start.11) | collective-permute-done | bytes 1048608 | tf_op jit(solution)/shard_map/ppermute | solution.py:531
  111.7 12.1 %collective-permute-done.12 = bf16[512,1024]{1,0:T(8,128)(2,1)} collective-permute-done((bf16[512,1024]{1,0:T(8,128)(2,1)S(1)}, bf16[512,1024]{1,0:T(8,128)(2,1)}, u32[]{:S(2)}, u32[]{:S(2)}) %collective-permute-start.12) | collective-permute-done | bytes 1048608 | tf_op jit(solution)/shard_map/ppermute | solution.py:531
  123.8 5.5 %collective-permute-start.13 = (bf16[512,1024]{1,0:T(8,128)(2,1)}, bf16[512,1024]{1,0:T(8,128)(2,1)}, u32[]{:S(2)}, u32[]{:S(2)}) collective-permute-start(bf16[512,1024]{1,0:T(8,128)(2,1)} %collective-permute-done.12), channel_id=1, source_target_pairs={{1,0},{5,4},{9,8},{13,12},{17,16},{21,20},{25,24},{29,28}} | collective-permute-start | bytes 3145736 | tf_op jit(solution)/shard_map/ppermute | solution.py:531
  137.0 4.4 all-to-all-start.1
  144.2 15.2 %collective-permute-done.13 = bf16[512,1024]{1,0:T(8,128)(2,1)} collective-permute-done((bf16[512,1024]{1,0:T(8,128)(2,1)}, bf16[512,1024]{1,0:T(8,128)(2,1)}, u32[]{:S(2)}, u32[]{:S(2)}) %collective-permute-start.13) | collective-permute-done | bytes 1048608 | tf_op jit(solution)/shard_map/ppermute | solution.py:531
  163.9 7.4 %project_qkv.1.q_ref.k_ref.v_ref = bf16[2048,768]{1,0:T(8,128)(2,1)} custom-call(bf16[2048,1024]{1,0:T(8,128)(2,1)} %pad_maximum_fusion.tok_ref, f32[1,1024]{1,0:T(1,128)S(1)} %reshape.167.gain_ref, bf16[1024,768]{1,0:T(8,128)(2,1)S(1)} %bitcast.113, f32[2048,128]{1,0:T(8,128)S(1)} %get-tuple-element.144.cos_ref, f32[2048,128]{1,0:T(8,128)S(1)} %copy-done.1), custom_call_target="tpu_custom_call" | custom-call | flops 3221225472 | bytes 14680064 | tf_op jit(solution)/shard_map/project_qkv/pallas_call | solution.py:62
  171.2 21.4 %attend_forward.1 = (bf16[2048,256]{1,0:T(8,128)(2,1)}, f32[2048,2]{1,0:T(8,128)S(1)}) custom-call(s32[32]{0:T(128)S(1)} %reshape_squeeze.24.chosen_ref, s32[32]{0:T(128)S(1)} %reshape_squeeze.25.counts_ref, bf16[2048,768]{1,0:T(8,128)(2,1)} %project_qkv.1.q_ref.k_ref.v_ref, bf16[2048,768]{1,0:T(8,128)(2,1)} %project_qkv.1.q_ref.k_ref.v_ref, ...), custom_call_target="tpu_custom_call" | custom-call | flops 3221225472 | bytes 4194304 | tf_op jit(solution)/shard_map/attend_forward/pallas_call | solution.py:157
  193.7 7.2 %all-to-all-start.2 = ((bf16[4,512,256]{2,1,0:T(8,128)(2,1)}), bf16[4,512,256]{2,1,0:T(8,128)(2,1)S(1)}, u32[]{:S(2)}, u32[]{:S(2)}) async-start(bf16[4,512,256]{2,1,0:T(8,128)(2,1)} %bitcast.8), calls=%async_computation.2 | async-start | bytes 2097152 | tf_op jit(solution)/shard_map/all_to_all | solution.py:631
  201.5 12.0 %all-to-all-done.2 = bf16[4,512,256]{2,1,0:T(8,128)(2,1)S(1)} async-done(((bf16[4,512,256]{2,1,0:T(8,128)(2,1)}), bf16[4,512,256]{2,1,0:T(8,128)(2,1)S(1)}, u32[]{:S(2)}, u32[]{:S(2)}) %all-to-all-start.2) | async-done | bytes 1048608 | tf_op jit(solution)/shard_map/all_to_all | solution.py:631
  214.7 43.9 %feed_forward.1 = (bf16[512,1024]{1,0:T(8,128)(2,1)}, f32[512,1024]{1,0:T(8,128)}, bf16[512,1024]{1,0:T(8,128)(2,1)}, f32[1,1024]{1,0:T(1,128)}, bf16[8,4736,256]{2,1,0:T(8,128)(2,1)}) custom-call(bf16[512,1024]{1,0:T(8,128)(2,1)} %bitcast.118, bf16[512,1024]{1,0:T(8,128)(2,1)} %bitcast.135, bf16[512,1024]{1,0:T(8,128)(2,1)} %bitcast.147, ...), custom_call_target="tpu_custom_call" | custom-call | flops 29796335616 | bytes 38797312 | tf_op jit(solution)/shard_map/feed_forward/pallas_call | solution.py:480
  260.8 7.0 %all-to-all-start.3 = ((bf16[512,4,256]{2,0,1:T(8,128)(2,1)}), bf16[512,4,256]{2,0,1:T(8,128)(2,1)S(1)}, u32[]{:S(2)}, u32[]{:S(2)}) async-start(bf16[512,4,256]{2,0,1:T(8,128)(2,1)} %bitcast.109), calls=%async_computation.3 | async-start | bytes 2097152 | tf_op jit(solution)/shard_map/all_to_all | solution.py:637
  267.9 12.6 %all-to-all-done.3 = bf16[512,4,256]{2,0,1:T(8,128)(2,1)S(1)} async-done(((bf16[512,4,256]{2,0,1:T(8,128)(2,1)}), bf16[512,4,256]{2,0,1:T(8,128)(2,1)S(1)}, u32[]{:S(2)}, u32[]{:S(2)}) %all-to-all-start.3) | async-done | bytes 1048608 | tf_op jit(solution)/shard_map/all_to_all | solution.py:637
  281.9 39.1 %attend_backward.1 = (bf16[2048,1024]{1,0:T(8,128)(2,1)}, bf16[1024,768]{1,0:T(8,128)(2,1)}, f32[1,1024]{1,0:T(1,128)S(1)}) custom-call(s32[32]{0:T(128)S(1)} %reshape_squeeze.24.chosen_ref, s32[32]{0:T(128)S(1)} %reshape_squeeze.25.counts_ref, bf16[2048,768]{1,0:T(8,128)(2,1)} %project_qkv.1.q_ref.k_ref.v_ref, ...), custom_call_target="tpu_custom_call" | custom-call | flops 8053063680 | bytes 8388608 | tf_op jit(solution)/shard_map/attend_backward/pallas_call | solution.py:295
  333.1 9.9 %collective-permute-done.23 = bf16[136,768]{1,0:T(8,128)(2,1)S(1)} collective-permute-done((bf16[136,768]{1,0:T(8,128)(2,1)S(1)}, bf16[136,768]{1,0:T(8,128)(2,1)S(1)}, u32[]{:S(2)}, u32[]{:S(2)}) %collective-permute-start.23) | collective-permute-done | bytes 208928 | tf_op jit(solution)/shard_map/ppermute | solution.py:580
  343.0 7.9 %collective-permute-done.25 = bf16[136,768]{1,0:T(8,128)(2,1)S(1)} collective-permute-done((bf16[136,768]{1,0:T(8,128)(2,1)S(1)}, bf16[136,768]{1,0:T(8,128)(2,1)S(1)}, u32[]{:S(2)}, u32[]{:S(2)}) %collective-permute-start.25) | collective-permute-done | bytes 208928 | tf_op jit(solution)/shard_map/ppermute | solution.py:580
  368.9 21.3 %collective-permute-done.29 = bf16[40,768]{1,0:T(8,128)(2,1)S(1)} collective-permute-done((bf16[40,768]{1,0:T(8,128)(2,1)S(1)}, bf16[40,768]{1,0:T(8,128)(2,1)S(1)}, u32[]{:S(2)}, u32[]{:S(2)}) %collective-permute-start.29) | collective-permute-done | bytes 61472 | tf_op jit(solution)/shard_map/ppermute | solution.py:580
  406.2 17.1 %collective-permute-done.26 = bf16[512,1024]{1,0:T(8,128)(2,1)S(1)} collective-permute-done((bf16[512,1024]{1,0:T(8,128)(2,1)S(1)}, bf16[512,1024]{1,0:T(8,128)(2,1)S(1)}, u32[]{:S(2)}, u32[]{:S(2)}) %collective-permute-start.26) | collective-permute-done | bytes 1048608 | tf_op jit(solution)/shard_map/ppermute | solution.py:568
  436.2 34.4 %collective-permute-done.31 = bf16[1184,256]{1,0:T(8,128)(2,1)S(1)} collective-permute-done((bf16[1184,256]{1,0:T(8,128)(2,1)S(1)}, bf16[1184,256]{1,0:T(8,128)(2,1)S(1)}, u32[]{:S(2)}, u32[]{:S(2)}) %collective-permute-start.31) | collective-permute-done | bytes 606240 | tf_op jit(solution)/shard_map/ppermute | solution.py:580
  470.6 10.2 %collective-permute-done.32 = bf16[1184,256]{1,0:T(8,128)(2,1)S(1)} collective-permute-done((bf16[1184,256]{1,0:T(8,128)(2,1)S(1)}, bf16[1184,256]{1,0:T(8,128)(2,1)S(1)}, u32[]{:S(2)}, u32[]{:S(2)}) %collective-permute-start.32) | collective-permute-done | bytes 606240 | tf_op jit(solution)/shard_map/ppermute | solution.py:580
  (190 shorter events, 139.0 us)
Async XLA Ops:
  7.2 134.3 %all-gather.4.cloned.1.call-start = ((), (), s32[]{:S(2)}) async-start(), calls=%async_computation.5 | async-start | bytes 2211840 | tf_op jit(solution)/shard_map/all_gather | solution.py:615
  24.6 190.1 %all-gather.8.cloned.1.call-start = ((), (), s32[]{:S(2)}) async-start(), calls=%async_computation.7 | async-start | bytes 6488064 | tf_op jit(solution)/shard_map/all_gather | solution.py:626
  75.5 139.2 %all-gather.6.cloned.1.call-start = ((), (), s32[]{:S(2)}) async-start(), calls=%async_computation.6 | async-start | bytes 15335424 | tf_op jit(solution)/shard_map/all_gather | solution.py:619
  77.4 23.4 %collective-permute-start.11 = (bf16[512,1024]{1,0:T(8,128)(2,1)S(1)}, bf16[512,1024]{1,0:T(8,128)(2,1)S(1)}, u32[]{:S(2)}, u32[]{:S(2)}) collective-permute-start(bf16[512,1024]{1,0:T(8,128)(2,1)S(1)} %bitcast.119), channel_id=1, source_target_pairs={{1,0},{2,1},{3,2},{5,4},{6,5},{7,6},{9,8},{10,9},{11,10},{13,12},{... | collective-permute-start | bytes 3145736 | tf_op jit(solution)/shard_map/ppermute | solution.py:531
  81.8 23.3 %collective-permute-start.8 = (bf16[512,1024]{1,0:T(8,128)(2,1)S(1)}, bf16[512,1024]{1,0:T(8,128)(2,1)}, u32[]{:S(2)}, u32[]{:S(2)}) collective-permute-start(bf16[512,1024]{1,0:T(8,128)(2,1)S(1)} %bitcast.120), channel_id=1, source_target_pairs={{0,1},{1,2},{2,3},{4,5},{5,6},{6,7},{8,9},{9,10},{10,11},{12,13},{... | collective-permute-start | bytes 3145736 | tf_op jit(solution)/shard_map/ppermute | solution.py:530
  100.8 23.0 %collective-permute-start.12 = (bf16[512,1024]{1,0:T(8,128)(2,1)S(1)}, bf16[512,1024]{1,0:T(8,128)(2,1)}, u32[]{:S(2)}, u32[]{:S(2)}) collective-permute-start(bf16[512,1024]{1,0:T(8,128)(2,1)S(1)} %collective-permute-done.11), channel_id=1, source_target_pairs={{1,0},{2,1},{5,4},{6,5},{9,8},{10,9},{13,12},{14,13},{17,16},{18,1... | collective-permute-start | bytes 3145736 | tf_op jit(solution)/shard_map/ppermute | solution.py:531
  105.2 24.1 %collective-permute-start.9 = (bf16[512,1024]{1,0:T(8,128)(2,1)}, bf16[512,1024]{1,0:T(8,128)(2,1)}, u32[]{:S(2)}, u32[]{:S(2)}) collective-permute-start(bf16[512,1024]{1,0:T(8,128)(2,1)} %collective-permute-done.8), channel_id=1, source_target_pairs={{1,2},{2,3},{5,6},{6,7},{9,10},{10,11},{13,14},{14,15},{17,18},{18... | collective-permute-start | bytes 3145736 | tf_op jit(solution)/shard_map/ppermute | solution.py:530
  123.8 35.6 %collective-permute-start.13 = (bf16[512,1024]{1,0:T(8,128)(2,1)}, bf16[512,1024]{1,0:T(8,128)(2,1)}, u32[]{:S(2)}, u32[]{:S(2)}) collective-permute-start(bf16[512,1024]{1,0:T(8,128)(2,1)} %collective-permute-done.12), channel_id=1, source_target_pairs={{1,0},{5,4},{9,8},{13,12},{17,16},{21,20},{25,24},{29,28}} | collective-permute-start | bytes 3145736 | tf_op jit(solution)/shard_map/ppermute | solution.py:531
  129.2 30.1 %collective-permute-start.10 = (bf16[512,1024]{1,0:T(8,128)(2,1)}, bf16[512,1024]{1,0:T(8,128)(2,1)}, u32[]{:S(2)}, u32[]{:S(2)}) collective-permute-start(bf16[512,1024]{1,0:T(8,128)(2,1)} %collective-permute-done.9), channel_id=1, source_target_pairs={{2,3},{6,7},{10,11},{14,15},{18,19},{22,23},{26,27},{30,31}} | collective-permute-start | bytes 3145736 | tf_op jit(solution)/shard_map/ppermute | solution.py:530
  137.0 34.3 %all-to-all-start.1 = ((bf16[4,256,512]{2,1,0:T(8,128)(2,1)}), bf16[4,256,512]{2,1,0:T(8,128)(2,1)}, u32[]{:S(2)}, u32[]{:S(2)}) async-start(bf16[4,256,512]{2,1,0:T(8,128)(2,1)} %pad_maximum_fusion.4), calls=%async_computation.1 | async-start | bytes 2097152 | tf_op jit(solution)/shard_map/all_to_all | solution.py:625
  193.7 19.9 %all-to-all-start.2 = ((bf16[4,512,256]{2,1,0:T(8,128)(2,1)}), bf16[4,512,256]{2,1,0:T(8,128)(2,1)S(1)}, u32[]{:S(2)}, u32[]{:S(2)}) async-start(bf16[4,512,256]{2,1,0:T(8,128)(2,1)} %bitcast.8), calls=%async_computation.2 | async-start | bytes 2097152 | tf_op jit(solution)/shard_map/all_to_all | solution.py:631
  200.9 226.5 %reduce-scatter.2.cloned.1.call-start = ((), (), s32[]{:S(2)}) async-start(), calls=%async_computation.8 | async-start | bytes 21823488 | tf_op jit(solution)/shard_map/reduce_scatter | solution.py:638
  325.2 28.3 %collective-permute-start.18 = (bf16[512,1024]{1,0:T(8,128)(2,1)}, bf16[512,1024]{1,0:T(8,128)(2,1)}, u32[]{:S(2)}, u32[]{:S(2)}) collective-permute-start(bf16[512,1024]{1,0:T(8,128)(2,1)} %get-tuple-element.68), channel_id=1, source_target_pairs={{0,1},{4,5},{8,9},{12,13},{16,17},{20,21},{24,25},{28,29}} | collective-permute-start | bytes 3145736 | tf_op jit(solution)/shard_map/ppermute | solution.py:568
  326.5 27.1 %collective-permute-start.19 = (bf16[512,1024]{1,0:T(8,128)(2,1)S(1)}, bf16[512,1024]{1,0:T(8,128)(2,1)}, u32[]{:S(2)}, u32[]{:S(2)}) collective-permute-start(bf16[512,1024]{1,0:T(8,128)(2,1)S(1)} %get-tuple-element.69), channel_id=1, source_target_pairs={{3,2},{7,6},{11,10},{15,14},{19,18},{23,22},{27,26},{31,30}} | collective-permute-start | bytes 3145736 | tf_op jit(solution)/shard_map/ppermute | solution.py:569
  357.7 36.8 %collective-permute-start.21 = (bf16[512,1024]{1,0:T(8,128)(2,1)}, bf16[512,1024]{1,0:T(8,128)(2,1)S(1)}, u32[]{:S(2)}, u32[]{:S(2)}) collective-permute-start(bf16[512,1024]{1,0:T(8,128)(2,1)} %get-tuple-element.75), channel_id=1, source_target_pairs={{0,1},{1,2},{4,5},{5,6},{8,9},{9,10},{12,13},{13,14},{16,17},{17,1... | collective-permute-start | bytes 3145736 | tf_op jit(solution)/shard_map/ppermute | solution.py:568
  362.1 32.5 %collective-permute-start.22 = (bf16[512,1024]{1,0:T(8,128)(2,1)S(1)}, bf16[512,1024]{1,0:T(8,128)(2,1)}, u32[]{:S(2)}, u32[]{:S(2)}) collective-permute-start(bf16[512,1024]{1,0:T(8,128)(2,1)S(1)} %get-tuple-element.76), channel_id=1, source_target_pairs={{2,1},{3,2},{6,5},{7,6},{10,9},{11,10},{14,13},{15,14},{18,17},{19... | collective-permute-start | bytes 3145736 | tf_op jit(solution)/shard_map/ppermute | solution.py:569
  363.4 26.8 %collective-permute-start.29 = (bf16[40,768]{1,0:T(8,128)(2,1)S(1)}, bf16[40,768]{1,0:T(8,128)(2,1)S(1)}, u32[]{:S(2)}, u32[]{:S(2)}) collective-permute-start(bf16[40,768]{1,0:T(8,128)(2,1)S(1)} %get-tuple-element.122), channel_id=1, source_target_pairs={{0,2},{1,3},{2,0},{3,1},{4,6},{5,7},{6,4},{7,5},{8,10},{9,11},{10,... | collective-permute-start | bytes 184328 | tf_op jit(solution)/shard_map/ppermute | solution.py:580
  365.9 28.0 %collective-permute-start.30 = (bf16[40,768]{1,0:T(8,128)(2,1)S(1)}, bf16[40,768]{1,0:T(8,128)(2,1)S(1)}, u32[]{:S(2)}, u32[]{:S(2)}) collective-permute-start(bf16[40,768]{1,0:T(8,128)(2,1)S(1)} %get-tuple-element.123), channel_id=1, source_target_pairs={{0,3},{1,0},{2,1},{3,2},{4,7},{5,4},{6,5},{7,6},{8,11},{9,8},{10,9... | collective-permute-start | bytes 184328 | tf_op jit(solution)/shard_map/ppermute | solution.py:580
  367.6 26.3 %collective-permute-start.28 = (bf16[40,768]{1,0:T(8,128)(2,1)S(1)}, bf16[40,768]{1,0:T(8,128)(2,1)S(1)}, u32[]{:S(2)}, u32[]{:S(2)}) collective-permute-start(bf16[40,768]{1,0:T(8,128)(2,1)S(1)} %get-tuple-element.124), channel_id=1, source_target_pairs={{0,1},{1,2},{2,3},{3,0},{4,5},{5,6},{6,7},{7,4},{8,9},{9,10},{10,1... | collective-permute-start | bytes 184328 | tf_op jit(solution)/shard_map/ppermute | solution.py:580
  397.5 25.9 %collective-permute-start.26 = (bf16[512,1024]{1,0:T(8,128)(2,1)S(1)}, bf16[512,1024]{1,0:T(8,128)(2,1)S(1)}, u32[]{:S(2)}, u32[]{:S(2)}) collective-permute-start(bf16[512,1024]{1,0:T(8,128)(2,1)S(1)} %get-tuple-element.79), channel_id=1, source_target_pairs={{0,1},{1,2},{2,3},{4,5},{5,6},{6,7},{8,9},{9,10},{10,11},{12,13},{... | collective-permute-start | bytes 3145736 | tf_op jit(solution)/shard_map/ppermute | solution.py:568
  399.4 25.9 %collective-permute-start.27 = (bf16[512,1024]{1,0:T(8,128)(2,1)S(1)}, bf16[512,1024]{1,0:T(8,128)(2,1)S(1)}, u32[]{:S(2)}, u32[]{:S(2)}) collective-permute-start(bf16[512,1024]{1,0:T(8,128)(2,1)S(1)} %get-tuple-element.80), channel_id=1, source_target_pairs={{1,0},{2,1},{3,2},{5,4},{6,5},{7,6},{9,8},{10,9},{11,10},{13,12},{... | collective-permute-start | bytes 3145736 | tf_op jit(solution)/shard_map/ppermute | solution.py:569
  430.5 40.2 %collective-permute-start.31 = (bf16[1184,256]{1,0:T(8,128)(2,1)S(1)}, bf16[1184,256]{1,0:T(8,128)(2,1)S(1)}, u32[]{:S(2)}, u32[]{:S(2)}) collective-permute-start(bf16[1184,256]{1,0:T(8,128)(2,1)S(1)} %get-tuple-element.102), channel_id=1, source_target_pairs={{0,1},{1,2},{2,3},{3,0},{4,5},{5,6},{6,7},{7,4},{8,9},{9,10},{10,1... | collective-permute-start | bytes 1818632 | tf_op jit(solution)/shard_map/ppermute | solution.py:580
  430.5 50.3 %collective-permute-start.32 = (bf16[1184,256]{1,0:T(8,128)(2,1)S(1)}, bf16[1184,256]{1,0:T(8,128)(2,1)S(1)}, u32[]{:S(2)}, u32[]{:S(2)}) collective-permute-start(bf16[1184,256]{1,0:T(8,128)(2,1)S(1)} %get-tuple-element.103), channel_id=1, source_target_pairs={{0,2},{1,3},{2,0},{3,1},{4,6},{5,7},{6,4},{7,5},{8,10},{9,11},{10,... | collective-permute-start | bytes 1818632 | tf_op jit(solution)/shard_map/ppermute | solution.py:580
  434.7 49.6 %collective-permute-start.33 = (bf16[1184,256]{1,0:T(8,128)(2,1)S(1)}, bf16[1184,256]{1,0:T(8,128)(2,1)S(1)}, u32[]{:S(2)}, u32[]{:S(2)}) collective-permute-start(bf16[1184,256]{1,0:T(8,128)(2,1)S(1)} %get-tuple-element.104), channel_id=1, source_target_pairs={{0,3},{1,0},{2,1},{3,2},{4,7},{5,4},{6,5},{7,6},{8,11},{9,8},{10,9... | collective-permute-start | bytes 1818632 | tf_op jit(solution)/shard_map/ppermute | solution.py:580
  (34 other events, 414.3 us)
Sparse Core Ops, SparseCore 0:
  24.7 27.5 all-gather.3
  75.6 43.2 all-gather.7
  120.8 76.1 all-gather.5
  258.7 139.0 reduce-scatter.1

commit v9 on v5

--- a/solution.py
+++ b/solution.py
@@ -191,8 +191,7 @@
 
 def backward_kernel(
     heads, top, chosen_ref, counts_ref, q_ref, k_ref, v_ref, mk_ref, mv_ref, go_ref, out_ref, lse_ref,
-    cos_ref, sin_ref, tok_ref, gain_ref, w_ref, partial_ref, grad_w_ref, gain_grad_ref,
-    gk_s, gv_s, gq_s, grad_s, gw_s,
+    cos_ref, sin_ref, w_ref, partial_ref, grad_ref, gk_s, gv_s, gq_s,
 ):
     block = pl.num_programs(0) - 1 - pl.program_id(0)
     rows = q_ref.shape[0]
@@ -207,8 +206,6 @@
     def _():
         gk_s[...] = jnp.zeros_like(gk_s)
         gv_s[...] = jnp.zeros_like(gv_s)
-        gw_s[...] = jnp.zeros_like(gw_s)
-        gain_grad_ref[...] = jnp.zeros_like(gain_grad_ref)
 
     def spread(column):
         return jnp.transpose(jnp.broadcast_to(column, (rows, HEAD_DIM)))[:1]
@@ -264,30 +261,17 @@
     for head in range(heads):
         columns = slice(head * HEAD_DIM, (head + 1) * HEAD_DIM)
         at = head * HEAD_DIM
-        grad_s[:, at : at + HEAD_DIM] = unturn(gq_s[:, columns] * SCALE).astype(BF16)
+        grad_ref[:, at : at + HEAD_DIM] = unturn(gq_s[:, columns] * SCALE).astype(BF16)
         grad_key = gk_s[own, columns] * (1.0 / LOG2E)
-        grad_s[:, wide + at : wide + at + HEAD_DIM] = unturn(grad_key).astype(BF16)
-        grad_s[:, 2 * wide + at : 2 * wide + at + HEAD_DIM] = gv_s[own, columns].astype(BF16)
-
-    tokens = tok_ref[...].astype(F32)
-    tokens = tokens * lax.rsqrt(jnp.mean(tokens * tokens, -1, keepdims=True) + EPSILON)
-    normed = (tokens * gain_ref[...]).astype(BF16)
-    grad = grad_s[...]
-    partial = dot(grad, w_ref[...], NT)
-    partial_ref[...] = partial.astype(BF16)
-    gain_grad_ref[...] += jnp.sum(partial * tokens, 0, keepdims=True)
-    gw_s[...] += dot(normed, grad, TN)
-
-    @pl.when(block == 0)
-    def _():
-        grad_w_ref[...] = gw_s[...].astype(BF16)
-
-
-def attend_backward(
-    chosen, counts, qkv, memory, grad_out, out, lse, cosine, sine, tokens_all, gain, w_qkv, heads, top
-):
+        grad_ref[:, wide + at : wide + at + HEAD_DIM] = unturn(grad_key).astype(BF16)
+        grad_ref[:, 2 * wide + at : 2 * wide + at + HEAD_DIM] = gv_s[own, columns].astype(BF16)
+
+    partial_ref[...] = dot(grad_ref[...], w_ref[...], NT).astype(BF16)
+
+
+def attend_backward(chosen, counts, qkv, memory, grad_out, out, lse, cosine, sine, w_qkv, heads, top):
     length = qkv.shape[0]
-    width = tokens_all.shape[1]
+    width = w_qkv.shape[0]
     wide = heads * HEAD_DIM
     rows = min(2 * QBLK, length)
     mem_rows = memory.shape[0]
@@ -308,27 +292,21 @@
                 pl.BlockSpec((rows, heads), lambda i, *_: (last - i, 0)),
                 pl.BlockSpec((rows, HEAD_DIM), lambda i, *_: (last - i, 0)),
                 pl.BlockSpec((rows, HEAD_DIM), lambda i, *_: (last - i, 0)),
-                pl.BlockSpec((rows, width), lambda i, *_: (last - i, 0)),
-                pl.BlockSpec((1, width), lambda i, *_: (0, 0)),
                 pl.BlockSpec((width, 3 * wide), lambda i, *_: (0, 0)),
             ],
             out_specs=[
                 pl.BlockSpec((rows, width), lambda i, *_: (last - i, 0)),
-                pl.BlockSpec((width, 3 * wide), lambda i, *_: (0, 0)),
-                pl.BlockSpec((1, width), lambda i, *_: (0, 0)),
+                pl.BlockSpec((rows, 3 * wide), lambda i, *_: (last - i, 0)),
             ],
             scratch_shapes=[
                 pltpu.VMEM((length, wide), F32),
                 pltpu.VMEM((length, wide), F32),
                 pltpu.VMEM((rows, wide), F32),
-                pltpu.VMEM((rows, 3 * wide), BF16),
-                pltpu.VMEM((width, 3 * wide), F32),
             ],
         ),
         out_shape=[
             jax.ShapeDtypeStruct((length, width), BF16),
-            jax.ShapeDtypeStruct((width, 3 * wide), BF16),
-            jax.ShapeDtypeStruct((1, width), F32),
+            jax.ShapeDtypeStruct((length, 3 * wide), BF16),
         ],
         compiler_params=pltpu.CompilerParams(vmem_limit_bytes=48 * MIB),
         cost_estimate=pl.CostEstimate(
@@ -338,7 +316,7 @@
         ),
         name="attend_backward",
     )(
-        chosen, counts, qkv, qkv, qkv, memory, memory, grad_out, out, lse, cosine, sine, tokens_all, gain, w_qkv
+        chosen, counts, qkv, qkv, qkv, memory, memory, grad_out, out, lse, cosine, sine, w_qkv
     )
 
 
@@ -515,6 +493,54 @@
     )(tokens, attended, upstream, gain, weights, weights, weights, w_down)
 
 
+def projection_grads_kernel(tok_ref, gain_ref, w_ref, grad_ref, grad_w_ref, gain_grad_ref, raw_s):
+    step = pl.program_id(0)
+
+    @pl.when(step == 0)
+    def _():
+        raw_s[...] = jnp.zeros_like(raw_s)
+
+    tokens = tok_ref[...].astype(F32)
+    tokens = tokens * lax.rsqrt(jnp.mean(tokens * tokens, -1, keepdims=True) + EPSILON)
+    raw_s[...] += dot(tokens.astype(BF16), grad_ref[...], TN)
+
+    @pl.when(step == pl.num_programs(0) - 1)
+    def _():
+        raw = raw_s[...]
+        gain_grad_ref[...] = jnp.sum(raw * w_ref[...].astype(F32), -1, keepdims=True)
+        grad_w_ref[...] = (raw * gain_ref[...]).astype(BF16)
+
+
+def projection_grads(tokens_all, gain_column, w_qkv, grad):
+    length, width = tokens_all.shape
+    columns = grad.shape[1]
+    rows = min(2 * QBLK, length)
+    return pl.pallas_call(
+        projection_grads_kernel,
+        grid=(length // rows,),
+        in_specs=[
+            pl.BlockSpec((rows, width), lambda i: (i, 0)),
+            pl.BlockSpec((width, 1), lambda i: (0, 0)),
+            pl.BlockSpec((width, columns), lambda i: (0, 0)),
+            pl.BlockSpec((rows, columns), lambda i: (i, 0)),
+        ],
+        out_specs=[
+            pl.BlockSpec((width, columns), lambda i: (0, 0)),
+            pl.BlockSpec((width, 1), lambda i: (0, 0)),
+        ],
+        out_shape=[
+            jax.ShapeDtypeStruct((width, columns), BF16),
+            jax.ShapeDtypeStruct((width, 1), F32),
+        ],
+        scratch_shapes=[pltpu.VMEM((width, columns), F32)],
+        compiler_params=pltpu.CompilerParams(vmem_limit_bytes=48 * MIB),
+        cost_estimate=pl.CostEstimate(
+            flops=2 * length * width * columns, bytes_accessed=2 * length * (width + columns), transcendentals=0
+        ),
+        name="projection_grads",
+    )(tokens_all, gain_column, w_qkv, grad)
+
+
 def after(value, earlier):
     return lax.optimization_barrier((value, earlier))[0]
 
@@ -602,7 +628,7 @@
     shards = jnp.concatenate([w_out, w_gate, w_up], 1)
     (near, near_down), steps = chain_gather((shards, w_down), "fsdp")
     (gathered,), token_steps = chain_gather((after(mine, steps[-2]),), "fsdp")
-    parcel = lax.all_gather(parcel, DP, axis=0, tiled=True)
+    parcel = lax.all_gather(after(parcel, steps[0]), DP, axis=0, tiled=True)
     w_qkv = parcel[:, :share].reshape(width, 3 * wide)
     gain_one = parcel[:, share, :share].reshape(1, width).astype(F32)
     gain_two = parcel[:, share, share : 2 * share].reshape(1, width).astype(F32)
@@ -627,14 +653,14 @@
     grad_heads = lax.all_to_all(grad_attended, "fsdp", 1, 0, tiled=True)
     grads = lax.psum_scatter(grads, DP, scatter_dimension=0, tiled=True)[0]
 
-    partial, grad_w_qkv, gain_one_grad = attend_backward(
-        chosen_all, counts_all, qkv, memory, grad_heads, attended_heads, lse, cosine, sine, gathered, gain_one,
-        w_qkv, heads, top,
+    partial, grad_qkv = attend_backward(
+        chosen_all, counts_all, qkv, memory, grad_heads, attended_heads, lse, cosine, sine, w_qkv, heads, top
     )
     own_term, steps = chain_scatter(partial, "fsdp")
+    grad_w_qkv, gain_one_grad = projection_grads(gathered, gain_one.reshape(width, 1), w_qkv, grad_qkv)
     grads = after(grads, steps[-1])
 
-    gains = jnp.concatenate([gain_one_grad, gain_two_grad], 0).reshape(2, span, -1).transpose(1, 0, 2)
+    gains = jnp.stack([gain_one_grad.reshape(span, -1), gain_two_grad.reshape(span, -1)], 1)
     gains = jnp.pad(gains.astype(BF16), ((0, 0), (0, extra - 2), (0, 3 * wide - gains.shape[2])))
     late = jnp.concatenate([grad_w_qkv.reshape(span, -1, 3 * wide), gains], 1)
     late = late.reshape(span // 2, 2, late.shape[1], 3 * wide)

time: 477 us -> 482 us (1.010); the launches traced: 475 us -> 473 us
  blocking collectives: 30.5 us -> 15.8 us
  starting transfers between devices: 67 us -> 73.4 us
    all_to_all x1 -> x0, blocking collectives: 14.7 us -> none  [body(): parcel = lax.all_to_all(parcel, 'fsdp', 0, 0, tiled=True)]
    pallas_call x0 -> x1, Pallas kernels: none -> 7.98 us  [projection_grads(): pl.pallas_call(projection_grads_kernel, grid=(length // rows,), in_specs=...]
    ppermute x9, waiting for transfers between devices: 75.8 us -> 81.3 us  [chain_gather(): falling = tuple((lax.ppermute(block, axis, down) for block in falling))]
    pallas_call x1, Pallas kernels: 38.7 us -> 33.8 us  [attend_backward(): pl.pallas_call(functools.partial(backward_kernel, heads, top), grid_spec=...]
  transfers between devices with their start and end apart: 34 -> 35, of which waited for: 15 -> 15; matrix products, arithmetic and copies ran while one was open for 9% -> 11% of each run, Pallas kernels for 14% -> 15%
where the time goes in v9:
time: 482 us; the launch traced here: 473 us
  waiting for transfers between devices  190 us (39%)
  Pallas kernels  114 us (24%)
  starting transfers between devices  73.4 us (15%)
  other arithmetic  36.5 us (8%)
  local copies, waits for them, and re-layouts  28.4 us (6%)
  blocking collectives  15.8 us (3%)
  between operations  14.7 us (3%)
    ppermute x9, waiting for transfers between devices, chain_gather(): falling = tuple((lax.ppermute(block, axis, down) for block in falling))  81.3 us
    ppermute x3, waiting for transfers between devices, chain_scatter(): rising = lax.ppermute(up, axis, [(i, i + 1) for i in range(step + 1)])  52.3 us
    pallas_call x1, Pallas kernels, feed_forward(): pl.pallas_call(functools.partial(ffn_kernel, span, merged), grid=(steps,)...  43.9 us
    pallas_call x1, Pallas kernels, attend_backward(): pl.pallas_call(functools.partial(backward_kernel, heads, top), grid_spec=...  33.8 us
    pallas_call x1, Pallas kernels, attend_forward(): pl.pallas_call(functools.partial(forward_kernel, heads, top), grid_spec=p...  21.4 us
    ppermute x9, starting transfers between devices, chain_gather(): rising = tuple((lax.ppermute(block, axis, up) for block in rising))  21.1 us
    all_to_all x1, blocking collectives, body(): lax.all_to_all(late, 'chip', 0, 0, tiled=True).astype(F32)  15.8 us
    all_to_all x1, waiting for transfers between devices, body(): grad_heads = lax.all_to_all(grad_attended, 'fsdp', 1, 0, tiled=True)  15.6 us
  transfers between devices with their start and end apart: 35, of which 15 were waited for; matrix products, arithmetic and copies ran while one was open for 11% of the time, Pallas kernels for 15%

profile of v9, /device:TPU:0, one launch (start us, length us, event | category | flops | bytes accessed | tf_op | source)
XLA Modules:
  0.0 473.2 jit_solution(16752821894966252123)
XLA Ops:
  11.2 5.6 %collective-permute-start = (bf16[32,6656]{1,0:T(8,128)(2,1)S(1)}, bf16[32,6656]{1,0:T(8,128)(2,1)S(1)}, u32[]{:S(2)}, u32[]{:S(2)}) collective-permute-start(bf16[32,6656]{1,0:T(8,128)(2,1)S(1)} %constant_dynamic-update-slice_fusion), channel_id=1, source_target_pairs={{0,1},{1,2},{2,3},{4,5},{5,6},{6,7},{8,9},{9,10},{10,11},{12,13},{... | collective-permute-start | bytes 1277960 | tf_op jit(solution)/shard_map/ppermute | solution.py:556
  43.2 14.4 %collective-permute-done.7 = bf16[88,1024]{1,0:T(8,128)(2,1)S(1)} collective-permute-done((bf16[88,1024]{1,0:T(8,128)(2,1)S(1)}, bf16[88,1024]{1,0:T(8,128)(2,1)S(1)}, u32[]{:S(2)}, u32[]{:S(2)}) %collective-permute-start.7) | collective-permute-done | bytes 180256 | tf_op jit(solution)/shard_map/ppermute | solution.py:557
  61.6 11.5 %collective-permute-done.17 = bf16[88,1024]{1,0:T(8,128)(2,1)} collective-permute-done((bf16[88,1024]{1,0:T(8,128)(2,1)S(1)}, bf16[88,1024]{1,0:T(8,128)(2,1)}, u32[]{:S(2)}, u32[]{:S(2)}) %collective-permute-start.17) | collective-permute-done | bytes 180256 | tf_op jit(solution)/shard_map/ppermute | solution.py:557
  78.5 5.6 %collective-permute-start.8 = (bf16[512,1024]{1,0:T(8,128)(2,1)S(1)}, bf16[512,1024]{1,0:T(8,128)(2,1)}, u32[]{:S(2)}, u32[]{:S(2)}) collective-permute-start(bf16[512,1024]{1,0:T(8,128)(2,1)S(1)} %bitcast.87), channel_id=1, source_target_pairs={{0,1},{1,2},{2,3},{4,5},{5,6},{6,7},{8,9},{9,10},{10,11},{12,13},{... | collective-permute-start | bytes 3145736 | tf_op jit(solution)/shard_map/ppermute | solution.py:556
  84.0 16.5 %collective-permute-done.11 = bf16[512,1024]{1,0:T(8,128)(2,1)S(1)} collective-permute-done((bf16[512,1024]{1,0:T(8,128)(2,1)S(1)}, bf16[512,1024]{1,0:T(8,128)(2,1)S(1)}, u32[]{:S(2)}, u32[]{:S(2)}) %collective-permute-start.11) | collective-permute-done | bytes 1048608 | tf_op jit(solution)/shard_map/ppermute | solution.py:557
  106.5 17.1 %collective-permute-done.12 = bf16[512,1024]{1,0:T(8,128)(2,1)} collective-permute-done((bf16[512,1024]{1,0:T(8,128)(2,1)S(1)}, bf16[512,1024]{1,0:T(8,128)(2,1)}, u32[]{:S(2)}, u32[]{:S(2)}) %collective-permute-start.12) | collective-permute-done | bytes 1048608 | tf_op jit(solution)/shard_map/ppermute | solution.py:557
  132.7 5.9 %all-to-all-start.1 = ((bf16[4,256,512]{2,1,0:T(8,128)(2,1)}), bf16[4,256,512]{2,1,0:T(8,128)(2,1)}, u32[]{:S(2)}, u32[]{:S(2)}) async-start(bf16[4,256,512]{2,1,0:T(8,128)(2,1)} %pad_maximum_fusion.5), calls=%async_computation.1 | async-start | bytes 2097152 | tf_op jit(solution)/shard_map/all_to_all | solution.py:641
  141.4 18.0 %collective-permute-done.13 = bf16[512,1024]{1,0:T(8,128)(2,1)} collective-permute-done((bf16[512,1024]{1,0:T(8,128)(2,1)}, bf16[512,1024]{1,0:T(8,128)(2,1)}, u32[]{:S(2)}, u32[]{:S(2)}) %collective-permute-start.13) | collective-permute-done | bytes 1048608 | tf_op jit(solution)/shard_map/ppermute | solution.py:557
  164.1 7.4 %project_qkv.1.q_ref.k_ref.v_ref = bf16[2048,768]{1,0:T(8,128)(2,1)} custom-call(bf16[2048,1024]{1,0:T(8,128)(2,1)} %pad_maximum_fusion.tok_ref, f32[1,1024]{1,0:T(1,128)S(1)} %reshape.191.gain_ref, bf16[1024,768]{1,0:T(8,128)(2,1)S(1)} %bitcast.81, f32[2048,128]{1,0:T(8,128)S(1)} %get-tuple-element.127.cos_ref, f32[2048,128]{1,0:T(8,128)S(1)} %copy-done.2), custom_call_target="tpu_custom_call" | custom-call | flops 3221225472 | bytes 14680064 | tf_op jit(solution)/shard_map/project_qkv/pallas_call | solution.py:62
  171.5 21.4 %attend_forward.1 = (bf16[2048,256]{1,0:T(8,128)(2,1)}, f32[2048,2]{1,0:T(8,128)S(1)}) custom-call(s32[32]{0:T(128)S(1)} %reshape_squeeze.24.chosen_ref, s32[32]{0:T(128)S(1)} %reshape_squeeze.25.counts_ref, bf16[2048,768]{1,0:T(8,128)(2,1)} %project_qkv.1.q_ref.k_ref.v_ref, bf16[2048,768]{1,0:T(8,128)(2,1)} %project_qkv.1.q_ref.k_ref.v_ref, ...), custom_call_target="tpu_custom_call" | custom-call | flops 3221225472 | bytes 4194304 | tf_op jit(solution)/shard_map/attend_forward/pallas_call | solution.py:157
  192.9 4.6 all-to-all-start.2
  198.4 15.1 %all-to-all-done.2 = bf16[4,512,256]{2,1,0:T(8,128)(2,1)S(1)} async-done(((bf16[4,512,256]{2,1,0:T(8,128)(2,1)}), bf16[4,512,256]{2,1,0:T(8,128)(2,1)S(1)}, u32[]{:S(2)}, u32[]{:S(2)}) %all-to-all-start.2) | async-done | bytes 1048608 | tf_op jit(solution)/shard_map/all_to_all | solution.py:647
  214.6 43.9 %feed_forward.1 = (bf16[512,1024]{1,0:T(8,128)(2,1)}, f32[512,1024]{1,0:T(8,128)}, bf16[512,1024]{1,0:T(8,128)(2,1)}, f32[1,1024]{1,0:T(1,128)}, bf16[8,4736,256]{2,1,0:T(8,128)(2,1)}) custom-call(bf16[512,1024]{1,0:T(8,128)(2,1)} %bitcast.85, bf16[512,1024]{1,0:T(8,128)(2,1)} %bitcast.101, bf16[512,1024]{1,0:T(8,128)(2,1)} %bitcast.118, ...), custom_call_target="tpu_custom_call" | custom-call | flops 29796335616 | bytes 38797312 | tf_op jit(solution)/shard_map/feed_forward/pallas_call | solution.py:458
  264.7 15.6 %all-to-all-done.3 = bf16[512,4,256]{2,0,1:T(8,128)(2,1)S(1)} async-done(((bf16[512,4,256]{2,0,1:T(8,128)(2,1)}), bf16[512,4,256]{2,0,1:T(8,128)(2,1)S(1)}, u32[]{:S(2)}, u32[]{:S(2)}) %all-to-all-start.3) | async-done | bytes 1048608 | tf_op jit(solution)/shard_map/all_to_all | solution.py:653
  280.3 33.8 %attend_backward.1 = (bf16[2048,1024]{1,0:T(8,128)(2,1)}, bf16[2048,768]{1,0:T(8,128)(2,1)}) custom-call(s32[32]{0:T(128)S(1)} %reshape_squeeze.24.chosen_ref, s32[32]{0:T(128)S(1)} %reshape_squeeze.25.counts_ref, bf16[2048,768]{1,0:T(8,128)(2,1)} %project_qkv.1.q_ref.k_ref.v_ref, bf16[2048,768]{1,0:T(8,128)(2,1)} %project_qkv.1.q_ref.k_ref.v_ref, ...), custom_call_target="tpu_custom_call" | custom-call | flops 8053063680 | bytes 8388608 | tf_op jit(solution)/shard_map/attend_backward/pallas_call | solution.py:279
  318.7 20.5 %collective-permute-done.18 = bf16[512,1024]{1,0:T(8,128)(2,1)S(1)} collective-permute-done((bf16[512,1024]{1,0:T(8,128)(2,1)S(1)}, bf16[512,1024]{1,0:T(8,128)(2,1)S(1)}, u32[]{:S(2)}, u32[]{:S(2)}) %collective-permute-start.18) | collective-permute-done | bytes 1048608 | tf_op jit(solution)/shard_map/ppermute | solution.py:593
  343.1 4.5 collective-permute-start.20
  348.3 22.0 %collective-permute-done.20 = bf16[512,1024]{1,0:T(8,128)(2,1)S(1)} collective-permute-done((bf16[512,1024]{1,0:T(8,128)(2,1)}, bf16[512,1024]{1,0:T(8,128)(2,1)S(1)}, u32[]{:S(2)}, u32[]{:S(2)}) %collective-permute-start.20) | collective-permute-done | bytes 1048608 | tf_op jit(solution)/shard_map/ppermute | solution.py:593
  372.9 8.6 %collective-permute-start.22 = (bf16[512,1024]{1,0:T(8,128)(2,1)S(1)}, bf16[512,1024]{1,0:T(8,128)(2,1)}, u32[]{:S(2)}, u32[]{:S(2)}) collective-permute-start(bf16[512,1024]{1,0:T(8,128)(2,1)S(1)} %get-tuple-element.80), channel_id=1, source_target_pairs={{0,1},{1,2},{2,3},{4,5},{5,6},{6,7},{8,9},{9,10},{10,11},{12,13},{... | collective-permute-start | bytes 3145736 | tf_op jit(solution)/shard_map/ppermute | solution.py:593
  383.0 9.8 %collective-permute-done.22 = bf16[512,1024]{1,0:T(8,128)(2,1)} collective-permute-done((bf16[512,1024]{1,0:T(8,128)(2,1)S(1)}, bf16[512,1024]{1,0:T(8,128)(2,1)}, u32[]{:S(2)}, u32[]{:S(2)}) %collective-permute-start.22) | collective-permute-done | bytes 1048608 | tf_op jit(solution)/shard_map/ppermute | solution.py:593
  392.8 5.5 %collective-permute-done.23 = bf16[512,1024]{1,0:T(8,128)(2,1)} collective-permute-done((bf16[512,1024]{1,0:T(8,128)(2,1)S(1)}, bf16[512,1024]{1,0:T(8,128)(2,1)}, u32[]{:S(2)}, u32[]{:S(2)}) %collective-permute-start.23) | collective-permute-done | bytes 1048608 | tf_op jit(solution)/shard_map/ppermute | solution.py:594
  406.2 8.0 %projection_grads.1 = (bf16[1024,768]{1,0:T(8,128)(2,1)S(1)}, f32[1024,1]{1,0:T(8,128)S(1)}) custom-call(bf16[2048,1024]{1,0:T(8,128)(2,1)} %pad_maximum_fusion.tok_ref, f32[1024,1]{1,0:T(8,128)S(1)} %copy-done.3, bf16[1024,768]{1,0:T(8,128)(2,1)S(1)} %bitcast.83, bf16[2048,768]{1,0:T(8,128)(2,1)} %get-tuple-element.84.grad_ref), custom_call_target="tpu_custom_call" | custom-call | flops 3221225472 | bytes 7340032 | tf_op jit(solution)/shard_map/projection_grads/pallas_call | solution.py:518
  418.2 15.8 %all_to_all.58 = bf16[4,136,768]{2,1,0:T(8,128)(2,1)S(1)} all-to-all(bf16[4,136,768]{2,1,0:T(8,128)(2,1)S(1)} %fusion.4), channel_id=1, replica_groups=mesh['chip'=4,'core'=2,'fsdp'=4] {'chip'}, dimensions={0} | all-to-all | bytes 1671168 | tf_op jit(solution)/shard_map/all_to_all | solution.py:671
  438.4 15.3 %all-to-all-done.5 = bf16[4,40,768]{2,1,0:T(8,128)(2,1)S(1)} async-done(((bf16[4,40,768]{2,1,0:T(8,128)(2,1)}), bf16[4,40,768]{2,1,0:T(8,128)(2,1)S(1)}, u32[]{:S(2)}, u32[]{:S(2)}) %all-to-all-start.5) | async-done | bytes 245792 | tf_op jit(solution)/shard_map/all_to_all | solution.py:675
  (170 shorter events, 112.3 us)
Async XLA Ops:
  9.9 28.4 %collective-permute-start.2 = (bf16[32,6656]{1,0:T(8,128)(2,1)S(1)}, bf16[32,6656]{1,0:T(8,128)(2,1)S(1)}, u32[]{:S(2)}, u32[]{:S(2)}) collective-permute-start(bf16[32,6656]{1,0:T(8,128)(2,1)S(1)} %constant_dynamic-update-slice_fusion), channel_id=1, source_target_pairs={{1,0},{2,1},{3,2},{5,4},{6,5},{7,6},{9,8},{10,9},{11,10},{13,12},{... | collective-permute-start | bytes 1277960 | tf_op jit(solution)/shard_map/ppermute | solution.py:557
  11.2 27.1 %collective-permute-start = (bf16[32,6656]{1,0:T(8,128)(2,1)S(1)}, bf16[32,6656]{1,0:T(8,128)(2,1)S(1)}, u32[]{:S(2)}, u32[]{:S(2)}) collective-permute-start(bf16[32,6656]{1,0:T(8,128)(2,1)S(1)} %constant_dynamic-update-slice_fusion), channel_id=1, source_target_pairs={{0,1},{1,2},{2,3},{4,5},{5,6},{6,7},{8,9},{9,10},{10,11},{12,13},{... | collective-permute-start | bytes 1277960 | tf_op jit(solution)/shard_map/ppermute | solution.py:556
  27.0 111.7 %all-gather.4.cloned.1.call-start = ((), (), s32[]{:S(2)}) async-start(), calls=%async_computation.8 | async-start | bytes 2211840 | tf_op jit(solution)/shard_map/all_gather | solution.py:631
  39.1 175.5 %all-gather.8.cloned.1.call-start = ((), (), s32[]{:S(2)}) async-start(), calls=%async_computation.10 | async-start | bytes 6488064 | tf_op jit(solution)/shard_map/all_gather | solution.py:642
  39.2 18.4 %collective-permute-start.4 = (bf16[32,6656]{1,0:T(8,128)(2,1)S(1)}, bf16[32,6656]{1,0:T(8,128)(2,1)S(1)}, u32[]{:S(2)}, u32[]{:S(2)}) collective-permute-start(bf16[32,6656]{1,0:T(8,128)(2,1)S(1)} %collective-permute-done), channel_id=1, source_target_pairs={{1,2},{2,3},{5,6},{6,7},{9,10},{10,11},{13,14},{14,15},{17,18},{18... | collective-permute-start | bytes 1277960 | tf_op jit(solution)/shard_map/ppermute | solution.py:556
  39.9 17.7 %collective-permute-start.6 = (bf16[32,6656]{1,0:T(8,128)(2,1)S(1)}, bf16[32,6656]{1,0:T(8,128)(2,1)S(1)}, u32[]{:S(2)}, u32[]{:S(2)}) collective-permute-start(bf16[32,6656]{1,0:T(8,128)(2,1)S(1)} %collective-permute-done.2), channel_id=1, source_target_pairs={{1,0},{2,1},{5,4},{6,5},{9,8},{10,9},{13,12},{14,13},{17,16},{18,1... | collective-permute-start | bytes 1277960 | tf_op jit(solution)/shard_map/ppermute | solution.py:557
  75.3 139.3 %all-gather.6.cloned.1.call-start = ((), (), s32[]{:S(2)}) async-start(), calls=%async_computation.9 | async-start | bytes 15335424 | tf_op jit(solution)/shard_map/all_gather | solution.py:635
  77.2 23.3 %collective-permute-start.11 = (bf16[512,1024]{1,0:T(8,128)(2,1)S(1)}, bf16[512,1024]{1,0:T(8,128)(2,1)S(1)}, u32[]{:S(2)}, u32[]{:S(2)}) collective-permute-start(bf16[512,1024]{1,0:T(8,128)(2,1)S(1)} %bitcast.86), channel_id=1, source_target_pairs={{1,0},{2,1},{3,2},{5,4},{6,5},{7,6},{9,8},{10,9},{11,10},{13,12},{... | collective-permute-start | bytes 3145736 | tf_op jit(solution)/shard_map/ppermute | solution.py:557
  78.5 23.3 %collective-permute-start.8 = (bf16[512,1024]{1,0:T(8,128)(2,1)S(1)}, bf16[512,1024]{1,0:T(8,128)(2,1)}, u32[]{:S(2)}, u32[]{:S(2)}) collective-permute-start(bf16[512,1024]{1,0:T(8,128)(2,1)S(1)} %bitcast.87), channel_id=1, source_target_pairs={{0,1},{1,2},{2,3},{4,5},{5,6},{6,7},{8,9},{9,10},{10,11},{12,13},{... | collective-permute-start | bytes 3145736 | tf_op jit(solution)/shard_map/ppermute | solution.py:556
  100.5 23.1 %collective-permute-start.12 = (bf16[512,1024]{1,0:T(8,128)(2,1)S(1)}, bf16[512,1024]{1,0:T(8,128)(2,1)}, u32[]{:S(2)}, u32[]{:S(2)}) collective-permute-start(bf16[512,1024]{1,0:T(8,128)(2,1)S(1)} %collective-permute-done.11), channel_id=1, source_target_pairs={{1,0},{2,1},{5,4},{6,5},{9,8},{10,9},{13,12},{14,13},{17,16},{18,1... | collective-permute-start | bytes 3145736 | tf_op jit(solution)/shard_map/ppermute | solution.py:557
  101.8 23.1 %collective-permute-start.9 = (bf16[512,1024]{1,0:T(8,128)(2,1)}, bf16[512,1024]{1,0:T(8,128)(2,1)}, u32[]{:S(2)}, u32[]{:S(2)}) collective-permute-start(bf16[512,1024]{1,0:T(8,128)(2,1)} %collective-permute-done.8), channel_id=1, source_target_pairs={{1,2},{2,3},{5,6},{6,7},{9,10},{10,11},{13,14},{14,15},{17,18},{18... | collective-permute-start | bytes 3145736 | tf_op jit(solution)/shard_map/ppermute | solution.py:556
  123.6 35.8 %collective-permute-start.13 = (bf16[512,1024]{1,0:T(8,128)(2,1)}, bf16[512,1024]{1,0:T(8,128)(2,1)}, u32[]{:S(2)}, u32[]{:S(2)}) collective-permute-start(bf16[512,1024]{1,0:T(8,128)(2,1)} %collective-permute-done.12), channel_id=1, source_target_pairs={{1,0},{5,4},{9,8},{13,12},{17,16},{21,20},{25,24},{29,28}} | collective-permute-start | bytes 3145736 | tf_op jit(solution)/shard_map/ppermute | solution.py:557
  124.9 34.5 %collective-permute-start.10 = (bf16[512,1024]{1,0:T(8,128)(2,1)}, bf16[512,1024]{1,0:T(8,128)(2,1)}, u32[]{:S(2)}, u32[]{:S(2)}) collective-permute-start(bf16[512,1024]{1,0:T(8,128)(2,1)} %collective-permute-done.9), channel_id=1, source_target_pairs={{2,3},{6,7},{10,11},{14,15},{18,19},{22,23},{26,27},{30,31}} | collective-permute-start | bytes 3145736 | tf_op jit(solution)/shard_map/ppermute | solution.py:556
  132.7 38.9 %all-to-all-start.1 = ((bf16[4,256,512]{2,1,0:T(8,128)(2,1)}), bf16[4,256,512]{2,1,0:T(8,128)(2,1)}, u32[]{:S(2)}, u32[]{:S(2)}) async-start(bf16[4,256,512]{2,1,0:T(8,128)(2,1)} %pad_maximum_fusion.5), calls=%async_computation.1 | async-start | bytes 2097152 | tf_op jit(solution)/shard_map/all_to_all | solution.py:641
  192.9 20.6 %all-to-all-start.2 = ((bf16[4,512,256]{2,1,0:T(8,128)(2,1)}), bf16[4,512,256]{2,1,0:T(8,128)(2,1)S(1)}, u32[]{:S(2)}, u32[]{:S(2)}) async-start(bf16[4,512,256]{2,1,0:T(8,128)(2,1)} %bitcast.8), calls=%async_computation.2 | async-start | bytes 2097152 | tf_op jit(solution)/shard_map/all_to_all | solution.py:647
  197.6 200.7 %reduce-scatter.3.cloned.1.call-start = ((), (), s32[]{:S(2)}) async-start(), calls=%async_computation.11 | async-start | bytes 21823488 | tf_op jit(solution)/shard_map/reduce_scatter | solution.py:654
  260.8 19.5 %all-to-all-start.3 = ((bf16[512,4,256]{2,0,1:T(8,128)(2,1)}), bf16[512,4,256]{2,0,1:T(8,128)(2,1)S(1)}, u32[]{:S(2)}, u32[]{:S(2)}) async-start(bf16[512,4,256]{2,0,1:T(8,128)(2,1)} %bitcast.91), calls=%async_computation.3 | async-start | bytes 2097152 | tf_op jit(solution)/shard_map/all_to_all | solution.py:653
  264.4 198.5 %reduce-scatter.5.cloned.1.call-start = ((), (), s32[]{:S(2)}) async-start(), calls=%async_computation.12 | async-start | bytes 3031040 | tf_op jit(solution)/shard_map/reduce_scatter | solution.py:701
  315.7 23.5 %collective-permute-start.18 = (bf16[512,1024]{1,0:T(8,128)(2,1)S(1)}, bf16[512,1024]{1,0:T(8,128)(2,1)S(1)}, u32[]{:S(2)}, u32[]{:S(2)}) collective-permute-start(bf16[512,1024]{1,0:T(8,128)(2,1)S(1)} %get-tuple-element.72), channel_id=1, source_target_pairs={{0,1},{4,5},{8,9},{12,13},{16,17},{20,21},{24,25},{28,29}} | collective-permute-start | bytes 3145736 | tf_op jit(solution)/shard_map/ppermute | solution.py:593
  317.1 22.2 %collective-permute-start.19 = (bf16[512,1024]{1,0:T(8,128)(2,1)S(1)}, bf16[512,1024]{1,0:T(8,128)(2,1)}, u32[]{:S(2)}, u32[]{:S(2)}) collective-permute-start(bf16[512,1024]{1,0:T(8,128)(2,1)S(1)} %get-tuple-element.73), channel_id=1, source_target_pairs={{3,2},{7,6},{11,10},{15,14},{19,18},{23,22},{27,26},{31,30}} | collective-permute-start | bytes 3145736 | tf_op jit(solution)/shard_map/ppermute | solution.py:594
  343.1 27.3 %collective-permute-start.20 = (bf16[512,1024]{1,0:T(8,128)(2,1)}, bf16[512,1024]{1,0:T(8,128)(2,1)S(1)}, u32[]{:S(2)}, u32[]{:S(2)}) collective-permute-start(bf16[512,1024]{1,0:T(8,128)(2,1)} %get-tuple-element.76), channel_id=1, source_target_pairs={{0,1},{1,2},{4,5},{5,6},{8,9},{9,10},{12,13},{13,14},{16,17},{17,1... | collective-permute-start | bytes 3145736 | tf_op jit(solution)/shard_map/ppermute | solution.py:593
  347.6 22.8 %collective-permute-start.21 = (bf16[512,1024]{1,0:T(8,128)(2,1)S(1)}, bf16[512,1024]{1,0:T(8,128)(2,1)S(1)}, u32[]{:S(2)}, u32[]{:S(2)}) collective-permute-start(bf16[512,1024]{1,0:T(8,128)(2,1)S(1)} %get-tuple-element.77), channel_id=1, source_target_pairs={{2,1},{3,2},{6,5},{7,6},{10,9},{11,10},{14,13},{15,14},{18,17},{19... | collective-permute-start | bytes 3145736 | tf_op jit(solution)/shard_map/ppermute | solution.py:594
  372.9 19.9 %collective-permute-start.22 = (bf16[512,1024]{1,0:T(8,128)(2,1)S(1)}, bf16[512,1024]{1,0:T(8,128)(2,1)}, u32[]{:S(2)}, u32[]{:S(2)}) collective-permute-start(bf16[512,1024]{1,0:T(8,128)(2,1)S(1)} %get-tuple-element.80), channel_id=1, source_target_pairs={{0,1},{1,2},{2,3},{4,5},{5,6},{6,7},{8,9},{9,10},{10,11},{12,13},{... | collective-permute-start | bytes 3145736 | tf_op jit(solution)/shard_map/ppermute | solution.py:593
  434.9 18.8 %all-to-all-start.5 = ((bf16[4,40,768]{2,1,0:T(8,128)(2,1)}), bf16[4,40,768]{2,1,0:T(8,128)(2,1)S(1)}, u32[]{:S(2)}, u32[]{:S(2)}) async-start(bf16[4,40,768]{2,1,0:T(8,128)(2,1)} %fusion.12), calls=%async_computation.5 | async-start | bytes 491520 | tf_op jit(solution)/shard_map/all_to_all | solution.py:675
  (26 other events, 263.8 us)
Sparse Core Ops, SparseCore 0:
  39.3 27.3 all-gather.3
  75.4 41.5 all-gather.7
  118.9 76.5 all-gather.5
  258.7 127.6 reduce-scatter.2
  403.0 51.1 reduce-scatter.4

commit v10 on v9

--- a/solution.py
+++ b/solution.py
@@ -575,6 +575,20 @@
     return results, steps
 
 
+def shift_gather(block, axis, meanwhile):
+    size = lax.axis_size(axis)
+    place = lax.axis_index(axis)
+    taken = [block]
+    for far in range(1, size):
+        taken.append(lax.ppermute(block, axis, [(i, (i + far) % size) for i in range(size)]))
+    taken = after(taken, meanwhile)
+    ordered = []
+    for index in range(size):
+        cases = [taken[(mine - index) % size] for mine in range(size)]
+        ordered.append(lax.select_n(place, *cases) if size > 2 else lax.select_n(place > 0, *cases))
+    return ordered
+
+
 def chain_scatter(partial, axis):
     size = lax.axis_size(axis)
     place = lax.axis_index(axis)
@@ -626,23 +640,26 @@
     picks = parcel[:, share + 1, : choices.shape[0]].astype(jnp.int32).reshape(ring, 2, -1)
     chosen_all, counts_all = picks[:, 0].reshape(-1), picks[:, 1].reshape(-1)
     shards = jnp.concatenate([w_out, w_gate, w_up], 1)
-    (near, near_down), steps = chain_gather((shards, w_down), "fsdp")
-    (gathered,), token_steps = chain_gather((after(mine, steps[-2]),), "fsdp")
-    parcel = lax.all_gather(after(parcel, steps[0]), DP, axis=0, tiled=True)
+    (near,), steps = chain_gather((shards,), "fsdp")
+    (gathered,), token_steps = chain_gather((after(mine, steps[-1]),), "fsdp")
+    parcel = lax.all_gather(parcel, DP, axis=0, tiled=True)
     w_qkv = parcel[:, :share].reshape(width, 3 * wide)
     gain_one = parcel[:, share, :share].reshape(1, width).astype(F32)
     gain_two = parcel[:, share, share : 2 * share].reshape(1, width).astype(F32)
-    first = lax.all_gather(jnp.concatenate(near, 0), DP, axis=0, tiled=True)
+    first = lax.all_gather(after(jnp.concatenate(near, 0), parcel), DP, axis=0, tiled=True)
     gathered = jnp.concatenate(gathered, 0)
 
     memory = jnp.concatenate(
         [m[0].reshape(-1, ring, wide).transpose(1, 0, 2) for m in (memory_keys, memory_values)], 2
     )
     memory = lax.all_to_all(after(memory, token_steps[-2]), "fsdp", 0, 0, tiled=True).reshape(-1, 2 * wide)
-    down_full = lax.all_gather(jnp.concatenate(near_down, 0), DP, axis=0, tiled=True)
 
     cosine, sine = rotary_tables(length)
     qkv = project_qkv(gathered, gain_one, w_qkv, cosine, sine, heads)
+    near_down = jnp.concatenate(shift_gather(after(w_down, (token_steps[-1], memory)), "fsdp", qkv), 0)
+    near_down = after(near_down, first)
+    down_full = lax.all_gather(near_down, DP, axis=0, tiled=True)
+    qkv = after(qkv, near_down)
     attended_heads, lse = attend_forward(chosen_all, counts_all, qkv, memory, heads, top)
     attended = lax.all_to_all(attended_heads, "fsdp", 0, 1, tiled=True)
 
@@ -698,7 +715,8 @@
     inner = jnp.mean(scaled * own, -1, keepdims=True)
     tokens_grad = (grad_middle + factor * scaled - own * (factor * factor * factor * inner)).astype(BF16)
 
-    pieces = lax.psum_scatter(pieces, "fsdp", scatter_dimension=0, tiled=True)[0].astype(F32)
+    pieces = lax.psum_scatter(pieces, "fsdp", scatter_dimension=0, tiled=True)
+    pieces = after(pieces, (tokens_grad, projections, gain_shares))[0].astype(F32)
     down_share = pieces[: lanes * tall].reshape(lanes, tall, strip).transpose(1, 0, 2).reshape(tall, width)
     others = pieces[lanes * tall :].reshape(-1, share, strip).transpose(1, 0, 2).reshape(share, -1)
     return (

time: 482 us -> 498 us (1.033)
  waiting for transfers between devices: 190 us -> 210 us
    all_to_all x1, waiting for transfers between devices: 15.6 us -> 25.9 us  [body(): grad_heads = lax.all_to_all(grad_attended, 'fsdp', 1, 0, tiled=True)]
    ppermute x9 -> x6, starting transfers between devices: 21.1 us -> 13.9 us  [chain_gather(): rising = tuple((lax.ppermute(block, axis, up) for block in rising))]
    ppermute x0 -> x3, starting transfers between devices: none -> 6.94 us  [shift_gather(): lax.ppermute(block, axis, [(i, (i + far) % size) for i in range(size)])]
    ppermute x3, waiting for transfers between devices: 52.3 us -> 58.3 us  [chain_scatter(): rising = lax.ppermute(up, axis, [(i, i + 1) for i in range(step + 1)])]
    ppermute x9 -> x6, starting transfers between devices: 11.6 us -> 7.69 us  [chain_gather(): falling = tuple((lax.ppermute(block, axis, down) for block in falling))]
    ppermute x9 -> x6, waiting for transfers between devices: 81.3 us -> 84.1 us  [chain_gather(): falling = tuple((lax.ppermute(block, axis, down) for block in falling))]
  transfers between devices with their start and end apart: 35 -> 32, of which waited for: 15 -> 16; matrix products, arithmetic and copies ran while one was open for 11% -> 9% of each run, Pallas kernels for 15% -> 14%
where the time goes in v10:
time: 498 us; the launch traced here: 490 us
  waiting for transfers between devices  210 us (42%)
  Pallas kernels  113 us (23%)
  starting transfers between devices  70.8 us (14%)
  other arithmetic  36 us (7%)
  local copies, waits for them, and re-layouts  29.7 us (6%)
  blocking collectives  15.3 us (3%)
  between operations  14.8 us (3%)
    ppermute x6, waiting for transfers between devices, chain_gather(): falling = tuple((lax.ppermute(block, axis, down) for block in falling))  84.1 us
    ppermute x3, waiting for transfers between devices, chain_scatter(): rising = lax.ppermute(up, axis, [(i, i + 1) for i in range(step + 1)])  58.3 us
    pallas_call x1, Pallas kernels, feed_forward(): pl.pallas_call(functools.partial(ffn_kernel, span, merged), grid=(steps,)...  43.8 us
    pallas_call x1, Pallas kernels, attend_backward(): pl.pallas_call(functools.partial(backward_kernel, heads, top), grid_spec=...  32.6 us
    all_to_all x1, waiting for transfers between devices, body(): grad_heads = lax.all_to_all(grad_attended, 'fsdp', 1, 0, tiled=True)  25.9 us
    pallas_call x1, Pallas kernels, attend_forward(): pl.pallas_call(functools.partial(forward_kernel, heads, top), grid_spec=p...  21.4 us
    all_to_all x1, waiting for transfers between devices, body(): late = lax.all_to_all(late, 'fsdp', 0, 0, tiled=True).astype(F32)  15.3 us
    all_to_all x1, blocking collectives, body(): lax.all_to_all(late, 'chip', 0, 0, tiled=True).astype(F32)  15.3 us
  transfers between devices with their start and end apart: 32, of which 16 were waited for; matrix products, arithmetic and copies ran while one was open for 9% of the time, Pallas kernels for 14%

profile of v10, /device:TPU:0, one launch (start us, length us, event | category | flops | bytes accessed | tf_op | source)
XLA Modules:
  0.0 489.7 jit_solution(6673910303319939147)
XLA Ops:
  13.1 6.3 %all-to-all-start = ((bf16[4,40,768]{2,1,0:T(8,128)(2,1)}), bf16[4,40,768]{2,1,0:T(8,128)(2,1)S(1)}, u32[]{:S(2)}, u32[]{:S(2)}) async-start(bf16[4,40,768]{2,1,0:T(8,128)(2,1)} %copy.71), calls=%async_computation | async-start | bytes 491520 | tf_op jit(solution)/shard_map/all_to_all | solution.py:639
  29.8 5.8 %collective-permute-done.3 = bf16[32,6656]{1,0:T(8,128)(2,1)S(1)} collective-permute-done((bf16[32,6656]{1,0:T(8,128)(2,1)S(1)}, bf16[32,6656]{1,0:T(8,128)(2,1)S(1)}, u32[]{:S(2)}, u32[]{:S(2)}) %collective-permute-start.3) | collective-permute-done | bytes 426016 | tf_op jit(solution)/shard_map/ppermute | solution.py:557
  37.6 11.3 %collective-permute-done.4 = bf16[32,6656]{1,0:T(8,128)(2,1)S(1)} collective-permute-done((bf16[32,6656]{1,0:T(8,128)(2,1)S(1)}, bf16[32,6656]{1,0:T(8,128)(2,1)S(1)}, u32[]{:S(2)}, u32[]{:S(2)}) %collective-permute-start.4) | collective-permute-done | bytes 426016 | tf_op jit(solution)/shard_map/ppermute | solution.py:557
  51.0 10.3 %collective-permute-done.5 = bf16[32,6656]{1,0:T(8,128)(2,1)S(1)} collective-permute-done((bf16[32,6656]{1,0:T(8,128)(2,1)S(1)}, bf16[32,6656]{1,0:T(8,128)(2,1)S(1)}, u32[]{:S(2)}, u32[]{:S(2)}) %collective-permute-start.5) | collective-permute-done | bytes 426016 | tf_op jit(solution)/shard_map/ppermute | solution.py:557
  64.4 4.6 collective-permute-start.6
  69.1 18.9 %collective-permute-done.9 = bf16[512,1024]{1,0:T(8,128)(2,1)S(1)} collective-permute-done((bf16[512,1024]{1,0:T(8,128)(2,1)S(1)}, bf16[512,1024]{1,0:T(8,128)(2,1)S(1)}, u32[]{:S(2)}, u32[]{:S(2)}) %collective-permute-start.9) | collective-permute-done | bytes 1048608 | tf_op jit(solution)/shard_map/ppermute | solution.py:557
  95.0 17.0 %collective-permute-done.10 = bf16[512,1024]{1,0:T(8,128)(2,1)} collective-permute-done((bf16[512,1024]{1,0:T(8,128)(2,1)S(1)}, bf16[512,1024]{1,0:T(8,128)(2,1)}, u32[]{:S(2)}, u32[]{:S(2)}) %collective-permute-start.10) | collective-permute-done | bytes 1048608 | tf_op jit(solution)/shard_map/ppermute | solution.py:557
  115.0 5.6 %all-to-all-start.1 = ((bf16[4,256,512]{2,1,0:T(8,128)(2,1)}), bf16[4,256,512]{2,1,0:T(8,128)(2,1)}, u32[]{:S(2)}, u32[]{:S(2)}) async-start(bf16[4,256,512]{2,1,0:T(8,128)(2,1)} %pad_maximum_fusion.5), calls=%async_computation.1 | async-start | bytes 2097152 | tf_op jit(solution)/shard_map/all_to_all | solution.py:655
  128.5 20.8 %collective-permute-done.11 = bf16[512,1024]{1,0:T(8,128)(2,1)} collective-permute-done((bf16[512,1024]{1,0:T(8,128)(2,1)}, bf16[512,1024]{1,0:T(8,128)(2,1)}, u32[]{:S(2)}, u32[]{:S(2)}) %collective-permute-start.11) | collective-permute-done | bytes 1048608 | tf_op jit(solution)/shard_map/ppermute | solution.py:557
  154.7 6.2 %collective-permute-start.14 = (bf16[88,1024]{1,0:T(8,128)(2,1)S(1)}, bf16[88,1024]{1,0:T(8,128)(2,1)S(1)}, u32[]{:S(2)}, u32[]{:S(2)}) collective-permute-start(bf16[88,1024]{1,0:T(8,128)(2,1)S(1)} %copy-done.11), channel_id=1, source_target_pairs={{0,3},{1,0},{2,1},{3,2},{4,7},{5,4},{6,5},{7,6},{8,11},{9,8},{10,9... | collective-permute-start | bytes 540680 | tf_op jit(solution)/shard_map/ppermute | solution.py:583
  162.9 7.5 %project_qkv.1.q_ref.k_ref.v_ref = bf16[2048,768]{1,0:T(8,128)(2,1)} custom-call(bf16[2048,1024]{1,0:T(8,128)(2,1)} %pad_maximum_fusion.tok_ref, f32[1,1024]{1,0:T(1,128)S(1)} %reshape.191.gain_ref, bf16[1024,768]{1,0:T(8,128)(2,1)S(1)} %bitcast.80, f32[2048,128]{1,0:T(8,128)S(1)} %get-tuple-element.119.cos_ref, f32[2048,128]{1,0:T(8,128)S(1)} %copy-done.2), custom_call_target="tpu_custom_call" | custom-call | flops 3221225472 | bytes 14680064 | tf_op jit(solution)/shard_map/project_qkv/pallas_call | solution.py:62
  172.4 21.4 %attend_forward.1 = (bf16[2048,256]{1,0:T(8,128)(2,1)}, f32[2048,2]{1,0:T(8,128)S(1)}) custom-call(s32[32]{0:T(128)S(1)} %reshape_squeeze.24.chosen_ref, s32[32]{0:T(128)S(1)} %reshape_squeeze.25.counts_ref, bf16[2048,768]{1,0:T(8,128)(2,1)} %project_qkv.1.q_ref.k_ref.v_ref, bf16[2048,768]{1,0:T(8,128)(2,1)} %project_qkv.1.q_ref.k_ref.v_ref, ...), custom_call_target="tpu_custom_call" | custom-call | flops 3221225472 | bytes 4194304 | tf_op jit(solution)/shard_map/attend_forward/pallas_call | solution.py:157
  198.9 15.2 %all-to-all-done.2 = bf16[4,512,256]{2,1,0:T(8,128)(2,1)S(1)} async-done(((bf16[4,512,256]{2,1,0:T(8,128)(2,1)}), bf16[4,512,256]{2,1,0:T(8,128)(2,1)S(1)}, u32[]{:S(2)}, u32[]{:S(2)}) %all-to-all-start.2) | async-done | bytes 1048608 | tf_op jit(solution)/shard_map/all_to_all | solution.py:664
  215.8 43.8 %feed_forward.1 = (bf16[512,1024]{1,0:T(8,128)(2,1)}, f32[512,1024]{1,0:T(8,128)}, bf16[512,1024]{1,0:T(8,128)(2,1)}, f32[1,1024]{1,0:T(1,128)}, bf16[8,4736,256]{2,1,0:T(8,128)(2,1)}) custom-call(bf16[512,1024]{1,0:T(8,128)(2,1)} %bitcast.85, bf16[512,1024]{1,0:T(8,128)(2,1)} %bitcast.101, bf16[512,1024]{1,0:T(8,128)(2,1)} %bitcast.118, ...), custom_call_target="tpu_custom_call" | custom-call | flops 29796335616 | bytes 38797312 | tf_op jit(solution)/shard_map/feed_forward/pallas_call | solution.py:458
  266.7 25.9 %all-to-all-done.3 = bf16[512,4,256]{2,0,1:T(8,128)(2,1)S(1)} async-done(((bf16[512,4,256]{2,0,1:T(8,128)(2,1)}), bf16[512,4,256]{2,0,1:T(8,128)(2,1)S(1)}, u32[]{:S(2)}, u32[]{:S(2)}) %all-to-all-start.3) | async-done | bytes 1048608 | tf_op jit(solution)/shard_map/all_to_all | solution.py:670
  292.6 32.6 %attend_backward.1 = (bf16[2048,1024]{1,0:T(8,128)(2,1)}, bf16[2048,768]{1,0:T(8,128)(2,1)}) custom-call(s32[32]{0:T(128)S(1)} %reshape_squeeze.24.chosen_ref, s32[32]{0:T(128)S(1)} %reshape_squeeze.25.counts_ref, bf16[2048,768]{1,0:T(8,128)(2,1)} %project_qkv.1.q_ref.k_ref.v_ref, bf16[2048,768]{1,0:T(8,128)(2,1)} %project_qkv.1.q_ref.k_ref.v_ref, ...), custom_call_target="tpu_custom_call" | custom-call | flops 8053063680 | bytes 8388608 | tf_op jit(solution)/shard_map/attend_backward/pallas_call | solution.py:279
  329.9 20.3 %collective-permute-done.15 = bf16[512,1024]{1,0:T(8,128)(2,1)S(1)} collective-permute-done((bf16[512,1024]{1,0:T(8,128)(2,1)S(1)}, bf16[512,1024]{1,0:T(8,128)(2,1)S(1)}, u32[]{:S(2)}, u32[]{:S(2)}) %collective-permute-start.15) | collective-permute-done | bytes 1048608 | tf_op jit(solution)/shard_map/ppermute | solution.py:607
  359.2 20.7 %collective-permute-done.17 = bf16[512,1024]{1,0:T(8,128)(2,1)S(1)} collective-permute-done((bf16[512,1024]{1,0:T(8,128)(2,1)}, bf16[512,1024]{1,0:T(8,128)(2,1)S(1)}, u32[]{:S(2)}, u32[]{:S(2)}) %collective-permute-start.17) | collective-permute-done | bytes 1048608 | tf_op jit(solution)/shard_map/ppermute | solution.py:607
  382.4 7.9 %collective-permute-start.19 = (bf16[512,1024]{1,0:T(8,128)(2,1)S(1)}, bf16[512,1024]{1,0:T(8,128)(2,1)}, u32[]{:S(2)}, u32[]{:S(2)}) collective-permute-start(bf16[512,1024]{1,0:T(8,128)(2,1)S(1)} %get-tuple-element.71), channel_id=1, source_target_pairs={{0,1},{1,2},{2,3},{4,5},{5,6},{6,7},{8,9},{9,10},{10,11},{12,13},{... | collective-permute-start | bytes 3145736 | tf_op jit(solution)/shard_map/ppermute | solution.py:607
  391.8 17.4 %collective-permute-done.19 = bf16[512,1024]{1,0:T(8,128)(2,1)} collective-permute-done((bf16[512,1024]{1,0:T(8,128)(2,1)S(1)}, bf16[512,1024]{1,0:T(8,128)(2,1)}, u32[]{:S(2)}, u32[]{:S(2)}) %collective-permute-start.19) | collective-permute-done | bytes 1048608 | tf_op jit(solution)/shard_map/ppermute | solution.py:607
  409.2 5.2 %collective-permute-done.20 = bf16[512,1024]{1,0:T(8,128)(2,1)} collective-permute-done((bf16[512,1024]{1,0:T(8,128)(2,1)S(1)}, bf16[512,1024]{1,0:T(8,128)(2,1)}, u32[]{:S(2)}, u32[]{:S(2)}) %collective-permute-start.20) | collective-permute-done | bytes 1048608 | tf_op jit(solution)/shard_map/ppermute | solution.py:608
  422.3 7.8 %projection_grads.1 = (bf16[1024,768]{1,0:T(8,128)(2,1)S(1)}, f32[1024,1]{1,0:T(8,128)S(1)}) custom-call(bf16[2048,1024]{1,0:T(8,128)(2,1)} %pad_maximum_fusion.tok_ref, f32[1024,1]{1,0:T(8,128)S(1)} %copy-done.3, bf16[1024,768]{1,0:T(8,128)(2,1)S(1)} %bitcast.82, bf16[2048,768]{1,0:T(8,128)(2,1)} %get-tuple-element.75.grad_ref), custom_call_target="tpu_custom_call" | custom-call | flops 3221225472 | bytes 7340032 | tf_op jit(solution)/shard_map/projection_grads/pallas_call | solution.py:518
  434.1 15.3 %all_to_all.58 = bf16[4,136,768]{2,1,0:T(8,128)(2,1)S(1)} all-to-all(bf16[4,136,768]{2,1,0:T(8,128)(2,1)S(1)} %fusion.4), channel_id=1, replica_groups=mesh['chip'=4,'core'=2,'fsdp'=4] {'chip'}, dimensions={0} | all-to-all | bytes 1671168 | tf_op jit(solution)/shard_map/all_to_all | solution.py:688
  453.8 15.3 %all-to-all-done.5 = bf16[4,40,768]{2,1,0:T(8,128)(2,1)S(1)} async-done(((bf16[4,40,768]{2,1,0:T(8,128)(2,1)}), bf16[4,40,768]{2,1,0:T(8,128)(2,1)S(1)}, u32[]{:S(2)}, u32[]{:S(2)}) %all-to-all-start.5) | async-done | bytes 245792 | tf_op jit(solution)/shard_map/all_to_all | solution.py:692
  (164 shorter events, 111.9 us)
Async XLA Ops:
  13.1 15.9 %all-to-all-start = ((bf16[4,40,768]{2,1,0:T(8,128)(2,1)}), bf16[4,40,768]{2,1,0:T(8,128)(2,1)S(1)}, u32[]{:S(2)}, u32[]{:S(2)}) async-start(bf16[4,40,768]{2,1,0:T(8,128)(2,1)} %copy.71), calls=%async_computation | async-start | bytes 491520 | tf_op jit(solution)/shard_map/all_to_all | solution.py:639
  19.5 43.4 %all-gather.4.cloned.1.call-start = ((), (), s32[]{:S(2)}) async-start(), calls=%async_computation.8 | async-start | bytes 2211840 | tf_op jit(solution)/shard_map/all_gather | solution.py:645
  20.4 15.3 %collective-permute-start.3 = (bf16[32,6656]{1,0:T(8,128)(2,1)S(1)}, bf16[32,6656]{1,0:T(8,128)(2,1)S(1)}, u32[]{:S(2)}, u32[]{:S(2)}) collective-permute-start(bf16[32,6656]{1,0:T(8,128)(2,1)S(1)} %constant_dynamic-update-slice_fusion), channel_id=1, source_target_pairs={{1,0},{2,1},{3,2},{5,4},{6,5},{7,6},{9,8},{10,9},{11,10},{13,12},{... | collective-permute-start | bytes 1277960 | tf_op jit(solution)/shard_map/ppermute | solution.py:557
  29.8 141.6 %all-gather.6.cloned.1.call-start = ((), (), s32[]{:S(2)}) async-start(), calls=%async_computation.9 | async-start | bytes 15335424 | tf_op jit(solution)/shard_map/all_gather | solution.py:649
  63.2 24.8 %collective-permute-start.9 = (bf16[512,1024]{1,0:T(8,128)(2,1)S(1)}, bf16[512,1024]{1,0:T(8,128)(2,1)S(1)}, u32[]{:S(2)}, u32[]{:S(2)}) collective-permute-start(bf16[512,1024]{1,0:T(8,128)(2,1)S(1)} %bitcast.86), channel_id=1, source_target_pairs={{1,0},{2,1},{3,2},{5,4},{6,5},{7,6},{9,8},{10,9},{11,10},{13,12},{... | collective-permute-start | bytes 3145736 | tf_op jit(solution)/shard_map/ppermute | solution.py:557
  64.4 24.8 %collective-permute-start.6 = (bf16[512,1024]{1,0:T(8,128)(2,1)S(1)}, bf16[512,1024]{1,0:T(8,128)(2,1)S(1)}, u32[]{:S(2)}, u32[]{:S(2)}) collective-permute-start(bf16[512,1024]{1,0:T(8,128)(2,1)S(1)} %bitcast.87), channel_id=1, source_target_pairs={{0,1},{1,2},{2,3},{4,5},{5,6},{6,7},{8,9},{9,10},{10,11},{12,13},{... | collective-permute-start | bytes 3145736 | tf_op jit(solution)/shard_map/ppermute | solution.py:556
  87.9 24.1 %collective-permute-start.10 = (bf16[512,1024]{1,0:T(8,128)(2,1)S(1)}, bf16[512,1024]{1,0:T(8,128)(2,1)}, u32[]{:S(2)}, u32[]{:S(2)}) collective-permute-start(bf16[512,1024]{1,0:T(8,128)(2,1)S(1)} %collective-permute-done.9), channel_id=1, source_target_pairs={{1,0},{2,1},{5,4},{6,5},{9,8},{10,9},{13,12},{14,13},{17,16},{18,1... | collective-permute-start | bytes 3145736 | tf_op jit(solution)/shard_map/ppermute | solution.py:557
  89.2 24.0 %collective-permute-start.7 = (bf16[512,1024]{1,0:T(8,128)(2,1)S(1)}, bf16[512,1024]{1,0:T(8,128)(2,1)}, u32[]{:S(2)}, u32[]{:S(2)}) collective-permute-start(bf16[512,1024]{1,0:T(8,128)(2,1)S(1)} %collective-permute-done.6), channel_id=1, source_target_pairs={{1,2},{2,3},{5,6},{6,7},{9,10},{10,11},{13,14},{14,15},{17,18},{18... | collective-permute-start | bytes 3145736 | tf_op jit(solution)/shard_map/ppermute | solution.py:556
  112.0 37.4 %collective-permute-start.11 = (bf16[512,1024]{1,0:T(8,128)(2,1)}, bf16[512,1024]{1,0:T(8,128)(2,1)}, u32[]{:S(2)}, u32[]{:S(2)}) collective-permute-start(bf16[512,1024]{1,0:T(8,128)(2,1)} %collective-permute-done.10), channel_id=1, source_target_pairs={{1,0},{5,4},{9,8},{13,12},{17,16},{21,20},{25,24},{29,28}} | collective-permute-start | bytes 3145736 | tf_op jit(solution)/shard_map/ppermute | solution.py:557
  113.3 36.1 %collective-permute-start.8 = (bf16[512,1024]{1,0:T(8,128)(2,1)}, bf16[512,1024]{1,0:T(8,128)(2,1)}, u32[]{:S(2)}, u32[]{:S(2)}) collective-permute-start(bf16[512,1024]{1,0:T(8,128)(2,1)} %collective-permute-done.7), channel_id=1, source_target_pairs={{2,3},{6,7},{10,11},{14,15},{18,19},{22,23},{26,27},{30,31}} | collective-permute-start | bytes 3145736 | tf_op jit(solution)/shard_map/ppermute | solution.py:556
  115.0 39.7 %all-to-all-start.1 = ((bf16[4,256,512]{2,1,0:T(8,128)(2,1)}), bf16[4,256,512]{2,1,0:T(8,128)(2,1)}, u32[]{:S(2)}, u32[]{:S(2)}) async-start(bf16[4,256,512]{2,1,0:T(8,128)(2,1)} %pad_maximum_fusion.5), calls=%async_computation.1 | async-start | bytes 2097152 | tf_op jit(solution)/shard_map/all_to_all | solution.py:655
  120.5 95.2 %all-gather.8.cloned.1.call-start = ((), (), s32[]{:S(2)}) async-start(), calls=%async_computation.10 | async-start | bytes 6488064 | tf_op jit(solution)/shard_map/all_gather | solution.py:661
  154.7 15.6 %collective-permute-start.14 = (bf16[88,1024]{1,0:T(8,128)(2,1)S(1)}, bf16[88,1024]{1,0:T(8,128)(2,1)S(1)}, u32[]{:S(2)}, u32[]{:S(2)}) collective-permute-start(bf16[88,1024]{1,0:T(8,128)(2,1)S(1)} %copy-done.11), channel_id=1, source_target_pairs={{0,3},{1,0},{2,1},{3,2},{4,7},{5,4},{6,5},{7,6},{8,11},{9,8},{10,9... | collective-permute-start | bytes 540680 | tf_op jit(solution)/shard_map/ppermute | solution.py:583
  193.7 20.4 %all-to-all-start.2 = ((bf16[4,512,256]{2,1,0:T(8,128)(2,1)}), bf16[4,512,256]{2,1,0:T(8,128)(2,1)S(1)}, u32[]{:S(2)}, u32[]{:S(2)}) async-start(bf16[4,512,256]{2,1,0:T(8,128)(2,1)} %bitcast.8), calls=%async_computation.2 | async-start | bytes 2097152 | tf_op jit(solution)/shard_map/all_to_all | solution.py:664
  198.3 216.1 %reduce-scatter.3.cloned.1.call-start = ((), (), s32[]{:S(2)}) async-start(), calls=%async_computation.11 | async-start | bytes 21823488 | tf_op jit(solution)/shard_map/reduce_scatter | solution.py:671
  261.9 30.7 %all-to-all-start.3 = ((bf16[512,4,256]{2,0,1:T(8,128)(2,1)}), bf16[512,4,256]{2,0,1:T(8,128)(2,1)S(1)}, u32[]{:S(2)}, u32[]{:S(2)}) async-start(bf16[512,4,256]{2,0,1:T(8,128)(2,1)} %bitcast.90), calls=%async_computation.3 | async-start | bytes 2097152 | tf_op jit(solution)/shard_map/all_to_all | solution.py:670
  266.5 211.8 %reduce-scatter.5.cloned.1.call-start = ((), (), s32[]{:S(2)}) async-start(), calls=%async_computation.12 | async-start | bytes 3031040 | tf_op jit(solution)/shard_map/reduce_scatter | solution.py:718
  326.9 23.3 %collective-permute-start.15 = (bf16[512,1024]{1,0:T(8,128)(2,1)S(1)}, bf16[512,1024]{1,0:T(8,128)(2,1)S(1)}, u32[]{:S(2)}, u32[]{:S(2)}) collective-permute-start(bf16[512,1024]{1,0:T(8,128)(2,1)S(1)} %get-tuple-element.63), channel_id=1, source_target_pairs={{0,1},{4,5},{8,9},{12,13},{16,17},{20,21},{24,25},{28,29}} | collective-permute-start | bytes 3145736 | tf_op jit(solution)/shard_map/ppermute | solution.py:607
  328.3 21.9 %collective-permute-start.16 = (bf16[512,1024]{1,0:T(8,128)(2,1)S(1)}, bf16[512,1024]{1,0:T(8,128)(2,1)}, u32[]{:S(2)}, u32[]{:S(2)}) collective-permute-start(bf16[512,1024]{1,0:T(8,128)(2,1)S(1)} %get-tuple-element.64), channel_id=1, source_target_pairs={{3,2},{7,6},{11,10},{15,14},{19,18},{23,22},{27,26},{31,30}} | collective-permute-start | bytes 3145736 | tf_op jit(solution)/shard_map/ppermute | solution.py:608
  354.0 25.9 %collective-permute-start.17 = (bf16[512,1024]{1,0:T(8,128)(2,1)}, bf16[512,1024]{1,0:T(8,128)(2,1)S(1)}, u32[]{:S(2)}, u32[]{:S(2)}) collective-permute-start(bf16[512,1024]{1,0:T(8,128)(2,1)} %get-tuple-element.67), channel_id=1, source_target_pairs={{0,1},{1,2},{4,5},{5,6},{8,9},{9,10},{12,13},{13,14},{16,17},{17,1... | collective-permute-start | bytes 3145736 | tf_op jit(solution)/shard_map/ppermute | solution.py:607
  358.4 21.4 %collective-permute-start.18 = (bf16[512,1024]{1,0:T(8,128)(2,1)S(1)}, bf16[512,1024]{1,0:T(8,128)(2,1)S(1)}, u32[]{:S(2)}, u32[]{:S(2)}) collective-permute-start(bf16[512,1024]{1,0:T(8,128)(2,1)S(1)} %get-tuple-element.68), channel_id=1, source_target_pairs={{2,1},{3,2},{6,5},{7,6},{10,9},{11,10},{14,13},{15,14},{18,17},{19... | collective-permute-start | bytes 3145736 | tf_op jit(solution)/shard_map/ppermute | solution.py:608
  382.4 26.8 %collective-permute-start.19 = (bf16[512,1024]{1,0:T(8,128)(2,1)S(1)}, bf16[512,1024]{1,0:T(8,128)(2,1)}, u32[]{:S(2)}, u32[]{:S(2)}) collective-permute-start(bf16[512,1024]{1,0:T(8,128)(2,1)S(1)} %get-tuple-element.71), channel_id=1, source_target_pairs={{0,1},{1,2},{2,3},{4,5},{5,6},{6,7},{8,9},{9,10},{10,11},{12,13},{... | collective-permute-start | bytes 3145736 | tf_op jit(solution)/shard_map/ppermute | solution.py:607
  390.3 24.1 %collective-permute-start.20 = (bf16[512,1024]{1,0:T(8,128)(2,1)S(1)}, bf16[512,1024]{1,0:T(8,128)(2,1)}, u32[]{:S(2)}, u32[]{:S(2)}) collective-permute-start(bf16[512,1024]{1,0:T(8,128)(2,1)S(1)} %get-tuple-element.72), channel_id=1, source_target_pairs={{1,0},{2,1},{3,2},{5,4},{6,5},{7,6},{9,8},{10,9},{11,10},{13,12},{... | collective-permute-start | bytes 3145736 | tf_op jit(solution)/shard_map/ppermute | solution.py:608
  450.3 18.8 %all-to-all-start.5 = ((bf16[4,40,768]{2,1,0:T(8,128)(2,1)}), bf16[4,40,768]{2,1,0:T(8,128)(2,1)S(1)}, u32[]{:S(2)}, u32[]{:S(2)}) async-start(bf16[4,40,768]{2,1,0:T(8,128)(2,1)} %fusion.11), calls=%async_computation.5 | async-start | bytes 491520 | tf_op jit(solution)/shard_map/all_to_all | solution.py:692
  (23 other events, 194.7 us)
Sparse Core Ops, SparseCore 0:
  29.9 25.5 all-gather.3
  63.0 77.9 all-gather.5
  171.5 44.2 all-gather.7
  259.8 128.4 reduce-scatter.2
  419.0 50.4 reduce-scatter.4

commit v11 on v9

--- a/solution.py
+++ b/solution.py
@@ -97,35 +97,18 @@
     return jnp.concatenate(rows, 0)
 
 
-def forward_kernel(
-    heads, top, chosen_ref, counts_ref, q_ref, k_ref, v_ref, mk_ref, mv_ref, out_ref, lse_ref, acc_s, peak_s
-):
+def local_kernel(heads, q_ref, k_ref, v_ref, out_ref, lse_ref, acc_s, peak_s):
     block = pl.program_id(0)
     rows = q_ref.shape[0]
-    subs = rows // QBLK
     own = pl.ds(pl.multiple_of(block * rows, rows), rows)
     causal = lax.broadcasted_iota(jnp.int32, (rows, rows), 0) >= lax.broadcasted_iota(jnp.int32, (rows, rows), 1)
     ones = jnp.ones((rows, HEAD_DIM), BF16)
-    mem_ones = jnp.ones((top * MBLK, HEAD_DIM), BF16)
-    biases = [memory_bias(counts_ref, (block * subs + sub) * top, top, 1) for sub in range(subs)]
     for head in range(heads):
         columns = slice(head * HEAD_DIM, (head + 1) * HEAD_DIM)
-        remote = []
-        for sub in range(subs):
-            keys = pick_memory(mk_ref, chosen_ref, (block * subs + sub) * top, top, columns)
-            query = q_ref[sub * QBLK : (sub + 1) * QBLK, columns]
-            remote.append(dot(query, keys, NT) + biases[sub])
-        local = jnp.where(causal, dot(q_ref[:, columns], k_ref[own, columns], NT), NEGATIVE)
-        peak = jnp.max(local, -1, keepdims=True)
-        peak = jnp.maximum(peak, jnp.concatenate([jnp.max(r, -1, keepdims=True) for r in remote], 0))
+        scores = jnp.where(causal, dot(q_ref[:, columns], k_ref[own, columns], NT), NEGATIVE)
+        peak = jnp.max(scores, -1, keepdims=True)
         values = jnp.concatenate([v_ref[own, columns], ones], 1)
-        acc = dot(jnp.exp2(local - peak).astype(BF16), values)
-        more = []
-        for sub in range(subs):
-            values = pick_memory(mv_ref, chosen_ref, (block * subs + sub) * top, top, columns)
-            weights = jnp.exp2(remote[sub] - peak[sub * QBLK : (sub + 1) * QBLK]).astype(BF16)
-            more.append(dot(weights, jnp.concatenate([values, mem_ones], 1)))
-        acc_s[head] = acc + jnp.concatenate(more, 0)
+        acc_s[head] = dot(jnp.exp2(scores - peak).astype(BF16), values)
         peak_s[head] = jnp.broadcast_to(peak, (rows, HEAD_DIM))
 
     def step(index, carry):
@@ -145,35 +128,88 @@
     for head in range(heads):
         columns = slice(head * HEAD_DIM, (head + 1) * HEAD_DIM)
         total = acc_s[head][:, HEAD_DIM:]
-        out_ref[:, columns] = (acc_s[head][:, :HEAD_DIM] / total).astype(BF16)
+        out_ref[:, columns] = acc_s[head][:, :HEAD_DIM] / total
         lse_ref[:, head : head + 1] = peak_s[head][:, :1] + jnp.log2(total[:, :1])
 
 
-def attend_forward(chosen, counts, qkv, memory, heads, top):
+def attend_local(qkv, heads):
+    length = qkv.shape[0]
+    wide = heads * HEAD_DIM
+    rows = min(2 * QBLK, length)
+    return pl.pallas_call(
+        functools.partial(local_kernel, heads),
+        grid=(length // rows,),
+        in_specs=[
+            pl.BlockSpec((rows, wide), lambda i: (i, 0)),
+            pl.BlockSpec((length, wide), lambda i: (0, 1)),
+            pl.BlockSpec((length, wide), lambda i: (0, 2)),
+        ],
+        out_specs=[
+            pl.BlockSpec((rows, wide), lambda i: (i, 0)),
+            pl.BlockSpec((rows, heads), lambda i: (i, 0)),
+        ],
+        out_shape=[
+            jax.ShapeDtypeStruct((length, wide), F32),
+            jax.ShapeDtypeStruct((length, heads), F32),
+        ],
+        scratch_shapes=[
+            pltpu.VMEM((heads, rows, 2 * HEAD_DIM), F32),
+            pltpu.VMEM((heads, rows, HEAD_DIM), F32),
+        ],
+        compiler_params=pltpu.CompilerParams(vmem_limit_bytes=48 * MIB),
+        cost_estimate=pl.CostEstimate(
+            flops=2 * heads * length * HEAD_DIM * length,
+            bytes_accessed=8 * length * wide,
+            transcendentals=heads * length * length // 2,
+        ),
+        name="attend_local",
+    )(qkv, qkv, qkv)
+
+
+def memory_kernel(
+    heads, top, chosen_ref, counts_ref, q_ref, mk_ref, mv_ref, local_ref, local_lse_ref, out_ref, lse_ref
+):
+    block = pl.program_id(0)
+    subs = q_ref.shape[0] // QBLK
+    ones = jnp.ones((top * MBLK, HEAD_DIM), BF16)
+    for sub in range(subs):
+        base = (block * subs + sub) * top
+        rows = slice(sub * QBLK, (sub + 1) * QBLK)
+        bias = memory_bias(counts_ref, base, top, 1)
+        for head in range(heads):
+            columns = slice(head * HEAD_DIM, (head + 1) * HEAD_DIM)
+            keys = pick_memory(mk_ref, chosen_ref, base, top, columns)
+            values = pick_memory(mv_ref, chosen_ref, base, top, columns)
+            scores = dot(q_ref[rows, columns], keys, NT) + bias
+            local_lse = local_lse_ref[rows, head : head + 1]
+            peak = jnp.maximum(jnp.max(scores, -1, keepdims=True), local_lse)
+            acc = dot(jnp.exp2(scores - peak).astype(BF16), jnp.concatenate([values, ones], 1))
+            local = jnp.exp2(local_lse - peak)
+            total = acc[:, HEAD_DIM:] + local
+            out_ref[rows, columns] = ((acc[:, :HEAD_DIM] + local_ref[rows, columns] * local) / total).astype(BF16)
+            lse_ref[rows, head : head + 1] = peak + jnp.log2(total[:, :1])
+
+
+def attend_memory(chosen, counts, qkv, memory, local, local_lse, heads, top):
     length = qkv.shape[0]
     wide = heads * HEAD_DIM
     rows = min(2 * QBLK, length)
     mem_rows = memory.shape[0]
+    by_rows = pl.BlockSpec((rows, wide), lambda i, *_: (i, 0))
+    stats = pl.BlockSpec((rows, heads), lambda i, *_: (i, 0))
     return pl.pallas_call(
-        functools.partial(forward_kernel, heads, top),
+        functools.partial(memory_kernel, heads, top),
         grid_spec=pltpu.PrefetchScalarGridSpec(
             num_scalar_prefetch=2,
             grid=(length // rows,),
             in_specs=[
-                pl.BlockSpec((rows, wide), lambda i, *_: (i, 0)),
-                pl.BlockSpec((length, wide), lambda i, *_: (0, 1)),
-                pl.BlockSpec((length, wide), lambda i, *_: (0, 2)),
+                by_rows,
                 pl.BlockSpec((mem_rows, wide), lambda i, *_: (0, 0)),
                 pl.BlockSpec((mem_rows, wide), lambda i, *_: (0, 1)),
+                by_rows,
+                stats,
             ],
-            out_specs=[
-                pl.BlockSpec((rows, wide), lambda i, *_: (i, 0)),
-                pl.BlockSpec((rows, heads), lambda i, *_: (i, 0)),
-            ],
-            scratch_shapes=[
-                pltpu.VMEM((heads, rows, 2 * HEAD_DIM), F32),
-                pltpu.VMEM((heads, rows, HEAD_DIM), F32),
-            ],
+            out_specs=[by_rows, stats],
         ),
         out_shape=[
             jax.ShapeDtypeStruct((length, wide), BF16),
@@ -181,12 +217,12 @@
         ],
         compiler_params=pltpu.CompilerParams(vmem_limit_bytes=48 * MIB),
         cost_estimate=pl.CostEstimate(
-            flops=4 * heads * length * HEAD_DIM * (length // 2 + top * MBLK),
+            flops=4 * heads * length * HEAD_DIM * top * MBLK,
             bytes_accessed=8 * length * wide,
-            transcendentals=heads * length * (length // 2 + top * MBLK),
+            transcendentals=heads * length * top * MBLK,
         ),
-        name="attend_forward",
-    )(chosen, counts, qkv, qkv, qkv, memory, memory)
+        name="attend_memory",
+    )(chosen, counts, qkv, memory, memory, local, local_lse)
 
 
 def backward_kernel(
@@ -583,18 +619,26 @@
     def block(index):
         return lax.dynamic_slice_in_dim(partial, jnp.clip(index, 0, size - 1) * rows, rows, 0).astype(F32)
 
-    rising = falling = None
-    steps = []
+    arrived = []
     for step in range(size - 1):
         up, down = block(size - 1 - step + place), block(step - size + 1 + place)
         if step:
-            up, down = up + rising.astype(F32), down + falling.astype(F32)
+            up, down = up + arrived[-1][0].astype(F32), down + arrived[-1][1].astype(F32)
         up, down = lax.optimization_barrier((up.astype(BF16), down.astype(BF16)))
         rising = lax.ppermute(up, axis, [(i, i + 1) for i in range(step + 1)])
         falling = lax.ppermute(down, axis, [(i, i - 1) for i in range(size - 1 - step, size)])
-        rising, falling = lax.optimization_barrier((rising, falling))
-        steps.append((rising, falling))
-    return block(place), steps
+        arrived.append(lax.optimization_barrier((rising, falling)))
+    return block(place), arrived
+
+
+def direct_exchange(blocks, axis):
+    size = lax.axis_size(axis)
+    place = lax.axis_index(axis)
+    taken = [lax.dynamic_index_in_dim(blocks, place, 0, keepdims=False)]
+    for far in range(1, size):
+        give = lax.dynamic_index_in_dim(blocks, (place + far) % size, 0, keepdims=False)
+        taken.append(lax.ppermute(give, axis, [(i, (i + far) % size) for i in range(size)]))
+    return taken
 
 
 def body(
@@ -628,7 +672,7 @@
     shards = jnp.concatenate([w_out, w_gate, w_up], 1)
     (near, near_down), steps = chain_gather((shards, w_down), "fsdp")
     (gathered,), token_steps = chain_gather((after(mine, steps[-2]),), "fsdp")
-    parcel = lax.all_gather(after(parcel, steps[0]), DP, axis=0, tiled=True)
+    parcel = lax.all_gather(parcel, DP, axis=0, tiled=True)
     w_qkv = parcel[:, :share].reshape(width, 3 * wide)
     gain_one = parcel[:, share, :share].reshape(1, width).astype(F32)
     gain_two = parcel[:, share, share : 2 * share].reshape(1, width).astype(F32)
@@ -638,12 +682,13 @@
     memory = jnp.concatenate(
         [m[0].reshape(-1, ring, wide).transpose(1, 0, 2) for m in (memory_keys, memory_values)], 2
     )
-    memory = lax.all_to_all(after(memory, token_steps[-2]), "fsdp", 0, 0, tiled=True).reshape(-1, 2 * wide)
+    memory = lax.all_to_all(after(memory, token_steps[-1]), "fsdp", 0, 0, tiled=True).reshape(-1, 2 * wide)
     down_full = lax.all_gather(jnp.concatenate(near_down, 0), DP, axis=0, tiled=True)
 
     cosine, sine = rotary_tables(length)
     qkv = project_qkv(gathered, gain_one, w_qkv, cosine, sine, heads)
-    attended_heads, lse = attend_forward(chosen_all, counts_all, qkv, memory, heads, top)
+    local, local_lse = attend_local(qkv, heads)
+    attended_heads, lse = attend_memory(chosen_all, counts_all, qkv, memory, local, local_lse, heads, top)
     attended = lax.all_to_all(attended_heads, "fsdp", 0, 1, tiled=True)
 
     upstream = cotangent[0]
@@ -656,10 +701,10 @@
     partial, grad_qkv = attend_backward(
         chosen_all, counts_all, qkv, memory, grad_heads, attended_heads, lse, cosine, sine, w_qkv, heads, top
     )
-    own_term, steps = chain_scatter(partial, "fsdp")
+    own_term, arrived = chain_scatter(partial, "fsdp")
+    grads = after(grads, arrived[-1])
+
     grad_w_qkv, gain_one_grad = projection_grads(gathered, gain_one.reshape(width, 1), w_qkv, grad_qkv)
-    grads = after(grads, steps[-1])
-
     gains = jnp.stack([gain_one_grad.reshape(span, -1), gain_two_grad.reshape(span, -1)], 1)
     gains = jnp.pad(gains.astype(BF16), ((0, 0), (0, extra - 2), (0, 3 * wide - gains.shape[2])))
     late = jnp.concatenate([grad_w_qkv.reshape(span, -1, 3 * wide), gains], 1)
@@ -667,18 +712,8 @@
     core = lax.axis_index("core")
     taken = lax.ppermute(lax.dynamic_index_in_dim(late, 1 - core, 1, keepdims=False), "core", [(0, 1), (1, 0)])
     late = lax.dynamic_index_in_dim(late, core, 1, keepdims=False).astype(F32) + taken.astype(F32)
-    late = after(late.astype(BF16), steps[0])
-    late = jnp.sum(lax.all_to_all(late, "chip", 0, 0, tiled=True).astype(F32), 0).astype(BF16)
-    gains = late[-extra : 2 - extra, : ring * share].reshape(2, ring, share).transpose(1, 0, 2)
-    gains = jnp.pad(gains, ((0, 0), (0, extra - 2), (0, 3 * wide - share)))
-    late = jnp.concatenate([late[:-extra].reshape(ring, share, 3 * wide), gains], 1)
-    late = lax.all_to_all(late, "fsdp", 0, 0, tiled=True).astype(F32)
-    projections = [
-        late[:, :share, part * wide : (part + 1) * wide].transpose(1, 0, 2).reshape(share, width)
-        for part in range(3)
-    ]
-    gain_shares = jnp.sum(late[:, share : share + 2, :share], 0)
-
+    late = after(late.astype(BF16), arrived[0])
+    late = sum(piece.astype(F32) for piece in direct_exchange(late, "chip")).astype(BF16)
     strip = grads.shape[1]
     lanes = width // strip
     tall = w_down.shape[0]
@@ -690,7 +725,7 @@
         grads = grads[ring * tall * lanes :]
     grads = grads.reshape(-1, ring, share, strip).transpose(1, 0, 2, 3)
     pieces = jnp.concatenate([down.reshape(ring, -1, strip), grads.reshape(ring, -1, strip)], 1)
-    rising, falling = steps[-1]
+    rising, falling = arrived[-1]
     grad_normed = own_term + rising.astype(F32) + falling.astype(F32)
     own = mine.astype(F32)
     factor = lax.rsqrt(jnp.mean(own * own, -1, keepdims=True) + EPSILON)
@@ -698,7 +733,18 @@
     inner = jnp.mean(scaled * own, -1, keepdims=True)
     tokens_grad = (grad_middle + factor * scaled - own * (factor * factor * factor * inner)).astype(BF16)
 
-    pieces = lax.psum_scatter(pieces, "fsdp", scatter_dimension=0, tiled=True)[0].astype(F32)
+    gains = late[-extra : 2 - extra, : ring * share].reshape(2, ring, share).transpose(1, 0, 2)
+    gains = jnp.pad(gains, ((0, 0), (0, extra - 2), (0, 3 * wide - share)))
+    late = jnp.concatenate([late[:-extra].reshape(ring, share, 3 * wide), gains], 1)
+    late = after(lax.all_to_all(late, "fsdp", 0, 0, tiled=True), tokens_grad).astype(F32)
+    projections = [
+        late[:, :share, part * wide : (part + 1) * wide].transpose(1, 0, 2).reshape(share, width)
+        for part in range(3)
+    ]
+    gain_shares = jnp.sum(late[:, share : share + 2, :share], 0)
+
+    pieces = lax.psum_scatter(pieces, "fsdp", scatter_dimension=0, tiled=True)
+    pieces = after(pieces, (tokens_grad, projections, gain_shares))[0].astype(F32)
     down_share = pieces[: lanes * tall].reshape(lanes, tall, strip).transpose(1, 0, 2).reshape(tall, width)
     others = pieces[lanes * tall :].reshape(-1, share, strip).transpose(1, 0, 2).reshape(share, -1)
     return (

time: 482 us -> 489 us (1.015)
  local copies, waits for them, and re-layouts: 28.4 us -> 33.5 us
  starting transfers between devices: 73.4 us -> 68.4 us
    ppermute x9, waiting for transfers between devices: 81.3 us -> 66.3 us  [chain_gather(): falling = tuple((lax.ppermute(block, axis, down) for block in falling))]
    ppermute x0 -> x3, waiting for transfers between devices: none -> 8.48 us  [direct_exchange(): lax.ppermute(give, axis, [(i, (i + far) % size) for i in range(size)])]
    all_to_all x3 -> x2, waiting for transfers between devices: 15.4 us -> 8.62 us  [the longest x1 8.62 us: body(): lax.all_to_all(late, 'fsdp', 0, 0, tiled=True)]
    all_to_all x3 -> x2, starting transfers between devices: 13.6 us -> 7.44 us  [the longest x1 4.04 us: body(): lax.all_to_all(after(memory, token_steps[-1]), 'fsdp', 0, 0, tiled=True)]
    all_to_all x1, waiting for transfers between devices: 15.6 us -> 21.7 us  [body(): grad_heads = lax.all_to_all(grad_attended, 'fsdp', 1, 0, tiled=True)]
    convert_element_type x2 -> x4, other arithmetic: 0.24 us -> 5.74 us  [the longest x1 3.01 us: body(): (grad_middle + factor * scaled - own * (factor * factor * factor * inner)...]
    pallas_call x1 -> x2, Pallas kernels: 21.4 us -> 23.7 us  [the longest x1 15.7 us: attend_local(): pl.pallas_call(functools.partial(local_kernel, heads), grid=(length // ro...]
  transfers between devices with their start and end apart: 35 -> 37, of which waited for: 15 -> 16; matrix products, arithmetic and copies ran while one was open for 11% -> 10% of each run, Pallas kernels for 15% -> 15%
where the time goes in v11:
time: 489 us; the launch traced here: 480 us
  waiting for transfers between devices  194 us (40%)
  Pallas kernels  116 us (24%)
  starting transfers between devices  68.4 us (14%)
  other arithmetic  39.9 us (8%)
  local copies, waits for them, and re-layouts  33.5 us (7%)
  between operations  14.9 us (3%)
  blocking collectives  14.7 us (3%)
    ppermute x9, waiting for transfers between devices, chain_gather(): falling = tuple((lax.ppermute(block, axis, down) for block in falling))  66.3 us
    ppermute x3, waiting for transfers between devices, chain_scatter(): rising = lax.ppermute(up, axis, [(i, i + 1) for i in range(step + 1)])  57.2 us
    pallas_call x1, Pallas kernels, feed_forward(): pl.pallas_call(functools.partial(ffn_kernel, span, merged), grid=(steps,)...  43.9 us
    pallas_call x1, Pallas kernels, attend_backward(): pl.pallas_call(functools.partial(backward_kernel, heads, top), grid_spec=...  32.2 us
    all_to_all x1, waiting for transfers between devices, body(): grad_heads = lax.all_to_all(grad_attended, 'fsdp', 1, 0, tiled=True)  21.7 us
    ppermute x9, starting transfers between devices, chain_gather(): rising = tuple((lax.ppermute(block, axis, up) for block in rising))  18.8 us
    all_to_all x1, waiting for transfers between devices, body(): attended = lax.all_to_all(attended_heads, 'fsdp', 0, 1, tiled=True)  18 us
    pallas_call x1, Pallas kernels, attend_local(): pl.pallas_call(functools.partial(local_kernel, heads), grid=(length // ro...  15.7 us
  transfers between devices with their start and end apart: 37, of which 16 were waited for; matrix products, arithmetic and copies ran while one was open for 10% of the time, Pallas kernels for 15%

profile of v11, /device:TPU:0, one launch (start us, length us, event | category | flops | bytes accessed | tf_op | source)
XLA Modules:
  0.0 480.5 jit_solution(11520250382277065744)
XLA Ops:
  12.6 14.7 %all_to_all.53 = bf16[4,40,768]{2,1,0:T(8,128)(2,1)} all-to-all(bf16[4,40,768]{2,1,0:T(8,128)(2,1)S(1)} %copy.66), channel_id=1, replica_groups=mesh['chip'=4,'core'=2,'fsdp'=4] {'fsdp'}, dimensions={0} | all-to-all | bytes 491520 | tf_op jit(solution)/shard_map/all_to_all | solution.py:669
  28.8 4.6 collective-permute-start
  36.8 6.8 %collective-permute-done.1 = bf16[88,1024]{1,0:T(8,128)(2,1)S(1)} collective-permute-done((bf16[88,1024]{1,0:T(8,128)(2,1)S(1)}, bf16[88,1024]{1,0:T(8,128)(2,1)S(1)}, u32[]{:S(2)}, u32[]{:S(2)}) %collective-permute-start.1) | collective-permute-done | bytes 180256 | tf_op jit(solution)/shard_map/ppermute | solution.py:592
  48.3 13.4 %collective-permute-done.7 = bf16[88,1024]{1,0:T(8,128)(2,1)} collective-permute-done((bf16[88,1024]{1,0:T(8,128)(2,1)S(1)}, bf16[88,1024]{1,0:T(8,128)(2,1)}, u32[]{:S(2)}, u32[]{:S(2)}) %collective-permute-start.7) | collective-permute-done | bytes 180256 | tf_op jit(solution)/shard_map/ppermute | solution.py:593
  66.3 10.6 %collective-permute-done.17 = bf16[88,1024]{1,0:T(8,128)(2,1)} collective-permute-done((bf16[88,1024]{1,0:T(8,128)(2,1)}, bf16[88,1024]{1,0:T(8,128)(2,1)}, u32[]{:S(2)}, u32[]{:S(2)}) %collective-permute-start.17) | collective-permute-done | bytes 180256 | tf_op jit(solution)/shard_map/ppermute | solution.py:593
  82.2 4.6 collective-permute-start.8
  86.8 17.4 %collective-permute-done.11 = bf16[512,1024]{1,0:T(8,128)(2,1)S(1)} collective-permute-done((bf16[512,1024]{1,0:T(8,128)(2,1)S(1)}, bf16[512,1024]{1,0:T(8,128)(2,1)S(1)}, u32[]{:S(2)}, u32[]{:S(2)}) %collective-permute-start.11) | collective-permute-done | bytes 1048608 | tf_op jit(solution)/shard_map/ppermute | solution.py:593
  111.4 16.0 %collective-permute-done.12 = bf16[512,1024]{1,0:T(8,128)(2,1)} collective-permute-done((bf16[512,1024]{1,0:T(8,128)(2,1)S(1)}, bf16[512,1024]{1,0:T(8,128)(2,1)}, u32[]{:S(2)}, u32[]{:S(2)}) %collective-permute-start.12) | collective-permute-done | bytes 1048608 | tf_op jit(solution)/shard_map/ppermute | solution.py:593
  139.7 9.0 %collective-permute-done.13 = bf16[512,1024]{1,0:T(8,128)(2,1)S(1)} collective-permute-done((bf16[512,1024]{1,0:T(8,128)(2,1)}, bf16[512,1024]{1,0:T(8,128)(2,1)S(1)}, u32[]{:S(2)}, u32[]{:S(2)}) %collective-permute-start.13) | collective-permute-done | bytes 1048608 | tf_op jit(solution)/shard_map/ppermute | solution.py:593
  159.6 7.8 %project_qkv.1.q_ref.k_ref.v_ref = bf16[2048,768]{1,0:T(8,128)(2,1)} custom-call(bf16[2048,1024]{1,0:T(8,128)(2,1)} %pad_maximum_fusion.tok_ref, f32[1,1024]{1,0:T(1,128)S(1)} %reshape.193.gain_ref, bf16[1024,768]{1,0:T(8,128)(2,1)S(1)} %bitcast.88, f32[2048,128]{1,0:T(8,128)S(1)} %copy-done.3, f32[2048,128]{1,0:T(8,128)S(1)} %copy-done.5), custom_call_target="tpu_custom_call" | custom-call | flops 3221225472 | bytes 14680064 | tf_op jit(solution)/shard_map/project_qkv/pallas_call | solution.py:62
  167.3 15.7 %attend_local.1 = (f32[2048,256]{1,0:T(8,128)S(1)}, f32[2048,2]{1,0:T(8,128)S(1)}) custom-call(bf16[2048,768]{1,0:T(8,128)(2,1)} %project_qkv.1.q_ref.k_ref.v_ref, bf16[2048,768]{1,0:T(8,128)(2,1)} %project_qkv.1.q_ref.k_ref.v_ref, bf16[2048,768]{1,0:T(8,128)(2,1)} %project_qkv.1.q_ref.k_ref.v_ref), custom_call_target="tpu_custom_call" | custom-call | flops 2147483648 | bytes 4194304 | tf_op jit(solution)/shard_map/attend_local/pallas_call | solution.py:139
  184.4 8.0 %attend_memory.1 = (bf16[2048,256]{1,0:T(8,128)(2,1)}, f32[2048,2]{1,0:T(8,128)S(1)}) custom-call(s32[32]{0:T(128)S(1)} %reshape_squeeze.24.chosen_ref, s32[32]{0:T(128)S(1)} %reshape_squeeze.25.counts_ref, bf16[2048,768]{1,0:T(8,128)(2,1)} %project_qkv.1.q_ref.k_ref.v_ref, bf16[1024,512]{1,0:T(8,128)(2,1)S(1)} %bitcast.84, bf16[1024,512]{1,0:T(8,128)(2,1)S(1)} %bitcast.85, ...), custom_call_target="tpu_custom_call" | custom-call | flops 1073741824 | bytes 4194304 | tf_op jit(solution)/shard_map/attend_memory/pallas_call | solution.py:200
  192.4 5.1 %all-to-all-start.2 = ((bf16[4,512,256]{2,1,0:T(8,128)(2,1)}), bf16[4,512,256]{2,1,0:T(8,128)(2,1)S(1)}, u32[]{:S(2)}, u32[]{:S(2)}) async-start(bf16[4,512,256]{2,1,0:T(8,128)(2,1)} %bitcast.8), calls=%async_computation.2 | async-start | bytes 2097152 | tf_op jit(solution)/shard_map/all_to_all | solution.py:692
  198.4 18.0 %all-to-all-done.2 = bf16[4,512,256]{2,1,0:T(8,128)(2,1)S(1)} async-done(((bf16[4,512,256]{2,1,0:T(8,128)(2,1)}), bf16[4,512,256]{2,1,0:T(8,128)(2,1)S(1)}, u32[]{:S(2)}, u32[]{:S(2)}) %all-to-all-start.2) | async-done | bytes 1048608 | tf_op jit(solution)/shard_map/all_to_all | solution.py:692
  217.5 43.9 %feed_forward.1 = (bf16[512,1024]{1,0:T(8,128)(2,1)}, f32[512,1024]{1,0:T(8,128)}, bf16[512,1024]{1,0:T(8,128)(2,1)}, f32[1,1024]{1,0:T(1,128)}, bf16[8,4736,256]{2,1,0:T(8,128)(2,1)}) custom-call(bf16[512,1024]{1,0:T(8,128)(2,1)} %bitcast.94, bf16[512,1024]{1,0:T(8,128)(2,1)} %bitcast.109, bf16[512,1024]{1,0:T(8,128)(2,1)} %bitcast.125, ...), custom_call_target="tpu_custom_call" | custom-call | flops 29796335616 | bytes 38797312 | tf_op jit(solution)/shard_map/feed_forward/pallas_call | solution.py:494
  267.5 21.7 %all-to-all-done.3 = bf16[512,4,256]{2,0,1:T(8,128)(2,1)S(1)} async-done(((bf16[512,4,256]{2,0,1:T(8,128)(2,1)}), bf16[512,4,256]{2,0,1:T(8,128)(2,1)S(1)}, u32[]{:S(2)}, u32[]{:S(2)}) %all-to-all-start.3) | async-done | bytes 1048608 | tf_op jit(solution)/shard_map/all_to_all | solution.py:698
  290.5 32.2 %attend_backward.1 = (bf16[2048,1024]{1,0:T(8,128)(2,1)}, bf16[2048,768]{1,0:T(8,128)(2,1)}) custom-call(s32[32]{0:T(128)S(1)} %reshape_squeeze.24.chosen_ref, s32[32]{0:T(128)S(1)} %reshape_squeeze.25.counts_ref, bf16[2048,768]{1,0:T(8,128)(2,1)} %project_qkv.1.q_ref.k_ref.v_ref, bf16[2048,768]{1,0:T(8,128)(2,1)} %project_qkv.1.q_ref.k_ref.v_ref, ...), custom_call_target="tpu_custom_call" | custom-call | flops 8053063680 | bytes 8388608 | tf_op jit(solution)/shard_map/attend_backward/pallas_call | solution.py:315
  327.4 19.5 %collective-permute-done.18 = bf16[512,1024]{1,0:T(8,128)(2,1)S(1)} collective-permute-done((bf16[512,1024]{1,0:T(8,128)(2,1)S(1)}, bf16[512,1024]{1,0:T(8,128)(2,1)S(1)}, u32[]{:S(2)}, u32[]{:S(2)}) %collective-permute-start.18) | collective-permute-done | bytes 1048608 | tf_op jit(solution)/shard_map/ppermute | solution.py:628
  355.9 20.0 %collective-permute-done.20 = bf16[512,1024]{1,0:T(8,128)(2,1)S(1)} collective-permute-done((bf16[512,1024]{1,0:T(8,128)(2,1)}, bf16[512,1024]{1,0:T(8,128)(2,1)S(1)}, u32[]{:S(2)}, u32[]{:S(2)}) %collective-permute-start.20) | collective-permute-done | bytes 1048608 | tf_op jit(solution)/shard_map/ppermute | solution.py:628
  379.9 7.1 %collective-permute-start.22 = (bf16[512,1024]{1,0:T(8,128)(2,1)}, bf16[512,1024]{1,0:T(8,128)(2,1)S(1)}, u32[]{:S(2)}, u32[]{:S(2)}) collective-permute-start(bf16[512,1024]{1,0:T(8,128)(2,1)} %get-tuple-element.84), channel_id=1, source_target_pairs={{0,1},{1,2},{2,3},{4,5},{5,6},{6,7},{8,9},{9,10},{10,11},{12,13},{... | collective-permute-start | bytes 3145736 | tf_op jit(solution)/shard_map/ppermute | solution.py:628
  388.6 17.7 %collective-permute-done.22 = bf16[512,1024]{1,0:T(8,128)(2,1)S(1)} collective-permute-done((bf16[512,1024]{1,0:T(8,128)(2,1)}, bf16[512,1024]{1,0:T(8,128)(2,1)S(1)}, u32[]{:S(2)}, u32[]{:S(2)}) %collective-permute-start.22) | collective-permute-done | bytes 1048608 | tf_op jit(solution)/shard_map/ppermute | solution.py:628
  418.8 7.9 %projection_grads.1 = (bf16[1024,768]{1,0:T(8,128)(2,1)S(1)}, f32[1024,1]{1,0:T(8,128)S(1)}) custom-call(bf16[2048,1024]{1,0:T(8,128)(2,1)} %pad_maximum_fusion.tok_ref, f32[1024,1]{1,0:T(8,128)S(1)} %copy-done.6, bf16[1024,768]{1,0:T(8,128)(2,1)S(1)} %bitcast.90, bf16[2048,768]{1,0:T(8,128)(2,1)} %get-tuple-element.88.grad_ref), custom_call_target="tpu_custom_call" | custom-call | flops 3221225472 | bytes 7340032 | tf_op jit(solution)/shard_map/projection_grads/pallas_call | solution.py:554
  438.6 4.6 collective-permute-done.25
  458.0 8.6 %all-to-all-done.4 = bf16[4,40,768]{2,1,0:T(8,128)(2,1)S(1)} async-done(((bf16[4,40,768]{2,1,0:T(8,128)(2,1)}), bf16[4,40,768]{2,1,0:T(8,128)(2,1)S(1)}, u32[]{:S(2)}, u32[]{:S(2)}) %all-to-all-start.4) | async-done | bytes 245792 | tf_op jit(solution)/shard_map/all_to_all | solution.py:739
  (201 shorter events, 130.8 us)
Async XLA Ops:
  7.2 129.9 %all-gather.4.cloned.1.call-start = ((), (), s32[]{:S(2)}) async-start(), calls=%async_computation.7 | async-start | bytes 2211840 | tf_op jit(solution)/shard_map/all_gather | solution.py:675
  27.4 190.1 %all-gather.8.cloned.1.call-start = ((), (), s32[]{:S(2)}) async-start(), calls=%async_computation.9 | async-start | bytes 6488064 | tf_op jit(solution)/shard_map/all_gather | solution.py:686
  27.5 16.2 %collective-permute-start.2 = (bf16[32,6656]{1,0:T(8,128)(2,1)S(1)}, bf16[32,6656]{1,0:T(8,128)(2,1)S(1)}, u32[]{:S(2)}, u32[]{:S(2)}) collective-permute-start(bf16[32,6656]{1,0:T(8,128)(2,1)S(1)} %constant_dynamic-update-slice_fusion), channel_id=1, source_target_pairs={{1,0},{2,1},{3,2},{5,4},{6,5},{7,6},{9,8},{10,9},{11,10},{13,12},{... | collective-permute-start | bytes 1277960 | tf_op jit(solution)/shard_map/ppermute | solution.py:593
  43.7 18.0 %collective-permute-start.4 = (bf16[32,6656]{1,0:T(8,128)(2,1)S(1)}, bf16[32,6656]{1,0:T(8,128)(2,1)S(1)}, u32[]{:S(2)}, u32[]{:S(2)}) collective-permute-start(bf16[32,6656]{1,0:T(8,128)(2,1)S(1)} %collective-permute-done), channel_id=1, source_target_pairs={{1,2},{2,3},{5,6},{6,7},{9,10},{10,11},{13,14},{14,15},{17,18},{18... | collective-permute-start | bytes 1277960 | tf_op jit(solution)/shard_map/ppermute | solution.py:592
  44.4 17.3 %collective-permute-start.6 = (bf16[32,6656]{1,0:T(8,128)(2,1)S(1)}, bf16[32,6656]{1,0:T(8,128)(2,1)S(1)}, u32[]{:S(2)}, u32[]{:S(2)}) collective-permute-start(bf16[32,6656]{1,0:T(8,128)(2,1)S(1)} %collective-permute-done.2), channel_id=1, source_target_pairs={{1,0},{2,1},{5,4},{6,5},{9,8},{10,9},{13,12},{14,13},{17,16},{18,1... | collective-permute-start | bytes 1277960 | tf_op jit(solution)/shard_map/ppermute | solution.py:593
  79.0 138.5 %all-gather.6.cloned.1.call-start = ((), (), s32[]{:S(2)}) async-start(), calls=%async_computation.8 | async-start | bytes 15335424 | tf_op jit(solution)/shard_map/all_gather | solution.py:679
  80.9 23.3 %collective-permute-start.11 = (bf16[512,1024]{1,0:T(8,128)(2,1)S(1)}, bf16[512,1024]{1,0:T(8,128)(2,1)S(1)}, u32[]{:S(2)}, u32[]{:S(2)}) collective-permute-start(bf16[512,1024]{1,0:T(8,128)(2,1)S(1)} %bitcast.95), channel_id=1, source_target_pairs={{1,0},{2,1},{3,2},{5,4},{6,5},{7,6},{9,8},{10,9},{11,10},{13,12},{... | collective-permute-start | bytes 3145736 | tf_op jit(solution)/shard_map/ppermute | solution.py:593
  82.2 23.3 %collective-permute-start.8 = (bf16[512,1024]{1,0:T(8,128)(2,1)S(1)}, bf16[512,1024]{1,0:T(8,128)(2,1)S(1)}, u32[]{:S(2)}, u32[]{:S(2)}) collective-permute-start(bf16[512,1024]{1,0:T(8,128)(2,1)S(1)} %bitcast.96), channel_id=1, source_target_pairs={{0,1},{1,2},{2,3},{4,5},{5,6},{6,7},{8,9},{9,10},{10,11},{12,13},{... | collective-permute-start | bytes 3145736 | tf_op jit(solution)/shard_map/ppermute | solution.py:592
  104.3 23.1 %collective-permute-start.12 = (bf16[512,1024]{1,0:T(8,128)(2,1)S(1)}, bf16[512,1024]{1,0:T(8,128)(2,1)}, u32[]{:S(2)}, u32[]{:S(2)}) collective-permute-start(bf16[512,1024]{1,0:T(8,128)(2,1)S(1)} %collective-permute-done.11), channel_id=1, source_target_pairs={{1,0},{2,1},{5,4},{6,5},{9,8},{10,9},{13,12},{14,13},{17,16},{18,1... | collective-permute-start | bytes 3145736 | tf_op jit(solution)/shard_map/ppermute | solution.py:593
  105.6 23.1 %collective-permute-start.9 = (bf16[512,1024]{1,0:T(8,128)(2,1)S(1)}, bf16[512,1024]{1,0:T(8,128)(2,1)}, u32[]{:S(2)}, u32[]{:S(2)}) collective-permute-start(bf16[512,1024]{1,0:T(8,128)(2,1)S(1)} %collective-permute-done.8), channel_id=1, source_target_pairs={{1,2},{2,3},{5,6},{6,7},{9,10},{10,11},{13,14},{14,15},{17,18},{18... | collective-permute-start | bytes 3145736 | tf_op jit(solution)/shard_map/ppermute | solution.py:592
  127.4 21.3 %collective-permute-start.13 = (bf16[512,1024]{1,0:T(8,128)(2,1)}, bf16[512,1024]{1,0:T(8,128)(2,1)S(1)}, u32[]{:S(2)}, u32[]{:S(2)}) collective-permute-start(bf16[512,1024]{1,0:T(8,128)(2,1)} %collective-permute-done.12), channel_id=1, source_target_pairs={{1,0},{5,4},{9,8},{13,12},{17,16},{21,20},{25,24},{29,28}} | collective-permute-start | bytes 3145736 | tf_op jit(solution)/shard_map/ppermute | solution.py:593
  128.7 20.1 %collective-permute-start.10 = (bf16[512,1024]{1,0:T(8,128)(2,1)}, bf16[512,1024]{1,0:T(8,128)(2,1)}, u32[]{:S(2)}, u32[]{:S(2)}) collective-permute-start(bf16[512,1024]{1,0:T(8,128)(2,1)} %collective-permute-done.9), channel_id=1, source_target_pairs={{2,3},{6,7},{10,11},{14,15},{18,19},{22,23},{26,27},{30,31}} | collective-permute-start | bytes 3145736 | tf_op jit(solution)/shard_map/ppermute | solution.py:592
  149.7 34.7 %all-to-all-start.1 = ((bf16[4,256,512]{2,1,0:T(8,128)(2,1)}), bf16[4,256,512]{2,1,0:T(8,128)(2,1)S(1)}, u32[]{:S(2)}, u32[]{:S(2)}) async-start(bf16[4,256,512]{2,1,0:T(8,128)(2,1)} %pad_maximum_fusion.5), calls=%async_computation.1 | async-start | bytes 2097152 | tf_op jit(solution)/shard_map/all_to_all | solution.py:685
  192.4 23.9 %all-to-all-start.2 = ((bf16[4,512,256]{2,1,0:T(8,128)(2,1)}), bf16[4,512,256]{2,1,0:T(8,128)(2,1)S(1)}, u32[]{:S(2)}, u32[]{:S(2)}) async-start(bf16[4,512,256]{2,1,0:T(8,128)(2,1)} %bitcast.8), calls=%async_computation.2 | async-start | bytes 2097152 | tf_op jit(solution)/shard_map/all_to_all | solution.py:692
  197.5 212.9 %reduce-scatter.3.cloned.1.call-start = ((), (), s32[]{:S(2)}) async-start(), calls=%async_computation.10 | async-start | bytes 21823488 | tf_op jit(solution)/shard_map/reduce_scatter | solution.py:699
  263.7 25.6 %all-to-all-start.3 = ((bf16[512,4,256]{2,0,1:T(8,128)(2,1)}), bf16[512,4,256]{2,0,1:T(8,128)(2,1)S(1)}, u32[]{:S(2)}, u32[]{:S(2)}) async-start(bf16[512,4,256]{2,0,1:T(8,128)(2,1)} %bitcast.99), calls=%async_computation.3 | async-start | bytes 2097152 | tf_op jit(solution)/shard_map/all_to_all | solution.py:698
  267.3 202.0 %reduce-scatter.5.cloned.1.call-start = ((), (), s32[]{:S(2)}) async-start(), calls=%async_computation.11 | async-start | bytes 3031040 | tf_op jit(solution)/shard_map/reduce_scatter | solution.py:746
  324.4 22.5 %collective-permute-start.18 = (bf16[512,1024]{1,0:T(8,128)(2,1)S(1)}, bf16[512,1024]{1,0:T(8,128)(2,1)S(1)}, u32[]{:S(2)}, u32[]{:S(2)}) collective-permute-start(bf16[512,1024]{1,0:T(8,128)(2,1)S(1)} %get-tuple-element.76), channel_id=1, source_target_pairs={{0,1},{4,5},{8,9},{12,13},{16,17},{20,21},{24,25},{28,29}} | collective-permute-start | bytes 3145736 | tf_op jit(solution)/shard_map/ppermute | solution.py:628
  325.8 21.2 %collective-permute-start.19 = (bf16[512,1024]{1,0:T(8,128)(2,1)S(1)}, bf16[512,1024]{1,0:T(8,128)(2,1)}, u32[]{:S(2)}, u32[]{:S(2)}) collective-permute-start(bf16[512,1024]{1,0:T(8,128)(2,1)S(1)} %get-tuple-element.77), channel_id=1, source_target_pairs={{3,2},{7,6},{11,10},{15,14},{19,18},{23,22},{27,26},{31,30}} | collective-permute-start | bytes 3145736 | tf_op jit(solution)/shard_map/ppermute | solution.py:629
  350.8 25.0 %collective-permute-start.20 = (bf16[512,1024]{1,0:T(8,128)(2,1)}, bf16[512,1024]{1,0:T(8,128)(2,1)S(1)}, u32[]{:S(2)}, u32[]{:S(2)}) collective-permute-start(bf16[512,1024]{1,0:T(8,128)(2,1)} %get-tuple-element.80), channel_id=1, source_target_pairs={{0,1},{1,2},{4,5},{5,6},{8,9},{9,10},{12,13},{13,14},{16,17},{17,1... | collective-permute-start | bytes 3145736 | tf_op jit(solution)/shard_map/ppermute | solution.py:628
  355.2 20.7 %collective-permute-start.21 = (bf16[512,1024]{1,0:T(8,128)(2,1)S(1)}, bf16[512,1024]{1,0:T(8,128)(2,1)S(1)}, u32[]{:S(2)}, u32[]{:S(2)}) collective-permute-start(bf16[512,1024]{1,0:T(8,128)(2,1)S(1)} %get-tuple-element.81), channel_id=1, source_target_pairs={{2,1},{3,2},{6,5},{7,6},{10,9},{11,10},{14,13},{15,14},{18,17},{19... | collective-permute-start | bytes 3145736 | tf_op jit(solution)/shard_map/ppermute | solution.py:629
  379.9 26.4 %collective-permute-start.22 = (bf16[512,1024]{1,0:T(8,128)(2,1)}, bf16[512,1024]{1,0:T(8,128)(2,1)S(1)}, u32[]{:S(2)}, u32[]{:S(2)}) collective-permute-start(bf16[512,1024]{1,0:T(8,128)(2,1)} %get-tuple-element.84), channel_id=1, source_target_pairs={{0,1},{1,2},{2,3},{4,5},{5,6},{6,7},{8,9},{9,10},{10,11},{12,13},{... | collective-permute-start | bytes 3145736 | tf_op jit(solution)/shard_map/ppermute | solution.py:628
  387.0 23.4 %collective-permute-start.23 = (bf16[512,1024]{1,0:T(8,128)(2,1)}, bf16[512,1024]{1,0:T(8,128)(2,1)S(1)}, u32[]{:S(2)}, u32[]{:S(2)}) collective-permute-start(bf16[512,1024]{1,0:T(8,128)(2,1)} %get-tuple-element.85), channel_id=1, source_target_pairs={{1,0},{2,1},{3,2},{5,4},{6,5},{7,6},{9,8},{10,9},{11,10},{13,12},{... | collective-permute-start | bytes 3145736 | tf_op jit(solution)/shard_map/ppermute | solution.py:629
  449.3 17.3 %all-to-all-start.4 = ((bf16[4,40,768]{2,1,0:T(8,128)(2,1)}), bf16[4,40,768]{2,1,0:T(8,128)(2,1)S(1)}, u32[]{:S(2)}, u32[]{:S(2)}) async-start(bf16[4,40,768]{2,1,0:T(8,128)(2,1)} %fusion.10), calls=%async_computation.4 | async-start | bytes 491520 | tf_op jit(solution)/shard_map/all_to_all | solution.py:739
  (40 other events, 388.7 us)
Sparse Core Ops, SparseCore 0:
  27.5 26.4 all-gather.3
  79.1 41.5 all-gather.7
  122.6 76.5 all-gather.5
  261.6 127.5 reduce-scatter.2
  415.6 50.5 reduce-scatter.4

commit v12 on v9

--- a/solution.py
+++ b/solution.py
@@ -189,115 +189,234 @@
     )(chosen, counts, qkv, qkv, qkv, memory, memory)
 
 
-def backward_kernel(
-    heads, top, chosen_ref, counts_ref, q_ref, k_ref, v_ref, mk_ref, mv_ref, go_ref, out_ref, lse_ref,
-    cos_ref, sin_ref, w_ref, partial_ref, grad_ref, gk_s, gv_s, gq_s,
+def spread_rows(column):
+    rows = column.shape[0]
+    return jnp.transpose(jnp.broadcast_to(column, (rows, HEAD_DIM)))[:1]
+
+
+def score_grads(query, grad_out, out, lse, keys, values, mask):
+    delta = jnp.sum(grad_out.astype(F32) * out.astype(F32), -1, keepdims=True)
+    weights = jnp.exp2(mask(dot(keys, query, NT)) - spread_rows(lse))
+    grad_weights = dot(values, grad_out, NT)
+    return weights.astype(BF16), (weights * (grad_weights - spread_rows(delta))).astype(BF16)
+
+
+def causal_mask(rows):
+    key_at = lax.broadcasted_iota(jnp.int32, (rows, rows), 0)
+    query_at = lax.broadcasted_iota(jnp.int32, (rows, rows), 1)
+    return lambda scores: jnp.where(query_at >= key_at, scores, NEGATIVE)
+
+
+def memory_query_grad(chosen_ref, counts_ref, base, top, query, grad_out, out, lse, mk_ref, mv_ref, columns):
+    keys = pick_memory(mk_ref, chosen_ref, base, top, columns)
+    values = pick_memory(mv_ref, chosen_ref, base, top, columns)
+    bias = memory_bias(counts_ref, base, top, 0)
+    _, grad_scores = score_grads(query, grad_out, out, lse, keys, values, lambda scores: scores + bias)
+    return dot(grad_scores, keys, TN)
+
+
+def block_grads(heads, grad_query, grad_key, grad_value, cosine, sine):
+    def unturn(value):
+        return (value * cosine - pltpu.roll(value, HEAD_DIM // 2, 1) * sine).astype(BF16)
+
+    parts = []
+    for part, array in enumerate((grad_query * SCALE, grad_key * (1.0 / LOG2E), grad_value)):
+        for head in range(heads):
+            value = array[:, head * HEAD_DIM : (head + 1) * HEAD_DIM]
+            parts.append(unturn(value) if part < 2 else value.astype(BF16))
+    return jnp.concatenate(parts, 1)
+
+
+def first_block_kernel(
+    heads, top, chosen_ref, counts_ref, plan_ref, qkv_ref, mk_ref, mv_ref, go_ref, out_ref, lse_ref, cos_ref, sin_ref,
+    w_ref, partial_ref, grad_ref, gq_ref, gk_ref, gv_ref,
 ):
-    block = pl.num_programs(0) - 1 - pl.program_id(0)
-    rows = q_ref.shape[0]
+    rows = partial_ref.shape[0]
     subs = rows // QBLK
     wide = heads * HEAD_DIM
+    others = go_ref.shape[0] // rows - 1
+    block, is_last = plan_ref[0], plan_ref[1]
     own = pl.ds(pl.multiple_of(block * rows, rows), rows)
-    key_at = lax.broadcasted_iota(jnp.int32, (rows, rows), 0)
-    query_at = lax.broadcasted_iota(jnp.int32, (rows, rows), 1)
-    causal = query_at >= key_at
-
-    @pl.when(pl.program_id(0) == 0)
-    def _():
-        gk_s[...] = jnp.zeros_like(gk_s)
-        gv_s[...] = jnp.zeros_like(gv_s)
-
-    def spread(column):
-        return jnp.transpose(jnp.broadcast_to(column, (rows, HEAD_DIM)))[:1]
-
-    stats = []
-    for head in range(heads):
-        columns = slice(head * HEAD_DIM, (head + 1) * HEAD_DIM)
-        delta = jnp.sum(go_ref[:, columns].astype(F32) * out_ref[:, columns].astype(F32), -1, keepdims=True)
-        stats.append((spread(lse_ref[:, head : head + 1]), spread(delta)))
-
-    def pair(head, queries, keys, values, mask):
-        columns = slice(head * HEAD_DIM, (head + 1) * HEAD_DIM)
-        lse, delta = stats[head]
-        scores = mask(dot(keys, q_ref[queries, columns], NT))
-        weights = jnp.exp2(scores - lse[:, queries])
-        grad_weights = dot(values, go_ref[queries, columns], NT)
-        return weights.astype(BF16), (weights * (grad_weights - delta[:, queries])).astype(BF16)
-
-    every = slice(0, rows)
+    gq_ref[...] = jnp.zeros_like(gq_ref)
+    gk_ref[...] = jnp.zeros_like(gk_ref)
+    gv_ref[...] = jnp.zeros_like(gv_ref)
+
+    def pair(queries, keys, mask):
+        for head in range(heads):
+            at = head * HEAD_DIM
+            columns = slice(at, at + HEAD_DIM)
+            query, grad_out = qkv_ref[queries, columns], go_ref[queries, columns]
+            key = qkv_ref[keys, wide + at : wide + at + HEAD_DIM]
+            value = qkv_ref[keys, 2 * wide + at : 2 * wide + at + HEAD_DIM]
+            lse = lse_ref[queries, head : head + 1]
+            weights, grad_scores = score_grads(query, grad_out, out_ref[queries, columns], lse, key, value, mask)
+            gk_ref[keys, columns] += dot(grad_scores, query)
+            gv_ref[keys, columns] += dot(weights, grad_out)
+            gq_ref[queries, columns] += dot(grad_scores, key, TN)
+
     for head in range(heads):
         columns = slice(head * HEAD_DIM, (head + 1) * HEAD_DIM)
         for sub in range(subs):
-            base = (block * subs + sub) * top
-            queries = slice(sub * QBLK, (sub + 1) * QBLK)
-            keys = pick_memory(mk_ref, chosen_ref, base, top, columns)
-            values = pick_memory(mv_ref, chosen_ref, base, top, columns)
-            bias = memory_bias(counts_ref, base, top, 0)
-            _, grad_scores = pair(head, queries, keys, values, lambda scores: scores + bias)
-            gq_s[queries, columns] = dot(grad_scores, keys, TN)
-
-    def local(head, there, mask):
-        columns = slice(head * HEAD_DIM, (head + 1) * HEAD_DIM)
-        keys = k_ref[there, columns]
-        weights, grad_scores = pair(head, every, keys, v_ref[there, columns], mask)
-        gk_s[there, columns] += dot(grad_scores, q_ref[:, columns])
-        gv_s[there, columns] += dot(weights, go_ref[:, columns])
-        gq_s[:, columns] += dot(grad_scores, keys, TN)
-
-    for head in range(heads):
-        local(head, own, lambda scores: jnp.where(causal, scores, NEGATIVE))
+            here = pl.ds(pl.multiple_of(block * rows + sub * QBLK, QBLK), QBLK)
+            gq_ref[here, columns] += memory_query_grad(
+                chosen_ref, counts_ref, (block * subs + sub) * top, top, qkv_ref[here, columns], go_ref[here, columns],
+                out_ref[here, columns], lse_ref[here, head : head + 1], mk_ref, mv_ref, columns,
+            )
+    pair(own, own, causal_mask(rows))
 
     def step(index, carry):
-        for head in range(heads):
-            local(head, pl.ds(pl.multiple_of(index * rows, rows), rows), lambda scores: scores)
+        other = jnp.where(is_last == 1, index, index + 1)
+        queries = jnp.where(is_last == 1, block, other)
+        keys = jnp.where(is_last == 1, other, block)
+        pair(
+            pl.ds(pl.multiple_of(queries * rows, rows), rows),
+            pl.ds(pl.multiple_of(keys * rows, rows), rows),
+            lambda scores: scores,
+        )
         return carry
 
-    lax.fori_loop(0, block, step, 0)
-    cosine, sine = cos_ref[...], sin_ref[...]
-
-    def unturn(value):
-        return value * cosine - pltpu.roll(value, HEAD_DIM // 2, 1) * sine
-
-    for head in range(heads):
-        columns = slice(head * HEAD_DIM, (head + 1) * HEAD_DIM)
-        at = head * HEAD_DIM
-        grad_ref[:, at : at + HEAD_DIM] = unturn(gq_s[:, columns] * SCALE).astype(BF16)
-        grad_key = gk_s[own, columns] * (1.0 / LOG2E)
-        grad_ref[:, wide + at : wide + at + HEAD_DIM] = unturn(grad_key).astype(BF16)
-        grad_ref[:, 2 * wide + at : 2 * wide + at + HEAD_DIM] = gv_s[own, columns].astype(BF16)
-
-    partial_ref[...] = dot(grad_ref[...], w_ref[...], NT).astype(BF16)
-
-
-def attend_backward(chosen, counts, qkv, memory, grad_out, out, lse, cosine, sine, w_qkv, heads, top):
+    lax.fori_loop(0, others, step, 0)
+    grad = block_grads(
+        heads, gq_ref[own, :], gk_ref[own, :], gv_ref[own, :], cos_ref[own, :], sin_ref[own, :]
+    )
+    grad_ref[...] = grad
+    partial_ref[...] = dot(grad, w_ref[...], NT).astype(BF16)
+
+
+def first_block(plan, chosen, counts, qkv, memory, grad_out, out, lse, cosine, sine, w_qkv, heads, top):
     length = qkv.shape[0]
     width = w_qkv.shape[0]
     wide = heads * HEAD_DIM
     rows = min(2 * QBLK, length)
     mem_rows = memory.shape[0]
-    last = length // rows - 1
+
+    def whole(array):
+        return pl.BlockSpec(array.shape, lambda i, *_: (0, 0))
+
+    sums = pl.BlockSpec((length, wide), lambda i, *_: (0, 0))
     return pl.pallas_call(
-        functools.partial(backward_kernel, heads, top),
+        functools.partial(first_block_kernel, heads, top),
         grid_spec=pltpu.PrefetchScalarGridSpec(
-            num_scalar_prefetch=2,
-            grid=(last + 1,),
+            num_scalar_prefetch=3,
+            grid=(1,),
             in_specs=[
-                pl.BlockSpec((rows, wide), lambda i, *_: (last - i, 0)),
+                whole(qkv),
+                pl.BlockSpec((mem_rows, wide), lambda i, *_: (0, 0)),
+                pl.BlockSpec((mem_rows, wide), lambda i, *_: (0, 1)),
+                whole(grad_out),
+                whole(out),
+                whole(lse),
+                whole(cosine),
+                whole(sine),
+                whole(w_qkv),
+            ],
+            out_specs=[
+                pl.BlockSpec((rows, width), lambda i, *_: (0, 0)),
+                pl.BlockSpec((rows, 3 * wide), lambda i, *_: (0, 0)),
+                sums,
+                sums,
+                sums,
+            ],
+        ),
+        out_shape=[
+            jax.ShapeDtypeStruct((rows, width), BF16),
+            jax.ShapeDtypeStruct((rows, 3 * wide), BF16),
+            *[jax.ShapeDtypeStruct((length, wide), F32)] * 3,
+        ],
+        compiler_params=pltpu.CompilerParams(vmem_limit_bytes=60 * MIB),
+        cost_estimate=pl.CostEstimate(
+            flops=4 * heads * length * HEAD_DIM * length,
+            bytes_accessed=40 * length * wide,
+            transcendentals=heads * length * rows,
+        ),
+        name="first_block",
+    )(chosen, counts, plan, qkv, memory, memory, grad_out, out, lse, cosine, sine, w_qkv)
+
+
+def other_blocks_kernel(
+    heads, top, chosen_ref, counts_ref, plan_ref, q_ref, k_ref, v_ref, mk_ref, mv_ref, go_ref, out_ref, lse_ref,
+    cos_ref, sin_ref, w_ref, gq_in, gk_in, gv_in, partial_ref, grad_ref, gk_s, gv_s, gq_s,
+):
+    low = plan_ref[0]
+    block = low + pl.num_programs(0) - 1 - pl.program_id(0)
+    rows = q_ref.shape[0]
+    subs = rows // QBLK
+    own = pl.ds(pl.multiple_of(block * rows, rows), rows)
+
+    @pl.when(pl.program_id(0) == 0)
+    def _():
+        gk_s[...] = gk_in[...]
+        gv_s[...] = gv_in[...]
+
+    for head in range(heads):
+        columns = slice(head * HEAD_DIM, (head + 1) * HEAD_DIM)
+        for sub in range(subs):
+            here = slice(sub * QBLK, (sub + 1) * QBLK)
+            gq_s[here, columns] = gq_in[here, columns] + memory_query_grad(
+                chosen_ref, counts_ref, (block * subs + sub) * top, top, q_ref[here, columns], go_ref[here, columns],
+                out_ref[here, columns], lse_ref[here, head : head + 1], mk_ref, mv_ref, columns,
+            )
+
+    def local(there, mask):
+        for head in range(heads):
+            columns = slice(head * HEAD_DIM, (head + 1) * HEAD_DIM)
+            query, grad_out = q_ref[:, columns], go_ref[:, columns]
+            key = k_ref[there, columns]
+            weights, grad_scores = score_grads(
+                query, grad_out, out_ref[:, columns], lse_ref[:, head : head + 1], key, v_ref[there, columns], mask
+            )
+            gk_s[there, columns] += dot(grad_scores, query)
+            gv_s[there, columns] += dot(weights, grad_out)
+            gq_s[:, columns] += dot(grad_scores, key, TN)
+
+    local(own, causal_mask(rows))
+
+    def step(index, carry):
+        local(pl.ds(pl.multiple_of(index * rows, rows), rows), lambda scores: scores)
+        return carry
+
+    lax.fori_loop(low, block, step, 0)
+    grad = block_grads(heads, gq_s[...], gk_s[own, :], gv_s[own, :], cos_ref[...], sin_ref[...])
+    grad_ref[...] = grad
+    partial_ref[...] = dot(grad, w_ref[...], NT).astype(BF16)
+
+
+def other_blocks(plan, chosen, counts, qkv, memory, grad_out, out, lse, cosine, sine, w_qkv, sums, heads, top):
+    length = qkv.shape[0]
+    width = w_qkv.shape[0]
+    wide = heads * HEAD_DIM
+    rows = min(2 * QBLK, length)
+    count = length // rows - 1
+    mem_rows = memory.shape[0]
+
+    def by_rows(columns, at=0):
+        return pl.BlockSpec((rows, columns), lambda i, c, n, plan: (plan[0] + count - 1 - i, at))
+
+    def result(columns):
+        return pl.BlockSpec((rows, columns), lambda i, *_: (count - 1 - i, 0))
+
+    return pl.pallas_call(
+        functools.partial(other_blocks_kernel, heads, top),
+        grid_spec=pltpu.PrefetchScalarGridSpec(
+            num_scalar_prefetch=3,
+            grid=(count,),
+            in_specs=[
+                by_rows(wide),
                 pl.BlockSpec((length, wide), lambda i, *_: (0, 1)),
                 pl.BlockSpec((length, wide), lambda i, *_: (0, 2)),
                 pl.BlockSpec((mem_rows, wide), lambda i, *_: (0, 0)),
                 pl.BlockSpec((mem_rows, wide), lambda i, *_: (0, 1)),
-                pl.BlockSpec((rows, wide), lambda i, *_: (last - i, 0)),
-                pl.BlockSpec((rows, wide), lambda i, *_: (last - i, 0)),
-                pl.BlockSpec((rows, heads), lambda i, *_: (last - i, 0)),
-                pl.BlockSpec((rows, HEAD_DIM), lambda i, *_: (last - i, 0)),
-                pl.BlockSpec((rows, HEAD_DIM), lambda i, *_: (last - i, 0)),
+                by_rows(wide),
+                by_rows(wide),
+                by_rows(heads),
+                by_rows(HEAD_DIM),
+                by_rows(HEAD_DIM),
                 pl.BlockSpec((width, 3 * wide), lambda i, *_: (0, 0)),
+                by_rows(wide),
+                pl.BlockSpec((length, wide), lambda i, *_: (0, 0)),
+                pl.BlockSpec((length, wide), lambda i, *_: (0, 0)),
             ],
-            out_specs=[
-                pl.BlockSpec((rows, width), lambda i, *_: (last - i, 0)),
-                pl.BlockSpec((rows, 3 * wide), lambda i, *_: (last - i, 0)),
-            ],
+            out_specs=[result(width), result(3 * wide)],
             scratch_shapes=[
                 pltpu.VMEM((length, wide), F32),
                 pltpu.VMEM((length, wide), F32),
@@ -305,19 +424,17 @@
             ],
         ),
         out_shape=[
-            jax.ShapeDtypeStruct((length, width), BF16),
-            jax.ShapeDtypeStruct((length, 3 * wide), BF16),
+            jax.ShapeDtypeStruct((count * rows, width), BF16),
+            jax.ShapeDtypeStruct((count * rows, 3 * wide), BF16),
         ],
-        compiler_params=pltpu.CompilerParams(vmem_limit_bytes=48 * MIB),
+        compiler_params=pltpu.CompilerParams(vmem_limit_bytes=60 * MIB),
         cost_estimate=pl.CostEstimate(
-            flops=10 * heads * length * HEAD_DIM * (length // 2 + top * MBLK),
-            bytes_accessed=16 * length * wide,
-            transcendentals=heads * length * (length // 2 + top * MBLK),
-        ),
-        name="attend_backward",
-    )(
-        chosen, counts, qkv, qkv, qkv, memory, memory, grad_out, out, lse, cosine, sine, w_qkv
-    )
+            flops=6 * heads * length * HEAD_DIM * (length + top * MBLK),
+            bytes_accessed=40 * length * wide,
+            transcendentals=heads * length * (length // 3 + top * MBLK),
+        ),
+        name="other_blocks",
+    )(chosen, counts, plan, qkv, qkv, qkv, memory, memory, grad_out, out, lse, cosine, sine, w_qkv, *sums)
 
 
 def ffn_kernel(
@@ -493,7 +610,7 @@
     )(tokens, attended, upstream, gain, weights, weights, weights, w_down)
 
 
-def projection_grads_kernel(tok_ref, gain_ref, w_ref, grad_ref, grad_w_ref, gain_grad_ref, raw_s):
+def projection_grads_kernel(order_ref, tok_ref, gain_ref, w_ref, grad_ref, grad_w_ref, gain_grad_ref, raw_s):
     step = pl.program_id(0)
 
     @pl.when(step == 0)
@@ -511,34 +628,37 @@
         grad_w_ref[...] = (raw * gain_ref[...]).astype(BF16)
 
 
-def projection_grads(tokens_all, gain_column, w_qkv, grad):
+def projection_grads(order, tokens_all, gain_column, w_qkv, grad):
     length, width = tokens_all.shape
     columns = grad.shape[1]
     rows = min(2 * QBLK, length)
     return pl.pallas_call(
         projection_grads_kernel,
-        grid=(length // rows,),
-        in_specs=[
-            pl.BlockSpec((rows, width), lambda i: (i, 0)),
-            pl.BlockSpec((width, 1), lambda i: (0, 0)),
-            pl.BlockSpec((width, columns), lambda i: (0, 0)),
-            pl.BlockSpec((rows, columns), lambda i: (i, 0)),
-        ],
-        out_specs=[
-            pl.BlockSpec((width, columns), lambda i: (0, 0)),
-            pl.BlockSpec((width, 1), lambda i: (0, 0)),
-        ],
+        grid_spec=pltpu.PrefetchScalarGridSpec(
+            num_scalar_prefetch=1,
+            grid=(length // rows,),
+            in_specs=[
+                pl.BlockSpec((rows, width), lambda i, order: (order[i], 0)),
+                pl.BlockSpec((width, 1), lambda i, _: (0, 0)),
+                pl.BlockSpec((width, columns), lambda i, _: (0, 0)),
+                pl.BlockSpec((rows, columns), lambda i, _: (i, 0)),
+            ],
+            out_specs=[
+                pl.BlockSpec((width, columns), lambda i, _: (0, 0)),
+                pl.BlockSpec((width, 1), lambda i, _: (0, 0)),
+            ],
+            scratch_shapes=[pltpu.VMEM((width, columns), F32)],
+        ),
         out_shape=[
             jax.ShapeDtypeStruct((width, columns), BF16),
             jax.ShapeDtypeStruct((width, 1), F32),
         ],
-        scratch_shapes=[pltpu.VMEM((width, columns), F32)],
         compiler_params=pltpu.CompilerParams(vmem_limit_bytes=48 * MIB),
         cost_estimate=pl.CostEstimate(
             flops=2 * length * width * columns, bytes_accessed=2 * length * (width + columns), transcendentals=0
         ),
         name="projection_grads",
-    )(tokens_all, gain_column, w_qkv, grad)
+    )(order, tokens_all, gain_column, w_qkv, grad)
 
 
 def after(value, earlier):
@@ -575,26 +695,29 @@
     return results, steps
 
 
-def chain_scatter(partial, axis):
+def chain_scatter(block, axis):
     size = lax.axis_size(axis)
     place = lax.axis_index(axis)
-    rows = partial.shape[0] // size
-
-    def block(index):
-        return lax.dynamic_slice_in_dim(partial, jnp.clip(index, 0, size - 1) * rows, rows, 0).astype(F32)
-
-    rising = falling = None
-    steps = []
+    arrived = []
     for step in range(size - 1):
-        up, down = block(size - 1 - step + place), block(step - size + 1 + place)
+        up, down = block(step, size - 1 - step + place), block(step, step - size + 1 + place)
         if step:
-            up, down = up + rising.astype(F32), down + falling.astype(F32)
+            up, down = up + arrived[-1][0].astype(F32), down + arrived[-1][1].astype(F32)
         up, down = lax.optimization_barrier((up.astype(BF16), down.astype(BF16)))
         rising = lax.ppermute(up, axis, [(i, i + 1) for i in range(step + 1)])
         falling = lax.ppermute(down, axis, [(i, i - 1) for i in range(size - 1 - step, size)])
-        rising, falling = lax.optimization_barrier((rising, falling))
-        steps.append((rising, falling))
-    return block(place), steps
+        arrived.append(lax.optimization_barrier((rising, falling)))
+    return block(size, place), arrived
+
+
+def direct_exchange(blocks, axis):
+    size = lax.axis_size(axis)
+    place = lax.axis_index(axis)
+    taken = [lax.dynamic_index_in_dim(blocks, place, 0, keepdims=False)]
+    for far in range(1, size):
+        give = lax.dynamic_index_in_dim(blocks, (place + far) % size, 0, keepdims=False)
+        taken.append(lax.ppermute(give, axis, [(i, (i + far) % size) for i in range(size)]))
+    return taken
 
 
 def body(
@@ -628,7 +751,7 @@
     shards = jnp.concatenate([w_out, w_gate, w_up], 1)
     (near, near_down), steps = chain_gather((shards, w_down), "fsdp")
     (gathered,), token_steps = chain_gather((after(mine, steps[-2]),), "fsdp")
-    parcel = lax.all_gather(after(parcel, steps[0]), DP, axis=0, tiled=True)
+    parcel = lax.all_gather(parcel, DP, axis=0, tiled=True)
     w_qkv = parcel[:, :share].reshape(width, 3 * wide)
     gain_one = parcel[:, share, :share].reshape(1, width).astype(F32)
     gain_two = parcel[:, share, share : 2 * share].reshape(1, width).astype(F32)
@@ -653,13 +776,38 @@
     grad_heads = lax.all_to_all(grad_attended, "fsdp", 1, 0, tiled=True)
     grads = lax.psum_scatter(grads, DP, scatter_dimension=0, tiled=True)[0]
 
-    partial, grad_qkv = attend_backward(
-        chosen_all, counts_all, qkv, memory, grad_heads, attended_heads, lse, cosine, sine, w_qkv, heads, top
+    place = lax.axis_index("fsdp").astype(jnp.int32)
+    count = length // min(2 * QBLK, length)
+    is_last = (place < ring // 2).astype(jnp.int32)
+    first_number = jnp.where(is_last == 1, count - 1, 0).astype(jnp.int32)
+    low = 1 - is_last
+    first_partial, first_grad, *sums = first_block(
+        jnp.stack([first_number, is_last]), chosen_all, counts_all, qkv, memory, grad_heads, attended_heads, lse,
+        cosine, sine, w_qkv, heads, top,
     )
-    own_term, steps = chain_scatter(partial, "fsdp")
-    grad_w_qkv, gain_one_grad = projection_grads(gathered, gain_one.reshape(width, 1), w_qkv, grad_qkv)
-    grads = after(grads, steps[-1])
-
+    other_partial, other_grad = other_blocks(
+        low.reshape(1), chosen_all, counts_all, qkv, memory, grad_heads, attended_heads, lse, cosine, sine, w_qkv,
+        sums, heads, top,
+    )
+    grad_qkv = jnp.concatenate([first_grad, other_grad], 0)
+    order = jnp.concatenate([first_number.reshape(1), low + jnp.arange(count - 1, dtype=jnp.int32)])
+    block_rows = first_partial.shape[0]
+
+    def term(step, index):
+        start = jnp.clip(index, 0, ring - 1) * rows
+        at = jnp.clip(start - low * block_rows, 0, other_partial.shape[0] - rows)
+        near = jnp.clip(start - first_number * block_rows, 0, block_rows - rows)
+        from_first = lax.dynamic_slice_in_dim(first_partial, near, rows, 0)
+        if step == 0:
+            return from_first.astype(F32)
+        from_others = lax.dynamic_slice_in_dim(other_partial, at, rows, 0)
+        inside = (start >= first_number * block_rows) & (start < (first_number + 1) * block_rows)
+        return jnp.where(inside, from_first, from_others).astype(F32)
+
+    own_term, arrived = chain_scatter(term, "fsdp")
+    grads = after(grads, arrived[-1])
+
+    grad_w_qkv, gain_one_grad = projection_grads(order, gathered, gain_one.reshape(width, 1), w_qkv, grad_qkv)
     gains = jnp.stack([gain_one_grad.reshape(span, -1), gain_two_grad.reshape(span, -1)], 1)
     gains = jnp.pad(gains.astype(BF16), ((0, 0), (0, extra - 2), (0, 3 * wide - gains.shape[2])))
     late = jnp.concatenate([grad_w_qkv.reshape(span, -1, 3 * wide), gains], 1)
@@ -667,18 +815,8 @@
     core = lax.axis_index("core")
     taken = lax.ppermute(lax.dynamic_index_in_dim(late, 1 - core, 1, keepdims=False), "core", [(0, 1), (1, 0)])
     late = lax.dynamic_index_in_dim(late, core, 1, keepdims=False).astype(F32) + taken.astype(F32)
-    late = after(late.astype(BF16), steps[0])
-    late = jnp.sum(lax.all_to_all(late, "chip", 0, 0, tiled=True).astype(F32), 0).astype(BF16)
-    gains = late[-extra : 2 - extra, : ring * share].reshape(2, ring, share).transpose(1, 0, 2)
-    gains = jnp.pad(gains, ((0, 0), (0, extra - 2), (0, 3 * wide - share)))
-    late = jnp.concatenate([late[:-extra].reshape(ring, share, 3 * wide), gains], 1)
-    late = lax.all_to_all(late, "fsdp", 0, 0, tiled=True).astype(F32)
-    projections = [
-        late[:, :share, part * wide : (part + 1) * wide].transpose(1, 0, 2).reshape(share, width)
-        for part in range(3)
-    ]
-    gain_shares = jnp.sum(late[:, share : share + 2, :share], 0)
-
+    late = after(late.astype(BF16), arrived[0])
+    late = sum(piece.astype(F32) for piece in direct_exchange(late, "chip")).astype(BF16)
     strip = grads.shape[1]
     lanes = width // strip
     tall = w_down.shape[0]
@@ -690,7 +828,7 @@
         grads = grads[ring * tall * lanes :]
     grads = grads.reshape(-1, ring, share, strip).transpose(1, 0, 2, 3)
     pieces = jnp.concatenate([down.reshape(ring, -1, strip), grads.reshape(ring, -1, strip)], 1)
-    rising, falling = steps[-1]
+    rising, falling = arrived[-1]
     grad_normed = own_term + rising.astype(F32) + falling.astype(F32)
     own = mine.astype(F32)
     factor = lax.rsqrt(jnp.mean(own * own, -1, keepdims=True) + EPSILON)
@@ -698,7 +836,18 @@
     inner = jnp.mean(scaled * own, -1, keepdims=True)
     tokens_grad = (grad_middle + factor * scaled - own * (factor * factor * factor * inner)).astype(BF16)
 
-    pieces = lax.psum_scatter(pieces, "fsdp", scatter_dimension=0, tiled=True)[0].astype(F32)
+    gains = late[-extra : 2 - extra, : ring * share].reshape(2, ring, share).transpose(1, 0, 2)
+    gains = jnp.pad(gains, ((0, 0), (0, extra - 2), (0, 3 * wide - share)))
+    late = jnp.concatenate([late[:-extra].reshape(ring, share, 3 * wide), gains], 1)
+    late = after(lax.all_to_all(late, "fsdp", 0, 0, tiled=True), tokens_grad).astype(F32)
+    projections = [
+        late[:, :share, part * wide : (part + 1) * wide].transpose(1, 0, 2).reshape(share, width)
+        for part in range(3)
+    ]
+    gain_shares = jnp.sum(late[:, share : share + 2, :share], 0)
+
+    pieces = lax.psum_scatter(pieces, "fsdp", scatter_dimension=0, tiled=True)
+    pieces = after(pieces, (tokens_grad, projections, gain_shares))[0].astype(F32)
     down_share = pieces[: lanes * tall].reshape(lanes, tall, strip).transpose(1, 0, 2).reshape(tall, width)
     others = pieces[lanes * tall :].reshape(-1, share, strip).transpose(1, 0, 2).reshape(share, -1)
     return (

time: 482 us -> 471 us (0.977)
  waiting for transfers between devices: 190 us -> 163 us
  Pallas kernels: 114 us -> 127 us
  other arithmetic: 36.5 us -> 44.2 us
    ppermute x3, waiting for transfers between devices: 52.3 us -> 28.1 us  [chain_scatter(): rising = lax.ppermute(up, axis, [(i, i + 1) for i in range(step + 1)])]
    pallas_call x2 -> x3, Pallas kernels: 41.8 us -> 54.4 us  [the longest x1 26.4 us: other_blocks(): pl.pallas_call(functools.partial(other_blocks_kernel, heads, top), grid_s...]
    all_to_all x2 -> x1, waiting for transfers between devices: 15.3 us -> 6.56 us  [body(): lax.all_to_all(late, 'fsdp', 0, 0, tiled=True)]
    ppermute x0 -> x3, waiting for transfers between devices: none -> 8.67 us  [direct_exchange(): lax.ppermute(give, axis, [(i, (i + far) % size) for i in range(size)])]
    convert_element_type x2 -> x4, other arithmetic: 0.24 us -> 6.41 us  [the longest x1 3.69 us: body(): (grad_middle + factor * scaled - own * (factor * factor * factor * inner)...]
    ppermute x9, waiting for transfers between devices: 81.3 us -> 75.5 us  [chain_gather(): falling = tuple((lax.ppermute(block, axis, down) for block in falling))]
  transfers between devices with their start and end apart: 35 -> 37, of which waited for: 15 -> 17; matrix products, arithmetic and copies ran while one was open for 11% -> 11% of each run, Pallas kernels for 15% -> 18%
where the time goes in v12:
time: 471 us; the launch traced here: 462 us
  waiting for transfers between devices  163 us (35%)
  Pallas kernels  127 us (27%)
  starting transfers between devices  70 us (15%)
  other arithmetic  44.2 us (9%)
  local copies, waits for them, and re-layouts  27.8 us (6%)
  between operations  14.9 us (3%)
  blocking collectives  14.7 us (3%)
    ppermute x9, waiting for transfers between devices, chain_gather(): falling = tuple((lax.ppermute(block, axis, down) for block in falling))  75.5 us
    pallas_call x1, Pallas kernels, feed_forward(): pl.pallas_call(functools.partial(ffn_kernel, span, merged), grid=(steps,)...  44 us
    ppermute x3, waiting for transfers between devices, chain_scatter(): rising = lax.ppermute(up, axis, [(i, i + 1) for i in range(step + 1)])  28.1 us
    pallas_call x1, Pallas kernels, other_blocks(): pl.pallas_call(functools.partial(other_blocks_kernel, heads, top), grid_s...  26.4 us
    pallas_call x1, Pallas kernels, attend_forward(): pl.pallas_call(functools.partial(forward_kernel, heads, top), grid_spec=p...  21.4 us
    ppermute x9, starting transfers between devices, chain_gather(): rising = tuple((lax.ppermute(block, axis, up) for block in rising))  19.6 us
    pallas_call x1, Pallas kernels, first_block(): pl.pallas_call(functools.partial(first_block_kernel, heads, top), grid_sp...  19.5 us
    all_to_all x1, waiting for transfers between devices, body(): attended = lax.all_to_all(attended_heads, 'fsdp', 0, 1, tiled=True)  15 us
  transfers between devices with their start and end apart: 37, of which 17 were waited for; matrix products, arithmetic and copies ran while one was open for 11% of the time, Pallas kernels for 18%

profile of v12, /device:TPU:0, one launch (start us, length us, event | category | flops | bytes accessed | tf_op | source)
XLA Modules:
  0.0 462.2 jit_solution(7600809728930751524)
XLA Ops:
  12.6 14.7 %all_to_all.53 = bf16[4,40,768]{2,1,0:T(8,128)(2,1)} all-to-all(bf16[4,40,768]{2,1,0:T(8,128)(2,1)S(1)} %copy.66), channel_id=1, replica_groups=mesh['chip'=4,'core'=2,'fsdp'=4] {'fsdp'}, dimensions={0} | all-to-all | bytes 491520 | tf_op jit(solution)/shard_map/all_to_all | solution.py:748
  28.8 4.6 collective-permute-start
  36.8 6.8 %collective-permute-done.1 = bf16[88,1024]{1,0:T(8,128)(2,1)S(1)} collective-permute-done((bf16[88,1024]{1,0:T(8,128)(2,1)S(1)}, bf16[88,1024]{1,0:T(8,128)(2,1)S(1)}, u32[]{:S(2)}, u32[]{:S(2)}) %collective-permute-start.1) | collective-permute-done | bytes 180256 | tf_op jit(solution)/shard_map/ppermute | solution.py:676
  48.3 13.4 %collective-permute-done.7 = bf16[88,1024]{1,0:T(8,128)(2,1)} collective-permute-done((bf16[88,1024]{1,0:T(8,128)(2,1)S(1)}, bf16[88,1024]{1,0:T(8,128)(2,1)}, u32[]{:S(2)}, u32[]{:S(2)}) %collective-permute-start.7) | collective-permute-done | bytes 180256 | tf_op jit(solution)/shard_map/ppermute | solution.py:677
  66.3 10.5 %collective-permute-done.17 = bf16[88,1024]{1,0:T(8,128)(2,1)} collective-permute-done((bf16[88,1024]{1,0:T(8,128)(2,1)}, bf16[88,1024]{1,0:T(8,128)(2,1)}, u32[]{:S(2)}, u32[]{:S(2)}) %collective-permute-start.17) | collective-permute-done | bytes 180256 | tf_op jit(solution)/shard_map/ppermute | solution.py:677
  82.2 5.6 %collective-permute-start.8 = (bf16[512,1024]{1,0:T(8,128)(2,1)S(1)}, bf16[512,1024]{1,0:T(8,128)(2,1)}, u32[]{:S(2)}, u32[]{:S(2)}) collective-permute-start(bf16[512,1024]{1,0:T(8,128)(2,1)S(1)} %bitcast.94), channel_id=1, source_target_pairs={{0,1},{1,2},{2,3},{4,5},{5,6},{6,7},{8,9},{9,10},{10,11},{12,13},{... | collective-permute-start | bytes 3145736 | tf_op jit(solution)/shard_map/ppermute | solution.py:676
  87.7 16.5 %collective-permute-done.11 = bf16[512,1024]{1,0:T(8,128)(2,1)S(1)} collective-permute-done((bf16[512,1024]{1,0:T(8,128)(2,1)S(1)}, bf16[512,1024]{1,0:T(8,128)(2,1)S(1)}, u32[]{:S(2)}, u32[]{:S(2)}) %collective-permute-start.11) | collective-permute-done | bytes 1048608 | tf_op jit(solution)/shard_map/ppermute | solution.py:677
  110.2 17.1 %collective-permute-done.12 = bf16[512,1024]{1,0:T(8,128)(2,1)} collective-permute-done((bf16[512,1024]{1,0:T(8,128)(2,1)S(1)}, bf16[512,1024]{1,0:T(8,128)(2,1)}, u32[]{:S(2)}, u32[]{:S(2)}) %collective-permute-start.12) | collective-permute-done | bytes 1048608 | tf_op jit(solution)/shard_map/ppermute | solution.py:677
  136.4 5.6 %all-to-all-start.1 = ((bf16[4,256,512]{2,1,0:T(8,128)(2,1)}), bf16[4,256,512]{2,1,0:T(8,128)(2,1)}, u32[]{:S(2)}, u32[]{:S(2)}) async-start(bf16[4,256,512]{2,1,0:T(8,128)(2,1)} %pad_maximum_fusion.6), calls=%async_computation.1 | async-start | bytes 2097152 | tf_op jit(solution)/shard_map/all_to_all | solution.py:764
  144.8 18.0 %collective-permute-done.13 = bf16[512,1024]{1,0:T(8,128)(2,1)} collective-permute-done((bf16[512,1024]{1,0:T(8,128)(2,1)}, bf16[512,1024]{1,0:T(8,128)(2,1)}, u32[]{:S(2)}, u32[]{:S(2)}) %collective-permute-start.13) | collective-permute-done | bytes 1048608 | tf_op jit(solution)/shard_map/ppermute | solution.py:677
  167.5 7.4 %project_qkv.1.q_ref.k_ref.v_ref.qkv_ref = bf16[2048,768]{1,0:T(8,128)(2,1)} custom-call(bf16[2048,1024]{1,0:T(8,128)(2,1)} %pad_maximum_fusion.tok_ref, f32[1,1024]{1,0:T(1,128)S(1)} %reshape.198.gain_ref, bf16[1024,768]{1,0:T(8,128)(2,1)S(1)} %bitcast.87, f32[2048,128]{1,0:T(8,128)S(1)} %get-tuple-element.140.cos_ref, f32[2048,128]{1,0:T(8,128)S(1)} %copy-done.3), custom_call_target="tpu_custom_call" | custom-call | flops 3221225472 | bytes 14680064 | tf_op jit(solution)/shard_map/project_qkv/pallas_call | solution.py:62
  174.9 21.4 %attend_forward.1 = (bf16[2048,256]{1,0:T(8,128)(2,1)}, f32[2048,2]{1,0:T(8,128)S(1)}) custom-call(s32[32]{0:T(128)S(1)} %reshape_squeeze.24.chosen_ref, s32[32]{0:T(128)S(1)} %reshape_squeeze.25.counts_ref, bf16[2048,768]{1,0:T(8,128)(2,1)} %project_qkv.1.q_ref.k_ref.v_ref.qkv_ref, bf16[2048,768]{1,0:T(8,128)(2,1)} %project_qkv.1.q_ref.k_ref.v_ref.qkv_ref, ...), custom_call_target="tpu_custom_call" | custom-call | flops 3221225472 | bytes 4194304 | tf_op jit(solution)/shard_map/attend_forward/pallas_call | solution.py:157
  202.7 15.0 %all-to-all-done.2 = bf16[4,512,256]{2,1,0:T(8,128)(2,1)S(1)} async-done(((bf16[4,512,256]{2,1,0:T(8,128)(2,1)}), bf16[4,512,256]{2,1,0:T(8,128)(2,1)S(1)}, u32[]{:S(2)}, u32[]{:S(2)}) %all-to-all-start.2) | async-done | bytes 1048608 | tf_op jit(solution)/shard_map/all_to_all | solution.py:770
  218.9 44.0 %feed_forward.1 = (bf16[512,1024]{1,0:T(8,128)(2,1)}, f32[512,1024]{1,0:T(8,128)}, bf16[512,1024]{1,0:T(8,128)(2,1)}, f32[1,1024]{1,0:T(1,128)}, bf16[8,4736,256]{2,1,0:T(8,128)(2,1)}) custom-call(bf16[512,1024]{1,0:T(8,128)(2,1)} %bitcast.92, bf16[512,1024]{1,0:T(8,128)(2,1)} %bitcast.110, bf16[512,1024]{1,0:T(8,128)(2,1)} %bitcast.125, ...), custom_call_target="tpu_custom_call" | custom-call | flops 29796335616 | bytes 38797312 | tf_op jit(solution)/shard_map/feed_forward/pallas_call | solution.py:575
  269.8 14.8 %all-to-all-done.3 = bf16[512,4,256]{2,0,1:T(8,128)(2,1)S(1)} async-done(((bf16[512,4,256]{2,0,1:T(8,128)(2,1)}), bf16[512,4,256]{2,0,1:T(8,128)(2,1)S(1)}, u32[]{:S(2)}, u32[]{:S(2)}) %all-to-all-start.3) | async-done | bytes 1048608 | tf_op jit(solution)/shard_map/all_to_all | solution.py:776
  285.6 19.5 %first_block.1 = (bf16[512,1024]{1,0:T(8,128)(2,1)}, bf16[512,768]{1,0:T(8,128)(2,1)}, f32[2048,256]{1,0:T(8,128)}, f32[2048,256]{1,0:T(8,128)}, f32[2048,256]{1,0:T(8,128)}) custom-call(s32[32]{0:T(128)} %copy-done.5, s32[32]{0:T(128)} %copy-done.4, s32[2]{0:T(128)} %pad_add_fusion.plan_ref, bf16[2048,768]{1,0:T(8,128)(2,1)} %project_qkv.1.q_ref.k_ref.v_ref.qkv_ref, ...), custom_call_target="tpu_custom_call" | custom-call | flops 4294967296 | bytes 20971520 | tf_op jit(solution)/shard_map/first_block/pallas_call | solution.py:297
  307.5 26.4 %other_blocks.1 = (bf16[1536,1024]{1,0:T(8,128)(2,1)}, bf16[1536,768]{1,0:T(8,128)(2,1)}) custom-call(s32[32]{0:T(128)} %copy-done.5, s32[32]{0:T(128)} %copy-done.4, s32[1]{0:T(128)} %bitcast.16.plan_ref, bf16[2048,768]{1,0:T(8,128)(2,1)} %project_qkv.1.q_ref.k_ref.v_ref.qkv_ref, bf16[2048,768]{1,0:T(8,128)(2,1)} %project_qkv.1.q_ref.k_ref.v_ref.qkv_ref, ...), custom_call_target="tpu_custom_call" | custom-call | flops 8053063680 | bytes 20971520 | tf_op jit(solution)/shard_map/other_blocks/pallas_call | solution.py:398
  340.7 18.6 %collective-permute-done.20 = bf16[512,1024]{1,0:T(8,128)(2,1)S(1)} collective-permute-done((bf16[512,1024]{1,0:T(8,128)(2,1)}, bf16[512,1024]{1,0:T(8,128)(2,1)S(1)}, u32[]{:S(2)}, u32[]{:S(2)}) %collective-permute-start.20) | collective-permute-done | bytes 1048608 | tf_op jit(solution)/shard_map/ppermute | solution.py:707
  363.4 9.0 %collective-permute-start.22 = (bf16[512,1024]{1,0:T(8,128)(2,1)}, bf16[512,1024]{1,0:T(8,128)(2,1)S(1)}, u32[]{:S(2)}, u32[]{:S(2)}) collective-permute-start(bf16[512,1024]{1,0:T(8,128)(2,1)} %get-tuple-element.89), channel_id=1, source_target_pairs={{0,1},{1,2},{2,3},{4,5},{5,6},{6,7},{8,9},{9,10},{10,11},{12,13},{... | collective-permute-start | bytes 3145736 | tf_op jit(solution)/shard_map/ppermute | solution.py:707
  375.5 9.5 %collective-permute-done.22 = bf16[512,1024]{1,0:T(8,128)(2,1)S(1)} collective-permute-done((bf16[512,1024]{1,0:T(8,128)(2,1)}, bf16[512,1024]{1,0:T(8,128)(2,1)S(1)}, u32[]{:S(2)}, u32[]{:S(2)}) %collective-permute-start.22) | collective-permute-done | bytes 1048608 | tf_op jit(solution)/shard_map/ppermute | solution.py:707
  400.0 8.5 %projection_grads.1 = (bf16[1024,768]{1,0:T(8,128)(2,1)S(1)}, f32[1024,1]{1,0:T(8,128)S(1)}) custom-call(s32[4]{0:T(128)S(1)} %pad_add_fusion.1.order_ref, bf16[2048,1024]{1,0:T(8,128)(2,1)} %pad_maximum_fusion.tok_ref, f32[1024,1]{1,0:T(8,128)S(1)} %reshape.204.gain_ref, bf16[1024,768]{1,0:T(8,128)(2,1)S(1)} %bitcast.90, ...), custom_call_target="tpu_custom_call" | custom-call | flops 3221225472 | bytes 7340032 | tf_op jit(solution)/shard_map/projection_grads/pallas_call | solution.py:635
  419.8 5.0 %collective-permute-done.25 = bf16[136,768]{1,0:T(8,128)(2,1)} collective-permute-done((bf16[136,768]{1,0:T(8,128)(2,1)}, bf16[136,768]{1,0:T(8,128)(2,1)}, u32[]{:S(2)}, u32[]{:S(2)}) %collective-permute-start.25) | collective-permute-done | bytes 208928 | tf_op jit(solution)/shard_map/ppermute | solution.py:719
  430.7 4.6 all-to-all-start.4
  441.9 6.6 %all-to-all-done.4 = bf16[4,40,768]{2,1,0:T(8,128)(2,1)S(1)} async-done(((bf16[4,40,768]{2,1,0:T(8,128)(2,1)}), bf16[4,40,768]{2,1,0:T(8,128)(2,1)S(1)}, u32[]{:S(2)}, u32[]{:S(2)}) %all-to-all-start.4) | async-done | bytes 245792 | tf_op jit(solution)/shard_map/all_to_all | solution.py:842
  (198 shorter events, 124.3 us)
Async XLA Ops:
  7.2 134.9 %all-gather.4.cloned.1.call-start = ((), (), s32[]{:S(2)}) async-start(), calls=%async_computation.7 | async-start | bytes 2211840 | tf_op jit(solution)/shard_map/all_gather | solution.py:754
  27.4 191.5 %all-gather.8.cloned.1.call-start = ((), (), s32[]{:S(2)}) async-start(), calls=%async_computation.9 | async-start | bytes 6488064 | tf_op jit(solution)/shard_map/all_gather | solution.py:765
  27.5 16.2 %collective-permute-start.2 = (bf16[32,6656]{1,0:T(8,128)(2,1)S(1)}, bf16[32,6656]{1,0:T(8,128)(2,1)S(1)}, u32[]{:S(2)}, u32[]{:S(2)}) collective-permute-start(bf16[32,6656]{1,0:T(8,128)(2,1)S(1)} %constant_dynamic-update-slice_fusion), channel_id=1, source_target_pairs={{1,0},{2,1},{3,2},{5,4},{6,5},{7,6},{9,8},{10,9},{11,10},{13,12},{... | collective-permute-start | bytes 1277960 | tf_op jit(solution)/shard_map/ppermute | solution.py:677
  43.7 18.0 %collective-permute-start.4 = (bf16[32,6656]{1,0:T(8,128)(2,1)S(1)}, bf16[32,6656]{1,0:T(8,128)(2,1)S(1)}, u32[]{:S(2)}, u32[]{:S(2)}) collective-permute-start(bf16[32,6656]{1,0:T(8,128)(2,1)S(1)} %collective-permute-done), channel_id=1, source_target_pairs={{1,2},{2,3},{5,6},{6,7},{9,10},{10,11},{13,14},{14,15},{17,18},{18... | collective-permute-start | bytes 1277960 | tf_op jit(solution)/shard_map/ppermute | solution.py:676
  44.4 17.3 %collective-permute-start.6 = (bf16[32,6656]{1,0:T(8,128)(2,1)S(1)}, bf16[32,6656]{1,0:T(8,128)(2,1)S(1)}, u32[]{:S(2)}, u32[]{:S(2)}) collective-permute-start(bf16[32,6656]{1,0:T(8,128)(2,1)S(1)} %collective-permute-done.2), channel_id=1, source_target_pairs={{1,0},{2,1},{5,4},{6,5},{9,8},{10,9},{13,12},{14,13},{17,16},{18,1... | collective-permute-start | bytes 1277960 | tf_op jit(solution)/shard_map/ppermute | solution.py:677
  79.0 139.8 %all-gather.6.cloned.1.call-start = ((), (), s32[]{:S(2)}) async-start(), calls=%async_computation.8 | async-start | bytes 15335424 | tf_op jit(solution)/shard_map/all_gather | solution.py:758
  80.9 23.3 %collective-permute-start.11 = (bf16[512,1024]{1,0:T(8,128)(2,1)S(1)}, bf16[512,1024]{1,0:T(8,128)(2,1)S(1)}, u32[]{:S(2)}, u32[]{:S(2)}) collective-permute-start(bf16[512,1024]{1,0:T(8,128)(2,1)S(1)} %bitcast.93), channel_id=1, source_target_pairs={{1,0},{2,1},{3,2},{5,4},{6,5},{7,6},{9,8},{10,9},{11,10},{13,12},{... | collective-permute-start | bytes 3145736 | tf_op jit(solution)/shard_map/ppermute | solution.py:677
  82.2 23.3 %collective-permute-start.8 = (bf16[512,1024]{1,0:T(8,128)(2,1)S(1)}, bf16[512,1024]{1,0:T(8,128)(2,1)}, u32[]{:S(2)}, u32[]{:S(2)}) collective-permute-start(bf16[512,1024]{1,0:T(8,128)(2,1)S(1)} %bitcast.94), channel_id=1, source_target_pairs={{0,1},{1,2},{2,3},{4,5},{5,6},{6,7},{8,9},{9,10},{10,11},{12,13},{... | collective-permute-start | bytes 3145736 | tf_op jit(solution)/shard_map/ppermute | solution.py:676
  104.2 23.1 %collective-permute-start.12 = (bf16[512,1024]{1,0:T(8,128)(2,1)S(1)}, bf16[512,1024]{1,0:T(8,128)(2,1)}, u32[]{:S(2)}, u32[]{:S(2)}) collective-permute-start(bf16[512,1024]{1,0:T(8,128)(2,1)S(1)} %collective-permute-done.11), channel_id=1, source_target_pairs={{1,0},{2,1},{5,4},{6,5},{9,8},{10,9},{13,12},{14,13},{17,16},{18,1... | collective-permute-start | bytes 3145736 | tf_op jit(solution)/shard_map/ppermute | solution.py:677
  105.5 23.1 %collective-permute-start.9 = (bf16[512,1024]{1,0:T(8,128)(2,1)}, bf16[512,1024]{1,0:T(8,128)(2,1)}, u32[]{:S(2)}, u32[]{:S(2)}) collective-permute-start(bf16[512,1024]{1,0:T(8,128)(2,1)} %collective-permute-done.8), channel_id=1, source_target_pairs={{1,2},{2,3},{5,6},{6,7},{9,10},{10,11},{13,14},{14,15},{17,18},{18... | collective-permute-start | bytes 3145736 | tf_op jit(solution)/shard_map/ppermute | solution.py:676
  127.3 35.5 %collective-permute-start.13 = (bf16[512,1024]{1,0:T(8,128)(2,1)}, bf16[512,1024]{1,0:T(8,128)(2,1)}, u32[]{:S(2)}, u32[]{:S(2)}) collective-permute-start(bf16[512,1024]{1,0:T(8,128)(2,1)} %collective-permute-done.12), channel_id=1, source_target_pairs={{1,0},{5,4},{9,8},{13,12},{17,16},{21,20},{25,24},{29,28}} | collective-permute-start | bytes 3145736 | tf_op jit(solution)/shard_map/ppermute | solution.py:677
  128.6 34.2 %collective-permute-start.10 = (bf16[512,1024]{1,0:T(8,128)(2,1)}, bf16[512,1024]{1,0:T(8,128)(2,1)}, u32[]{:S(2)}, u32[]{:S(2)}) collective-permute-start(bf16[512,1024]{1,0:T(8,128)(2,1)} %collective-permute-done.9), channel_id=1, source_target_pairs={{2,3},{6,7},{10,11},{14,15},{18,19},{22,23},{26,27},{30,31}} | collective-permute-start | bytes 3145736 | tf_op jit(solution)/shard_map/ppermute | solution.py:676
  136.4 38.5 %all-to-all-start.1 = ((bf16[4,256,512]{2,1,0:T(8,128)(2,1)}), bf16[4,256,512]{2,1,0:T(8,128)(2,1)}, u32[]{:S(2)}, u32[]{:S(2)}) async-start(bf16[4,256,512]{2,1,0:T(8,128)(2,1)} %pad_maximum_fusion.6), calls=%async_computation.1 | async-start | bytes 2097152 | tf_op jit(solution)/shard_map/all_to_all | solution.py:764
  197.3 20.5 %all-to-all-start.2 = ((bf16[4,512,256]{2,1,0:T(8,128)(2,1)}), bf16[4,512,256]{2,1,0:T(8,128)(2,1)S(1)}, u32[]{:S(2)}, u32[]{:S(2)}) async-start(bf16[4,512,256]{2,1,0:T(8,128)(2,1)} %bitcast.8), calls=%async_computation.2 | async-start | bytes 2097152 | tf_op jit(solution)/shard_map/all_to_all | solution.py:770
  201.8 188.8 %reduce-scatter.3.cloned.1.call-start = ((), (), s32[]{:S(2)}) async-start(), calls=%async_computation.10 | async-start | bytes 21823488 | tf_op jit(solution)/shard_map/reduce_scatter | solution.py:777
  265.1 19.5 %all-to-all-start.3 = ((bf16[512,4,256]{2,0,1:T(8,128)(2,1)}), bf16[512,4,256]{2,0,1:T(8,128)(2,1)S(1)}, u32[]{:S(2)}, u32[]{:S(2)}) async-start(bf16[512,4,256]{2,0,1:T(8,128)(2,1)} %bitcast.86), calls=%async_computation.3 | async-start | bytes 2097152 | tf_op jit(solution)/shard_map/all_to_all | solution.py:776
  268.7 182.3 %reduce-scatter.5.cloned.1.call-start = ((), (), s32[]{:S(2)}) async-start(), calls=%async_computation.11 | async-start | bytes 3031040 | tf_op jit(solution)/shard_map/reduce_scatter | solution.py:849
  305.1 28.8 %collective-permute-start.18 = (bf16[512,1024]{1,0:T(8,128)(2,1)}, bf16[512,1024]{1,0:T(8,128)(2,1)S(1)}, u32[]{:S(2)}, u32[]{:S(2)}) collective-permute-start(bf16[512,1024]{1,0:T(8,128)(2,1)} %get-tuple-element.82), channel_id=1, source_target_pairs={{0,1},{4,5},{8,9},{12,13},{16,17},{20,21},{24,25},{28,29}} | collective-permute-start | bytes 3145736 | tf_op jit(solution)/shard_map/ppermute | solution.py:707
  306.6 27.3 %collective-permute-start.19 = (bf16[512,1024]{1,0:T(8,128)(2,1)}, bf16[512,1024]{1,0:T(8,128)(2,1)S(1)}, u32[]{:S(2)}, u32[]{:S(2)}) collective-permute-start(bf16[512,1024]{1,0:T(8,128)(2,1)} %get-tuple-element.82), channel_id=1, source_target_pairs={{3,2},{7,6},{11,10},{15,14},{19,18},{23,22},{27,26},{31,30}} | collective-permute-start | bytes 3145736 | tf_op jit(solution)/shard_map/ppermute | solution.py:708
  338.1 21.1 %collective-permute-start.20 = (bf16[512,1024]{1,0:T(8,128)(2,1)}, bf16[512,1024]{1,0:T(8,128)(2,1)S(1)}, u32[]{:S(2)}, u32[]{:S(2)}) collective-permute-start(bf16[512,1024]{1,0:T(8,128)(2,1)} %get-tuple-element.85), channel_id=1, source_target_pairs={{0,1},{1,2},{4,5},{5,6},{8,9},{9,10},{12,13},{13,14},{16,17},{17,1... | collective-permute-start | bytes 3145736 | tf_op jit(solution)/shard_map/ppermute | solution.py:707
  339.9 19.3 %collective-permute-start.21 = (bf16[512,1024]{1,0:T(8,128)(2,1)}, bf16[512,1024]{1,0:T(8,128)(2,1)S(1)}, u32[]{:S(2)}, u32[]{:S(2)}) collective-permute-start(bf16[512,1024]{1,0:T(8,128)(2,1)} %get-tuple-element.86), channel_id=1, source_target_pairs={{2,1},{3,2},{6,5},{7,6},{10,9},{11,10},{14,13},{15,14},{18,17},{19... | collective-permute-start | bytes 3145736 | tf_op jit(solution)/shard_map/ppermute | solution.py:708
  363.4 21.6 %collective-permute-start.22 = (bf16[512,1024]{1,0:T(8,128)(2,1)}, bf16[512,1024]{1,0:T(8,128)(2,1)S(1)}, u32[]{:S(2)}, u32[]{:S(2)}) collective-permute-start(bf16[512,1024]{1,0:T(8,128)(2,1)} %get-tuple-element.89), channel_id=1, source_target_pairs={{0,1},{1,2},{2,3},{4,5},{5,6},{6,7},{8,9},{9,10},{10,11},{12,13},{... | collective-permute-start | bytes 3145736 | tf_op jit(solution)/shard_map/ppermute | solution.py:707
  372.5 17.0 %collective-permute-start.23 = (bf16[512,1024]{1,0:T(8,128)(2,1)}, bf16[512,1024]{1,0:T(8,128)(2,1)}, u32[]{:S(2)}, u32[]{:S(2)}) collective-permute-start(bf16[512,1024]{1,0:T(8,128)(2,1)} %get-tuple-element.90), channel_id=1, source_target_pairs={{1,0},{2,1},{3,2},{5,4},{6,5},{7,6},{9,8},{10,9},{11,10},{13,12},{... | collective-permute-start | bytes 3145736 | tf_op jit(solution)/shard_map/ppermute | solution.py:708
  430.7 17.7 %all-to-all-start.4 = ((bf16[4,40,768]{2,1,0:T(8,128)(2,1)}), bf16[4,40,768]{2,1,0:T(8,128)(2,1)S(1)}, u32[]{:S(2)}, u32[]{:S(2)}) async-start(bf16[4,40,768]{2,1,0:T(8,128)(2,1)} %fusion.10), calls=%async_computation.4 | async-start | bytes 491520 | tf_op jit(solution)/shard_map/all_to_all | solution.py:842
  (37 other events, 490.5 us)
Sparse Core Ops, SparseCore 0:
  27.5 26.4 all-gather.3
  79.1 41.5 all-gather.7
  122.6 76.5 all-gather.5
  263.0 127.5 reduce-scatter.2
  395.3 51.9 reduce-scatter.4

commit v13 on v12

--- a/solution.py
+++ b/solution.py
@@ -37,8 +37,31 @@
     return jnp.concatenate([cosine, cosine], 1), jnp.concatenate([-sine, sine], 1)
 
 
-def qkv_kernel(heads, tok_ref, gain_ref, w_ref, cos_ref, sin_ref, qkv_ref):
-    rows = tok_ref[...].astype(F32)
+def qkv_kernel(heads, count, which_ref, gain_ref, w_ref, cos_ref, sin_ref, *refs):
+    sources = refs[:count]
+    qkv_ref, tokens_ref, held, sems = refs[count:]
+    step, steps = pl.program_id(0), pl.num_programs(0)
+    slot = step % 2
+
+    def fetch(index, place):
+        for number, source in enumerate(sources):
+
+            @pl.when(which_ref[index] == number)
+            def _():
+                pltpu.make_async_copy(source, held.at[place], sems.at[place]).start()
+
+    @pl.when(step == 0)
+    def _():
+        fetch(0, 0)
+
+    @pl.when(step + 1 < steps)
+    def _():
+        fetch(step + 1, 1 - slot)
+
+    pltpu.make_async_copy(sources[0], held.at[slot], sems.at[slot]).wait()
+    tokens = held[slot]
+    tokens_ref[...] = tokens
+    rows = tokens.astype(F32)
     factor = lax.rsqrt(jnp.mean(rows * rows, -1, keepdims=True) + EPSILON)
     normed = (rows * factor * gain_ref[...]).astype(BF16)
     cosine, sine = cos_ref[...], sin_ref[...]
@@ -55,28 +78,39 @@
             qkv_ref[:, at : at + HEAD_DIM] = value.astype(BF16)
 
 
-def project_qkv(tokens_all, gain, w_qkv, cosine, sine, heads):
-    length, width = tokens_all.shape
+def project_qkv(which, blocks, gain, w_qkv, cosine, sine, heads):
+    rows, width = blocks[0].shape
     columns = w_qkv.shape[1]
-    block = 2 * QBLK
+    size = which.shape[0]
+    length = size * rows
     return pl.pallas_call(
-        functools.partial(qkv_kernel, heads),
-        grid=(length // block,),
-        in_specs=[
-            pl.BlockSpec((block, width), lambda i: (i, 0)),
-            pl.BlockSpec((1, width), lambda i: (0, 0)),
-            pl.BlockSpec((width, columns), lambda i: (0, 0)),
-            pl.BlockSpec((block, HEAD_DIM), lambda i: (i, 0)),
-            pl.BlockSpec((block, HEAD_DIM), lambda i: (i, 0)),
+        functools.partial(qkv_kernel, heads, len(blocks)),
+        grid_spec=pltpu.PrefetchScalarGridSpec(
+            num_scalar_prefetch=1,
+            grid=(size,),
+            in_specs=[
+                pl.BlockSpec((1, width), lambda i, _: (0, 0)),
+                pl.BlockSpec((width, columns), lambda i, _: (0, 0)),
+                pl.BlockSpec((rows, HEAD_DIM), lambda i, _: (i, 0)),
+                pl.BlockSpec((rows, HEAD_DIM), lambda i, _: (i, 0)),
+                *[pl.BlockSpec(memory_space=pl.ANY) for _ in blocks],
+            ],
+            out_specs=[
+                pl.BlockSpec((rows, columns), lambda i, _: (i, 0)),
+                pl.BlockSpec((rows, width), lambda i, _: (i, 0)),
+            ],
+            scratch_shapes=[pltpu.VMEM((2, rows, width), BF16), pltpu.SemaphoreType.DMA((2,))],
+        ),
+        out_shape=[
+            jax.ShapeDtypeStruct((length, columns), BF16),
+            jax.ShapeDtypeStruct((length, width), BF16),
         ],
-        out_specs=pl.BlockSpec((block, columns), lambda i: (i, 0)),
-        out_shape=jax.ShapeDtypeStruct((length, columns), BF16),
-        compiler_params=pltpu.CompilerParams(vmem_limit_bytes=48 * MIB),
+        compiler_params=pltpu.CompilerParams(vmem_limit_bytes=60 * MIB),
         cost_estimate=pl.CostEstimate(
             flops=2 * length * width * columns, bytes_accessed=4 * length * (width + columns), transcendentals=0
         ),
         name="project_qkv",
-    )(tokens_all, gain, w_qkv, cosine, sine)
+    )(which, gain, w_qkv, cosine, sine, *blocks)
 
 
 def memory_bias(counts_ref, base, top, axis):
@@ -277,7 +311,7 @@
 
     lax.fori_loop(0, others, step, 0)
     grad = block_grads(
-        heads, gq_ref[own, :], gk_ref[own, :], gv_ref[own, :], cos_ref[own, :], sin_ref[own, :]
+        heads, gq_ref[own, :], gk_ref[own, :], gv_ref[own, :], cos_ref[...], sin_ref[...]
     )
     grad_ref[...] = grad
     partial_ref[...] = dot(grad, w_ref[...], NT).astype(BF16)
@@ -306,8 +340,8 @@
                 whole(grad_out),
                 whole(out),
                 whole(lse),
-                whole(cosine),
-                whole(sine),
+                pl.BlockSpec((rows, HEAD_DIM), lambda i, c, n, plan: (plan[0], 0)),
+                pl.BlockSpec((rows, HEAD_DIM), lambda i, c, n, plan: (plan[0], 0)),
                 whole(w_qkv),
             ],
             out_specs=[
@@ -750,13 +784,12 @@
     chosen_all, counts_all = picks[:, 0].reshape(-1), picks[:, 1].reshape(-1)
     shards = jnp.concatenate([w_out, w_gate, w_up], 1)
     (near, near_down), steps = chain_gather((shards, w_down), "fsdp")
-    (gathered,), token_steps = chain_gather((after(mine, steps[-2]),), "fsdp")
-    parcel = lax.all_gather(parcel, DP, axis=0, tiled=True)
+    _, token_steps = chain_gather((after(mine, steps[-2]),), "fsdp")
+    parcel = lax.all_gather(after(parcel, steps[0]), DP, axis=0, tiled=True)
     w_qkv = parcel[:, :share].reshape(width, 3 * wide)
     gain_one = parcel[:, share, :share].reshape(1, width).astype(F32)
     gain_two = parcel[:, share, share : 2 * share].reshape(1, width).astype(F32)
     first = lax.all_gather(jnp.concatenate(near, 0), DP, axis=0, tiled=True)
-    gathered = jnp.concatenate(gathered, 0)
 
     memory = jnp.concatenate(
         [m[0].reshape(-1, ring, wide).transpose(1, 0, 2) for m in (memory_keys, memory_values)], 2
@@ -765,7 +798,11 @@
     down_full = lax.all_gather(jnp.concatenate(near_down, 0), DP, axis=0, tiled=True)
 
     cosine, sine = rotary_tables(length)
-    qkv = project_qkv(gathered, gain_one, w_qkv, cosine, sine, heads)
+    place = lax.axis_index("fsdp").astype(jnp.int32)
+    spots = jnp.arange(ring, dtype=jnp.int32)
+    which = jnp.where(spots <= place, place - spots, ring - 1 + spots - place)
+    arrivals = [mine, *[step[0][0] for step in token_steps], *[step[1][0] for step in token_steps]]
+    qkv, gathered = project_qkv(which, arrivals, gain_one, w_qkv, cosine, sine, heads)
     attended_heads, lse = attend_forward(chosen_all, counts_all, qkv, memory, heads, top)
     attended = lax.all_to_all(attended_heads, "fsdp", 0, 1, tiled=True)
 
@@ -776,7 +813,6 @@
     grad_heads = lax.all_to_all(grad_attended, "fsdp", 1, 0, tiled=True)
     grads = lax.psum_scatter(grads, DP, scatter_dimension=0, tiled=True)[0]
 
-    place = lax.axis_index("fsdp").astype(jnp.int32)
     count = length // min(2 * QBLK, length)
     is_last = (place < ring // 2).astype(jnp.int32)
     first_number = jnp.where(is_last == 1, count - 1, 0).astype(jnp.int32)

time: 471 us -> 483 us (1.025)
  waiting for transfers between devices: 163 us -> 190 us
  blocking collectives: 14.7 us -> 0 us
  local copies, waits for them, and re-layouts: 27.8 us -> 33.8 us
    all_to_all x1 -> x0, blocking collectives: 14.7 us -> none  [body(): parcel = lax.all_to_all(parcel, 'fsdp', 0, 0, tiled=True)]
    ppermute x3, waiting for transfers between devices: 28.1 us -> 39.3 us  [chain_scatter(): rising = lax.ppermute(up, axis, [(i, i + 1) for i in range(step + 1)])]
    all_to_all x1, waiting for transfers between devices: 14.8 us -> 22.8 us  [body(): grad_heads = lax.all_to_all(grad_attended, 'fsdp', 1, 0, tiled=True)]
    ppermute x9, waiting for transfers between devices: 75.5 us -> 83.3 us  [chain_gather(): falling = tuple((lax.ppermute(block, axis, down) for block in falling))]
    all_to_all x1, waiting for transfers between devices: 15 us -> 21 us  [body(): attended = lax.all_to_all(attended_heads, 'fsdp', 0, 1, tiled=True)]
  transfers between devices with their start and end apart: 37 -> 38, of which waited for: 17 -> 16; matrix products, arithmetic and copies ran while one was open for 11% -> 11% of each run, Pallas kernels for 18% -> 17%
where the time goes in v13:
time: 483 us; the launch traced here: 477 us
  waiting for transfers between devices  190 us (39%)
  Pallas kernels  127 us (26%)
  starting transfers between devices  71.4 us (15%)
  other arithmetic  40.7 us (8%)
  local copies, waits for them, and re-layouts  33.8 us (7%)
  between operations  14.8 us (3%)
    ppermute x9, waiting for transfers between devices, chain_gather(): falling = tuple((lax.ppermute(block, axis, down) for block in falling))  83.3 us
    pallas_call x1, Pallas kernels, feed_forward(): pl.pallas_call(functools.partial(ffn_kernel, span, merged), grid=(steps,)...  44 us
    ppermute x3, waiting for transfers between devices, chain_scatter(): rising = lax.ppermute(up, axis, [(i, i + 1) for i in range(step + 1)])  39.3 us
    pallas_call x1, Pallas kernels, other_blocks(): pl.pallas_call(functools.partial(other_blocks_kernel, heads, top), grid_s...  26.4 us
    all_to_all x1, waiting for transfers between devices, body(): grad_heads = lax.all_to_all(grad_attended, 'fsdp', 1, 0, tiled=True)  22.8 us
    ppermute x9, starting transfers between devices, chain_gather(): rising = tuple((lax.ppermute(block, axis, up) for block in rising))  21.6 us
    pallas_call x1, Pallas kernels, attend_forward(): pl.pallas_call(functools.partial(forward_kernel, heads, top), grid_spec=p...  21.2 us
    all_to_all x1, waiting for transfers between devices, body(): attended = lax.all_to_all(attended_heads, 'fsdp', 0, 1, tiled=True)  21 us
  transfers between devices with their start and end apart: 38, of which 16 were waited for; matrix products, arithmetic and copies ran while one was open for 11% of the time, Pallas kernels for 17%

profile of v13, /device:TPU:0, one launch (start us, length us, event | category | flops | bytes accessed | tf_op | source)
XLA Modules:
  0.0 477.1 jit_solution(16574302819409238924)
XLA Ops:
  11.2 5.6 %collective-permute-start = (bf16[32,6656]{1,0:T(8,128)(2,1)S(1)}, bf16[32,6656]{1,0:T(8,128)(2,1)S(1)}, u32[]{:S(2)}, u32[]{:S(2)}) collective-permute-start(bf16[32,6656]{1,0:T(8,128)(2,1)S(1)} %constant_dynamic-update-slice_fusion), channel_id=1, source_target_pairs={{0,1},{1,2},{2,3},{4,5},{5,6},{6,7},{8,9},{9,10},{10,11},{12,13},{... | collective-permute-start | bytes 1277960 | tf_op jit(solution)/shard_map/ppermute | solution.py:710
  22.7 4.3 all-to-all-start
  43.8 13.9 %collective-permute-done.7 = bf16[88,1024]{1,0:T(8,128)(2,1)} collective-permute-done((bf16[88,1024]{1,0:T(8,128)(2,1)S(1)}, bf16[88,1024]{1,0:T(8,128)(2,1)}, u32[]{:S(2)}, u32[]{:S(2)}) %collective-permute-start.7) | collective-permute-done | bytes 180256 | tf_op jit(solution)/shard_map/ppermute | solution.py:711
  62.3 10.7 %collective-permute-done.17 = bf16[88,1024]{1,0:T(8,128)(2,1)} collective-permute-done((bf16[88,1024]{1,0:T(8,128)(2,1)}, bf16[88,1024]{1,0:T(8,128)(2,1)}, u32[]{:S(2)}, u32[]{:S(2)}) %collective-permute-start.17) | collective-permute-done | bytes 180256 | tf_op jit(solution)/shard_map/ppermute | solution.py:711
  78.3 5.5 %collective-permute-start.8 = (bf16[512,1024]{1,0:T(8,128)(2,1)S(1)}, bf16[512,1024]{1,0:T(8,128)(2,1)}, u32[]{:S(2)}, u32[]{:S(2)}) collective-permute-start(bf16[512,1024]{1,0:T(8,128)(2,1)S(1)} %bitcast.103), channel_id=1, source_target_pairs={{0,1},{1,2},{2,3},{4,5},{5,6},{6,7},{8,9},{9,10},{10,11},{12,13},{... | collective-permute-start | bytes 3145736 | tf_op jit(solution)/shard_map/ppermute | solution.py:710
  83.9 16.5 %collective-permute-done.11.refs_4_ = bf16[512,1024]{1,0:T(8,128)(2,1)S(1)} collective-permute-done((bf16[512,1024]{1,0:T(8,128)(2,1)S(1)}, bf16[512,1024]{1,0:T(8,128)(2,1)S(1)}, u32[]{:S(2)}, u32[]{:S(2)}) %collective-permute-start.11) | collective-permute-done | bytes 1048608 | tf_op jit(solution)/shard_map/ppermute | solution.py:711
  105.9 16.7 %collective-permute-done.12.refs_5_ = bf16[512,1024]{1,0:T(8,128)(2,1)} collective-permute-done((bf16[512,1024]{1,0:T(8,128)(2,1)S(1)}, bf16[512,1024]{1,0:T(8,128)(2,1)}, u32[]{:S(2)}, u32[]{:S(2)}) %collective-permute-start.12) | collective-permute-done | bytes 1048608 | tf_op jit(solution)/shard_map/ppermute | solution.py:711
  122.6 5.7 %all-to-all-start.1 = ((bf16[4,256,512]{2,1,0:T(8,128)(2,1)}), bf16[4,256,512]{2,1,0:T(8,128)(2,1)S(1)}, u32[]{:S(2)}, u32[]{:S(2)}) async-start(bf16[4,256,512]{2,1,0:T(8,128)(2,1)} %pad_maximum_fusion.5), calls=%async_computation.1 | async-start | bytes 2097152 | tf_op jit(solution)/shard_map/all_to_all | solution.py:797
  141.6 21.6 %collective-permute-done.13.refs_6_ = bf16[512,1024]{1,0:T(8,128)(2,1)S(1)} collective-permute-done((bf16[512,1024]{1,0:T(8,128)(2,1)}, bf16[512,1024]{1,0:T(8,128)(2,1)S(1)}, u32[]{:S(2)}, u32[]{:S(2)}) %collective-permute-start.13) | collective-permute-done | bytes 1048608 | tf_op jit(solution)/shard_map/ppermute | solution.py:711
  164.5 10.3 %project_qkv.1 = (bf16[2048,768]{1,0:T(8,128)(2,1)}, bf16[2048,1024]{1,0:T(8,128)(2,1)}) custom-call(s32[4]{0:T(128)} %compare_select_fusion.which_ref, f32[1,1024]{1,0:T(1,128)} %reshape.198.gain_ref, bf16[1024,768]{1,0:T(8,128)(2,1)} %bitcast.87, f32[2048,128]{1,0:T(8,128)} %get-tuple-element.142.cos_ref, f32[2048,128]{1,0:T(8,128)} %get-tuple-element.143.sin_ref, ...), custom_call_target="tpu_custom_call" | custom-call | flops 3221225472 | bytes 14680064 | tf_op jit(solution)/shard_map/project_qkv/pallas_call | solution.py:86
  174.8 21.2 %attend_forward.1 = (bf16[2048,256]{1,0:T(8,128)(2,1)}, f32[2048,2]{1,0:T(8,128)S(1)}) custom-call(s32[32]{0:T(128)S(1)} %reshape_squeeze.24.chosen_ref, s32[32]{0:T(128)S(1)} %reshape_squeeze.25.counts_ref, bf16[2048,768]{1,0:T(8,128)(2,1)} %get-tuple-element.70.q_ref.k_ref.v_ref.qkv_ref, bf16[2048,768]{1,0:T(8,128)(2,1)} %get-tuple-element.70.q_ref.k_ref.v_ref.qkv_ref, ...), custom_call_target="tpu_custom_call" | custom-call | flops 3221225472 | bytes 4194304 | tf_op jit(solution)/shard_map/attend_forward/pallas_call | solution.py:191
  201.5 21.0 %all-to-all-done.2 = bf16[4,512,256]{2,1,0:T(8,128)(2,1)S(1)} async-done(((bf16[4,512,256]{2,1,0:T(8,128)(2,1)}), bf16[4,512,256]{2,1,0:T(8,128)(2,1)S(1)}, u32[]{:S(2)}, u32[]{:S(2)}) %all-to-all-start.2) | async-done | bytes 1048608 | tf_op jit(solution)/shard_map/all_to_all | solution.py:807
  223.6 44.0 %feed_forward.1 = (bf16[512,1024]{1,0:T(8,128)(2,1)}, f32[512,1024]{1,0:T(8,128)}, bf16[512,1024]{1,0:T(8,128)(2,1)}, f32[1,1024]{1,0:T(1,128)}, bf16[8,4736,256]{2,1,0:T(8,128)(2,1)}) custom-call(bf16[512,1024]{1,0:T(8,128)(2,1)} %bitcast.101, bf16[512,1024]{1,0:T(8,128)(2,1)} %bitcast.116, bf16[512,1024]{1,0:T(8,128)(2,1)} %bitcast.131, ...), custom_call_target="tpu_custom_call" | custom-call | flops 29796335616 | bytes 38797312 | tf_op jit(solution)/shard_map/feed_forward/pallas_call | solution.py:609
  274.4 22.8 %all-to-all-done.3 = bf16[512,4,256]{2,0,1:T(8,128)(2,1)S(1)} async-done(((bf16[512,4,256]{2,0,1:T(8,128)(2,1)}), bf16[512,4,256]{2,0,1:T(8,128)(2,1)S(1)}, u32[]{:S(2)}, u32[]{:S(2)}) %all-to-all-start.3) | async-done | bytes 1048608 | tf_op jit(solution)/shard_map/all_to_all | solution.py:813
  298.2 16.9 %first_block.1 = (bf16[512,1024]{1,0:T(8,128)(2,1)}, bf16[512,768]{1,0:T(8,128)(2,1)}, f32[2048,256]{1,0:T(8,128)}, f32[2048,256]{1,0:T(8,128)}, f32[2048,256]{1,0:T(8,128)}) custom-call(s32[32]{0:T(128)} %copy-done.3, s32[32]{0:T(128)} %copy-done.2, s32[2]{0:T(128)} %pad_add_fusion.plan_ref, bf16[2048,768]{1,0:T(8,128)(2,1)} %get-tuple-element.70.q_ref.k_ref.v_ref.qkv_ref, ...), custom_call_target="tpu_custom_call" | custom-call | flops 4294967296 | bytes 20971520 | tf_op jit(solution)/shard_map/first_block/pallas_call | solution.py:331
  317.7 26.4 %other_blocks.1 = (bf16[1536,1024]{1,0:T(8,128)(2,1)}, bf16[1536,768]{1,0:T(8,128)(2,1)}) custom-call(s32[32]{0:T(128)} %copy-done.3, s32[32]{0:T(128)} %copy-done.2, s32[1]{0:T(128)} %bitcast.16.plan_ref, bf16[2048,768]{1,0:T(8,128)(2,1)} %get-tuple-element.70.q_ref.k_ref.v_ref.qkv_ref, bf16[2048,768]{1,0:T(8,128)(2,1)} %get-tuple-element.70.q_ref.k_ref.v_ref.qkv_ref, ...), custom_call_target="tpu_custom_call" | custom-call | flops 8053063680 | bytes 20971520 | tf_op jit(solution)/shard_map/other_blocks/pallas_call | solution.py:432
  344.1 4.2 add_convert_fusion.2
  350.4 21.6 %collective-permute-done.20 = bf16[512,1024]{1,0:T(8,128)(2,1)S(1)} collective-permute-done((bf16[512,1024]{1,0:T(8,128)(2,1)}, bf16[512,1024]{1,0:T(8,128)(2,1)S(1)}, u32[]{:S(2)}, u32[]{:S(2)}) %collective-permute-start.20) | collective-permute-done | bytes 1048608 | tf_op jit(solution)/shard_map/ppermute | solution.py:741
  372.1 4.4 add_convert_fusion
  376.5 6.5 %collective-permute-start.22 = (bf16[512,1024]{1,0:T(8,128)(2,1)}, bf16[512,1024]{1,0:T(8,128)(2,1)S(1)}, u32[]{:S(2)}, u32[]{:S(2)}) collective-permute-start(bf16[512,1024]{1,0:T(8,128)(2,1)} %get-tuple-element.94), channel_id=1, source_target_pairs={{0,1},{1,2},{2,3},{4,5},{5,6},{6,7},{8,9},{9,10},{10,11},{12,13},{... | collective-permute-start | bytes 3145736 | tf_op jit(solution)/shard_map/ppermute | solution.py:741
  386.0 17.7 %collective-permute-done.22 = bf16[512,1024]{1,0:T(8,128)(2,1)S(1)} collective-permute-done((bf16[512,1024]{1,0:T(8,128)(2,1)}, bf16[512,1024]{1,0:T(8,128)(2,1)S(1)}, u32[]{:S(2)}, u32[]{:S(2)}) %collective-permute-start.22) | collective-permute-done | bytes 1048608 | tf_op jit(solution)/shard_map/ppermute | solution.py:741
  417.2 8.2 %projection_grads.1 = (bf16[1024,768]{1,0:T(8,128)(2,1)S(1)}, f32[1024,1]{1,0:T(8,128)S(1)}) custom-call(s32[4]{0:T(128)S(1)} %pad_add_fusion.1.order_ref, bf16[2048,1024]{1,0:T(8,128)(2,1)} %get-tuple-element.98.tok_ref, f32[1024,1]{1,0:T(8,128)S(1)} %reshape.204.gain_ref, bf16[1024,768]{1,0:T(8,128)(2,1)S(1)} %bitcast.90, ...), custom_call_target="tpu_custom_call" | custom-call | flops 3221225472 | bytes 7340032 | tf_op jit(solution)/shard_map/projection_grads/pallas_call | solution.py:669
  437.0 4.8 %collective-permute-done.25 = bf16[136,768]{1,0:T(8,128)(2,1)} collective-permute-done((bf16[136,768]{1,0:T(8,128)(2,1)}, bf16[136,768]{1,0:T(8,128)(2,1)}, u32[]{:S(2)}, u32[]{:S(2)}) %collective-permute-start.25) | collective-permute-done | bytes 208928 | tf_op jit(solution)/shard_map/ppermute | solution.py:753
  457.6 5.8 %all-to-all-done.4 = bf16[4,40,768]{2,1,0:T(8,128)(2,1)S(1)} async-done(((bf16[4,40,768]{2,1,0:T(8,128)(2,1)}), bf16[4,40,768]{2,1,0:T(8,128)(2,1)S(1)}, u32[]{:S(2)}, u32[]{:S(2)}) %all-to-all-start.4) | async-done | bytes 245792 | tf_op jit(solution)/shard_map/all_to_all | solution.py:878
  (198 shorter events, 126.0 us)
Async XLA Ops:
  9.9 28.4 %collective-permute-start.2 = (bf16[32,6656]{1,0:T(8,128)(2,1)S(1)}, bf16[32,6656]{1,0:T(8,128)(2,1)S(1)}, u32[]{:S(2)}, u32[]{:S(2)}) collective-permute-start(bf16[32,6656]{1,0:T(8,128)(2,1)S(1)} %constant_dynamic-update-slice_fusion), channel_id=1, source_target_pairs={{1,0},{2,1},{3,2},{5,4},{6,5},{7,6},{9,8},{10,9},{11,10},{13,12},{... | collective-permute-start | bytes 1277960 | tf_op jit(solution)/shard_map/ppermute | solution.py:711
  11.2 27.1 %collective-permute-start = (bf16[32,6656]{1,0:T(8,128)(2,1)S(1)}, bf16[32,6656]{1,0:T(8,128)(2,1)S(1)}, u32[]{:S(2)}, u32[]{:S(2)}) collective-permute-start(bf16[32,6656]{1,0:T(8,128)(2,1)S(1)} %constant_dynamic-update-slice_fusion), channel_id=1, source_target_pairs={{0,1},{1,2},{2,3},{4,5},{5,6},{6,7},{8,9},{9,10},{10,11},{12,13},{... | collective-permute-start | bytes 1277960 | tf_op jit(solution)/shard_map/ppermute | solution.py:710
  27.0 110.2 %all-gather.4.cloned.1.call-start = ((), (), s32[]{:S(2)}) async-start(), calls=%async_computation.7 | async-start | bytes 2211840 | tf_op jit(solution)/shard_map/all_gather | solution.py:788
  39.1 184.6 %all-gather.8.cloned.1.call-start = ((), (), s32[]{:S(2)}) async-start(), calls=%async_computation.9 | async-start | bytes 6488064 | tf_op jit(solution)/shard_map/all_gather | solution.py:798
  39.1 18.5 %collective-permute-start.4 = (bf16[32,6656]{1,0:T(8,128)(2,1)S(1)}, bf16[32,6656]{1,0:T(8,128)(2,1)S(1)}, u32[]{:S(2)}, u32[]{:S(2)}) collective-permute-start(bf16[32,6656]{1,0:T(8,128)(2,1)S(1)} %collective-permute-done), channel_id=1, source_target_pairs={{1,2},{2,3},{5,6},{6,7},{9,10},{10,11},{13,14},{14,15},{17,18},{18... | collective-permute-start | bytes 1277960 | tf_op jit(solution)/shard_map/ppermute | solution.py:710
  39.8 17.8 %collective-permute-start.6 = (bf16[32,6656]{1,0:T(8,128)(2,1)S(1)}, bf16[32,6656]{1,0:T(8,128)(2,1)S(1)}, u32[]{:S(2)}, u32[]{:S(2)}) collective-permute-start(bf16[32,6656]{1,0:T(8,128)(2,1)S(1)} %collective-permute-done.2), channel_id=1, source_target_pairs={{1,0},{2,1},{5,4},{6,5},{9,8},{10,9},{13,12},{14,13},{17,16},{18,1... | collective-permute-start | bytes 1277960 | tf_op jit(solution)/shard_map/ppermute | solution.py:711
  75.1 148.5 %all-gather.6.cloned.1.call-start = ((), (), s32[]{:S(2)}) async-start(), calls=%async_computation.8 | async-start | bytes 15335424 | tf_op jit(solution)/shard_map/all_gather | solution.py:792
  77.0 23.3 %collective-permute-start.11 = (bf16[512,1024]{1,0:T(8,128)(2,1)S(1)}, bf16[512,1024]{1,0:T(8,128)(2,1)S(1)}, u32[]{:S(2)}, u32[]{:S(2)}) collective-permute-start(bf16[512,1024]{1,0:T(8,128)(2,1)S(1)} %bitcast.102), channel_id=1, source_target_pairs={{1,0},{2,1},{3,2},{5,4},{6,5},{7,6},{9,8},{10,9},{11,10},{13,12},{... | collective-permute-start | bytes 3145736 | tf_op jit(solution)/shard_map/ppermute | solution.py:711
  78.3 23.3 %collective-permute-start.8 = (bf16[512,1024]{1,0:T(8,128)(2,1)S(1)}, bf16[512,1024]{1,0:T(8,128)(2,1)}, u32[]{:S(2)}, u32[]{:S(2)}) collective-permute-start(bf16[512,1024]{1,0:T(8,128)(2,1)S(1)} %bitcast.103), channel_id=1, source_target_pairs={{0,1},{1,2},{2,3},{4,5},{5,6},{6,7},{8,9},{9,10},{10,11},{12,13},{... | collective-permute-start | bytes 3145736 | tf_op jit(solution)/shard_map/ppermute | solution.py:710
  100.4 22.2 %collective-permute-start.12 = (bf16[512,1024]{1,0:T(8,128)(2,1)S(1)}, bf16[512,1024]{1,0:T(8,128)(2,1)}, u32[]{:S(2)}, u32[]{:S(2)}) collective-permute-start(bf16[512,1024]{1,0:T(8,128)(2,1)S(1)} %collective-permute-done.11.refs_4_), channel_id=1, source_target_pairs={{1,0},{2,1},{5,4},{6,5},{9,8},{10,9},{13,12},{14,13},{17,16},{18,1... | collective-permute-start | bytes 3145736 | tf_op jit(solution)/shard_map/ppermute | solution.py:711
  101.7 20.9 %collective-permute-start.9 = (bf16[512,1024]{1,0:T(8,128)(2,1)}, bf16[512,1024]{1,0:T(8,128)(2,1)}, u32[]{:S(2)}, u32[]{:S(2)}) collective-permute-start(bf16[512,1024]{1,0:T(8,128)(2,1)} %collective-permute-done.8.refs_1_), channel_id=1, source_target_pairs={{1,2},{2,3},{5,6},{6,7},{9,10},{10,11},{13,14},{14,15},{17,18},{18... | collective-permute-start | bytes 3145736 | tf_op jit(solution)/shard_map/ppermute | solution.py:710
  122.6 52.2 %all-to-all-start.1 = ((bf16[4,256,512]{2,1,0:T(8,128)(2,1)}), bf16[4,256,512]{2,1,0:T(8,128)(2,1)S(1)}, u32[]{:S(2)}, u32[]{:S(2)}) async-start(bf16[4,256,512]{2,1,0:T(8,128)(2,1)} %pad_maximum_fusion.5), calls=%async_computation.1 | async-start | bytes 2097152 | tf_op jit(solution)/shard_map/all_to_all | solution.py:797
  128.3 34.9 %collective-permute-start.13 = (bf16[512,1024]{1,0:T(8,128)(2,1)}, bf16[512,1024]{1,0:T(8,128)(2,1)S(1)}, u32[]{:S(2)}, u32[]{:S(2)}) collective-permute-start(bf16[512,1024]{1,0:T(8,128)(2,1)} %collective-permute-done.12.refs_5_), channel_id=1, source_target_pairs={{1,0},{5,4},{9,8},{13,12},{17,16},{21,20},{25,24},{29,28}} | collective-permute-start | bytes 3145736 | tf_op jit(solution)/shard_map/ppermute | solution.py:711
  129.6 33.6 %collective-permute-start.10 = (bf16[512,1024]{1,0:T(8,128)(2,1)}, bf16[512,1024]{1,0:T(8,128)(2,1)S(1)}, u32[]{:S(2)}, u32[]{:S(2)}) collective-permute-start(bf16[512,1024]{1,0:T(8,128)(2,1)} %collective-permute-done.9.refs_2_), channel_id=1, source_target_pairs={{2,3},{6,7},{10,11},{14,15},{18,19},{22,23},{26,27},{30,31}} | collective-permute-start | bytes 3145736 | tf_op jit(solution)/shard_map/ppermute | solution.py:710
  197.1 25.4 %all-to-all-start.2 = ((bf16[4,512,256]{2,1,0:T(8,128)(2,1)}), bf16[4,512,256]{2,1,0:T(8,128)(2,1)S(1)}, u32[]{:S(2)}, u32[]{:S(2)}) async-start(bf16[4,512,256]{2,1,0:T(8,128)(2,1)} %bitcast.8), calls=%async_computation.2 | async-start | bytes 2097152 | tf_op jit(solution)/shard_map/all_to_all | solution.py:807
  200.6 207.3 %reduce-scatter.3.cloned.1.call-start = ((), (), s32[]{:S(2)}) async-start(), calls=%async_computation.10 | async-start | bytes 21823488 | tf_op jit(solution)/shard_map/reduce_scatter | solution.py:814
  269.9 27.3 %all-to-all-start.3 = ((bf16[512,4,256]{2,0,1:T(8,128)(2,1)}), bf16[512,4,256]{2,0,1:T(8,128)(2,1)S(1)}, u32[]{:S(2)}, u32[]{:S(2)}) async-start(bf16[512,4,256]{2,0,1:T(8,128)(2,1)} %bitcast.86), calls=%async_computation.3 | async-start | bytes 2097152 | tf_op jit(solution)/shard_map/all_to_all | solution.py:813
  273.5 192.5 %reduce-scatter.5.cloned.1.call-start = ((), (), s32[]{:S(2)}) async-start(), calls=%async_computation.11 | async-start | bytes 3031040 | tf_op jit(solution)/shard_map/reduce_scatter | solution.py:885
  315.1 29.0 %collective-permute-start.18 = (bf16[512,1024]{1,0:T(8,128)(2,1)}, bf16[512,1024]{1,0:T(8,128)(2,1)S(1)}, u32[]{:S(2)}, u32[]{:S(2)}) collective-permute-start(bf16[512,1024]{1,0:T(8,128)(2,1)} %get-tuple-element.87), channel_id=1, source_target_pairs={{0,1},{4,5},{8,9},{12,13},{16,17},{20,21},{24,25},{28,29}} | collective-permute-start | bytes 3145736 | tf_op jit(solution)/shard_map/ppermute | solution.py:741
  316.4 27.6 %collective-permute-start.19 = (bf16[512,1024]{1,0:T(8,128)(2,1)}, bf16[512,1024]{1,0:T(8,128)(2,1)S(1)}, u32[]{:S(2)}, u32[]{:S(2)}) collective-permute-start(bf16[512,1024]{1,0:T(8,128)(2,1)} %get-tuple-element.87), channel_id=1, source_target_pairs={{3,2},{7,6},{11,10},{15,14},{19,18},{23,22},{27,26},{31,30}} | collective-permute-start | bytes 3145736 | tf_op jit(solution)/shard_map/ppermute | solution.py:742
  348.3 23.8 %collective-permute-start.20 = (bf16[512,1024]{1,0:T(8,128)(2,1)}, bf16[512,1024]{1,0:T(8,128)(2,1)S(1)}, u32[]{:S(2)}, u32[]{:S(2)}) collective-permute-start(bf16[512,1024]{1,0:T(8,128)(2,1)} %get-tuple-element.90), channel_id=1, source_target_pairs={{0,1},{1,2},{4,5},{5,6},{8,9},{9,10},{12,13},{13,14},{16,17},{17,1... | collective-permute-start | bytes 3145736 | tf_op jit(solution)/shard_map/ppermute | solution.py:741
  349.7 22.4 %collective-permute-start.21 = (bf16[512,1024]{1,0:T(8,128)(2,1)}, bf16[512,1024]{1,0:T(8,128)(2,1)S(1)}, u32[]{:S(2)}, u32[]{:S(2)}) collective-permute-start(bf16[512,1024]{1,0:T(8,128)(2,1)} %get-tuple-element.91), channel_id=1, source_target_pairs={{2,1},{3,2},{6,5},{7,6},{10,9},{11,10},{14,13},{15,14},{18,17},{19... | collective-permute-start | bytes 3145736 | tf_op jit(solution)/shard_map/ppermute | solution.py:742
  376.5 27.2 %collective-permute-start.22 = (bf16[512,1024]{1,0:T(8,128)(2,1)}, bf16[512,1024]{1,0:T(8,128)(2,1)S(1)}, u32[]{:S(2)}, u32[]{:S(2)}) collective-permute-start(bf16[512,1024]{1,0:T(8,128)(2,1)} %get-tuple-element.94), channel_id=1, source_target_pairs={{0,1},{1,2},{2,3},{4,5},{5,6},{6,7},{8,9},{9,10},{10,11},{12,13},{... | collective-permute-start | bytes 3145736 | tf_op jit(solution)/shard_map/ppermute | solution.py:741
  383.0 24.9 %collective-permute-start.23 = (bf16[512,1024]{1,0:T(8,128)(2,1)}, bf16[512,1024]{1,0:T(8,128)(2,1)}, u32[]{:S(2)}, u32[]{:S(2)}) collective-permute-start(bf16[512,1024]{1,0:T(8,128)(2,1)} %get-tuple-element.95), channel_id=1, source_target_pairs={{1,0},{2,1},{3,2},{5,4},{6,5},{7,6},{9,8},{10,9},{11,10},{13,12},{... | collective-permute-start | bytes 3145736 | tf_op jit(solution)/shard_map/ppermute | solution.py:742
  (38 other events, 442.6 us)
Sparse Core Ops, SparseCore 0:
  39.2 27.3 all-gather.3
  75.3 41.5 all-gather.7
  118.7 76.5 all-gather.5
  267.8 127.4 reduce-scatter.2
  412.5 49.2 reduce-scatter.4

commit v14 on v12

--- a/solution.py
+++ b/solution.py
@@ -194,11 +194,15 @@
     return jnp.transpose(jnp.broadcast_to(column, (rows, HEAD_DIM)))[:1]
 
 
-def score_grads(query, grad_out, out, lse, keys, values, mask):
+def row_stats(grad_out, out, lse):
     delta = jnp.sum(grad_out.astype(F32) * out.astype(F32), -1, keepdims=True)
-    weights = jnp.exp2(mask(dot(keys, query, NT)) - spread_rows(lse))
+    return jnp.concatenate([spread_rows(lse), spread_rows(delta)], 0)
+
+
+def score_grads(query, grad_out, stats, keys, values, mask):
+    weights = jnp.exp2(mask(dot(keys, query, NT)) - stats[:1])
     grad_weights = dot(values, grad_out, NT)
-    return weights.astype(BF16), (weights * (grad_weights - spread_rows(delta))).astype(BF16)
+    return weights.astype(BF16), (weights * (grad_weights - stats[1:2])).astype(BF16)
 
 
 def causal_mask(rows):
@@ -207,11 +211,11 @@
     return lambda scores: jnp.where(query_at >= key_at, scores, NEGATIVE)
 
 
-def memory_query_grad(chosen_ref, counts_ref, base, top, query, grad_out, out, lse, mk_ref, mv_ref, columns):
+def memory_query_grad(chosen_ref, counts_ref, base, top, query, grad_out, stats, mk_ref, mv_ref, columns):
     keys = pick_memory(mk_ref, chosen_ref, base, top, columns)
     values = pick_memory(mv_ref, chosen_ref, base, top, columns)
     bias = memory_bias(counts_ref, base, top, 0)
-    _, grad_scores = score_grads(query, grad_out, out, lse, keys, values, lambda scores: scores + bias)
+    _, grad_scores = score_grads(query, grad_out, stats, keys, values, lambda scores: scores + bias)
     return dot(grad_scores, keys, TN)
 
 
@@ -229,7 +233,7 @@
 
 def first_block_kernel(
     heads, top, chosen_ref, counts_ref, plan_ref, qkv_ref, mk_ref, mv_ref, go_ref, out_ref, lse_ref, cos_ref, sin_ref,
-    w_ref, partial_ref, grad_ref, gq_ref, gk_ref, gv_ref,
+    w_ref, partial_ref, grad_ref, gq_ref, gk_ref, gv_ref, stats_s,
 ):
     rows = partial_ref.shape[0]
     subs = rows // QBLK
@@ -241,15 +245,21 @@
     gk_ref[...] = jnp.zeros_like(gk_ref)
     gv_ref[...] = jnp.zeros_like(gv_ref)
 
-    def pair(queries, keys, mask):
+    def note_stats(slot, here):
+        for head in range(heads):
+            columns = slice(head * HEAD_DIM, (head + 1) * HEAD_DIM)
+            stats_s[slot, head] = row_stats(go_ref[here, columns], out_ref[here, columns], lse_ref[here, head : head + 1])
+
+    note_stats(0, own)
+
+    def pair(slot, queries, keys, mask):
         for head in range(heads):
             at = head * HEAD_DIM
             columns = slice(at, at + HEAD_DIM)
             query, grad_out = qkv_ref[queries, columns], go_ref[queries, columns]
             key = qkv_ref[keys, wide + at : wide + at + HEAD_DIM]
             value = qkv_ref[keys, 2 * wide + at : 2 * wide + at + HEAD_DIM]
-            lse = lse_ref[queries, head : head + 1]
-            weights, grad_scores = score_grads(query, grad_out, out_ref[queries, columns], lse, key, value, mask)
+            weights, grad_scores = score_grads(query, grad_out, stats_s[slot, head], key, value, mask)
             gk_ref[keys, columns] += dot(grad_scores, query)
             gv_ref[keys, columns] += dot(weights, grad_out)
             gq_ref[queries, columns] += dot(grad_scores, key, TN)
@@ -260,24 +270,28 @@
             here = pl.ds(pl.multiple_of(block * rows + sub * QBLK, QBLK), QBLK)
             gq_ref[here, columns] += memory_query_grad(
                 chosen_ref, counts_ref, (block * subs + sub) * top, top, qkv_ref[here, columns], go_ref[here, columns],
-                out_ref[here, columns], lse_ref[here, head : head + 1], mk_ref, mv_ref, columns,
+                stats_s[0, head][:, sub * QBLK : (sub + 1) * QBLK], mk_ref, mv_ref, columns,
             )
-    pair(own, own, causal_mask(rows))
+    pair(0, own, own, causal_mask(rows))
 
     def step(index, carry):
         other = jnp.where(is_last == 1, index, index + 1)
-        queries = jnp.where(is_last == 1, block, other)
-        keys = jnp.where(is_last == 1, other, block)
-        pair(
-            pl.ds(pl.multiple_of(queries * rows, rows), rows),
-            pl.ds(pl.multiple_of(keys * rows, rows), rows),
-            lambda scores: scores,
-        )
+        there = pl.ds(pl.multiple_of(other * rows, rows), rows)
+
+        @pl.when(is_last == 1)
+        def _():
+            pair(0, own, there, lambda scores: scores)
+
+        @pl.when(is_last == 0)
+        def _():
+            note_stats(1, there)
+            pair(1, there, own, lambda scores: scores)
+
         return carry
 
     lax.fori_loop(0, others, step, 0)
     grad = block_grads(
-        heads, gq_ref[own, :], gk_ref[own, :], gv_ref[own, :], cos_ref[own, :], sin_ref[own, :]
+        heads, gq_ref[own, :], gk_ref[own, :], gv_ref[own, :], cos_ref[...], sin_ref[...]
     )
     grad_ref[...] = grad
     partial_ref[...] = dot(grad, w_ref[...], NT).astype(BF16)
@@ -306,8 +320,8 @@
                 whole(grad_out),
                 whole(out),
                 whole(lse),
-                whole(cosine),
-                whole(sine),
+                pl.BlockSpec((rows, HEAD_DIM), lambda i, c, n, plan: (plan[0], 0)),
+                pl.BlockSpec((rows, HEAD_DIM), lambda i, c, n, plan: (plan[0], 0)),
                 whole(w_qkv),
             ],
             out_specs=[
@@ -317,6 +331,7 @@
                 sums,
                 sums,
             ],
+            scratch_shapes=[pltpu.VMEM((2, heads, 2, rows), F32)],
         ),
         out_shape=[
             jax.ShapeDtypeStruct((rows, width), BF16),
@@ -348,13 +363,15 @@
         gk_s[...] = gk_in[...]
         gv_s[...] = gv_in[...]
 
+    stats = []
     for head in range(heads):
         columns = slice(head * HEAD_DIM, (head + 1) * HEAD_DIM)
+        stats.append(row_stats(go_ref[:, columns], out_ref[:, columns], lse_ref[:, head : head + 1]))
         for sub in range(subs):
             here = slice(sub * QBLK, (sub + 1) * QBLK)
             gq_s[here, columns] = gq_in[here, columns] + memory_query_grad(
                 chosen_ref, counts_ref, (block * subs + sub) * top, top, q_ref[here, columns], go_ref[here, columns],
-                out_ref[here, columns], lse_ref[here, head : head + 1], mk_ref, mv_ref, columns,
+                stats[head][:, here], mk_ref, mv_ref, columns,
             )
 
     def local(there, mask):
@@ -362,9 +379,7 @@
             columns = slice(head * HEAD_DIM, (head + 1) * HEAD_DIM)
             query, grad_out = q_ref[:, columns], go_ref[:, columns]
             key = k_ref[there, columns]
-            weights, grad_scores = score_grads(
-                query, grad_out, out_ref[:, columns], lse_ref[:, head : head + 1], key, v_ref[there, columns], mask
-            )
+            weights, grad_scores = score_grads(query, grad_out, stats[head], key, v_ref[there, columns], mask)
             gk_s[there, columns] += dot(grad_scores, query)
             gv_s[there, columns] += dot(weights, grad_out)
             gq_s[:, columns] += dot(grad_scores, key, TN)
@@ -751,7 +766,7 @@
     shards = jnp.concatenate([w_out, w_gate, w_up], 1)
     (near, near_down), steps = chain_gather((shards, w_down), "fsdp")
     (gathered,), token_steps = chain_gather((after(mine, steps[-2]),), "fsdp")
-    parcel = lax.all_gather(parcel, DP, axis=0, tiled=True)
+    parcel = lax.all_gather(after(parcel, steps[0]), DP, axis=0, tiled=True)
     w_qkv = parcel[:, :share].reshape(width, 3 * wide)
     gain_one = parcel[:, share, :share].reshape(1, width).astype(F32)
     gain_two = parcel[:, share, share : 2 * share].reshape(1, width).astype(F32)

time: 471 us -> 468 us (level)
  blocking collectives: 14.7 us -> 0 us
  starting transfers between devices: 70 us -> 77.6 us
    all_to_all x1 -> x0, blocking collectives: 14.7 us -> none  [body(): parcel = lax.all_to_all(parcel, 'fsdp', 0, 0, tiled=True)]
    ppermute x9, waiting for transfers between devices: 75.5 us -> 81.7 us  [chain_gather(): falling = tuple((lax.ppermute(block, axis, down) for block in falling))]
  transfers between devices with their start and end apart: 37 -> 38, of which waited for: 17 -> 18; matrix products, arithmetic and copies ran while one was open for 11% -> 12% of each run, Pallas kernels for 18% -> 17%
where the time goes in v14:
time: 468 us; the launch traced here: 459 us
  waiting for transfers between devices  166 us (35%)
  Pallas kernels  124 us (26%)
  starting transfers between devices  77.6 us (17%)
  other arithmetic  44.2 us (9%)
  local copies, waits for them, and re-layouts  31.9 us (7%)
  between operations  14.8 us (3%)
    ppermute x9, waiting for transfers between devices, chain_gather(): falling = tuple((lax.ppermute(block, axis, down) for block in falling))  81.7 us
    pallas_call x1, Pallas kernels, feed_forward(): pl.pallas_call(functools.partial(ffn_kernel, span, merged), grid=(steps,)...  44 us
    ppermute x3, waiting for transfers between devices, chain_scatter(): rising = lax.ppermute(up, axis, [(i, i + 1) for i in range(step + 1)])  26.1 us
    pallas_call x1, Pallas kernels, other_blocks(): pl.pallas_call(functools.partial(other_blocks_kernel, heads, top), grid_s...  24.7 us
    pallas_call x1, Pallas kernels, attend_forward(): pl.pallas_call(functools.partial(forward_kernel, heads, top), grid_spec=p...  21.4 us
    ppermute x9, starting transfers between devices, chain_gather(): rising = tuple((lax.ppermute(block, axis, up) for block in rising))  21.1 us
    pallas_call x1, Pallas kernels, first_block(): pl.pallas_call(functools.partial(first_block_kernel, heads, top), grid_sp...  18.3 us
    all_to_all x1, waiting for transfers between devices, body(): attended = lax.all_to_all(attended_heads, 'fsdp', 0, 1, tiled=True)  15 us
  transfers between devices with their start and end apart: 38, of which 18 were waited for; matrix products, arithmetic and copies ran while one was open for 12% of the time, Pallas kernels for 17%

profile of v14, /device:TPU:0, one launch (start us, length us, event | category | flops | bytes accessed | tf_op | source)
XLA Modules:
  0.0 459.2 jit_solution(13750883491315895415)
XLA Ops:
  11.2 5.6 %collective-permute-start = (bf16[32,6656]{1,0:T(8,128)(2,1)S(1)}, bf16[32,6656]{1,0:T(8,128)(2,1)S(1)}, u32[]{:S(2)}, u32[]{:S(2)}) collective-permute-start(bf16[32,6656]{1,0:T(8,128)(2,1)S(1)} %constant_dynamic-update-slice_fusion), channel_id=1, source_target_pairs={{0,1},{1,2},{2,3},{4,5},{5,6},{6,7},{8,9},{9,10},{10,11},{12,13},{... | collective-permute-start | bytes 1277960 | tf_op jit(solution)/shard_map/ppermute | solution.py:691
  43.2 14.5 %collective-permute-done.7 = bf16[88,1024]{1,0:T(8,128)(2,1)S(1)} collective-permute-done((bf16[88,1024]{1,0:T(8,128)(2,1)S(1)}, bf16[88,1024]{1,0:T(8,128)(2,1)S(1)}, u32[]{:S(2)}, u32[]{:S(2)}) %collective-permute-start.7) | collective-permute-done | bytes 180256 | tf_op jit(solution)/shard_map/ppermute | solution.py:692
  61.7 11.5 %collective-permute-done.17 = bf16[88,1024]{1,0:T(8,128)(2,1)} collective-permute-done((bf16[88,1024]{1,0:T(8,128)(2,1)S(1)}, bf16[88,1024]{1,0:T(8,128)(2,1)}, u32[]{:S(2)}, u32[]{:S(2)}) %collective-permute-start.17) | collective-permute-done | bytes 180256 | tf_op jit(solution)/shard_map/ppermute | solution.py:692
  78.6 5.6 %collective-permute-start.8 = (bf16[512,1024]{1,0:T(8,128)(2,1)S(1)}, bf16[512,1024]{1,0:T(8,128)(2,1)}, u32[]{:S(2)}, u32[]{:S(2)}) collective-permute-start(bf16[512,1024]{1,0:T(8,128)(2,1)S(1)} %bitcast.94), channel_id=1, source_target_pairs={{0,1},{1,2},{2,3},{4,5},{5,6},{6,7},{8,9},{9,10},{10,11},{12,13},{... | collective-permute-start | bytes 3145736 | tf_op jit(solution)/shard_map/ppermute | solution.py:691
  84.1 16.4 %collective-permute-done.11 = bf16[512,1024]{1,0:T(8,128)(2,1)S(1)} collective-permute-done((bf16[512,1024]{1,0:T(8,128)(2,1)S(1)}, bf16[512,1024]{1,0:T(8,128)(2,1)S(1)}, u32[]{:S(2)}, u32[]{:S(2)}) %collective-permute-start.11) | collective-permute-done | bytes 1048608 | tf_op jit(solution)/shard_map/ppermute | solution.py:692
  106.6 17.1 %collective-permute-done.12 = bf16[512,1024]{1,0:T(8,128)(2,1)} collective-permute-done((bf16[512,1024]{1,0:T(8,128)(2,1)S(1)}, bf16[512,1024]{1,0:T(8,128)(2,1)}, u32[]{:S(2)}, u32[]{:S(2)}) %collective-permute-start.12) | collective-permute-done | bytes 1048608 | tf_op jit(solution)/shard_map/ppermute | solution.py:692
  132.7 5.6 %all-to-all-start.1 = ((bf16[4,256,512]{2,1,0:T(8,128)(2,1)}), bf16[4,256,512]{2,1,0:T(8,128)(2,1)}, u32[]{:S(2)}, u32[]{:S(2)}) async-start(bf16[4,256,512]{2,1,0:T(8,128)(2,1)} %pad_maximum_fusion.6), calls=%async_computation.1 | async-start | bytes 2097152 | tf_op jit(solution)/shard_map/all_to_all | solution.py:779
  141.2 18.3 %collective-permute-done.13 = bf16[512,1024]{1,0:T(8,128)(2,1)} collective-permute-done((bf16[512,1024]{1,0:T(8,128)(2,1)}, bf16[512,1024]{1,0:T(8,128)(2,1)}, u32[]{:S(2)}, u32[]{:S(2)}) %collective-permute-start.13) | collective-permute-done | bytes 1048608 | tf_op jit(solution)/shard_map/ppermute | solution.py:692
  164.3 7.4 %project_qkv.1.q_ref.k_ref.v_ref.qkv_ref = bf16[2048,768]{1,0:T(8,128)(2,1)} custom-call(bf16[2048,1024]{1,0:T(8,128)(2,1)} %pad_maximum_fusion.tok_ref, f32[1,1024]{1,0:T(1,128)S(1)} %reshape.198.gain_ref, bf16[1024,768]{1,0:T(8,128)(2,1)S(1)} %bitcast.87, f32[2048,128]{1,0:T(8,128)S(1)} %get-tuple-element.142.cos_ref, f32[2048,128]{1,0:T(8,128)S(1)} %copy-done.3), custom_call_target="tpu_custom_call" | custom-call | flops 3221225472 | bytes 14680064 | tf_op jit(solution)/shard_map/project_qkv/pallas_call | solution.py:62
  171.6 21.4 %attend_forward.1 = (bf16[2048,256]{1,0:T(8,128)(2,1)}, f32[2048,2]{1,0:T(8,128)S(1)}) custom-call(s32[32]{0:T(128)S(1)} %reshape_squeeze.24.chosen_ref, s32[32]{0:T(128)S(1)} %reshape_squeeze.25.counts_ref, bf16[2048,768]{1,0:T(8,128)(2,1)} %project_qkv.1.q_ref.k_ref.v_ref.qkv_ref, bf16[2048,768]{1,0:T(8,128)(2,1)} %project_qkv.1.q_ref.k_ref.v_ref.qkv_ref, ...), custom_call_target="tpu_custom_call" | custom-call | flops 3221225472 | bytes 4194304 | tf_op jit(solution)/shard_map/attend_forward/pallas_call | solution.py:157
  194.0 4.7 %all-to-all-start.2 = ((bf16[4,512,256]{2,1,0:T(8,128)(2,1)}), bf16[4,512,256]{2,1,0:T(8,128)(2,1)S(1)}, u32[]{:S(2)}, u32[]{:S(2)}) async-start(bf16[4,512,256]{2,1,0:T(8,128)(2,1)} %bitcast.8), calls=%async_computation.2 | async-start | bytes 2097152 | tf_op jit(solution)/shard_map/all_to_all | solution.py:785
  199.6 15.0 %all-to-all-done.2 = bf16[4,512,256]{2,1,0:T(8,128)(2,1)S(1)} async-done(((bf16[4,512,256]{2,1,0:T(8,128)(2,1)}), bf16[4,512,256]{2,1,0:T(8,128)(2,1)S(1)}, u32[]{:S(2)}, u32[]{:S(2)}) %all-to-all-start.2) | async-done | bytes 1048608 | tf_op jit(solution)/shard_map/all_to_all | solution.py:785
  215.8 44.0 %feed_forward.1 = (bf16[512,1024]{1,0:T(8,128)(2,1)}, f32[512,1024]{1,0:T(8,128)}, bf16[512,1024]{1,0:T(8,128)(2,1)}, f32[1,1024]{1,0:T(1,128)}, bf16[8,4736,256]{2,1,0:T(8,128)(2,1)}) custom-call(bf16[512,1024]{1,0:T(8,128)(2,1)} %bitcast.92, bf16[512,1024]{1,0:T(8,128)(2,1)} %bitcast.110, bf16[512,1024]{1,0:T(8,128)(2,1)} %bitcast.125, ...), custom_call_target="tpu_custom_call" | custom-call | flops 29796335616 | bytes 38797312 | tf_op jit(solution)/shard_map/feed_forward/pallas_call | solution.py:590
  266.7 14.8 %all-to-all-done.3 = bf16[512,4,256]{2,0,1:T(8,128)(2,1)S(1)} async-done(((bf16[512,4,256]{2,0,1:T(8,128)(2,1)}), bf16[512,4,256]{2,0,1:T(8,128)(2,1)S(1)}, u32[]{:S(2)}, u32[]{:S(2)}) %all-to-all-start.3) | async-done | bytes 1048608 | tf_op jit(solution)/shard_map/all_to_all | solution.py:791
  282.5 18.3 %first_block.1 = (bf16[512,1024]{1,0:T(8,128)(2,1)}, bf16[512,768]{1,0:T(8,128)(2,1)}, f32[2048,256]{1,0:T(8,128)}, f32[2048,256]{1,0:T(8,128)}, f32[2048,256]{1,0:T(8,128)}) custom-call(s32[32]{0:T(128)} %copy-done.5, s32[32]{0:T(128)} %copy-done.4, s32[2]{0:T(128)} %pad_add_fusion.plan_ref, bf16[2048,768]{1,0:T(8,128)(2,1)} %project_qkv.1.q_ref.k_ref.v_ref.qkv_ref, ...), custom_call_target="tpu_custom_call" | custom-call | flops 4294967296 | bytes 20971520 | tf_op jit(solution)/shard_map/first_block/pallas_call | solution.py:311
  303.1 24.7 %other_blocks.1 = (bf16[1536,1024]{1,0:T(8,128)(2,1)}, bf16[1536,768]{1,0:T(8,128)(2,1)}) custom-call(s32[32]{0:T(128)} %copy-done.5, s32[32]{0:T(128)} %copy-done.4, s32[1]{0:T(128)} %bitcast.16.plan_ref, bf16[2048,768]{1,0:T(8,128)(2,1)} %project_qkv.1.q_ref.k_ref.v_ref.qkv_ref, bf16[2048,768]{1,0:T(8,128)(2,1)} %project_qkv.1.q_ref.k_ref.v_ref.qkv_ref, ...), custom_call_target="tpu_custom_call" | custom-call | flops 8053063680 | bytes 20971520 | tf_op jit(solution)/shard_map/other_blocks/pallas_call | solution.py:413
  334.1 16.6 %collective-permute-done.20 = bf16[512,1024]{1,0:T(8,128)(2,1)S(1)} collective-permute-done((bf16[512,1024]{1,0:T(8,128)(2,1)}, bf16[512,1024]{1,0:T(8,128)(2,1)S(1)}, u32[]{:S(2)}, u32[]{:S(2)}) %collective-permute-start.20) | collective-permute-done | bytes 1048608 | tf_op jit(solution)/shard_map/ppermute | solution.py:722
  354.8 11.1 %collective-permute-start.22 = (bf16[512,1024]{1,0:T(8,128)(2,1)}, bf16[512,1024]{1,0:T(8,128)(2,1)S(1)}, u32[]{:S(2)}, u32[]{:S(2)}) collective-permute-start(bf16[512,1024]{1,0:T(8,128)(2,1)} %get-tuple-element.91), channel_id=1, source_target_pairs={{0,1},{1,2},{2,3},{4,5},{5,6},{6,7},{8,9},{9,10},{10,11},{12,13},{... | collective-permute-start | bytes 3145736 | tf_op jit(solution)/shard_map/ppermute | solution.py:722
  369.0 9.5 %collective-permute-done.22 = bf16[512,1024]{1,0:T(8,128)(2,1)S(1)} collective-permute-done((bf16[512,1024]{1,0:T(8,128)(2,1)}, bf16[512,1024]{1,0:T(8,128)(2,1)S(1)}, u32[]{:S(2)}, u32[]{:S(2)}) %collective-permute-start.22) | collective-permute-done | bytes 1048608 | tf_op jit(solution)/shard_map/ppermute | solution.py:722
  383.0 4.6 %reduce-scatter.3.cloned.1.call-done = bf16[1,4736,256]{2,1,0:T(8,128)(2,1)} async-done(((bf16[8,4736,256]{2,1,0:T(8,128)(2,1)}), bf16[1,4736,256]{2,1,0:T(8,128)(2,1)}) %reduce-scatter.3.cloned.1.call-update) | async-done | bytes 2424848 | tf_op jit(solution)/shard_map/reduce_scatter | solution.py:792
  396.9 8.5 %projection_grads.1 = (bf16[1024,768]{1,0:T(8,128)(2,1)S(1)}, f32[1024,1]{1,0:T(8,128)S(1)}) custom-call(s32[4]{0:T(128)S(1)} %pad_add_fusion.1.order_ref, bf16[2048,1024]{1,0:T(8,128)(2,1)} %pad_maximum_fusion.tok_ref, f32[1024,1]{1,0:T(8,128)S(1)} %reshape.204.gain_ref, bf16[1024,768]{1,0:T(8,128)(2,1)S(1)} %bitcast.90, ...), custom_call_target="tpu_custom_call" | custom-call | flops 3221225472 | bytes 7340032 | tf_op jit(solution)/shard_map/projection_grads/pallas_call | solution.py:650
  416.8 5.0 %collective-permute-done.25 = bf16[136,768]{1,0:T(8,128)(2,1)} collective-permute-done((bf16[136,768]{1,0:T(8,128)(2,1)}, bf16[136,768]{1,0:T(8,128)(2,1)}, u32[]{:S(2)}, u32[]{:S(2)}) %collective-permute-start.25) | collective-permute-done | bytes 208928 | tf_op jit(solution)/shard_map/ppermute | solution.py:734
  427.7 4.6 %all-to-all-start.4 = ((bf16[4,40,768]{2,1,0:T(8,128)(2,1)}), bf16[4,40,768]{2,1,0:T(8,128)(2,1)S(1)}, u32[]{:S(2)}, u32[]{:S(2)}) async-start(bf16[4,40,768]{2,1,0:T(8,128)(2,1)} %fusion.10), calls=%async_computation.4 | async-start | bytes 491520 | tf_op jit(solution)/shard_map/all_to_all | solution.py:857
  438.8 6.6 %all-to-all-done.4 = bf16[4,40,768]{2,1,0:T(8,128)(2,1)S(1)} async-done(((bf16[4,40,768]{2,1,0:T(8,128)(2,1)}), bf16[4,40,768]{2,1,0:T(8,128)(2,1)S(1)}, u32[]{:S(2)}, u32[]{:S(2)}) %all-to-all-start.4) | async-done | bytes 245792 | tf_op jit(solution)/shard_map/all_to_all | solution.py:857
  (199 shorter events, 133.0 us)
Async XLA Ops:
  9.9 28.4 %collective-permute-start.2 = (bf16[32,6656]{1,0:T(8,128)(2,1)S(1)}, bf16[32,6656]{1,0:T(8,128)(2,1)S(1)}, u32[]{:S(2)}, u32[]{:S(2)}) collective-permute-start(bf16[32,6656]{1,0:T(8,128)(2,1)S(1)} %constant_dynamic-update-slice_fusion), channel_id=1, source_target_pairs={{1,0},{2,1},{3,2},{5,4},{6,5},{7,6},{9,8},{10,9},{11,10},{13,12},{... | collective-permute-start | bytes 1277960 | tf_op jit(solution)/shard_map/ppermute | solution.py:692
  11.2 27.1 %collective-permute-start = (bf16[32,6656]{1,0:T(8,128)(2,1)S(1)}, bf16[32,6656]{1,0:T(8,128)(2,1)S(1)}, u32[]{:S(2)}, u32[]{:S(2)}) collective-permute-start(bf16[32,6656]{1,0:T(8,128)(2,1)S(1)} %constant_dynamic-update-slice_fusion), channel_id=1, source_target_pairs={{0,1},{1,2},{2,3},{4,5},{5,6},{6,7},{8,9},{9,10},{10,11},{12,13},{... | collective-permute-start | bytes 1277960 | tf_op jit(solution)/shard_map/ppermute | solution.py:691
  27.0 111.5 %all-gather.4.cloned.1.call-start = ((), (), s32[]{:S(2)}) async-start(), calls=%async_computation.7 | async-start | bytes 2211840 | tf_op jit(solution)/shard_map/all_gather | solution.py:769
  39.1 176.6 %all-gather.8.cloned.1.call-start = ((), (), s32[]{:S(2)}) async-start(), calls=%async_computation.9 | async-start | bytes 6488064 | tf_op jit(solution)/shard_map/all_gather | solution.py:780
  39.2 18.5 %collective-permute-start.4 = (bf16[32,6656]{1,0:T(8,128)(2,1)S(1)}, bf16[32,6656]{1,0:T(8,128)(2,1)S(1)}, u32[]{:S(2)}, u32[]{:S(2)}) collective-permute-start(bf16[32,6656]{1,0:T(8,128)(2,1)S(1)} %collective-permute-done), channel_id=1, source_target_pairs={{1,2},{2,3},{5,6},{6,7},{9,10},{10,11},{13,14},{14,15},{17,18},{18... | collective-permute-start | bytes 1277960 | tf_op jit(solution)/shard_map/ppermute | solution.py:691
  39.9 17.8 %collective-permute-start.6 = (bf16[32,6656]{1,0:T(8,128)(2,1)S(1)}, bf16[32,6656]{1,0:T(8,128)(2,1)S(1)}, u32[]{:S(2)}, u32[]{:S(2)}) collective-permute-start(bf16[32,6656]{1,0:T(8,128)(2,1)S(1)} %collective-permute-done.2), channel_id=1, source_target_pairs={{1,0},{2,1},{5,4},{6,5},{9,8},{10,9},{13,12},{14,13},{17,16},{18,1... | collective-permute-start | bytes 1277960 | tf_op jit(solution)/shard_map/ppermute | solution.py:692
  75.4 140.3 %all-gather.6.cloned.1.call-start = ((), (), s32[]{:S(2)}) async-start(), calls=%async_computation.8 | async-start | bytes 15335424 | tf_op jit(solution)/shard_map/all_gather | solution.py:773
  77.3 23.3 %collective-permute-start.11 = (bf16[512,1024]{1,0:T(8,128)(2,1)S(1)}, bf16[512,1024]{1,0:T(8,128)(2,1)S(1)}, u32[]{:S(2)}, u32[]{:S(2)}) collective-permute-start(bf16[512,1024]{1,0:T(8,128)(2,1)S(1)} %bitcast.93), channel_id=1, source_target_pairs={{1,0},{2,1},{3,2},{5,4},{6,5},{7,6},{9,8},{10,9},{11,10},{13,12},{... | collective-permute-start | bytes 3145736 | tf_op jit(solution)/shard_map/ppermute | solution.py:692
  78.6 23.3 %collective-permute-start.8 = (bf16[512,1024]{1,0:T(8,128)(2,1)S(1)}, bf16[512,1024]{1,0:T(8,128)(2,1)}, u32[]{:S(2)}, u32[]{:S(2)}) collective-permute-start(bf16[512,1024]{1,0:T(8,128)(2,1)S(1)} %bitcast.94), channel_id=1, source_target_pairs={{0,1},{1,2},{2,3},{4,5},{5,6},{6,7},{8,9},{9,10},{10,11},{12,13},{... | collective-permute-start | bytes 3145736 | tf_op jit(solution)/shard_map/ppermute | solution.py:691
  100.6 23.1 %collective-permute-start.12 = (bf16[512,1024]{1,0:T(8,128)(2,1)S(1)}, bf16[512,1024]{1,0:T(8,128)(2,1)}, u32[]{:S(2)}, u32[]{:S(2)}) collective-permute-start(bf16[512,1024]{1,0:T(8,128)(2,1)S(1)} %collective-permute-done.11), channel_id=1, source_target_pairs={{1,0},{2,1},{5,4},{6,5},{9,8},{10,9},{13,12},{14,13},{17,16},{18,1... | collective-permute-start | bytes 3145736 | tf_op jit(solution)/shard_map/ppermute | solution.py:692
  101.9 23.1 %collective-permute-start.9 = (bf16[512,1024]{1,0:T(8,128)(2,1)}, bf16[512,1024]{1,0:T(8,128)(2,1)}, u32[]{:S(2)}, u32[]{:S(2)}) collective-permute-start(bf16[512,1024]{1,0:T(8,128)(2,1)} %collective-permute-done.8), channel_id=1, source_target_pairs={{1,2},{2,3},{5,6},{6,7},{9,10},{10,11},{13,14},{14,15},{17,18},{18... | collective-permute-start | bytes 3145736 | tf_op jit(solution)/shard_map/ppermute | solution.py:691
  123.7 35.8 %collective-permute-start.13 = (bf16[512,1024]{1,0:T(8,128)(2,1)}, bf16[512,1024]{1,0:T(8,128)(2,1)}, u32[]{:S(2)}, u32[]{:S(2)}) collective-permute-start(bf16[512,1024]{1,0:T(8,128)(2,1)} %collective-permute-done.12), channel_id=1, source_target_pairs={{1,0},{5,4},{9,8},{13,12},{17,16},{21,20},{25,24},{29,28}} | collective-permute-start | bytes 3145736 | tf_op jit(solution)/shard_map/ppermute | solution.py:692
  125.0 34.5 %collective-permute-start.10 = (bf16[512,1024]{1,0:T(8,128)(2,1)}, bf16[512,1024]{1,0:T(8,128)(2,1)}, u32[]{:S(2)}, u32[]{:S(2)}) collective-permute-start(bf16[512,1024]{1,0:T(8,128)(2,1)} %collective-permute-done.9), channel_id=1, source_target_pairs={{2,3},{6,7},{10,11},{14,15},{18,19},{22,23},{26,27},{30,31}} | collective-permute-start | bytes 3145736 | tf_op jit(solution)/shard_map/ppermute | solution.py:691
  132.7 38.9 %all-to-all-start.1 = ((bf16[4,256,512]{2,1,0:T(8,128)(2,1)}), bf16[4,256,512]{2,1,0:T(8,128)(2,1)}, u32[]{:S(2)}, u32[]{:S(2)}) async-start(bf16[4,256,512]{2,1,0:T(8,128)(2,1)} %pad_maximum_fusion.6), calls=%async_computation.1 | async-start | bytes 2097152 | tf_op jit(solution)/shard_map/all_to_all | solution.py:779
  194.0 20.6 %all-to-all-start.2 = ((bf16[4,512,256]{2,1,0:T(8,128)(2,1)}), bf16[4,512,256]{2,1,0:T(8,128)(2,1)S(1)}, u32[]{:S(2)}, u32[]{:S(2)}) async-start(bf16[4,512,256]{2,1,0:T(8,128)(2,1)} %bitcast.8), calls=%async_computation.2 | async-start | bytes 2097152 | tf_op jit(solution)/shard_map/all_to_all | solution.py:785
  198.7 188.9 %reduce-scatter.3.cloned.1.call-start = ((), (), s32[]{:S(2)}) async-start(), calls=%async_computation.10 | async-start | bytes 21823488 | tf_op jit(solution)/shard_map/reduce_scatter | solution.py:792
  262.0 19.5 %all-to-all-start.3 = ((bf16[512,4,256]{2,0,1:T(8,128)(2,1)}), bf16[512,4,256]{2,0,1:T(8,128)(2,1)S(1)}, u32[]{:S(2)}, u32[]{:S(2)}) async-start(bf16[512,4,256]{2,0,1:T(8,128)(2,1)} %bitcast.86), calls=%async_computation.3 | async-start | bytes 2097152 | tf_op jit(solution)/shard_map/all_to_all | solution.py:791
  265.6 182.4 %reduce-scatter.5.cloned.1.call-start = ((), (), s32[]{:S(2)}) async-start(), calls=%async_computation.11 | async-start | bytes 3031040 | tf_op jit(solution)/shard_map/reduce_scatter | solution.py:864
  300.8 27.0 %collective-permute-start.18 = (bf16[512,1024]{1,0:T(8,128)(2,1)}, bf16[512,1024]{1,0:T(8,128)(2,1)S(1)}, u32[]{:S(2)}, u32[]{:S(2)}) collective-permute-start(bf16[512,1024]{1,0:T(8,128)(2,1)} %get-tuple-element.84), channel_id=1, source_target_pairs={{0,1},{4,5},{8,9},{12,13},{16,17},{20,21},{24,25},{28,29}} | collective-permute-start | bytes 3145736 | tf_op jit(solution)/shard_map/ppermute | solution.py:722
  302.1 25.6 %collective-permute-start.19 = (bf16[512,1024]{1,0:T(8,128)(2,1)}, bf16[512,1024]{1,0:T(8,128)(2,1)S(1)}, u32[]{:S(2)}, u32[]{:S(2)}) collective-permute-start(bf16[512,1024]{1,0:T(8,128)(2,1)} %get-tuple-element.84), channel_id=1, source_target_pairs={{3,2},{7,6},{11,10},{15,14},{19,18},{23,22},{27,26},{31,30}} | collective-permute-start | bytes 3145736 | tf_op jit(solution)/shard_map/ppermute | solution.py:723
  331.9 18.7 %collective-permute-start.20 = (bf16[512,1024]{1,0:T(8,128)(2,1)}, bf16[512,1024]{1,0:T(8,128)(2,1)S(1)}, u32[]{:S(2)}, u32[]{:S(2)}) collective-permute-start(bf16[512,1024]{1,0:T(8,128)(2,1)} %get-tuple-element.87), channel_id=1, source_target_pairs={{0,1},{1,2},{4,5},{5,6},{8,9},{9,10},{12,13},{13,14},{16,17},{17,1... | collective-permute-start | bytes 3145736 | tf_op jit(solution)/shard_map/ppermute | solution.py:722
  333.3 17.4 %collective-permute-start.21 = (bf16[512,1024]{1,0:T(8,128)(2,1)}, bf16[512,1024]{1,0:T(8,128)(2,1)S(1)}, u32[]{:S(2)}, u32[]{:S(2)}) collective-permute-start(bf16[512,1024]{1,0:T(8,128)(2,1)} %get-tuple-element.88), channel_id=1, source_target_pairs={{2,1},{3,2},{6,5},{7,6},{10,9},{11,10},{14,13},{15,14},{18,17},{19... | collective-permute-start | bytes 3145736 | tf_op jit(solution)/shard_map/ppermute | solution.py:723
  354.8 23.7 %collective-permute-start.22 = (bf16[512,1024]{1,0:T(8,128)(2,1)}, bf16[512,1024]{1,0:T(8,128)(2,1)S(1)}, u32[]{:S(2)}, u32[]{:S(2)}) collective-permute-start(bf16[512,1024]{1,0:T(8,128)(2,1)} %get-tuple-element.91), channel_id=1, source_target_pairs={{0,1},{1,2},{2,3},{4,5},{5,6},{6,7},{8,9},{9,10},{10,11},{12,13},{... | collective-permute-start | bytes 3145736 | tf_op jit(solution)/shard_map/ppermute | solution.py:722
  427.7 17.7 %all-to-all-start.4 = ((bf16[4,40,768]{2,1,0:T(8,128)(2,1)}), bf16[4,40,768]{2,1,0:T(8,128)(2,1)S(1)}, u32[]{:S(2)}, u32[]{:S(2)}) async-start(bf16[4,40,768]{2,1,0:T(8,128)(2,1)} %fusion.10), calls=%async_computation.4 | async-start | bytes 491520 | tf_op jit(solution)/shard_map/all_to_all | solution.py:857
  (38 other events, 485.4 us)
Sparse Core Ops, SparseCore 0:
  39.3 27.3 all-gather.3
  75.5 41.5 all-gather.7
  119.0 76.5 all-gather.5
  259.9 127.6 reduce-scatter.2
  392.2 51.9 reduce-scatter.4

commit v15 on v14

--- a/solution.py
+++ b/solution.py
@@ -103,30 +103,27 @@
     block = pl.program_id(0)
     rows = q_ref.shape[0]
     subs = rows // QBLK
-    own = pl.ds(pl.multiple_of(block * rows, rows), rows)
-    causal = lax.broadcasted_iota(jnp.int32, (rows, rows), 0) >= lax.broadcasted_iota(jnp.int32, (rows, rows), 1)
     ones = jnp.ones((rows, HEAD_DIM), BF16)
     mem_ones = jnp.ones((top * MBLK, HEAD_DIM), BF16)
-    biases = [memory_bias(counts_ref, (block * subs + sub) * top, top, 1) for sub in range(subs)]
-    for head in range(heads):
-        columns = slice(head * HEAD_DIM, (head + 1) * HEAD_DIM)
-        remote = []
-        for sub in range(subs):
-            keys = pick_memory(mk_ref, chosen_ref, (block * subs + sub) * top, top, columns)
-            query = q_ref[sub * QBLK : (sub + 1) * QBLK, columns]
-            remote.append(dot(query, keys, NT) + biases[sub])
-        local = jnp.where(causal, dot(q_ref[:, columns], k_ref[own, columns], NT), NEGATIVE)
-        peak = jnp.max(local, -1, keepdims=True)
-        peak = jnp.maximum(peak, jnp.concatenate([jnp.max(r, -1, keepdims=True) for r in remote], 0))
-        values = jnp.concatenate([v_ref[own, columns], ones], 1)
-        acc = dot(jnp.exp2(local - peak).astype(BF16), values)
-        more = []
-        for sub in range(subs):
-            values = pick_memory(mv_ref, chosen_ref, (block * subs + sub) * top, top, columns)
-            weights = jnp.exp2(remote[sub] - peak[sub * QBLK : (sub + 1) * QBLK]).astype(BF16)
-            more.append(dot(weights, jnp.concatenate([values, mem_ones], 1)))
-        acc_s[head] = acc + jnp.concatenate(more, 0)
-        peak_s[head] = jnp.broadcast_to(peak, (rows, HEAD_DIM))
+    for sub in range(subs):
+        base = (block * subs + sub) * top
+        here = slice(sub * QBLK, (sub + 1) * QBLK)
+        span = (sub + 1) * QBLK
+        seen = pl.ds(pl.multiple_of(block * rows, rows), span)
+        row = lax.broadcasted_iota(jnp.int32, (QBLK, span), 0) + sub * QBLK
+        causal = row >= lax.broadcasted_iota(jnp.int32, (QBLK, span), 1)
+        bias = memory_bias(counts_ref, base, top, 1)
+        for head in range(heads):
+            columns = slice(head * HEAD_DIM, (head + 1) * HEAD_DIM)
+            query = q_ref[here, columns]
+            remote = dot(query, pick_memory(mk_ref, chosen_ref, base, top, columns), NT) + bias
+            local = jnp.where(causal, dot(query, k_ref[seen, columns], NT), NEGATIVE)
+            peak = jnp.maximum(jnp.max(local, -1, keepdims=True), jnp.max(remote, -1, keepdims=True))
+            values = jnp.concatenate([v_ref[seen, columns], ones[:span]], 1)
+            acc = dot(jnp.exp2(local - peak).astype(BF16), values)
+            values = jnp.concatenate([pick_memory(mv_ref, chosen_ref, base, top, columns), mem_ones], 1)
+            acc_s[head, here] = acc + dot(jnp.exp2(remote - peak).astype(BF16), values)
+            peak_s[head, here] = jnp.broadcast_to(peak, (QBLK, HEAD_DIM))
 
     def step(index, carry):
         there = pl.ds(pl.multiple_of(index * rows, rows), rows)
@@ -454,7 +451,7 @@
 
 def ffn_kernel(
     span, merged, tok_ref, att_ref, cot_ref, gain_ref, out_w, gate_w, up_w, down_w,
-    mixed_ref, grad_mid_ref, grad_att_ref, gain_grad_ref, grads_ref, *rest,
+    mixed_ref, grad_mid_ref, grad_att_ref, gain_grad_ref, out_grads_ref, grads_ref, *rest,
 ):
     if not merged:
         down_grads_ref, rest = rest[0], rest[1:]
@@ -482,7 +479,7 @@
 
     def copy_out(kind, which, index):
         source = (gate_s, up_s)[kind].at[which]
-        start = first + (lanes + kind * steps + index) * share
+        start = first + (kind * steps + index) * share
         target = grads_ref.at[:, pl.ds(start, share), :]
         return pltpu.make_async_copy(source, target, sems.at[kind, which])
 
@@ -547,7 +544,7 @@
             out_s[lane] = dot(turned_att, branch[:, columns]).astype(BF16).reshape(span, share, wide)
             more = pltpu.make_async_copy(
                 out_s.at[lane],
-                grads_ref.at[:, pl.ds(first + lane * share, share), :],
+                out_grads_ref.at[:, :, pl.ds(lane * wide, wide)],
                 late_sems.at[len(copies)],
             )
             more.start()
@@ -569,12 +566,13 @@
     share = width // span
     tall = hidden_width // span
     merged = tall % 16 == 0
-    total = (lanes + 2 * steps) * share + (lanes * tall if merged else 0)
+    total = 2 * steps * share + (lanes * tall if merged else 0)
     shapes = [
         jax.ShapeDtypeStruct((rows, width), BF16),
         jax.ShapeDtypeStruct((rows, width), F32),
         jax.ShapeDtypeStruct((rows, width), BF16),
         jax.ShapeDtypeStruct((1, width), F32),
+        jax.ShapeDtypeStruct((span, share, width), BF16),
         jax.ShapeDtypeStruct((span, total, wide), BF16),
     ]
     specs = [
@@ -582,6 +580,7 @@
         pl.BlockSpec((rows, width), lambda i: (0, 0)),
         pl.BlockSpec((rows, width), lambda i: (0, 0)),
         pl.BlockSpec((1, width), lambda i: (0, 0)),
+        pl.BlockSpec(memory_space=pl.ANY),
         pl.BlockSpec(memory_space=pl.ANY),
     ]
     if not merged:
@@ -625,7 +624,9 @@
     )(tokens, attended, upstream, gain, weights, weights, weights, w_down)
 
 
-def projection_grads_kernel(order_ref, tok_ref, gain_ref, w_ref, grad_ref, grad_w_ref, gain_grad_ref, raw_s):
+def projection_grads_kernel(
+    order_ref, tok_ref, gain_ref, w_ref, first_ref, other_ref, grad_w_ref, gain_grad_ref, raw_s
+):
     step = pl.program_id(0)
 
     @pl.when(step == 0)
@@ -634,7 +635,8 @@
 
     tokens = tok_ref[...].astype(F32)
     tokens = tokens * lax.rsqrt(jnp.mean(tokens * tokens, -1, keepdims=True) + EPSILON)
-    raw_s[...] += dot(tokens.astype(BF16), grad_ref[...], TN)
+    grad = jnp.where(step == 0, first_ref[...], other_ref[...])
+    raw_s[...] += dot(tokens.astype(BF16), grad, TN)
 
     @pl.when(step == pl.num_programs(0) - 1)
     def _():
@@ -643,9 +645,9 @@
         grad_w_ref[...] = (raw * gain_ref[...]).astype(BF16)
 
 
-def projection_grads(order, tokens_all, gain_column, w_qkv, grad):
+def projection_grads(order, tokens_all, gain_column, w_qkv, first_grad, other_grad):
     length, width = tokens_all.shape
-    columns = grad.shape[1]
+    columns = first_grad.shape[1]
     rows = min(2 * QBLK, length)
     return pl.pallas_call(
         projection_grads_kernel,
@@ -656,7 +658,8 @@
                 pl.BlockSpec((rows, width), lambda i, order: (order[i], 0)),
                 pl.BlockSpec((width, 1), lambda i, _: (0, 0)),
                 pl.BlockSpec((width, columns), lambda i, _: (0, 0)),
-                pl.BlockSpec((rows, columns), lambda i, _: (i, 0)),
+                pl.BlockSpec((rows, columns), lambda i, _: (0, 0)),
+                pl.BlockSpec((rows, columns), lambda i, _: (jnp.maximum(i - 1, 0), 0)),
             ],
             out_specs=[
                 pl.BlockSpec((width, columns), lambda i, _: (0, 0)),
@@ -673,7 +676,7 @@
             flops=2 * length * width * columns, bytes_accessed=2 * length * (width + columns), transcendentals=0
         ),
         name="projection_grads",
-    )(order, tokens_all, gain_column, w_qkv, grad)
+    )(order, tokens_all, gain_column, w_qkv, first_grad, other_grad)
 
 
 def after(value, earlier):
@@ -710,7 +713,7 @@
     return results, steps
 
 
-def chain_scatter(block, axis):
+def chain_scatter(block, axis, waits):
     size = lax.axis_size(axis)
     place = lax.axis_index(axis)
     arrived = []
@@ -718,7 +721,9 @@
         up, down = block(step, size - 1 - step + place), block(step, step - size + 1 + place)
         if step:
             up, down = up + arrived[-1][0].astype(F32), down + arrived[-1][1].astype(F32)
-        up, down = lax.optimization_barrier((up.astype(BF16), down.astype(BF16)))
+        ready = waits[step - 1](sent) if 0 < step <= len(waits) else None
+        up, down, _ = lax.optimization_barrier((up.astype(BF16), down.astype(BF16), ready))
+        sent = up, down
         rising = lax.ppermute(up, axis, [(i, i + 1) for i in range(step + 1)])
         falling = lax.ppermute(down, axis, [(i, i - 1) for i in range(size - 1 - step, size)])
         arrived.append(lax.optimization_barrier((rising, falling)))
@@ -785,11 +790,25 @@
     attended = lax.all_to_all(attended_heads, "fsdp", 0, 1, tiled=True)
 
     upstream = cotangent[0]
-    mixed, grad_middle, grad_attended, gain_two_grad, grads, *grad_down = feed_forward(
+    mixed, grad_middle, grad_attended, gain_two_grad, out_grads, grads, *grad_down = feed_forward(
         mine, attended, upstream, gain_two, first, down_full, span
     )
     grad_heads = lax.all_to_all(grad_attended, "fsdp", 1, 0, tiled=True)
     grads = lax.psum_scatter(grads, DP, scatter_dimension=0, tiled=True)[0]
+
+    core = lax.axis_index("core")
+
+    def over_cores(array):
+        array = array.reshape((span // 2, 2) + array.shape[1:])
+        taken = lax.ppermute(lax.dynamic_index_in_dim(array, 1 - core, 1, keepdims=False), "core", [(0, 1), (1, 0)])
+        return (lax.dynamic_index_in_dim(array, core, 1, keepdims=False).astype(F32) + taken.astype(F32)).astype(BF16)
+
+    def over_chips(array):
+        return sum(piece.astype(F32) for piece in direct_exchange(array, "chip")).astype(BF16)
+
+    out_grads = over_cores(out_grads)
+    grad_heads = after(grad_heads, out_grads)
+    out_grads = over_chips(out_grads)
 
     place = lax.axis_index("fsdp").astype(jnp.int32)
     count = length // min(2 * QBLK, length)
@@ -804,7 +823,6 @@
         low.reshape(1), chosen_all, counts_all, qkv, memory, grad_heads, attended_heads, lse, cosine, sine, w_qkv,
         sums, heads, top,
     )
-    grad_qkv = jnp.concatenate([first_grad, other_grad], 0)
     order = jnp.concatenate([first_number.reshape(1), low + jnp.arange(count - 1, dtype=jnp.int32)])
     block_rows = first_partial.shape[0]
 
@@ -819,19 +837,24 @@
         inside = (start >= first_number * block_rows) & (start < (first_number + 1) * block_rows)
         return jnp.where(inside, from_first, from_others).astype(F32)
 
-    own_term, arrived = chain_scatter(term, "fsdp")
+    kept = []
+
+    def make_projection_grads(sent):
+        kept.extend(
+            projection_grads(
+                order, gathered, gain_one.reshape(width, 1), w_qkv, after(first_grad, sent), after(other_grad, sent)
+            )
+        )
+        return kept
+
+    own_term, arrived = chain_scatter(term, "fsdp", [lambda sent: out_grads, make_projection_grads])
+    grad_w_qkv, gain_one_grad = kept
     grads = after(grads, arrived[-1])
 
-    grad_w_qkv, gain_one_grad = projection_grads(order, gathered, gain_one.reshape(width, 1), w_qkv, grad_qkv)
     gains = jnp.stack([gain_one_grad.reshape(span, -1), gain_two_grad.reshape(span, -1)], 1)
     gains = jnp.pad(gains.astype(BF16), ((0, 0), (0, extra - 2), (0, 3 * wide - gains.shape[2])))
     late = jnp.concatenate([grad_w_qkv.reshape(span, -1, 3 * wide), gains], 1)
-    late = late.reshape(span // 2, 2, late.shape[1], 3 * wide)
-    core = lax.axis_index("core")
-    taken = lax.ppermute(lax.dynamic_index_in_dim(late, 1 - core, 1, keepdims=False), "core", [(0, 1), (1, 0)])
-    late = lax.dynamic_index_in_dim(late, core, 1, keepdims=False).astype(F32) + taken.astype(F32)
-    late = after(late.astype(BF16), arrived[0])
-    late = sum(piece.astype(F32) for piece in direct_exchange(late, "chip")).astype(BF16)
+    late = over_chips(after(over_cores(late), arrived[0]))
     strip = grads.shape[1]
     lanes = width // strip
     tall = w_down.shape[0]
@@ -854,7 +877,10 @@
     gains = late[-extra : 2 - extra, : ring * share].reshape(2, ring, share).transpose(1, 0, 2)
     gains = jnp.pad(gains, ((0, 0), (0, extra - 2), (0, 3 * wide - share)))
     late = jnp.concatenate([late[:-extra].reshape(ring, share, 3 * wide), gains], 1)
+    out_grads = jnp.pad(out_grads.reshape(ring, share, width), ((0, 0), (0, extra), (0, 0)))
+    late = jnp.concatenate([late, out_grads], 2)
     late = after(lax.all_to_all(late, "fsdp", 0, 0, tiled=True), tokens_grad).astype(F32)
+    out_share = jnp.sum(late[:, :share, 3 * wide :], 0)
     projections = [
         late[:, :share, part * wide : (part + 1) * wide].transpose(1, 0, 2).reshape(share, width)
         for part in range(3)
@@ -862,16 +888,16 @@
     gain_shares = jnp.sum(late[:, share : share + 2, :share], 0)
 
     pieces = lax.psum_scatter(pieces, "fsdp", scatter_dimension=0, tiled=True)
-    pieces = after(pieces, (tokens_grad, projections, gain_shares))[0].astype(F32)
+    pieces = after(pieces, (tokens_grad, projections, out_share, gain_shares))[0].astype(F32)
     down_share = pieces[: lanes * tall].reshape(lanes, tall, strip).transpose(1, 0, 2).reshape(tall, width)
     others = pieces[lanes * tall :].reshape(-1, share, strip).transpose(1, 0, 2).reshape(share, -1)
     return (
         mixed[None],
         tokens_grad[None],
         *projections,
-        others[:, :width],
-        others[:, width : width + hidden_width],
-        others[:, width + hidden_width :],
+        out_share,
+        others[:, :hidden_width],
+        others[:, hidden_width:],
         down_share,
         gain_shares[0],
         gain_shares[1],

time: 468 us -> 475 us (1.015)
    all_to_all x1, waiting for transfers between devices: 6.57 us -> 19.8 us  [body(): lax.all_to_all(late, 'fsdp', 0, 0, tiled=True)]
    all_to_all x1, waiting for transfers between devices: 14.8 us -> 5.36 us  [body(): grad_heads = lax.all_to_all(grad_attended, 'fsdp', 1, 0, tiled=True)]
    convert_element_type x4 -> x6, other arithmetic: 11 us -> 14.8 us  [the longest x2 9.28 us: chain_scatter(): down.astype(BF16)]
    ppermute x3 -> x6, waiting for transfers between devices: 8.65 us -> 9.76 us  [direct_exchange(): lax.ppermute(give, axis, [(i, (i + far) % size) for i in range(size)])]
    unnamed x53 -> x59, local copies, waits for them, and re-layouts: 9.32 us -> 9.99 us
  transfers between devices with their start and end apart: 38 -> 42, of which waited for: 18 -> 18; matrix products, arithmetic and copies ran while one was open for 12% -> 14% of each run, Pallas kernels for 17% -> 17%
where the time goes in v15:
time: 475 us; the launch traced here: 467 us
  waiting for transfers between devices  168 us (35%)
  Pallas kernels  123 us (26%)
  starting transfers between devices  78.5 us (17%)
  other arithmetic  47.2 us (10%)
  local copies, waits for them, and re-layouts  35.4 us (7%)
  between operations  14.8 us (3%)
    ppermute x9, waiting for transfers between devices, chain_gather(): falling = tuple((lax.ppermute(block, axis, down) for block in falling))  81.8 us
    pallas_call x1, Pallas kernels, feed_forward(): pl.pallas_call(functools.partial(ffn_kernel, span, merged), grid=(steps,)...  44 us
    pallas_call x1, Pallas kernels, other_blocks(): pl.pallas_call(functools.partial(other_blocks_kernel, heads, top), grid_s...  24.6 us
    ppermute x3, waiting for transfers between devices, chain_scatter(): rising = lax.ppermute(up, axis, [(i, i + 1) for i in range(step + 1)])  24 us
    ppermute x9, starting transfers between devices, chain_gather(): rising = tuple((lax.ppermute(block, axis, up) for block in rising))  21.1 us
    pallas_call x1, Pallas kernels, attend_forward(): pl.pallas_call(functools.partial(forward_kernel, heads, top), grid_spec=p...  19.9 us
    all_to_all x1, waiting for transfers between devices, body(): lax.all_to_all(late, 'fsdp', 0, 0, tiled=True)  19.8 us
    pallas_call x1, Pallas kernels, first_block(): pl.pallas_call(functools.partial(first_block_kernel, heads, top), grid_sp...  18 us
  transfers between devices with their start and end apart: 42, of which 18 were waited for; matrix products, arithmetic and copies ran while one was open for 14% of the time, Pallas kernels for 17%

profile of v15, /device:TPU:0, one launch (start us, length us, event | category | flops | bytes accessed | tf_op | source)
XLA Modules:
  0.0 466.5 jit_solution(885968416016496837)
XLA Ops:
  11.2 5.6 %collective-permute-start = (bf16[32,6656]{1,0:T(8,128)(2,1)S(1)}, bf16[32,6656]{1,0:T(8,128)(2,1)S(1)}, u32[]{:S(2)}, u32[]{:S(2)}) collective-permute-start(bf16[32,6656]{1,0:T(8,128)(2,1)S(1)} %constant_dynamic-update-slice_fusion), channel_id=1, source_target_pairs={{0,1},{1,2},{2,3},{4,5},{5,6},{6,7},{8,9},{9,10},{10,11},{12,13},{... | collective-permute-start | bytes 1277960 | tf_op jit(solution)/shard_map/ppermute | solution.py:694
  43.2 14.5 %collective-permute-done.7 = bf16[88,1024]{1,0:T(8,128)(2,1)S(1)} collective-permute-done((bf16[88,1024]{1,0:T(8,128)(2,1)S(1)}, bf16[88,1024]{1,0:T(8,128)(2,1)S(1)}, u32[]{:S(2)}, u32[]{:S(2)}) %collective-permute-start.7) | collective-permute-done | bytes 180256 | tf_op jit(solution)/shard_map/ppermute | solution.py:695
  61.7 11.5 %collective-permute-done.17 = bf16[88,1024]{1,0:T(8,128)(2,1)} collective-permute-done((bf16[88,1024]{1,0:T(8,128)(2,1)S(1)}, bf16[88,1024]{1,0:T(8,128)(2,1)}, u32[]{:S(2)}, u32[]{:S(2)}) %collective-permute-start.17) | collective-permute-done | bytes 180256 | tf_op jit(solution)/shard_map/ppermute | solution.py:695
  78.6 5.6 %collective-permute-start.8 = (bf16[512,1024]{1,0:T(8,128)(2,1)S(1)}, bf16[512,1024]{1,0:T(8,128)(2,1)}, u32[]{:S(2)}, u32[]{:S(2)}) collective-permute-start(bf16[512,1024]{1,0:T(8,128)(2,1)S(1)} %bitcast.110), channel_id=1, source_target_pairs={{0,1},{1,2},{2,3},{4,5},{5,6},{6,7},{8,9},{9,10},{10,11},{12,13},{... | collective-permute-start | bytes 3145736 | tf_op jit(solution)/shard_map/ppermute | solution.py:694
  84.1 16.5 %collective-permute-done.11 = bf16[512,1024]{1,0:T(8,128)(2,1)S(1)} collective-permute-done((bf16[512,1024]{1,0:T(8,128)(2,1)S(1)}, bf16[512,1024]{1,0:T(8,128)(2,1)S(1)}, u32[]{:S(2)}, u32[]{:S(2)}) %collective-permute-start.11) | collective-permute-done | bytes 1048608 | tf_op jit(solution)/shard_map/ppermute | solution.py:695
  106.6 17.1 %collective-permute-done.12 = bf16[512,1024]{1,0:T(8,128)(2,1)} collective-permute-done((bf16[512,1024]{1,0:T(8,128)(2,1)S(1)}, bf16[512,1024]{1,0:T(8,128)(2,1)}, u32[]{:S(2)}, u32[]{:S(2)}) %collective-permute-start.12) | collective-permute-done | bytes 1048608 | tf_op jit(solution)/shard_map/ppermute | solution.py:695
  132.7 5.5 %all-to-all-start.1 = ((bf16[4,256,512]{2,1,0:T(8,128)(2,1)}), bf16[4,256,512]{2,1,0:T(8,128)(2,1)}, u32[]{:S(2)}, u32[]{:S(2)}) async-start(bf16[4,256,512]{2,1,0:T(8,128)(2,1)} %pad_maximum_fusion.5), calls=%async_computation.1 | async-start | bytes 2097152 | tf_op jit(solution)/shard_map/all_to_all | solution.py:784
  141.1 18.4 %collective-permute-done.13 = bf16[512,1024]{1,0:T(8,128)(2,1)} collective-permute-done((bf16[512,1024]{1,0:T(8,128)(2,1)}, bf16[512,1024]{1,0:T(8,128)(2,1)}, u32[]{:S(2)}, u32[]{:S(2)}) %collective-permute-start.13) | collective-permute-done | bytes 1048608 | tf_op jit(solution)/shard_map/ppermute | solution.py:695
  164.3 7.4 %project_qkv.1.q_ref.k_ref.v_ref.qkv_ref = bf16[2048,768]{1,0:T(8,128)(2,1)} custom-call(bf16[2048,1024]{1,0:T(8,128)(2,1)} %pad_maximum_fusion.tok_ref, f32[1,1024]{1,0:T(1,128)S(1)} %reshape.210.gain_ref, bf16[1024,768]{1,0:T(8,128)(2,1)S(1)} %bitcast.103, f32[2048,128]{1,0:T(8,128)S(1)} %get-tuple-element.153.cos_ref, f32[2048,128]{1,0:T(8,128)S(1)} %copy-done.3), custom_call_target="tpu_custom_call" | custom-call | flops 3221225472 | bytes 14680064 | tf_op jit(solution)/shard_map/project_qkv/pallas_call | solution.py:62
  171.7 19.9 %attend_forward.1 = (bf16[2048,256]{1,0:T(8,128)(2,1)}, f32[2048,2]{1,0:T(8,128)S(1)}) custom-call(s32[32]{0:T(128)S(1)} %reshape_squeeze.24.chosen_ref, s32[32]{0:T(128)S(1)} %reshape_squeeze.25.counts_ref, bf16[2048,768]{1,0:T(8,128)(2,1)} %project_qkv.1.q_ref.k_ref.v_ref.qkv_ref, bf16[2048,768]{1,0:T(8,128)(2,1)} %project_qkv.1.q_ref.k_ref.v_ref.qkv_ref, ...), custom_call_target="tpu_custom_call" | custom-call | flops 3221225472 | bytes 4194304 | tf_op jit(solution)/shard_map/attend_forward/pallas_call | solution.py:154
  192.5 4.6 all-to-all-start.2
  198.1 15.0 %all-to-all-done.2 = bf16[4,512,256]{2,1,0:T(8,128)(2,1)S(1)} async-done(((bf16[4,512,256]{2,1,0:T(8,128)(2,1)}), bf16[4,512,256]{2,1,0:T(8,128)(2,1)S(1)}, u32[]{:S(2)}, u32[]{:S(2)}) %all-to-all-start.2) | async-done | bytes 1048608 | tf_op jit(solution)/shard_map/all_to_all | solution.py:790
  214.2 44.0 %feed_forward.1 = (bf16[512,1024]{1,0:T(8,128)(2,1)}, f32[512,1024]{1,0:T(8,128)}, bf16[512,1024]{1,0:T(8,128)(2,1)}, f32[1,1024]{1,0:T(1,128)}, bf16[8,128,1024...) custom-call(bf16[512,1024]{1,0:T(8,128)(2,1)} %bitcast.108, bf16[512,1024]{1,0:T(8,128)(2,1)} %bitcast.126, ...), custom_call_target="tpu_custom_call" | custom-call | flops 29796335616 | bytes 38797312 | tf_op jit(solution)/shard_map/feed_forward/pallas_call | solution.py:589
  260.5 4.3 all-to-all-start.3
  275.4 5.4 %all-to-all-done.3 = bf16[512,4,256]{2,0,1:T(8,128)(2,1)} async-done(((bf16[512,4,256]{2,0,1:T(8,128)(2,1)}), bf16[512,4,256]{2,0,1:T(8,128)(2,1)}, u32[]{:S(2)}, u32[]{:S(2)}) %all-to-all-start.3) | async-done | bytes 1048608 | tf_op jit(solution)/shard_map/all_to_all | solution.py:796
  280.8 18.0 %first_block.1 = (bf16[512,1024]{1,0:T(8,128)(2,1)}, bf16[512,768]{1,0:T(8,128)(2,1)}, f32[2048,256]{1,0:T(8,128)}, f32[2048,256]{1,0:T(8,128)}, f32[2048,256]{1,0:T(8,128)}) custom-call(s32[32]{0:T(128)} %copy-done.6, s32[32]{0:T(128)} %copy-done.5, s32[2]{0:T(128)} %pad_add_fusion.plan_ref, bf16[2048,768]{1,0:T(8,128)(2,1)} %project_qkv.1.q_ref.k_ref.v_ref.qkv_ref, ...), custom_call_target="tpu_custom_call" | custom-call | flops 4294967296 | bytes 20971520 | tf_op jit(solution)/shard_map/first_block/pallas_call | solution.py:308
  303.1 24.6 %other_blocks.1 = (bf16[1536,1024]{1,0:T(8,128)(2,1)}, bf16[1536,768]{1,0:T(8,128)(2,1)}) custom-call(s32[32]{0:T(128)} %copy-done.6, s32[32]{0:T(128)} %copy-done.5, s32[1]{0:T(128)} %bitcast.19.plan_ref, bf16[2048,768]{1,0:T(8,128)(2,1)} %project_qkv.1.q_ref.k_ref.v_ref.qkv_ref, bf16[2048,768]{1,0:T(8,128)(2,1)} %project_qkv.1.q_ref.k_ref.v_ref.qkv_ref, ...), custom_call_target="tpu_custom_call" | custom-call | flops 8053063680 | bytes 20971520 | tf_op jit(solution)/shard_map/other_blocks/pallas_call | solution.py:410
  329.7 5.1 %add_convert_fusion.2 = (bf16[512,1024]{1,0:T(8,128)(2,1)}, bf16[512,1024]{1,0:T(8,128)(2,1)}) fusion(bf16[512,1024]{1,0:T(8,128)(2,1)} %copy-done.19, bf16[512,1024]{1,0:T(8,128)(2,1)S(1)} %copy-done.9, bf16[1536,1024]{1,0:T(8,128)(2,1)} %get-tuple-element.88, s32[]{:T(128)S(6)} %min.47, pred[]{:T(512)S(6)} %and.37, bf16[512,1024]{1,0:T(8,128)(2,1)} %copy-done.18, ...), kind=kLoop, calls=%fused_computation.14 | loop fusion | flops 5242880 | bytes 7340042 | tf_op jit(solution)/shard_map/convert_element_type | solution.py:725
  343.2 8.7 %projection_grads.1 = (bf16[1024,768]{1,0:T(8,128)(2,1)S(1)}, f32[1024,1]{1,0:T(8,128)S(1)}) custom-call(s32[4]{0:T(128)S(1)} %pad_add_fusion.1.order_ref, bf16[2048,1024]{1,0:T(8,128)(2,1)} %pad_maximum_fusion.tok_ref, f32[1024,1]{1,0:T(8,128)S(1)} %copy-done.4, bf16[1024,768]{1,0:T(8,128)(2,1)S(1)} %bitcast.106, bf16[512,768]{1,0:T(8,128)(2,1)S(1)} %copy-done.8, ...), custom_call_target="tpu_custom_call" | custom-call | flops 3221225472 | bytes 7340032 | tf_op jit(solution)/shard_map/projection_grads/pallas_call | solution.py:652
  351.9 5.6 %collective-permute-done.24 = bf16[512,1024]{1,0:T(8,128)(2,1)} collective-permute-done((bf16[512,1024]{1,0:T(8,128)(2,1)}, bf16[512,1024]{1,0:T(8,128)(2,1)}, u32[]{:S(2)}, u32[]{:S(2)}) %collective-permute-start.24) | collective-permute-done | bytes 1048608 | tf_op jit(solution)/shard_map/ppermute | solution.py:727
  361.8 8.1 %collective-permute-start.26 = (bf16[512,1024]{1,0:T(8,128)(2,1)}, bf16[512,1024]{1,0:T(8,128)(2,1)S(1)}, u32[]{:S(2)}, u32[]{:S(2)}) collective-permute-start(bf16[512,1024]{1,0:T(8,128)(2,1)} %get-tuple-element.103), channel_id=1, source_target_pairs={{0,1},{1,2},{2,3},{4,5},{5,6},{6,7},{8,9},{9,10},{10,11},{12,13},{... | collective-permute-start | bytes 3145736 | tf_op jit(solution)/shard_map/ppermute | solution.py:727
  371.7 18.4 %collective-permute-done.26 = bf16[512,1024]{1,0:T(8,128)(2,1)S(1)} collective-permute-done((bf16[512,1024]{1,0:T(8,128)(2,1)}, bf16[512,1024]{1,0:T(8,128)(2,1)S(1)}, u32[]{:S(2)}, u32[]{:S(2)}) %collective-permute-start.26) | collective-permute-done | bytes 1048608 | tf_op jit(solution)/shard_map/ppermute | solution.py:727
  407.5 6.1 %collective-permute-done.29 = bf16[136,768]{1,0:T(8,128)(2,1)} collective-permute-done((bf16[136,768]{1,0:T(8,128)(2,1)}, bf16[136,768]{1,0:T(8,128)(2,1)}, u32[]{:S(2)}, u32[]{:S(2)}) %collective-permute-start.29) | collective-permute-done | bytes 208928 | tf_op jit(solution)/shard_map/ppermute | solution.py:739
  431.9 19.8 %all-to-all-done.4 = bf16[4,40,1792]{2,1,0:T(8,128)(2,1)} async-done(((bf16[4,40,1792]{2,1,0:T(8,128)(2,1)}), bf16[4,40,1792]{2,1,0:T(8,128)(2,1)}, u32[]{:S(2)}, u32[]{:S(2)}) %all-to-all-start.4) | async-done | bytes 573472 | tf_op jit(solution)/shard_map/all_to_all | solution.py:882
  (216 shorter events, 142.1 us)
Async XLA Ops:
  9.9 28.4 %collective-permute-start.2 = (bf16[32,6656]{1,0:T(8,128)(2,1)S(1)}, bf16[32,6656]{1,0:T(8,128)(2,1)S(1)}, u32[]{:S(2)}, u32[]{:S(2)}) collective-permute-start(bf16[32,6656]{1,0:T(8,128)(2,1)S(1)} %constant_dynamic-update-slice_fusion), channel_id=1, source_target_pairs={{1,0},{2,1},{3,2},{5,4},{6,5},{7,6},{9,8},{10,9},{11,10},{13,12},{... | collective-permute-start | bytes 1277960 | tf_op jit(solution)/shard_map/ppermute | solution.py:695
  11.2 27.1 %collective-permute-start = (bf16[32,6656]{1,0:T(8,128)(2,1)S(1)}, bf16[32,6656]{1,0:T(8,128)(2,1)S(1)}, u32[]{:S(2)}, u32[]{:S(2)}) collective-permute-start(bf16[32,6656]{1,0:T(8,128)(2,1)S(1)} %constant_dynamic-update-slice_fusion), channel_id=1, source_target_pairs={{0,1},{1,2},{2,3},{4,5},{5,6},{6,7},{8,9},{9,10},{10,11},{12,13},{... | collective-permute-start | bytes 1277960 | tf_op jit(solution)/shard_map/ppermute | solution.py:694
  27.0 111.4 %all-gather.4.cloned.1.call-start = ((), (), s32[]{:S(2)}) async-start(), calls=%async_computation.7 | async-start | bytes 2211840 | tf_op jit(solution)/shard_map/all_gather | solution.py:774
  39.1 175.1 %all-gather.8.cloned.1.call-start = ((), (), s32[]{:S(2)}) async-start(), calls=%async_computation.9 | async-start | bytes 6488064 | tf_op jit(solution)/shard_map/all_gather | solution.py:785
  75.4 138.8 %all-gather.6.cloned.1.call-start = ((), (), s32[]{:S(2)}) async-start(), calls=%async_computation.8 | async-start | bytes 15335424 | tf_op jit(solution)/shard_map/all_gather | solution.py:778
  77.3 23.3 %collective-permute-start.11 = (bf16[512,1024]{1,0:T(8,128)(2,1)S(1)}, bf16[512,1024]{1,0:T(8,128)(2,1)S(1)}, u32[]{:S(2)}, u32[]{:S(2)}) collective-permute-start(bf16[512,1024]{1,0:T(8,128)(2,1)S(1)} %bitcast.109), channel_id=1, source_target_pairs={{1,0},{2,1},{3,2},{5,4},{6,5},{7,6},{9,8},{10,9},{11,10},{13,12},{... | collective-permute-start | bytes 3145736 | tf_op jit(solution)/shard_map/ppermute | solution.py:695
  78.6 23.3 %collective-permute-start.8 = (bf16[512,1024]{1,0:T(8,128)(2,1)S(1)}, bf16[512,1024]{1,0:T(8,128)(2,1)}, u32[]{:S(2)}, u32[]{:S(2)}) collective-permute-start(bf16[512,1024]{1,0:T(8,128)(2,1)S(1)} %bitcast.110), channel_id=1, source_target_pairs={{0,1},{1,2},{2,3},{4,5},{5,6},{6,7},{8,9},{9,10},{10,11},{12,13},{... | collective-permute-start | bytes 3145736 | tf_op jit(solution)/shard_map/ppermute | solution.py:694
  100.6 23.1 %collective-permute-start.12 = (bf16[512,1024]{1,0:T(8,128)(2,1)S(1)}, bf16[512,1024]{1,0:T(8,128)(2,1)}, u32[]{:S(2)}, u32[]{:S(2)}) collective-permute-start(bf16[512,1024]{1,0:T(8,128)(2,1)S(1)} %collective-permute-done.11), channel_id=1, source_target_pairs={{1,0},{2,1},{5,4},{6,5},{9,8},{10,9},{13,12},{14,13},{17,16},{18,1... | collective-permute-start | bytes 3145736 | tf_op jit(solution)/shard_map/ppermute | solution.py:695
  101.9 23.1 %collective-permute-start.9 = (bf16[512,1024]{1,0:T(8,128)(2,1)}, bf16[512,1024]{1,0:T(8,128)(2,1)}, u32[]{:S(2)}, u32[]{:S(2)}) collective-permute-start(bf16[512,1024]{1,0:T(8,128)(2,1)} %collective-permute-done.8), channel_id=1, source_target_pairs={{1,2},{2,3},{5,6},{6,7},{9,10},{10,11},{13,14},{14,15},{17,18},{18... | collective-permute-start | bytes 3145736 | tf_op jit(solution)/shard_map/ppermute | solution.py:694
  123.7 35.8 %collective-permute-start.13 = (bf16[512,1024]{1,0:T(8,128)(2,1)}, bf16[512,1024]{1,0:T(8,128)(2,1)}, u32[]{:S(2)}, u32[]{:S(2)}) collective-permute-start(bf16[512,1024]{1,0:T(8,128)(2,1)} %collective-permute-done.12), channel_id=1, source_target_pairs={{1,0},{5,4},{9,8},{13,12},{17,16},{21,20},{25,24},{29,28}} | collective-permute-start | bytes 3145736 | tf_op jit(solution)/shard_map/ppermute | solution.py:695
  125.0 34.5 %collective-permute-start.10 = (bf16[512,1024]{1,0:T(8,128)(2,1)}, bf16[512,1024]{1,0:T(8,128)(2,1)}, u32[]{:S(2)}, u32[]{:S(2)}) collective-permute-start(bf16[512,1024]{1,0:T(8,128)(2,1)} %collective-permute-done.9), channel_id=1, source_target_pairs={{2,3},{6,7},{10,11},{14,15},{18,19},{22,23},{26,27},{30,31}} | collective-permute-start | bytes 3145736 | tf_op jit(solution)/shard_map/ppermute | solution.py:694
  132.7 38.9 %all-to-all-start.1 = ((bf16[4,256,512]{2,1,0:T(8,128)(2,1)}), bf16[4,256,512]{2,1,0:T(8,128)(2,1)}, u32[]{:S(2)}, u32[]{:S(2)}) async-start(bf16[4,256,512]{2,1,0:T(8,128)(2,1)} %pad_maximum_fusion.5), calls=%async_computation.1 | async-start | bytes 2097152 | tf_op jit(solution)/shard_map/all_to_all | solution.py:784
  192.5 20.5 %all-to-all-start.2 = ((bf16[4,512,256]{2,1,0:T(8,128)(2,1)}), bf16[4,512,256]{2,1,0:T(8,128)(2,1)S(1)}, u32[]{:S(2)}, u32[]{:S(2)}) async-start(bf16[4,512,256]{2,1,0:T(8,128)(2,1)} %bitcast.8), calls=%async_computation.2 | async-start | bytes 2097152 | tf_op jit(solution)/shard_map/all_to_all | solution.py:790
  197.2 197.1 %reduce-scatter.3.cloned.1.call-start = ((), (), s32[]{:S(2)}) async-start(), calls=%async_computation.10 | async-start | bytes 19464192 | tf_op jit(solution)/shard_map/reduce_scatter | solution.py:797
  264.8 191.3 %reduce-scatter.5.cloned.1.call-start = ((), (), s32[]{:S(2)}) async-start(), calls=%async_computation.11 | async-start | bytes 2703360 | tf_op jit(solution)/shard_map/reduce_scatter | solution.py:890
  272.0 29.1 %collective-permute-start.21 = (bf16[128,1024]{1,0:T(8,128)(2,1)}, bf16[128,1024]{1,0:T(8,128)(2,1)S(1)}, u32[]{:S(2)}, u32[]{:S(2)}) collective-permute-start(bf16[128,1024]{1,0:T(8,128)(2,1)} %get-tuple-element.134), channel_id=1, source_target_pairs={{0,8},{8,16},{16,24},{24,0},{1,9},{9,17},{17,25},{25,1},{2,10},{10... | collective-permute-start | bytes 786440 | tf_op jit(solution)/shard_map/ppermute | solution.py:739
  273.1 28.1 %collective-permute-start.23 = (bf16[128,1024]{1,0:T(8,128)(2,1)}, bf16[128,1024]{1,0:T(8,128)(2,1)}, u32[]{:S(2)}, u32[]{:S(2)}) collective-permute-start(bf16[128,1024]{1,0:T(8,128)(2,1)} %get-tuple-element.135), channel_id=1, source_target_pairs={{0,24},{8,0},{16,8},{24,16},{1,25},{9,1},{17,9},{25,17},{2,26},{10... | collective-permute-start | bytes 786440 | tf_op jit(solution)/shard_map/ppermute | solution.py:739
  275.4 26.4 %collective-permute-start.22 = (bf16[128,1024]{1,0:T(8,128)(2,1)}, bf16[128,1024]{1,0:T(8,128)(2,1)}, u32[]{:S(2)}, u32[]{:S(2)}) collective-permute-start(bf16[128,1024]{1,0:T(8,128)(2,1)} %get-tuple-element.136), channel_id=1, source_target_pairs={{0,16},{8,24},{16,0},{24,8},{1,17},{9,25},{17,1},{25,9},{2,18},{10... | collective-permute-start | bytes 786440 | tf_op jit(solution)/shard_map/ppermute | solution.py:739
  298.8 29.0 %collective-permute-start.19 = (bf16[512,1024]{1,0:T(8,128)(2,1)}, bf16[512,1024]{1,0:T(8,128)(2,1)S(1)}, u32[]{:S(2)}, u32[]{:S(2)}) collective-permute-start(bf16[512,1024]{1,0:T(8,128)(2,1)} %get-tuple-element.90), channel_id=1, source_target_pairs={{0,1},{4,5},{8,9},{12,13},{16,17},{20,21},{24,25},{28,29}} | collective-permute-start | bytes 3145736 | tf_op jit(solution)/shard_map/ppermute | solution.py:727
  300.2 27.6 %collective-permute-start.20 = (bf16[512,1024]{1,0:T(8,128)(2,1)}, bf16[512,1024]{1,0:T(8,128)(2,1)S(1)}, u32[]{:S(2)}, u32[]{:S(2)}) collective-permute-start(bf16[512,1024]{1,0:T(8,128)(2,1)} %get-tuple-element.90), channel_id=1, source_target_pairs={{3,2},{7,6},{11,10},{15,14},{19,18},{23,22},{27,26},{31,30}} | collective-permute-start | bytes 3145736 | tf_op jit(solution)/shard_map/ppermute | solution.py:728
  334.8 22.8 %collective-permute-start.24 = (bf16[512,1024]{1,0:T(8,128)(2,1)}, bf16[512,1024]{1,0:T(8,128)(2,1)}, u32[]{:S(2)}, u32[]{:S(2)}) collective-permute-start(bf16[512,1024]{1,0:T(8,128)(2,1)} %get-tuple-element.93), channel_id=1, source_target_pairs={{0,1},{1,2},{4,5},{5,6},{8,9},{9,10},{12,13},{13,14},{16,17},{17,1... | collective-permute-start | bytes 3145736 | tf_op jit(solution)/shard_map/ppermute | solution.py:727
  361.8 28.4 %collective-permute-start.26 = (bf16[512,1024]{1,0:T(8,128)(2,1)}, bf16[512,1024]{1,0:T(8,128)(2,1)S(1)}, u32[]{:S(2)}, u32[]{:S(2)}) collective-permute-start(bf16[512,1024]{1,0:T(8,128)(2,1)} %get-tuple-element.103), channel_id=1, source_target_pairs={{0,1},{1,2},{2,3},{4,5},{5,6},{6,7},{8,9},{9,10},{10,11},{12,13},{... | collective-permute-start | bytes 3145736 | tf_op jit(solution)/shard_map/ppermute | solution.py:727
  369.9 24.4 %collective-permute-start.27 = (bf16[512,1024]{1,0:T(8,128)(2,1)}, bf16[512,1024]{1,0:T(8,128)(2,1)}, u32[]{:S(2)}, u32[]{:S(2)}) collective-permute-start(bf16[512,1024]{1,0:T(8,128)(2,1)} %get-tuple-element.104), channel_id=1, source_target_pairs={{1,0},{2,1},{3,2},{5,4},{6,5},{7,6},{9,8},{10,9},{11,10},{13,12},{... | collective-permute-start | bytes 3145736 | tf_op jit(solution)/shard_map/ppermute | solution.py:728
  421.2 30.5 %all-to-all-start.4 = ((bf16[4,40,1792]{2,1,0:T(8,128)(2,1)}), bf16[4,40,1792]{2,1,0:T(8,128)(2,1)}, u32[]{:S(2)}, u32[]{:S(2)}) async-start(bf16[4,40,1792]{2,1,0:T(8,128)(2,1)} %fusion.10), calls=%async_computation.4 | async-start | bytes 1146880 | tf_op jit(solution)/shard_map/all_to_all | solution.py:882
  (45 other events, 567.9 us)
Sparse Core Ops, SparseCore 0:
  39.3 27.3 all-gather.3
  75.5 41.5 all-gather.7
  119.0 76.5 all-gather.5
  258.3 118.2 reduce-scatter.2
  398.7 50.6 reduce-scatter.4

commit v16 on v15

--- a/solution.py
+++ b/solution.py
@@ -806,10 +806,6 @@
     def over_chips(array):
         return sum(piece.astype(F32) for piece in direct_exchange(array, "chip")).astype(BF16)
 
-    out_grads = over_cores(out_grads)
-    grad_heads = after(grad_heads, out_grads)
-    out_grads = over_chips(out_grads)
-
     place = lax.axis_index("fsdp").astype(jnp.int32)
     count = length // min(2 * QBLK, length)
     is_last = (place < ring // 2).astype(jnp.int32)
@@ -847,14 +843,10 @@
         )
         return kept
 
-    own_term, arrived = chain_scatter(term, "fsdp", [lambda sent: out_grads, make_projection_grads])
+    own_term, arrived = chain_scatter(term, "fsdp", [lambda sent: None, make_projection_grads])
     grad_w_qkv, gain_one_grad = kept
     grads = after(grads, arrived[-1])
 
-    gains = jnp.stack([gain_one_grad.reshape(span, -1), gain_two_grad.reshape(span, -1)], 1)
-    gains = jnp.pad(gains.astype(BF16), ((0, 0), (0, extra - 2), (0, 3 * wide - gains.shape[2])))
-    late = jnp.concatenate([grad_w_qkv.reshape(span, -1, 3 * wide), gains], 1)
-    late = over_chips(after(over_cores(late), arrived[0]))
     strip = grads.shape[1]
     lanes = width // strip
     tall = w_down.shape[0]
@@ -866,6 +858,14 @@
         grads = grads[ring * tall * lanes :]
     grads = grads.reshape(-1, ring, share, strip).transpose(1, 0, 2, 3)
     pieces = jnp.concatenate([down.reshape(ring, -1, strip), grads.reshape(ring, -1, strip)], 1)
+
+    gains = jnp.stack([gain_one_grad.reshape(span, -1), gain_two_grad.reshape(span, -1)], 1)
+    gains = jnp.pad(gains.astype(BF16), ((0, 0), (0, extra - 2), (0, 3 * wide - gains.shape[2])))
+    late = jnp.concatenate([grad_w_qkv.reshape(span, -1, 3 * wide), gains], 1)
+    late = jnp.concatenate([late, jnp.pad(out_grads, ((0, 0), (0, extra), (0, 0)))], 2)
+    late = over_chips(over_cores(after(late, pieces)))
+    late, out_grads = late[:, : 3 * wide], late[:-extra, 3 * wide :]
+
     rising, falling = arrived[-1]
     grad_normed = own_term + rising.astype(F32) + falling.astype(F32)
     own = mine.astype(F32)

time: 475 us -> 469 us (0.987)
  waiting for transfers between devices: 168 us -> 162 us
    ppermute x3, waiting for transfers between devices: 24 us -> 9.75 us  [chain_scatter(): rising = lax.ppermute(up, axis, [(i, i + 1) for i in range(step + 1)])]
    ppermute x6 -> x3, waiting for transfers between devices: 9.76 us -> 20.4 us  [direct_exchange(): lax.ppermute(give, axis, [(i, (i + far) % size) for i in range(size)])]
    all_to_all x1, waiting for transfers between devices: 19.8 us -> 9.17 us  [body(): lax.all_to_all(late, 'fsdp', 0, 0, tiled=True)]
    all_to_all x1, waiting for transfers between devices: 5.36 us -> 14.8 us  [body(): grad_heads = lax.all_to_all(grad_attended, 'fsdp', 1, 0, tiled=True)]
    unnamed x59 -> x62, local copies, waits for them, and re-layouts: 9.99 us -> 9.24 us
  transfers between devices with their start and end apart: 42 -> 38, of which waited for: 18 -> 16; matrix products, arithmetic and copies ran while one was open for 14% -> 14% of each run, Pallas kernels for 17% -> 17%
where the time goes in v16:
time: 469 us; the launch traced here: 460 us
  waiting for transfers between devices  162 us (35%)
  Pallas kernels  122 us (26%)
  starting transfers between devices  77.1 us (16%)
  other arithmetic  50.5 us (11%)
  local copies, waits for them, and re-layouts  34.2 us (7%)
  between operations  14.8 us (3%)
    ppermute x9, waiting for transfers between devices, chain_gather(): falling = tuple((lax.ppermute(block, axis, down) for block in falling))  81.7 us
    pallas_call x1, Pallas kernels, feed_forward(): pl.pallas_call(functools.partial(ffn_kernel, span, merged), grid=(steps,)...  44 us
    pallas_call x1, Pallas kernels, other_blocks(): pl.pallas_call(functools.partial(other_blocks_kernel, heads, top), grid_s...  24.9 us
    ppermute x9, starting transfers between devices, chain_gather(): rising = tuple((lax.ppermute(block, axis, up) for block in rising))  21.1 us
    ppermute x3, waiting for transfers between devices, direct_exchange(): lax.ppermute(give, axis, [(i, (i + far) % size) for i in range(size)])  20.4 us
    pallas_call x1, Pallas kernels, attend_forward(): pl.pallas_call(functools.partial(forward_kernel, heads, top), grid_spec=p...  19.9 us
    pallas_call x1, Pallas kernels, first_block(): pl.pallas_call(functools.partial(first_block_kernel, heads, top), grid_sp...  17.7 us
    all_to_all x1, waiting for transfers between devices, body(): attended = lax.all_to_all(attended_heads, 'fsdp', 0, 1, tiled=True)  15 us
  transfers between devices with their start and end apart: 38, of which 16 were waited for; matrix products, arithmetic and copies ran while one was open for 14% of the time, Pallas kernels for 17%

profile of v16, /device:TPU:0, one launch (start us, length us, event | category | flops | bytes accessed | tf_op | source)
XLA Modules:
  0.0 460.5 jit_solution(17129423201399413827)
XLA Ops:
  11.2 5.6 %collective-permute-start = (bf16[32,6656]{1,0:T(8,128)(2,1)S(1)}, bf16[32,6656]{1,0:T(8,128)(2,1)S(1)}, u32[]{:S(2)}, u32[]{:S(2)}) collective-permute-start(bf16[32,6656]{1,0:T(8,128)(2,1)S(1)} %constant_dynamic-update-slice_fusion), channel_id=1, source_target_pairs={{0,1},{1,2},{2,3},{4,5},{5,6},{6,7},{8,9},{9,10},{10,11},{12,13},{... | collective-permute-start | bytes 1277960 | tf_op jit(solution)/shard_map/ppermute | solution.py:694
  43.2 14.5 %collective-permute-done.7 = bf16[88,1024]{1,0:T(8,128)(2,1)S(1)} collective-permute-done((bf16[88,1024]{1,0:T(8,128)(2,1)S(1)}, bf16[88,1024]{1,0:T(8,128)(2,1)S(1)}, u32[]{:S(2)}, u32[]{:S(2)}) %collective-permute-start.7) | collective-permute-done | bytes 180256 | tf_op jit(solution)/shard_map/ppermute | solution.py:695
  61.6 11.5 %collective-permute-done.17 = bf16[88,1024]{1,0:T(8,128)(2,1)} collective-permute-done((bf16[88,1024]{1,0:T(8,128)(2,1)S(1)}, bf16[88,1024]{1,0:T(8,128)(2,1)}, u32[]{:S(2)}, u32[]{:S(2)}) %collective-permute-start.17) | collective-permute-done | bytes 180256 | tf_op jit(solution)/shard_map/ppermute | solution.py:695
  78.6 5.6 %collective-permute-start.8 = (bf16[512,1024]{1,0:T(8,128)(2,1)S(1)}, bf16[512,1024]{1,0:T(8,128)(2,1)}, u32[]{:S(2)}, u32[]{:S(2)}) collective-permute-start(bf16[512,1024]{1,0:T(8,128)(2,1)S(1)} %bitcast.98), channel_id=1, source_target_pairs={{0,1},{1,2},{2,3},{4,5},{5,6},{6,7},{8,9},{9,10},{10,11},{12,13},{... | collective-permute-start | bytes 3145736 | tf_op jit(solution)/shard_map/ppermute | solution.py:694
  84.1 16.5 %collective-permute-done.11 = bf16[512,1024]{1,0:T(8,128)(2,1)S(1)} collective-permute-done((bf16[512,1024]{1,0:T(8,128)(2,1)S(1)}, bf16[512,1024]{1,0:T(8,128)(2,1)S(1)}, u32[]{:S(2)}, u32[]{:S(2)}) %collective-permute-start.11) | collective-permute-done | bytes 1048608 | tf_op jit(solution)/shard_map/ppermute | solution.py:695
  106.6 17.1 %collective-permute-done.12 = bf16[512,1024]{1,0:T(8,128)(2,1)} collective-permute-done((bf16[512,1024]{1,0:T(8,128)(2,1)S(1)}, bf16[512,1024]{1,0:T(8,128)(2,1)}, u32[]{:S(2)}, u32[]{:S(2)}) %collective-permute-start.12) | collective-permute-done | bytes 1048608 | tf_op jit(solution)/shard_map/ppermute | solution.py:695
  132.7 5.5 %all-to-all-start.1 = ((bf16[4,256,512]{2,1,0:T(8,128)(2,1)}), bf16[4,256,512]{2,1,0:T(8,128)(2,1)}, u32[]{:S(2)}, u32[]{:S(2)}) async-start(bf16[4,256,512]{2,1,0:T(8,128)(2,1)} %pad_maximum_fusion.5), calls=%async_computation.1 | async-start | bytes 2097152 | tf_op jit(solution)/shard_map/all_to_all | solution.py:784
  141.1 18.4 %collective-permute-done.13 = bf16[512,1024]{1,0:T(8,128)(2,1)} collective-permute-done((bf16[512,1024]{1,0:T(8,128)(2,1)}, bf16[512,1024]{1,0:T(8,128)(2,1)}, u32[]{:S(2)}, u32[]{:S(2)}) %collective-permute-start.13) | collective-permute-done | bytes 1048608 | tf_op jit(solution)/shard_map/ppermute | solution.py:695
  164.3 7.4 %project_qkv.1.q_ref.k_ref.v_ref.qkv_ref = bf16[2048,768]{1,0:T(8,128)(2,1)} custom-call(bf16[2048,1024]{1,0:T(8,128)(2,1)} %pad_maximum_fusion.tok_ref, f32[1,1024]{1,0:T(1,128)S(1)} %reshape.205.gain_ref, bf16[1024,768]{1,0:T(8,128)(2,1)S(1)} %bitcast.89, f32[2048,128]{1,0:T(8,128)S(1)} %get-tuple-element.148.cos_ref, f32[2048,128]{1,0:T(8,128)S(1)} %copy-done.3), custom_call_target="tpu_custom_call" | custom-call | flops 3221225472 | bytes 14680064 | tf_op jit(solution)/shard_map/project_qkv/pallas_call | solution.py:62
  171.7 19.9 %attend_forward.1 = (bf16[2048,256]{1,0:T(8,128)(2,1)}, f32[2048,2]{1,0:T(8,128)S(1)}) custom-call(s32[32]{0:T(128)S(1)} %reshape_squeeze.24.chosen_ref, s32[32]{0:T(128)S(1)} %reshape_squeeze.25.counts_ref, bf16[2048,768]{1,0:T(8,128)(2,1)} %project_qkv.1.q_ref.k_ref.v_ref.qkv_ref, bf16[2048,768]{1,0:T(8,128)(2,1)} %project_qkv.1.q_ref.k_ref.v_ref.qkv_ref, ...), custom_call_target="tpu_custom_call" | custom-call | flops 3221225472 | bytes 4194304 | tf_op jit(solution)/shard_map/attend_forward/pallas_call | solution.py:154
  192.5 4.6 %all-to-all-start.2 = ((bf16[4,512,256]{2,1,0:T(8,128)(2,1)}), bf16[4,512,256]{2,1,0:T(8,128)(2,1)S(1)}, u32[]{:S(2)}, u32[]{:S(2)}) async-start(bf16[4,512,256]{2,1,0:T(8,128)(2,1)} %bitcast.8), calls=%async_computation.2 | async-start | bytes 2097152 | tf_op jit(solution)/shard_map/all_to_all | solution.py:790
  198.1 15.0 %all-to-all-done.2 = bf16[4,512,256]{2,1,0:T(8,128)(2,1)S(1)} async-done(((bf16[4,512,256]{2,1,0:T(8,128)(2,1)}), bf16[4,512,256]{2,1,0:T(8,128)(2,1)S(1)}, u32[]{:S(2)}, u32[]{:S(2)}) %all-to-all-start.2) | async-done | bytes 1048608 | tf_op jit(solution)/shard_map/all_to_all | solution.py:790
  214.2 44.0 %feed_forward.1 = (bf16[512,1024]{1,0:T(8,128)(2,1)}, f32[512,1024]{1,0:T(8,128)}, bf16[512,1024]{1,0:T(8,128)(2,1)}, f32[1,1024]{1,0:T(1,128)}, bf16[8,128,1024...) custom-call(bf16[512,1024]{1,0:T(8,128)(2,1)} %bitcast.96, bf16[512,1024]{1,0:T(8,128)(2,1)} %bitcast.113, ...), custom_call_target="tpu_custom_call" | custom-call | flops 29796335616 | bytes 38797312 | tf_op jit(solution)/shard_map/feed_forward/pallas_call | solution.py:589
  265.1 14.8 %all-to-all-done.3 = bf16[512,4,256]{2,0,1:T(8,128)(2,1)S(1)} async-done(((bf16[512,4,256]{2,0,1:T(8,128)(2,1)}), bf16[512,4,256]{2,0,1:T(8,128)(2,1)S(1)}, u32[]{:S(2)}, u32[]{:S(2)}) %all-to-all-start.3) | async-done | bytes 1048608 | tf_op jit(solution)/shard_map/all_to_all | solution.py:796
  280.9 17.7 %first_block.1 = (bf16[512,1024]{1,0:T(8,128)(2,1)}, bf16[512,768]{1,0:T(8,128)(2,1)}, f32[2048,256]{1,0:T(8,128)}, f32[2048,256]{1,0:T(8,128)}, f32[2048,256]{1,0:T(8,128)}) custom-call(s32[32]{0:T(128)} %copy-done.7, s32[32]{0:T(128)} %copy-done.6, s32[2]{0:T(128)} %pad_add_fusion.plan_ref, bf16[2048,768]{1,0:T(8,128)(2,1)} %project_qkv.1.q_ref.k_ref.v_ref.qkv_ref, ...), custom_call_target="tpu_custom_call" | custom-call | flops 4294967296 | bytes 20971520 | tf_op jit(solution)/shard_map/first_block/pallas_call | solution.py:308
  302.0 24.9 %other_blocks.1 = (bf16[1536,1024]{1,0:T(8,128)(2,1)}, bf16[1536,768]{1,0:T(8,128)(2,1)}) custom-call(s32[32]{0:T(128)} %copy-done.7, s32[32]{0:T(128)} %copy-done.6, s32[1]{0:T(128)} %bitcast.16.plan_ref, bf16[2048,768]{1,0:T(8,128)(2,1)} %project_qkv.1.q_ref.k_ref.v_ref.qkv_ref, bf16[2048,768]{1,0:T(8,128)(2,1)} %project_qkv.1.q_ref.k_ref.v_ref.qkv_ref, ...), custom_call_target="tpu_custom_call" | custom-call | flops 8053063680 | bytes 20971520 | tf_op jit(solution)/shard_map/other_blocks/pallas_call | solution.py:410
  327.9 5.1 %add_convert_fusion.2 = (bf16[512,1024]{1,0:T(8,128)(2,1)}, bf16[512,1024]{1,0:T(8,128)(2,1)}) fusion(bf16[512,1024]{1,0:T(8,128)(2,1)} %collective-permute-done.19, bf16[512,1024]{1,0:T(8,128)(2,1)S(1)} %copy-done.10, bf16[1536,1024]{1,0:T(8,128)(2,1)} %get-tuple-element.85, s32[]{:T(128)S(6)} %min.47, pred[]{:T(512)S(6)} %and.34, ...), kind=kLoop, calls=%fused_computation.17 | loop fusion | flops 5242880 | bytes 7340042 | tf_op jit(solution)/shard_map/convert_element_type | solution.py:725
  341.4 8.5 %projection_grads.1 = (bf16[1024,768]{1,0:T(8,128)(2,1)S(1)}, f32[1024,1]{1,0:T(8,128)S(1)}) custom-call(s32[4]{0:T(128)S(1)} %pad_add_fusion.1.order_ref, bf16[2048,1024]{1,0:T(8,128)(2,1)} %pad_maximum_fusion.tok_ref, f32[1024,1]{1,0:T(8,128)S(1)} %copy-done.5, bf16[1024,768]{1,0:T(8,128)(2,1)S(1)} %bitcast.92, bf16[512,768]{1,0:T(8,128)(2,1)S(1)} %copy-done.9, ...), custom_call_target="tpu_custom_call" | custom-call | flops 3221225472 | bytes 7340032 | tf_op jit(solution)/shard_map/projection_grads/pallas_call | solution.py:652
  357.5 7.9 %collective-permute-start.22 = (bf16[512,1024]{1,0:T(8,128)(2,1)}, bf16[512,1024]{1,0:T(8,128)(2,1)S(1)}, u32[]{:S(2)}, u32[]{:S(2)}) collective-permute-start(bf16[512,1024]{1,0:T(8,128)(2,1)} %get-tuple-element.100), channel_id=1, source_target_pairs={{0,1},{1,2},{2,3},{4,5},{5,6},{6,7},{8,9},{9,10},{10,11},{12,13},{... | collective-permute-start | bytes 3145736 | tf_op jit(solution)/shard_map/ppermute | solution.py:727
  371.5 6.4 %collective-permute-done.22 = bf16[512,1024]{1,0:T(8,128)(2,1)S(1)} collective-permute-done((bf16[512,1024]{1,0:T(8,128)(2,1)}, bf16[512,1024]{1,0:T(8,128)(2,1)S(1)}, u32[]{:S(2)}, u32[]{:S(2)}) %collective-permute-start.22) | collective-permute-done | bytes 1048608 | tf_op jit(solution)/shard_map/ppermute | solution.py:727
  377.9 4.5 collective-permute-done.23
  401.0 10.4 %collective-permute-done.25 = bf16[136,1792]{1,0:T(8,128)(2,1)S(1)} collective-permute-done((bf16[136,1792]{1,0:T(8,128)(2,1)}, bf16[136,1792]{1,0:T(8,128)(2,1)S(1)}, u32[]{:S(2)}, u32[]{:S(2)}) %collective-permute-start.25) | collective-permute-done | bytes 487456 | tf_op jit(solution)/shard_map/ppermute | solution.py:739
  411.3 10.1 %collective-permute-done.27 = bf16[136,1792]{1,0:T(8,128)(2,1)} collective-permute-done((bf16[136,1792]{1,0:T(8,128)(2,1)S(1)}, bf16[136,1792]{1,0:T(8,128)(2,1)}, u32[]{:S(2)}, u32[]{:S(2)}) %collective-permute-start.27) | collective-permute-done | bytes 487456 | tf_op jit(solution)/shard_map/ppermute | solution.py:739
  436.4 9.2 %all-to-all-done.4 = bf16[4,40,1792]{2,1,0:T(8,128)(2,1)} async-done(((bf16[4,40,1792]{2,1,0:T(8,128)(2,1)}), bf16[4,40,1792]{2,1,0:T(8,128)(2,1)}, u32[]{:S(2)}, u32[]{:S(2)}) %all-to-all-start.4) | async-done | bytes 573472 | tf_op jit(solution)/shard_map/all_to_all | solution.py:882
  (208 shorter events, 141.0 us)
Async XLA Ops:
  9.9 28.4 %collective-permute-start.2 = (bf16[32,6656]{1,0:T(8,128)(2,1)S(1)}, bf16[32,6656]{1,0:T(8,128)(2,1)S(1)}, u32[]{:S(2)}, u32[]{:S(2)}) collective-permute-start(bf16[32,6656]{1,0:T(8,128)(2,1)S(1)} %constant_dynamic-update-slice_fusion), channel_id=1, source_target_pairs={{1,0},{2,1},{3,2},{5,4},{6,5},{7,6},{9,8},{10,9},{11,10},{13,12},{... | collective-permute-start | bytes 1277960 | tf_op jit(solution)/shard_map/ppermute | solution.py:695
  11.2 27.1 %collective-permute-start = (bf16[32,6656]{1,0:T(8,128)(2,1)S(1)}, bf16[32,6656]{1,0:T(8,128)(2,1)S(1)}, u32[]{:S(2)}, u32[]{:S(2)}) collective-permute-start(bf16[32,6656]{1,0:T(8,128)(2,1)S(1)} %constant_dynamic-update-slice_fusion), channel_id=1, source_target_pairs={{0,1},{1,2},{2,3},{4,5},{5,6},{6,7},{8,9},{9,10},{10,11},{12,13},{... | collective-permute-start | bytes 1277960 | tf_op jit(solution)/shard_map/ppermute | solution.py:694
  27.0 111.4 %all-gather.4.cloned.1.call-start = ((), (), s32[]{:S(2)}) async-start(), calls=%async_computation.7 | async-start | bytes 2211840 | tf_op jit(solution)/shard_map/all_gather | solution.py:774
  39.1 175.0 %all-gather.8.cloned.1.call-start = ((), (), s32[]{:S(2)}) async-start(), calls=%async_computation.9 | async-start | bytes 6488064 | tf_op jit(solution)/shard_map/all_gather | solution.py:785
  39.2 18.4 %collective-permute-start.4 = (bf16[32,6656]{1,0:T(8,128)(2,1)S(1)}, bf16[32,6656]{1,0:T(8,128)(2,1)S(1)}, u32[]{:S(2)}, u32[]{:S(2)}) collective-permute-start(bf16[32,6656]{1,0:T(8,128)(2,1)S(1)} %collective-permute-done), channel_id=1, source_target_pairs={{1,2},{2,3},{5,6},{6,7},{9,10},{10,11},{13,14},{14,15},{17,18},{18... | collective-permute-start | bytes 1277960 | tf_op jit(solution)/shard_map/ppermute | solution.py:694
  75.4 138.8 %all-gather.6.cloned.1.call-start = ((), (), s32[]{:S(2)}) async-start(), calls=%async_computation.8 | async-start | bytes 15335424 | tf_op jit(solution)/shard_map/all_gather | solution.py:778
  77.3 23.3 %collective-permute-start.11 = (bf16[512,1024]{1,0:T(8,128)(2,1)S(1)}, bf16[512,1024]{1,0:T(8,128)(2,1)S(1)}, u32[]{:S(2)}, u32[]{:S(2)}) collective-permute-start(bf16[512,1024]{1,0:T(8,128)(2,1)S(1)} %bitcast.97), channel_id=1, source_target_pairs={{1,0},{2,1},{3,2},{5,4},{6,5},{7,6},{9,8},{10,9},{11,10},{13,12},{... | collective-permute-start | bytes 3145736 | tf_op jit(solution)/shard_map/ppermute | solution.py:695
  78.6 23.3 %collective-permute-start.8 = (bf16[512,1024]{1,0:T(8,128)(2,1)S(1)}, bf16[512,1024]{1,0:T(8,128)(2,1)}, u32[]{:S(2)}, u32[]{:S(2)}) collective-permute-start(bf16[512,1024]{1,0:T(8,128)(2,1)S(1)} %bitcast.98), channel_id=1, source_target_pairs={{0,1},{1,2},{2,3},{4,5},{5,6},{6,7},{8,9},{9,10},{10,11},{12,13},{... | collective-permute-start | bytes 3145736 | tf_op jit(solution)/shard_map/ppermute | solution.py:694
  100.6 23.1 %collective-permute-start.12 = (bf16[512,1024]{1,0:T(8,128)(2,1)S(1)}, bf16[512,1024]{1,0:T(8,128)(2,1)}, u32[]{:S(2)}, u32[]{:S(2)}) collective-permute-start(bf16[512,1024]{1,0:T(8,128)(2,1)S(1)} %collective-permute-done.11), channel_id=1, source_target_pairs={{1,0},{2,1},{5,4},{6,5},{9,8},{10,9},{13,12},{14,13},{17,16},{18,1... | collective-permute-start | bytes 3145736 | tf_op jit(solution)/shard_map/ppermute | solution.py:695
  101.9 23.1 %collective-permute-start.9 = (bf16[512,1024]{1,0:T(8,128)(2,1)}, bf16[512,1024]{1,0:T(8,128)(2,1)}, u32[]{:S(2)}, u32[]{:S(2)}) collective-permute-start(bf16[512,1024]{1,0:T(8,128)(2,1)} %collective-permute-done.8), channel_id=1, source_target_pairs={{1,2},{2,3},{5,6},{6,7},{9,10},{10,11},{13,14},{14,15},{17,18},{18... | collective-permute-start | bytes 3145736 | tf_op jit(solution)/shard_map/ppermute | solution.py:694
  123.7 35.8 %collective-permute-start.13 = (bf16[512,1024]{1,0:T(8,128)(2,1)}, bf16[512,1024]{1,0:T(8,128)(2,1)}, u32[]{:S(2)}, u32[]{:S(2)}) collective-permute-start(bf16[512,1024]{1,0:T(8,128)(2,1)} %collective-permute-done.12), channel_id=1, source_target_pairs={{1,0},{5,4},{9,8},{13,12},{17,16},{21,20},{25,24},{29,28}} | collective-permute-start | bytes 3145736 | tf_op jit(solution)/shard_map/ppermute | solution.py:695
  125.0 34.5 %collective-permute-start.10 = (bf16[512,1024]{1,0:T(8,128)(2,1)}, bf16[512,1024]{1,0:T(8,128)(2,1)}, u32[]{:S(2)}, u32[]{:S(2)}) collective-permute-start(bf16[512,1024]{1,0:T(8,128)(2,1)} %collective-permute-done.9), channel_id=1, source_target_pairs={{2,3},{6,7},{10,11},{14,15},{18,19},{22,23},{26,27},{30,31}} | collective-permute-start | bytes 3145736 | tf_op jit(solution)/shard_map/ppermute | solution.py:694
  132.7 38.9 %all-to-all-start.1 = ((bf16[4,256,512]{2,1,0:T(8,128)(2,1)}), bf16[4,256,512]{2,1,0:T(8,128)(2,1)}, u32[]{:S(2)}, u32[]{:S(2)}) async-start(bf16[4,256,512]{2,1,0:T(8,128)(2,1)} %pad_maximum_fusion.5), calls=%async_computation.1 | async-start | bytes 2097152 | tf_op jit(solution)/shard_map/all_to_all | solution.py:784
  192.5 20.5 %all-to-all-start.2 = ((bf16[4,512,256]{2,1,0:T(8,128)(2,1)}), bf16[4,512,256]{2,1,0:T(8,128)(2,1)S(1)}, u32[]{:S(2)}, u32[]{:S(2)}) async-start(bf16[4,512,256]{2,1,0:T(8,128)(2,1)} %bitcast.8), calls=%async_computation.2 | async-start | bytes 2097152 | tf_op jit(solution)/shard_map/all_to_all | solution.py:790
  197.2 185.2 %reduce-scatter.3.cloned.1.call-start = ((), (), s32[]{:S(2)}) async-start(), calls=%async_computation.10 | async-start | bytes 19464192 | tf_op jit(solution)/shard_map/reduce_scatter | solution.py:797
  260.4 19.5 %all-to-all-start.3 = ((bf16[512,4,256]{2,0,1:T(8,128)(2,1)}), bf16[512,4,256]{2,0,1:T(8,128)(2,1)S(1)}, u32[]{:S(2)}, u32[]{:S(2)}) async-start(bf16[512,4,256]{2,0,1:T(8,128)(2,1)} %bitcast.88), calls=%async_computation.3 | async-start | bytes 2097152 | tf_op jit(solution)/shard_map/all_to_all | solution.py:796
  264.0 186.0 %reduce-scatter.5.cloned.1.call-start = ((), (), s32[]{:S(2)}) async-start(), calls=%async_computation.11 | async-start | bytes 2703360 | tf_op jit(solution)/shard_map/reduce_scatter | solution.py:890
  298.6 28.3 %collective-permute-start.18 = (bf16[512,1024]{1,0:T(8,128)(2,1)}, bf16[512,1024]{1,0:T(8,128)(2,1)S(1)}, u32[]{:S(2)}, u32[]{:S(2)}) collective-permute-start(bf16[512,1024]{1,0:T(8,128)(2,1)} %get-tuple-element.87), channel_id=1, source_target_pairs={{0,1},{4,5},{8,9},{12,13},{16,17},{20,21},{24,25},{28,29}} | collective-permute-start | bytes 3145736 | tf_op jit(solution)/shard_map/ppermute | solution.py:727
  300.2 26.7 %collective-permute-start.19 = (bf16[512,1024]{1,0:T(8,128)(2,1)}, bf16[512,1024]{1,0:T(8,128)(2,1)}, u32[]{:S(2)}, u32[]{:S(2)}) collective-permute-start(bf16[512,1024]{1,0:T(8,128)(2,1)} %get-tuple-element.87), channel_id=1, source_target_pairs={{3,2},{7,6},{11,10},{15,14},{19,18},{23,22},{27,26},{31,30}} | collective-permute-start | bytes 3145736 | tf_op jit(solution)/shard_map/ppermute | solution.py:728
  333.0 20.3 %collective-permute-start.20 = (bf16[512,1024]{1,0:T(8,128)(2,1)}, bf16[512,1024]{1,0:T(8,128)(2,1)}, u32[]{:S(2)}, u32[]{:S(2)}) collective-permute-start(bf16[512,1024]{1,0:T(8,128)(2,1)} %get-tuple-element.90), channel_id=1, source_target_pairs={{0,1},{1,2},{4,5},{5,6},{8,9},{9,10},{12,13},{13,14},{16,17},{17,1... | collective-permute-start | bytes 3145736 | tf_op jit(solution)/shard_map/ppermute | solution.py:727
  357.5 20.5 %collective-permute-start.22 = (bf16[512,1024]{1,0:T(8,128)(2,1)}, bf16[512,1024]{1,0:T(8,128)(2,1)S(1)}, u32[]{:S(2)}, u32[]{:S(2)}) collective-permute-start(bf16[512,1024]{1,0:T(8,128)(2,1)} %get-tuple-element.100), channel_id=1, source_target_pairs={{0,1},{1,2},{2,3},{4,5},{5,6},{6,7},{8,9},{9,10},{10,11},{12,13},{... | collective-permute-start | bytes 3145736 | tf_op jit(solution)/shard_map/ppermute | solution.py:727
  397.9 23.5 %collective-permute-start.27 = (bf16[136,1792]{1,0:T(8,128)(2,1)S(1)}, bf16[136,1792]{1,0:T(8,128)(2,1)}, u32[]{:S(2)}, u32[]{:S(2)}) collective-permute-start(bf16[136,1792]{1,0:T(8,128)(2,1)S(1)} %get-tuple-element.126), channel_id=1, source_target_pairs={{0,24},{8,0},{16,8},{24,16},{1,25},{9,1},{17,9},{25,17},{2,26},{10... | collective-permute-start | bytes 1462280 | tf_op jit(solution)/shard_map/ppermute | solution.py:739
  399.1 22.3 %collective-permute-start.26 = (bf16[136,1792]{1,0:T(8,128)(2,1)S(1)}, bf16[136,1792]{1,0:T(8,128)(2,1)}, u32[]{:S(2)}, u32[]{:S(2)}) collective-permute-start(bf16[136,1792]{1,0:T(8,128)(2,1)S(1)} %get-tuple-element.127), channel_id=1, source_target_pairs={{0,16},{8,24},{16,0},{24,8},{1,17},{9,25},{17,1},{25,9},{2,18},{10... | collective-permute-start | bytes 1462280 | tf_op jit(solution)/shard_map/ppermute | solution.py:739
  425.7 19.9 %all-to-all-start.4 = ((bf16[4,40,1792]{2,1,0:T(8,128)(2,1)}), bf16[4,40,1792]{2,1,0:T(8,128)(2,1)}, u32[]{:S(2)}, u32[]{:S(2)}) async-start(bf16[4,40,1792]{2,1,0:T(8,128)(2,1)} %fusion.14), calls=%async_computation.5 | async-start | bytes 1146880 | tf_op jit(solution)/shard_map/all_to_all | solution.py:882
  (43 other events, 516.1 us)
Sparse Core Ops, SparseCore 0:
  39.3 27.3 all-gather.3
  75.5 41.5 all-gather.7
  119.0 76.5 all-gather.5
  258.3 117.6 reduce-scatter.2
  388.6 43.3 reduce-scatter.4

commit v17 on v16

--- a/solution.py
+++ b/solution.py
@@ -799,12 +799,14 @@
     core = lax.axis_index("core")
 
     def over_cores(array):
-        array = array.reshape((span // 2, 2) + array.shape[1:])
+        array = array.reshape((-1, 2) + array.shape[1:])
         taken = lax.ppermute(lax.dynamic_index_in_dim(array, 1 - core, 1, keepdims=False), "core", [(0, 1), (1, 0)])
         return (lax.dynamic_index_in_dim(array, core, 1, keepdims=False).astype(F32) + taken.astype(F32)).astype(BF16)
 
     def over_chips(array):
         return sum(piece.astype(F32) for piece in direct_exchange(array, "chip")).astype(BF16)
+
+    out_grads = over_chips(out_grads.reshape((span // 2, 2) + out_grads.shape[1:]))
 
     place = lax.axis_index("fsdp").astype(jnp.int32)
     count = length // min(2 * QBLK, length)
@@ -843,7 +845,7 @@
         )
         return kept
 
-    own_term, arrived = chain_scatter(term, "fsdp", [lambda sent: None, make_projection_grads])
+    own_term, arrived = chain_scatter(term, "fsdp", [lambda sent: out_grads, make_projection_grads])
     grad_w_qkv, gain_one_grad = kept
     grads = after(grads, arrived[-1])
 
@@ -862,9 +864,8 @@
     gains = jnp.stack([gain_one_grad.reshape(span, -1), gain_two_grad.reshape(span, -1)], 1)
     gains = jnp.pad(gains.astype(BF16), ((0, 0), (0, extra - 2), (0, 3 * wide - gains.shape[2])))
     late = jnp.concatenate([grad_w_qkv.reshape(span, -1, 3 * wide), gains], 1)
-    late = jnp.concatenate([late, jnp.pad(out_grads, ((0, 0), (0, extra), (0, 0)))], 2)
     late = over_chips(over_cores(after(late, pieces)))
-    late, out_grads = late[:, : 3 * wide], late[:-extra, 3 * wide :]
+    out_grads = over_cores(after(out_grads, pieces))[0]
 
     rising, falling = arrived[-1]
     grad_normed = own_term + rising.astype(F32) + falling.astype(F32)

time: 469 us -> 468 us (level)
  starting transfers between devices: 77.1 us -> 82.4 us
  other arithmetic: 50.5 us -> 45.7 us
    all_to_all x1, waiting for transfers between devices: 9.17 us -> 22.2 us  [body(): lax.all_to_all(late, 'fsdp', 0, 0, tiled=True)]
    ppermute x3 -> x6, waiting for transfers between devices: 20.4 us -> 8.18 us  [direct_exchange(): lax.ppermute(give, axis, [(i, (i + far) % size) for i in range(size)])]
    all_to_all x1, waiting for transfers between devices: 14.8 us -> 9.06 us  [body(): grad_heads = lax.all_to_all(grad_attended, 'fsdp', 1, 0, tiled=True)]
    ppermute x3, waiting for transfers between devices: 9.75 us -> 14.8 us  [chain_scatter(): rising = lax.ppermute(up, axis, [(i, i + 1) for i in range(step + 1)])]
    unnamed x62 -> x66, local copies, waits for them, and re-layouts: 9.24 us -> 10.3 us
  transfers between devices with their start and end apart: 38 -> 42, of which waited for: 16 -> 16; matrix products, arithmetic and copies ran while one was open for 14% -> 13% of each run, Pallas kernels for 17% -> 17%
where the time goes in v17:
time: 468 us; the launch traced here: 459 us
  waiting for transfers between devices  159 us (34%)
  Pallas kernels  122 us (26%)
  starting transfers between devices  82.4 us (18%)
  other arithmetic  45.7 us (10%)
  local copies, waits for them, and re-layouts  35 us (7%)
  between operations  14.8 us (3%)
    ppermute x9, waiting for transfers between devices, chain_gather(): falling = tuple((lax.ppermute(block, axis, down) for block in falling))  81.8 us
    pallas_call x1, Pallas kernels, feed_forward(): pl.pallas_call(functools.partial(ffn_kernel, span, merged), grid=(steps,)...  44 us
    pallas_call x1, Pallas kernels, other_blocks(): pl.pallas_call(functools.partial(other_blocks_kernel, heads, top), grid_s...  24.9 us
    all_to_all x1, waiting for transfers between devices, body(): lax.all_to_all(late, 'fsdp', 0, 0, tiled=True)  22.2 us
    ppermute x9, starting transfers between devices, chain_gather(): rising = tuple((lax.ppermute(block, axis, up) for block in rising))  21.1 us
    pallas_call x1, Pallas kernels, attend_forward(): pl.pallas_call(functools.partial(forward_kernel, heads, top), grid_spec=p...  19.9 us
    pallas_call x1, Pallas kernels, first_block(): pl.pallas_call(functools.partial(first_block_kernel, heads, top), grid_sp...  17.7 us
    all_to_all x1, waiting for transfers between devices, body(): attended = lax.all_to_all(attended_heads, 'fsdp', 0, 1, tiled=True)  15 us
  transfers between devices with their start and end apart: 42, of which 16 were waited for; matrix products, arithmetic and copies ran while one was open for 13% of the time, Pallas kernels for 17%

profile of v17, /device:TPU:0, one launch (start us, length us, event | category | flops | bytes accessed | tf_op | source)
XLA Modules:
  0.0 459.1 jit_solution(5438558982444945649)
XLA Ops:
  11.2 5.6 %collective-permute-start = (bf16[32,6656]{1,0:T(8,128)(2,1)S(1)}, bf16[32,6656]{1,0:T(8,128)(2,1)S(1)}, u32[]{:S(2)}, u32[]{:S(2)}) collective-permute-start(bf16[32,6656]{1,0:T(8,128)(2,1)S(1)} %constant_dynamic-update-slice_fusion), channel_id=1, source_target_pairs={{0,1},{1,2},{2,3},{4,5},{5,6},{6,7},{8,9},{9,10},{10,11},{12,13},{... | collective-permute-start | bytes 1277960 | tf_op jit(solution)/shard_map/ppermute | solution.py:694
  22.7 4.3 all-to-all-start
  43.2 14.5 %collective-permute-done.7 = bf16[88,1024]{1,0:T(8,128)(2,1)S(1)} collective-permute-done((bf16[88,1024]{1,0:T(8,128)(2,1)S(1)}, bf16[88,1024]{1,0:T(8,128)(2,1)S(1)}, u32[]{:S(2)}, u32[]{:S(2)}) %collective-permute-start.7) | collective-permute-done | bytes 180256 | tf_op jit(solution)/shard_map/ppermute | solution.py:695
  61.7 11.5 %collective-permute-done.17 = bf16[88,1024]{1,0:T(8,128)(2,1)} collective-permute-done((bf16[88,1024]{1,0:T(8,128)(2,1)S(1)}, bf16[88,1024]{1,0:T(8,128)(2,1)}, u32[]{:S(2)}, u32[]{:S(2)}) %collective-permute-start.17) | collective-permute-done | bytes 180256 | tf_op jit(solution)/shard_map/ppermute | solution.py:695
  78.5 5.6 %collective-permute-start.8 = (bf16[512,1024]{1,0:T(8,128)(2,1)S(1)}, bf16[512,1024]{1,0:T(8,128)(2,1)}, u32[]{:S(2)}, u32[]{:S(2)}) collective-permute-start(bf16[512,1024]{1,0:T(8,128)(2,1)S(1)} %bitcast.106), channel_id=1, source_target_pairs={{0,1},{1,2},{2,3},{4,5},{5,6},{6,7},{8,9},{9,10},{10,11},{12,13},{... | collective-permute-start | bytes 3145736 | tf_op jit(solution)/shard_map/ppermute | solution.py:694
  84.1 16.5 %collective-permute-done.11 = bf16[512,1024]{1,0:T(8,128)(2,1)S(1)} collective-permute-done((bf16[512,1024]{1,0:T(8,128)(2,1)S(1)}, bf16[512,1024]{1,0:T(8,128)(2,1)S(1)}, u32[]{:S(2)}, u32[]{:S(2)}) %collective-permute-start.11) | collective-permute-done | bytes 1048608 | tf_op jit(solution)/shard_map/ppermute | solution.py:695
  106.6 17.1 %collective-permute-done.12 = bf16[512,1024]{1,0:T(8,128)(2,1)} collective-permute-done((bf16[512,1024]{1,0:T(8,128)(2,1)S(1)}, bf16[512,1024]{1,0:T(8,128)(2,1)}, u32[]{:S(2)}, u32[]{:S(2)}) %collective-permute-start.12) | collective-permute-done | bytes 1048608 | tf_op jit(solution)/shard_map/ppermute | solution.py:695
  132.7 5.5 %all-to-all-start.1 = ((bf16[4,256,512]{2,1,0:T(8,128)(2,1)}), bf16[4,256,512]{2,1,0:T(8,128)(2,1)}, u32[]{:S(2)}, u32[]{:S(2)}) async-start(bf16[4,256,512]{2,1,0:T(8,128)(2,1)} %pad_maximum_fusion.5), calls=%async_computation.1 | async-start | bytes 2097152 | tf_op jit(solution)/shard_map/all_to_all | solution.py:784
  141.1 18.4 %collective-permute-done.13 = bf16[512,1024]{1,0:T(8,128)(2,1)} collective-permute-done((bf16[512,1024]{1,0:T(8,128)(2,1)}, bf16[512,1024]{1,0:T(8,128)(2,1)}, u32[]{:S(2)}, u32[]{:S(2)}) %collective-permute-start.13) | collective-permute-done | bytes 1048608 | tf_op jit(solution)/shard_map/ppermute | solution.py:695
  164.2 7.4 %project_qkv.1.q_ref.k_ref.v_ref.qkv_ref = bf16[2048,768]{1,0:T(8,128)(2,1)} custom-call(bf16[2048,1024]{1,0:T(8,128)(2,1)} %pad_maximum_fusion.tok_ref, f32[1,1024]{1,0:T(1,128)S(1)} %reshape.214.gain_ref, bf16[1024,768]{1,0:T(8,128)(2,1)S(1)} %bitcast.99, f32[2048,128]{1,0:T(8,128)S(1)} %get-tuple-element.153.cos_ref, f32[2048,128]{1,0:T(8,128)S(1)} %copy-done.3), custom_call_target="tpu_custom_call" | custom-call | flops 3221225472 | bytes 14680064 | tf_op jit(solution)/shard_map/project_qkv/pallas_call | solution.py:62
  171.6 19.9 %attend_forward.1 = (bf16[2048,256]{1,0:T(8,128)(2,1)}, f32[2048,2]{1,0:T(8,128)S(1)}) custom-call(s32[32]{0:T(128)S(1)} %reshape_squeeze.27.chosen_ref, s32[32]{0:T(128)S(1)} %reshape_squeeze.28.counts_ref, bf16[2048,768]{1,0:T(8,128)(2,1)} %project_qkv.1.q_ref.k_ref.v_ref.qkv_ref, bf16[2048,768]{1,0:T(8,128)(2,1)} %project_qkv.1.q_ref.k_ref.v_ref.qkv_ref, ...), custom_call_target="tpu_custom_call" | custom-call | flops 3221225472 | bytes 4194304 | tf_op jit(solution)/shard_map/attend_forward/pallas_call | solution.py:154
  192.5 4.6 %all-to-all-start.2 = ((bf16[4,512,256]{2,1,0:T(8,128)(2,1)}), bf16[4,512,256]{2,1,0:T(8,128)(2,1)S(1)}, u32[]{:S(2)}, u32[]{:S(2)}) async-start(bf16[4,512,256]{2,1,0:T(8,128)(2,1)} %bitcast.8), calls=%async_computation.2 | async-start | bytes 2097152 | tf_op jit(solution)/shard_map/all_to_all | solution.py:790
  198.0 15.0 %all-to-all-done.2 = bf16[4,512,256]{2,1,0:T(8,128)(2,1)S(1)} async-done(((bf16[4,512,256]{2,1,0:T(8,128)(2,1)}), bf16[4,512,256]{2,1,0:T(8,128)(2,1)S(1)}, u32[]{:S(2)}, u32[]{:S(2)}) %all-to-all-start.2) | async-done | bytes 1048608 | tf_op jit(solution)/shard_map/all_to_all | solution.py:790
  214.1 44.0 %feed_forward.1 = (bf16[512,1024]{1,0:T(8,128)(2,1)}, f32[512,1024]{1,0:T(8,128)}, bf16[512,1024]{1,0:T(8,128)(2,1)}, f32[1,1024]{1,0:T(1,128)}, bf16[8,128,1024...) custom-call(bf16[512,1024]{1,0:T(8,128)(2,1)} %bitcast.104, bf16[512,1024]{1,0:T(8,128)(2,1)} %bitcast.125, ...), custom_call_target="tpu_custom_call" | custom-call | flops 29796335616 | bytes 38797312 | tf_op jit(solution)/shard_map/feed_forward/pallas_call | solution.py:589
  270.8 9.1 %all-to-all-done.3 = bf16[512,4,256]{2,0,1:T(8,128)(2,1)S(1)} async-done(((bf16[512,4,256]{2,0,1:T(8,128)(2,1)}), bf16[512,4,256]{2,0,1:T(8,128)(2,1)S(1)}, u32[]{:S(2)}, u32[]{:S(2)}) %all-to-all-start.3) | async-done | bytes 1048608 | tf_op jit(solution)/shard_map/all_to_all | solution.py:796
  280.9 17.7 %first_block.1 = (bf16[512,1024]{1,0:T(8,128)(2,1)}, bf16[512,768]{1,0:T(8,128)(2,1)}, f32[2048,256]{1,0:T(8,128)}, f32[2048,256]{1,0:T(8,128)}, f32[2048,256]{1,0:T(8,128)}) custom-call(s32[32]{0:T(128)} %copy-done.8, s32[32]{0:T(128)} %copy-done.7, s32[2]{0:T(128)} %pad_add_fusion.plan_ref, bf16[2048,768]{1,0:T(8,128)(2,1)} %project_qkv.1.q_ref.k_ref.v_ref.qkv_ref, ...), custom_call_target="tpu_custom_call" | custom-call | flops 4294967296 | bytes 20971520 | tf_op jit(solution)/shard_map/first_block/pallas_call | solution.py:308
  304.6 24.9 %other_blocks.1 = (bf16[1536,1024]{1,0:T(8,128)(2,1)}, bf16[1536,768]{1,0:T(8,128)(2,1)}) custom-call(s32[32]{0:T(128)} %copy-done.8, s32[32]{0:T(128)} %copy-done.7, s32[1]{0:T(128)} %bitcast.16.plan_ref, bf16[2048,768]{1,0:T(8,128)(2,1)} %project_qkv.1.q_ref.k_ref.v_ref.qkv_ref, bf16[2048,768]{1,0:T(8,128)(2,1)} %project_qkv.1.q_ref.k_ref.v_ref.qkv_ref, ...), custom_call_target="tpu_custom_call" | custom-call | flops 8053063680 | bytes 20971520 | tf_op jit(solution)/shard_map/other_blocks/pallas_call | solution.py:410
  330.5 5.0 %add_convert_fusion.2 = (bf16[512,1024]{1,0:T(8,128)(2,1)}, bf16[512,1024]{1,0:T(8,128)(2,1)}) fusion(bf16[512,1024]{1,0:T(8,128)(2,1)} %collective-permute-done.19, bf16[512,1024]{1,0:T(8,128)(2,1)S(1)} %copy-done.11, bf16[1536,1024]{1,0:T(8,128)(2,1)} %get-tuple-element.86, s32[]{:T(128)S(6)} %min.47, pred[]{:T(512)S(6)} %and.37, ...), kind=kLoop, calls=%fused_computation.14 | loop fusion | flops 5242880 | bytes 7340042 | tf_op jit(solution)/shard_map/convert_element_type | solution.py:725
  344.0 8.6 %projection_grads.1 = (bf16[1024,768]{1,0:T(8,128)(2,1)S(1)}, f32[1024,1]{1,0:T(8,128)S(1)}) custom-call(s32[4]{0:T(128)S(1)} %pad_add_fusion.1.order_ref, bf16[2048,1024]{1,0:T(8,128)(2,1)} %pad_maximum_fusion.tok_ref, f32[1024,1]{1,0:T(8,128)S(1)} %copy-done.6, bf16[1024,768]{1,0:T(8,128)(2,1)S(1)} %bitcast.102, bf16[512,768]{1,0:T(8,128)(2,1)S(1)} %copy-done.10, ...), custom_call_target="tpu_custom_call" | custom-call | flops 3221225472 | bytes 7340032 | tf_op jit(solution)/shard_map/projection_grads/pallas_call | solution.py:652
  360.6 8.4 %collective-permute-start.25 = (bf16[512,1024]{1,0:T(8,128)(2,1)}, bf16[512,1024]{1,0:T(8,128)(2,1)S(1)}, u32[]{:S(2)}, u32[]{:S(2)}) collective-permute-start(bf16[512,1024]{1,0:T(8,128)(2,1)} %get-tuple-element.102), channel_id=1, source_target_pairs={{0,1},{1,2},{2,3},{4,5},{5,6},{6,7},{8,9},{9,10},{10,11},{12,13},{... | collective-permute-start | bytes 3145736 | tf_op jit(solution)/shard_map/ppermute | solution.py:727
  370.6 11.0 %collective-permute-done.25 = bf16[512,1024]{1,0:T(8,128)(2,1)S(1)} collective-permute-done((bf16[512,1024]{1,0:T(8,128)(2,1)}, bf16[512,1024]{1,0:T(8,128)(2,1)S(1)}, u32[]{:S(2)}, u32[]{:S(2)}) %collective-permute-start.25) | collective-permute-done | bytes 1048608 | tf_op jit(solution)/shard_map/ppermute | solution.py:727
  381.6 4.5 collective-permute-done.26
  400.3 4.5 collective-permute-done.28
  421.9 22.2 %all-to-all-done.4 = bf16[4,40,1792]{2,1,0:T(8,128)(2,1)} async-done(((bf16[4,40,1792]{2,1,0:T(8,128)(2,1)}), bf16[4,40,1792]{2,1,0:T(8,128)(2,1)}, u32[]{:S(2)}, u32[]{:S(2)}) %all-to-all-start.4) | async-done | bytes 573472 | tf_op jit(solution)/shard_map/all_to_all | solution.py:883
  (223 shorter events, 138.5 us)
Async XLA Ops:
  9.9 28.4 %collective-permute-start.2 = (bf16[32,6656]{1,0:T(8,128)(2,1)S(1)}, bf16[32,6656]{1,0:T(8,128)(2,1)S(1)}, u32[]{:S(2)}, u32[]{:S(2)}) collective-permute-start(bf16[32,6656]{1,0:T(8,128)(2,1)S(1)} %constant_dynamic-update-slice_fusion), channel_id=1, source_target_pairs={{1,0},{2,1},{3,2},{5,4},{6,5},{7,6},{9,8},{10,9},{11,10},{13,12},{... | collective-permute-start | bytes 1277960 | tf_op jit(solution)/shard_map/ppermute | solution.py:695
  11.2 27.1 %collective-permute-start = (bf16[32,6656]{1,0:T(8,128)(2,1)S(1)}, bf16[32,6656]{1,0:T(8,128)(2,1)S(1)}, u32[]{:S(2)}, u32[]{:S(2)}) collective-permute-start(bf16[32,6656]{1,0:T(8,128)(2,1)S(1)} %constant_dynamic-update-slice_fusion), channel_id=1, source_target_pairs={{0,1},{1,2},{2,3},{4,5},{5,6},{6,7},{8,9},{9,10},{10,11},{12,13},{... | collective-permute-start | bytes 1277960 | tf_op jit(solution)/shard_map/ppermute | solution.py:694
  27.0 111.4 %all-gather.4.cloned.1.call-start = ((), (), s32[]{:S(2)}) async-start(), calls=%async_computation.7 | async-start | bytes 2211840 | tf_op jit(solution)/shard_map/all_gather | solution.py:774
  39.1 175.0 %all-gather.8.cloned.1.call-start = ((), (), s32[]{:S(2)}) async-start(), calls=%async_computation.9 | async-start | bytes 6488064 | tf_op jit(solution)/shard_map/all_gather | solution.py:785
  75.4 138.8 %all-gather.6.cloned.1.call-start = ((), (), s32[]{:S(2)}) async-start(), calls=%async_computation.8 | async-start | bytes 15335424 | tf_op jit(solution)/shard_map/all_gather | solution.py:778
  77.3 23.3 %collective-permute-start.11 = (bf16[512,1024]{1,0:T(8,128)(2,1)S(1)}, bf16[512,1024]{1,0:T(8,128)(2,1)S(1)}, u32[]{:S(2)}, u32[]{:S(2)}) collective-permute-start(bf16[512,1024]{1,0:T(8,128)(2,1)S(1)} %bitcast.105), channel_id=1, source_target_pairs={{1,0},{2,1},{3,2},{5,4},{6,5},{7,6},{9,8},{10,9},{11,10},{13,12},{... | collective-permute-start | bytes 3145736 | tf_op jit(solution)/shard_map/ppermute | solution.py:695
  78.5 23.3 %collective-permute-start.8 = (bf16[512,1024]{1,0:T(8,128)(2,1)S(1)}, bf16[512,1024]{1,0:T(8,128)(2,1)}, u32[]{:S(2)}, u32[]{:S(2)}) collective-permute-start(bf16[512,1024]{1,0:T(8,128)(2,1)S(1)} %bitcast.106), channel_id=1, source_target_pairs={{0,1},{1,2},{2,3},{4,5},{5,6},{6,7},{8,9},{9,10},{10,11},{12,13},{... | collective-permute-start | bytes 3145736 | tf_op jit(solution)/shard_map/ppermute | solution.py:694
  100.6 23.1 %collective-permute-start.12 = (bf16[512,1024]{1,0:T(8,128)(2,1)S(1)}, bf16[512,1024]{1,0:T(8,128)(2,1)}, u32[]{:S(2)}, u32[]{:S(2)}) collective-permute-start(bf16[512,1024]{1,0:T(8,128)(2,1)S(1)} %collective-permute-done.11), channel_id=1, source_target_pairs={{1,0},{2,1},{5,4},{6,5},{9,8},{10,9},{13,12},{14,13},{17,16},{18,1... | collective-permute-start | bytes 3145736 | tf_op jit(solution)/shard_map/ppermute | solution.py:695
  101.9 23.1 %collective-permute-start.9 = (bf16[512,1024]{1,0:T(8,128)(2,1)}, bf16[512,1024]{1,0:T(8,128)(2,1)}, u32[]{:S(2)}, u32[]{:S(2)}) collective-permute-start(bf16[512,1024]{1,0:T(8,128)(2,1)} %collective-permute-done.8), channel_id=1, source_target_pairs={{1,2},{2,3},{5,6},{6,7},{9,10},{10,11},{13,14},{14,15},{17,18},{18... | collective-permute-start | bytes 3145736 | tf_op jit(solution)/shard_map/ppermute | solution.py:694
  123.7 35.8 %collective-permute-start.13 = (bf16[512,1024]{1,0:T(8,128)(2,1)}, bf16[512,1024]{1,0:T(8,128)(2,1)}, u32[]{:S(2)}, u32[]{:S(2)}) collective-permute-start(bf16[512,1024]{1,0:T(8,128)(2,1)} %collective-permute-done.12), channel_id=1, source_target_pairs={{1,0},{5,4},{9,8},{13,12},{17,16},{21,20},{25,24},{29,28}} | collective-permute-start | bytes 3145736 | tf_op jit(solution)/shard_map/ppermute | solution.py:695
  125.0 34.5 %collective-permute-start.10 = (bf16[512,1024]{1,0:T(8,128)(2,1)}, bf16[512,1024]{1,0:T(8,128)(2,1)}, u32[]{:S(2)}, u32[]{:S(2)}) collective-permute-start(bf16[512,1024]{1,0:T(8,128)(2,1)} %collective-permute-done.9), channel_id=1, source_target_pairs={{2,3},{6,7},{10,11},{14,15},{18,19},{22,23},{26,27},{30,31}} | collective-permute-start | bytes 3145736 | tf_op jit(solution)/shard_map/ppermute | solution.py:694
  132.7 38.9 %all-to-all-start.1 = ((bf16[4,256,512]{2,1,0:T(8,128)(2,1)}), bf16[4,256,512]{2,1,0:T(8,128)(2,1)}, u32[]{:S(2)}, u32[]{:S(2)}) async-start(bf16[4,256,512]{2,1,0:T(8,128)(2,1)} %pad_maximum_fusion.5), calls=%async_computation.1 | async-start | bytes 2097152 | tf_op jit(solution)/shard_map/all_to_all | solution.py:784
  192.5 20.5 %all-to-all-start.2 = ((bf16[4,512,256]{2,1,0:T(8,128)(2,1)}), bf16[4,512,256]{2,1,0:T(8,128)(2,1)S(1)}, u32[]{:S(2)}, u32[]{:S(2)}) async-start(bf16[4,512,256]{2,1,0:T(8,128)(2,1)} %bitcast.8), calls=%async_computation.2 | async-start | bytes 2097152 | tf_op jit(solution)/shard_map/all_to_all | solution.py:790
  197.1 188.9 %reduce-scatter.3.cloned.1.call-start = ((), (), s32[]{:S(2)}) async-start(), calls=%async_computation.10 | async-start | bytes 19464192 | tf_op jit(solution)/shard_map/reduce_scatter | solution.py:797
  260.4 19.5 %all-to-all-start.3 = ((bf16[512,4,256]{2,0,1:T(8,128)(2,1)}), bf16[512,4,256]{2,0,1:T(8,128)(2,1)S(1)}, u32[]{:S(2)}, u32[]{:S(2)}) async-start(bf16[512,4,256]{2,0,1:T(8,128)(2,1)} %bitcast.97), calls=%async_computation.3 | async-start | bytes 2097152 | tf_op jit(solution)/shard_map/all_to_all | solution.py:796
  264.0 184.6 %reduce-scatter.5.cloned.1.call-start = ((), (), s32[]{:S(2)}) async-start(), calls=%async_computation.11 | async-start | bytes 2703360 | tf_op jit(solution)/shard_map/reduce_scatter | solution.py:891
  265.3 36.7 %collective-permute-start.20 = (bf16[2,128,1024]{2,1,0:T(8,128)(2,1)}, bf16[2,128,1024]{2,1,0:T(8,128)(2,1)}, u32[]{:S(2)}, u32[]{:S(2)}) collective-permute-start(bf16[2,128,1024]{2,1,0:T(8,128)(2,1)} %get-tuple-element.127), channel_id=1, source_target_pairs={{0,8},{8,16},{16,24},{24,0},{1,9},{9,17},{17,25},{25,1},{2,10},{10... | collective-permute-start | bytes 1572872 | tf_op jit(solution)/shard_map/ppermute | solution.py:739
  266.8 35.2 %collective-permute-start.22 = (bf16[2,128,1024]{2,1,0:T(8,128)(2,1)}, bf16[2,128,1024]{2,1,0:T(8,128)(2,1)}, u32[]{:S(2)}, u32[]{:S(2)}) collective-permute-start(bf16[2,128,1024]{2,1,0:T(8,128)(2,1)} %get-tuple-element.128), channel_id=1, source_target_pairs={{0,24},{8,0},{16,8},{24,16},{1,25},{9,1},{17,9},{25,17},{2,26},{10... | collective-permute-start | bytes 1572872 | tf_op jit(solution)/shard_map/ppermute | solution.py:739
  268.7 33.3 %collective-permute-start.21 = (bf16[2,128,1024]{2,1,0:T(8,128)(2,1)}, bf16[2,128,1024]{2,1,0:T(8,128)(2,1)}, u32[]{:S(2)}, u32[]{:S(2)}) collective-permute-start(bf16[2,128,1024]{2,1,0:T(8,128)(2,1)} %get-tuple-element.129), channel_id=1, source_target_pairs={{0,16},{8,24},{16,0},{24,8},{1,17},{9,25},{17,1},{25,9},{2,18},{10... | collective-permute-start | bytes 1572872 | tf_op jit(solution)/shard_map/ppermute | solution.py:739
  298.6 30.9 %collective-permute-start.18 = (bf16[512,1024]{1,0:T(8,128)(2,1)}, bf16[512,1024]{1,0:T(8,128)(2,1)S(1)}, u32[]{:S(2)}, u32[]{:S(2)}) collective-permute-start(bf16[512,1024]{1,0:T(8,128)(2,1)} %get-tuple-element.88), channel_id=1, source_target_pairs={{0,1},{4,5},{8,9},{12,13},{16,17},{20,21},{24,25},{28,29}} | collective-permute-start | bytes 3145736 | tf_op jit(solution)/shard_map/ppermute | solution.py:727
  300.2 29.3 %collective-permute-start.19 = (bf16[512,1024]{1,0:T(8,128)(2,1)}, bf16[512,1024]{1,0:T(8,128)(2,1)}, u32[]{:S(2)}, u32[]{:S(2)}) collective-permute-start(bf16[512,1024]{1,0:T(8,128)(2,1)} %get-tuple-element.88), channel_id=1, source_target_pairs={{3,2},{7,6},{11,10},{15,14},{19,18},{23,22},{27,26},{31,30}} | collective-permute-start | bytes 3145736 | tf_op jit(solution)/shard_map/ppermute | solution.py:728
  335.5 20.9 %collective-permute-start.23 = (bf16[512,1024]{1,0:T(8,128)(2,1)}, bf16[512,1024]{1,0:T(8,128)(2,1)}, u32[]{:S(2)}, u32[]{:S(2)}) collective-permute-start(bf16[512,1024]{1,0:T(8,128)(2,1)} %get-tuple-element.92), channel_id=1, source_target_pairs={{0,1},{1,2},{4,5},{5,6},{8,9},{9,10},{12,13},{13,14},{16,17},{17,1... | collective-permute-start | bytes 3145736 | tf_op jit(solution)/shard_map/ppermute | solution.py:727
  360.6 21.0 %collective-permute-start.25 = (bf16[512,1024]{1,0:T(8,128)(2,1)}, bf16[512,1024]{1,0:T(8,128)(2,1)S(1)}, u32[]{:S(2)}, u32[]{:S(2)}) collective-permute-start(bf16[512,1024]{1,0:T(8,128)(2,1)} %get-tuple-element.102), channel_id=1, source_target_pairs={{0,1},{1,2},{2,3},{4,5},{5,6},{6,7},{8,9},{9,10},{10,11},{12,13},{... | collective-permute-start | bytes 3145736 | tf_op jit(solution)/shard_map/ppermute | solution.py:727
  411.2 33.0 %all-to-all-start.4 = ((bf16[4,40,1792]{2,1,0:T(8,128)(2,1)}), bf16[4,40,1792]{2,1,0:T(8,128)(2,1)}, u32[]{:S(2)}, u32[]{:S(2)}) async-start(bf16[4,40,1792]{2,1,0:T(8,128)(2,1)} %fusion.14), calls=%async_computation.5 | async-start | bytes 1146880 | tf_op jit(solution)/shard_map/all_to_all | solution.py:883
  (49 other events, 572.3 us)
Sparse Core Ops, SparseCore 0:
  39.3 27.3 all-gather.3
  75.5 41.5 all-gather.7
  119.0 76.5 all-gather.5
  258.3 117.6 reduce-scatter.2
  390.5 51.6 reduce-scatter.4

commit v18 on v17

--- a/solution.py
+++ b/solution.py
@@ -230,7 +230,7 @@
 
 def first_block_kernel(
     heads, top, chosen_ref, counts_ref, plan_ref, qkv_ref, mk_ref, mv_ref, go_ref, out_ref, lse_ref, cos_ref, sin_ref,
-    w_ref, partial_ref, grad_ref, gq_ref, gk_ref, gv_ref, stats_s,
+    w_ref, partial_ref, whole_ref, grad_ref, gq_ref, gk_ref, gv_ref, stats_s,
 ):
     rows = partial_ref.shape[0]
     subs = rows // QBLK
@@ -291,7 +291,9 @@
         heads, gq_ref[own, :], gk_ref[own, :], gv_ref[own, :], cos_ref[...], sin_ref[...]
     )
     grad_ref[...] = grad
-    partial_ref[...] = dot(grad, w_ref[...], NT).astype(BF16)
+    partial = dot(grad, w_ref[...], NT).astype(BF16)
+    partial_ref[...] = partial
+    whole_ref[...] = partial
 
 
 def first_block(plan, chosen, counts, qkv, memory, grad_out, out, lse, cosine, sine, w_qkv, heads, top):
@@ -323,6 +325,7 @@
             ],
             out_specs=[
                 pl.BlockSpec((rows, width), lambda i, *_: (0, 0)),
+                pl.BlockSpec((rows, width), lambda i, c, n, plan: (plan[0], 0)),
                 pl.BlockSpec((rows, 3 * wide), lambda i, *_: (0, 0)),
                 sums,
                 sums,
@@ -332,6 +335,7 @@
         ),
         out_shape=[
             jax.ShapeDtypeStruct((rows, width), BF16),
+            jax.ShapeDtypeStruct((length, width), BF16),
             jax.ShapeDtypeStruct((rows, 3 * wide), BF16),
             *[jax.ShapeDtypeStruct((length, wide), F32)] * 3,
         ],
@@ -347,7 +351,7 @@
 
 def other_blocks_kernel(
     heads, top, chosen_ref, counts_ref, plan_ref, q_ref, k_ref, v_ref, mk_ref, mv_ref, go_ref, out_ref, lse_ref,
-    cos_ref, sin_ref, w_ref, gq_in, gk_in, gv_in, partial_ref, grad_ref, gk_s, gv_s, gq_s,
+    cos_ref, sin_ref, w_ref, gq_in, gk_in, gv_in, _, partial_ref, grad_ref, gk_s, gv_s, gq_s,
 ):
     low = plan_ref[0]
     block = low + pl.num_programs(0) - 1 - pl.program_id(0)
@@ -393,7 +397,7 @@
     partial_ref[...] = dot(grad, w_ref[...], NT).astype(BF16)
 
 
-def other_blocks(plan, chosen, counts, qkv, memory, grad_out, out, lse, cosine, sine, w_qkv, sums, heads, top):
+def other_blocks(plan, chosen, counts, qkv, memory, grad_out, out, lse, cosine, sine, w_qkv, sums, partials, heads, top):
     length = qkv.shape[0]
     width = w_qkv.shape[0]
     wide = heads * HEAD_DIM
@@ -427,8 +431,9 @@
                 by_rows(wide),
                 pl.BlockSpec((length, wide), lambda i, *_: (0, 0)),
                 pl.BlockSpec((length, wide), lambda i, *_: (0, 0)),
+                pl.BlockSpec(memory_space=pl.ANY),
             ],
-            out_specs=[result(width), result(3 * wide)],
+            out_specs=[by_rows(width), result(3 * wide)],
             scratch_shapes=[
                 pltpu.VMEM((length, wide), F32),
                 pltpu.VMEM((length, wide), F32),
@@ -436,9 +441,10 @@
             ],
         ),
         out_shape=[
-            jax.ShapeDtypeStruct((count * rows, width), BF16),
+            jax.ShapeDtypeStruct((length, width), BF16),
             jax.ShapeDtypeStruct((count * rows, 3 * wide), BF16),
         ],
+        input_output_aliases={17: 0},
         compiler_params=pltpu.CompilerParams(vmem_limit_bytes=60 * MIB),
         cost_estimate=pl.CostEstimate(
             flops=6 * heads * length * HEAD_DIM * (length + top * MBLK),
@@ -446,7 +452,7 @@
             transcendentals=heads * length * (length // 3 + top * MBLK),
         ),
         name="other_blocks",
-    )(chosen, counts, plan, qkv, qkv, qkv, memory, memory, grad_out, out, lse, cosine, sine, w_qkv, *sums)
+    )(chosen, counts, plan, qkv, qkv, qkv, memory, memory, grad_out, out, lse, cosine, sine, w_qkv, *sums, partials)
 
 
 def ffn_kernel(
@@ -813,27 +819,23 @@
     is_last = (place < ring // 2).astype(jnp.int32)
     first_number = jnp.where(is_last == 1, count - 1, 0).astype(jnp.int32)
     low = 1 - is_last
-    first_partial, first_grad, *sums = first_block(
+    first_partial, partials, first_grad, *sums = first_block(
         jnp.stack([first_number, is_last]), chosen_all, counts_all, qkv, memory, grad_heads, attended_heads, lse,
         cosine, sine, w_qkv, heads, top,
     )
-    other_partial, other_grad = other_blocks(
+    partials, other_grad = other_blocks(
         low.reshape(1), chosen_all, counts_all, qkv, memory, grad_heads, attended_heads, lse, cosine, sine, w_qkv,
-        sums, heads, top,
+        sums, partials, heads, top,
     )
     order = jnp.concatenate([first_number.reshape(1), low + jnp.arange(count - 1, dtype=jnp.int32)])
     block_rows = first_partial.shape[0]
 
     def term(step, index):
         start = jnp.clip(index, 0, ring - 1) * rows
-        at = jnp.clip(start - low * block_rows, 0, other_partial.shape[0] - rows)
-        near = jnp.clip(start - first_number * block_rows, 0, block_rows - rows)
-        from_first = lax.dynamic_slice_in_dim(first_partial, near, rows, 0)
         if step == 0:
-            return from_first.astype(F32)
-        from_others = lax.dynamic_slice_in_dim(other_partial, at, rows, 0)
-        inside = (start >= first_number * block_rows) & (start < (first_number + 1) * block_rows)
-        return jnp.where(inside, from_first, from_others).astype(F32)
+            near = jnp.clip(start - first_number * block_rows, 0, block_rows - rows)
+            return lax.dynamic_slice_in_dim(first_partial, near, rows, 0).astype(F32)
+        return lax.dynamic_slice_in_dim(partials, start, rows, 0).astype(F32)
 
     kept = []
 

time: 468 us -> 466 us (level)
    unnamed x66 -> x56, local copies, waits for them, and re-layouts: 10.3 us -> 10.2 us
  transfers between devices with their start and end apart: 42 -> 42, of which waited for: 16 -> 16; matrix products, arithmetic and copies ran while one was open for 13% -> 12% of each run, Pallas kernels for 17% -> 17%
where the time goes in v18:
time: 466 us; the launch traced here: 457 us
  waiting for transfers between devices  161 us (35%)
  Pallas kernels  123 us (26%)
  starting transfers between devices  82.7 us (18%)
  other arithmetic  41.8 us (9%)
  local copies, waits for them, and re-layouts  34.3 us (7%)
  between operations  14.8 us (3%)
    ppermute x9, waiting for transfers between devices, chain_gather(): falling = tuple((lax.ppermute(block, axis, down) for block in falling))  81.7 us
    pallas_call x1, Pallas kernels, feed_forward(): pl.pallas_call(functools.partial(ffn_kernel, span, merged), grid=(steps,)...  44 us
    pallas_call x1, Pallas kernels, other_blocks(): pl.pallas_call(functools.partial(other_blocks_kernel, heads, top), grid_s...  24.7 us
    all_to_all x1, waiting for transfers between devices, body(): lax.all_to_all(late, 'fsdp', 0, 0, tiled=True)  23.7 us
    ppermute x9, starting transfers between devices, chain_gather(): rising = tuple((lax.ppermute(block, axis, up) for block in rising))  21.1 us
    pallas_call x1, Pallas kernels, attend_forward(): pl.pallas_call(functools.partial(forward_kernel, heads, top), grid_spec=p...  19.9 us
    pallas_call x1, Pallas kernels, first_block(): pl.pallas_call(functools.partial(first_block_kernel, heads, top), grid_sp...  17.7 us
    all_to_all x1, waiting for transfers between devices, body(): attended = lax.all_to_all(attended_heads, 'fsdp', 0, 1, tiled=True)  15 us
  transfers between devices with their start and end apart: 42, of which 16 were waited for; matrix products, arithmetic and copies ran while one was open for 12% of the time, Pallas kernels for 17%

profile of v18, /device:TPU:0, one launch (start us, length us, event | category | flops | bytes accessed | tf_op | source)
XLA Modules:
  0.0 457.3 jit_solution(3885644144957500484)
XLA Ops:
  11.2 5.6 %collective-permute-start = (bf16[32,6656]{1,0:T(8,128)(2,1)S(1)}, bf16[32,6656]{1,0:T(8,128)(2,1)S(1)}, u32[]{:S(2)}, u32[]{:S(2)}) collective-permute-start(bf16[32,6656]{1,0:T(8,128)(2,1)S(1)} %constant_dynamic-update-slice_fusion), channel_id=1, source_target_pairs={{0,1},{1,2},{2,3},{4,5},{5,6},{6,7},{8,9},{9,10},{10,11},{12,13},{... | collective-permute-start | bytes 1277960 | tf_op jit(solution)/shard_map/ppermute | solution.py:700
  43.2 14.5 %collective-permute-done.7 = bf16[88,1024]{1,0:T(8,128)(2,1)S(1)} collective-permute-done((bf16[88,1024]{1,0:T(8,128)(2,1)S(1)}, bf16[88,1024]{1,0:T(8,128)(2,1)S(1)}, u32[]{:S(2)}, u32[]{:S(2)}) %collective-permute-start.7) | collective-permute-done | bytes 180256 | tf_op jit(solution)/shard_map/ppermute | solution.py:701
  61.6 11.5 %collective-permute-done.17 = bf16[88,1024]{1,0:T(8,128)(2,1)} collective-permute-done((bf16[88,1024]{1,0:T(8,128)(2,1)S(1)}, bf16[88,1024]{1,0:T(8,128)(2,1)}, u32[]{:S(2)}, u32[]{:S(2)}) %collective-permute-start.17) | collective-permute-done | bytes 180256 | tf_op jit(solution)/shard_map/ppermute | solution.py:701
  78.6 5.6 %collective-permute-start.8 = (bf16[512,1024]{1,0:T(8,128)(2,1)S(1)}, bf16[512,1024]{1,0:T(8,128)(2,1)}, u32[]{:S(2)}, u32[]{:S(2)}) collective-permute-start(bf16[512,1024]{1,0:T(8,128)(2,1)S(1)} %bitcast.106), channel_id=1, source_target_pairs={{0,1},{1,2},{2,3},{4,5},{5,6},{6,7},{8,9},{9,10},{10,11},{12,13},{... | collective-permute-start | bytes 3145736 | tf_op jit(solution)/shard_map/ppermute | solution.py:700
  84.1 16.5 %collective-permute-done.11 = bf16[512,1024]{1,0:T(8,128)(2,1)S(1)} collective-permute-done((bf16[512,1024]{1,0:T(8,128)(2,1)S(1)}, bf16[512,1024]{1,0:T(8,128)(2,1)S(1)}, u32[]{:S(2)}, u32[]{:S(2)}) %collective-permute-start.11) | collective-permute-done | bytes 1048608 | tf_op jit(solution)/shard_map/ppermute | solution.py:701
  106.6 17.1 %collective-permute-done.12 = bf16[512,1024]{1,0:T(8,128)(2,1)} collective-permute-done((bf16[512,1024]{1,0:T(8,128)(2,1)S(1)}, bf16[512,1024]{1,0:T(8,128)(2,1)}, u32[]{:S(2)}, u32[]{:S(2)}) %collective-permute-start.12) | collective-permute-done | bytes 1048608 | tf_op jit(solution)/shard_map/ppermute | solution.py:701
  132.7 5.5 %all-to-all-start.1 = ((bf16[4,256,512]{2,1,0:T(8,128)(2,1)}), bf16[4,256,512]{2,1,0:T(8,128)(2,1)}, u32[]{:S(2)}, u32[]{:S(2)}) async-start(bf16[4,256,512]{2,1,0:T(8,128)(2,1)} %pad_maximum_fusion.5), calls=%async_computation.1 | async-start | bytes 2097152 | tf_op jit(solution)/shard_map/all_to_all | solution.py:790
  141.1 18.3 %collective-permute-done.13 = bf16[512,1024]{1,0:T(8,128)(2,1)} collective-permute-done((bf16[512,1024]{1,0:T(8,128)(2,1)}, bf16[512,1024]{1,0:T(8,128)(2,1)}, u32[]{:S(2)}, u32[]{:S(2)}) %collective-permute-start.13) | collective-permute-done | bytes 1048608 | tf_op jit(solution)/shard_map/ppermute | solution.py:701
  164.2 7.4 %project_qkv.1.q_ref.k_ref.v_ref.qkv_ref = bf16[2048,768]{1,0:T(8,128)(2,1)} custom-call(bf16[2048,1024]{1,0:T(8,128)(2,1)} %pad_maximum_fusion.tok_ref, f32[1,1024]{1,0:T(1,128)S(1)} %reshape.214.gain_ref, bf16[1024,768]{1,0:T(8,128)(2,1)S(1)} %bitcast.99, f32[2048,128]{1,0:T(8,128)S(1)} %get-tuple-element.155.cos_ref, f32[2048,128]{1,0:T(8,128)S(1)} %copy-done.3), custom_call_target="tpu_custom_call" | custom-call | flops 3221225472 | bytes 14680064 | tf_op jit(solution)/shard_map/project_qkv/pallas_call | solution.py:62
  171.6 19.9 %attend_forward.1 = (bf16[2048,256]{1,0:T(8,128)(2,1)}, f32[2048,2]{1,0:T(8,128)S(1)}) custom-call(s32[32]{0:T(128)S(1)} %reshape_squeeze.27.chosen_ref, s32[32]{0:T(128)S(1)} %reshape_squeeze.28.counts_ref, bf16[2048,768]{1,0:T(8,128)(2,1)} %project_qkv.1.q_ref.k_ref.v_ref.qkv_ref, bf16[2048,768]{1,0:T(8,128)(2,1)} %project_qkv.1.q_ref.k_ref.v_ref.qkv_ref, ...), custom_call_target="tpu_custom_call" | custom-call | flops 3221225472 | bytes 4194304 | tf_op jit(solution)/shard_map/attend_forward/pallas_call | solution.py:154
  192.5 4.6 %all-to-all-start.2 = ((bf16[4,512,256]{2,1,0:T(8,128)(2,1)}), bf16[4,512,256]{2,1,0:T(8,128)(2,1)S(1)}, u32[]{:S(2)}, u32[]{:S(2)}) async-start(bf16[4,512,256]{2,1,0:T(8,128)(2,1)} %bitcast.8), calls=%async_computation.2 | async-start | bytes 2097152 | tf_op jit(solution)/shard_map/all_to_all | solution.py:796
  198.1 15.0 %all-to-all-done.2 = bf16[4,512,256]{2,1,0:T(8,128)(2,1)S(1)} async-done(((bf16[4,512,256]{2,1,0:T(8,128)(2,1)}), bf16[4,512,256]{2,1,0:T(8,128)(2,1)S(1)}, u32[]{:S(2)}, u32[]{:S(2)}) %all-to-all-start.2) | async-done | bytes 1048608 | tf_op jit(solution)/shard_map/all_to_all | solution.py:796
  214.2 44.0 %feed_forward.1 = (bf16[512,1024]{1,0:T(8,128)(2,1)}, f32[512,1024]{1,0:T(8,128)}, bf16[512,1024]{1,0:T(8,128)(2,1)}, f32[1,1024]{1,0:T(1,128)}, bf16[8,128,1024...) custom-call(bf16[512,1024]{1,0:T(8,128)(2,1)} %bitcast.104, bf16[512,1024]{1,0:T(8,128)(2,1)} %bitcast.124, ...), custom_call_target="tpu_custom_call" | custom-call | flops 29796335616 | bytes 38797312 | tf_op jit(solution)/shard_map/feed_forward/pallas_call | solution.py:595
  270.9 9.0 %all-to-all-done.3 = bf16[512,4,256]{2,0,1:T(8,128)(2,1)S(1)} async-done(((bf16[512,4,256]{2,0,1:T(8,128)(2,1)}), bf16[512,4,256]{2,0,1:T(8,128)(2,1)S(1)}, u32[]{:S(2)}, u32[]{:S(2)}) %all-to-all-start.3) | async-done | bytes 1048608 | tf_op jit(solution)/shard_map/all_to_all | solution.py:802
  280.9 17.7 %first_block.1 = (bf16[512,1024]{1,0:T(8,128)(2,1)}, bf16[2048,1024]{1,0:T(8,128)(2,1)}, bf16[512,768]{1,0:T(8,128)(2,1)}, f32[2048,256]{1,0:T(8,128)}, f32[2048,256]{1,0:T(8,128)}, /*index=5*/f32[2048,256]{1,0:T(8,128)}) custom-call(s32[32]{0:T(128)} %copy-done.8, s32[32]{0:T(128)} %copy-done.7, s32[2]{0:T(128)} %pad_add_fusion.plan_ref, ...), custom_call_target="tpu_custom_call" | custom-call | flops 4294967296 | bytes 20971520 | tf_op jit(solution)/shard_map/first_block/pallas_call | solution.py:310
  304.6 24.7 %other_blocks.1 = (bf16[2048,1024]{1,0:T(8,128)(2,1)}, bf16[1536,768]{1,0:T(8,128)(2,1)}) custom-call(s32[32]{0:T(128)} %copy-done.8, s32[32]{0:T(128)} %copy-done.7, s32[1]{0:T(128)} %bitcast.12.plan_ref, bf16[2048,768]{1,0:T(8,128)(2,1)} %project_qkv.1.q_ref.k_ref.v_ref.qkv_ref, ...), custom_call_target="tpu_custom_call", output_to_operand_aliasing={{0}: (17, {})} | custom-call | flops 8053063680 | bytes 20971520 | tf_op jit(solution)/shard_map/other_blocks/pallas_call | solution.py:414
  330.3 4.7 %add_convert_fusion.2 = (bf16[512,1024]{1,0:T(8,128)(2,1)}, bf16[512,1024]{1,0:T(8,128)(2,1)}) fusion(bf16[512,1024]{1,0:T(8,128)(2,1)} %collective-permute-done.19, bf16[2048,1024]{1,0:T(8,128)(2,1)} %get-tuple-element.87, s32[]{:T(128)S(6)} %select_n.326, bf16[512,1024]{1,0:T(8,128)(2,1)} %copy-done.19, s32[]{:T(128)S(6)} %select_n.325), kind=kLoop, calls=%fused_computation.14 | loop fusion | flops 4194304 | bytes 6291464 | tf_op jit(solution)/shard_map/convert_element_type | solution.py:731
  343.6 8.9 %projection_grads.1 = (bf16[1024,768]{1,0:T(8,128)(2,1)S(1)}, f32[1024,1]{1,0:T(8,128)S(1)}) custom-call(s32[4]{0:T(128)S(1)} %pad_add_fusion.1.order_ref, bf16[2048,1024]{1,0:T(8,128)(2,1)} %pad_maximum_fusion.tok_ref, f32[1024,1]{1,0:T(8,128)S(1)} %copy-done.6, bf16[1024,768]{1,0:T(8,128)(2,1)S(1)} %bitcast.102, bf16[512,768]{1,0:T(8,128)(2,1)S(1)} %copy-done.10, ...), custom_call_target="tpu_custom_call" | custom-call | flops 3221225472 | bytes 7340032 | tf_op jit(solution)/shard_map/projection_grads/pallas_call | solution.py:658
  352.6 5.1 %collective-permute-done.23 = bf16[512,1024]{1,0:T(8,128)(2,1)} collective-permute-done((bf16[512,1024]{1,0:T(8,128)(2,1)}, bf16[512,1024]{1,0:T(8,128)(2,1)}, u32[]{:S(2)}, u32[]{:S(2)}) %collective-permute-start.23) | collective-permute-done | bytes 1048608 | tf_op jit(solution)/shard_map/ppermute | solution.py:733
  360.4 9.1 %collective-permute-start.25 = (bf16[512,1024]{1,0:T(8,128)(2,1)S(1)}, bf16[512,1024]{1,0:T(8,128)(2,1)}, u32[]{:S(2)}, u32[]{:S(2)}) collective-permute-start(bf16[512,1024]{1,0:T(8,128)(2,1)S(1)} %get-tuple-element.104), channel_id=1, source_target_pairs={{0,1},{1,2},{2,3},{4,5},{5,6},{6,7},{8,9},{9,10},{10,11},{12,13},{... | collective-permute-start | bytes 3145736 | tf_op jit(solution)/shard_map/ppermute | solution.py:733
  370.9 9.8 %collective-permute-done.25 = bf16[512,1024]{1,0:T(8,128)(2,1)} collective-permute-done((bf16[512,1024]{1,0:T(8,128)(2,1)S(1)}, bf16[512,1024]{1,0:T(8,128)(2,1)}, u32[]{:S(2)}, u32[]{:S(2)}) %collective-permute-start.25) | collective-permute-done | bytes 1048608 | tf_op jit(solution)/shard_map/ppermute | solution.py:733
  380.8 5.4 %collective-permute-done.26 = bf16[512,1024]{1,0:T(8,128)(2,1)} collective-permute-done((bf16[512,1024]{1,0:T(8,128)(2,1)S(1)}, bf16[512,1024]{1,0:T(8,128)(2,1)}, u32[]{:S(2)}, u32[]{:S(2)}) %collective-permute-start.26) | collective-permute-done | bytes 1048608 | tf_op jit(solution)/shard_map/ppermute | solution.py:734
  400.6 4.4 collective-permute-done.28
  419.9 23.7 %all-to-all-done.4 = bf16[4,40,1792]{2,1,0:T(8,128)(2,1)S(1)} async-done(((bf16[4,40,1792]{2,1,0:T(8,128)(2,1)}), bf16[4,40,1792]{2,1,0:T(8,128)(2,1)S(1)}, u32[]{:S(2)}, u32[]{:S(2)}) %all-to-all-start.4) | async-done | bytes 573472 | tf_op jit(solution)/shard_map/all_to_all | solution.py:885
  (213 shorter events, 134.5 us)
Async XLA Ops:
  9.9 28.4 %collective-permute-start.2 = (bf16[32,6656]{1,0:T(8,128)(2,1)S(1)}, bf16[32,6656]{1,0:T(8,128)(2,1)S(1)}, u32[]{:S(2)}, u32[]{:S(2)}) collective-permute-start(bf16[32,6656]{1,0:T(8,128)(2,1)S(1)} %constant_dynamic-update-slice_fusion), channel_id=1, source_target_pairs={{1,0},{2,1},{3,2},{5,4},{6,5},{7,6},{9,8},{10,9},{11,10},{13,12},{... | collective-permute-start | bytes 1277960 | tf_op jit(solution)/shard_map/ppermute | solution.py:701
  11.2 27.1 %collective-permute-start = (bf16[32,6656]{1,0:T(8,128)(2,1)S(1)}, bf16[32,6656]{1,0:T(8,128)(2,1)S(1)}, u32[]{:S(2)}, u32[]{:S(2)}) collective-permute-start(bf16[32,6656]{1,0:T(8,128)(2,1)S(1)} %constant_dynamic-update-slice_fusion), channel_id=1, source_target_pairs={{0,1},{1,2},{2,3},{4,5},{5,6},{6,7},{8,9},{9,10},{10,11},{12,13},{... | collective-permute-start | bytes 1277960 | tf_op jit(solution)/shard_map/ppermute | solution.py:700
  27.0 111.4 %all-gather.4.cloned.1.call-start = ((), (), s32[]{:S(2)}) async-start(), calls=%async_computation.7 | async-start | bytes 2211840 | tf_op jit(solution)/shard_map/all_gather | solution.py:780
  39.1 175.0 %all-gather.8.cloned.1.call-start = ((), (), s32[]{:S(2)}) async-start(), calls=%async_computation.9 | async-start | bytes 6488064 | tf_op jit(solution)/shard_map/all_gather | solution.py:791
  75.4 138.8 %all-gather.6.cloned.1.call-start = ((), (), s32[]{:S(2)}) async-start(), calls=%async_computation.8 | async-start | bytes 15335424 | tf_op jit(solution)/shard_map/all_gather | solution.py:784
  77.3 23.3 %collective-permute-start.11 = (bf16[512,1024]{1,0:T(8,128)(2,1)S(1)}, bf16[512,1024]{1,0:T(8,128)(2,1)S(1)}, u32[]{:S(2)}, u32[]{:S(2)}) collective-permute-start(bf16[512,1024]{1,0:T(8,128)(2,1)S(1)} %bitcast.105), channel_id=1, source_target_pairs={{1,0},{2,1},{3,2},{5,4},{6,5},{7,6},{9,8},{10,9},{11,10},{13,12},{... | collective-permute-start | bytes 3145736 | tf_op jit(solution)/shard_map/ppermute | solution.py:701
  78.6 23.3 %collective-permute-start.8 = (bf16[512,1024]{1,0:T(8,128)(2,1)S(1)}, bf16[512,1024]{1,0:T(8,128)(2,1)}, u32[]{:S(2)}, u32[]{:S(2)}) collective-permute-start(bf16[512,1024]{1,0:T(8,128)(2,1)S(1)} %bitcast.106), channel_id=1, source_target_pairs={{0,1},{1,2},{2,3},{4,5},{5,6},{6,7},{8,9},{9,10},{10,11},{12,13},{... | collective-permute-start | bytes 3145736 | tf_op jit(solution)/shard_map/ppermute | solution.py:700
  100.6 23.1 %collective-permute-start.12 = (bf16[512,1024]{1,0:T(8,128)(2,1)S(1)}, bf16[512,1024]{1,0:T(8,128)(2,1)}, u32[]{:S(2)}, u32[]{:S(2)}) collective-permute-start(bf16[512,1024]{1,0:T(8,128)(2,1)S(1)} %collective-permute-done.11), channel_id=1, source_target_pairs={{1,0},{2,1},{5,4},{6,5},{9,8},{10,9},{13,12},{14,13},{17,16},{18,1... | collective-permute-start | bytes 3145736 | tf_op jit(solution)/shard_map/ppermute | solution.py:701
  101.9 23.1 %collective-permute-start.9 = (bf16[512,1024]{1,0:T(8,128)(2,1)}, bf16[512,1024]{1,0:T(8,128)(2,1)}, u32[]{:S(2)}, u32[]{:S(2)}) collective-permute-start(bf16[512,1024]{1,0:T(8,128)(2,1)} %collective-permute-done.8), channel_id=1, source_target_pairs={{1,2},{2,3},{5,6},{6,7},{9,10},{10,11},{13,14},{14,15},{17,18},{18... | collective-permute-start | bytes 3145736 | tf_op jit(solution)/shard_map/ppermute | solution.py:700
  123.7 35.8 %collective-permute-start.13 = (bf16[512,1024]{1,0:T(8,128)(2,1)}, bf16[512,1024]{1,0:T(8,128)(2,1)}, u32[]{:S(2)}, u32[]{:S(2)}) collective-permute-start(bf16[512,1024]{1,0:T(8,128)(2,1)} %collective-permute-done.12), channel_id=1, source_target_pairs={{1,0},{5,4},{9,8},{13,12},{17,16},{21,20},{25,24},{29,28}} | collective-permute-start | bytes 3145736 | tf_op jit(solution)/shard_map/ppermute | solution.py:701
  125.0 34.5 %collective-permute-start.10 = (bf16[512,1024]{1,0:T(8,128)(2,1)}, bf16[512,1024]{1,0:T(8,128)(2,1)}, u32[]{:S(2)}, u32[]{:S(2)}) collective-permute-start(bf16[512,1024]{1,0:T(8,128)(2,1)} %collective-permute-done.9), channel_id=1, source_target_pairs={{2,3},{6,7},{10,11},{14,15},{18,19},{22,23},{26,27},{30,31}} | collective-permute-start | bytes 3145736 | tf_op jit(solution)/shard_map/ppermute | solution.py:700
  132.7 38.9 %all-to-all-start.1 = ((bf16[4,256,512]{2,1,0:T(8,128)(2,1)}), bf16[4,256,512]{2,1,0:T(8,128)(2,1)}, u32[]{:S(2)}, u32[]{:S(2)}) async-start(bf16[4,256,512]{2,1,0:T(8,128)(2,1)} %pad_maximum_fusion.5), calls=%async_computation.1 | async-start | bytes 2097152 | tf_op jit(solution)/shard_map/all_to_all | solution.py:790
  192.5 20.5 %all-to-all-start.2 = ((bf16[4,512,256]{2,1,0:T(8,128)(2,1)}), bf16[4,512,256]{2,1,0:T(8,128)(2,1)S(1)}, u32[]{:S(2)}, u32[]{:S(2)}) async-start(bf16[4,512,256]{2,1,0:T(8,128)(2,1)} %bitcast.8), calls=%async_computation.2 | async-start | bytes 2097152 | tf_op jit(solution)/shard_map/all_to_all | solution.py:796
  197.1 189.1 %reduce-scatter.3.cloned.1.call-start = ((), (), s32[]{:S(2)}) async-start(), calls=%async_computation.10 | async-start | bytes 19464192 | tf_op jit(solution)/shard_map/reduce_scatter | solution.py:803
  264.0 182.8 %reduce-scatter.5.cloned.1.call-start = ((), (), s32[]{:S(2)}) async-start(), calls=%async_computation.11 | async-start | bytes 2703360 | tf_op jit(solution)/shard_map/reduce_scatter | solution.py:893
  265.4 36.7 %collective-permute-start.20 = (bf16[2,128,1024]{2,1,0:T(8,128)(2,1)}, bf16[2,128,1024]{2,1,0:T(8,128)(2,1)}, u32[]{:S(2)}, u32[]{:S(2)}) collective-permute-start(bf16[2,128,1024]{2,1,0:T(8,128)(2,1)} %get-tuple-element.129), channel_id=1, source_target_pairs={{0,8},{8,16},{16,24},{24,0},{1,9},{9,17},{17,25},{25,1},{2,10},{10... | collective-permute-start | bytes 1572872 | tf_op jit(solution)/shard_map/ppermute | solution.py:745
  266.9 35.2 %collective-permute-start.22 = (bf16[2,128,1024]{2,1,0:T(8,128)(2,1)}, bf16[2,128,1024]{2,1,0:T(8,128)(2,1)}, u32[]{:S(2)}, u32[]{:S(2)}) collective-permute-start(bf16[2,128,1024]{2,1,0:T(8,128)(2,1)} %get-tuple-element.130), channel_id=1, source_target_pairs={{0,24},{8,0},{16,8},{24,16},{1,25},{9,1},{17,9},{25,17},{2,26},{10... | collective-permute-start | bytes 1572872 | tf_op jit(solution)/shard_map/ppermute | solution.py:745
  268.8 33.3 %collective-permute-start.21 = (bf16[2,128,1024]{2,1,0:T(8,128)(2,1)}, bf16[2,128,1024]{2,1,0:T(8,128)(2,1)}, u32[]{:S(2)}, u32[]{:S(2)}) collective-permute-start(bf16[2,128,1024]{2,1,0:T(8,128)(2,1)} %get-tuple-element.131), channel_id=1, source_target_pairs={{0,16},{8,24},{16,0},{24,8},{1,17},{9,25},{17,1},{25,9},{2,18},{10... | collective-permute-start | bytes 1572872 | tf_op jit(solution)/shard_map/ppermute | solution.py:745
  298.7 30.7 %collective-permute-start.18 = (bf16[512,1024]{1,0:T(8,128)(2,1)}, bf16[512,1024]{1,0:T(8,128)(2,1)S(1)}, u32[]{:S(2)}, u32[]{:S(2)}) collective-permute-start(bf16[512,1024]{1,0:T(8,128)(2,1)} %get-tuple-element.90), channel_id=1, source_target_pairs={{0,1},{4,5},{8,9},{12,13},{16,17},{20,21},{24,25},{28,29}} | collective-permute-start | bytes 3145736 | tf_op jit(solution)/shard_map/ppermute | solution.py:733
  300.2 29.1 %collective-permute-start.19 = (bf16[512,1024]{1,0:T(8,128)(2,1)}, bf16[512,1024]{1,0:T(8,128)(2,1)}, u32[]{:S(2)}, u32[]{:S(2)}) collective-permute-start(bf16[512,1024]{1,0:T(8,128)(2,1)} %get-tuple-element.90), channel_id=1, source_target_pairs={{3,2},{7,6},{11,10},{15,14},{19,18},{23,22},{27,26},{31,30}} | collective-permute-start | bytes 3145736 | tf_op jit(solution)/shard_map/ppermute | solution.py:734
  335.0 22.7 %collective-permute-start.23 = (bf16[512,1024]{1,0:T(8,128)(2,1)}, bf16[512,1024]{1,0:T(8,128)(2,1)}, u32[]{:S(2)}, u32[]{:S(2)}) collective-permute-start(bf16[512,1024]{1,0:T(8,128)(2,1)} %get-tuple-element.94), channel_id=1, source_target_pairs={{0,1},{1,2},{4,5},{5,6},{8,9},{9,10},{12,13},{13,14},{16,17},{17,1... | collective-permute-start | bytes 3145736 | tf_op jit(solution)/shard_map/ppermute | solution.py:733
  337.5 20.2 %collective-permute-start.24 = (bf16[512,1024]{1,0:T(8,128)(2,1)}, bf16[512,1024]{1,0:T(8,128)(2,1)}, u32[]{:S(2)}, u32[]{:S(2)}) collective-permute-start(bf16[512,1024]{1,0:T(8,128)(2,1)} %get-tuple-element.95), channel_id=1, source_target_pairs={{2,1},{3,2},{6,5},{7,6},{10,9},{11,10},{14,13},{15,14},{18,17},{19... | collective-permute-start | bytes 3145736 | tf_op jit(solution)/shard_map/ppermute | solution.py:734
  360.4 20.4 %collective-permute-start.25 = (bf16[512,1024]{1,0:T(8,128)(2,1)S(1)}, bf16[512,1024]{1,0:T(8,128)(2,1)}, u32[]{:S(2)}, u32[]{:S(2)}) collective-permute-start(bf16[512,1024]{1,0:T(8,128)(2,1)S(1)} %get-tuple-element.104), channel_id=1, source_target_pairs={{0,1},{1,2},{2,3},{4,5},{5,6},{6,7},{8,9},{9,10},{10,11},{12,13},{... | collective-permute-start | bytes 3145736 | tf_op jit(solution)/shard_map/ppermute | solution.py:733
  409.9 33.6 %all-to-all-start.4 = ((bf16[4,40,1792]{2,1,0:T(8,128)(2,1)}), bf16[4,40,1792]{2,1,0:T(8,128)(2,1)S(1)}, u32[]{:S(2)}, u32[]{:S(2)}) async-start(bf16[4,40,1792]{2,1,0:T(8,128)(2,1)} %fusion.14), calls=%async_computation.5 | async-start | bytes 1146880 | tf_op jit(solution)/shard_map/all_to_all | solution.py:885
  (44 other events, 493.8 us)
Sparse Core Ops, SparseCore 0:
  39.3 27.3 all-gather.3
  75.5 41.5 all-gather.7
  119.0 76.5 all-gather.5
  258.3 117.6 reduce-scatter.2
  390.7 51.7 reduce-scatter.4

commit v19 on v18

--- a/solution.py
+++ b/solution.py
@@ -847,7 +847,7 @@
         )
         return kept
 
-    own_term, arrived = chain_scatter(term, "fsdp", [lambda sent: out_grads, make_projection_grads])
+    own_term, arrived = chain_scatter(term, "fsdp", [lambda sent: None, lambda sent: (out_grads, make_projection_grads(sent))])
     grad_w_qkv, gain_one_grad = kept
     grads = after(grads, arrived[-1])
 
@@ -877,18 +877,17 @@
     inner = jnp.mean(scaled * own, -1, keepdims=True)
     tokens_grad = (grad_middle + factor * scaled - own * (factor * factor * factor * inner)).astype(BF16)
 
-    gains = late[-extra : 2 - extra, : ring * share].reshape(2, ring, share).transpose(1, 0, 2)
-    gains = jnp.pad(gains, ((0, 0), (0, extra - 2), (0, 3 * wide - share)))
-    late = jnp.concatenate([late[:-extra].reshape(ring, share, 3 * wide), gains], 1)
-    out_grads = jnp.pad(out_grads.reshape(ring, share, width), ((0, 0), (0, extra), (0, 0)))
-    late = jnp.concatenate([late, out_grads], 2)
+    gains = late[-extra : 2 - extra, : ring * share].reshape(2, ring, share).transpose(1, 2, 0)
+    gains = jnp.pad(gains, ((0, 0), (0, 0), (0, HEAD_DIM - 2)))
+    late = late[:-extra].reshape(ring, share, 3 * wide)
+    late = jnp.concatenate([late, out_grads.reshape(ring, share, width), gains], 2)
     late = after(lax.all_to_all(late, "fsdp", 0, 0, tiled=True), tokens_grad).astype(F32)
-    out_share = jnp.sum(late[:, :share, 3 * wide :], 0)
     projections = [
-        late[:, :share, part * wide : (part + 1) * wide].transpose(1, 0, 2).reshape(share, width)
+        late[:, :, part * wide : (part + 1) * wide].transpose(1, 0, 2).reshape(share, width)
         for part in range(3)
     ]
-    gain_shares = jnp.sum(late[:, share : share + 2, :share], 0)
+    summed = jnp.sum(late[:, :, 3 * wide :], 0)
+    out_share, gain_shares = summed[:, :width], summed[:, width : width + 2]
 
     pieces = lax.psum_scatter(pieces, "fsdp", scatter_dimension=0, tiled=True)
     pieces = after(pieces, (tokens_grad, projections, out_share, gain_shares))[0].astype(F32)
@@ -902,8 +901,8 @@
         others[:, :hidden_width],
         others[:, hidden_width:],
         down_share,
-        gain_shares[0],
-        gain_shares[1],
+        gain_shares[:, 0],
+        gain_shares[:, 1],
     )
 
 

time: 466 us -> 472 us (1.013)
  waiting for transfers between devices: 161 us -> 168 us
    all_to_all x1, waiting for transfers between devices: 9.04 us -> 14.8 us  [body(): grad_heads = lax.all_to_all(grad_attended, 'fsdp', 1, 0, tiled=True)]
    unnamed x56 -> x55, local copies, waits for them, and re-layouts: 10.2 us -> 8.48 us
  transfers between devices with their start and end apart: 42 -> 42, of which waited for: 16 -> 18; matrix products, arithmetic and copies ran while one was open for 12% -> 12% of each run, Pallas kernels for 17% -> 17%
where the time goes in v19:
time: 472 us; the launch traced here: 463 us
  waiting for transfers between devices  168 us (36%)
  Pallas kernels  122 us (26%)
  starting transfers between devices  84.3 us (18%)
  other arithmetic  40.2 us (9%)
  local copies, waits for them, and re-layouts  33.3 us (7%)
  between operations  14.7 us (3%)
    ppermute x9, waiting for transfers between devices, chain_gather(): falling = tuple((lax.ppermute(block, axis, down) for block in falling))  81.8 us
    pallas_call x1, Pallas kernels, feed_forward(): pl.pallas_call(functools.partial(ffn_kernel, span, merged), grid=(steps,)...  44 us
    pallas_call x1, Pallas kernels, other_blocks(): pl.pallas_call(functools.partial(other_blocks_kernel, heads, top), grid_s...  24.5 us
    all_to_all x1, waiting for transfers between devices, body(): lax.all_to_all(late, 'fsdp', 0, 0, tiled=True)  21.7 us
    ppermute x9, starting transfers between devices, chain_gather(): rising = tuple((lax.ppermute(block, axis, up) for block in rising))  21.1 us
    pallas_call x1, Pallas kernels, attend_forward(): pl.pallas_call(functools.partial(forward_kernel, heads, top), grid_spec=p...  19.9 us
    pallas_call x1, Pallas kernels, first_block(): pl.pallas_call(functools.partial(first_block_kernel, heads, top), grid_sp...  18 us
    all_to_all x1, waiting for transfers between devices, body(): attended = lax.all_to_all(attended_heads, 'fsdp', 0, 1, tiled=True)  15 us
  transfers between devices with their start and end apart: 42, of which 18 were waited for; matrix products, arithmetic and copies ran while one was open for 12% of the time, Pallas kernels for 17%

profile of v19, /device:TPU:0, one launch (start us, length us, event | category | flops | bytes accessed | tf_op | source)
XLA Modules:
  0.0 463.1 jit_solution(7359637195250168600)
XLA Ops:
  11.2 5.6 %collective-permute-start = (bf16[32,6656]{1,0:T(8,128)(2,1)S(1)}, bf16[32,6656]{1,0:T(8,128)(2,1)S(1)}, u32[]{:S(2)}, u32[]{:S(2)}) collective-permute-start(bf16[32,6656]{1,0:T(8,128)(2,1)S(1)} %constant_dynamic-update-slice_fusion), channel_id=1, source_target_pairs={{0,1},{1,2},{2,3},{4,5},{5,6},{6,7},{8,9},{9,10},{10,11},{12,13},{... | collective-permute-start | bytes 1277960 | tf_op jit(solution)/shard_map/ppermute | solution.py:700
  43.2 14.5 %collective-permute-done.7 = bf16[88,1024]{1,0:T(8,128)(2,1)S(1)} collective-permute-done((bf16[88,1024]{1,0:T(8,128)(2,1)S(1)}, bf16[88,1024]{1,0:T(8,128)(2,1)S(1)}, u32[]{:S(2)}, u32[]{:S(2)}) %collective-permute-start.7) | collective-permute-done | bytes 180256 | tf_op jit(solution)/shard_map/ppermute | solution.py:701
  61.7 11.5 %collective-permute-done.17 = bf16[88,1024]{1,0:T(8,128)(2,1)} collective-permute-done((bf16[88,1024]{1,0:T(8,128)(2,1)S(1)}, bf16[88,1024]{1,0:T(8,128)(2,1)}, u32[]{:S(2)}, u32[]{:S(2)}) %collective-permute-start.17) | collective-permute-done | bytes 180256 | tf_op jit(solution)/shard_map/ppermute | solution.py:701
  78.5 5.6 %collective-permute-start.8 = (bf16[512,1024]{1,0:T(8,128)(2,1)S(1)}, bf16[512,1024]{1,0:T(8,128)(2,1)}, u32[]{:S(2)}, u32[]{:S(2)}) collective-permute-start(bf16[512,1024]{1,0:T(8,128)(2,1)S(1)} %bitcast.100), channel_id=1, source_target_pairs={{0,1},{1,2},{2,3},{4,5},{5,6},{6,7},{8,9},{9,10},{10,11},{12,13},{... | collective-permute-start | bytes 3145736 | tf_op jit(solution)/shard_map/ppermute | solution.py:700
  84.1 16.5 %collective-permute-done.11 = bf16[512,1024]{1,0:T(8,128)(2,1)S(1)} collective-permute-done((bf16[512,1024]{1,0:T(8,128)(2,1)S(1)}, bf16[512,1024]{1,0:T(8,128)(2,1)S(1)}, u32[]{:S(2)}, u32[]{:S(2)}) %collective-permute-start.11) | collective-permute-done | bytes 1048608 | tf_op jit(solution)/shard_map/ppermute | solution.py:701
  106.6 17.1 %collective-permute-done.12 = bf16[512,1024]{1,0:T(8,128)(2,1)} collective-permute-done((bf16[512,1024]{1,0:T(8,128)(2,1)S(1)}, bf16[512,1024]{1,0:T(8,128)(2,1)}, u32[]{:S(2)}, u32[]{:S(2)}) %collective-permute-start.12) | collective-permute-done | bytes 1048608 | tf_op jit(solution)/shard_map/ppermute | solution.py:701
  132.7 5.5 %all-to-all-start.1 = ((bf16[4,256,512]{2,1,0:T(8,128)(2,1)}), bf16[4,256,512]{2,1,0:T(8,128)(2,1)}, u32[]{:S(2)}, u32[]{:S(2)}) async-start(bf16[4,256,512]{2,1,0:T(8,128)(2,1)} %pad_maximum_fusion.5), calls=%async_computation.1 | async-start | bytes 2097152 | tf_op jit(solution)/shard_map/all_to_all | solution.py:790
  141.1 18.4 %collective-permute-done.13 = bf16[512,1024]{1,0:T(8,128)(2,1)} collective-permute-done((bf16[512,1024]{1,0:T(8,128)(2,1)}, bf16[512,1024]{1,0:T(8,128)(2,1)}, u32[]{:S(2)}, u32[]{:S(2)}) %collective-permute-start.13) | collective-permute-done | bytes 1048608 | tf_op jit(solution)/shard_map/ppermute | solution.py:701
  164.2 7.4 %project_qkv.1.q_ref.k_ref.v_ref.qkv_ref = bf16[2048,768]{1,0:T(8,128)(2,1)} custom-call(bf16[2048,1024]{1,0:T(8,128)(2,1)} %pad_maximum_fusion.tok_ref, f32[1,1024]{1,0:T(1,128)S(1)} %reshape.214.gain_ref, bf16[1024,768]{1,0:T(8,128)(2,1)S(1)} %bitcast.93, f32[2048,128]{1,0:T(8,128)S(1)} %get-tuple-element.155.cos_ref, f32[2048,128]{1,0:T(8,128)S(1)} %copy-done.3), custom_call_target="tpu_custom_call" | custom-call | flops 3221225472 | bytes 14680064 | tf_op jit(solution)/shard_map/project_qkv/pallas_call | solution.py:62
  171.6 19.9 %attend_forward.1 = (bf16[2048,256]{1,0:T(8,128)(2,1)}, f32[2048,2]{1,0:T(8,128)S(1)}) custom-call(s32[32]{0:T(128)S(1)} %reshape_squeeze.27.chosen_ref, s32[32]{0:T(128)S(1)} %reshape_squeeze.28.counts_ref, bf16[2048,768]{1,0:T(8,128)(2,1)} %project_qkv.1.q_ref.k_ref.v_ref.qkv_ref, bf16[2048,768]{1,0:T(8,128)(2,1)} %project_qkv.1.q_ref.k_ref.v_ref.qkv_ref, ...), custom_call_target="tpu_custom_call" | custom-call | flops 3221225472 | bytes 4194304 | tf_op jit(solution)/shard_map/attend_forward/pallas_call | solution.py:154
  192.5 4.6 %all-to-all-start.2 = ((bf16[4,512,256]{2,1,0:T(8,128)(2,1)}), bf16[4,512,256]{2,1,0:T(8,128)(2,1)S(1)}, u32[]{:S(2)}, u32[]{:S(2)}) async-start(bf16[4,512,256]{2,1,0:T(8,128)(2,1)} %bitcast.8), calls=%async_computation.2 | async-start | bytes 2097152 | tf_op jit(solution)/shard_map/all_to_all | solution.py:796
  198.1 15.0 %all-to-all-done.2 = bf16[4,512,256]{2,1,0:T(8,128)(2,1)S(1)} async-done(((bf16[4,512,256]{2,1,0:T(8,128)(2,1)}), bf16[4,512,256]{2,1,0:T(8,128)(2,1)S(1)}, u32[]{:S(2)}, u32[]{:S(2)}) %all-to-all-start.2) | async-done | bytes 1048608 | tf_op jit(solution)/shard_map/all_to_all | solution.py:796
  214.2 44.0 %feed_forward.1 = (bf16[512,1024]{1,0:T(8,128)(2,1)}, f32[512,1024]{1,0:T(8,128)}, bf16[512,1024]{1,0:T(8,128)(2,1)}, f32[1,1024]{1,0:T(1,128)}, bf16[8,128,1024...) custom-call(bf16[512,1024]{1,0:T(8,128)(2,1)} %bitcast.98, bf16[512,1024]{1,0:T(8,128)(2,1)} %bitcast.118, ...), custom_call_target="tpu_custom_call" | custom-call | flops 29796335616 | bytes 38797312 | tf_op jit(solution)/shard_map/feed_forward/pallas_call | solution.py:595
  265.1 14.8 %all-to-all-done.3 = bf16[512,4,256]{2,0,1:T(8,128)(2,1)S(1)} async-done(((bf16[512,4,256]{2,0,1:T(8,128)(2,1)}), bf16[512,4,256]{2,0,1:T(8,128)(2,1)S(1)}, u32[]{:S(2)}, u32[]{:S(2)}) %all-to-all-start.3) | async-done | bytes 1048608 | tf_op jit(solution)/shard_map/all_to_all | solution.py:802
  280.9 18.0 %first_block.1 = (bf16[512,1024]{1,0:T(8,128)(2,1)}, bf16[2048,1024]{1,0:T(8,128)(2,1)}, bf16[512,768]{1,0:T(8,128)(2,1)}, f32[2048,256]{1,0:T(8,128)}, f32[2048,256]{1,0:T(8,128)}, /*index=5*/f32[2048,256]{1,0:T(8,128)}) custom-call(s32[32]{0:T(128)} %copy-done.8, s32[32]{0:T(128)} %copy-done.7, s32[2]{0:T(128)} %pad_add_fusion.plan_ref, ...), custom_call_target="tpu_custom_call" | custom-call | flops 4294967296 | bytes 20971520 | tf_op jit(solution)/shard_map/first_block/pallas_call | solution.py:310
  308.0 24.5 %other_blocks.1 = (bf16[2048,1024]{1,0:T(8,128)(2,1)}, bf16[1536,768]{1,0:T(8,128)(2,1)}) custom-call(s32[32]{0:T(128)} %copy-done.8, s32[32]{0:T(128)} %copy-done.7, s32[1]{0:T(128)} %bitcast.12.plan_ref, bf16[2048,768]{1,0:T(8,128)(2,1)} %project_qkv.1.q_ref.k_ref.v_ref.qkv_ref, ...), custom_call_target="tpu_custom_call", output_to_operand_aliasing={{0}: (17, {})} | custom-call | flops 8053063680 | bytes 20971520 | tf_op jit(solution)/shard_map/other_blocks/pallas_call | solution.py:414
  346.7 8.5 %projection_grads.1 = (bf16[1024,768]{1,0:T(8,128)(2,1)S(1)}, f32[1024,1]{1,0:T(8,128)S(1)}) custom-call(s32[4]{0:T(128)S(1)} %pad_add_fusion.1.order_ref, bf16[2048,1024]{1,0:T(8,128)(2,1)} %pad_maximum_fusion.tok_ref, f32[1024,1]{1,0:T(8,128)S(1)} %copy-done.6, bf16[1024,768]{1,0:T(8,128)(2,1)S(1)} %bitcast.96, bf16[512,768]{1,0:T(8,128)(2,1)S(1)} %copy-done.10, ...), custom_call_target="tpu_custom_call" | custom-call | flops 3221225472 | bytes 7340032 | tf_op jit(solution)/shard_map/projection_grads/pallas_call | solution.py:658
  361.6 9.7 %collective-permute-start.25 = (bf16[512,1024]{1,0:T(8,128)(2,1)S(1)}, bf16[512,1024]{1,0:T(8,128)(2,1)}, u32[]{:S(2)}, u32[]{:S(2)}) collective-permute-start(bf16[512,1024]{1,0:T(8,128)(2,1)S(1)} %get-tuple-element.104), channel_id=1, source_target_pairs={{0,1},{1,2},{2,3},{4,5},{5,6},{6,7},{8,9},{9,10},{10,11},{12,13},{... | collective-permute-start | bytes 3145736 | tf_op jit(solution)/shard_map/ppermute | solution.py:733
  372.8 9.8 %collective-permute-done.25 = bf16[512,1024]{1,0:T(8,128)(2,1)} collective-permute-done((bf16[512,1024]{1,0:T(8,128)(2,1)S(1)}, bf16[512,1024]{1,0:T(8,128)(2,1)}, u32[]{:S(2)}, u32[]{:S(2)}) %collective-permute-start.25) | collective-permute-done | bytes 1048608 | tf_op jit(solution)/shard_map/ppermute | solution.py:733
  382.6 5.4 %collective-permute-done.26 = bf16[512,1024]{1,0:T(8,128)(2,1)} collective-permute-done((bf16[512,1024]{1,0:T(8,128)(2,1)S(1)}, bf16[512,1024]{1,0:T(8,128)(2,1)}, u32[]{:S(2)}, u32[]{:S(2)}) %collective-permute-start.26) | collective-permute-done | bytes 1048608 | tf_op jit(solution)/shard_map/ppermute | solution.py:734
  388.1 4.6 reduce-scatter.3.cloned.1.call-done
  406.9 4.6 collective-permute-done.28
  416.2 4.6 all-to-all-start.4
  427.4 21.7 %all-to-all-done.4 = bf16[4,32,1920]{2,1,0:T(8,128)(2,1)S(1)} async-done(((bf16[4,32,1920]{2,1,0:T(8,128)(2,1)}), bf16[4,32,1920]{2,1,0:T(8,128)(2,1)S(1)}, u32[]{:S(2)}, u32[]{:S(2)}) %all-to-all-start.4) | async-done | bytes 491552 | tf_op jit(solution)/shard_map/all_to_all | solution.py:884
  (211 shorter events, 136.8 us)
Async XLA Ops:
  9.9 28.4 %collective-permute-start.2 = (bf16[32,6656]{1,0:T(8,128)(2,1)S(1)}, bf16[32,6656]{1,0:T(8,128)(2,1)S(1)}, u32[]{:S(2)}, u32[]{:S(2)}) collective-permute-start(bf16[32,6656]{1,0:T(8,128)(2,1)S(1)} %constant_dynamic-update-slice_fusion), channel_id=1, source_target_pairs={{1,0},{2,1},{3,2},{5,4},{6,5},{7,6},{9,8},{10,9},{11,10},{13,12},{... | collective-permute-start | bytes 1277960 | tf_op jit(solution)/shard_map/ppermute | solution.py:701
  11.2 27.1 %collective-permute-start = (bf16[32,6656]{1,0:T(8,128)(2,1)S(1)}, bf16[32,6656]{1,0:T(8,128)(2,1)S(1)}, u32[]{:S(2)}, u32[]{:S(2)}) collective-permute-start(bf16[32,6656]{1,0:T(8,128)(2,1)S(1)} %constant_dynamic-update-slice_fusion), channel_id=1, source_target_pairs={{0,1},{1,2},{2,3},{4,5},{5,6},{6,7},{8,9},{9,10},{10,11},{12,13},{... | collective-permute-start | bytes 1277960 | tf_op jit(solution)/shard_map/ppermute | solution.py:700
  27.0 111.4 %all-gather.4.cloned.1.call-start = ((), (), s32[]{:S(2)}) async-start(), calls=%async_computation.7 | async-start | bytes 2211840 | tf_op jit(solution)/shard_map/all_gather | solution.py:780
  39.1 175.0 %all-gather.8.cloned.1.call-start = ((), (), s32[]{:S(2)}) async-start(), calls=%async_computation.9 | async-start | bytes 6488064 | tf_op jit(solution)/shard_map/all_gather | solution.py:791
  75.4 138.8 %all-gather.6.cloned.1.call-start = ((), (), s32[]{:S(2)}) async-start(), calls=%async_computation.8 | async-start | bytes 15335424 | tf_op jit(solution)/shard_map/all_gather | solution.py:784
  77.3 23.3 %collective-permute-start.11 = (bf16[512,1024]{1,0:T(8,128)(2,1)S(1)}, bf16[512,1024]{1,0:T(8,128)(2,1)S(1)}, u32[]{:S(2)}, u32[]{:S(2)}) collective-permute-start(bf16[512,1024]{1,0:T(8,128)(2,1)S(1)} %bitcast.99), channel_id=1, source_target_pairs={{1,0},{2,1},{3,2},{5,4},{6,5},{7,6},{9,8},{10,9},{11,10},{13,12},{... | collective-permute-start | bytes 3145736 | tf_op jit(solution)/shard_map/ppermute | solution.py:701
  78.5 23.3 %collective-permute-start.8 = (bf16[512,1024]{1,0:T(8,128)(2,1)S(1)}, bf16[512,1024]{1,0:T(8,128)(2,1)}, u32[]{:S(2)}, u32[]{:S(2)}) collective-permute-start(bf16[512,1024]{1,0:T(8,128)(2,1)S(1)} %bitcast.100), channel_id=1, source_target_pairs={{0,1},{1,2},{2,3},{4,5},{5,6},{6,7},{8,9},{9,10},{10,11},{12,13},{... | collective-permute-start | bytes 3145736 | tf_op jit(solution)/shard_map/ppermute | solution.py:700
  100.6 23.1 %collective-permute-start.12 = (bf16[512,1024]{1,0:T(8,128)(2,1)S(1)}, bf16[512,1024]{1,0:T(8,128)(2,1)}, u32[]{:S(2)}, u32[]{:S(2)}) collective-permute-start(bf16[512,1024]{1,0:T(8,128)(2,1)S(1)} %collective-permute-done.11), channel_id=1, source_target_pairs={{1,0},{2,1},{5,4},{6,5},{9,8},{10,9},{13,12},{14,13},{17,16},{18,1... | collective-permute-start | bytes 3145736 | tf_op jit(solution)/shard_map/ppermute | solution.py:701
  101.9 23.1 %collective-permute-start.9 = (bf16[512,1024]{1,0:T(8,128)(2,1)}, bf16[512,1024]{1,0:T(8,128)(2,1)}, u32[]{:S(2)}, u32[]{:S(2)}) collective-permute-start(bf16[512,1024]{1,0:T(8,128)(2,1)} %collective-permute-done.8), channel_id=1, source_target_pairs={{1,2},{2,3},{5,6},{6,7},{9,10},{10,11},{13,14},{14,15},{17,18},{18... | collective-permute-start | bytes 3145736 | tf_op jit(solution)/shard_map/ppermute | solution.py:700
  123.7 35.8 %collective-permute-start.13 = (bf16[512,1024]{1,0:T(8,128)(2,1)}, bf16[512,1024]{1,0:T(8,128)(2,1)}, u32[]{:S(2)}, u32[]{:S(2)}) collective-permute-start(bf16[512,1024]{1,0:T(8,128)(2,1)} %collective-permute-done.12), channel_id=1, source_target_pairs={{1,0},{5,4},{9,8},{13,12},{17,16},{21,20},{25,24},{29,28}} | collective-permute-start | bytes 3145736 | tf_op jit(solution)/shard_map/ppermute | solution.py:701
  125.0 34.5 %collective-permute-start.10 = (bf16[512,1024]{1,0:T(8,128)(2,1)}, bf16[512,1024]{1,0:T(8,128)(2,1)}, u32[]{:S(2)}, u32[]{:S(2)}) collective-permute-start(bf16[512,1024]{1,0:T(8,128)(2,1)} %collective-permute-done.9), channel_id=1, source_target_pairs={{2,3},{6,7},{10,11},{14,15},{18,19},{22,23},{26,27},{30,31}} | collective-permute-start | bytes 3145736 | tf_op jit(solution)/shard_map/ppermute | solution.py:700
  132.7 38.9 %all-to-all-start.1 = ((bf16[4,256,512]{2,1,0:T(8,128)(2,1)}), bf16[4,256,512]{2,1,0:T(8,128)(2,1)}, u32[]{:S(2)}, u32[]{:S(2)}) async-start(bf16[4,256,512]{2,1,0:T(8,128)(2,1)} %pad_maximum_fusion.5), calls=%async_computation.1 | async-start | bytes 2097152 | tf_op jit(solution)/shard_map/all_to_all | solution.py:790
  192.5 20.5 %all-to-all-start.2 = ((bf16[4,512,256]{2,1,0:T(8,128)(2,1)}), bf16[4,512,256]{2,1,0:T(8,128)(2,1)S(1)}, u32[]{:S(2)}, u32[]{:S(2)}) async-start(bf16[4,512,256]{2,1,0:T(8,128)(2,1)} %bitcast.8), calls=%async_computation.2 | async-start | bytes 2097152 | tf_op jit(solution)/shard_map/all_to_all | solution.py:796
  197.1 195.5 %reduce-scatter.3.cloned.1.call-start = ((), (), s32[]{:S(2)}) async-start(), calls=%async_computation.10 | async-start | bytes 19464192 | tf_op jit(solution)/shard_map/reduce_scatter | solution.py:803
  264.0 188.6 %reduce-scatter.5.cloned.1.call-start = ((), (), s32[]{:S(2)}) async-start(), calls=%async_computation.11 | async-start | bytes 2703360 | tf_op jit(solution)/shard_map/reduce_scatter | solution.py:892
  298.9 33.5 %collective-permute-start.18 = (bf16[512,1024]{1,0:T(8,128)(2,1)}, bf16[512,1024]{1,0:T(8,128)(2,1)S(1)}, u32[]{:S(2)}, u32[]{:S(2)}) collective-permute-start(bf16[512,1024]{1,0:T(8,128)(2,1)} %get-tuple-element.90), channel_id=1, source_target_pairs={{0,1},{4,5},{8,9},{12,13},{16,17},{20,21},{24,25},{28,29}} | collective-permute-start | bytes 3145736 | tf_op jit(solution)/shard_map/ppermute | solution.py:733
  300.5 31.9 %collective-permute-start.19 = (bf16[512,1024]{1,0:T(8,128)(2,1)}, bf16[512,1024]{1,0:T(8,128)(2,1)}, u32[]{:S(2)}, u32[]{:S(2)}) collective-permute-start(bf16[512,1024]{1,0:T(8,128)(2,1)} %get-tuple-element.90), channel_id=1, source_target_pairs={{3,2},{7,6},{11,10},{15,14},{19,18},{23,22},{27,26},{31,30}} | collective-permute-start | bytes 3145736 | tf_op jit(solution)/shard_map/ppermute | solution.py:734
  303.4 39.7 %collective-permute-start.22 = (bf16[2,128,1024]{2,1,0:T(8,128)(2,1)}, bf16[2,128,1024]{2,1,0:T(8,128)(2,1)S(1)}, u32[]{:S(2)}, u32[]{:S(2)}) collective-permute-start(bf16[2,128,1024]{2,1,0:T(8,128)(2,1)} %get-tuple-element.131), channel_id=1, source_target_pairs={{0,8},{8,16},{16,24},{24,0},{1,9},{9,17},{17,25},{25,1},{2,10},{10... | collective-permute-start | bytes 1572872 | tf_op jit(solution)/shard_map/ppermute | solution.py:745
  304.9 38.3 %collective-permute-start.24 = (bf16[2,128,1024]{2,1,0:T(8,128)(2,1)}, bf16[2,128,1024]{2,1,0:T(8,128)(2,1)S(1)}, u32[]{:S(2)}, u32[]{:S(2)}) collective-permute-start(bf16[2,128,1024]{2,1,0:T(8,128)(2,1)} %get-tuple-element.132), channel_id=1, source_target_pairs={{0,24},{8,0},{16,8},{24,16},{1,25},{9,1},{17,9},{25,17},{2,26},{10... | collective-permute-start | bytes 1572872 | tf_op jit(solution)/shard_map/ppermute | solution.py:745
  306.5 36.7 %collective-permute-start.23 = (bf16[2,128,1024]{2,1,0:T(8,128)(2,1)}, bf16[2,128,1024]{2,1,0:T(8,128)(2,1)S(1)}, u32[]{:S(2)}, u32[]{:S(2)}) collective-permute-start(bf16[2,128,1024]{2,1,0:T(8,128)(2,1)} %get-tuple-element.133), channel_id=1, source_target_pairs={{0,16},{8,24},{16,0},{24,8},{1,17},{9,25},{17,1},{25,9},{2,18},{10... | collective-permute-start | bytes 1572872 | tf_op jit(solution)/shard_map/ppermute | solution.py:745
  336.7 22.4 %collective-permute-start.20 = (bf16[512,1024]{1,0:T(8,128)(2,1)}, bf16[512,1024]{1,0:T(8,128)(2,1)}, u32[]{:S(2)}, u32[]{:S(2)}) collective-permute-start(bf16[512,1024]{1,0:T(8,128)(2,1)} %get-tuple-element.93), channel_id=1, source_target_pairs={{0,1},{1,2},{4,5},{5,6},{8,9},{9,10},{12,13},{13,14},{16,17},{17,1... | collective-permute-start | bytes 3145736 | tf_op jit(solution)/shard_map/ppermute | solution.py:733
  339.2 19.8 %collective-permute-start.21 = (bf16[512,1024]{1,0:T(8,128)(2,1)}, bf16[512,1024]{1,0:T(8,128)(2,1)}, u32[]{:S(2)}, u32[]{:S(2)}) collective-permute-start(bf16[512,1024]{1,0:T(8,128)(2,1)} %get-tuple-element.94), channel_id=1, source_target_pairs={{2,1},{3,2},{6,5},{7,6},{10,9},{11,10},{14,13},{15,14},{18,17},{19... | collective-permute-start | bytes 3145736 | tf_op jit(solution)/shard_map/ppermute | solution.py:734
  361.6 21.1 %collective-permute-start.25 = (bf16[512,1024]{1,0:T(8,128)(2,1)S(1)}, bf16[512,1024]{1,0:T(8,128)(2,1)}, u32[]{:S(2)}, u32[]{:S(2)}) collective-permute-start(bf16[512,1024]{1,0:T(8,128)(2,1)S(1)} %get-tuple-element.104), channel_id=1, source_target_pairs={{0,1},{1,2},{2,3},{4,5},{5,6},{6,7},{8,9},{9,10},{10,11},{12,13},{... | collective-permute-start | bytes 3145736 | tf_op jit(solution)/shard_map/ppermute | solution.py:733
  416.2 32.9 %all-to-all-start.4 = ((bf16[4,32,1920]{2,1,0:T(8,128)(2,1)}), bf16[4,32,1920]{2,1,0:T(8,128)(2,1)S(1)}, u32[]{:S(2)}, u32[]{:S(2)}) async-start(bf16[4,32,1920]{2,1,0:T(8,128)(2,1)} %fusion.11), calls=%async_computation.5 | async-start | bytes 983040 | tf_op jit(solution)/shard_map/all_to_all | solution.py:884
  (43 other events, 505.8 us)
Sparse Core Ops, SparseCore 0:
  39.3 27.3 all-gather.3
  75.5 41.5 all-gather.7
  119.0 76.5 all-gather.5
  258.3 134.3 reduce-scatter.2
  397.1 52.7 reduce-scatter.4

commit v20 on v19

--- a/solution.py
+++ b/solution.py
@@ -847,7 +847,7 @@
         )
         return kept
 
-    own_term, arrived = chain_scatter(term, "fsdp", [lambda sent: None, lambda sent: (out_grads, make_projection_grads(sent))])
+    own_term, arrived = chain_scatter(term, "fsdp", [lambda sent: out_grads, make_projection_grads])
     grad_w_qkv, gain_one_grad = kept
     grads = after(grads, arrived[-1])
 

time: 472 us -> 464 us (0.983)
  waiting for transfers between devices: 168 us -> 158 us
    all_to_all x1, waiting for transfers between devices: 14.8 us -> 9.02 us  [body(): grad_heads = lax.all_to_all(grad_attended, 'fsdp', 1, 0, tiled=True)]
    unnamed x55 -> x57, local copies, waits for them, and re-layouts: 8.48 us -> 10.4 us
  transfers between devices with their start and end apart: 42 -> 42, of which waited for: 18 -> 16; matrix products, arithmetic and copies ran while one was open for 12% -> 13% of each run, Pallas kernels for 17% -> 17%
where the time goes in v20:
time: 464 us; the launch traced here: 455 us
  waiting for transfers between devices  158 us (34%)
  Pallas kernels  123 us (27%)
  starting transfers between devices  82.6 us (18%)
  other arithmetic  41.1 us (9%)
  local copies, waits for them, and re-layouts  35.3 us (8%)
  between operations  14.8 us (3%)
    ppermute x9, waiting for transfers between devices, chain_gather(): falling = tuple((lax.ppermute(block, axis, down) for block in falling))  81.7 us
    pallas_call x1, Pallas kernels, feed_forward(): pl.pallas_call(functools.partial(ffn_kernel, span, merged), grid=(steps,)...  44 us
    pallas_call x1, Pallas kernels, other_blocks(): pl.pallas_call(functools.partial(other_blocks_kernel, heads, top), grid_s...  24.7 us
    ppermute x9, starting transfers between devices, chain_gather(): rising = tuple((lax.ppermute(block, axis, up) for block in rising))  21.1 us
    all_to_all x1, waiting for transfers between devices, body(): lax.all_to_all(late, 'fsdp', 0, 0, tiled=True)  21 us
    pallas_call x1, Pallas kernels, attend_forward(): pl.pallas_call(functools.partial(forward_kernel, heads, top), grid_spec=p...  19.9 us
    pallas_call x1, Pallas kernels, first_block(): pl.pallas_call(functools.partial(first_block_kernel, heads, top), grid_sp...  17.7 us
    all_to_all x1, waiting for transfers between devices, body(): attended = lax.all_to_all(attended_heads, 'fsdp', 0, 1, tiled=True)  15 us
  transfers between devices with their start and end apart: 42, of which 16 were waited for; matrix products, arithmetic and copies ran while one was open for 13% of the time, Pallas kernels for 17%

profile of v20, /device:TPU:0, one launch (start us, length us, event | category | flops | bytes accessed | tf_op | source)
XLA Modules:
  0.0 454.8 jit_solution(7809989952821653303)
XLA Ops:
  11.2 5.6 %collective-permute-start = (bf16[32,6656]{1,0:T(8,128)(2,1)S(1)}, bf16[32,6656]{1,0:T(8,128)(2,1)S(1)}, u32[]{:S(2)}, u32[]{:S(2)}) collective-permute-start(bf16[32,6656]{1,0:T(8,128)(2,1)S(1)} %constant_dynamic-update-slice_fusion), channel_id=1, source_target_pairs={{0,1},{1,2},{2,3},{4,5},{5,6},{6,7},{8,9},{9,10},{10,11},{12,13},{... | collective-permute-start | bytes 1277960 | tf_op jit(solution)/shard_map/ppermute | solution.py:700
  43.2 14.5 %collective-permute-done.7 = bf16[88,1024]{1,0:T(8,128)(2,1)S(1)} collective-permute-done((bf16[88,1024]{1,0:T(8,128)(2,1)S(1)}, bf16[88,1024]{1,0:T(8,128)(2,1)S(1)}, u32[]{:S(2)}, u32[]{:S(2)}) %collective-permute-start.7) | collective-permute-done | bytes 180256 | tf_op jit(solution)/shard_map/ppermute | solution.py:701
  61.6 11.5 %collective-permute-done.17 = bf16[88,1024]{1,0:T(8,128)(2,1)} collective-permute-done((bf16[88,1024]{1,0:T(8,128)(2,1)S(1)}, bf16[88,1024]{1,0:T(8,128)(2,1)}, u32[]{:S(2)}, u32[]{:S(2)}) %collective-permute-start.17) | collective-permute-done | bytes 180256 | tf_op jit(solution)/shard_map/ppermute | solution.py:701
  78.5 5.6 %collective-permute-start.8 = (bf16[512,1024]{1,0:T(8,128)(2,1)S(1)}, bf16[512,1024]{1,0:T(8,128)(2,1)}, u32[]{:S(2)}, u32[]{:S(2)}) collective-permute-start(bf16[512,1024]{1,0:T(8,128)(2,1)S(1)} %bitcast.100), channel_id=1, source_target_pairs={{0,1},{1,2},{2,3},{4,5},{5,6},{6,7},{8,9},{9,10},{10,11},{12,13},{... | collective-permute-start | bytes 3145736 | tf_op jit(solution)/shard_map/ppermute | solution.py:700
  84.1 16.5 %collective-permute-done.11 = bf16[512,1024]{1,0:T(8,128)(2,1)S(1)} collective-permute-done((bf16[512,1024]{1,0:T(8,128)(2,1)S(1)}, bf16[512,1024]{1,0:T(8,128)(2,1)S(1)}, u32[]{:S(2)}, u32[]{:S(2)}) %collective-permute-start.11) | collective-permute-done | bytes 1048608 | tf_op jit(solution)/shard_map/ppermute | solution.py:701
  106.6 17.1 %collective-permute-done.12 = bf16[512,1024]{1,0:T(8,128)(2,1)} collective-permute-done((bf16[512,1024]{1,0:T(8,128)(2,1)S(1)}, bf16[512,1024]{1,0:T(8,128)(2,1)}, u32[]{:S(2)}, u32[]{:S(2)}) %collective-permute-start.12) | collective-permute-done | bytes 1048608 | tf_op jit(solution)/shard_map/ppermute | solution.py:701
  132.7 5.5 %all-to-all-start.1 = ((bf16[4,256,512]{2,1,0:T(8,128)(2,1)}), bf16[4,256,512]{2,1,0:T(8,128)(2,1)}, u32[]{:S(2)}, u32[]{:S(2)}) async-start(bf16[4,256,512]{2,1,0:T(8,128)(2,1)} %pad_maximum_fusion.5), calls=%async_computation.1 | async-start | bytes 2097152 | tf_op jit(solution)/shard_map/all_to_all | solution.py:790
  141.1 18.4 %collective-permute-done.13 = bf16[512,1024]{1,0:T(8,128)(2,1)} collective-permute-done((bf16[512,1024]{1,0:T(8,128)(2,1)}, bf16[512,1024]{1,0:T(8,128)(2,1)}, u32[]{:S(2)}, u32[]{:S(2)}) %collective-permute-start.13) | collective-permute-done | bytes 1048608 | tf_op jit(solution)/shard_map/ppermute | solution.py:701
  164.2 7.4 %project_qkv.1.q_ref.k_ref.v_ref.qkv_ref = bf16[2048,768]{1,0:T(8,128)(2,1)} custom-call(bf16[2048,1024]{1,0:T(8,128)(2,1)} %pad_maximum_fusion.tok_ref, f32[1,1024]{1,0:T(1,128)S(1)} %reshape.214.gain_ref, bf16[1024,768]{1,0:T(8,128)(2,1)S(1)} %bitcast.93, f32[2048,128]{1,0:T(8,128)S(1)} %get-tuple-element.155.cos_ref, f32[2048,128]{1,0:T(8,128)S(1)} %copy-done.3), custom_call_target="tpu_custom_call" | custom-call | flops 3221225472 | bytes 14680064 | tf_op jit(solution)/shard_map/project_qkv/pallas_call | solution.py:62
  171.6 19.9 %attend_forward.1 = (bf16[2048,256]{1,0:T(8,128)(2,1)}, f32[2048,2]{1,0:T(8,128)S(1)}) custom-call(s32[32]{0:T(128)S(1)} %reshape_squeeze.27.chosen_ref, s32[32]{0:T(128)S(1)} %reshape_squeeze.28.counts_ref, bf16[2048,768]{1,0:T(8,128)(2,1)} %project_qkv.1.q_ref.k_ref.v_ref.qkv_ref, bf16[2048,768]{1,0:T(8,128)(2,1)} %project_qkv.1.q_ref.k_ref.v_ref.qkv_ref, ...), custom_call_target="tpu_custom_call" | custom-call | flops 3221225472 | bytes 4194304 | tf_op jit(solution)/shard_map/attend_forward/pallas_call | solution.py:154
  192.5 4.6 %all-to-all-start.2 = ((bf16[4,512,256]{2,1,0:T(8,128)(2,1)}), bf16[4,512,256]{2,1,0:T(8,128)(2,1)S(1)}, u32[]{:S(2)}, u32[]{:S(2)}) async-start(bf16[4,512,256]{2,1,0:T(8,128)(2,1)} %bitcast.8), calls=%async_computation.2 | async-start | bytes 2097152 | tf_op jit(solution)/shard_map/all_to_all | solution.py:796
  198.1 15.0 %all-to-all-done.2 = bf16[4,512,256]{2,1,0:T(8,128)(2,1)S(1)} async-done(((bf16[4,512,256]{2,1,0:T(8,128)(2,1)}), bf16[4,512,256]{2,1,0:T(8,128)(2,1)S(1)}, u32[]{:S(2)}, u32[]{:S(2)}) %all-to-all-start.2) | async-done | bytes 1048608 | tf_op jit(solution)/shard_map/all_to_all | solution.py:796
  214.2 44.0 %feed_forward.1 = (bf16[512,1024]{1,0:T(8,128)(2,1)}, f32[512,1024]{1,0:T(8,128)}, bf16[512,1024]{1,0:T(8,128)(2,1)}, f32[1,1024]{1,0:T(1,128)}, bf16[8,128,1024...) custom-call(bf16[512,1024]{1,0:T(8,128)(2,1)} %bitcast.98, bf16[512,1024]{1,0:T(8,128)(2,1)} %bitcast.118, ...), custom_call_target="tpu_custom_call" | custom-call | flops 29796335616 | bytes 38797312 | tf_op jit(solution)/shard_map/feed_forward/pallas_call | solution.py:595
  270.9 9.0 %all-to-all-done.3 = bf16[512,4,256]{2,0,1:T(8,128)(2,1)S(1)} async-done(((bf16[512,4,256]{2,0,1:T(8,128)(2,1)}), bf16[512,4,256]{2,0,1:T(8,128)(2,1)S(1)}, u32[]{:S(2)}, u32[]{:S(2)}) %all-to-all-start.3) | async-done | bytes 1048608 | tf_op jit(solution)/shard_map/all_to_all | solution.py:802
  280.9 17.7 %first_block.1 = (bf16[512,1024]{1,0:T(8,128)(2,1)}, bf16[2048,1024]{1,0:T(8,128)(2,1)}, bf16[512,768]{1,0:T(8,128)(2,1)}, f32[2048,256]{1,0:T(8,128)}, f32[2048,256]{1,0:T(8,128)}, /*index=5*/f32[2048,256]{1,0:T(8,128)}) custom-call(s32[32]{0:T(128)} %copy-done.8, s32[32]{0:T(128)} %copy-done.7, s32[2]{0:T(128)} %pad_add_fusion.plan_ref, ...), custom_call_target="tpu_custom_call" | custom-call | flops 4294967296 | bytes 20971520 | tf_op jit(solution)/shard_map/first_block/pallas_call | solution.py:310
  304.6 24.7 %other_blocks.1 = (bf16[2048,1024]{1,0:T(8,128)(2,1)}, bf16[1536,768]{1,0:T(8,128)(2,1)}) custom-call(s32[32]{0:T(128)} %copy-done.8, s32[32]{0:T(128)} %copy-done.7, s32[1]{0:T(128)} %bitcast.12.plan_ref, bf16[2048,768]{1,0:T(8,128)(2,1)} %project_qkv.1.q_ref.k_ref.v_ref.qkv_ref, ...), custom_call_target="tpu_custom_call", output_to_operand_aliasing={{0}: (17, {})} | custom-call | flops 8053063680 | bytes 20971520 | tf_op jit(solution)/shard_map/other_blocks/pallas_call | solution.py:414
  330.3 4.7 %add_convert_fusion.2 = (bf16[512,1024]{1,0:T(8,128)(2,1)}, bf16[512,1024]{1,0:T(8,128)(2,1)}) fusion(bf16[512,1024]{1,0:T(8,128)(2,1)} %collective-permute-done.19, bf16[2048,1024]{1,0:T(8,128)(2,1)} %get-tuple-element.87, s32[]{:T(128)S(6)} %select_n.326, bf16[512,1024]{1,0:T(8,128)(2,1)} %copy-done.19, s32[]{:T(128)S(6)} %select_n.325), kind=kLoop, calls=%fused_computation.14 | loop fusion | flops 4194304 | bytes 6291464 | tf_op jit(solution)/shard_map/convert_element_type | solution.py:731
  343.6 8.9 %projection_grads.1 = (bf16[1024,768]{1,0:T(8,128)(2,1)S(1)}, f32[1024,1]{1,0:T(8,128)S(1)}) custom-call(s32[4]{0:T(128)S(1)} %pad_add_fusion.1.order_ref, bf16[2048,1024]{1,0:T(8,128)(2,1)} %pad_maximum_fusion.tok_ref, f32[1024,1]{1,0:T(8,128)S(1)} %copy-done.6, bf16[1024,768]{1,0:T(8,128)(2,1)S(1)} %bitcast.96, bf16[512,768]{1,0:T(8,128)(2,1)S(1)} %copy-done.10, ...), custom_call_target="tpu_custom_call" | custom-call | flops 3221225472 | bytes 7340032 | tf_op jit(solution)/shard_map/projection_grads/pallas_call | solution.py:658
  352.5 5.1 %collective-permute-done.23 = bf16[512,1024]{1,0:T(8,128)(2,1)} collective-permute-done((bf16[512,1024]{1,0:T(8,128)(2,1)}, bf16[512,1024]{1,0:T(8,128)(2,1)}, u32[]{:S(2)}, u32[]{:S(2)}) %collective-permute-start.23) | collective-permute-done | bytes 1048608 | tf_op jit(solution)/shard_map/ppermute | solution.py:733
  360.4 9.0 %collective-permute-start.25 = (bf16[512,1024]{1,0:T(8,128)(2,1)S(1)}, bf16[512,1024]{1,0:T(8,128)(2,1)}, u32[]{:S(2)}, u32[]{:S(2)}) collective-permute-start(bf16[512,1024]{1,0:T(8,128)(2,1)S(1)} %get-tuple-element.104), channel_id=1, source_target_pairs={{0,1},{1,2},{2,3},{4,5},{5,6},{6,7},{8,9},{9,10},{10,11},{12,13},{... | collective-permute-start | bytes 3145736 | tf_op jit(solution)/shard_map/ppermute | solution.py:733
  370.9 9.8 %collective-permute-done.25 = bf16[512,1024]{1,0:T(8,128)(2,1)} collective-permute-done((bf16[512,1024]{1,0:T(8,128)(2,1)S(1)}, bf16[512,1024]{1,0:T(8,128)(2,1)}, u32[]{:S(2)}, u32[]{:S(2)}) %collective-permute-start.25) | collective-permute-done | bytes 1048608 | tf_op jit(solution)/shard_map/ppermute | solution.py:733
  380.7 5.5 %collective-permute-done.26 = bf16[512,1024]{1,0:T(8,128)(2,1)} collective-permute-done((bf16[512,1024]{1,0:T(8,128)(2,1)S(1)}, bf16[512,1024]{1,0:T(8,128)(2,1)}, u32[]{:S(2)}, u32[]{:S(2)}) %collective-permute-start.26) | collective-permute-done | bytes 1048608 | tf_op jit(solution)/shard_map/ppermute | solution.py:734
  400.5 4.4 collective-permute-done.28
  419.9 21.0 %all-to-all-done.4 = bf16[4,32,1920]{2,1,0:T(8,128)(2,1)S(1)} async-done(((bf16[4,32,1920]{2,1,0:T(8,128)(2,1)}), bf16[4,32,1920]{2,1,0:T(8,128)(2,1)S(1)}, u32[]{:S(2)}, u32[]{:S(2)}) %all-to-all-start.4) | async-done | bytes 491552 | tf_op jit(solution)/shard_map/all_to_all | solution.py:884
  (213 shorter events, 134.7 us)
Async XLA Ops:
  9.9 28.4 %collective-permute-start.2 = (bf16[32,6656]{1,0:T(8,128)(2,1)S(1)}, bf16[32,6656]{1,0:T(8,128)(2,1)S(1)}, u32[]{:S(2)}, u32[]{:S(2)}) collective-permute-start(bf16[32,6656]{1,0:T(8,128)(2,1)S(1)} %constant_dynamic-update-slice_fusion), channel_id=1, source_target_pairs={{1,0},{2,1},{3,2},{5,4},{6,5},{7,6},{9,8},{10,9},{11,10},{13,12},{... | collective-permute-start | bytes 1277960 | tf_op jit(solution)/shard_map/ppermute | solution.py:701
  11.2 27.1 %collective-permute-start = (bf16[32,6656]{1,0:T(8,128)(2,1)S(1)}, bf16[32,6656]{1,0:T(8,128)(2,1)S(1)}, u32[]{:S(2)}, u32[]{:S(2)}) collective-permute-start(bf16[32,6656]{1,0:T(8,128)(2,1)S(1)} %constant_dynamic-update-slice_fusion), channel_id=1, source_target_pairs={{0,1},{1,2},{2,3},{4,5},{5,6},{6,7},{8,9},{9,10},{10,11},{12,13},{... | collective-permute-start | bytes 1277960 | tf_op jit(solution)/shard_map/ppermute | solution.py:700
  27.0 111.4 %all-gather.4.cloned.1.call-start = ((), (), s32[]{:S(2)}) async-start(), calls=%async_computation.7 | async-start | bytes 2211840 | tf_op jit(solution)/shard_map/all_gather | solution.py:780
  39.1 175.0 %all-gather.8.cloned.1.call-start = ((), (), s32[]{:S(2)}) async-start(), calls=%async_computation.9 | async-start | bytes 6488064 | tf_op jit(solution)/shard_map/all_gather | solution.py:791
  75.4 138.8 %all-gather.6.cloned.1.call-start = ((), (), s32[]{:S(2)}) async-start(), calls=%async_computation.8 | async-start | bytes 15335424 | tf_op jit(solution)/shard_map/all_gather | solution.py:784
  77.2 23.3 %collective-permute-start.11 = (bf16[512,1024]{1,0:T(8,128)(2,1)S(1)}, bf16[512,1024]{1,0:T(8,128)(2,1)S(1)}, u32[]{:S(2)}, u32[]{:S(2)}) collective-permute-start(bf16[512,1024]{1,0:T(8,128)(2,1)S(1)} %bitcast.99), channel_id=1, source_target_pairs={{1,0},{2,1},{3,2},{5,4},{6,5},{7,6},{9,8},{10,9},{11,10},{13,12},{... | collective-permute-start | bytes 3145736 | tf_op jit(solution)/shard_map/ppermute | solution.py:701
  78.5 23.3 %collective-permute-start.8 = (bf16[512,1024]{1,0:T(8,128)(2,1)S(1)}, bf16[512,1024]{1,0:T(8,128)(2,1)}, u32[]{:S(2)}, u32[]{:S(2)}) collective-permute-start(bf16[512,1024]{1,0:T(8,128)(2,1)S(1)} %bitcast.100), channel_id=1, source_target_pairs={{0,1},{1,2},{2,3},{4,5},{5,6},{6,7},{8,9},{9,10},{10,11},{12,13},{... | collective-permute-start | bytes 3145736 | tf_op jit(solution)/shard_map/ppermute | solution.py:700
  100.6 23.1 %collective-permute-start.12 = (bf16[512,1024]{1,0:T(8,128)(2,1)S(1)}, bf16[512,1024]{1,0:T(8,128)(2,1)}, u32[]{:S(2)}, u32[]{:S(2)}) collective-permute-start(bf16[512,1024]{1,0:T(8,128)(2,1)S(1)} %collective-permute-done.11), channel_id=1, source_target_pairs={{1,0},{2,1},{5,4},{6,5},{9,8},{10,9},{13,12},{14,13},{17,16},{18,1... | collective-permute-start | bytes 3145736 | tf_op jit(solution)/shard_map/ppermute | solution.py:701
  101.9 23.1 %collective-permute-start.9 = (bf16[512,1024]{1,0:T(8,128)(2,1)}, bf16[512,1024]{1,0:T(8,128)(2,1)}, u32[]{:S(2)}, u32[]{:S(2)}) collective-permute-start(bf16[512,1024]{1,0:T(8,128)(2,1)} %collective-permute-done.8), channel_id=1, source_target_pairs={{1,2},{2,3},{5,6},{6,7},{9,10},{10,11},{13,14},{14,15},{17,18},{18... | collective-permute-start | bytes 3145736 | tf_op jit(solution)/shard_map/ppermute | solution.py:700
  123.7 35.8 %collective-permute-start.13 = (bf16[512,1024]{1,0:T(8,128)(2,1)}, bf16[512,1024]{1,0:T(8,128)(2,1)}, u32[]{:S(2)}, u32[]{:S(2)}) collective-permute-start(bf16[512,1024]{1,0:T(8,128)(2,1)} %collective-permute-done.12), channel_id=1, source_target_pairs={{1,0},{5,4},{9,8},{13,12},{17,16},{21,20},{25,24},{29,28}} | collective-permute-start | bytes 3145736 | tf_op jit(solution)/shard_map/ppermute | solution.py:701
  125.0 34.5 %collective-permute-start.10 = (bf16[512,1024]{1,0:T(8,128)(2,1)}, bf16[512,1024]{1,0:T(8,128)(2,1)}, u32[]{:S(2)}, u32[]{:S(2)}) collective-permute-start(bf16[512,1024]{1,0:T(8,128)(2,1)} %collective-permute-done.9), channel_id=1, source_target_pairs={{2,3},{6,7},{10,11},{14,15},{18,19},{22,23},{26,27},{30,31}} | collective-permute-start | bytes 3145736 | tf_op jit(solution)/shard_map/ppermute | solution.py:700
  132.7 38.9 %all-to-all-start.1 = ((bf16[4,256,512]{2,1,0:T(8,128)(2,1)}), bf16[4,256,512]{2,1,0:T(8,128)(2,1)}, u32[]{:S(2)}, u32[]{:S(2)}) async-start(bf16[4,256,512]{2,1,0:T(8,128)(2,1)} %pad_maximum_fusion.5), calls=%async_computation.1 | async-start | bytes 2097152 | tf_op jit(solution)/shard_map/all_to_all | solution.py:790
  192.5 20.5 %all-to-all-start.2 = ((bf16[4,512,256]{2,1,0:T(8,128)(2,1)}), bf16[4,512,256]{2,1,0:T(8,128)(2,1)S(1)}, u32[]{:S(2)}, u32[]{:S(2)}) async-start(bf16[4,512,256]{2,1,0:T(8,128)(2,1)} %bitcast.8), calls=%async_computation.2 | async-start | bytes 2097152 | tf_op jit(solution)/shard_map/all_to_all | solution.py:796
  197.1 189.0 %reduce-scatter.3.cloned.1.call-start = ((), (), s32[]{:S(2)}) async-start(), calls=%async_computation.10 | async-start | bytes 19464192 | tf_op jit(solution)/shard_map/reduce_scatter | solution.py:803
  264.0 180.3 %reduce-scatter.5.cloned.1.call-start = ((), (), s32[]{:S(2)}) async-start(), calls=%async_computation.11 | async-start | bytes 2703360 | tf_op jit(solution)/shard_map/reduce_scatter | solution.py:892
  265.4 36.7 %collective-permute-start.20 = (bf16[2,128,1024]{2,1,0:T(8,128)(2,1)}, bf16[2,128,1024]{2,1,0:T(8,128)(2,1)}, u32[]{:S(2)}, u32[]{:S(2)}) collective-permute-start(bf16[2,128,1024]{2,1,0:T(8,128)(2,1)} %get-tuple-element.131), channel_id=1, source_target_pairs={{0,8},{8,16},{16,24},{24,0},{1,9},{9,17},{17,25},{25,1},{2,10},{10... | collective-permute-start | bytes 1572872 | tf_op jit(solution)/shard_map/ppermute | solution.py:745
  266.9 35.2 %collective-permute-start.22 = (bf16[2,128,1024]{2,1,0:T(8,128)(2,1)}, bf16[2,128,1024]{2,1,0:T(8,128)(2,1)}, u32[]{:S(2)}, u32[]{:S(2)}) collective-permute-start(bf16[2,128,1024]{2,1,0:T(8,128)(2,1)} %get-tuple-element.132), channel_id=1, source_target_pairs={{0,24},{8,0},{16,8},{24,16},{1,25},{9,1},{17,9},{25,17},{2,26},{10... | collective-permute-start | bytes 1572872 | tf_op jit(solution)/shard_map/ppermute | solution.py:745
  268.8 33.3 %collective-permute-start.21 = (bf16[2,128,1024]{2,1,0:T(8,128)(2,1)}, bf16[2,128,1024]{2,1,0:T(8,128)(2,1)}, u32[]{:S(2)}, u32[]{:S(2)}) collective-permute-start(bf16[2,128,1024]{2,1,0:T(8,128)(2,1)} %get-tuple-element.133), channel_id=1, source_target_pairs={{0,16},{8,24},{16,0},{24,8},{1,17},{9,25},{17,1},{25,9},{2,18},{10... | collective-permute-start | bytes 1572872 | tf_op jit(solution)/shard_map/ppermute | solution.py:745
  298.6 30.7 %collective-permute-start.18 = (bf16[512,1024]{1,0:T(8,128)(2,1)}, bf16[512,1024]{1,0:T(8,128)(2,1)S(1)}, u32[]{:S(2)}, u32[]{:S(2)}) collective-permute-start(bf16[512,1024]{1,0:T(8,128)(2,1)} %get-tuple-element.90), channel_id=1, source_target_pairs={{0,1},{4,5},{8,9},{12,13},{16,17},{20,21},{24,25},{28,29}} | collective-permute-start | bytes 3145736 | tf_op jit(solution)/shard_map/ppermute | solution.py:733
  300.2 29.1 %collective-permute-start.19 = (bf16[512,1024]{1,0:T(8,128)(2,1)}, bf16[512,1024]{1,0:T(8,128)(2,1)}, u32[]{:S(2)}, u32[]{:S(2)}) collective-permute-start(bf16[512,1024]{1,0:T(8,128)(2,1)} %get-tuple-element.90), channel_id=1, source_target_pairs={{3,2},{7,6},{11,10},{15,14},{19,18},{23,22},{27,26},{31,30}} | collective-permute-start | bytes 3145736 | tf_op jit(solution)/shard_map/ppermute | solution.py:734
  335.0 22.7 %collective-permute-start.23 = (bf16[512,1024]{1,0:T(8,128)(2,1)}, bf16[512,1024]{1,0:T(8,128)(2,1)}, u32[]{:S(2)}, u32[]{:S(2)}) collective-permute-start(bf16[512,1024]{1,0:T(8,128)(2,1)} %get-tuple-element.94), channel_id=1, source_target_pairs={{0,1},{1,2},{4,5},{5,6},{8,9},{9,10},{12,13},{13,14},{16,17},{17,1... | collective-permute-start | bytes 3145736 | tf_op jit(solution)/shard_map/ppermute | solution.py:733
  337.5 20.2 %collective-permute-start.24 = (bf16[512,1024]{1,0:T(8,128)(2,1)}, bf16[512,1024]{1,0:T(8,128)(2,1)}, u32[]{:S(2)}, u32[]{:S(2)}) collective-permute-start(bf16[512,1024]{1,0:T(8,128)(2,1)} %get-tuple-element.95), channel_id=1, source_target_pairs={{2,1},{3,2},{6,5},{7,6},{10,9},{11,10},{14,13},{15,14},{18,17},{19... | collective-permute-start | bytes 3145736 | tf_op jit(solution)/shard_map/ppermute | solution.py:734
  360.4 20.3 %collective-permute-start.25 = (bf16[512,1024]{1,0:T(8,128)(2,1)S(1)}, bf16[512,1024]{1,0:T(8,128)(2,1)}, u32[]{:S(2)}, u32[]{:S(2)}) collective-permute-start(bf16[512,1024]{1,0:T(8,128)(2,1)S(1)} %get-tuple-element.104), channel_id=1, source_target_pairs={{0,1},{1,2},{2,3},{4,5},{5,6},{6,7},{8,9},{9,10},{10,11},{12,13},{... | collective-permute-start | bytes 3145736 | tf_op jit(solution)/shard_map/ppermute | solution.py:733
  409.9 31.0 %all-to-all-start.4 = ((bf16[4,32,1920]{2,1,0:T(8,128)(2,1)}), bf16[4,32,1920]{2,1,0:T(8,128)(2,1)S(1)}, u32[]{:S(2)}, u32[]{:S(2)}) async-start(bf16[4,32,1920]{2,1,0:T(8,128)(2,1)} %fusion.11), calls=%async_computation.5 | async-start | bytes 983040 | tf_op jit(solution)/shard_map/all_to_all | solution.py:884
  (44 other events, 493.8 us)
Sparse Core Ops, SparseCore 0:
  39.3 27.3 all-gather.3
  75.5 41.5 all-gather.7
  119.0 76.5 all-gather.5
  258.3 117.7 reduce-scatter.2
  390.6 50.4 reduce-scatter.4
